TPU v7x, 32 devices: a whole 2x2x4 slice. The times are simulated.
32 devices in a mesh: node: 4 (over x, core), local: 8 (over z, y).
Axes of the slice: x: 2, y: 2, z: 4, core: 2. Of those that a mesh axis runs over, the one named last changes fastest.
Arguments:
- partials: bfloat16 [4, 8, 1048576], P('node', 'local'), may hold values from -8 to 8
- signs: int32 [1048576], replicated, may hold values 0 or 1
Outputs:
- reduced: float32 [1048576], P(('node', 'local'))
- rotated_max: float32 [8192], P(('node', 'local'))
Inputs may be any that keep to these rules, and one draw needn't show every extreme that they name: `signs`: 0 selects the sign +1 and 1 the sign -1 of a position.
All inputs are finite; a program needn't handle non-finite values.
Results may differ from a plain program's by a relative error of at most 0.0003.
Values may be sent and summed in bfloat16 or wider, within the bound.
No kernel may reach another device: no remote copies, remote signals or barrier semaphores. Data moves between devices by JAX's collectives and lax.ppermute only.
A program may use at most 64 MiB of HBM per device.

v0:
```python
import jax
import jax.numpy as jnp
from jax import lax
from jax.sharding import PartitionSpec as P

ROT = 256
QGROUP = 128


def sylvester():
    positions = jnp.arange(ROT, dtype=jnp.int32)
    parity = jnp.zeros((ROT, ROT), dtype=jnp.int32)
    for level in range(ROT.bit_length() - 1):
        column = positions >> level & 1
        parity = parity + column[:, None] * column[None, :]
    return (1 - 2 * (parity % 2)).astype(jnp.float32)


def power_scale(largest):
    scaling = jnp.full(largest.shape, 2.0 ** (-37), dtype=jnp.float32)
    for power in range(-30, 31):
        scaling = jnp.where(largest >= 2.0**power, jnp.float32(2.0 ** (power - 7)), scaling)
    return scaling


def quantize(scaled):
    magnitude = jnp.abs(scaled)
    spacing = jnp.full(scaled.shape, 2.0 ** (-9), dtype=jnp.float32)
    for power in range(-5, 8):
        spacing = jnp.where(magnitude >= 2.0**power, jnp.float32(2.0 ** (power - 3)), spacing)
    return jnp.sign(scaled) * jnp.floor(magnitude / spacing + 0.5) * spacing


def encode(values):
    grouped = values.reshape(values.shape[:-1] + (values.shape[-1] // QGROUP, QGROUP))
    largest = jnp.max(jnp.abs(grouped), axis=-1)
    scaling = power_scale(largest)
    coded = quantize(grouped / scaling[..., None]).astype(jnp.bfloat16)
    return (coded.reshape(values.shape), scaling.astype(jnp.bfloat16))


def decode(coded, scales):
    grouped = coded.reshape(coded.shape[:-1] + (coded.shape[-1] // QGROUP, QGROUP))
    values = grouped.astype(jnp.float32) * scales.astype(jnp.float32)[..., None]
    return values.reshape(coded.shape)


def local_section(coded, scales):
    got_coded, got_scales = (
        lax.all_to_all(coded, "local", split_axis=1, concat_axis=1, tiled=True),
        lax.all_to_all(scales, "local", split_axis=1, concat_axis=1, tiled=True),
    )
    return encode(jnp.sum(decode(got_coded, got_scales), axis=1))


def shards(partials, signs):
    values = partials.reshape(-1)
    length = values.shape[0]
    members = lax.axis_size("local")
    groups = lax.axis_size("node")
    portion = length // (members * groups)
    matrix = sylvester()
    signed = values * (1 - 2 * signs).astype(jnp.bfloat16)
    rotated = jnp.dot(
        signed.reshape(-1, ROT), matrix.astype(jnp.bfloat16), preferred_element_type=jnp.float32
    ).reshape(-1)
    coded, scales = encode(rotated)
    coded = coded.reshape(groups, members, portion)
    scales = scales.reshape(groups, members, portion // QGROUP)
    coded, scales = (
        lax.all_to_all(coded, "node", split_axis=0, concat_axis=0, tiled=True),
        lax.all_to_all(scales, "node", split_axis=0, concat_axis=0, tiled=True),
    )
    first_coded, first_scales = local_section(coded, scales)
    second = jnp.sum(decode(first_coded, first_scales), axis=0)
    rotated_max = jnp.max(jnp.abs(second.reshape(-1, QGROUP)), axis=-1) / jnp.sqrt(jnp.float32(ROT))
    node_index = lax.axis_index("node")
    local_index = lax.axis_index("local")
    offset = node_index * (length // groups) + local_index * portion
    own_flips = (1 - 2 * lax.dynamic_slice_in_dim(signs, offset, portion)).astype(jnp.float32)
    turned_back = jnp.dot(
        second.reshape(-1, ROT),
        matrix,
        precision=lax.Precision.HIGHEST,
        preferred_element_type=jnp.float32,
    ).reshape(-1)
    reduced = turned_back / ROT * own_flips
    return (reduced, rotated_max)


def solution(mesh):
    in_specs = (P("node", "local", None), P())
    out_specs = (P(("node", "local")), P(("node", "local")))
    return jax.shard_map(shards, mesh=mesh, in_specs=in_specs, out_specs=out_specs, check_vma=False)
```

profile of v0, /device:TPU:0, one launch (start us, length us, event | category | flops | bytes accessed | tf_op | source)
XLA Modules:
  0.0 186.5 jit_solution(11349597689158673873)
XLA Ops:
  0.7 44.5 %reduce.4 = bf16[1048576]{0:T(1024)(128)(2,1)S(1)} reduce(bf16[1,1,1048576]{2,1,0:T(2,128)(2,1)} %param.2, bf16[]{:T(256)} %constant.14), dimensions={0,1}, to_apply=%param.2.reduce_sub_computation | reduce | bytes 4194306 | tf_op args[0]
  45.2 4.3 %fusion = bf16[1048576]{0:T(1024)(128)(2,1)} fusion(bf16[1048576]{0:T(1024)(128)(2,1)S(1)} %reduce.4, s32[1048576]{0:T(1024)} %param.3), kind=kLoop, calls=%fused_computation.12 | loop fusion | flops 4194304 | bytes 8388608 | tf_op jit(solution)/shard_map/mul | solution.py:63
  49.5 2.7 %reshape.507 = bf16[4096,256]{1,0:T(8,128)(2,1)S(1)} reshape(bf16[1048576]{0:T(1024)(128)(2,1)} %fusion) | data formatting | bytes 4194304 | tf_op jit(solution)/shard_map/reshape | solution.py:65
  52.2 4.3 %fusion.19 = (f32[4096,256]{1,0:T(8,128)}, f32[4096,256]{1,0:T(8,128)}) fusion(bf16[4096,256]{1,0:T(8,128)(2,1)S(1)} %reshape.507, s32[256]{0:T(256)S(1)} %get-tuple-element.53, s32[256]{0:T(256)S(1)} %get-tuple-element.54, s32[256]{0:T(256)S(1)} %get-tuple-element.55, s32[256]{0:T(256)S(1)} %get-tuple-element.56, s32[256]{0:T(256)S(1)} %get-tuple-element.57, ...), kind=kOutput, calls=%fused_computation.105 | convolution fusion | flops 539885568 | bytes 10493952 | tf_op jit(solution)/shard_map/dot_general | solution.py:64
  56.4 4.7 %abs.31 = f32[8192,128]{1,0:T(8,128)} reshape(f32[4096,256]{1,0:T(8,128)} %get-tuple-element.51) | data formatting | bytes 8388608 | tf_op jit(solution)/shard_map/abs | solution.py:36
  61.1 3.3 %reduce_max.27 = f32[8192]{0:T(1024)S(1)} reduce(f32[8192,128]{1,0:T(8,128)} %abs.31, f32[]{:T(128)} %constant.91.clone.1), dimensions={1}, to_apply=%region_0.1 | reduce | flops 1040384 | bytes 4227076 | tf_op jit(solution)/shard_map/reduce_max | solution.py:36
  64.5 0.2 broadcast_compare_fusion
  65.7 0.8 fusion.18
  66.5 4.2 %all-to-all-start.2 = ((bf16[4,8,256]{2,1,0:T(8,128)(2,1)}), bf16[4,8,256]{2,1,0:T(8,128)(2,1)S(1)}, u32[]{:S(2)}, u32[]{:S(2)}) async-start(bf16[4,8,256]{2,1,0:T(8,128)(2,1)} %get-tuple-element.4), calls=%async_computation.2 | async-start | bytes 32768 | tf_op jit(solution)/shard_map/all_to_all | solution.py:72
  70.7 0.2 copy.12
  70.9 5.0 %reshape_reshape.4 = f32[4,8,32768]{2,1,0:T(8,128)} reshape(f32[4096,256]{1,0:T(8,128)} %get-tuple-element.52) | data formatting | bytes 8388608 | tf_op jit(solution)/shard_map/reshape;reshape | solution.py:35
  75.9 8.6 %multiply_convert_fusion = bf16[4,8,32768]{2,1,0:T(8,128)(2,1)} fusion(f32[4,8,32768]{2,1,0:T(8,128)} %reshape_reshape.4, f32[4,8,256]{1,2,0:T(8,128)S(1)} %copy.12), kind=kLoop, calls=%fused_computation.2 | loop fusion | flops 36700160 | bytes 6324224 | tf_op jit(solution)/shard_map/convert_element_type | solution.py:38
  84.5 0.0 all-to-all-done.2
  84.5 3.6 %all-to-all-start = ((bf16[4,8,32768]{2,1,0:T(8,128)(2,1)}), bf16[4,8,32768]{2,1,0:T(8,128)(2,1)S(1)}, u32[]{:S(2)}, u32[]{:S(2)}) async-start(bf16[4,8,32768]{2,1,0:T(8,128)(2,1)} %multiply_convert_fusion), calls=%async_computation | async-start | bytes 4194304 | tf_op jit(solution)/shard_map/all_to_all | solution.py:71
  88.2 0.6 copy.14
  88.8 25.1 %all-to-all-done = bf16[4,8,32768]{2,1,0:T(8,128)(2,1)S(1)} async-done(((bf16[4,8,32768]{2,1,0:T(8,128)(2,1)}), bf16[4,8,32768]{2,1,0:T(8,128)(2,1)S(1)}, u32[]{:S(2)}, u32[]{:S(2)}) %all-to-all-start) | async-done | bytes 2097184 | tf_op jit(solution)/shard_map/all_to_all | solution.py:71
  113.8 6.3 %all-to-all-start.3 = ((bf16[4,8,256]{2,0,1:T(4,128)(2,1)}), bf16[4,8,256]{2,0,1:T(4,128)(2,1)S(1)}, u32[]{:S(2)}, u32[]{:S(2)}) async-start(bf16[4,8,256]{2,0,1:T(4,128)(2,1)} %copy.14), calls=%async_computation.3 | async-start | bytes 32768 | tf_op jit(solution)/shard_map/all_to_all | solution.py:51
  120.2 3.0 %copy.13 = bf16[4,8,32768]{2,0,1:T(4,128)(2,1)} copy(bf16[4,8,32768]{2,1,0:T(8,128)(2,1)S(1)} %all-to-all-done) | data formatting | bytes 4194304 | tf_op jit(solution)/shard_map/all_to_all | solution.py:71
  123.2 3.6 %all-to-all-done.3 = bf16[4,8,256]{2,0,1:T(4,128)(2,1)S(1)} async-done(((bf16[4,8,256]{2,0,1:T(4,128)(2,1)}), bf16[4,8,256]{2,0,1:T(4,128)(2,1)S(1)}, u32[]{:S(2)}, u32[]{:S(2)}) %all-to-all-start.3) | async-done | bytes 16416 | tf_op jit(solution)/shard_map/all_to_all | solution.py:51
  126.7 3.6 %all-to-all-start.1 = ((bf16[4,8,32768]{2,0,1:T(4,128)(2,1)}), bf16[4,8,32768]{2,0,1:T(4,128)(2,1)S(1)}, u32[]{:S(2)}, u32[]{:S(2)}) async-start(bf16[4,8,32768]{2,0,1:T(4,128)(2,1)} %copy.13), calls=%async_computation.1 | async-start | bytes 4194304 | tf_op jit(solution)/shard_map/all_to_all | solution.py:50
  130.4 2.6 %mul.262 = f32[4,8,256,128]{3,2,0,1:T(8,128)} broadcast(bf16[4,8,256]{2,0,1:T(4,128)(2,1)S(1)} %all-to-all-done.3), dimensions={0,1,2} | broadcast | bytes 4210688 | tf_op jit(solution)/shard_map/mul | solution.py:44
  133.0 5.6 %mul.263 = f32[4,8,32768]{2,0,1:T(4,128)} reshape(f32[4,8,256,128]{3,2,0,1:T(8,128)} %mul.262) | data formatting | bytes 8388608 | tf_op jit(solution)/shard_map/mul | solution.py:44
  138.6 38.6 %all-to-all-done.1 = bf16[4,8,32768]{2,0,1:T(4,128)(2,1)S(1)} async-done(((bf16[4,8,32768]{2,0,1:T(4,128)(2,1)}), bf16[4,8,32768]{2,0,1:T(4,128)(2,1)S(1)}, u32[]{:S(2)}, u32[]{:S(2)}) %all-to-all-start.1) | async-done | bytes 2097184 | tf_op jit(solution)/shard_map/all_to_all | solution.py:50
  177.2 3.5 %multiply_reduce_fusion = f32[4,32768]{1,0:T(4,128)S(1)} fusion(f32[4,8,32768]{2,0,1:T(4,128)} %mul.263, bf16[4,8,32768]{2,0,1:T(4,128)(2,1)S(1)} %all-to-all-done.1), kind=kLoop, calls=%fused_computation.1 | loop fusion | flops 3014656 | bytes 6815744 | tf_op jit(solution)/shard_map/reduce_sum | solution.py:53
  180.7 0.1 abs_bitcast_fusion
  180.9 0.2 bitcast_reduce_fusion
  181.1 0.2 broadcast_bitcast_fusion
  181.3 0.2 broadcast_bitcast_fusion.1
  181.5 2.0 %fusion.2 = f32[32768]{0:T(1024)S(1)} fusion(f32[1,4,256,128]{3,2,1,0:T(8,128)S(1)} %broadcast_bitcast_fusion, f32[4,32768]{1,0:T(4,128)S(1)} %multiply_reduce_fusion, f32[1,4,256,128]{3,2,1,0:T(8,128)S(1)} %broadcast_bitcast_fusion.1), kind=kLoop, calls=%fused_computation.16 | loop fusion | flops 4947968 | bytes 1703936 | tf_op jit(solution)/shard_map/reduce_sum | solution.py:75
  183.5 0.1 bitcast_reduce_fusion.1
  183.7 0.6 fusion.1
  184.3 0.1 copy.18
  184.4 0.6 broadcast_multiply_fusion
  184.9 1.6 convert_multiply_fusion
  (53 shorter events, 0.7 us)
Async XLA Ops:
  66.5 18.0 %all-to-all-start.2 = ((bf16[4,8,256]{2,1,0:T(8,128)(2,1)}), bf16[4,8,256]{2,1,0:T(8,128)(2,1)S(1)}, u32[]{:S(2)}, u32[]{:S(2)}) async-start(bf16[4,8,256]{2,1,0:T(8,128)(2,1)} %get-tuple-element.4), calls=%async_computation.2 | async-start | bytes 32768 | tf_op jit(solution)/shard_map/all_to_all | solution.py:72
  84.5 29.3 %all-to-all-start = ((bf16[4,8,32768]{2,1,0:T(8,128)(2,1)}), bf16[4,8,32768]{2,1,0:T(8,128)(2,1)S(1)}, u32[]{:S(2)}, u32[]{:S(2)}) async-start(bf16[4,8,32768]{2,1,0:T(8,128)(2,1)} %multiply_convert_fusion), calls=%async_computation | async-start | bytes 4194304 | tf_op jit(solution)/shard_map/all_to_all | solution.py:71
  113.8 12.9 %all-to-all-start.3 = ((bf16[4,8,256]{2,0,1:T(4,128)(2,1)}), bf16[4,8,256]{2,0,1:T(4,128)(2,1)S(1)}, u32[]{:S(2)}, u32[]{:S(2)}) async-start(bf16[4,8,256]{2,0,1:T(4,128)(2,1)} %copy.14), calls=%async_computation.3 | async-start | bytes 32768 | tf_op jit(solution)/shard_map/all_to_all | solution.py:51
  126.7 50.4 %all-to-all-start.1 = ((bf16[4,8,32768]{2,0,1:T(4,128)(2,1)}), bf16[4,8,32768]{2,0,1:T(4,128)(2,1)S(1)}, u32[]{:S(2)}, u32[]{:S(2)}) async-start(bf16[4,8,32768]{2,0,1:T(4,128)(2,1)} %copy.13), calls=%async_computation.1 | async-start | bytes 4194304 | tf_op jit(solution)/shard_map/all_to_all | solution.py:50
where the time goes:
time: 187 us
  other arithmetic  70.1 us (37%)
  waiting for transfers between devices  67.2 us (36%)
  local copies, waits for them, and re-layouts  25.5 us (14%)
  starting transfers between devices  17.8 us (10%)
  matrix products  4.86 us (3%)
    unnamed x2, other arithmetic  44.7 us
    all_to_all x1, waiting for transfers between devices, local_section(): lax.all_to_all(coded, 'local', split_axis=1, concat_axis=1, tiled=True)  38.6 us
    all_to_all x1, waiting for transfers between devices, shards(): lax.all_to_all(coded, 'node', split_axis=0, concat_axis=0, tiled=True)  25.1 us
    convert_element_type x1, other arithmetic, encode(): coded = quantize(grouped / scaling[..., None]).astype(jnp.bfloat16)  8.63 us
    mul x2, local copies, waits for them, and re-layouts, decode(): values = grouped.astype(jnp.float32) * scales.astype(jnp.float32)[..., None]  8.23 us
    all_to_all x1, starting transfers between devices, local_section(): lax.all_to_all(scales, 'local', split_axis=1, concat_axis=1, tiled=True)  6.34 us
    another operation x1, local copies, waits for them, and re-layouts, encode(): values.reshape(values.shape[:-1] + (values.shape[-1] // QGROUP, QGROUP))  4.97 us
    abs x1, local copies, waits for them, and re-layouts, encode(): largest = jnp.max(jnp.abs(grouped), axis=-1)  4.7 us
  transfers between devices with their start and end apart: 4, of which 3 were waited for; matrix products, arithmetic and copies ran while one was open for 14% of the time, Pallas kernels for 0%

commit v1 on v0

v1 whole, which is shorter than its diff:
```python
import functools
import jax
import jax.numpy as jnp
from jax import lax
from jax.experimental import pallas as pl
from jax.experimental.pallas import tpu as pltpu
from jax.sharding import PartitionSpec as P

ROT = 256
QGROUP = 128
HALVES = ROT // QGROUP
LANES = 128
VMEM_LIMIT = 40 * 1024 * 1024


def sylvester():
    positions = jnp.arange(ROT, dtype=jnp.int32)
    parity = jnp.zeros((ROT, ROT), dtype=jnp.int32)
    for level in range(ROT.bit_length() - 1):
        column = positions >> level & 1
        parity = parity + column[:, None] * column[None, :]
    return (1 - 2 * (parity % 2)).astype(jnp.float32)


def leading_power(x):
    q = x * jnp.float32(2.0**23 + 1.0)
    return q - q * jnp.float32(1.0 - 2.0**-24)


def recode(values):
    columns = values.shape[1]
    magnitude = jnp.abs(values)
    grouped = magnitude.reshape(values.shape[0] // QGROUP, QGROUP, columns)
    largest = jnp.max(grouped, axis=1, keepdims=True)
    top = leading_power(jnp.clip(largest, 2.0**-30, 2.0**30))
    scale = top * jnp.float32(2.0**-7)
    least = scale * jnp.float32(2.0**-6)
    power = jnp.maximum(leading_power(grouped), least)
    shift = power * jnp.float32(2.0**20)
    nudged = grouped + power * jnp.float32(2.0**-4)
    nearest = (nudged + shift) - shift
    spacing = power * jnp.float32(2.0**-3)
    floored = jnp.where(nearest > nudged, nearest - spacing, nearest).reshape(values.shape)
    return jnp.where(values < 0.0, -floored, floored)


def rotate_kernel(sections, matrix_ref, *refs):
    value_refs = refs[:sections]
    sign_refs = refs[sections : 2 * sections]
    out_ref, turned = refs[2 * sections :]
    rows = sign_refs[0].shape[0]
    blocks = rows // HALVES
    for section in range(sections):
        values = value_refs[section][...].astype(jnp.float32).reshape(rows, LANES)
        turned[...] = jnp.where(sign_refs[section][...] == 0, values, -values)
        halves = [turned[pl.ds(half, blocks, stride=HALVES), :] for half in range(HALVES)]
        signed = jnp.concatenate(halves, axis=1).astype(jnp.bfloat16)
        rotated = lax.dot_general(
            matrix_ref[...], signed, (((1,), (1,)), ((), ())), preferred_element_type=jnp.float32
        )
        out_ref[0, :, section * blocks : (section + 1) * blocks] = recode(rotated).astype(jnp.bfloat16)


def rotate(values, signs, matrix, members, groups, first_section, sections):
    length = values.shape[1]
    portion = length // (members * groups)
    blocks = portion // ROT
    rows = portion // LANES

    def place(section, member):
        return (first_section + section) * members + member

    value_specs = [
        pl.BlockSpec((1, portion), functools.partial(lambda s, l: (0, place(s, l)), s)) for s in range(sections)
    ]
    sign_specs = [
        pl.BlockSpec((rows, LANES), functools.partial(lambda s, l: (place(s, l), 0), s)) for s in range(sections)
    ]
    count = sections * members * portion
    return pl.pallas_call(
        functools.partial(rotate_kernel, sections),
        grid=(members,),
        in_specs=[pl.BlockSpec((ROT, ROT), lambda l: (0, 0))] + value_specs + sign_specs,
        out_specs=pl.BlockSpec((1, ROT, sections * blocks), lambda l: (l, 0, 0)),
        out_shape=jax.ShapeDtypeStruct((members, ROT, sections * blocks), jnp.bfloat16),
        scratch_shapes=[pltpu.VMEM((rows, LANES), jnp.float32)],
        compiler_params=pltpu.CompilerParams(vmem_limit_bytes=VMEM_LIMIT),
        cost_estimate=pl.CostEstimate(flops=2 * count * ROT, bytes_accessed=10 * count, transcendentals=0),
        name="rotate_code",
    )(matrix, *([values] * sections), *([signs] * sections))


def group_sum_kernel(parts_ref, out_ref):
    total = parts_ref[0].astype(jnp.float32)
    for member in range(1, parts_ref.shape[0]):
        total = total + parts_ref[member].astype(jnp.float32)
    first = recode(total).astype(jnp.bfloat16)
    sections, _, blocks = out_ref.shape
    for section in range(sections):
        out_ref[section] = first[:, section * blocks : (section + 1) * blocks]


def group_sum(parts, sections):
    members, _, columns = parts.shape
    blocks = columns // sections
    together = sections if blocks % LANES else 1
    return pl.pallas_call(
        group_sum_kernel,
        grid=(sections // together,),
        in_specs=[pl.BlockSpec((members, ROT, together * blocks), lambda n: (0, 0, n))],
        out_specs=pl.BlockSpec((together, ROT, blocks), lambda n: (n, 0, 0)),
        out_shape=jax.ShapeDtypeStruct((sections, ROT, blocks), jnp.bfloat16),
        compiler_params=pltpu.CompilerParams(vmem_limit_bytes=VMEM_LIMIT),
        cost_estimate=pl.CostEstimate(
            flops=20 * sections * ROT * blocks, bytes_accessed=2 * parts.size, transcendentals=0
        ),
        name="group_sum_code",
    )(parts)


def finish_kernel(place_ref, matrix_ref, parts_ref, sign_ref, out_ref, max_ref):
    del place_ref
    second = parts_ref[0].astype(jnp.float32)
    for group in range(1, parts_ref.shape[0]):
        second = second + parts_ref[group].astype(jnp.float32)
    blocks = second.shape[1]
    natural = second.T
    block = lax.broadcasted_iota(jnp.int32, (blocks, HALVES * blocks), 0)
    lane = lax.broadcasted_iota(jnp.int32, (blocks, HALVES * blocks), 1)
    largest = jnp.zeros((1, HALVES * blocks), jnp.float32)
    for half in range(HALVES):
        peak = jnp.max(jnp.abs(natural[:, half * QGROUP : (half + 1) * QGROUP]), axis=1, keepdims=True)
        chosen = jnp.where(lane == HALVES * block + half, peak, 0.0)
        largest = jnp.maximum(largest, jnp.max(chosen, axis=0, keepdims=True))
    max_ref[...] = largest * jnp.float32(ROT**-0.5)
    turned = jnp.dot(
        natural, matrix_ref[...], precision=lax.Precision.HIGHEST, preferred_element_type=jnp.float32
    ) * jnp.float32(1.0 / ROT)
    for half in range(HALVES):
        at = pl.ds(half, blocks, stride=HALVES)
        part = turned[:, half * QGROUP : (half + 1) * QGROUP]
        out_ref[at, :] = jnp.where(sign_ref[at, :] == 0, part, -part)


def finish(parts, signs, matrix, place):
    groups, _, blocks = parts.shape
    rows = blocks * HALVES
    return pl.pallas_call(
        finish_kernel,
        grid_spec=pltpu.PrefetchScalarGridSpec(
            num_scalar_prefetch=1,
            grid=(1,),
            in_specs=[
                pl.BlockSpec((ROT, ROT), lambda i, p: (0, 0)),
                pl.BlockSpec((groups, ROT, blocks), lambda i, p: (0, 0, 0)),
                pl.BlockSpec((rows, LANES), lambda i, p: (p[0], 0)),
            ],
            out_specs=[
                pl.BlockSpec((rows, LANES), lambda i, p: (0, 0)),
                pl.BlockSpec((1, rows), lambda i, p: (0, 0)),
            ],
        ),
        out_shape=[
            jax.ShapeDtypeStruct((rows, LANES), jnp.float32),
            jax.ShapeDtypeStruct((1, rows), jnp.float32),
        ],
        compiler_params=pltpu.CompilerParams(vmem_limit_bytes=VMEM_LIMIT),
        name="sum_unrotate",
    )(place, matrix, parts, signs)


def shards(partials, signs):
    length = partials.shape[-1]
    members = lax.axis_size("local")
    groups = lax.axis_size("node")
    matrix = sylvester()
    values = partials.reshape(1, length)
    sign_rows = signs.reshape(length // LANES, LANES)
    coded = rotate(values, sign_rows, matrix.astype(jnp.bfloat16), members, groups, 0, groups)
    coded = lax.all_to_all(coded, "local", split_axis=0, concat_axis=0, tiled=True)
    first = group_sum(coded, groups)
    first = lax.all_to_all(first, "node", split_axis=0, concat_axis=0, tiled=True)
    place = (lax.axis_index("node") * members + lax.axis_index("local")).astype(jnp.int32).reshape(1)
    reduced, rotated_max = finish(first, sign_rows, matrix, place)
    return (reduced.reshape(-1), rotated_max.reshape(-1))


def solution(mesh):
    in_specs = (P("node", "local", None), P())
    out_specs = (P(("node", "local")), P(("node", "local")))
    return jax.shard_map(shards, mesh=mesh, in_specs=in_specs, out_specs=out_specs, check_vma=False)
```

time: 187 us -> 81.3 us (0.43)
  other arithmetic: 70.1 us -> 0.39 us
  waiting for transfers between devices: 67.2 us -> 6 us
  blocking collectives: 0 us -> 55.3 us
  local copies, waits for them, and re-layouts: 25.5 us -> 6.56 us
  starting transfers between devices: 17.8 us -> 3.4 us
  Pallas kernels: 0 us -> 8.59 us
  matrix products: 4.86 us -> 0 us
    all_to_all x4 -> x1, waiting for transfers between devices: 67.2 us -> 6 us  [shards(): lax.all_to_all(first, 'node', split_axis=0, concat_axis=0, tiled=True)]
    all_to_all x0 -> x1, blocking collectives: none -> 55.3 us  [shards(): lax.all_to_all(coded, 'local', split_axis=0, concat_axis=0, tiled=True)]
    unnamed x2 -> x0, other arithmetic: 44.7 us -> none
    all_to_all x4 -> x1, starting transfers between devices: 17.8 us -> 3.4 us  [shards(): lax.all_to_all(first, 'node', split_axis=0, concat_axis=0, tiled=True)]
    convert_element_type x3 -> x1, other arithmetic: 9.53 us -> 0.37 us  [shards(): matrix.astype(jnp.bfloat16)]
    pallas_call x0 -> x3, Pallas kernels: none -> 8.59 us  [the longest x1 5.58 us: rotate(): pl.pallas_call(functools.partial(rotate_kernel, sections), grid=(members,...]
    mul x2 -> x0, local copies, waits for them, and re-layouts: 8.23 us -> none  [decode(): values = grouped.astype(jnp.float32) * scales.astype(jnp.float32)[..., None]]
    unnamed x3 -> x6, local copies, waits for them, and re-layouts: 0.45 us -> 6.56 us
  transfers between devices with their start and end apart: 4 -> 1, of which waited for: 3 -> 1; matrix products, arithmetic and copies ran while one was open for 14% -> 0% of each run, Pallas kernels for 0% -> 0%
where the time goes in v1:
time: 81.3 us; the launch traced here: 80.9 us
  blocking collectives  55.3 us (68%)
  Pallas kernels  8.59 us (11%)
  local copies, waits for them, and re-layouts  6.56 us (8%)
  waiting for transfers between devices  6 us (7%)
  starting transfers between devices  3.4 us (4%)
    all_to_all x1, blocking collectives, shards(): lax.all_to_all(coded, 'local', split_axis=0, concat_axis=0, tiled=True)  55.3 us
    unnamed x6, local copies, waits for them, and re-layouts  6.56 us
    all_to_all x1, waiting for transfers between devices, shards(): lax.all_to_all(first, 'node', split_axis=0, concat_axis=0, tiled=True)  6 us
    pallas_call x1, Pallas kernels, rotate(): pl.pallas_call(functools.partial(rotate_kernel, sections), grid=(members,...  5.58 us
    all_to_all x1, starting transfers between devices, shards(): lax.all_to_all(first, 'node', split_axis=0, concat_axis=0, tiled=True)  3.4 us
    pallas_call x1, Pallas kernels, group_sum(): pl.pallas_call(group_sum_kernel, grid=(sections // together,), in_specs=[...  2.03 us
  transfers between devices with their start and end apart: 1, of which 1 were waited for; matrix products, arithmetic and copies ran while one was open for 0% of the time, Pallas kernels for 0%

profile of v1, /device:TPU:0, one launch (start us, length us, event | category | flops | bytes accessed | tf_op | source)
XLA Modules:
  0.0 80.9 jit_solution(3809883107369157238)
XLA Ops:
  0.7 0.4 fusion.4
  1.0 0.0 copy-start
  1.1 2.2 %copy-done = s32[1048576]{0:T(1024)S(1)} copy-done((s32[1048576]{0:T(1024)S(1)}, s32[1048576]{0:T(1024)}, u32[]{:S(2)}) %copy-start) | copy-done | bytes 4194328
  3.2 0.0 copy-start.2
  3.2 2.2 %copy-done.2 = bf16[1,1,1048576]{2,1,0:T(2,128)(2,1)S(1)} copy-done((bf16[1,1,1048576]{2,1,0:T(2,128)(2,1)S(1)}, bf16[1,1,1048576]{2,1,0:T(2,128)(2,1)}, u32[]{:S(2)}) %copy-start.2) | copy-done | bytes 2097176
  5.4 5.6 %rotate_code.1 = bf16[8,256,512]{2,1,0:T(8,128)(2,1)S(1)} custom-call(bf16[256,256]{1,0:T(8,128)(2,1)S(1)} %get-tuple-element.6.matrix_ref, bf16[1,1048576]{1,0:T(2,128)(2,1)S(1)} %bitcast.10, bf16[1,1048576]{1,0:T(2,128)(2,1)S(1)} %bitcast.11, bf16[1,1048576]{1,0:T(2,128)(2,1)S(1)} %bitcast.12, bf16[1,1048576]{1,0:T(2,128)(2,1)S(1)} %bitcast.13, ...), custom_call_target="tpu_custom_call" | custom-call | flops 536870912 | bytes 10485760 | tf_op jit(solution)/shard_map/rotate_code/pallas_call | solution.py:80
  11.0 55.3 %all_to_all.10.parts_ref = bf16[8,256,512]{2,1,0:T(8,128)(2,1)S(1)} all-to-all(bf16[8,256,512]{2,1,0:T(8,128)(2,1)S(1)} %rotate_code.1), channel_id=1, replica_groups=mesh['node'=4,'local'=8] {'local'}, dimensions={0} | all-to-all | bytes 4194304 | tf_op jit(solution)/shard_map/all_to_all | solution.py:180
  66.3 2.0 %group_sum_code.1 = bf16[4,256,128]{2,1,0:T(8,128)(2,1)} custom-call(bf16[8,256,512]{2,1,0:T(8,128)(2,1)S(1)} %all_to_all.10.parts_ref), custom_call_target="tpu_custom_call" | custom-call | flops 2621440 | bytes 2097152 | tf_op jit(solution)/shard_map/group_sum_code/pallas_call | solution.py:107
  68.4 3.4 %all-to-all-start.1 = ((bf16[4,256,128]{2,1,0:T(8,128)(2,1)}), bf16[4,256,128]{2,1,0:T(8,128)(2,1)S(1)}, u32[]{:S(2)}, u32[]{:S(2)}) async-start(bf16[4,256,128]{2,1,0:T(8,128)(2,1)} %group_sum_code.1), calls=%async_computation.1 | async-start | bytes 524288 | tf_op jit(solution)/shard_map/all_to_all | solution.py:182
  71.8 6.0 %all-to-all-done.1.parts_ref = bf16[4,256,128]{2,1,0:T(8,128)(2,1)S(1)} async-done(((bf16[4,256,128]{2,1,0:T(8,128)(2,1)}), bf16[4,256,128]{2,1,0:T(8,128)(2,1)S(1)}, u32[]{:S(2)}, u32[]{:S(2)}) %all-to-all-start.1) | async-done | bytes 262176 | tf_op jit(solution)/shard_map/all_to_all | solution.py:182
  77.8 0.0 copy-start.1
  77.8 2.2 %copy-done.1 = s32[1048576]{0:T(1024)S(1)} copy-done((s32[1048576]{0:T(1024)S(1)}, s32[1048576]{0:T(1024)}, u32[]{:S(2)}) %copy-start.1) | copy-done | bytes 4194328
  80.0 1.0 %sum_unrotate.1 = (f32[256,128]{1,0:T(8,128)}, f32[1,256]{1,0:T(1,128)}) custom-call(s32[1]{0:T(128)} %bitcast.place_ref, f32[256,256]{1,0:T(8,128)S(1)} %get-tuple-element.7.matrix_ref, bf16[4,256,128]{2,1,0:T(8,128)(2,1)S(1)} %all-to-all-done.1.parts_ref, s32[8192,128]{1,0:T(8,128)S(1)} %bitcast.9), custom_call_target="tpu_custom_call" | custom-call | tf_op jit(solution)/shard_map/sum_unrotate/pallas_call | solution.py:148
  (4 shorter events, 0.0 us)
Async XLA Ops:
  1.0 2.2 %copy-start = (s32[1048576]{0:T(1024)S(1)}, s32[1048576]{0:T(1024)}, u32[]{:S(2)}) copy-start(s32[1048576]{0:T(1024)} %param.3) | copy-start | bytes 12582916
  3.2 2.2 %copy-start.2 = (bf16[1,1,1048576]{2,1,0:T(2,128)(2,1)S(1)}, bf16[1,1,1048576]{2,1,0:T(2,128)(2,1)}, u32[]{:S(2)}) copy-start(bf16[1,1,1048576]{2,1,0:T(2,128)(2,1)} %param.2) | copy-start | bytes 6291460
  68.4 9.4 %all-to-all-start.1 = ((bf16[4,256,128]{2,1,0:T(8,128)(2,1)}), bf16[4,256,128]{2,1,0:T(8,128)(2,1)S(1)}, u32[]{:S(2)}, u32[]{:S(2)}) async-start(bf16[4,256,128]{2,1,0:T(8,128)(2,1)} %group_sum_code.1), calls=%async_computation.1 | async-start | bytes 524288 | tf_op jit(solution)/shard_map/all_to_all | solution.py:182
  77.8 2.2 %copy-start.1 = (s32[1048576]{0:T(1024)S(1)}, s32[1048576]{0:T(1024)}, u32[]{:S(2)}) copy-start(s32[1048576]{0:T(1024)} %param.3) | copy-start | bytes 12582916

commit v2 on v1

--- a/solution.py
+++ b/solution.py
@@ -1,6 +1,7 @@
 import functools
 import jax
 import jax.numpy as jnp
+import numpy as np
 from jax import lax
 from jax.experimental import pallas as pl
 from jax.experimental.pallas import tpu as pltpu
@@ -10,16 +11,15 @@
 QGROUP = 128
 HALVES = ROT // QGROUP
 LANES = 128
-VMEM_LIMIT = 40 * 1024 * 1024
+VMEM_LIMIT = 60 * 1024 * 1024
+SUM_VMEM_LIMIT = 24 * 1024 * 1024
 
 
 def sylvester():
-    positions = jnp.arange(ROT, dtype=jnp.int32)
-    parity = jnp.zeros((ROT, ROT), dtype=jnp.int32)
-    for level in range(ROT.bit_length() - 1):
-        column = positions >> level & 1
-        parity = parity + column[:, None] * column[None, :]
-    return (1 - 2 * (parity % 2)).astype(jnp.float32)
+    matrix = np.ones((1, 1), np.float32)
+    while matrix.shape[0] < ROT:
+        matrix = np.kron(np.array([[1, 1], [1, -1]], np.float32), matrix)
+    return matrix
 
 
 def leading_power(x):
@@ -44,7 +44,8 @@
     return jnp.where(values < 0.0, -floored, floored)
 
 
-def rotate_kernel(sections, matrix_ref, *refs):
+def rotate_kernel(sections, place_ref, matrix_ref, *refs):
+    del place_ref
     value_refs = refs[:sections]
     sign_refs = refs[sections : 2 * sections]
     out_ref, turned = refs[2 * sections :]
@@ -61,61 +62,90 @@
         out_ref[0, :, section * blocks : (section + 1) * blocks] = recode(rotated).astype(jnp.bfloat16)
 
 
-def rotate(values, signs, matrix, members, groups, first_section, sections):
+def rotate(values, signs, matrix, first_member, count, members, groups):
     length = values.shape[1]
     portion = length // (members * groups)
     blocks = portion // ROT
     rows = portion // LANES
 
-    def place(section, member):
-        return (first_section + section) * members + member
+    def place(section, member, first):
+        return section * members + first[0] + member
 
     value_specs = [
-        pl.BlockSpec((1, portion), functools.partial(lambda s, l: (0, place(s, l)), s)) for s in range(sections)
+        pl.BlockSpec((1, portion), functools.partial(lambda s, l, f: (0, place(s, l, f)), s)) for s in range(groups)
     ]
     sign_specs = [
-        pl.BlockSpec((rows, LANES), functools.partial(lambda s, l: (place(s, l), 0), s)) for s in range(sections)
+        pl.BlockSpec((rows, LANES), functools.partial(lambda s, l, f: (place(s, l, f), 0), s)) for s in range(groups)
     ]
-    count = sections * members * portion
-    return pl.pallas_call(
-        functools.partial(rotate_kernel, sections),
-        grid=(members,),
-        in_specs=[pl.BlockSpec((ROT, ROT), lambda l: (0, 0))] + value_specs + sign_specs,
-        out_specs=pl.BlockSpec((1, ROT, sections * blocks), lambda l: (l, 0, 0)),
-        out_shape=jax.ShapeDtypeStruct((members, ROT, sections * blocks), jnp.bfloat16),
-        scratch_shapes=[pltpu.VMEM((rows, LANES), jnp.float32)],
+    entries = groups * count * portion
+    return pl.pallas_call(
+        functools.partial(rotate_kernel, groups),
+        grid_spec=pltpu.PrefetchScalarGridSpec(
+            num_scalar_prefetch=1,
+            grid=(count,),
+            in_specs=[pl.BlockSpec((ROT, ROT), lambda l, f: (0, 0))] + value_specs + sign_specs,
+            out_specs=pl.BlockSpec((1, ROT, groups * blocks), lambda l, f: (l, 0, 0)),
+            scratch_shapes=[pltpu.VMEM((rows, LANES), jnp.float32)],
+        ),
+        out_shape=jax.ShapeDtypeStruct((count, ROT, groups * blocks), jnp.bfloat16),
         compiler_params=pltpu.CompilerParams(vmem_limit_bytes=VMEM_LIMIT),
-        cost_estimate=pl.CostEstimate(flops=2 * count * ROT, bytes_accessed=10 * count, transcendentals=0),
+        cost_estimate=pl.CostEstimate(flops=2 * entries * ROT, bytes_accessed=10 * entries, transcendentals=0),
         name="rotate_code",
-    )(matrix, *([values] * sections), *([signs] * sections))
-
-
-def group_sum_kernel(parts_ref, out_ref):
+    )(first_member, matrix, *([values] * groups), *([signs] * groups))
+
+
+def add_parts(parts_ref):
     total = parts_ref[0].astype(jnp.float32)
-    for member in range(1, parts_ref.shape[0]):
-        total = total + parts_ref[member].astype(jnp.float32)
-    first = recode(total).astype(jnp.bfloat16)
+    for part in range(1, parts_ref.shape[0]):
+        total = total + parts_ref[part].astype(jnp.float32)
+    return total
+
+
+def far_sum_kernel(parts_ref, out_ref):
+    out_ref[...] = add_parts(parts_ref)
+
+
+def far_sum(parts):
+    members, _, columns = parts.shape
+    tile = LANES if columns % LANES == 0 else columns
+    return pl.pallas_call(
+        far_sum_kernel,
+        grid=(columns // tile,),
+        in_specs=[pl.BlockSpec((members, ROT, tile), lambda n: (0, 0, n))],
+        out_specs=pl.BlockSpec((ROT, tile), lambda n: (0, n)),
+        out_shape=jax.ShapeDtypeStruct((ROT, columns), jnp.float32),
+        compiler_params=pltpu.CompilerParams(vmem_limit_bytes=SUM_VMEM_LIMIT),
+        cost_estimate=pl.CostEstimate(flops=2 * parts.size, bytes_accessed=3 * parts.size, transcendentals=0),
+        name="far_sum",
+    )(parts)
+
+
+def group_sum_kernel(parts_ref, far_ref, out_ref):
+    first = recode(add_parts(parts_ref) + far_ref[...]).astype(jnp.bfloat16)
     sections, _, blocks = out_ref.shape
     for section in range(sections):
         out_ref[section] = first[:, section * blocks : (section + 1) * blocks]
 
 
-def group_sum(parts, sections):
+def group_sum(parts, far, sections):
     members, _, columns = parts.shape
     blocks = columns // sections
     together = sections if blocks % LANES else 1
     return pl.pallas_call(
         group_sum_kernel,
         grid=(sections // together,),
-        in_specs=[pl.BlockSpec((members, ROT, together * blocks), lambda n: (0, 0, n))],
+        in_specs=[
+            pl.BlockSpec((members, ROT, together * blocks), lambda n: (0, 0, n)),
+            pl.BlockSpec((ROT, together * blocks), lambda n: (0, n)),
+        ],
         out_specs=pl.BlockSpec((together, ROT, blocks), lambda n: (n, 0, 0)),
         out_shape=jax.ShapeDtypeStruct((sections, ROT, blocks), jnp.bfloat16),
-        compiler_params=pltpu.CompilerParams(vmem_limit_bytes=VMEM_LIMIT),
+        compiler_params=pltpu.CompilerParams(vmem_limit_bytes=SUM_VMEM_LIMIT),
         cost_estimate=pl.CostEstimate(
-            flops=20 * sections * ROT * blocks, bytes_accessed=2 * parts.size, transcendentals=0
+            flops=20 * sections * ROT * blocks, bytes_accessed=3 * parts.size, transcendentals=0
         ),
         name="group_sum_code",
-    )(parts)
+    )(parts, far)
 
 
 def finish_kernel(place_ref, matrix_ref, parts_ref, sign_ref, out_ref, max_ref):
@@ -173,15 +203,28 @@
     length = partials.shape[-1]
     members = lax.axis_size("local")
     groups = lax.axis_size("node")
+    half = members // 2
     matrix = sylvester()
+    binary = jnp.asarray(matrix, jnp.bfloat16)
     values = partials.reshape(1, length)
     sign_rows = signs.reshape(length // LANES, LANES)
-    coded = rotate(values, sign_rows, matrix.astype(jnp.bfloat16), members, groups, 0, groups)
-    coded = lax.all_to_all(coded, "local", split_axis=0, concat_axis=0, tiled=True)
-    first = group_sum(coded, groups)
+    node = lax.axis_index("node").astype(jnp.int32)
+    member = lax.axis_index("local").astype(jnp.int32)
+    near_first = (member - lax.rem(member, half)).reshape(1)
+    far_first = half - near_first
+    sides = [list(range(half)), list(range(half, members))]
+
+    def exchange(parts):
+        return lax.all_to_all(parts, "local", split_axis=0, concat_axis=0, axis_index_groups=sides, tiled=True)
+
+    far = exchange(rotate(values, sign_rows, binary, far_first, half, members, groups))
+    near = exchange(rotate(values, sign_rows, binary, near_first, half, members, groups))
+    across = [(m, (m + half) % members) for m in range(members)]
+    far = lax.ppermute(far_sum(far), "local", across)
+    first = group_sum(near, far, groups)
     first = lax.all_to_all(first, "node", split_axis=0, concat_axis=0, tiled=True)
-    place = (lax.axis_index("node") * members + lax.axis_index("local")).astype(jnp.int32).reshape(1)
-    reduced, rotated_max = finish(first, sign_rows, matrix, place)
+    place = (node * members + member).reshape(1)
+    reduced, rotated_max = finish(first, sign_rows, jnp.asarray(matrix), place)
     return (reduced.reshape(-1), rotated_max.reshape(-1))
 
 

time: 81.3 us -> 68.3 us (0.84)
  blocking collectives: 55.3 us -> 0 us
  waiting for transfers between devices: 6 us -> 35.7 us
  starting transfers between devices: 3.4 us -> 14.8 us
  Pallas kernels: 8.59 us -> 15.9 us
  local copies, waits for them, and re-layouts: 6.56 us -> 0.69 us
    all_to_all x1 -> x0, blocking collectives: 55.3 us -> none  [shards(): lax.all_to_all(coded, 'local', split_axis=0, concat_axis=0, tiled=True)]
    all_to_all x0 -> x2, waiting for transfers between devices: none -> 29.7 us  [exchange(): lax.all_to_all(parts, 'local', split_axis=0, concat_axis=0, axis_index_gr...]
    all_to_all x0 -> x2, starting transfers between devices: none -> 8.76 us  [exchange(): lax.all_to_all(parts, 'local', split_axis=0, concat_axis=0, axis_index_gr...]
    pallas_call x1 -> x3, Pallas kernels: 5.58 us -> 12 us  [the longest x2 11.6 us: rotate(): pl.pallas_call(functools.partial(rotate_kernel, groups), grid_spec=pltpu....]
    unnamed x6 -> x2, local copies, waits for them, and re-layouts: 6.56 us -> 0.69 us
    ppermute x0 -> x1, starting transfers between devices: none -> 2.66 us  [shards(): far = lax.ppermute(far_sum(far), 'local', across)]
    pallas_call x1, Pallas kernels: 0.98 us -> 2.03 us  [finish(): pl.pallas_call(finish_kernel, grid_spec=pltpu.PrefetchScalarGridSpec(num_...]
  transfers between devices with their start and end apart: 1 -> 4, of which waited for: 1 -> 3; matrix products, arithmetic and copies ran while one was open for 0% -> 0% of each run, Pallas kernels for 0% -> 9%
where the time goes in v2:
time: 68.3 us; the launch traced here: 67.8 us
  waiting for transfers between devices  35.7 us (52%)
  Pallas kernels  15.9 us (23%)
  starting transfers between devices  14.8 us (22%)
  local copies, waits for them, and re-layouts  0.69 us (1%)
    all_to_all x2, waiting for transfers between devices, exchange(): lax.all_to_all(parts, 'local', split_axis=0, concat_axis=0, axis_index_gr...  29.7 us
    pallas_call x2, Pallas kernels, rotate(): pl.pallas_call(functools.partial(rotate_kernel, groups), grid_spec=pltpu....  11.6 us
    all_to_all x2, starting transfers between devices, exchange(): lax.all_to_all(parts, 'local', split_axis=0, concat_axis=0, axis_index_gr...  8.76 us
    all_to_all x1, waiting for transfers between devices, shards(): lax.all_to_all(first, 'node', split_axis=0, concat_axis=0, tiled=True)  5.99 us
    all_to_all x1, starting transfers between devices, shards(): lax.all_to_all(first, 'node', split_axis=0, concat_axis=0, tiled=True)  3.4 us
    ppermute x1, starting transfers between devices, shards(): far = lax.ppermute(far_sum(far), 'local', across)  2.66 us
    pallas_call x1, Pallas kernels, finish(): pl.pallas_call(finish_kernel, grid_spec=pltpu.PrefetchScalarGridSpec(num_...  2.03 us
    pallas_call x1, Pallas kernels, group_sum(): pl.pallas_call(group_sum_kernel, grid=(sections // together,), in_specs=[...  1.86 us
  transfers between devices with their start and end apart: 4, of which 3 were waited for; matrix products, arithmetic and copies ran while one was open for 0% of the time, Pallas kernels for 9%

profile of v2, /device:TPU:0, one launch (start us, length us, event | category | flops | bytes accessed | tf_op | source)
XLA Modules:
  0.0 67.8 jit_solution(10733306691015171173)
XLA Ops:
  0.6 5.8 %rotate_code.3 = bf16[4,256,512]{2,1,0:T(8,128)(2,1)} custom-call(s32[1]{0:T(128)S(6)} %sub.7.place_ref, bf16[256,256]{1,0:T(8,128)(2,1)} %constant.21.clone.matrix_ref, bf16[1,1048576]{1,0:T(2,128)(2,1)} %bitcast.15, bf16[1,1048576]{1,0:T(2,128)(2,1)} %bitcast.16, bf16[1,1048576]{1,0:T(2,128)(2,1)} %bitcast.17, bf16[1,1048576]{1,0:T(2,128)(2,1)} %bitcast.18, ...), custom_call_target="tpu_custom_call" | custom-call | flops 268435456 | bytes 5242880 | tf_op jit(solution)/shard_map/rotate_code/pallas_call | solution.py:81
  6.5 5.2 %all-to-all-start.1 = ((bf16[4,256,512]{2,1,0:T(8,128)(2,1)}), bf16[4,256,512]{2,1,0:T(8,128)(2,1)S(1)}, u32[]{:S(2)}, u32[]{:S(2)}) async-start(bf16[4,256,512]{2,1,0:T(8,128)(2,1)} %rotate_code.3), calls=%async_computation.1 | async-start | bytes 2097152 | tf_op jit(solution)/shard_map/all_to_all | solution.py:218
  11.7 5.8 %rotate_code.2 = bf16[4,256,512]{2,1,0:T(8,128)(2,1)} custom-call(s32[1]{0:T(128)} %bitcast.1.place_ref, bf16[256,256]{1,0:T(8,128)(2,1)} %constant.21.clone.matrix_ref, bf16[1,1048576]{1,0:T(2,128)(2,1)} %bitcast.19, bf16[1,1048576]{1,0:T(2,128)(2,1)} %bitcast.20, bf16[1,1048576]{1,0:T(2,128)(2,1)} %bitcast.21, bf16[1,1048576]{1,0:T(2,128)(2,1)} %bitcast.22, ...), custom_call_target="tpu_custom_call" | custom-call | flops 268435456 | bytes 5242880 | tf_op jit(solution)/shard_map/rotate_code/pallas_call | solution.py:81
  17.5 7.8 %all-to-all-done.1.parts_ref = bf16[4,256,512]{2,1,0:T(8,128)(2,1)S(1)} async-done(((bf16[4,256,512]{2,1,0:T(8,128)(2,1)}), bf16[4,256,512]{2,1,0:T(8,128)(2,1)S(1)}, u32[]{:S(2)}, u32[]{:S(2)}) %all-to-all-start.1) | async-done | bytes 1048608 | tf_op jit(solution)/shard_map/all_to_all | solution.py:218
  25.3 3.5 %all-to-all-start = ((bf16[4,256,512]{2,1,0:T(8,128)(2,1)}), bf16[4,256,512]{2,1,0:T(8,128)(2,1)S(1)}, u32[]{:S(2)}, u32[]{:S(2)}) async-start(bf16[4,256,512]{2,1,0:T(8,128)(2,1)} %rotate_code.2), calls=%async_computation | async-start | bytes 2097152 | tf_op jit(solution)/shard_map/all_to_all | solution.py:218
  28.9 0.4 far_sum.1
  29.3 2.7 %collective-permute-start = (f32[256,512]{1,0:T(8,128)S(1)}, f32[256,512]{1,0:T(8,128)S(1)}, u32[]{:S(2)}, u32[]{:S(2)}) collective-permute-start(f32[256,512]{1,0:T(8,128)S(1)} %far_sum.1), channel_id=1, source_target_pairs={{0,4},{1,5},{2,6},{3,7},{4,0},{5,1},{6,2},{7,3},{8,12},{9,13},{10,... | collective-permute-start | bytes 1572872 | tf_op jit(solution)/shard_map/ppermute | solution.py:223
  32.0 21.8 %all-to-all-done.parts_ref = bf16[4,256,512]{2,1,0:T(8,128)(2,1)S(1)} async-done(((bf16[4,256,512]{2,1,0:T(8,128)(2,1)}), bf16[4,256,512]{2,1,0:T(8,128)(2,1)S(1)}, u32[]{:S(2)}, u32[]{:S(2)}) %all-to-all-start) | async-done | bytes 1048608 | tf_op jit(solution)/shard_map/all_to_all | solution.py:218
  53.8 0.0 collective-permute-done.far_ref
  53.8 1.9 %group_sum_code.1 = bf16[4,256,128]{2,1,0:T(8,128)(2,1)} custom-call(bf16[4,256,512]{2,1,0:T(8,128)(2,1)S(1)} %all-to-all-done.parts_ref, f32[256,512]{1,0:T(8,128)S(1)} %collective-permute-done.far_ref), custom_call_target="tpu_custom_call" | custom-call | flops 2621440 | bytes 1572864 | tf_op jit(solution)/shard_map/group_sum_code/pallas_call | solution.py:134
  55.7 3.4 %all-to-all-start.2 = ((bf16[4,256,128]{2,1,0:T(8,128)(2,1)}), bf16[4,256,128]{2,1,0:T(8,128)(2,1)S(1)}, u32[]{:S(2)}, u32[]{:S(2)}) async-start(bf16[4,256,128]{2,1,0:T(8,128)(2,1)} %group_sum_code.1), calls=%async_computation.2 | async-start | bytes 524288 | tf_op jit(solution)/shard_map/all_to_all | solution.py:225
  59.1 6.0 %all-to-all-done.2.parts_ref = bf16[4,256,128]{2,1,0:T(8,128)(2,1)S(1)} async-done(((bf16[4,256,128]{2,1,0:T(8,128)(2,1)}), bf16[4,256,128]{2,1,0:T(8,128)(2,1)S(1)}, u32[]{:S(2)}, u32[]{:S(2)}) %all-to-all-start.2) | async-done | bytes 262176 | tf_op jit(solution)/shard_map/all_to_all | solution.py:225
  65.1 0.0 copy-start
  65.1 0.7 %copy-done = bf16[4,256,128]{2,1,0:T(8,128)(2,1)} copy-done((bf16[4,256,128]{2,1,0:T(8,128)(2,1)}, bf16[4,256,128]{2,1,0:T(8,128)(2,1)S(1)}, u32[]{:S(2)}) %copy-start) | copy-done | bytes 262168
  65.8 2.0 %sum_unrotate.1 = (f32[256,128]{1,0:T(8,128)}, f32[1,256]{1,0:T(1,128)}) custom-call(s32[1]{0:T(128)} %bitcast.place_ref, f32[256,256]{1,0:T(8,128)} %constant.22.clone.matrix_ref, bf16[4,256,128]{2,1,0:T(8,128)(2,1)} %copy-done, s32[8192,128]{1,0:T(8,128)} %bitcast.14), custom_call_target="tpu_custom_call" | custom-call | tf_op jit(solution)/shard_map/sum_unrotate/pallas_call | solution.py:178
Async XLA Ops:
  6.5 18.9 %all-to-all-start.1 = ((bf16[4,256,512]{2,1,0:T(8,128)(2,1)}), bf16[4,256,512]{2,1,0:T(8,128)(2,1)S(1)}, u32[]{:S(2)}, u32[]{:S(2)}) async-start(bf16[4,256,512]{2,1,0:T(8,128)(2,1)} %rotate_code.3), calls=%async_computation.1 | async-start | bytes 2097152 | tf_op jit(solution)/shard_map/all_to_all | solution.py:218
  25.3 28.5 %all-to-all-start = ((bf16[4,256,512]{2,1,0:T(8,128)(2,1)}), bf16[4,256,512]{2,1,0:T(8,128)(2,1)S(1)}, u32[]{:S(2)}, u32[]{:S(2)}) async-start(bf16[4,256,512]{2,1,0:T(8,128)(2,1)} %rotate_code.2), calls=%async_computation | async-start | bytes 2097152 | tf_op jit(solution)/shard_map/all_to_all | solution.py:218
  29.3 24.5 %collective-permute-start = (f32[256,512]{1,0:T(8,128)S(1)}, f32[256,512]{1,0:T(8,128)S(1)}, u32[]{:S(2)}, u32[]{:S(2)}) collective-permute-start(f32[256,512]{1,0:T(8,128)S(1)} %far_sum.1), channel_id=1, source_target_pairs={{0,4},{1,5},{2,6},{3,7},{4,0},{5,1},{6,2},{7,3},{8,12},{9,13},{10,... | collective-permute-start | bytes 1572872 | tf_op jit(solution)/shard_map/ppermute | solution.py:223
  55.7 9.4 %all-to-all-start.2 = ((bf16[4,256,128]{2,1,0:T(8,128)(2,1)}), bf16[4,256,128]{2,1,0:T(8,128)(2,1)S(1)}, u32[]{:S(2)}, u32[]{:S(2)}) async-start(bf16[4,256,128]{2,1,0:T(8,128)(2,1)} %group_sum_code.1), calls=%async_computation.2 | async-start | bytes 524288 | tf_op jit(solution)/shard_map/all_to_all | solution.py:225
  65.1 0.7 %copy-start = (bf16[4,256,128]{2,1,0:T(8,128)(2,1)}, bf16[4,256,128]{2,1,0:T(8,128)(2,1)S(1)}, u32[]{:S(2)}) copy-start(bf16[4,256,128]{2,1,0:T(8,128)(2,1)S(1)} %all-to-all-done.2.parts_ref) | copy-start | bytes 786436

commit v3 on v2

v3 whole, which is shorter than its diff:
```python
import functools
import jax
import jax.numpy as jnp
import numpy as np
from jax import lax
from jax.experimental import pallas as pl
from jax.experimental.pallas import tpu as pltpu
from jax.sharding import PartitionSpec as P

ROT = 256
QGROUP = 128
HALVES = ROT // QGROUP
LANES = 128
VMEM_LIMIT = 60 * 1024 * 1024
SUM_VMEM_LIMIT = 24 * 1024 * 1024


def sylvester():
    matrix = np.ones((1, 1), np.float32)
    while matrix.shape[0] < ROT:
        matrix = np.kron(np.array([[1, 1], [1, -1]], np.float32), matrix)
    return matrix


def partner(index, step, count):
    if count & (count - 1) == 0:
        return index ^ step
    return (index + step) % count


def leading_power(x):
    q = x * jnp.float32(2.0**23 + 1.0)
    return q - q * jnp.float32(1.0 - 2.0**-24)


def recode(values):
    magnitude = jnp.abs(values)
    largest = jnp.max(magnitude, axis=0, keepdims=True)
    scale = leading_power(jnp.clip(largest, 2.0**-30, 2.0**30)) * jnp.float32(2.0**-7)
    least = scale * jnp.float32(2.0**-6)
    power = jnp.maximum(leading_power(magnitude), least)
    shift = power * jnp.float32(2.0**20)
    nudged = magnitude + power * jnp.float32(2.0**-4)
    nearest = (nudged + shift) - shift
    spacing = power * jnp.float32(2.0**-3)
    floored = jnp.where(nearest > nudged, nearest - spacing, nearest)
    return jnp.where(values < 0.0, -floored, floored)


def rotate_kernel(sections, place_ref, matrix_ref, *refs):
    del place_ref
    value_refs = refs[:sections]
    sign_refs = refs[sections : 2 * sections]
    out_refs = refs[2 * sections : -1]
    turned = refs[-1]
    rows = sign_refs[0].shape[0]
    blocks = rows // HALVES
    for section in range(sections):
        values = value_refs[section][...].astype(jnp.float32).reshape(rows, LANES)
        turned[...] = jnp.where(sign_refs[section][...] == 0, values, -values)
        halves = [turned[pl.ds(half, blocks, stride=HALVES), :] for half in range(HALVES)]
        signed = jnp.concatenate(halves, axis=1).astype(jnp.bfloat16)
        rotated = lax.dot_general(
            matrix_ref[...], signed, (((1,), (1,)), ((), ())), preferred_element_type=jnp.float32
        )
        columns = slice(section * blocks, (section + 1) * blocks)
        for half in range(HALVES):
            coded = recode(rotated[half * QGROUP : (half + 1) * QGROUP]).astype(jnp.bfloat16)
            if len(out_refs) == 1:
                out_refs[0][half * QGROUP : (half + 1) * QGROUP, columns] = coded
            else:
                out_refs[half][:, columns] = coded


def rotate(values, signs, matrix, place, other, step, members, groups, split):
    length = values.shape[1]
    portion = length // (members * groups)
    blocks = portion // ROT
    rows = portion // LANES
    half = members // 2

    def position(section, at):
        first = half - at[1] if other else at[1]
        return partner(at[0], section, groups) * members + first + partner(at[2], step, half)

    value_specs = [
        pl.BlockSpec((1, portion), functools.partial(lambda s, i, at: (0, position(s, at)), s)) for s in range(groups)
    ]
    sign_specs = [
        pl.BlockSpec((rows, LANES), functools.partial(lambda s, i, at: (position(s, at), 0), s)) for s in range(groups)
    ]
    entries = groups * portion
    shape = (QGROUP if split else ROT, groups * blocks)
    outs = HALVES if split else 1
    return pl.pallas_call(
        functools.partial(rotate_kernel, groups),
        grid_spec=pltpu.PrefetchScalarGridSpec(
            num_scalar_prefetch=1,
            grid=(1,),
            in_specs=[pl.BlockSpec((ROT, ROT), lambda i, at: (0, 0))] + value_specs + sign_specs,
            out_specs=[pl.BlockSpec(shape, lambda i, at: (0, 0))] * outs,
            scratch_shapes=[pltpu.VMEM((rows, LANES), jnp.float32)],
        ),
        out_shape=[jax.ShapeDtypeStruct(shape, jnp.bfloat16)] * outs,
        compiler_params=pltpu.CompilerParams(vmem_limit_bytes=VMEM_LIMIT),
        cost_estimate=pl.CostEstimate(flops=2 * entries * ROT, bytes_accessed=10 * entries, transcendentals=0),
        name="rotate_code",
    )(place, matrix, *([values] * groups), *([signs] * groups))


def add_all(refs):
    total = refs[0][...].astype(jnp.float32)
    for ref in refs[1:]:
        total = total + ref[...].astype(jnp.float32)
    return total


def far_sum_kernel(*refs):
    refs[-1][...] = add_all(refs[:-1])


def far_sum(parts):
    shape = parts[0].shape
    size = shape[0] * shape[1]
    return pl.pallas_call(
        far_sum_kernel,
        out_shape=jax.ShapeDtypeStruct(shape, jnp.float32),
        compiler_params=pltpu.CompilerParams(vmem_limit_bytes=SUM_VMEM_LIMIT),
        cost_estimate=pl.CostEstimate(
            flops=2 * len(parts) * size, bytes_accessed=(2 * len(parts) + 4) * size, transcendentals=0
        ),
        name="far_sum",
    )(*parts)


def group_sum_kernel(parts, *refs):
    first = recode(add_all(refs[:parts])).astype(jnp.bfloat16)
    blocks = refs[parts].shape[1]
    for section, out_ref in enumerate(refs[parts:]):
        out_ref[...] = first[:, section * blocks : (section + 1) * blocks]


def group_sum(near, far, half, groups):
    columns = near[0].shape[1]
    blocks = columns // groups
    size = QGROUP * columns
    count = len(near) + len(far)
    return pl.pallas_call(
        functools.partial(group_sum_kernel, count),
        grid=(1,),
        in_specs=[pl.BlockSpec((QGROUP, columns), lambda i: (half, 0))] * len(near)
        + [pl.BlockSpec((QGROUP, columns), lambda i: (0, 0))] * len(far),
        out_specs=[pl.BlockSpec((QGROUP, blocks), lambda i: (0, 0))] * groups,
        out_shape=[jax.ShapeDtypeStruct((QGROUP, blocks), jnp.bfloat16)] * groups,
        compiler_params=pltpu.CompilerParams(vmem_limit_bytes=SUM_VMEM_LIMIT),
        cost_estimate=pl.CostEstimate(flops=20 * size, bytes_accessed=2 * (count + 1) * size, transcendentals=0),
        name="group_sum_code",
    )(*near, *far)


def bfloat16_terms(values):
    terms = []
    for _ in range(3):
        terms.append(values.astype(jnp.bfloat16))
        values = values - terms[-1].astype(jnp.float32)
    return terms


def finish_kernel(groups, matrix_ref, sign_ref, *refs):
    out_ref, max_ref = refs[-2:]
    second = [add_all(refs[half * groups : (half + 1) * groups]) for half in range(HALVES)]
    blocks = second[0].shape[1]
    natural = jnp.concatenate([part.T for part in second], axis=1)
    block = lax.broadcasted_iota(jnp.int32, (blocks, HALVES * blocks), 0)
    lane = lax.broadcasted_iota(jnp.int32, (blocks, HALVES * blocks), 1)
    largest = jnp.zeros((1, HALVES * blocks), jnp.float32)
    for half in range(HALVES):
        peak = jnp.max(jnp.abs(natural[:, half * QGROUP : (half + 1) * QGROUP]), axis=1, keepdims=True)
        chosen = jnp.where(lane == HALVES * block + half, peak, 0.0)
        largest = jnp.maximum(largest, jnp.max(chosen, axis=0, keepdims=True))
    max_ref[...] = largest * jnp.float32(ROT**-0.5)
    high, middle, low = [
        jnp.dot(term, matrix_ref[...], preferred_element_type=jnp.float32) for term in bfloat16_terms(natural)
    ]
    turned = (high + (middle + low)) * jnp.float32(1.0 / ROT)
    for half in range(HALVES):
        at = pl.ds(half, blocks, stride=HALVES)
        part = turned[:, half * QGROUP : (half + 1) * QGROUP]
        out_ref[at, :] = jnp.where(sign_ref[at, :] == 0, part, -part)


def finish(parts, signs, matrix):
    groups = len(parts[0])
    rows = signs.shape[0]
    return pl.pallas_call(
        functools.partial(finish_kernel, groups),
        out_shape=[
            jax.ShapeDtypeStruct((rows, LANES), jnp.float32),
            jax.ShapeDtypeStruct((1, rows), jnp.float32),
        ],
        compiler_params=pltpu.CompilerParams(vmem_limit_bytes=SUM_VMEM_LIMIT),
        name="sum_unrotate",
    )(matrix, signs, *[part for half in parts for part in half])


def shards(partials, signs):
    length = partials.shape[-1]
    members = lax.axis_size("local")
    groups = lax.axis_size("node")
    half = members // 2
    binary = jnp.asarray(sylvester(), jnp.bfloat16)
    values = partials.reshape(1, length)
    sign_rows = signs.reshape(length // LANES, LANES)
    node = lax.axis_index("node").astype(jnp.int32)
    member = lax.axis_index("local").astype(jnp.int32)
    inner = lax.rem(member, half)
    place = jnp.stack([node, member - inner, inner])
    own_rows = sign_rows.shape[0] // (members * groups)
    own_signs = lax.dynamic_slice_in_dim(sign_rows, (node * members + member) * own_rows, own_rows)

    def turn(other, step, split):
        return rotate(values, sign_rows, binary, place, other, step, members, groups, split)

    def send(part, other, step):
        pairs = []
        for source in range(members):
            first, index = source // half * half, source % half
            pairs.append((source, (half - first if other else first) + partner(index, step, half)))
        return lax.ppermute(part, "local", pairs)

    def share(parts):
        moved = [parts[0]]
        for step in range(1, groups):
            pairs = [(source, partner(source, step, groups)) for source in range(groups)]
            moved.append(lax.ppermute(parts[step], "node", pairs))
        return moved

    summed, direct, near = [], [], []
    for step in list(range(1, half)) + [0]:
        for_sum, for_owner = turn(True, step, True)
        summed.append(send(for_sum, False, step) if step else for_sum)
        direct.append(send(for_owner, True, step))
    for step in list(range(1, half)) + [0]:
        (part,) = turn(False, step, False)
        near.append(send(part, False, step) if step else part)
    across = send(far_sum(summed), True, 0)
    second_half = share(group_sum(near, direct, 1, groups))
    first_half = share(group_sum(near, [across], 0, groups))
    reduced, rotated_max = finish([first_half, second_half], own_signs, binary)
    return (reduced.reshape(-1), rotated_max.reshape(-1))


def solution(mesh):
    in_specs = (P("node", "local", None), P())
    out_specs = (P(("node", "local")), P(("node", "local")))
    return jax.shard_map(shards, mesh=mesh, in_specs=in_specs, out_specs=out_specs, check_vma=False)
```

time: 68.3 us -> 71 us (1.040)
  waiting for transfers between devices: 35.7 us -> 14.1 us
  Pallas kernels: 15.9 us -> 28.5 us
  starting transfers between devices: 14.8 us -> 22.7 us
  local copies, waits for them, and re-layouts: 0.69 us -> 3.74 us
    all_to_all x3 -> x0, waiting for transfers between devices: 35.7 us -> none  [the longest x2 29.7 us: exchange(): lax.all_to_all(parts, 'local', split_axis=0, concat_axis=0, axis_index_gr...]
    ppermute x1 -> x17, starting transfers between devices: 2.66 us -> 22.7 us  [the longest x11 18.8 us: send(): return lax.ppermute(part, 'local', pairs)]
    pallas_call x2 -> x8, Pallas kernels: 11.6 us -> 27 us  [rotate(): pl.pallas_call(functools.partial(rotate_kernel, groups), grid_spec=pltpu....]
    ppermute x1 -> x17, waiting for transfers between devices: 0.01 us -> 14.1 us  [the longest x11 11.4 us: send(): return lax.ppermute(part, 'local', pairs)]
    all_to_all x3 -> x0, starting transfers between devices: 12.2 us -> none  [the longest x2 8.76 us: exchange(): lax.all_to_all(parts, 'local', split_axis=0, concat_axis=0, axis_index_gr...]
    pallas_call x3 -> x4, Pallas kernels: 4.32 us -> 1.56 us  [the longest x1 0.93 us: finish(): pl.pallas_call(functools.partial(finish_kernel, groups), out_shape=[jax.S...]
    unnamed x2 -> x18, local copies, waits for them, and re-layouts: 0.69 us -> 2.82 us
    dynamic_slice x0 -> x1, local copies, waits for them, and re-layouts: none -> 0.91 us  [shards(): lax.dynamic_slice_in_dim(sign_rows, (node * members + member) * own_rows,...]
  transfers between devices with their start and end apart: 4 -> 17, of which waited for: 3 -> 3; matrix products, arithmetic and copies ran while one was open for 0% -> 1% of each run, Pallas kernels for 9% -> 34%
where the time goes in v3:
time: 71 us; the launch traced here: 70.4 us
  Pallas kernels  28.5 us (40%)
  starting transfers between devices  22.7 us (32%)
  waiting for transfers between devices  14.1 us (20%)
  local copies, waits for them, and re-layouts  3.74 us (5%)
  between operations  0.77 us (1%)
    pallas_call x8, Pallas kernels, rotate(): pl.pallas_call(functools.partial(rotate_kernel, groups), grid_spec=pltpu....  27 us
    ppermute x11, starting transfers between devices, send(): return lax.ppermute(part, 'local', pairs)  18.8 us
    ppermute x11, waiting for transfers between devices, send(): return lax.ppermute(part, 'local', pairs)  11.4 us
    ppermute x6, starting transfers between devices, share(): moved.append(lax.ppermute(parts[step], 'node', pairs))  3.86 us
    unnamed x18, local copies, waits for them, and re-layouts  2.82 us
    ppermute x6, waiting for transfers between devices, share(): moved.append(lax.ppermute(parts[step], 'node', pairs))  2.66 us
  transfers between devices with their start and end apart: 17, of which 3 were waited for; matrix products, arithmetic and copies ran while one was open for 1% of the time, Pallas kernels for 34%

profile of v3, /device:TPU:0, one launch (start us, length us, event | category | flops | bytes accessed | tf_op | source)
XLA Modules:
  0.0 70.4 jit_solution(1946232367618551498)
XLA Ops:
  0.6 0.7 pad_add_fusion.place_ref
  1.3 3.3 %rotate_code.12 = (bf16[128,512]{1,0:T(8,128)(2,1)}, bf16[128,512]{1,0:T(8,128)(2,1)}) custom-call(s32[3]{0:T(128)} %pad_add_fusion.place_ref, bf16[256,256]{1,0:T(8,128)(2,1)} %constant.22.clone.matrix_ref, bf16[1,1048576]{1,0:T(2,128)(2,1)} %bitcast.40, bf16[1,1048576]{1,0:T(2,128)(2,1)} %bitcast.41, bf16[1,1048576]{1,0:T(2,128)(2,1)} %bitcast.42, ...), custom_call_target="tpu_custom_call" | custom-call | flops 67108864 | bytes 1310720 | tf_op jit(solution)/shard_map/rotate_code/pallas_call | solution.py:95
  4.6 3.0 %collective-permute-start.3 = (bf16[128,512]{1,0:T(8,128)(2,1)}, bf16[128,512]{1,0:T(8,128)(2,1)S(1)}, u32[]{:S(2)}, u32[]{:S(2)}) collective-permute-start(bf16[128,512]{1,0:T(8,128)(2,1)} %get-tuple-element.20), channel_id=1, source_target_pairs={{0,1},{1,0},{2,3},{3,2},{4,5},{5,4},{6,7},{7,6},{8,9},{9,8},{10,11... | collective-permute-start | bytes 393224 | tf_op jit(solution)/shard_map/ppermute | solution.py:229
  7.6 3.3 %rotate_code.13 = (bf16[128,512]{1,0:T(8,128)(2,1)}, bf16[128,512]{1,0:T(8,128)(2,1)}) custom-call(s32[3]{0:T(128)} %pad_add_fusion.place_ref, bf16[256,256]{1,0:T(8,128)(2,1)} %constant.22.clone.matrix_ref, bf16[1,1048576]{1,0:T(2,128)(2,1)} %bitcast.44, bf16[1,1048576]{1,0:T(2,128)(2,1)} %bitcast.45, bf16[1,1048576]{1,0:T(2,128)(2,1)} %bitcast.46, ...), custom_call_target="tpu_custom_call" | custom-call | flops 67108864 | bytes 1310720 | tf_op jit(solution)/shard_map/rotate_code/pallas_call | solution.py:95
  10.9 0.0 copy-start.8
  10.9 0.0 copy-start.7
  10.9 1.6 %collective-permute-start.4 = (bf16[128,512]{1,0:T(8,128)(2,1)}, bf16[128,512]{1,0:T(8,128)(2,1)S(1)}, u32[]{:S(2)}, u32[]{:S(2)}) collective-permute-start(bf16[128,512]{1,0:T(8,128)(2,1)} %get-tuple-element.21), channel_id=1, source_target_pairs={{0,2},{1,3},{2,0},{3,1},{4,6},{5,7},{6,4},{7,5},{8,10},{9,11},{10,... | collective-permute-start | bytes 393224 | tf_op jit(solution)/shard_map/ppermute | solution.py:229
  12.5 3.3 %rotate_code.14 = (bf16[128,512]{1,0:T(8,128)(2,1)}, bf16[128,512]{1,0:T(8,128)(2,1)}) custom-call(s32[3]{0:T(128)} %pad_add_fusion.place_ref, bf16[256,256]{1,0:T(8,128)(2,1)} %constant.22.clone.matrix_ref, bf16[1,1048576]{1,0:T(2,128)(2,1)} %bitcast.48, bf16[1,1048576]{1,0:T(2,128)(2,1)} %bitcast.49, bf16[1,1048576]{1,0:T(2,128)(2,1)} %bitcast.50, ...), custom_call_target="tpu_custom_call" | custom-call | flops 67108864 | bytes 1310720 | tf_op jit(solution)/shard_map/rotate_code/pallas_call | solution.py:95
  15.9 0.1 collective-permute-start.5
  16.0 0.0 copy-done.8
  16.0 3.8 %collective-permute-start.10 = (bf16[128,512]{1,0:T(8,128)(2,1)S(1)}, bf16[128,512]{1,0:T(8,128)(2,1)S(1)}, u32[]{:S(2)}, u32[]{:S(2)}) collective-permute-start(bf16[128,512]{1,0:T(8,128)(2,1)S(1)} %copy-done.8), channel_id=1, source_target_pairs={{0,5},{1,4},{2,7},{3,6},{4,1},{5,0},{6,3},{7,2},{8,13},{9,12},{10,... | collective-permute-start | bytes 393224 | tf_op jit(solution)/shard_map/ppermute | solution.py:229
  19.8 0.0 copy-done.7
  19.8 1.4 %collective-permute-start.11 = (bf16[128,512]{1,0:T(8,128)(2,1)S(1)}, bf16[128,512]{1,0:T(8,128)(2,1)S(1)}, u32[]{:S(2)}, u32[]{:S(2)}) collective-permute-start(bf16[128,512]{1,0:T(8,128)(2,1)S(1)} %copy-done.7), channel_id=1, source_target_pairs={{0,6},{1,7},{2,4},{3,5},{4,2},{5,3},{6,0},{7,1},{8,14},{9,15},{10,... | collective-permute-start | bytes 393224 | tf_op jit(solution)/shard_map/ppermute | solution.py:229
  21.2 3.4 %rotate_code.8 = bf16[256,512]{1,0:T(8,128)(2,1)} custom-call(s32[3]{0:T(128)} %pad_add_fusion.place_ref, bf16[256,256]{1,0:T(8,128)(2,1)} %constant.22.clone.matrix_ref, bf16[1,1048576]{1,0:T(2,128)(2,1)} %bitcast.55, bf16[1,1048576]{1,0:T(2,128)(2,1)} %bitcast.53, bf16[1,1048576]{1,0:T(2,128)(2,1)} %bitcast.54, bf16[1,1048576]{1,0:T(2,128)(2,1)} %bitcast.52, ...), custom_call_target="tpu_custom_call" | custom-call | flops 67108864 | bytes 1310720 | tf_op jit(solution)/shard_map/rotate_code/pallas_call | solution.py:95
  24.6 3.4 %rotate_code.9 = bf16[256,512]{1,0:T(8,128)(2,1)} custom-call(s32[3]{0:T(128)} %pad_add_fusion.place_ref, bf16[256,256]{1,0:T(8,128)(2,1)} %constant.22.clone.matrix_ref, bf16[1,1048576]{1,0:T(2,128)(2,1)} %bitcast.56, bf16[1,1048576]{1,0:T(2,128)(2,1)} %bitcast.57, bf16[1,1048576]{1,0:T(2,128)(2,1)} %bitcast.58, bf16[1,1048576]{1,0:T(2,128)(2,1)} %bitcast.59, ...), custom_call_target="tpu_custom_call" | custom-call | flops 67108864 | bytes 1310720 | tf_op jit(solution)/shard_map/rotate_code/pallas_call | solution.py:95
  27.9 0.0 copy-start.6
  27.9 0.0 copy-start.5
  27.9 0.0 copy-start.4
  27.9 3.5 %rotate_code.10 = bf16[256,512]{1,0:T(8,128)(2,1)} custom-call(s32[3]{0:T(128)} %pad_add_fusion.place_ref, bf16[256,256]{1,0:T(8,128)(2,1)} %constant.22.clone.matrix_ref, bf16[1,1048576]{1,0:T(2,128)(2,1)} %bitcast.60, bf16[1,1048576]{1,0:T(2,128)(2,1)} %bitcast.61, bf16[1,1048576]{1,0:T(2,128)(2,1)} %bitcast.62, bf16[1,1048576]{1,0:T(2,128)(2,1)} %bitcast.63, ...), custom_call_target="tpu_custom_call" | custom-call | flops 67108864 | bytes 1310720 | tf_op jit(solution)/shard_map/rotate_code/pallas_call | solution.py:95
  31.5 0.0 collective-permute-done.3.refs_0_
  31.5 0.0 copy-done.6
  31.5 2.5 %collective-permute-start.12 = (bf16[128,512]{1,0:T(8,128)(2,1)S(1)}, bf16[128,512]{1,0:T(8,128)(2,1)S(1)}, u32[]{:S(2)}, u32[]{:S(2)}) collective-permute-start(bf16[128,512]{1,0:T(8,128)(2,1)S(1)} %copy-done.6), channel_id=1, source_target_pairs={{0,7},{1,6},{2,5},{3,4},{4,3},{5,2},{6,1},{7,0},{8,15},{9,14},{10,... | collective-permute-start | bytes 393224 | tf_op jit(solution)/shard_map/ppermute | solution.py:229
  34.0 0.0 collective-permute-done.4.refs_1_
  34.0 0.0 copy-done.5
  34.0 1.5 %collective-permute-start = (bf16[256,512]{1,0:T(8,128)(2,1)S(1)}, bf16[256,512]{1,0:T(8,128)(2,1)S(1)}, u32[]{:S(2)}, u32[]{:S(2)}) collective-permute-start(bf16[256,512]{1,0:T(8,128)(2,1)S(1)} %copy-done.5), channel_id=1, source_target_pairs={{0,1},{1,0},{2,3},{3,2},{4,5},{5,4},{6,7},{7,6},{8,9},{9,8},{10,11... | collective-permute-start | bytes 786440 | tf_op jit(solution)/shard_map/ppermute | solution.py:229
  35.5 0.0 collective-permute-done.5.refs_2_
  35.5 0.0 copy-done.4
  35.5 0.0 collective-permute-start.1
  35.5 0.0 collective-permute-done.10.refs_4_
  35.5 2.0 %collective-permute-start.2 = (bf16[256,512]{1,0:T(8,128)(2,1)}, bf16[256,512]{1,0:T(8,128)(2,1)S(1)}, u32[]{:S(2)}, u32[]{:S(2)}) collective-permute-start(bf16[256,512]{1,0:T(8,128)(2,1)} %rotate_code.10), channel_id=1, source_target_pairs={{0,3},{1,2},{2,1},{3,0},{4,7},{5,6},{6,5},{7,4},{8,11},{9,10},{10,... | collective-permute-start | bytes 786440 | tf_op jit(solution)/shard_map/ppermute | solution.py:229
  37.5 3.3 %rotate_code.15 = (bf16[128,512]{1,0:T(8,128)(2,1)}, bf16[128,512]{1,0:T(8,128)(2,1)}) custom-call(s32[3]{0:T(128)} %pad_add_fusion.place_ref, bf16[256,256]{1,0:T(8,128)(2,1)} %constant.22.clone.matrix_ref, bf16[1,1048576]{1,0:T(2,128)(2,1)} %bitcast.64, bf16[1,1048576]{1,0:T(2,128)(2,1)} %bitcast.65, bf16[1,1048576]{1,0:T(2,128)(2,1)} %bitcast.66, ...), custom_call_target="tpu_custom_call" | custom-call | flops 67108864 | bytes 1310720 | tf_op jit(solution)/shard_map/rotate_code/pallas_call | solution.py:95
  40.8 0.9 %copy-done.3 = bf16[128,512]{1,0:T(8,128)(2,1)S(1)} copy-done((bf16[128,512]{1,0:T(8,128)(2,1)S(1)}, bf16[128,512]{1,0:T(8,128)(2,1)}, u32[]{:S(2)}) %copy-start.3) | copy-done | bytes 131096
  41.7 0.1 far_sum.1
  41.8 0.0 collective-permute-done.11.refs_5_
  41.8 0.1 collective-permute-start.6
  41.8 0.0 collective-permute-done.12.refs_6_
  41.9 0.0 copy-start
  41.9 2.9 %collective-permute-start.13 = (bf16[128,512]{1,0:T(8,128)(2,1)}, bf16[128,512]{1,0:T(8,128)(2,1)S(1)}, u32[]{:S(2)}, u32[]{:S(2)}) collective-permute-start(bf16[128,512]{1,0:T(8,128)(2,1)} %get-tuple-element.31), channel_id=1, source_target_pairs={{0,4},{1,5},{2,6},{3,7},{4,0},{5,1},{6,2},{7,3},{8,12},{9,13},{10,... | collective-permute-start | bytes 393224 | tf_op jit(solution)/shard_map/ppermute | solution.py:229
  44.8 3.4 %rotate_code.11.refs_3_ = bf16[256,512]{1,0:T(8,128)(2,1)} custom-call(s32[3]{0:T(128)} %pad_add_fusion.place_ref, bf16[256,256]{1,0:T(8,128)(2,1)} %constant.22.clone.matrix_ref, bf16[1,1048576]{1,0:T(2,128)(2,1)} %bitcast.68, bf16[1,1048576]{1,0:T(2,128)(2,1)} %bitcast.69, bf16[1,1048576]{1,0:T(2,128)(2,1)} %bitcast.70, bf16[1,1048576]{1,0:T(2,128)(2,1)} %bitcast.71, ...), custom_call_target="tpu_custom_call" | custom-call | flops 67108864 | bytes 1310720 | tf_op jit(solution)/shard_map/rotate_code/pallas_call | solution.py:95
  48.1 11.4 %collective-permute-done.13.refs_7_ = bf16[128,512]{1,0:T(8,128)(2,1)S(1)} collective-permute-done((bf16[128,512]{1,0:T(8,128)(2,1)}, bf16[128,512]{1,0:T(8,128)(2,1)S(1)}, u32[]{:S(2)}, u32[]{:S(2)}) %collective-permute-start.13) | collective-permute-done | bytes 131104 | tf_op jit(solution)/shard_map/ppermute | solution.py:229
  59.5 0.0 collective-permute-done.refs_0_
  59.5 0.0 collective-permute-done.1.refs_1_
  59.5 0.0 collective-permute-done.2.refs_2_
  59.6 0.0 copy-start.1
  59.6 0.9 %copy-done.1 = bf16[256,512]{1,0:T(8,128)(2,1)S(1)} copy-done((bf16[256,512]{1,0:T(8,128)(2,1)S(1)}, bf16[256,512]{1,0:T(8,128)(2,1)}, u32[]{:S(2)}) %copy-start.1) | copy-done | bytes 262168
  60.5 0.3 group_sum_code.3
  60.8 0.1 collective-permute-start.14
  60.9 1.6 %collective-permute-start.15 = (bf16[128,128]{1,0:T(8,128)(2,1)S(1)}, bf16[128,128]{1,0:T(8,128)(2,1)S(1)}, u32[]{:S(2)}, u32[]{:S(2)}) collective-permute-start(bf16[128,128]{1,0:T(8,128)(2,1)S(1)} %get-tuple-element.34), channel_id=1, source_target_pairs={{0,16},{8,24},{16,0},{24,8},{1,17},{9,25},{17,1},{25,9},{2,18},{10... | collective-permute-start | bytes 98312 | tf_op jit(solution)/shard_map/ppermute | solution.py:235
  62.5 0.3 collective-permute-start.16
  62.8 0.0 collective-permute-done.6.refs_4_
  62.8 0.9 %copy-done.2 = bf16[256,512]{1,0:T(8,128)(2,1)S(1)} copy-done((bf16[256,512]{1,0:T(8,128)(2,1)S(1)}, bf16[256,512]{1,0:T(8,128)(2,1)}, u32[]{:S(2)}) %copy-start.2) | copy-done | bytes 262168
  63.7 0.3 group_sum_code.2
  64.0 0.4 collective-permute-start.7
  64.4 1.5 %collective-permute-start.8 = (bf16[128,128]{1,0:T(8,128)(2,1)S(1)}, bf16[128,128]{1,0:T(8,128)(2,1)S(1)}, u32[]{:S(2)}, u32[]{:S(2)}) collective-permute-start(bf16[128,128]{1,0:T(8,128)(2,1)S(1)} %get-tuple-element.26), channel_id=1, source_target_pairs={{0,16},{8,24},{16,0},{24,8},{1,17},{9,25},{17,1},{25,9},{2,18},{10... | collective-permute-start | bytes 98312 | tf_op jit(solution)/shard_map/ppermute | solution.py:235
  65.9 0.0 collective-permute-done.14.refs_5_
  65.9 0.0 collective-permute-start.9
  65.9 0.9 %constant_dynamic-slice_fusion.sign_ref = s32[256,128]{1,0:T(8,128)S(1)} fusion(s32[8192,128]{1,0:T(8,128)} %bitcast.39, s32[]{:T(128)S(6)} %select_n.3), kind=kLoop, calls=%fused_computation.1 | loop fusion | bytes 262148 | tf_op jit(solution)/shard_map/dynamic_slice | solution.py:219
  66.8 0.0 collective-permute-done.15.refs_6_
  66.8 0.0 collective-permute-done.16.refs_7_
  66.9 0.0 collective-permute-done.7.refs_1_
  66.9 1.4 %collective-permute-done.8.refs_2_ = bf16[128,128]{1,0:T(8,128)(2,1)S(1)} collective-permute-done((bf16[128,128]{1,0:T(8,128)(2,1)S(1)}, bf16[128,128]{1,0:T(8,128)(2,1)S(1)}, u32[]{:S(2)}, u32[]{:S(2)}) %collective-permute-start.8) | collective-permute-done | bytes 32800 | tf_op jit(solution)/shard_map/ppermute | solution.py:235
  68.3 1.2 %collective-permute-done.9.refs_3_ = bf16[128,128]{1,0:T(8,128)(2,1)S(1)} collective-permute-done((bf16[128,128]{1,0:T(8,128)(2,1)S(1)}, bf16[128,128]{1,0:T(8,128)(2,1)S(1)}, u32[]{:S(2)}, u32[]{:S(2)}) %collective-permute-start.9) | collective-permute-done | bytes 32800 | tf_op jit(solution)/shard_map/ppermute | solution.py:235
  69.5 0.0 copy-done
  69.5 0.9 %sum_unrotate.1 = (f32[256,128]{1,0:T(8,128)}, f32[1,256]{1,0:T(1,128)}) custom-call(bf16[256,256]{1,0:T(8,128)(2,1)S(1)} %copy-done, s32[256,128]{1,0:T(8,128)S(1)} %constant_dynamic-slice_fusion.sign_ref, bf16[128,128]{1,0:T(8,128)(2,1)S(1)} %get-tuple-element.24.refs_0_, bf16[128,128]{1,0:T(8,128)(2,1)S(1)} %collective-permute-done.7.refs_1_, ...), custom_call_target="tpu_custom_call" | custom-call | tf_op jit(solution)/shard_map/sum_unrotate/pallas_call | solution.py:195
  (2 shorter events, 0.0 us)
Async XLA Ops:
  4.6 26.8 %collective-permute-start.3 = (bf16[128,512]{1,0:T(8,128)(2,1)}, bf16[128,512]{1,0:T(8,128)(2,1)S(1)}, u32[]{:S(2)}, u32[]{:S(2)}) collective-permute-start(bf16[128,512]{1,0:T(8,128)(2,1)} %get-tuple-element.20), channel_id=1, source_target_pairs={{0,1},{1,0},{2,3},{3,2},{4,5},{5,4},{6,7},{7,6},{8,9},{9,8},{10,11... | collective-permute-start | bytes 393224 | tf_op jit(solution)/shard_map/ppermute | solution.py:229
  10.9 5.0 %copy-start.8 = (bf16[128,512]{1,0:T(8,128)(2,1)S(1)}, bf16[128,512]{1,0:T(8,128)(2,1)}, u32[]{:S(2)}) copy-start(bf16[128,512]{1,0:T(8,128)(2,1)} %get-tuple-element.28) | copy-start | bytes 393220
  10.9 8.9 %copy-start.7 = (bf16[128,512]{1,0:T(8,128)(2,1)S(1)}, bf16[128,512]{1,0:T(8,128)(2,1)}, u32[]{:S(2)}) copy-start(bf16[128,512]{1,0:T(8,128)(2,1)} %get-tuple-element.29) | copy-start | bytes 393220
  10.9 23.0 %collective-permute-start.4 = (bf16[128,512]{1,0:T(8,128)(2,1)}, bf16[128,512]{1,0:T(8,128)(2,1)S(1)}, u32[]{:S(2)}, u32[]{:S(2)}) collective-permute-start(bf16[128,512]{1,0:T(8,128)(2,1)} %get-tuple-element.21), channel_id=1, source_target_pairs={{0,2},{1,3},{2,0},{3,1},{4,6},{5,7},{6,4},{7,5},{8,10},{9,11},{10,... | collective-permute-start | bytes 393224 | tf_op jit(solution)/shard_map/ppermute | solution.py:229
  15.9 19.6 %collective-permute-start.5 = (bf16[128,512]{1,0:T(8,128)(2,1)}, bf16[128,512]{1,0:T(8,128)(2,1)S(1)}, u32[]{:S(2)}, u32[]{:S(2)}) collective-permute-start(bf16[128,512]{1,0:T(8,128)(2,1)} %get-tuple-element.22), channel_id=1, source_target_pairs={{0,3},{1,2},{2,1},{3,0},{4,7},{5,6},{6,5},{7,4},{8,11},{9,10},{10,... | collective-permute-start | bytes 393224 | tf_op jit(solution)/shard_map/ppermute | solution.py:229
  16.0 19.5 %collective-permute-start.10 = (bf16[128,512]{1,0:T(8,128)(2,1)S(1)}, bf16[128,512]{1,0:T(8,128)(2,1)S(1)}, u32[]{:S(2)}, u32[]{:S(2)}) collective-permute-start(bf16[128,512]{1,0:T(8,128)(2,1)S(1)} %copy-done.8), channel_id=1, source_target_pairs={{0,5},{1,4},{2,7},{3,6},{4,1},{5,0},{6,3},{7,2},{8,13},{9,12},{10,... | collective-permute-start | bytes 393224 | tf_op jit(solution)/shard_map/ppermute | solution.py:229
  19.8 21.9 %collective-permute-start.11 = (bf16[128,512]{1,0:T(8,128)(2,1)S(1)}, bf16[128,512]{1,0:T(8,128)(2,1)S(1)}, u32[]{:S(2)}, u32[]{:S(2)}) collective-permute-start(bf16[128,512]{1,0:T(8,128)(2,1)S(1)} %copy-done.7), channel_id=1, source_target_pairs={{0,6},{1,7},{2,4},{3,5},{4,2},{5,3},{6,0},{7,1},{8,14},{9,15},{10,... | collective-permute-start | bytes 393224 | tf_op jit(solution)/shard_map/ppermute | solution.py:229
  27.9 3.5 %copy-start.6 = (bf16[128,512]{1,0:T(8,128)(2,1)S(1)}, bf16[128,512]{1,0:T(8,128)(2,1)}, u32[]{:S(2)}) copy-start(bf16[128,512]{1,0:T(8,128)(2,1)} %get-tuple-element.30) | copy-start | bytes 393220
  27.9 6.0 %copy-start.5 = (bf16[256,512]{1,0:T(8,128)(2,1)S(1)}, bf16[256,512]{1,0:T(8,128)(2,1)}, u32[]{:S(2)}) copy-start(bf16[256,512]{1,0:T(8,128)(2,1)} %rotate_code.8) | copy-start | bytes 786436
  27.9 7.5 %copy-start.4 = (bf16[256,512]{1,0:T(8,128)(2,1)S(1)}, bf16[256,512]{1,0:T(8,128)(2,1)}, u32[]{:S(2)}) copy-start(bf16[256,512]{1,0:T(8,128)(2,1)} %rotate_code.9) | copy-start | bytes 786436
  31.5 10.4 %collective-permute-start.12 = (bf16[128,512]{1,0:T(8,128)(2,1)S(1)}, bf16[128,512]{1,0:T(8,128)(2,1)S(1)}, u32[]{:S(2)}, u32[]{:S(2)}) collective-permute-start(bf16[128,512]{1,0:T(8,128)(2,1)S(1)} %copy-done.6), channel_id=1, source_target_pairs={{0,7},{1,6},{2,5},{3,4},{4,3},{5,2},{6,1},{7,0},{8,15},{9,14},{10,... | collective-permute-start | bytes 393224 | tf_op jit(solution)/shard_map/ppermute | solution.py:229
  34.0 25.6 %collective-permute-start = (bf16[256,512]{1,0:T(8,128)(2,1)S(1)}, bf16[256,512]{1,0:T(8,128)(2,1)S(1)}, u32[]{:S(2)}, u32[]{:S(2)}) collective-permute-start(bf16[256,512]{1,0:T(8,128)(2,1)S(1)} %copy-done.5), channel_id=1, source_target_pairs={{0,1},{1,0},{2,3},{3,2},{4,5},{5,4},{6,7},{7,6},{8,9},{9,8},{10,11... | collective-permute-start | bytes 786440 | tf_op jit(solution)/shard_map/ppermute | solution.py:229
  35.5 24.1 %collective-permute-start.1 = (bf16[256,512]{1,0:T(8,128)(2,1)S(1)}, bf16[256,512]{1,0:T(8,128)(2,1)S(1)}, u32[]{:S(2)}, u32[]{:S(2)}) collective-permute-start(bf16[256,512]{1,0:T(8,128)(2,1)S(1)} %copy-done.4), channel_id=1, source_target_pairs={{0,2},{1,3},{2,0},{3,1},{4,6},{5,7},{6,4},{7,5},{8,10},{9,11},{10,... | collective-permute-start | bytes 786440 | tf_op jit(solution)/shard_map/ppermute | solution.py:229
  35.5 24.1 %collective-permute-start.2 = (bf16[256,512]{1,0:T(8,128)(2,1)}, bf16[256,512]{1,0:T(8,128)(2,1)S(1)}, u32[]{:S(2)}, u32[]{:S(2)}) collective-permute-start(bf16[256,512]{1,0:T(8,128)(2,1)} %rotate_code.10), channel_id=1, source_target_pairs={{0,3},{1,2},{2,1},{3,0},{4,7},{5,6},{6,5},{7,4},{8,11},{9,10},{10,... | collective-permute-start | bytes 786440 | tf_op jit(solution)/shard_map/ppermute | solution.py:229
  40.8 0.9 %copy-start.3 = (bf16[128,512]{1,0:T(8,128)(2,1)S(1)}, bf16[128,512]{1,0:T(8,128)(2,1)}, u32[]{:S(2)}) copy-start(bf16[128,512]{1,0:T(8,128)(2,1)} %get-tuple-element.23.refs_3_) | copy-start | bytes 393220
  41.8 21.0 %collective-permute-start.6 = (f32[128,512]{1,0:T(8,128)S(1)}, f32[128,512]{1,0:T(8,128)S(1)}, u32[]{:S(2)}, u32[]{:S(2)}) collective-permute-start(f32[128,512]{1,0:T(8,128)S(1)} %far_sum.1), channel_id=1, source_target_pairs={{0,4},{1,5},{2,6},{3,7},{4,0},{5,1},{6,2},{7,3},{8,12},{9,13},{10,... | collective-permute-start | bytes 786440 | tf_op jit(solution)/shard_map/ppermute | solution.py:229
  41.9 27.7 %copy-start = (bf16[256,256]{1,0:T(8,128)(2,1)S(1)}, bf16[256,256]{1,0:T(8,128)(2,1)}, u32[]{:S(2)}) copy-start(bf16[256,256]{1,0:T(8,128)(2,1)} %constant.22.clone.matrix_ref) | copy-start | bytes 393220
  41.9 17.7 %collective-permute-start.13 = (bf16[128,512]{1,0:T(8,128)(2,1)}, bf16[128,512]{1,0:T(8,128)(2,1)S(1)}, u32[]{:S(2)}, u32[]{:S(2)}) collective-permute-start(bf16[128,512]{1,0:T(8,128)(2,1)} %get-tuple-element.31), channel_id=1, source_target_pairs={{0,4},{1,5},{2,6},{3,7},{4,0},{5,1},{6,2},{7,3},{8,12},{9,13},{10,... | collective-permute-start | bytes 393224 | tf_op jit(solution)/shard_map/ppermute | solution.py:229
  59.6 1.0 %copy-start.1 = (bf16[256,512]{1,0:T(8,128)(2,1)S(1)}, bf16[256,512]{1,0:T(8,128)(2,1)}, u32[]{:S(2)}) copy-start(bf16[256,512]{1,0:T(8,128)(2,1)} %rotate_code.11.refs_3_) | copy-start | bytes 786436
  60.8 5.1 %collective-permute-start.14 = (bf16[128,128]{1,0:T(8,128)(2,1)S(1)}, bf16[128,128]{1,0:T(8,128)(2,1)S(1)}, u32[]{:S(2)}, u32[]{:S(2)}) collective-permute-start(bf16[128,128]{1,0:T(8,128)(2,1)S(1)} %get-tuple-element.33), channel_id=1, source_target_pairs={{0,8},{8,0},{16,24},{24,16},{1,9},{9,1},{17,25},{25,17},{2,10},{10... | collective-permute-start | bytes 98312 | tf_op jit(solution)/shard_map/ppermute | solution.py:235
  60.9 5.9 %collective-permute-start.15 = (bf16[128,128]{1,0:T(8,128)(2,1)S(1)}, bf16[128,128]{1,0:T(8,128)(2,1)S(1)}, u32[]{:S(2)}, u32[]{:S(2)}) collective-permute-start(bf16[128,128]{1,0:T(8,128)(2,1)S(1)} %get-tuple-element.34), channel_id=1, source_target_pairs={{0,16},{8,24},{16,0},{24,8},{1,17},{9,25},{17,1},{25,9},{2,18},{10... | collective-permute-start | bytes 98312 | tf_op jit(solution)/shard_map/ppermute | solution.py:235
  62.5 4.4 %collective-permute-start.16 = (bf16[128,128]{1,0:T(8,128)(2,1)S(1)}, bf16[128,128]{1,0:T(8,128)(2,1)S(1)}, u32[]{:S(2)}, u32[]{:S(2)}) collective-permute-start(bf16[128,128]{1,0:T(8,128)(2,1)S(1)} %get-tuple-element.35), channel_id=1, source_target_pairs={{0,24},{8,16},{16,8},{24,0},{1,25},{9,17},{17,9},{25,1},{2,26},{10... | collective-permute-start | bytes 98312 | tf_op jit(solution)/shard_map/ppermute | solution.py:235
  62.8 1.0 %copy-start.2 = (bf16[256,512]{1,0:T(8,128)(2,1)S(1)}, bf16[256,512]{1,0:T(8,128)(2,1)}, u32[]{:S(2)}) copy-start(bf16[256,512]{1,0:T(8,128)(2,1)} %rotate_code.11.refs_3_) | copy-start | bytes 786436
  64.0 2.9 %collective-permute-start.7 = (bf16[128,128]{1,0:T(8,128)(2,1)S(1)}, bf16[128,128]{1,0:T(8,128)(2,1)S(1)}, u32[]{:S(2)}, u32[]{:S(2)}) collective-permute-start(bf16[128,128]{1,0:T(8,128)(2,1)S(1)} %get-tuple-element.25), channel_id=1, source_target_pairs={{0,8},{8,0},{16,24},{24,16},{1,9},{9,1},{17,25},{25,17},{2,10},{10... | collective-permute-start | bytes 98312 | tf_op jit(solution)/shard_map/ppermute | solution.py:235
  64.4 3.9 %collective-permute-start.8 = (bf16[128,128]{1,0:T(8,128)(2,1)S(1)}, bf16[128,128]{1,0:T(8,128)(2,1)S(1)}, u32[]{:S(2)}, u32[]{:S(2)}) collective-permute-start(bf16[128,128]{1,0:T(8,128)(2,1)S(1)} %get-tuple-element.26), channel_id=1, source_target_pairs={{0,16},{8,24},{16,0},{24,8},{1,17},{9,25},{17,1},{25,9},{2,18},{10... | collective-permute-start | bytes 98312 | tf_op jit(solution)/shard_map/ppermute | solution.py:235
  65.9 3.6 %collective-permute-start.9 = (bf16[128,128]{1,0:T(8,128)(2,1)S(1)}, bf16[128,128]{1,0:T(8,128)(2,1)S(1)}, u32[]{:S(2)}, u32[]{:S(2)}) collective-permute-start(bf16[128,128]{1,0:T(8,128)(2,1)S(1)} %get-tuple-element.27), channel_id=1, source_target_pairs={{0,24},{8,16},{16,8},{24,0},{1,25},{9,17},{17,9},{25,1},{2,26},{10... | collective-permute-start | bytes 98312 | tf_op jit(solution)/shard_map/ppermute | solution.py:235

commit v4 on v3

v4 whole, which is shorter than its diff:
```python
import functools
import jax
import jax.numpy as jnp
import numpy as np
from jax import lax
from jax.experimental import pallas as pl
from jax.experimental.pallas import tpu as pltpu
from jax.sharding import PartitionSpec as P

ROT = 256
QGROUP = 128
HALVES = ROT // QGROUP
LANES = 128
VMEM_LIMIT = 60 * 1024 * 1024
SUM_VMEM_LIMIT = 24 * 1024 * 1024


def sylvester():
    matrix = np.ones((1, 1), np.float32)
    while matrix.shape[0] < ROT:
        matrix = np.kron(np.array([[1, 1], [1, -1]], np.float32), matrix)
    return matrix


def partner(index, step, count):
    if count & (count - 1) == 0:
        return index ^ step
    return (index + step) % count


def leading_power(x):
    q = x * jnp.float32(2.0**23 + 1.0)
    return q - q * jnp.float32(1.0 - 2.0**-24)


def recode(values):
    magnitude = jnp.abs(values)
    largest = jnp.max(magnitude, axis=-2, keepdims=True)
    least = leading_power(jnp.clip(largest, 2.0**-30, 2.0**30)) * jnp.float32(2.0**-13)
    shift = leading_power(jnp.maximum(magnitude, least)) * jnp.float32(2.0**20)
    nearest = (magnitude + shift) - shift
    rest = magnitude - nearest
    coded = jnp.where(rest == shift * jnp.float32(2.0**-24), magnitude + rest, nearest)
    return jnp.where(values < 0.0, -coded, coded)


class Layout:
    def __init__(self, length, members, groups):
        self.members = members
        self.groups = groups
        self.half = members // 2
        self.portion = length // (members * groups)
        self.rows = self.portion // LANES
        self.blocks = self.portion // ROT
        self.together = 1
        if self.blocks < LANES and LANES % self.blocks == 0 and groups % (LANES // self.blocks) == 0:
            self.together = LANES // self.blocks
        self.units = groups // self.together
        self.columns = self.together * self.blocks

    def shape(self):
        return (self.units, QGROUP, self.columns)


def rotate_kernel(layout, other, steps, split, values_ref, signs_ref, matrix_ref, *refs):
    count = len(steps) * layout.units
    outs = len(steps) * (HALVES if split else 1)
    out_refs = refs[:outs]
    values, flips, turned, coded, value_sems, sign_sems, out_sems = refs[outs:]
    node = lax.axis_index("node")
    member = lax.axis_index("local")
    inner = lax.rem(member, layout.half)
    first = layout.half - (member - inner) if other else member - inner
    portion, rows = layout.portion, layout.rows

    def fetches(unit, part, place):
        return (
            pltpu.make_async_copy(
                values_ref.at[:, pl.ds(pl.multiple_of(place * portion, portion), portion)],
                values.at[unit, :, pl.ds(part * portion, portion)],
                value_sems.at[unit, part],
            ),
            pltpu.make_async_copy(
                signs_ref.at[pl.ds(pl.multiple_of(place * rows, rows), rows), :],
                flips.at[unit, pl.ds(part * rows, rows), :],
                sign_sems.at[unit, part],
            ),
        )

    for index, step in enumerate(steps):
        for section in range(layout.groups):
            place = partner(node, section, layout.groups) * layout.members + first + partner(inner, step, layout.half)
            unit = index * layout.units + section // layout.together
            for copy in fetches(unit, section % layout.together, place):
                copy.start()

    def results(index):
        if split:
            return [
                pltpu.make_async_copy(
                    coded.at[pl.ds(index * layout.units, layout.units), pl.ds(half * QGROUP, QGROUP), :],
                    out_refs[index * HALVES + half],
                    out_sems.at[index, half],
                )
                for half in range(HALVES)
            ]
        return [
            pltpu.make_async_copy(
                coded.at[pl.ds(index * layout.units, layout.units)], out_refs[index], out_sems.at[index, 0]
            )
        ]

    def body(unit, carry):
        for part in range(layout.together):
            for copy in fetches(unit, part, 0):
                copy.wait()
        wide = values[unit].astype(jnp.float32).reshape(layout.together * rows, LANES)
        turned[...] = jnp.where(flips[unit] == 0, wide, -wide)
        halves = [turned[pl.ds(half, layout.columns, stride=HALVES), :] for half in range(HALVES)]
        signed = jnp.concatenate(halves, axis=1).astype(jnp.bfloat16)
        rotated = lax.dot_general(
            matrix_ref[...], signed, (((1,), (1,)), ((), ())), preferred_element_type=jnp.float32
        )
        for half in range(HALVES):
            at = slice(half * QGROUP, (half + 1) * QGROUP)
            coded[unit, at, :] = recode(rotated[at]).astype(jnp.bfloat16)
        for index in range(len(steps)):

            @pl.when(unit == (index + 1) * layout.units - 1)
            def _():
                for copy in results(index):
                    copy.start()

        return carry

    lax.fori_loop(0, count, body, 0)
    for index in range(len(steps)):
        for copy in results(index):
            copy.wait()


def rotate(values, signs, matrix, layout, other, steps, split):
    count = len(steps) * layout.units
    entries = len(steps) * layout.groups * layout.portion
    outs = [layout.shape()] * (HALVES * len(steps))
    if not split:
        outs = [(layout.units, ROT, layout.columns)] * len(steps)
    return pl.pallas_call(
        functools.partial(rotate_kernel, layout, other, steps, split),
        in_specs=[
            pl.BlockSpec(memory_space=pl.ANY),
            pl.BlockSpec(memory_space=pl.ANY),
            pl.BlockSpec(memory_space=pltpu.VMEM),
        ],
        out_specs=[pl.BlockSpec(memory_space=pl.ANY)] * len(outs),
        out_shape=[jax.ShapeDtypeStruct(shape, jnp.bfloat16) for shape in outs],
        scratch_shapes=[
            pltpu.VMEM((count, 1, layout.together * layout.portion), jnp.bfloat16),
            pltpu.VMEM((count, layout.together * layout.rows, LANES), jnp.int32),
            pltpu.VMEM((layout.together * layout.rows, LANES), jnp.float32),
            pltpu.VMEM((count, ROT, layout.columns), jnp.bfloat16),
            pltpu.SemaphoreType.DMA((count, layout.together)),
            pltpu.SemaphoreType.DMA((count, layout.together)),
            pltpu.SemaphoreType.DMA((len(steps), HALVES)),
        ],
        compiler_params=pltpu.CompilerParams(vmem_limit_bytes=VMEM_LIMIT),
        cost_estimate=pl.CostEstimate(flops=2 * entries * ROT, bytes_accessed=10 * entries, transcendentals=0),
        name="rotate_code",
    )(values, signs, matrix)


def add_all(refs):
    total = refs[0][...].astype(jnp.float32)
    for ref in refs[1:]:
        total = total + ref[...].astype(jnp.float32)
    return total


def far_sum_kernel(*refs):
    refs[-1][...] = add_all(refs[:-1])


def far_sum(parts):
    size = parts[0].size
    return pl.pallas_call(
        far_sum_kernel,
        out_shape=jax.ShapeDtypeStruct(parts[0].shape, jnp.float32),
        compiler_params=pltpu.CompilerParams(vmem_limit_bytes=SUM_VMEM_LIMIT),
        cost_estimate=pl.CostEstimate(
            flops=2 * len(parts) * size, bytes_accessed=(2 * len(parts) + 4) * size, transcendentals=0
        ),
        name="far_sum",
    )(*parts)


def group_sum_kernel(layout, parts, *refs):
    first = recode(add_all(refs[:parts])).astype(jnp.bfloat16)
    for section, out_ref in enumerate(refs[parts:]):
        at = section % layout.together * layout.blocks
        out_ref[...] = first[section // layout.together, :, at : at + layout.blocks]


def group_sum(near, far, half, layout):
    size = far[0].size
    count = len(near) + len(far)
    return pl.pallas_call(
        functools.partial(group_sum_kernel, layout, count),
        grid=(1,),
        in_specs=[pl.BlockSpec(layout.shape(), lambda i: (0, half, 0))] * len(near)
        + [pl.BlockSpec(layout.shape(), lambda i: (0, 0, 0))] * len(far),
        out_specs=[pl.BlockSpec((QGROUP, layout.blocks), lambda i: (0, 0))] * layout.groups,
        out_shape=[jax.ShapeDtypeStruct((QGROUP, layout.blocks), jnp.bfloat16)] * layout.groups,
        compiler_params=pltpu.CompilerParams(vmem_limit_bytes=SUM_VMEM_LIMIT),
        cost_estimate=pl.CostEstimate(flops=20 * size, bytes_accessed=2 * (count + 1) * size, transcendentals=0),
        name="group_sum_code",
    )(*near, *far)


def bfloat16_terms(values):
    terms = []
    for _ in range(3):
        terms.append(values.astype(jnp.bfloat16))
        values = values - terms[-1].astype(jnp.float32)
    return terms


def finish_kernel(groups, matrix_ref, sign_ref, *refs):
    out_ref, max_ref = refs[-2:]
    second = [add_all(refs[half * groups : (half + 1) * groups]) for half in range(HALVES)]
    blocks = second[0].shape[1]
    natural = jnp.concatenate([part.T for part in second], axis=1)
    block = lax.broadcasted_iota(jnp.int32, (blocks, HALVES * blocks), 0)
    lane = lax.broadcasted_iota(jnp.int32, (blocks, HALVES * blocks), 1)
    largest = jnp.zeros((1, HALVES * blocks), jnp.float32)
    for half in range(HALVES):
        peak = jnp.max(jnp.abs(natural[:, half * QGROUP : (half + 1) * QGROUP]), axis=1, keepdims=True)
        chosen = jnp.where(lane == HALVES * block + half, peak, 0.0)
        largest = jnp.maximum(largest, jnp.max(chosen, axis=0, keepdims=True))
    max_ref[...] = largest * jnp.float32(ROT**-0.5)
    high, middle, low = [
        jnp.dot(term, matrix_ref[...], preferred_element_type=jnp.float32) for term in bfloat16_terms(natural)
    ]
    turned = (high + (middle + low)) * jnp.float32(1.0 / ROT)
    for half in range(HALVES):
        at = pl.ds(half, blocks, stride=HALVES)
        part = turned[:, half * QGROUP : (half + 1) * QGROUP]
        out_ref[at, :] = jnp.where(sign_ref[at, :] == 0, part, -part)


def finish(parts, signs, matrix):
    groups = len(parts[0])
    rows = signs.shape[0]
    return pl.pallas_call(
        functools.partial(finish_kernel, groups),
        out_shape=[
            jax.ShapeDtypeStruct((rows, LANES), jnp.float32),
            jax.ShapeDtypeStruct((1, rows), jnp.float32),
        ],
        compiler_params=pltpu.CompilerParams(vmem_limit_bytes=SUM_VMEM_LIMIT),
        name="sum_unrotate",
    )(matrix, signs, *[part for half in parts for part in half])


def shards(partials, signs):
    length = partials.shape[-1]
    members = lax.axis_size("local")
    groups = lax.axis_size("node")
    layout = Layout(length, members, groups)
    half = layout.half
    matrix = jnp.asarray(sylvester(), jnp.bfloat16)
    values = partials.reshape(1, length)
    sign_rows = signs.reshape(length // LANES, LANES)
    own = (lax.axis_index("node") * members + lax.axis_index("local")) * layout.rows
    own_signs = lax.dynamic_slice_in_dim(sign_rows, own, layout.rows)

    def send(part, other, step):
        pairs = []
        for source in range(members):
            first, index = source // half * half, source % half
            pairs.append((source, (half - first if other else first) + partner(index, step, half)))
        return lax.ppermute(part, "local", pairs)

    def share(parts):
        moved = [parts[0]]
        for step in range(1, groups):
            pairs = [(source, partner(source, step, groups)) for source in range(groups)]
            moved.append(lax.ppermute(parts[step], "node", pairs))
        return moved

    steps = list(range(half))
    far = rotate(values, sign_rows, matrix, layout, True, steps, True)
    direct = [send(far[HALVES * step + 1], True, step) for step in steps]
    summed = [far[0]] + [send(far[HALVES * step], False, step) for step in steps[1:]]
    near = rotate(values, sign_rows, matrix, layout, False, steps, False)
    near = [near[0]] + [send(near[step], False, step) for step in steps[1:]]
    across = send(far_sum(summed), True, 0)
    second_half = share(group_sum(near, direct, 1, layout))
    first_half = share(group_sum(near, [across], 0, layout))
    reduced, rotated_max = finish([first_half, second_half], own_signs, matrix)
    return (reduced.reshape(-1), rotated_max.reshape(-1))


def solution(mesh):
    in_specs = (P("node", "local", None), P())
    out_specs = (P(("node", "local")), P(("node", "local")))
    return jax.shard_map(shards, mesh=mesh, in_specs=in_specs, out_specs=out_specs, check_vma=False)
```

time: 71 us -> 63.7 us (0.90)
  Pallas kernels: 28.5 us -> 17.5 us
  waiting for transfers between devices: 14.1 us -> 19 us
  local copies, waits for them, and re-layouts: 3.74 us -> 2.83 us
    pallas_call x11 -> x5, Pallas kernels: 27.6 us -> 16.5 us  [the longest x2 15.6 us: rotate(): pl.pallas_call(functools.partial(rotate_kernel, layout, other, steps, spl...]
    ppermute x11, waiting for transfers between devices: 11.4 us -> 16.3 us  [send(): return lax.ppermute(part, 'local', pairs)]
    unnamed x18 -> x12, local copies, waits for them, and re-layouts: 2.82 us -> 1.92 us
    ppermute x11, starting transfers between devices: 18.8 us -> 19.5 us  [send(): return lax.ppermute(part, 'local', pairs)]
  transfers between devices with their start and end apart: 17 -> 17, of which waited for: 3 -> 6; matrix products, arithmetic and copies ran while one was open for 1% -> 1% of each run, Pallas kernels for 34% -> 14%
where the time goes in v4:
time: 63.7 us; the launch traced here: 63.5 us
  starting transfers between devices  23.4 us (37%)
  waiting for transfers between devices  19 us (30%)
  Pallas kernels  17.5 us (27%)
  local copies, waits for them, and re-layouts  2.83 us (4%)
  between operations  0.74 us (1%)
    ppermute x11, starting transfers between devices, send(): return lax.ppermute(part, 'local', pairs)  19.5 us
    ppermute x11, waiting for transfers between devices, send(): return lax.ppermute(part, 'local', pairs)  16.3 us
    pallas_call x2, Pallas kernels, rotate(): pl.pallas_call(functools.partial(rotate_kernel, layout, other, steps, spl...  15.6 us
    ppermute x6, starting transfers between devices, share(): moved.append(lax.ppermute(parts[step], 'node', pairs))  3.89 us
    ppermute x6, waiting for transfers between devices, share(): moved.append(lax.ppermute(parts[step], 'node', pairs))  2.71 us
    unnamed x12, local copies, waits for them, and re-layouts  1.92 us
  transfers between devices with their start and end apart: 17, of which 6 were waited for; matrix products, arithmetic and copies ran while one was open for 1% of the time, Pallas kernels for 14%

profile of v4, /device:TPU:0, one launch (start us, length us, event | category | flops | bytes accessed | tf_op | source)
XLA Modules:
  0.0 63.5 jit_solution(17181614847774562910)
XLA Ops:
  0.6 7.8 %rotate_code.3 = (bf16[4,128,128]{2,1,0:T(8,128)(2,1)}, bf16[4,128,128]{2,1,0:T(8,128)(2,1)}, bf16[4,128,128]{2,1,0:T(8,128)(2,1)}, bf16[4,128,128]{2,1,0:T(8,12...) custom-call(bf16[1,1048576]{1,0:T(2,128)(2,1)} %bitcast.7, ...), custom_call_target="tpu_custom_call" | custom-call | flops 268435456 | bytes 5242880 | tf_op jit(solution)/shard_map/rotate_code/pallas_call | solution.py:148
  8.4 3.0 %collective-permute-start.3 = (bf16[4,128,128]{2,1,0:T(8,128)(2,1)}, bf16[4,128,128]{2,1,0:T(8,128)(2,1)S(1)}, u32[]{:S(2)}, u32[]{:S(2)}) collective-permute-start(bf16[4,128,128]{2,1,0:T(8,128)(2,1)} %get-tuple-element.29), channel_id=1, source_target_pairs={{0,1},{1,0},{2,3},{3,2},{4,5},{5,4},{6,7},{7,6},{8,9},{9,8},{10,11... | collective-permute-start | bytes 393224 | tf_op jit(solution)/shard_map/ppermute | solution.py:281
  11.5 1.6 %collective-permute-start.4 = (bf16[4,128,128]{2,1,0:T(8,128)(2,1)}, bf16[4,128,128]{2,1,0:T(8,128)(2,1)S(1)}, u32[]{:S(2)}, u32[]{:S(2)}) collective-permute-start(bf16[4,128,128]{2,1,0:T(8,128)(2,1)} %get-tuple-element.30), channel_id=1, source_target_pairs={{0,2},{1,3},{2,0},{3,1},{4,6},{5,7},{6,4},{7,5},{8,10},{9,11},{10,... | collective-permute-start | bytes 393224 | tf_op jit(solution)/shard_map/ppermute | solution.py:281
  13.1 0.0 collective-permute-start.5
  13.1 3.0 %collective-permute-start.10 = (bf16[4,128,128]{2,1,0:T(8,128)(2,1)}, bf16[4,128,128]{2,1,0:T(8,128)(2,1)S(1)}, u32[]{:S(2)}, u32[]{:S(2)}) collective-permute-start(bf16[4,128,128]{2,1,0:T(8,128)(2,1)} %get-tuple-element.36), channel_id=1, source_target_pairs={{0,4},{1,5},{2,6},{3,7},{4,0},{5,1},{6,2},{7,3},{8,12},{9,13},{10,... | collective-permute-start | bytes 393224 | tf_op jit(solution)/shard_map/ppermute | solution.py:281
  16.0 0.0 copy-start.5
  16.0 0.0 copy-start.3
  16.0 0.0 copy-start.4
  16.0 0.0 copy-start
  16.0 1.4 %collective-permute-start.11 = (bf16[4,128,128]{2,1,0:T(8,128)(2,1)}, bf16[4,128,128]{2,1,0:T(8,128)(2,1)S(1)}, u32[]{:S(2)}, u32[]{:S(2)}) collective-permute-start(bf16[4,128,128]{2,1,0:T(8,128)(2,1)} %get-tuple-element.37), channel_id=1, source_target_pairs={{0,5},{1,4},{2,7},{3,6},{4,1},{5,0},{6,3},{7,2},{8,13},{9,12},{10,... | collective-permute-start | bytes 393224 | tf_op jit(solution)/shard_map/ppermute | solution.py:281
  17.4 7.8 %rotate_code.2 = (bf16[4,256,128]{2,1,0:T(8,128)(2,1)}, bf16[4,256,128]{2,1,0:T(8,128)(2,1)}, bf16[4,256,128]{2,1,0:T(8,128)(2,1)}, bf16[4,256,128]{2,1,0:T(8,128)(2,1)}) custom-call(bf16[1,1048576]{1,0:T(2,128)(2,1)} %bitcast.8, s32[8192,128]{1,0:T(8,128)} %bitcast.5, bf16[256,256]{1,0:T(8,128)(2,1)} %constant.18.clone.matrix_ref), custom_call_target="tpu_custom_call" | custom-call | flops 268435456 | bytes 5242880 | tf_op jit(solution)/shard_map/rotate_code/pallas_call | solution.py:148
  25.2 0.0 collective-permute-done.3.refs_1_
  25.2 0.0 copy-done.5
  25.2 3.7 %collective-permute-start.12 = (bf16[4,128,128]{2,1,0:T(8,128)(2,1)S(1)}, bf16[4,128,128]{2,1,0:T(8,128)(2,1)S(1)}, u32[]{:S(2)}, u32[]{:S(2)}) collective-permute-start(bf16[4,128,128]{2,1,0:T(8,128)(2,1)S(1)} %copy-done.5), channel_id=1, source_target_pairs={{0,6},{1,7},{2,4},{3,5},{4,2},{5,3},{6,0},{7,1},{8,14},{9,15},{10,... | collective-permute-start | bytes 393224 | tf_op jit(solution)/shard_map/ppermute | solution.py:281
  28.9 0.0 collective-permute-done.4.refs_2_
  28.9 0.5 collective-permute-start
  29.4 0.0 collective-permute-done.5.refs_3_
  29.4 0.0 collective-permute-start.1
  29.4 0.0 collective-permute-done.10.refs_4_
  29.4 3.0 %collective-permute-start.2 = (bf16[4,256,128]{2,1,0:T(8,128)(2,1)}, bf16[4,256,128]{2,1,0:T(8,128)(2,1)S(1)}, u32[]{:S(2)}, u32[]{:S(2)}) collective-permute-start(bf16[4,256,128]{2,1,0:T(8,128)(2,1)} %get-tuple-element.27), channel_id=1, source_target_pairs={{0,3},{1,2},{2,1},{3,0},{4,7},{5,6},{6,5},{7,4},{8,11},{9,10},{10,... | collective-permute-start | bytes 786440 | tf_op jit(solution)/shard_map/ppermute | solution.py:281
  32.4 0.0 copy-done.3
  32.4 0.1 far_sum.1
  32.4 0.2 collective-permute-done.11.refs_5_
  32.6 0.0 collective-permute-start.6
  32.6 1.0 %collective-permute-done.12.refs_6_ = bf16[4,128,128]{2,1,0:T(8,128)(2,1)S(1)} collective-permute-done((bf16[4,128,128]{2,1,0:T(8,128)(2,1)S(1)}, bf16[4,128,128]{2,1,0:T(8,128)(2,1)S(1)}, u32[]{:S(2)}, u32[]{:S(2)}) %collective-permute-start.12) | collective-permute-done | bytes 131104 | tf_op jit(solution)/shard_map/ppermute | solution.py:281
  33.6 0.0 copy-done.4
  33.6 3.5 %collective-permute-start.13 = (bf16[4,128,128]{2,1,0:T(8,128)(2,1)S(1)}, bf16[4,128,128]{2,1,0:T(8,128)(2,1)S(1)}, u32[]{:S(2)}, u32[]{:S(2)}) collective-permute-start(bf16[4,128,128]{2,1,0:T(8,128)(2,1)S(1)} %copy-done.4), channel_id=1, source_target_pairs={{0,7},{1,6},{2,5},{3,4},{4,3},{5,2},{6,1},{7,0},{8,15},{9,14},{10,... | collective-permute-start | bytes 393224 | tf_op jit(solution)/shard_map/ppermute | solution.py:281
  37.1 14.1 %collective-permute-done.13.refs_7_ = bf16[4,128,128]{2,1,0:T(8,128)(2,1)S(1)} collective-permute-done((bf16[4,128,128]{2,1,0:T(8,128)(2,1)S(1)}, bf16[4,128,128]{2,1,0:T(8,128)(2,1)S(1)}, u32[]{:S(2)}, u32[]{:S(2)}) %collective-permute-start.13) | collective-permute-done | bytes 131104 | tf_op jit(solution)/shard_map/ppermute | solution.py:281
  51.2 0.0 collective-permute-done.refs_1_
  51.2 0.0 collective-permute-done.1.refs_2_
  51.2 1.0 %collective-permute-done.2.refs_3_ = bf16[4,256,128]{2,1,0:T(8,128)(2,1)S(1)} collective-permute-done((bf16[4,256,128]{2,1,0:T(8,128)(2,1)}, bf16[4,256,128]{2,1,0:T(8,128)(2,1)S(1)}, u32[]{:S(2)}, u32[]{:S(2)}) %collective-permute-start.2) | collective-permute-done | bytes 262176 | tf_op jit(solution)/shard_map/ppermute | solution.py:281
  52.2 0.0 copy-start.1
  52.2 0.9 %copy-done.1 = bf16[4,256,128]{2,1,0:T(8,128)(2,1)S(1)} copy-done((bf16[4,256,128]{2,1,0:T(8,128)(2,1)S(1)}, bf16[4,256,128]{2,1,0:T(8,128)(2,1)}, u32[]{:S(2)}) %copy-start.1) | copy-done | bytes 262168
  53.1 0.5 group_sum_code.3
  53.6 0.1 collective-permute-start.14
  53.7 1.6 %collective-permute-start.15 = (bf16[128,128]{1,0:T(8,128)(2,1)S(1)}, bf16[128,128]{1,0:T(8,128)(2,1)S(1)}, u32[]{:S(2)}, u32[]{:S(2)}) collective-permute-start(bf16[128,128]{1,0:T(8,128)(2,1)S(1)} %get-tuple-element.42), channel_id=1, source_target_pairs={{0,16},{8,24},{16,0},{24,8},{1,17},{9,25},{17,1},{25,9},{2,18},{10... | collective-permute-start | bytes 98312 | tf_op jit(solution)/shard_map/ppermute | solution.py:287
  55.3 0.3 collective-permute-start.16
  55.5 0.0 collective-permute-done.6.refs_4_
  55.5 0.0 copy-start.2
  55.5 0.9 %copy-done.2 = bf16[4,256,128]{2,1,0:T(8,128)(2,1)S(1)} copy-done((bf16[4,256,128]{2,1,0:T(8,128)(2,1)S(1)}, bf16[4,256,128]{2,1,0:T(8,128)(2,1)}, u32[]{:S(2)}) %copy-start.2) | copy-done | bytes 262168
  56.5 0.4 group_sum_code.2
  56.9 0.4 collective-permute-start.7
  57.3 1.5 %collective-permute-start.8 = (bf16[128,128]{1,0:T(8,128)(2,1)S(1)}, bf16[128,128]{1,0:T(8,128)(2,1)S(1)}, u32[]{:S(2)}, u32[]{:S(2)}) collective-permute-start(bf16[128,128]{1,0:T(8,128)(2,1)S(1)} %get-tuple-element.34), channel_id=1, source_target_pairs={{0,16},{8,24},{16,0},{24,8},{1,17},{9,25},{17,1},{25,9},{2,18},{10... | collective-permute-start | bytes 98312 | tf_op jit(solution)/shard_map/ppermute | solution.py:287
  58.9 0.0 collective-permute-done.14.refs_5_
  58.9 0.0 collective-permute-start.9
  58.9 0.9 %constant_dynamic-slice_fusion.sign_ref = s32[256,128]{1,0:T(8,128)S(1)} fusion(s32[8192,128]{1,0:T(8,128)} %bitcast.6, s32[]{:T(128)S(6)} %select_n.3), kind=kLoop, calls=%fused_computation | loop fusion | bytes 262148 | tf_op jit(solution)/shard_map/dynamic_slice | solution.py:274
  59.8 0.0 collective-permute-done.15.refs_6_
  59.8 0.0 collective-permute-done.16.refs_7_
  59.8 0.0 collective-permute-done.7.refs_1_
  59.8 1.4 %collective-permute-done.8.refs_2_ = bf16[128,128]{1,0:T(8,128)(2,1)S(1)} collective-permute-done((bf16[128,128]{1,0:T(8,128)(2,1)S(1)}, bf16[128,128]{1,0:T(8,128)(2,1)S(1)}, u32[]{:S(2)}, u32[]{:S(2)}) %collective-permute-start.8) | collective-permute-done | bytes 32800 | tf_op jit(solution)/shard_map/ppermute | solution.py:287
  61.2 1.3 %collective-permute-done.9.refs_3_ = bf16[128,128]{1,0:T(8,128)(2,1)S(1)} collective-permute-done((bf16[128,128]{1,0:T(8,128)(2,1)S(1)}, bf16[128,128]{1,0:T(8,128)(2,1)S(1)}, u32[]{:S(2)}, u32[]{:S(2)}) %collective-permute-start.9) | collective-permute-done | bytes 32800 | tf_op jit(solution)/shard_map/ppermute | solution.py:287
  62.5 0.0 copy-done
  62.5 0.9 %sum_unrotate.1 = (f32[256,128]{1,0:T(8,128)}, f32[1,256]{1,0:T(1,128)}) custom-call(bf16[256,256]{1,0:T(8,128)(2,1)S(1)} %copy-done, s32[256,128]{1,0:T(8,128)S(1)} %constant_dynamic-slice_fusion.sign_ref, bf16[128,128]{1,0:T(8,128)(2,1)S(1)} %get-tuple-element.32.refs_0_, bf16[128,128]{1,0:T(8,128)(2,1)S(1)} %collective-permute-done.7.refs_1_, ...), custom_call_target="tpu_custom_call" | custom-call | tf_op jit(solution)/shard_map/sum_unrotate/pallas_call | solution.py:253
Async XLA Ops:
  8.4 16.7 %collective-permute-start.3 = (bf16[4,128,128]{2,1,0:T(8,128)(2,1)}, bf16[4,128,128]{2,1,0:T(8,128)(2,1)S(1)}, u32[]{:S(2)}, u32[]{:S(2)}) collective-permute-start(bf16[4,128,128]{2,1,0:T(8,128)(2,1)} %get-tuple-element.29), channel_id=1, source_target_pairs={{0,1},{1,0},{2,3},{3,2},{4,5},{5,4},{6,7},{7,6},{8,9},{9,8},{10,11... | collective-permute-start | bytes 393224 | tf_op jit(solution)/shard_map/ppermute | solution.py:281
  11.5 17.4 %collective-permute-start.4 = (bf16[4,128,128]{2,1,0:T(8,128)(2,1)}, bf16[4,128,128]{2,1,0:T(8,128)(2,1)S(1)}, u32[]{:S(2)}, u32[]{:S(2)}) collective-permute-start(bf16[4,128,128]{2,1,0:T(8,128)(2,1)} %get-tuple-element.30), channel_id=1, source_target_pairs={{0,2},{1,3},{2,0},{3,1},{4,6},{5,7},{6,4},{7,5},{8,10},{9,11},{10,... | collective-permute-start | bytes 393224 | tf_op jit(solution)/shard_map/ppermute | solution.py:281
  13.1 16.3 %collective-permute-start.5 = (bf16[4,128,128]{2,1,0:T(8,128)(2,1)}, bf16[4,128,128]{2,1,0:T(8,128)(2,1)S(1)}, u32[]{:S(2)}, u32[]{:S(2)}) collective-permute-start(bf16[4,128,128]{2,1,0:T(8,128)(2,1)} %get-tuple-element.31), channel_id=1, source_target_pairs={{0,3},{1,2},{2,1},{3,0},{4,7},{5,6},{6,5},{7,4},{8,11},{9,10},{10,... | collective-permute-start | bytes 393224 | tf_op jit(solution)/shard_map/ppermute | solution.py:281
  13.1 16.3 %collective-permute-start.10 = (bf16[4,128,128]{2,1,0:T(8,128)(2,1)}, bf16[4,128,128]{2,1,0:T(8,128)(2,1)S(1)}, u32[]{:S(2)}, u32[]{:S(2)}) collective-permute-start(bf16[4,128,128]{2,1,0:T(8,128)(2,1)} %get-tuple-element.36), channel_id=1, source_target_pairs={{0,4},{1,5},{2,6},{3,7},{4,0},{5,1},{6,2},{7,3},{8,12},{9,13},{10,... | collective-permute-start | bytes 393224 | tf_op jit(solution)/shard_map/ppermute | solution.py:281
  16.0 9.2 %copy-start.5 = (bf16[4,128,128]{2,1,0:T(8,128)(2,1)S(1)}, bf16[4,128,128]{2,1,0:T(8,128)(2,1)}, u32[]{:S(2)}) copy-start(bf16[4,128,128]{2,1,0:T(8,128)(2,1)} %get-tuple-element.38) | copy-start | bytes 393220
  16.0 16.3 %copy-start.3 = (bf16[4,128,128]{2,1,0:T(8,128)(2,1)S(1)}, bf16[4,128,128]{2,1,0:T(8,128)(2,1)}, u32[]{:S(2)}) copy-start(bf16[4,128,128]{2,1,0:T(8,128)(2,1)} %get-tuple-element.28.refs_0_) | copy-start | bytes 393220
  16.0 17.6 %copy-start.4 = (bf16[4,128,128]{2,1,0:T(8,128)(2,1)S(1)}, bf16[4,128,128]{2,1,0:T(8,128)(2,1)}, u32[]{:S(2)}) copy-start(bf16[4,128,128]{2,1,0:T(8,128)(2,1)} %get-tuple-element.39) | copy-start | bytes 393220
  16.0 46.5 %copy-start = (bf16[256,256]{1,0:T(8,128)(2,1)S(1)}, bf16[256,256]{1,0:T(8,128)(2,1)}, u32[]{:S(2)}) copy-start(bf16[256,256]{1,0:T(8,128)(2,1)} %constant.18.clone.matrix_ref) | copy-start | bytes 393220
  16.0 16.6 %collective-permute-start.11 = (bf16[4,128,128]{2,1,0:T(8,128)(2,1)}, bf16[4,128,128]{2,1,0:T(8,128)(2,1)S(1)}, u32[]{:S(2)}, u32[]{:S(2)}) collective-permute-start(bf16[4,128,128]{2,1,0:T(8,128)(2,1)} %get-tuple-element.37), channel_id=1, source_target_pairs={{0,5},{1,4},{2,7},{3,6},{4,1},{5,0},{6,3},{7,2},{8,13},{9,12},{10,... | collective-permute-start | bytes 393224 | tf_op jit(solution)/shard_map/ppermute | solution.py:281
  25.2 8.4 %collective-permute-start.12 = (bf16[4,128,128]{2,1,0:T(8,128)(2,1)S(1)}, bf16[4,128,128]{2,1,0:T(8,128)(2,1)S(1)}, u32[]{:S(2)}, u32[]{:S(2)}) collective-permute-start(bf16[4,128,128]{2,1,0:T(8,128)(2,1)S(1)} %copy-done.5), channel_id=1, source_target_pairs={{0,6},{1,7},{2,4},{3,5},{4,2},{5,3},{6,0},{7,1},{8,14},{9,15},{10,... | collective-permute-start | bytes 393224 | tf_op jit(solution)/shard_map/ppermute | solution.py:281
  28.9 22.3 %collective-permute-start = (bf16[4,256,128]{2,1,0:T(8,128)(2,1)}, bf16[4,256,128]{2,1,0:T(8,128)(2,1)S(1)}, u32[]{:S(2)}, u32[]{:S(2)}) collective-permute-start(bf16[4,256,128]{2,1,0:T(8,128)(2,1)} %get-tuple-element.25), channel_id=1, source_target_pairs={{0,1},{1,0},{2,3},{3,2},{4,5},{5,4},{6,7},{7,6},{8,9},{9,8},{10,11... | collective-permute-start | bytes 786440 | tf_op jit(solution)/shard_map/ppermute | solution.py:281
  29.4 21.8 %collective-permute-start.1 = (bf16[4,256,128]{2,1,0:T(8,128)(2,1)}, bf16[4,256,128]{2,1,0:T(8,128)(2,1)S(1)}, u32[]{:S(2)}, u32[]{:S(2)}) collective-permute-start(bf16[4,256,128]{2,1,0:T(8,128)(2,1)} %get-tuple-element.26), channel_id=1, source_target_pairs={{0,2},{1,3},{2,0},{3,1},{4,6},{5,7},{6,4},{7,5},{8,10},{9,11},{10,... | collective-permute-start | bytes 786440 | tf_op jit(solution)/shard_map/ppermute | solution.py:281
  29.4 22.8 %collective-permute-start.2 = (bf16[4,256,128]{2,1,0:T(8,128)(2,1)}, bf16[4,256,128]{2,1,0:T(8,128)(2,1)S(1)}, u32[]{:S(2)}, u32[]{:S(2)}) collective-permute-start(bf16[4,256,128]{2,1,0:T(8,128)(2,1)} %get-tuple-element.27), channel_id=1, source_target_pairs={{0,3},{1,2},{2,1},{3,0},{4,7},{5,6},{6,5},{7,4},{8,11},{9,10},{10,... | collective-permute-start | bytes 786440 | tf_op jit(solution)/shard_map/ppermute | solution.py:281
  32.6 22.9 %collective-permute-start.6 = (f32[4,128,128]{2,1,0:T(8,128)S(1)}, f32[4,128,128]{2,1,0:T(8,128)S(1)}, u32[]{:S(2)}, u32[]{:S(2)}) collective-permute-start(f32[4,128,128]{2,1,0:T(8,128)S(1)} %far_sum.1), channel_id=1, source_target_pairs={{0,4},{1,5},{2,6},{3,7},{4,0},{5,1},{6,2},{7,3},{8,12},{9,13},{10,... | collective-permute-start | bytes 786440 | tf_op jit(solution)/shard_map/ppermute | solution.py:281
  33.6 17.6 %collective-permute-start.13 = (bf16[4,128,128]{2,1,0:T(8,128)(2,1)S(1)}, bf16[4,128,128]{2,1,0:T(8,128)(2,1)S(1)}, u32[]{:S(2)}, u32[]{:S(2)}) collective-permute-start(bf16[4,128,128]{2,1,0:T(8,128)(2,1)S(1)} %copy-done.4), channel_id=1, source_target_pairs={{0,7},{1,6},{2,5},{3,4},{4,3},{5,2},{6,1},{7,0},{8,15},{9,14},{10,... | collective-permute-start | bytes 393224 | tf_op jit(solution)/shard_map/ppermute | solution.py:281
  52.2 1.0 %copy-start.1 = (bf16[4,256,128]{2,1,0:T(8,128)(2,1)S(1)}, bf16[4,256,128]{2,1,0:T(8,128)(2,1)}, u32[]{:S(2)}) copy-start(bf16[4,256,128]{2,1,0:T(8,128)(2,1)} %get-tuple-element.24.refs_0_) | copy-start | bytes 786436
  53.6 5.3 %collective-permute-start.14 = (bf16[128,128]{1,0:T(8,128)(2,1)S(1)}, bf16[128,128]{1,0:T(8,128)(2,1)S(1)}, u32[]{:S(2)}, u32[]{:S(2)}) collective-permute-start(bf16[128,128]{1,0:T(8,128)(2,1)S(1)} %get-tuple-element.41), channel_id=1, source_target_pairs={{0,8},{8,0},{16,24},{24,16},{1,9},{9,1},{17,25},{25,17},{2,10},{10... | collective-permute-start | bytes 98312 | tf_op jit(solution)/shard_map/ppermute | solution.py:287
  53.7 6.1 %collective-permute-start.15 = (bf16[128,128]{1,0:T(8,128)(2,1)S(1)}, bf16[128,128]{1,0:T(8,128)(2,1)S(1)}, u32[]{:S(2)}, u32[]{:S(2)}) collective-permute-start(bf16[128,128]{1,0:T(8,128)(2,1)S(1)} %get-tuple-element.42), channel_id=1, source_target_pairs={{0,16},{8,24},{16,0},{24,8},{1,17},{9,25},{17,1},{25,9},{2,18},{10... | collective-permute-start | bytes 98312 | tf_op jit(solution)/shard_map/ppermute | solution.py:287
  55.3 4.5 %collective-permute-start.16 = (bf16[128,128]{1,0:T(8,128)(2,1)S(1)}, bf16[128,128]{1,0:T(8,128)(2,1)S(1)}, u32[]{:S(2)}, u32[]{:S(2)}) collective-permute-start(bf16[128,128]{1,0:T(8,128)(2,1)S(1)} %get-tuple-element.43), channel_id=1, source_target_pairs={{0,24},{8,16},{16,8},{24,0},{1,25},{9,17},{17,9},{25,1},{2,26},{10... | collective-permute-start | bytes 98312 | tf_op jit(solution)/shard_map/ppermute | solution.py:287
  55.5 1.0 %copy-start.2 = (bf16[4,256,128]{2,1,0:T(8,128)(2,1)S(1)}, bf16[4,256,128]{2,1,0:T(8,128)(2,1)}, u32[]{:S(2)}) copy-start(bf16[4,256,128]{2,1,0:T(8,128)(2,1)} %get-tuple-element.24.refs_0_) | copy-start | bytes 786436
  56.9 2.9 %collective-permute-start.7 = (bf16[128,128]{1,0:T(8,128)(2,1)S(1)}, bf16[128,128]{1,0:T(8,128)(2,1)S(1)}, u32[]{:S(2)}, u32[]{:S(2)}) collective-permute-start(bf16[128,128]{1,0:T(8,128)(2,1)S(1)} %get-tuple-element.33), channel_id=1, source_target_pairs={{0,8},{8,0},{16,24},{24,16},{1,9},{9,1},{17,25},{25,17},{2,10},{10... | collective-permute-start | bytes 98312 | tf_op jit(solution)/shard_map/ppermute | solution.py:287
  57.3 3.9 %collective-permute-start.8 = (bf16[128,128]{1,0:T(8,128)(2,1)S(1)}, bf16[128,128]{1,0:T(8,128)(2,1)S(1)}, u32[]{:S(2)}, u32[]{:S(2)}) collective-permute-start(bf16[128,128]{1,0:T(8,128)(2,1)S(1)} %get-tuple-element.34), channel_id=1, source_target_pairs={{0,16},{8,24},{16,0},{24,8},{1,17},{9,25},{17,1},{25,9},{2,18},{10... | collective-permute-start | bytes 98312 | tf_op jit(solution)/shard_map/ppermute | solution.py:287
  58.9 3.7 %collective-permute-start.9 = (bf16[128,128]{1,0:T(8,128)(2,1)S(1)}, bf16[128,128]{1,0:T(8,128)(2,1)S(1)}, u32[]{:S(2)}, u32[]{:S(2)}) collective-permute-start(bf16[128,128]{1,0:T(8,128)(2,1)S(1)} %get-tuple-element.35), channel_id=1, source_target_pairs={{0,24},{8,16},{16,8},{24,0},{1,25},{9,17},{17,9},{25,1},{2,26},{10... | collective-permute-start | bytes 98312 | tf_op jit(solution)/shard_map/ppermute | solution.py:287

commit v5 on v4

v5 whole, which is shorter than its diff:
```python
import functools
import jax
import jax.numpy as jnp
from jax import lax
from jax.experimental import pallas as pl
from jax.experimental.pallas import tpu as pltpu
from jax.sharding import PartitionSpec as P

ROT = 256
QGROUP = 128
HALVES = ROT // QGROUP
LANES = 128
VMEM_LIMIT = 60 * 1024 * 1024
SUM_VMEM_LIMIT = 24 * 1024 * 1024


def sylvester():
    row = lax.broadcasted_iota(jnp.int32, (ROT, ROT), 0)
    column = lax.broadcasted_iota(jnp.int32, (ROT, ROT), 1)
    parity = lax.population_count(row & column) & 1
    return (1 - 2 * parity).astype(jnp.float32).astype(jnp.bfloat16)


def partner(index, step, count):
    if count & (count - 1) == 0:
        return index ^ step
    return (index + step) % count


def leading_power(x):
    q = x * jnp.float32(2.0**23 + 1.0)
    return q - q * jnp.float32(1.0 - 2.0**-24)


def recode(values):
    magnitude = jnp.abs(values)
    largest = jnp.max(magnitude, axis=-2, keepdims=True)
    least = leading_power(jnp.clip(largest, 2.0**-30, 2.0**30)) * jnp.float32(2.0**-13)
    shift = leading_power(jnp.maximum(magnitude, least)) * jnp.float32(2.0**20)
    nearest = (magnitude + shift) - shift
    rest = magnitude - nearest
    coded = jnp.where(rest == shift * jnp.float32(2.0**-24), magnitude + rest, nearest)
    return jnp.where(values < 0.0, -coded, coded)


class Layout:
    def __init__(self, length, members, groups):
        self.members = members
        self.groups = groups
        self.half = members // 2
        self.portion = length // (members * groups)
        self.rows = self.portion // LANES
        self.blocks = self.portion // ROT
        self.together = 1
        if self.blocks < LANES and LANES % self.blocks == 0 and groups % (LANES // self.blocks) == 0:
            self.together = LANES // self.blocks
        self.units = groups // self.together
        self.columns = self.together * self.blocks

    def shape(self):
        return (self.units, QGROUP, self.columns)


def rotate_kernel(layout, values_ref, signs_ref, *refs):
    half, units = layout.half, layout.units
    direct_ref, flips_ref = refs[:2]
    paired_refs = refs[2 : 2 + half]
    values, flips, turned, matrix, coded, value_sems, sign_sems, out_sems, flip_sem = refs[2 + half :]
    node = lax.axis_index("node")
    member = lax.axis_index("local")
    inner = lax.rem(member, half)
    near_first = member - inner
    portion, rows = layout.portion, layout.rows

    def owner(index):
        far = index % 2 == 0
        return jnp.where(far, half - near_first, near_first) + partner(inner, index // 2, half)

    def fetches(index, unit, part):
        section = unit * layout.together + part
        place = partner(node, section, layout.groups) * layout.members + owner(index)
        return (
            pltpu.make_async_copy(
                values_ref.at[:, pl.ds(pl.multiple_of(place * portion, portion), portion)],
                values.at[index, unit, :, pl.ds(part * portion, portion)],
                value_sems.at[index, unit, part],
            ),
            pltpu.make_async_copy(
                signs_ref.at[pl.ds(pl.multiple_of(place * rows, rows), rows), :],
                flips.at[index, unit, pl.ds(part * rows, rows), :],
                sign_sems.at[index, unit, part],
            ),
        )

    def pieces():
        return [(unit, part) for unit in range(units) for part in range(layout.together)]

    def own_flips():
        own = node * layout.members + member
        return pltpu.make_async_copy(
            signs_ref.at[pl.ds(pl.multiple_of(own * rows, rows), rows), :], flips_ref, flip_sem
        )

    def fetch(index, carry):
        for unit, part in pieces():
            for copy in fetches(index, unit, part):
                copy.start()
        return carry

    lax.fori_loop(0, layout.members, fetch, 0)
    own_flips().start()
    matrix[...] = sylvester()

    def direct(index):
        return pltpu.make_async_copy(coded.at[index, 1], direct_ref.at[owner(index)], out_sems.at[index, 1])

    def paired(index, step):
        return pltpu.make_async_copy(coded.at[index, 0], paired_refs[step].at[index % 2], out_sems.at[index, 0])

    def body(index, carry):
        for unit, part in pieces():
            for copy in fetches(index, unit, part):
                copy.wait()
        for unit in range(units):
            wide = values[index, unit].astype(jnp.float32).reshape(layout.together * rows, LANES)
            turned[unit] = jnp.where(flips[index, unit] == 0, wide, -wide)
            halves = [turned[unit, pl.ds(part, layout.columns, stride=HALVES), :] for part in range(HALVES)]
            signed = jnp.concatenate(halves, axis=1).astype(jnp.bfloat16)
            rotated = lax.dot_general(
                matrix[...], signed, (((1,), (1,)), ((), ())), preferred_element_type=jnp.float32
            )
            for part in range(HALVES):
                coded[index, part, unit] = recode(rotated[part * QGROUP : (part + 1) * QGROUP]).astype(jnp.bfloat16)
        direct(index).start()
        for step in range(half):

            @pl.when(index // 2 == step)
            def _():
                paired(index, step).start()

        return carry

    lax.fori_loop(0, layout.members, body, 0)

    def finish_copies(index, carry):
        direct(index).wait()
        paired(index, 0).wait()
        return carry

    lax.fori_loop(0, layout.members, finish_copies, 0)
    own_flips().wait()


def rotate(values, signs, layout):
    members, units, columns = layout.members, layout.units, layout.columns
    entries = members * layout.groups * layout.portion
    return pl.pallas_call(
        functools.partial(rotate_kernel, layout),
        in_specs=[pl.BlockSpec(memory_space=pl.ANY)] * 2,
        out_specs=[pl.BlockSpec(memory_space=pl.ANY)] * (2 + layout.half),
        out_shape=[
            jax.ShapeDtypeStruct((members,) + layout.shape(), jnp.bfloat16),
            jax.ShapeDtypeStruct((layout.rows, LANES), jnp.int32),
        ]
        + [jax.ShapeDtypeStruct((2,) + layout.shape(), jnp.bfloat16)] * layout.half,
        scratch_shapes=[
            pltpu.VMEM((members, units, 1, layout.together * layout.portion), jnp.bfloat16),
            pltpu.VMEM((members, units, layout.together * layout.rows, LANES), jnp.int32),
            pltpu.VMEM((units, layout.together * layout.rows, LANES), jnp.float32),
            pltpu.VMEM((ROT, ROT), jnp.bfloat16),
            pltpu.VMEM((members, HALVES) + layout.shape(), jnp.bfloat16),
            pltpu.SemaphoreType.DMA((members, units, layout.together)),
            pltpu.SemaphoreType.DMA((members, units, layout.together)),
            pltpu.SemaphoreType.DMA((members, HALVES)),
            pltpu.SemaphoreType.DMA,
        ],
        compiler_params=pltpu.CompilerParams(vmem_limit_bytes=VMEM_LIMIT),
        cost_estimate=pl.CostEstimate(flops=2 * entries * ROT, bytes_accessed=10 * entries, transcendentals=0),
        name="rotate_code",
    )(values, signs)


def add_all(arrays):
    total = arrays[0].astype(jnp.float32)
    for array in arrays[1:]:
        total = total + array.astype(jnp.float32)
    return total


def far_sum_kernel(*refs):
    refs[-1][...] = add_all([ref[0] for ref in refs[:-1]])


def far_sum(paired, layout):
    size = paired[0].size // 2
    return pl.pallas_call(
        far_sum_kernel,
        out_shape=jax.ShapeDtypeStruct(layout.shape(), jnp.float32),
        compiler_params=pltpu.CompilerParams(vmem_limit_bytes=SUM_VMEM_LIMIT),
        cost_estimate=pl.CostEstimate(
            flops=2 * len(paired) * size, bytes_accessed=(2 * len(paired) + 4) * size, transcendentals=0
        ),
        name="far_sum",
    )(*paired)


def write_sections(layout, total, out_refs):
    first = recode(total).astype(jnp.bfloat16)
    for section, out_ref in enumerate(out_refs):
        at = section % layout.together * layout.blocks
        out_ref[...] = first[section // layout.together, :, at : at + layout.blocks]


def direct_sum_kernel(layout, parts_ref, *out_refs):
    write_sections(layout, add_all([parts_ref[member] for member in range(layout.members)]), out_refs)


def paired_sum_kernel(layout, across_ref, *refs):
    near = [ref[1] for ref in refs[: layout.half]]
    write_sections(layout, add_all(near + [across_ref[...]]), refs[layout.half :])


def group_sum(kernel, layout, *parts):
    size = QGROUP * layout.units * layout.columns
    return pl.pallas_call(
        functools.partial(kernel, layout),
        out_shape=[jax.ShapeDtypeStruct((QGROUP, layout.blocks), jnp.bfloat16)] * layout.groups,
        compiler_params=pltpu.CompilerParams(vmem_limit_bytes=SUM_VMEM_LIMIT),
        cost_estimate=pl.CostEstimate(
            flops=30 * size, bytes_accessed=2 * (layout.members + 1) * size, transcendentals=0
        ),
        name="group_sum_code",
    )(*parts)


def bfloat16_terms(values):
    terms = []
    for _ in range(3):
        terms.append(values.astype(jnp.bfloat16))
        values = values - terms[-1].astype(jnp.float32)
    return terms


def finish_kernel(groups, sign_ref, *refs):
    out_ref, max_ref = refs[-2:]
    second = [
        add_all([ref[...] for ref in refs[half * groups : (half + 1) * groups]]) for half in range(HALVES)
    ]
    blocks = second[0].shape[1]
    natural = jnp.concatenate([part.T for part in second], axis=1)
    block = lax.broadcasted_iota(jnp.int32, (blocks, HALVES * blocks), 0)
    lane = lax.broadcasted_iota(jnp.int32, (blocks, HALVES * blocks), 1)
    largest = jnp.zeros((1, HALVES * blocks), jnp.float32)
    for half in range(HALVES):
        peak = jnp.max(jnp.abs(natural[:, half * QGROUP : (half + 1) * QGROUP]), axis=1, keepdims=True)
        chosen = jnp.where(lane == HALVES * block + half, peak, 0.0)
        largest = jnp.maximum(largest, jnp.max(chosen, axis=0, keepdims=True))
    max_ref[...] = largest * jnp.float32(ROT**-0.5)
    matrix = sylvester()
    high, middle, low = [
        jnp.dot(term, matrix, preferred_element_type=jnp.float32) for term in bfloat16_terms(natural)
    ]
    turned = (high + (middle + low)) * jnp.float32(1.0 / ROT)
    for half in range(HALVES):
        at = pl.ds(half, blocks, stride=HALVES)
        part = turned[:, half * QGROUP : (half + 1) * QGROUP]
        out_ref[at, :] = jnp.where(sign_ref[at, :] == 0, part, -part)


def finish(parts, signs):
    groups = len(parts[0])
    rows = signs.shape[0]
    return pl.pallas_call(
        functools.partial(finish_kernel, groups),
        out_shape=[
            jax.ShapeDtypeStruct((rows, LANES), jnp.float32),
            jax.ShapeDtypeStruct((1, rows), jnp.float32),
        ],
        compiler_params=pltpu.CompilerParams(vmem_limit_bytes=SUM_VMEM_LIMIT),
        name="sum_unrotate",
    )(signs, *[part for half in parts for part in half])


def shards(partials, signs):
    length = partials.shape[-1]
    members = lax.axis_size("local")
    groups = lax.axis_size("node")
    layout = Layout(length, members, groups)
    half = layout.half

    def swap(part, step):
        pairs = []
        for source in range(members):
            first, index = source // half * half, source % half
            pairs.append((source, first + partner(index, step, half)))
        return lax.ppermute(part, "local", pairs)

    def share(parts):
        moved = [parts[0]]
        for step in range(1, groups):
            pairs = [(source, partner(source, step, groups)) for source in range(groups)]
            moved.append(lax.ppermute(parts[step], "node", pairs))
        return moved

    direct, own_signs, *paired = rotate(partials.reshape(1, length), signs.reshape(length // LANES, LANES), layout)
    direct = lax.all_to_all(direct, "local", split_axis=0, concat_axis=0, tiled=True)
    paired = paired[:1] + [swap(paired[step], step) for step in range(1, half)]
    counterparts = [(member, (member + half) % members) for member in range(members)]
    across = lax.ppermute(far_sum(paired, layout), "local", counterparts)
    second_half = share(group_sum(direct_sum_kernel, layout, direct))
    first_half = share(group_sum(paired_sum_kernel, layout, across, *paired))
    reduced, rotated_max = finish([first_half, second_half], own_signs)
    return (reduced.reshape(-1), rotated_max.reshape(-1))


def solution(mesh):
    in_specs = (P("node", "local", None), P())
    out_specs = (P(("node", "local")), P(("node", "local")))
    return jax.shard_map(shards, mesh=mesh, in_specs=in_specs, out_specs=out_specs, check_vma=False)
```

time: 63.7 us -> 71.3 us (1.12)
  waiting for transfers between devices: 19 us -> 42.4 us
  Pallas kernels: 17.5 us -> 9.78 us
  starting transfers between devices: 23.4 us -> 17.3 us
  local copies, waits for them, and re-layouts: 2.83 us -> 0.96 us
    ppermute x11 -> x4, waiting for transfers between devices: 16.3 us -> 38.8 us  [the longest x3 27.8 us: swap(): return lax.ppermute(part, 'local', pairs)]
    ppermute x11 -> x4, starting transfers between devices: 19.5 us -> 5.99 us  [the longest x3 3.51 us: swap(): return lax.ppermute(part, 'local', pairs)]
    pallas_call x5 -> x4, Pallas kernels: 16.5 us -> 8.84 us  [the longest x1 8.16 us: rotate(): pl.pallas_call(functools.partial(rotate_kernel, layout), in_specs=[pl.Blo...]
    all_to_all x0 -> x1, starting transfers between devices: none -> 7.41 us  [shards(): lax.all_to_all(direct, 'local', split_axis=0, concat_axis=0, tiled=True)]
    unnamed x12 -> x4, local copies, waits for them, and re-layouts: 1.92 us -> 0.96 us
    dynamic_slice x1 -> x0, local copies, waits for them, and re-layouts: 0.91 us -> none  [shards(): own_signs = lax.dynamic_slice_in_dim(sign_rows, own, layout.rows)]
    ppermute x6, waiting for transfers between devices: 2.71 us -> 3.6 us  [share(): moved.append(lax.ppermute(parts[step], 'node', pairs))]
  transfers between devices with their start and end apart: 17 -> 11, of which waited for: 6 -> 7; matrix products, arithmetic and copies ran while one was open for 1% -> 0% of each run, Pallas kernels for 14% -> 1%
where the time goes in v5:
time: 71.3 us; the launch traced here: 71.1 us
  waiting for transfers between devices  42.4 us (59%)
  starting transfers between devices  17.3 us (24%)
  Pallas kernels  9.78 us (14%)
  local copies, waits for them, and re-layouts  0.96 us (1%)
    ppermute x3, waiting for transfers between devices, swap(): return lax.ppermute(part, 'local', pairs)  27.8 us
    ppermute x1, waiting for transfers between devices, shards(): across = lax.ppermute(far_sum(paired, layout), 'local', counterparts)  11 us
    pallas_call x1, Pallas kernels, rotate(): pl.pallas_call(functools.partial(rotate_kernel, layout), in_specs=[pl.Blo...  8.16 us
    all_to_all x1, starting transfers between devices, shards(): lax.all_to_all(direct, 'local', split_axis=0, concat_axis=0, tiled=True)  7.41 us
    ppermute x6, starting transfers between devices, share(): moved.append(lax.ppermute(parts[step], 'node', pairs))  3.89 us
    ppermute x6, waiting for transfers between devices, share(): moved.append(lax.ppermute(parts[step], 'node', pairs))  3.6 us
    ppermute x3, starting transfers between devices, swap(): return lax.ppermute(part, 'local', pairs)  3.51 us
    ppermute x1, starting transfers between devices, shards(): across = lax.ppermute(far_sum(paired, layout), 'local', counterparts)  2.48 us
  transfers between devices with their start and end apart: 11, of which 7 were waited for; matrix products, arithmetic and copies ran while one was open for 0% of the time, Pallas kernels for 1%

profile of v5, /device:TPU:0, one launch (start us, length us, event | category | flops | bytes accessed | tf_op | source)
XLA Modules:
  0.0 71.1 jit_solution(4554631927518438075)
XLA Ops:
  0.6 8.2 %rotate_code.1 = (bf16[8,4,128,128]{3,2,1,0:T(8,128)(2,1)}, s32[256,128]{1,0:T(8,128)}, bf16[2,4,128,128]{3,2,1,0:T(8,128)(2,1)}, bf16[2,4,128,128]{3,2,1,0:T(8,...) custom-call(bf16[1,1048576]{1,0:T(2,128)(2,1)} %bitcast.4, s32[8192,128]{1,0:T(8,128)} %bitcast.5), custom_call_target="tpu_custom_call" | custom-call | flops 536870912 | bytes 10485760 | tf_op jit(solution)/shard_map/rotate_code/pallas_call | solution.py:157
  8.8 0.0 copy-start.1
  8.8 7.4 %all-to-all-start = ((bf16[8,4,128,128]{3,2,1,0:T(8,128)(2,1)}), bf16[8,4,128,128]{3,2,1,0:T(8,128)(2,1)S(1)}, u32[]{:S(2)}, u32[]{:S(2)}) async-start(bf16[8,4,128,128]{3,2,1,0:T(8,128)(2,1)} %get-tuple-element.27), calls=%async_computation | async-start | bytes 2097152 | tf_op jit(solution)/shard_map/all_to_all | solution.py:306
  16.2 2.0 %collective-permute-start = (bf16[2,4,128,128]{3,2,1,0:T(8,128)(2,1)}, bf16[2,4,128,128]{3,2,1,0:T(8,128)(2,1)S(1)}, u32[]{:S(2)}, u32[]{:S(2)}) collective-permute-start(bf16[2,4,128,128]{3,2,1,0:T(8,128)(2,1)} %get-tuple-element.20), channel_id=1, source_target_pairs={{0,1},{1,0},{2,3},{3,2},{4,5},{5,4},{6,7},{7,6},{8,9},{9,8},{10,11... | collective-permute-start | bytes 786440 | tf_op jit(solution)/shard_map/ppermute | solution.py:296
  18.2 1.5 %collective-permute-start.1 = (bf16[2,4,128,128]{3,2,1,0:T(8,128)(2,1)}, bf16[2,4,128,128]{3,2,1,0:T(8,128)(2,1)S(1)}, u32[]{:S(2)}, u32[]{:S(2)}) collective-permute-start(bf16[2,4,128,128]{3,2,1,0:T(8,128)(2,1)} %get-tuple-element.21), channel_id=1, source_target_pairs={{0,2},{1,3},{2,0},{3,1},{4,6},{5,7},{6,4},{7,5},{8,10},{9,11},{10,... | collective-permute-start | bytes 786440 | tf_op jit(solution)/shard_map/ppermute | solution.py:296
  19.7 0.0 collective-permute-start.2
  19.7 14.3 %collective-permute-done.refs_1_ = bf16[2,4,128,128]{3,2,1,0:T(8,128)(2,1)S(1)} collective-permute-done((bf16[2,4,128,128]{3,2,1,0:T(8,128)(2,1)}, bf16[2,4,128,128]{3,2,1,0:T(8,128)(2,1)S(1)}, u32[]{:S(2)}, u32[]{:S(2)}) %collective-permute-start) | collective-permute-done | bytes 262176 | tf_op jit(solution)/shard_map/ppermute | solution.py:296
  34.1 8.5 %collective-permute-done.1.refs_2_ = bf16[2,4,128,128]{3,2,1,0:T(8,128)(2,1)S(1)} collective-permute-done((bf16[2,4,128,128]{3,2,1,0:T(8,128)(2,1)}, bf16[2,4,128,128]{3,2,1,0:T(8,128)(2,1)S(1)}, u32[]{:S(2)}, u32[]{:S(2)}) %collective-permute-start.1) | collective-permute-done | bytes 262176 | tf_op jit(solution)/shard_map/ppermute | solution.py:296
  42.5 5.0 %collective-permute-done.2.refs_3_ = bf16[2,4,128,128]{3,2,1,0:T(8,128)(2,1)S(1)} collective-permute-done((bf16[2,4,128,128]{3,2,1,0:T(8,128)(2,1)}, bf16[2,4,128,128]{3,2,1,0:T(8,128)(2,1)S(1)}, u32[]{:S(2)}, u32[]{:S(2)}) %collective-permute-start.2) | collective-permute-done | bytes 262176 | tf_op jit(solution)/shard_map/ppermute | solution.py:296
  47.6 0.0 copy-start
  47.6 0.9 %copy-done = bf16[2,4,128,128]{3,2,1,0:T(8,128)(2,1)S(1)} copy-done((bf16[2,4,128,128]{3,2,1,0:T(8,128)(2,1)S(1)}, bf16[2,4,128,128]{3,2,1,0:T(8,128)(2,1)}, u32[]{:S(2)}) %copy-start) | copy-done | bytes 262168
  48.5 0.1 far_sum.1
  48.6 2.5 %collective-permute-start.3 = (f32[4,128,128]{2,1,0:T(8,128)S(1)}, f32[4,128,128]{2,1,0:T(8,128)S(1)}, u32[]{:S(2)}, u32[]{:S(2)}) collective-permute-start(f32[4,128,128]{2,1,0:T(8,128)S(1)} %far_sum.1), channel_id=1, source_target_pairs={{0,4},{1,5},{2,6},{3,7},{4,0},{5,1},{6,2},{7,3},{8,12},{9,13},{10,... | collective-permute-start | bytes 786440 | tf_op jit(solution)/shard_map/ppermute | solution.py:309
  51.1 11.0 %collective-permute-done.3.across_ref = f32[4,128,128]{2,1,0:T(8,128)S(1)} collective-permute-done((f32[4,128,128]{2,1,0:T(8,128)S(1)}, f32[4,128,128]{2,1,0:T(8,128)S(1)}, u32[]{:S(2)}, u32[]{:S(2)}) %collective-permute-start.3) | collective-permute-done | bytes 262176 | tf_op jit(solution)/shard_map/ppermute | solution.py:309
  62.1 0.3 group_sum_code.2
  62.3 0.1 collective-permute-start.4
  62.4 1.6 %collective-permute-start.5 = (bf16[128,128]{1,0:T(8,128)(2,1)S(1)}, bf16[128,128]{1,0:T(8,128)(2,1)S(1)}, u32[]{:S(2)}, u32[]{:S(2)}) collective-permute-start(bf16[128,128]{1,0:T(8,128)(2,1)S(1)} %get-tuple-element.25), channel_id=1, source_target_pairs={{0,16},{8,24},{16,0},{24,8},{1,17},{9,25},{17,1},{25,9},{2,18},{10... | collective-permute-start | bytes 98312 | tf_op jit(solution)/shard_map/ppermute | solution.py:302
  64.0 0.3 collective-permute-start.6
  64.3 0.0 all-to-all-done.parts_ref
  64.3 0.3 group_sum_code.3
  64.6 0.4 collective-permute-start.7
  65.0 1.5 %collective-permute-start.8 = (bf16[128,128]{1,0:T(8,128)(2,1)S(1)}, bf16[128,128]{1,0:T(8,128)(2,1)S(1)}, u32[]{:S(2)}, u32[]{:S(2)}) collective-permute-start(bf16[128,128]{1,0:T(8,128)(2,1)S(1)} %get-tuple-element.30), channel_id=1, source_target_pairs={{0,16},{8,24},{16,0},{24,8},{1,17},{9,25},{17,1},{25,9},{2,18},{10... | collective-permute-start | bytes 98312 | tf_op jit(solution)/shard_map/ppermute | solution.py:302
  66.5 0.0 collective-permute-done.4.refs_1_
  66.5 0.0 collective-permute-start.9
  66.6 0.0 collective-permute-done.5.refs_2_
  66.6 0.7 %collective-permute-done.6.refs_3_ = bf16[128,128]{1,0:T(8,128)(2,1)S(1)} collective-permute-done((bf16[128,128]{1,0:T(8,128)(2,1)S(1)}, bf16[128,128]{1,0:T(8,128)(2,1)S(1)}, u32[]{:S(2)}, u32[]{:S(2)}) %collective-permute-start.6) | collective-permute-done | bytes 32800 | tf_op jit(solution)/shard_map/ppermute | solution.py:302
  67.3 0.0 collective-permute-done.7.refs_5_
  67.3 1.6 %collective-permute-done.8.refs_6_ = bf16[128,128]{1,0:T(8,128)(2,1)S(1)} collective-permute-done((bf16[128,128]{1,0:T(8,128)(2,1)S(1)}, bf16[128,128]{1,0:T(8,128)(2,1)S(1)}, u32[]{:S(2)}, u32[]{:S(2)}) %collective-permute-start.8) | collective-permute-done | bytes 32800 | tf_op jit(solution)/shard_map/ppermute | solution.py:302
  68.9 1.2 %collective-permute-done.9.refs_7_ = bf16[128,128]{1,0:T(8,128)(2,1)S(1)} collective-permute-done((bf16[128,128]{1,0:T(8,128)(2,1)S(1)}, bf16[128,128]{1,0:T(8,128)(2,1)S(1)}, u32[]{:S(2)}, u32[]{:S(2)}) %collective-permute-start.9) | collective-permute-done | bytes 32800 | tf_op jit(solution)/shard_map/ppermute | solution.py:302
  70.2 0.0 copy-done.1
  70.2 0.9 %sum_unrotate.1 = (f32[256,128]{1,0:T(8,128)}, f32[1,256]{1,0:T(1,128)}) custom-call(s32[256,128]{1,0:T(8,128)S(1)} %copy-done.1, bf16[128,128]{1,0:T(8,128)(2,1)S(1)} %get-tuple-element.23.refs_0_, bf16[128,128]{1,0:T(8,128)(2,1)S(1)} %collective-permute-done.4.refs_1_, bf16[128,128]{1,0:T(8,128)(2,1)S(1)} %collective-permute-done.5.refs_2_, ...), custom_call_target="tpu_custom_call" | custom-call | tf_op jit(solution)/shard_map/sum_unrotate/pallas_call | solution.py:273
Async XLA Ops:
  8.8 61.4 %copy-start.1 = (s32[256,128]{1,0:T(8,128)S(1)}, s32[256,128]{1,0:T(8,128)}, u32[]{:S(2)}) copy-start(s32[256,128]{1,0:T(8,128)} %get-tuple-element.18.sign_ref) | copy-start | bytes 393220
  8.8 55.5 %all-to-all-start = ((bf16[8,4,128,128]{3,2,1,0:T(8,128)(2,1)}), bf16[8,4,128,128]{3,2,1,0:T(8,128)(2,1)S(1)}, u32[]{:S(2)}, u32[]{:S(2)}) async-start(bf16[8,4,128,128]{3,2,1,0:T(8,128)(2,1)} %get-tuple-element.27), calls=%async_computation | async-start | bytes 2097152 | tf_op jit(solution)/shard_map/all_to_all | solution.py:306
  16.2 17.8 %collective-permute-start = (bf16[2,4,128,128]{3,2,1,0:T(8,128)(2,1)}, bf16[2,4,128,128]{3,2,1,0:T(8,128)(2,1)S(1)}, u32[]{:S(2)}, u32[]{:S(2)}) collective-permute-start(bf16[2,4,128,128]{3,2,1,0:T(8,128)(2,1)} %get-tuple-element.20), channel_id=1, source_target_pairs={{0,1},{1,0},{2,3},{3,2},{4,5},{5,4},{6,7},{7,6},{8,9},{9,8},{10,11... | collective-permute-start | bytes 786440 | tf_op jit(solution)/shard_map/ppermute | solution.py:296
  18.2 24.3 %collective-permute-start.1 = (bf16[2,4,128,128]{3,2,1,0:T(8,128)(2,1)}, bf16[2,4,128,128]{3,2,1,0:T(8,128)(2,1)S(1)}, u32[]{:S(2)}, u32[]{:S(2)}) collective-permute-start(bf16[2,4,128,128]{3,2,1,0:T(8,128)(2,1)} %get-tuple-element.21), channel_id=1, source_target_pairs={{0,2},{1,3},{2,0},{3,1},{4,6},{5,7},{6,4},{7,5},{8,10},{9,11},{10,... | collective-permute-start | bytes 786440 | tf_op jit(solution)/shard_map/ppermute | solution.py:296
  19.7 27.9 %collective-permute-start.2 = (bf16[2,4,128,128]{3,2,1,0:T(8,128)(2,1)}, bf16[2,4,128,128]{3,2,1,0:T(8,128)(2,1)S(1)}, u32[]{:S(2)}, u32[]{:S(2)}) collective-permute-start(bf16[2,4,128,128]{3,2,1,0:T(8,128)(2,1)} %get-tuple-element.22), channel_id=1, source_target_pairs={{0,3},{1,2},{2,1},{3,0},{4,7},{5,6},{6,5},{7,4},{8,11},{9,10},{10,... | collective-permute-start | bytes 786440 | tf_op jit(solution)/shard_map/ppermute | solution.py:296
  47.6 1.0 %copy-start = (bf16[2,4,128,128]{3,2,1,0:T(8,128)(2,1)S(1)}, bf16[2,4,128,128]{3,2,1,0:T(8,128)(2,1)}, u32[]{:S(2)}) copy-start(bf16[2,4,128,128]{3,2,1,0:T(8,128)(2,1)} %get-tuple-element.19.refs_0_) | copy-start | bytes 786436
  48.6 13.5 %collective-permute-start.3 = (f32[4,128,128]{2,1,0:T(8,128)S(1)}, f32[4,128,128]{2,1,0:T(8,128)S(1)}, u32[]{:S(2)}, u32[]{:S(2)}) collective-permute-start(f32[4,128,128]{2,1,0:T(8,128)S(1)} %far_sum.1), channel_id=1, source_target_pairs={{0,4},{1,5},{2,6},{3,7},{4,0},{5,1},{6,2},{7,3},{8,12},{9,13},{10,... | collective-permute-start | bytes 786440 | tf_op jit(solution)/shard_map/ppermute | solution.py:309
  62.3 4.2 %collective-permute-start.4 = (bf16[128,128]{1,0:T(8,128)(2,1)S(1)}, bf16[128,128]{1,0:T(8,128)(2,1)S(1)}, u32[]{:S(2)}, u32[]{:S(2)}) collective-permute-start(bf16[128,128]{1,0:T(8,128)(2,1)S(1)} %get-tuple-element.24), channel_id=1, source_target_pairs={{0,8},{8,0},{16,24},{24,16},{1,9},{9,1},{17,25},{25,17},{2,10},{10... | collective-permute-start | bytes 98312 | tf_op jit(solution)/shard_map/ppermute | solution.py:302
  62.4 4.2 %collective-permute-start.5 = (bf16[128,128]{1,0:T(8,128)(2,1)S(1)}, bf16[128,128]{1,0:T(8,128)(2,1)S(1)}, u32[]{:S(2)}, u32[]{:S(2)}) collective-permute-start(bf16[128,128]{1,0:T(8,128)(2,1)S(1)} %get-tuple-element.25), channel_id=1, source_target_pairs={{0,16},{8,24},{16,0},{24,8},{1,17},{9,25},{17,1},{25,9},{2,18},{10... | collective-permute-start | bytes 98312 | tf_op jit(solution)/shard_map/ppermute | solution.py:302
  64.0 3.3 %collective-permute-start.6 = (bf16[128,128]{1,0:T(8,128)(2,1)S(1)}, bf16[128,128]{1,0:T(8,128)(2,1)S(1)}, u32[]{:S(2)}, u32[]{:S(2)}) collective-permute-start(bf16[128,128]{1,0:T(8,128)(2,1)S(1)} %get-tuple-element.26), channel_id=1, source_target_pairs={{0,24},{8,16},{16,8},{24,0},{1,25},{9,17},{17,9},{25,1},{2,26},{10... | collective-permute-start | bytes 98312 | tf_op jit(solution)/shard_map/ppermute | solution.py:302
  64.6 2.7 %collective-permute-start.7 = (bf16[128,128]{1,0:T(8,128)(2,1)S(1)}, bf16[128,128]{1,0:T(8,128)(2,1)S(1)}, u32[]{:S(2)}, u32[]{:S(2)}) collective-permute-start(bf16[128,128]{1,0:T(8,128)(2,1)S(1)} %get-tuple-element.29), channel_id=1, source_target_pairs={{0,8},{8,0},{16,24},{24,16},{1,9},{9,1},{17,25},{25,17},{2,10},{10... | collective-permute-start | bytes 98312 | tf_op jit(solution)/shard_map/ppermute | solution.py:302
  65.0 3.9 %collective-permute-start.8 = (bf16[128,128]{1,0:T(8,128)(2,1)S(1)}, bf16[128,128]{1,0:T(8,128)(2,1)S(1)}, u32[]{:S(2)}, u32[]{:S(2)}) collective-permute-start(bf16[128,128]{1,0:T(8,128)(2,1)S(1)} %get-tuple-element.30), channel_id=1, source_target_pairs={{0,16},{8,24},{16,0},{24,8},{1,17},{9,25},{17,1},{25,9},{2,18},{10... | collective-permute-start | bytes 98312 | tf_op jit(solution)/shard_map/ppermute | solution.py:302
  66.5 3.6 %collective-permute-start.9 = (bf16[128,128]{1,0:T(8,128)(2,1)S(1)}, bf16[128,128]{1,0:T(8,128)(2,1)S(1)}, u32[]{:S(2)}, u32[]{:S(2)}) collective-permute-start(bf16[128,128]{1,0:T(8,128)(2,1)S(1)} %get-tuple-element.31), channel_id=1, source_target_pairs={{0,24},{8,16},{16,8},{24,0},{1,25},{9,17},{17,9},{25,1},{2,26},{10... | collective-permute-start | bytes 98312 | tf_op jit(solution)/shard_map/ppermute | solution.py:302

commit v6 on v5

v6 whole, which is shorter than its diff:
```python
import functools
import jax
import jax.numpy as jnp
from jax import lax
from jax.experimental import pallas as pl
from jax.experimental.pallas import tpu as pltpu
from jax.sharding import PartitionSpec as P

ROT = 256
QGROUP = 128
HALVES = ROT // QGROUP
LANES = 128
VMEM_LIMIT = 50 * 1024 * 1024
SUM_VMEM_LIMIT = 24 * 1024 * 1024


def sylvester():
    row = lax.broadcasted_iota(jnp.int32, (ROT, ROT), 0)
    column = lax.broadcasted_iota(jnp.int32, (ROT, ROT), 1)
    parity = lax.population_count(row & column) & 1
    return (1 - 2 * parity).astype(jnp.float32).astype(jnp.bfloat16)


def partner(index, step, count):
    if count & (count - 1) == 0:
        return index ^ step
    return (index + step) % count


def leading_power(x):
    q = x * jnp.float32(2.0**23 + 1.0)
    return q - q * jnp.float32(1.0 - 2.0**-24)


def recode(values):
    magnitude = jnp.abs(values)
    largest = jnp.max(magnitude, axis=-2, keepdims=True)
    least = leading_power(jnp.clip(largest, 2.0**-30, 2.0**30)) * jnp.float32(2.0**-13)
    shift = leading_power(jnp.maximum(magnitude, least)) * jnp.float32(2.0**20)
    nearest = (magnitude + shift) - shift
    rest = magnitude - nearest
    coded = jnp.where(rest == shift * jnp.float32(2.0**-24), magnitude + rest, nearest)
    return jnp.where(values < 0.0, -coded, coded)


class Layout:
    def __init__(self, length, members, groups):
        self.members = members
        self.groups = groups
        self.half = members // 2
        self.portion = length // (members * groups)
        self.rows = self.portion // LANES
        self.blocks = self.portion // ROT
        self.together = 1
        if self.blocks < LANES and LANES % self.blocks == 0 and groups % (LANES // self.blocks) == 0:
            self.together = LANES // self.blocks
        self.units = groups // self.together
        self.columns = self.together * self.blocks

    def shape(self):
        return (self.units, QGROUP, self.columns)


def rotate_kernel(layout, other, values_ref, signs_ref, *refs):
    values, flips, turned, matrix, value_sems, sign_sems = refs[-6:]
    out_refs = refs[:-6]
    half, portion, rows = layout.half, layout.portion, layout.rows
    node = lax.axis_index("node")
    member = lax.axis_index("local")
    inner = lax.rem(member, half)
    first = half - (member - inner) if other else member - inner

    def fetches(unit, part):
        place = partner(node, unit * layout.together + part, layout.groups) * layout.members + first
        return (
            pltpu.make_async_copy(
                values_ref.at[:, pl.ds(pl.multiple_of(place * portion, portion), half * portion)],
                values.at[unit, part],
                value_sems.at[unit, part],
            ),
            pltpu.make_async_copy(
                signs_ref.at[pl.ds(pl.multiple_of(place * rows, rows), half * rows), :],
                flips.at[unit, part],
                sign_sems.at[unit, part],
            ),
        )

    for unit in range(layout.units):
        for part in range(layout.together):
            for copy in fetches(unit, part):
                copy.start()
    matrix[...] = sylvester()

    def body(unit, carry):
        for part in range(layout.together):
            for copy in fetches(unit, part):
                copy.wait()
        for step in range(half):
            owner = partner(inner, step, half)
            at = pl.ds(pl.multiple_of(owner * portion, portion), portion)
            at_rows = pl.ds(pl.multiple_of(owner * rows, rows), rows)
            for part in range(layout.together):
                wide = values[unit, part, :, at].astype(jnp.float32).reshape(rows, LANES)
                turned[step, part * rows : (part + 1) * rows] = jnp.where(
                    flips[unit, part, at_rows, :] == 0, wide, -wide
                )
            halves = [turned[step, pl.ds(part, layout.columns, stride=HALVES), :] for part in range(HALVES)]
            signed = jnp.concatenate(halves, axis=1).astype(jnp.bfloat16)
            rotated = lax.dot_general(
                matrix[...], signed, (((1,), (1,)), ((), ())), preferred_element_type=jnp.float32
            )
            for part in range(HALVES):
                rows_of = slice(part * QGROUP, (part + 1) * QGROUP)
                coded = recode(rotated[rows_of]).astype(jnp.bfloat16)
                if other:
                    out_refs[step * HALVES + part][unit] = coded
                else:
                    out_refs[step][unit, rows_of] = coded
        return carry

    lax.fori_loop(0, layout.units, body, 0)
    if not other:
        out_refs[-1][...] = flips[0, 0, pl.ds(pl.multiple_of(inner * rows, rows), rows), :]


def rotate(values, signs, layout, other):
    half, units, columns = layout.half, layout.units, layout.columns
    entries = half * layout.groups * layout.portion
    if other:
        outs = [jax.ShapeDtypeStruct(layout.shape(), jnp.bfloat16)] * (HALVES * half)
    else:
        outs = [jax.ShapeDtypeStruct((units, ROT, columns), jnp.bfloat16)] * half
        outs.append(jax.ShapeDtypeStruct((layout.rows, LANES), jnp.int32))
    return pl.pallas_call(
        functools.partial(rotate_kernel, layout, other),
        in_specs=[pl.BlockSpec(memory_space=pltpu.HBM)] * 2,
        out_shape=outs,
        scratch_shapes=[
            pltpu.VMEM((units, layout.together, 1, half * layout.portion), jnp.bfloat16),
            pltpu.VMEM((units, layout.together, half * layout.rows, LANES), jnp.int32),
            pltpu.VMEM((half, layout.together * layout.rows, LANES), jnp.float32),
            pltpu.VMEM((ROT, ROT), jnp.bfloat16),
            pltpu.SemaphoreType.DMA((units, layout.together)),
            pltpu.SemaphoreType.DMA((units, layout.together)),
        ],
        compiler_params=pltpu.CompilerParams(vmem_limit_bytes=VMEM_LIMIT),
        cost_estimate=pl.CostEstimate(flops=2 * entries * ROT, bytes_accessed=10 * entries, transcendentals=0),
        name="rotate_code",
    )(values, signs)


def add_all(arrays):
    total = arrays[0].astype(jnp.float32)
    for array in arrays[1:]:
        total = total + array.astype(jnp.float32)
    return total


def far_sum_kernel(*refs):
    refs[-1][...] = add_all([ref[...] for ref in refs[:-1]])


def far_sum(parts, layout):
    size = parts[0].size
    return pl.pallas_call(
        far_sum_kernel,
        out_shape=jax.ShapeDtypeStruct(layout.shape(), jnp.float32),
        compiler_params=pltpu.CompilerParams(vmem_limit_bytes=SUM_VMEM_LIMIT),
        cost_estimate=pl.CostEstimate(
            flops=2 * len(parts) * size, bytes_accessed=(2 * len(parts) + 4) * size, transcendentals=0
        ),
        name="far_sum",
    )(*parts)


def group_sum_kernel(layout, half, across_ref, *refs):
    near = [ref[:, half * QGROUP : (half + 1) * QGROUP] for ref in refs[: layout.half]]
    first = recode(add_all(near + [across_ref[...]])).astype(jnp.bfloat16)
    for section, out_ref in enumerate(refs[layout.half :]):
        at = section % layout.together * layout.blocks
        out_ref[...] = first[section // layout.together, :, at : at + layout.blocks]


def group_sum(near, across, layout, half):
    size = across.size
    return pl.pallas_call(
        functools.partial(group_sum_kernel, layout, half),
        out_shape=[jax.ShapeDtypeStruct((QGROUP, layout.blocks), jnp.bfloat16)] * layout.groups,
        compiler_params=pltpu.CompilerParams(vmem_limit_bytes=SUM_VMEM_LIMIT),
        cost_estimate=pl.CostEstimate(
            flops=30 * size, bytes_accessed=2 * (layout.half + 3) * size, transcendentals=0
        ),
        name="group_sum_code",
    )(across, *near)


def bfloat16_terms(values):
    terms = []
    for _ in range(3):
        terms.append(values.astype(jnp.bfloat16))
        values = values - terms[-1].astype(jnp.float32)
    return terms


def finish_kernel(groups, sign_ref, *refs):
    out_ref, max_ref = refs[-2:]
    second = [
        add_all([ref[...] for ref in refs[half * groups : (half + 1) * groups]]) for half in range(HALVES)
    ]
    blocks = second[0].shape[1]
    natural = jnp.concatenate([part.T for part in second], axis=1)
    block = lax.broadcasted_iota(jnp.int32, (blocks, HALVES * blocks), 0)
    lane = lax.broadcasted_iota(jnp.int32, (blocks, HALVES * blocks), 1)
    largest = jnp.zeros((1, HALVES * blocks), jnp.float32)
    for half in range(HALVES):
        peak = jnp.max(jnp.abs(natural[:, half * QGROUP : (half + 1) * QGROUP]), axis=1, keepdims=True)
        chosen = jnp.where(lane == HALVES * block + half, peak, 0.0)
        largest = jnp.maximum(largest, jnp.max(chosen, axis=0, keepdims=True))
    max_ref[...] = largest * jnp.float32(ROT**-0.5)
    matrix = sylvester()
    high, middle, low = [
        jnp.dot(term, matrix, preferred_element_type=jnp.float32) for term in bfloat16_terms(natural)
    ]
    turned = (high + (middle + low)) * jnp.float32(1.0 / ROT)
    for half in range(HALVES):
        at = pl.ds(half, blocks, stride=HALVES)
        part = turned[:, half * QGROUP : (half + 1) * QGROUP]
        out_ref[at, :] = jnp.where(sign_ref[at, :] == 0, part, -part)


def finish(parts, signs):
    groups = len(parts[0])
    rows = signs.shape[0]
    return pl.pallas_call(
        functools.partial(finish_kernel, groups),
        out_shape=[
            jax.ShapeDtypeStruct((rows, LANES), jnp.float32),
            jax.ShapeDtypeStruct((1, rows), jnp.float32),
        ],
        compiler_params=pltpu.CompilerParams(vmem_limit_bytes=SUM_VMEM_LIMIT),
        name="sum_unrotate",
    )(signs, *[part for half in parts for part in half])


def shards(partials, signs):
    length = partials.shape[-1]
    members = lax.axis_size("local")
    groups = lax.axis_size("node")
    layout = Layout(length, members, groups)
    half = layout.half

    def swap(part, step):
        pairs = []
        for source in range(members):
            first, index = source // half * half, source % half
            pairs.append((source, first + partner(index, step, half)))
        return lax.ppermute(part, "local", pairs)

    def share(parts):
        moved = [parts[0]]
        for step in range(1, groups):
            pairs = [(source, partner(source, step, groups)) for source in range(groups)]
            moved.append(lax.ppermute(parts[step], "node", pairs))
        return moved

    values, sign_rows = partials.reshape(1, length), signs.reshape(length // LANES, LANES)
    counterparts = [(member, (member + half) % members) for member in range(members)]
    far = rotate(values, sign_rows, layout, True)
    across = []
    for part in range(HALVES):
        parts = [far[part]] + [swap(far[HALVES * step + part], step) for step in range(1, half)]
        across.append(lax.ppermute(far_sum(parts, layout), "local", counterparts))
    *near, own_signs = rotate(values, sign_rows, layout, False)
    near = near[:1] + [swap(near[step], step) for step in range(1, half)]
    first_half, second_half = [share(group_sum(near, across[part], layout, part)) for part in range(HALVES)]
    reduced, rotated_max = finish([first_half, second_half], own_signs)
    return (reduced.reshape(-1), rotated_max.reshape(-1))


def solution(mesh):
    in_specs = (P("node", "local", None), P())
    out_specs = (P(("node", "local")), P(("node", "local")))
    return jax.shard_map(shards, mesh=mesh, in_specs=in_specs, out_specs=out_specs, check_vma=False)
```

time: 71.3 us -> 54.1 us (0.76)
  waiting for transfers between devices: 42.4 us -> 15.4 us
  starting transfers between devices: 17.3 us -> 28.4 us
  local copies, waits for them, and re-layouts: 0.96 us -> 0 us
    ppermute x3 -> x9, waiting for transfers between devices: 27.8 us -> 10.1 us  [swap(): return lax.ppermute(part, 'local', pairs)]
    ppermute x3 -> x9, starting transfers between devices: 3.51 us -> 13.4 us  [swap(): return lax.ppermute(part, 'local', pairs)]
    ppermute x1 -> x2, waiting for transfers between devices: 11 us -> 2.26 us  [shards(): across.append(lax.ppermute(far_sum(parts, layout), 'local', counterparts))]
    ppermute x1 -> x2, starting transfers between devices: 2.48 us -> 11.1 us  [shards(): across.append(lax.ppermute(far_sum(parts, layout), 'local', counterparts))]
    all_to_all x1 -> x0, starting transfers between devices: 7.41 us -> none  [shards(): lax.all_to_all(direct, 'local', split_axis=0, concat_axis=0, tiled=True)]
    unnamed x4 -> x0, local copies, waits for them, and re-layouts: 0.96 us -> none
    pallas_call x3 -> x4, Pallas kernels: 8.77 us -> 8.44 us  [the longest x2 7.92 us: rotate(): pl.pallas_call(functools.partial(rotate_kernel, layout, other), in_specs=...]
  transfers between devices with their start and end apart: 11 -> 17, of which waited for: 7 -> 5; matrix products, arithmetic and copies ran while one was open for 0% -> 0% of each run, Pallas kernels for 1% -> 9%
where the time goes in v6:
time: 54.1 us; the launch traced here: 54 us
  starting transfers between devices  28.4 us (52%)
  waiting for transfers between devices  15.4 us (28%)
  Pallas kernels  9.51 us (18%)
  between operations  0.71 us (1%)
    ppermute x9, starting transfers between devices, swap(): return lax.ppermute(part, 'local', pairs)  13.4 us
    ppermute x2, starting transfers between devices, shards(): across.append(lax.ppermute(far_sum(parts, layout), 'local', counterparts))  11.1 us
    ppermute x9, waiting for transfers between devices, swap(): return lax.ppermute(part, 'local', pairs)  10.1 us
    pallas_call x2, Pallas kernels, rotate(): pl.pallas_call(functools.partial(rotate_kernel, layout, other), in_specs=...  7.92 us
    ppermute x6, starting transfers between devices, share(): moved.append(lax.ppermute(parts[step], 'node', pairs))  3.87 us
    ppermute x6, waiting for transfers between devices, share(): moved.append(lax.ppermute(parts[step], 'node', pairs))  3.03 us
    ppermute x2, waiting for transfers between devices, shards(): across.append(lax.ppermute(far_sum(parts, layout), 'local', counterparts))  2.26 us
  transfers between devices with their start and end apart: 17, of which 5 were waited for; matrix products, arithmetic and copies ran while one was open for 0% of the time, Pallas kernels for 9%

profile of v6, /device:TPU:0, one launch (start us, length us, event | category | flops | bytes accessed | tf_op | source)
XLA Modules:
  0.0 54.0 jit_solution(12044826150747332962)
XLA Ops:
  0.6 4.0 %rotate_code.3 = (bf16[4,128,128]{2,1,0:T(8,128)(2,1)S(1)}, bf16[4,128,128]{2,1,0:T(8,128)(2,1)S(1)}, bf16[4,128,128]{2,1,0:T(8,128)(2,1)S(1)}, bf16[4,128,128]{...) custom-call(bf16[1,1048576]{1,0:T(2,128)(2,1)} %bitcast.4, ...), custom_call_target="tpu_custom_call" | custom-call | flops 268435456 | bytes 5242880 | tf_op jit(solution)/shard_map/rotate_code/pallas_call | solution.py:134
  4.6 3.0 %collective-permute-start.10 = (bf16[4,128,128]{2,1,0:T(8,128)(2,1)S(1)}, bf16[4,128,128]{2,1,0:T(8,128)(2,1)S(1)}, u32[]{:S(2)}, u32[]{:S(2)}) collective-permute-start(bf16[4,128,128]{2,1,0:T(8,128)(2,1)S(1)} %get-tuple-element.39), channel_id=1, source_target_pairs={{0,1},{1,0},{2,3},{3,2},{4,5},{5,4},{6,7},{7,6},{8,9},{9,8},{10,11... | collective-permute-start | bytes 393224 | tf_op jit(solution)/shard_map/ppermute | solution.py:257
  7.6 1.6 %collective-permute-start.11 = (bf16[4,128,128]{2,1,0:T(8,128)(2,1)S(1)}, bf16[4,128,128]{2,1,0:T(8,128)(2,1)S(1)}, u32[]{:S(2)}, u32[]{:S(2)}) collective-permute-start(bf16[4,128,128]{2,1,0:T(8,128)(2,1)S(1)} %get-tuple-element.40), channel_id=1, source_target_pairs={{0,2},{1,3},{2,0},{3,1},{4,6},{5,7},{6,4},{7,5},{8,10},{9,11},{10,... | collective-permute-start | bytes 393224 | tf_op jit(solution)/shard_map/ppermute | solution.py:257
  9.2 0.0 collective-permute-start.12
  9.2 1.9 %collective-permute-start = (bf16[4,128,128]{2,1,0:T(8,128)(2,1)S(1)}, bf16[4,128,128]{2,1,0:T(8,128)(2,1)S(1)}, u32[]{:S(2)}, u32[]{:S(2)}) collective-permute-start(bf16[4,128,128]{2,1,0:T(8,128)(2,1)S(1)} %get-tuple-element.27), channel_id=1, source_target_pairs={{0,1},{1,0},{2,3},{3,2},{4,5},{5,4},{6,7},{7,6},{8,9},{9,8},{10,11... | collective-permute-start | bytes 393224 | tf_op jit(solution)/shard_map/ppermute | solution.py:257
  11.1 1.6 %collective-permute-start.1 = (bf16[4,128,128]{2,1,0:T(8,128)(2,1)S(1)}, bf16[4,128,128]{2,1,0:T(8,128)(2,1)S(1)}, u32[]{:S(2)}, u32[]{:S(2)}) collective-permute-start(bf16[4,128,128]{2,1,0:T(8,128)(2,1)S(1)} %get-tuple-element.28), channel_id=1, source_target_pairs={{0,2},{1,3},{2,0},{3,1},{4,6},{5,7},{6,4},{7,5},{8,10},{9,11},{10,... | collective-permute-start | bytes 393224 | tf_op jit(solution)/shard_map/ppermute | solution.py:257
  12.7 0.0 collective-permute-done.10.refs_1_
  12.7 1.7 %collective-permute-start.2 = (bf16[4,128,128]{2,1,0:T(8,128)(2,1)S(1)}, bf16[4,128,128]{2,1,0:T(8,128)(2,1)S(1)}, u32[]{:S(2)}, u32[]{:S(2)}) collective-permute-start(bf16[4,128,128]{2,1,0:T(8,128)(2,1)S(1)} %get-tuple-element.29), channel_id=1, source_target_pairs={{0,3},{1,2},{2,1},{3,0},{4,7},{5,6},{6,5},{7,4},{8,11},{9,10},{10,... | collective-permute-start | bytes 393224 | tf_op jit(solution)/shard_map/ppermute | solution.py:257
  14.4 4.0 %rotate_code.2 = (bf16[4,256,128]{2,1,0:T(8,128)(2,1)S(1)}, bf16[4,256,128]{2,1,0:T(8,128)(2,1)S(1)}, bf16[4,256,128]{2,1,0:T(8,128)(2,1)S(1)}, bf16[4,256,128]{2,1,0:T(8,128)(2,1)S(1)}, s32[256,128]{1,0:T(8,128)S(1)}) custom-call(bf16[1,1048576]{1,0:T(2,128)(2,1)} %bitcast.5, s32[8192,128]{1,0:T(8,128)} %bitcast.7), custom_call_target="tpu_custom_call" | custom-call | flops 268435456 | bytes 5242880 | tf_op jit(solution)/shard_map/rotate_code/pallas_call | solution.py:134
  18.3 0.0 collective-permute-done.11.refs_2_
  18.3 0.6 %collective-permute-start.4 = (bf16[4,256,128]{2,1,0:T(8,128)(2,1)S(1)}, bf16[4,256,128]{2,1,0:T(8,128)(2,1)S(1)}, u32[]{:S(2)}, u32[]{:S(2)}) collective-permute-start(bf16[4,256,128]{2,1,0:T(8,128)(2,1)S(1)} %get-tuple-element.31), channel_id=1, source_target_pairs={{0,1},{1,0},{2,3},{3,2},{4,5},{5,4},{6,7},{7,6},{8,9},{9,8},{10,11... | collective-permute-start | bytes 786440 | tf_op jit(solution)/shard_map/ppermute | solution.py:257
  18.9 0.0 collective-permute-done.12.refs_3_
  18.9 1.3 %collective-permute-start.5 = (bf16[4,256,128]{2,1,0:T(8,128)(2,1)S(1)}, bf16[4,256,128]{2,1,0:T(8,128)(2,1)S(1)}, u32[]{:S(2)}, u32[]{:S(2)}) collective-permute-start(bf16[4,256,128]{2,1,0:T(8,128)(2,1)S(1)} %get-tuple-element.32), channel_id=1, source_target_pairs={{0,2},{1,3},{2,0},{3,1},{4,6},{5,7},{6,4},{7,5},{8,10},{9,11},{10,... | collective-permute-start | bytes 786440 | tf_op jit(solution)/shard_map/ppermute | solution.py:257
  20.2 0.1 far_sum.3
  20.3 0.0 collective-permute-done.refs_1_
  20.3 1.7 %collective-permute-start.6 = (bf16[4,256,128]{2,1,0:T(8,128)(2,1)S(1)}, bf16[4,256,128]{2,1,0:T(8,128)(2,1)S(1)}, u32[]{:S(2)}, u32[]{:S(2)}) collective-permute-start(bf16[4,256,128]{2,1,0:T(8,128)(2,1)S(1)} %get-tuple-element.33), channel_id=1, source_target_pairs={{0,3},{1,2},{2,1},{3,0},{4,7},{5,6},{6,5},{7,4},{8,11},{9,10},{10,... | collective-permute-start | bytes 786440 | tf_op jit(solution)/shard_map/ppermute | solution.py:257
  22.0 0.0 collective-permute-done.1.refs_2_
  22.0 2.6 %collective-permute-start.13 = (f32[4,128,128]{2,1,0:T(8,128)S(1)}, f32[4,128,128]{2,1,0:T(8,128)S(1)}, u32[]{:S(2)}, u32[]{:S(2)}) collective-permute-start(f32[4,128,128]{2,1,0:T(8,128)S(1)} %far_sum.3), channel_id=1, source_target_pairs={{0,4},{1,5},{2,6},{3,7},{4,0},{5,1},{6,2},{7,3},{8,12},{9,13},{10,... | collective-permute-start | bytes 786440 | tf_op jit(solution)/shard_map/ppermute | solution.py:272
  24.6 0.0 collective-permute-done.2.refs_3_
  24.6 0.1 far_sum.2
  24.7 8.5 %collective-permute-start.3 = (f32[4,128,128]{2,1,0:T(8,128)S(1)}, f32[4,128,128]{2,1,0:T(8,128)S(1)}, u32[]{:S(2)}, u32[]{:S(2)}) collective-permute-start(f32[4,128,128]{2,1,0:T(8,128)S(1)} %far_sum.2), channel_id=1, source_target_pairs={{0,4},{1,5},{2,6},{3,7},{4,0},{5,1},{6,2},{7,3},{8,12},{9,13},{10,... | collective-permute-start | bytes 786440 | tf_op jit(solution)/shard_map/ppermute | solution.py:272
  33.2 0.0 collective-permute-done.4.refs_1_
  33.2 4.0 %collective-permute-done.5.refs_2_ = bf16[4,256,128]{2,1,0:T(8,128)(2,1)S(1)} collective-permute-done((bf16[4,256,128]{2,1,0:T(8,128)(2,1)S(1)}, bf16[4,256,128]{2,1,0:T(8,128)(2,1)S(1)}, u32[]{:S(2)}, u32[]{:S(2)}) %collective-permute-start.5) | collective-permute-done | bytes 262176 | tf_op jit(solution)/shard_map/ppermute | solution.py:257
  37.2 6.1 %collective-permute-done.6.refs_3_ = bf16[4,256,128]{2,1,0:T(8,128)(2,1)S(1)} collective-permute-done((bf16[4,256,128]{2,1,0:T(8,128)(2,1)S(1)}, bf16[4,256,128]{2,1,0:T(8,128)(2,1)S(1)}, u32[]{:S(2)}, u32[]{:S(2)}) %collective-permute-start.6) | collective-permute-done | bytes 262176 | tf_op jit(solution)/shard_map/ppermute | solution.py:257
  43.3 0.0 collective-permute-done.13.across_ref
  43.3 0.3 group_sum_code.3
  43.6 0.1 collective-permute-start.14
  43.7 1.7 %collective-permute-start.15 = (bf16[128,128]{1,0:T(8,128)(2,1)S(1)}, bf16[128,128]{1,0:T(8,128)(2,1)S(1)}, u32[]{:S(2)}, u32[]{:S(2)}) collective-permute-start(bf16[128,128]{1,0:T(8,128)(2,1)S(1)} %get-tuple-element.44), channel_id=1, source_target_pairs={{0,16},{8,24},{16,0},{24,8},{1,17},{9,25},{17,1},{25,9},{2,18},{10... | collective-permute-start | bytes 98312 | tf_op jit(solution)/shard_map/ppermute | solution.py:263
  45.3 0.2 collective-permute-start.16
  45.5 2.3 %collective-permute-done.3.across_ref = f32[4,128,128]{2,1,0:T(8,128)S(1)} collective-permute-done((f32[4,128,128]{2,1,0:T(8,128)S(1)}, f32[4,128,128]{2,1,0:T(8,128)S(1)}, u32[]{:S(2)}, u32[]{:S(2)}) %collective-permute-start.3) | collective-permute-done | bytes 262176 | tf_op jit(solution)/shard_map/ppermute | solution.py:272
  47.8 0.3 group_sum_code.2
  48.1 0.1 collective-permute-start.7
  48.1 1.5 %collective-permute-start.8 = (bf16[128,128]{1,0:T(8,128)(2,1)S(1)}, bf16[128,128]{1,0:T(8,128)(2,1)S(1)}, u32[]{:S(2)}, u32[]{:S(2)}) collective-permute-start(bf16[128,128]{1,0:T(8,128)(2,1)S(1)} %get-tuple-element.36), channel_id=1, source_target_pairs={{0,16},{8,24},{16,0},{24,8},{1,17},{9,25},{17,1},{25,9},{2,18},{10... | collective-permute-start | bytes 98312 | tf_op jit(solution)/shard_map/ppermute | solution.py:263
  49.7 0.0 collective-permute-done.14.refs_5_
  49.7 0.3 collective-permute-start.9
  50.0 0.0 collective-permute-done.15.refs_6_
  50.0 0.0 collective-permute-done.16.refs_7_
  50.0 0.0 collective-permute-done.7.refs_1_
  50.0 2.1 %collective-permute-done.8.refs_2_ = bf16[128,128]{1,0:T(8,128)(2,1)S(1)} collective-permute-done((bf16[128,128]{1,0:T(8,128)(2,1)S(1)}, bf16[128,128]{1,0:T(8,128)(2,1)S(1)}, u32[]{:S(2)}, u32[]{:S(2)}) %collective-permute-start.8) | collective-permute-done | bytes 32800 | tf_op jit(solution)/shard_map/ppermute | solution.py:263
  52.1 0.9 %collective-permute-done.9.refs_3_ = bf16[128,128]{1,0:T(8,128)(2,1)S(1)} collective-permute-done((bf16[128,128]{1,0:T(8,128)(2,1)S(1)}, bf16[128,128]{1,0:T(8,128)(2,1)S(1)}, u32[]{:S(2)}, u32[]{:S(2)}) %collective-permute-start.9) | collective-permute-done | bytes 32800 | tf_op jit(solution)/shard_map/ppermute | solution.py:263
  53.0 0.9 %sum_unrotate.1 = (f32[256,128]{1,0:T(8,128)}, f32[1,256]{1,0:T(1,128)}) custom-call(s32[256,128]{1,0:T(8,128)S(1)} %get-tuple-element.25.sign_ref, bf16[128,128]{1,0:T(8,128)(2,1)S(1)} %get-tuple-element.34.refs_0_, bf16[128,128]{1,0:T(8,128)(2,1)S(1)} %collective-permute-done.7.refs_1_, bf16[128,128]{1,0:T(8,128)(2,1)S(1)} %collective-permute-done.8.refs_2_, ...), custom_call_target="tpu_custom_call" | custom-call | tf_op jit(solution)/shard_map/sum_unrotate/pallas_call | solution.py:234
Async XLA Ops:
  4.6 8.1 %collective-permute-start.10 = (bf16[4,128,128]{2,1,0:T(8,128)(2,1)S(1)}, bf16[4,128,128]{2,1,0:T(8,128)(2,1)S(1)}, u32[]{:S(2)}, u32[]{:S(2)}) collective-permute-start(bf16[4,128,128]{2,1,0:T(8,128)(2,1)S(1)} %get-tuple-element.39), channel_id=1, source_target_pairs={{0,1},{1,0},{2,3},{3,2},{4,5},{5,4},{6,7},{7,6},{8,9},{9,8},{10,11... | collective-permute-start | bytes 393224 | tf_op jit(solution)/shard_map/ppermute | solution.py:257
  7.6 10.7 %collective-permute-start.11 = (bf16[4,128,128]{2,1,0:T(8,128)(2,1)S(1)}, bf16[4,128,128]{2,1,0:T(8,128)(2,1)S(1)}, u32[]{:S(2)}, u32[]{:S(2)}) collective-permute-start(bf16[4,128,128]{2,1,0:T(8,128)(2,1)S(1)} %get-tuple-element.40), channel_id=1, source_target_pairs={{0,2},{1,3},{2,0},{3,1},{4,6},{5,7},{6,4},{7,5},{8,10},{9,11},{10,... | collective-permute-start | bytes 393224 | tf_op jit(solution)/shard_map/ppermute | solution.py:257
  9.2 9.7 %collective-permute-start.12 = (bf16[4,128,128]{2,1,0:T(8,128)(2,1)S(1)}, bf16[4,128,128]{2,1,0:T(8,128)(2,1)S(1)}, u32[]{:S(2)}, u32[]{:S(2)}) collective-permute-start(bf16[4,128,128]{2,1,0:T(8,128)(2,1)S(1)} %get-tuple-element.41), channel_id=1, source_target_pairs={{0,3},{1,2},{2,1},{3,0},{4,7},{5,6},{6,5},{7,4},{8,11},{9,10},{10,... | collective-permute-start | bytes 393224 | tf_op jit(solution)/shard_map/ppermute | solution.py:257
  9.2 11.1 %collective-permute-start = (bf16[4,128,128]{2,1,0:T(8,128)(2,1)S(1)}, bf16[4,128,128]{2,1,0:T(8,128)(2,1)S(1)}, u32[]{:S(2)}, u32[]{:S(2)}) collective-permute-start(bf16[4,128,128]{2,1,0:T(8,128)(2,1)S(1)} %get-tuple-element.27), channel_id=1, source_target_pairs={{0,1},{1,0},{2,3},{3,2},{4,5},{5,4},{6,7},{7,6},{8,9},{9,8},{10,11... | collective-permute-start | bytes 393224 | tf_op jit(solution)/shard_map/ppermute | solution.py:257
  11.1 10.9 %collective-permute-start.1 = (bf16[4,128,128]{2,1,0:T(8,128)(2,1)S(1)}, bf16[4,128,128]{2,1,0:T(8,128)(2,1)S(1)}, u32[]{:S(2)}, u32[]{:S(2)}) collective-permute-start(bf16[4,128,128]{2,1,0:T(8,128)(2,1)S(1)} %get-tuple-element.28), channel_id=1, source_target_pairs={{0,2},{1,3},{2,0},{3,1},{4,6},{5,7},{6,4},{7,5},{8,10},{9,11},{10,... | collective-permute-start | bytes 393224 | tf_op jit(solution)/shard_map/ppermute | solution.py:257
  12.7 11.9 %collective-permute-start.2 = (bf16[4,128,128]{2,1,0:T(8,128)(2,1)S(1)}, bf16[4,128,128]{2,1,0:T(8,128)(2,1)S(1)}, u32[]{:S(2)}, u32[]{:S(2)}) collective-permute-start(bf16[4,128,128]{2,1,0:T(8,128)(2,1)S(1)} %get-tuple-element.29), channel_id=1, source_target_pairs={{0,3},{1,2},{2,1},{3,0},{4,7},{5,6},{6,5},{7,4},{8,11},{9,10},{10,... | collective-permute-start | bytes 393224 | tf_op jit(solution)/shard_map/ppermute | solution.py:257
  18.3 14.9 %collective-permute-start.4 = (bf16[4,256,128]{2,1,0:T(8,128)(2,1)S(1)}, bf16[4,256,128]{2,1,0:T(8,128)(2,1)S(1)}, u32[]{:S(2)}, u32[]{:S(2)}) collective-permute-start(bf16[4,256,128]{2,1,0:T(8,128)(2,1)S(1)} %get-tuple-element.31), channel_id=1, source_target_pairs={{0,1},{1,0},{2,3},{3,2},{4,5},{5,4},{6,7},{7,6},{8,9},{9,8},{10,11... | collective-permute-start | bytes 786440 | tf_op jit(solution)/shard_map/ppermute | solution.py:257
  18.9 18.3 %collective-permute-start.5 = (bf16[4,256,128]{2,1,0:T(8,128)(2,1)S(1)}, bf16[4,256,128]{2,1,0:T(8,128)(2,1)S(1)}, u32[]{:S(2)}, u32[]{:S(2)}) collective-permute-start(bf16[4,256,128]{2,1,0:T(8,128)(2,1)S(1)} %get-tuple-element.32), channel_id=1, source_target_pairs={{0,2},{1,3},{2,0},{3,1},{4,6},{5,7},{6,4},{7,5},{8,10},{9,11},{10,... | collective-permute-start | bytes 786440 | tf_op jit(solution)/shard_map/ppermute | solution.py:257
  20.3 23.0 %collective-permute-start.6 = (bf16[4,256,128]{2,1,0:T(8,128)(2,1)S(1)}, bf16[4,256,128]{2,1,0:T(8,128)(2,1)S(1)}, u32[]{:S(2)}, u32[]{:S(2)}) collective-permute-start(bf16[4,256,128]{2,1,0:T(8,128)(2,1)S(1)} %get-tuple-element.33), channel_id=1, source_target_pairs={{0,3},{1,2},{2,1},{3,0},{4,7},{5,6},{6,5},{7,4},{8,11},{9,10},{10,... | collective-permute-start | bytes 786440 | tf_op jit(solution)/shard_map/ppermute | solution.py:257
  22.0 21.3 %collective-permute-start.13 = (f32[4,128,128]{2,1,0:T(8,128)S(1)}, f32[4,128,128]{2,1,0:T(8,128)S(1)}, u32[]{:S(2)}, u32[]{:S(2)}) collective-permute-start(f32[4,128,128]{2,1,0:T(8,128)S(1)} %far_sum.3), channel_id=1, source_target_pairs={{0,4},{1,5},{2,6},{3,7},{4,0},{5,1},{6,2},{7,3},{8,12},{9,13},{10,... | collective-permute-start | bytes 786440 | tf_op jit(solution)/shard_map/ppermute | solution.py:272
  24.7 23.1 %collective-permute-start.3 = (f32[4,128,128]{2,1,0:T(8,128)S(1)}, f32[4,128,128]{2,1,0:T(8,128)S(1)}, u32[]{:S(2)}, u32[]{:S(2)}) collective-permute-start(f32[4,128,128]{2,1,0:T(8,128)S(1)} %far_sum.2), channel_id=1, source_target_pairs={{0,4},{1,5},{2,6},{3,7},{4,0},{5,1},{6,2},{7,3},{8,12},{9,13},{10,... | collective-permute-start | bytes 786440 | tf_op jit(solution)/shard_map/ppermute | solution.py:272
  43.6 6.1 %collective-permute-start.14 = (bf16[128,128]{1,0:T(8,128)(2,1)S(1)}, bf16[128,128]{1,0:T(8,128)(2,1)S(1)}, u32[]{:S(2)}, u32[]{:S(2)}) collective-permute-start(bf16[128,128]{1,0:T(8,128)(2,1)S(1)} %get-tuple-element.43), channel_id=1, source_target_pairs={{0,8},{8,0},{16,24},{24,16},{1,9},{9,1},{17,25},{25,17},{2,10},{10... | collective-permute-start | bytes 98312 | tf_op jit(solution)/shard_map/ppermute | solution.py:263
  43.7 6.3 %collective-permute-start.15 = (bf16[128,128]{1,0:T(8,128)(2,1)S(1)}, bf16[128,128]{1,0:T(8,128)(2,1)S(1)}, u32[]{:S(2)}, u32[]{:S(2)}) collective-permute-start(bf16[128,128]{1,0:T(8,128)(2,1)S(1)} %get-tuple-element.44), channel_id=1, source_target_pairs={{0,16},{8,24},{16,0},{24,8},{1,17},{9,25},{17,1},{25,9},{2,18},{10... | collective-permute-start | bytes 98312 | tf_op jit(solution)/shard_map/ppermute | solution.py:263
  45.3 4.7 %collective-permute-start.16 = (bf16[128,128]{1,0:T(8,128)(2,1)S(1)}, bf16[128,128]{1,0:T(8,128)(2,1)S(1)}, u32[]{:S(2)}, u32[]{:S(2)}) collective-permute-start(bf16[128,128]{1,0:T(8,128)(2,1)S(1)} %get-tuple-element.45), channel_id=1, source_target_pairs={{0,24},{8,16},{16,8},{24,0},{1,25},{9,17},{17,9},{25,1},{2,26},{10... | collective-permute-start | bytes 98312 | tf_op jit(solution)/shard_map/ppermute | solution.py:263
  48.1 2.0 %collective-permute-start.7 = (bf16[128,128]{1,0:T(8,128)(2,1)S(1)}, bf16[128,128]{1,0:T(8,128)(2,1)S(1)}, u32[]{:S(2)}, u32[]{:S(2)}) collective-permute-start(bf16[128,128]{1,0:T(8,128)(2,1)S(1)} %get-tuple-element.35), channel_id=1, source_target_pairs={{0,8},{8,0},{16,24},{24,16},{1,9},{9,1},{17,25},{25,17},{2,10},{10... | collective-permute-start | bytes 98312 | tf_op jit(solution)/shard_map/ppermute | solution.py:263
  48.1 4.0 %collective-permute-start.8 = (bf16[128,128]{1,0:T(8,128)(2,1)S(1)}, bf16[128,128]{1,0:T(8,128)(2,1)S(1)}, u32[]{:S(2)}, u32[]{:S(2)}) collective-permute-start(bf16[128,128]{1,0:T(8,128)(2,1)S(1)} %get-tuple-element.36), channel_id=1, source_target_pairs={{0,16},{8,24},{16,0},{24,8},{1,17},{9,25},{17,1},{25,9},{2,18},{10... | collective-permute-start | bytes 98312 | tf_op jit(solution)/shard_map/ppermute | solution.py:263
  49.7 3.3 %collective-permute-start.9 = (bf16[128,128]{1,0:T(8,128)(2,1)S(1)}, bf16[128,128]{1,0:T(8,128)(2,1)S(1)}, u32[]{:S(2)}, u32[]{:S(2)}) collective-permute-start(bf16[128,128]{1,0:T(8,128)(2,1)S(1)} %get-tuple-element.37), channel_id=1, source_target_pairs={{0,24},{8,16},{16,8},{24,0},{1,25},{9,17},{17,9},{25,1},{2,26},{10... | collective-permute-start | bytes 98312 | tf_op jit(solution)/shard_map/ppermute | solution.py:263

commit v7 on v6

--- a/solution.py
+++ b/solution.py
@@ -12,6 +12,7 @@
 LANES = 128
 VMEM_LIMIT = 50 * 1024 * 1024
 SUM_VMEM_LIMIT = 24 * 1024 * 1024
+AHEAD = 2
 
 
 def sylvester():
@@ -60,10 +61,14 @@
     def shape(self):
         return (self.units, QGROUP, self.columns)
 
+    def cuts(self, step, other):
+        return HALVES if other and self.half > 1 and step == self.half // 2 else 1
+
 
 def rotate_kernel(layout, other, values_ref, signs_ref, *refs):
     values, flips, turned, matrix, value_sems, sign_sems = refs[-6:]
-    out_refs = refs[:-6]
+    out_refs = list(refs[:-6])
+    step_refs = [[out_refs.pop(0) for _ in range(layout.cuts(step, other))] for step in range(layout.half)]
     half, portion, rows = layout.half, layout.portion, layout.rows
     node = lax.axis_index("node")
     member = lax.axis_index("local")
@@ -85,16 +90,24 @@
             ),
         )
 
-    for unit in range(layout.units):
+    def fetch(unit):
         for part in range(layout.together):
             for copy in fetches(unit, part):
                 copy.start()
+
+    for unit in range(min(AHEAD, layout.units)):
+        fetch(unit)
     matrix[...] = sylvester()
 
     def body(unit, carry):
         for part in range(layout.together):
             for copy in fetches(unit, part):
                 copy.wait()
+
+        @pl.when(unit + AHEAD < layout.units)
+        def _():
+            fetch(unit + AHEAD)
+
         for step in range(half):
             owner = partner(inner, step, half)
             at = pl.ds(pl.multiple_of(owner * portion, portion), portion)
@@ -112,24 +125,25 @@
             for part in range(HALVES):
                 rows_of = slice(part * QGROUP, (part + 1) * QGROUP)
                 coded = recode(rotated[rows_of]).astype(jnp.bfloat16)
-                if other:
-                    out_refs[step * HALVES + part][unit] = coded
+                if len(step_refs[step]) > 1:
+                    step_refs[step][part][unit] = coded
                 else:
-                    out_refs[step][unit, rows_of] = coded
+                    step_refs[step][0][unit, rows_of] = coded
         return carry
 
     lax.fori_loop(0, layout.units, body, 0)
     if not other:
-        out_refs[-1][...] = flips[0, 0, pl.ds(pl.multiple_of(inner * rows, rows), rows), :]
+        out_refs[0][...] = flips[0, 0, pl.ds(pl.multiple_of(inner * rows, rows), rows), :]
 
 
 def rotate(values, signs, layout, other):
     half, units, columns = layout.half, layout.units, layout.columns
     entries = half * layout.groups * layout.portion
-    if other:
-        outs = [jax.ShapeDtypeStruct(layout.shape(), jnp.bfloat16)] * (HALVES * half)
-    else:
-        outs = [jax.ShapeDtypeStruct((units, ROT, columns), jnp.bfloat16)] * half
+    outs = []
+    for step in range(half):
+        cuts = layout.cuts(step, other)
+        outs += [jax.ShapeDtypeStruct((units, ROT // cuts, columns), jnp.bfloat16)] * cuts
+    if not other:
         outs.append(jax.ShapeDtypeStruct((layout.rows, LANES), jnp.int32))
     return pl.pallas_call(
         functools.partial(rotate_kernel, layout, other),
@@ -156,42 +170,54 @@
     return total
 
 
-def far_sum_kernel(*refs):
-    refs[-1][...] = add_all([ref[...] for ref in refs[:-1]])
-
-
-def far_sum(parts, layout):
-    size = parts[0].size
-    return pl.pallas_call(
-        far_sum_kernel,
-        out_shape=jax.ShapeDtypeStruct(layout.shape(), jnp.float32),
+def far_sum_kernel(part, count, *refs):
+    arrays = []
+    for ref in refs[:count]:
+        cut = ref.shape[1] == QGROUP
+        arrays.append(ref[...] if cut else ref[:, part * QGROUP : (part + 1) * QGROUP])
+    refs[-1][...] = add_all(arrays)
+
+
+def far_sum(parts, layout, part, later):
+    size = QGROUP * layout.units * layout.columns
+    *later, total = pl.pallas_call(
+        functools.partial(far_sum_kernel, part, len(parts)),
+        in_specs=[pl.BlockSpec(memory_space=pltpu.VMEM)] * len(parts)
+        + [pl.BlockSpec(memory_space=pl.ANY)] * len(later),
+        out_specs=[pl.BlockSpec(memory_space=pl.ANY)] * len(later) + [pl.BlockSpec(memory_space=pltpu.VMEM)],
+        out_shape=[jax.ShapeDtypeStruct(array.shape, array.dtype) for array in later]
+        + [jax.ShapeDtypeStruct(layout.shape(), jnp.float32)],
+        input_output_aliases={len(parts) + index: index for index in range(len(later))},
         compiler_params=pltpu.CompilerParams(vmem_limit_bytes=SUM_VMEM_LIMIT),
         cost_estimate=pl.CostEstimate(
             flops=2 * len(parts) * size, bytes_accessed=(2 * len(parts) + 4) * size, transcendentals=0
         ),
         name="far_sum",
-    )(*parts)
-
-
-def group_sum_kernel(layout, half, across_ref, *refs):
-    near = [ref[:, half * QGROUP : (half + 1) * QGROUP] for ref in refs[: layout.half]]
-    first = recode(add_all(near + [across_ref[...]])).astype(jnp.bfloat16)
-    for section, out_ref in enumerate(refs[layout.half :]):
-        at = section % layout.together * layout.blocks
-        out_ref[...] = first[section // layout.together, :, at : at + layout.blocks]
-
-
-def group_sum(near, across, layout, half):
-    size = across.size
+    )(*parts, *later)
+    return total, later
+
+
+def group_sum_kernel(layout, *refs):
+    across_refs, near_refs, out_refs = refs[:HALVES], refs[HALVES : HALVES + layout.half], refs[HALVES + layout.half :]
+    for half, across_ref in enumerate(across_refs):
+        near = [ref[:, half * QGROUP : (half + 1) * QGROUP] for ref in near_refs]
+        first = recode(add_all(near + [across_ref[...]])).astype(jnp.bfloat16)
+        for section, out_ref in enumerate(out_refs):
+            at = section % layout.together * layout.blocks
+            out_ref[half] = first[section // layout.together, :, at : at + layout.blocks]
+
+
+def group_sum(near, across, layout):
+    size = ROT * layout.units * layout.columns
     return pl.pallas_call(
-        functools.partial(group_sum_kernel, layout, half),
-        out_shape=[jax.ShapeDtypeStruct((QGROUP, layout.blocks), jnp.bfloat16)] * layout.groups,
+        functools.partial(group_sum_kernel, layout),
+        out_shape=[jax.ShapeDtypeStruct((HALVES, QGROUP, layout.blocks), jnp.bfloat16)] * layout.groups,
         compiler_params=pltpu.CompilerParams(vmem_limit_bytes=SUM_VMEM_LIMIT),
         cost_estimate=pl.CostEstimate(
             flops=30 * size, bytes_accessed=2 * (layout.half + 3) * size, transcendentals=0
         ),
         name="group_sum_code",
-    )(across, *near)
+    )(*across, *near)
 
 
 def bfloat16_terms(values):
@@ -202,11 +228,9 @@
     return terms
 
 
-def finish_kernel(groups, sign_ref, *refs):
+def finish_kernel(sign_ref, *refs):
     out_ref, max_ref = refs[-2:]
-    second = [
-        add_all([ref[...] for ref in refs[half * groups : (half + 1) * groups]]) for half in range(HALVES)
-    ]
+    second = [add_all([ref[half] for ref in refs[:-2]]) for half in range(HALVES)]
     blocks = second[0].shape[1]
     natural = jnp.concatenate([part.T for part in second], axis=1)
     block = lax.broadcasted_iota(jnp.int32, (blocks, HALVES * blocks), 0)
@@ -229,17 +253,16 @@
 
 
 def finish(parts, signs):
-    groups = len(parts[0])
     rows = signs.shape[0]
     return pl.pallas_call(
-        functools.partial(finish_kernel, groups),
+        finish_kernel,
         out_shape=[
             jax.ShapeDtypeStruct((rows, LANES), jnp.float32),
             jax.ShapeDtypeStruct((1, rows), jnp.float32),
         ],
         compiler_params=pltpu.CompilerParams(vmem_limit_bytes=SUM_VMEM_LIMIT),
         name="sum_unrotate",
-    )(signs, *[part for half in parts for part in half])
+    )(signs, *parts)
 
 
 def shards(partials, signs):
@@ -265,15 +288,26 @@
 
     values, sign_rows = partials.reshape(1, length), signs.reshape(length // LANES, LANES)
     counterparts = [(member, (member + half) % members) for member in range(members)]
-    far = rotate(values, sign_rows, layout, True)
+    steps = list(range(half - 1, 0, -1))
+    outs = list(rotate(values, sign_rows, layout, True))
+    far = [[outs.pop(0) for _ in range(layout.cuts(step, True))] for step in range(half)]
+    last = []
+    for step in steps:
+        far[step][0] = swap(far[step][0], step)
+        last += [step] if len(far[step]) > 1 else []
+    for step in last:
+        far[step][1] = swap(far[step][1], step)
+    *near, own_signs = rotate(values, sign_rows, layout, False)
     across = []
     for part in range(HALVES):
-        parts = [far[part]] + [swap(far[HALVES * step + part], step) for step in range(1, half)]
-        across.append(lax.ppermute(far_sum(parts, layout), "local", counterparts))
-    *near, own_signs = rotate(values, sign_rows, layout, False)
-    near = near[:1] + [swap(near[step], step) for step in range(1, half)]
-    first_half, second_half = [share(group_sum(near, across[part], layout, part)) for part in range(HALVES)]
-    reduced, rotated_max = finish([first_half, second_half], own_signs)
+        later = near[1:] if part == 0 else []
+        total, later = far_sum([arrays[min(part, len(arrays) - 1)] for arrays in far], layout, part, later)
+        across.append(lax.ppermute(total, "local", counterparts))
+        if part == 0:
+            near = near[:1] + later
+    for step in steps:
+        near[step] = swap(near[step], step)
+    reduced, rotated_max = finish(share(group_sum(near, across, layout)), own_signs)
     return (reduced.reshape(-1), rotated_max.reshape(-1))
 
 

time: 54.1 us -> 53.7 us (level)
  starting transfers between devices: 28.4 us -> 15.3 us
  waiting for transfers between devices: 15.4 us -> 28 us
    ppermute x2, starting transfers between devices: 11.1 us -> 3.06 us  [shards(): across.append(lax.ppermute(total, 'local', counterparts))]
    ppermute x2, waiting for transfers between devices: 2.26 us -> 8.62 us  [shards(): across.append(lax.ppermute(total, 'local', counterparts))]
    ppermute x9 -> x7, waiting for transfers between devices: 10.1 us -> 15.9 us  [swap(): return lax.ppermute(part, 'local', pairs)]
    ppermute x9 -> x7, starting transfers between devices: 13.4 us -> 10.1 us  [swap(): return lax.ppermute(part, 'local', pairs)]
    ppermute x6 -> x3, starting transfers between devices: 3.87 us -> 2.21 us  [share(): moved.append(lax.ppermute(parts[step], 'node', pairs))]
    ppermute x6 -> x3, waiting for transfers between devices: 3.03 us -> 3.53 us  [share(): moved.append(lax.ppermute(parts[step], 'node', pairs))]
    pallas_call x5 -> x4, Pallas kernels: 1.59 us -> 1.58 us  [the longest x1 0.94 us: finish(): pl.pallas_call(finish_kernel, out_shape=[jax.ShapeDtypeStruct((rows, LANE...]
  transfers between devices with their start and end apart: 17 -> 12, of which waited for: 5 -> 7; matrix products, arithmetic and copies ran while one was open for 0% -> 0% of each run, Pallas kernels for 9% -> 8%
where the time goes in v7:
time: 53.7 us; the launch traced here: 53.5 us
  waiting for transfers between devices  28 us (52%)
  starting transfers between devices  15.3 us (28%)
  Pallas kernels  9.48 us (18%)
  between operations  0.67 us (1%)
    ppermute x7, waiting for transfers between devices, swap(): return lax.ppermute(part, 'local', pairs)  15.9 us
    ppermute x7, starting transfers between devices, swap(): return lax.ppermute(part, 'local', pairs)  10.1 us
    ppermute x2, waiting for transfers between devices, shards(): across.append(lax.ppermute(total, 'local', counterparts))  8.62 us
    pallas_call x2, Pallas kernels, rotate(): pl.pallas_call(functools.partial(rotate_kernel, layout, other), in_specs=...  7.9 us
    ppermute x3, waiting for transfers between devices, share(): moved.append(lax.ppermute(parts[step], 'node', pairs))  3.53 us
    ppermute x2, starting transfers between devices, shards(): across.append(lax.ppermute(total, 'local', counterparts))  3.06 us
    ppermute x3, starting transfers between devices, share(): moved.append(lax.ppermute(parts[step], 'node', pairs))  2.21 us
  transfers between devices with their start and end apart: 12, of which 7 were waited for; matrix products, arithmetic and copies ran while one was open for 0% of the time, Pallas kernels for 8%

profile of v7, /device:TPU:0, one launch (start us, length us, event | category | flops | bytes accessed | tf_op | source)
XLA Modules:
  0.0 53.5 jit_solution(4503999658827752818)
XLA Ops:
  0.6 4.0 %rotate_code.3 = (bf16[4,256,128]{2,1,0:T(8,128)(2,1)S(1)}, bf16[4,256,128]{2,1,0:T(8,128)(2,1)S(1)}, bf16[4,128,128]{2,1,0:T(8,128)(2,1)S(1)}, bf16[4,128,128]{2,1,0:T(8,128)(2,1)S(1)}, bf16[4,256,128]{2,1,0:T(8,128)(2,1)S(1)}) custom-call(bf16[1,1048576]{1,0:T(2,128)(2,1)} %bitcast.4, s32[8192,128]{1,0:T(8,128)} %bitcast.6), custom_call_target="tpu_custom_call" | custom-call | flops 268435456 | bytes 5242880 | tf_op jit(solution)/shard_map/rotate_code/pallas_call | solution.py:148
  4.6 3.0 %collective-permute-start = (bf16[4,256,128]{2,1,0:T(8,128)(2,1)S(1)}, bf16[4,256,128]{2,1,0:T(8,128)(2,1)S(1)}, u32[]{:S(2)}, u32[]{:S(2)}) collective-permute-start(bf16[4,256,128]{2,1,0:T(8,128)(2,1)S(1)} %get-tuple-element.24), channel_id=1, source_target_pairs={{0,1},{1,0},{2,3},{3,2},{4,5},{5,4},{6,7},{7,6},{8,9},{9,8},{10,11... | collective-permute-start | bytes 786440 | tf_op jit(solution)/shard_map/ppermute | solution.py:280
  7.6 1.5 %collective-permute-start.2 = (bf16[4,256,128]{2,1,0:T(8,128)(2,1)S(1)}, bf16[4,256,128]{2,1,0:T(8,128)(2,1)S(1)}, u32[]{:S(2)}, u32[]{:S(2)}) collective-permute-start(bf16[4,256,128]{2,1,0:T(8,128)(2,1)S(1)} %get-tuple-element.26), channel_id=1, source_target_pairs={{0,3},{1,2},{2,1},{3,0},{4,7},{5,6},{6,5},{7,4},{8,11},{9,10},{10,... | collective-permute-start | bytes 786440 | tf_op jit(solution)/shard_map/ppermute | solution.py:280
  9.1 0.1 collective-permute-start.1
  9.2 2.0 %collective-permute-start.4 = (bf16[4,128,128]{2,1,0:T(8,128)(2,1)S(1)}, bf16[4,128,128]{2,1,0:T(8,128)(2,1)S(1)}, u32[]{:S(2)}, u32[]{:S(2)}) collective-permute-start(bf16[4,128,128]{2,1,0:T(8,128)(2,1)S(1)} %get-tuple-element.31), channel_id=1, source_target_pairs={{0,2},{1,3},{2,0},{3,1},{4,6},{5,7},{6,4},{7,5},{8,10},{9,11},{10,... | collective-permute-start | bytes 393224 | tf_op jit(solution)/shard_map/ppermute | solution.py:280
  11.2 3.9 %rotate_code.2 = (bf16[4,256,128]{2,1,0:T(8,128)(2,1)S(1)}, bf16[4,256,128]{2,1,0:T(8,128)(2,1)S(1)}, bf16[4,256,128]{2,1,0:T(8,128)(2,1)S(1)}, bf16[4,256,128]{2,1,0:T(8,128)(2,1)S(1)}, s32[256,128]{1,0:T(8,128)S(1)}) custom-call(bf16[1,1048576]{1,0:T(2,128)(2,1)} %bitcast.5, s32[8192,128]{1,0:T(8,128)} %bitcast.7), custom_call_target="tpu_custom_call" | custom-call | flops 268435456 | bytes 5242880 | tf_op jit(solution)/shard_map/rotate_code/pallas_call | solution.py:148
  15.1 4.1 %collective-permute-done.1.refs_2_ = bf16[4,128,128]{2,1,0:T(8,128)(2,1)S(1)} collective-permute-done((bf16[4,128,128]{2,1,0:T(8,128)(2,1)S(1)}, bf16[4,128,128]{2,1,0:T(8,128)(2,1)S(1)}, u32[]{:S(2)}, u32[]{:S(2)}) %collective-permute-start.1) | collective-permute-done | bytes 131104 | tf_op jit(solution)/shard_map/ppermute | solution.py:280
  19.2 0.4 collective-permute-done.refs_1_
  19.5 0.0 collective-permute-done.2.refs_3_
  19.5 0.1 far_sum.2
  19.6 2.9 %collective-permute-start.3 = (f32[4,128,128]{2,1,0:T(8,128)S(1)}, f32[4,128,128]{2,1,0:T(8,128)S(1)}, u32[]{:S(2)}, u32[]{:S(2)}) collective-permute-start(f32[4,128,128]{2,1,0:T(8,128)S(1)} %get-tuple-element.30), channel_id=1, source_target_pairs={{0,4},{1,5},{2,6},{3,7},{4,0},{5,1},{6,2},{7,3},{8,12},{9,13},{10,... | collective-permute-start | bytes 786440 | tf_op jit(solution)/shard_map/ppermute | solution.py:305
  22.5 1.5 %collective-permute-start.6 = (bf16[4,256,128]{2,1,0:T(8,128)(2,1)S(1)}, bf16[4,256,128]{2,1,0:T(8,128)(2,1)S(1)}, u32[]{:S(2)}, u32[]{:S(2)}) collective-permute-start(bf16[4,256,128]{2,1,0:T(8,128)(2,1)S(1)} %get-tuple-element.33), channel_id=1, source_target_pairs={{0,1},{1,0},{2,3},{3,2},{4,5},{5,4},{6,7},{7,6},{8,9},{9,8},{10,11... | collective-permute-start | bytes 786440 | tf_op jit(solution)/shard_map/ppermute | solution.py:280
  24.0 1.6 %collective-permute-start.7 = (bf16[4,256,128]{2,1,0:T(8,128)(2,1)S(1)}, bf16[4,256,128]{2,1,0:T(8,128)(2,1)S(1)}, u32[]{:S(2)}, u32[]{:S(2)}) collective-permute-start(bf16[4,256,128]{2,1,0:T(8,128)(2,1)S(1)} %get-tuple-element.34), channel_id=1, source_target_pairs={{0,2},{1,3},{2,0},{3,1},{4,6},{5,7},{6,4},{7,5},{8,10},{9,11},{10,... | collective-permute-start | bytes 786440 | tf_op jit(solution)/shard_map/ppermute | solution.py:280
  25.6 0.4 collective-permute-start.8
  26.0 0.0 collective-permute-done.4.refs_2_
  26.0 0.1 far_sum.3
  26.1 0.2 collective-permute-start.5
  26.2 8.6 %collective-permute-done.3.refs_0_ = f32[4,128,128]{2,1,0:T(8,128)S(1)} collective-permute-done((f32[4,128,128]{2,1,0:T(8,128)S(1)}, f32[4,128,128]{2,1,0:T(8,128)S(1)}, u32[]{:S(2)}, u32[]{:S(2)}) %collective-permute-start.3) | collective-permute-done | bytes 262176 | tf_op jit(solution)/shard_map/ppermute | solution.py:305
  34.9 0.0 collective-permute-done.6.refs_3_
  34.9 8.4 %collective-permute-done.7.refs_4_ = bf16[4,256,128]{2,1,0:T(8,128)(2,1)S(1)} collective-permute-done((bf16[4,256,128]{2,1,0:T(8,128)(2,1)S(1)}, bf16[4,256,128]{2,1,0:T(8,128)(2,1)S(1)}, u32[]{:S(2)}, u32[]{:S(2)}) %collective-permute-start.7) | collective-permute-done | bytes 262176 | tf_op jit(solution)/shard_map/ppermute | solution.py:280
  43.2 3.1 %collective-permute-done.8.refs_5_ = bf16[4,256,128]{2,1,0:T(8,128)(2,1)S(1)} collective-permute-done((bf16[4,256,128]{2,1,0:T(8,128)(2,1)S(1)}, bf16[4,256,128]{2,1,0:T(8,128)(2,1)S(1)}, u32[]{:S(2)}, u32[]{:S(2)}) %collective-permute-start.8) | collective-permute-done | bytes 262176 | tf_op jit(solution)/shard_map/ppermute | solution.py:280
  46.3 0.0 collective-permute-done.5.refs_1_
  46.3 0.5 group_sum_code.1
  46.8 1.5 %collective-permute-start.10 = (bf16[2,128,128]{2,1,0:T(8,128)(2,1)S(1)}, bf16[2,128,128]{2,1,0:T(8,128)(2,1)S(1)}, u32[]{:S(2)}, u32[]{:S(2)}) collective-permute-start(bf16[2,128,128]{2,1,0:T(8,128)(2,1)S(1)} %get-tuple-element.38), channel_id=1, source_target_pairs={{0,16},{8,24},{16,0},{24,8},{1,17},{9,25},{17,1},{25,9},{2,18},{10... | collective-permute-start | bytes 196616 | tf_op jit(solution)/shard_map/ppermute | solution.py:286
  48.4 0.0 collective-permute-start.11
  48.4 0.7 %collective-permute-start.9 = (bf16[2,128,128]{2,1,0:T(8,128)(2,1)S(1)}, bf16[2,128,128]{2,1,0:T(8,128)(2,1)S(1)}, u32[]{:S(2)}, u32[]{:S(2)}) collective-permute-start(bf16[2,128,128]{2,1,0:T(8,128)(2,1)S(1)} %get-tuple-element.37), channel_id=1, source_target_pairs={{0,8},{8,0},{16,24},{24,16},{1,9},{9,1},{17,25},{25,17},{2,10},{10... | collective-permute-start | bytes 196616 | tf_op jit(solution)/shard_map/ppermute | solution.py:286
  49.0 2.1 %collective-permute-done.10.refs_2_ = bf16[2,128,128]{2,1,0:T(8,128)(2,1)S(1)} collective-permute-done((bf16[2,128,128]{2,1,0:T(8,128)(2,1)S(1)}, bf16[2,128,128]{2,1,0:T(8,128)(2,1)S(1)}, u32[]{:S(2)}, u32[]{:S(2)}) %collective-permute-start.10) | collective-permute-done | bytes 65568 | tf_op jit(solution)/shard_map/ppermute | solution.py:286
  51.2 1.4 %collective-permute-done.11.refs_3_ = bf16[2,128,128]{2,1,0:T(8,128)(2,1)S(1)} collective-permute-done((bf16[2,128,128]{2,1,0:T(8,128)(2,1)S(1)}, bf16[2,128,128]{2,1,0:T(8,128)(2,1)S(1)}, u32[]{:S(2)}, u32[]{:S(2)}) %collective-permute-start.11) | collective-permute-done | bytes 65568 | tf_op jit(solution)/shard_map/ppermute | solution.py:286
  52.6 0.0 collective-permute-done.9.refs_1_
  52.6 0.9 %sum_unrotate.1 = (f32[256,128]{1,0:T(8,128)}, f32[1,256]{1,0:T(1,128)}) custom-call(s32[256,128]{1,0:T(8,128)S(1)} %get-tuple-element.22.sign_ref, bf16[2,128,128]{2,1,0:T(8,128)(2,1)S(1)} %get-tuple-element.36.refs_0_, bf16[2,128,128]{2,1,0:T(8,128)(2,1)S(1)} %collective-permute-done.9.refs_1_, bf16[2,128,128]{2,1,0:T(8,128)(2,1)S(1)} %collective-permute-done.10.refs_2_, ...), custom_call_target="tpu_custom_call" | custom-call | tf_op jit(solution)/shard_map/sum_unrotate/pallas_call | solution.py:257
Async XLA Ops:
  4.6 15.0 %collective-permute-start = (bf16[4,256,128]{2,1,0:T(8,128)(2,1)S(1)}, bf16[4,256,128]{2,1,0:T(8,128)(2,1)S(1)}, u32[]{:S(2)}, u32[]{:S(2)}) collective-permute-start(bf16[4,256,128]{2,1,0:T(8,128)(2,1)S(1)} %get-tuple-element.24), channel_id=1, source_target_pairs={{0,1},{1,0},{2,3},{3,2},{4,5},{5,4},{6,7},{7,6},{8,9},{9,8},{10,11... | collective-permute-start | bytes 786440 | tf_op jit(solution)/shard_map/ppermute | solution.py:280
  7.6 11.9 %collective-permute-start.2 = (bf16[4,256,128]{2,1,0:T(8,128)(2,1)S(1)}, bf16[4,256,128]{2,1,0:T(8,128)(2,1)S(1)}, u32[]{:S(2)}, u32[]{:S(2)}) collective-permute-start(bf16[4,256,128]{2,1,0:T(8,128)(2,1)S(1)} %get-tuple-element.26), channel_id=1, source_target_pairs={{0,3},{1,2},{2,1},{3,0},{4,7},{5,6},{6,5},{7,4},{8,11},{9,10},{10,... | collective-permute-start | bytes 786440 | tf_op jit(solution)/shard_map/ppermute | solution.py:280
  9.1 10.0 %collective-permute-start.1 = (bf16[4,128,128]{2,1,0:T(8,128)(2,1)S(1)}, bf16[4,128,128]{2,1,0:T(8,128)(2,1)S(1)}, u32[]{:S(2)}, u32[]{:S(2)}) collective-permute-start(bf16[4,128,128]{2,1,0:T(8,128)(2,1)S(1)} %get-tuple-element.25), channel_id=1, source_target_pairs={{0,2},{1,3},{2,0},{3,1},{4,6},{5,7},{6,4},{7,5},{8,10},{9,11},{10,... | collective-permute-start | bytes 393224 | tf_op jit(solution)/shard_map/ppermute | solution.py:280
  9.2 16.8 %collective-permute-start.4 = (bf16[4,128,128]{2,1,0:T(8,128)(2,1)S(1)}, bf16[4,128,128]{2,1,0:T(8,128)(2,1)S(1)}, u32[]{:S(2)}, u32[]{:S(2)}) collective-permute-start(bf16[4,128,128]{2,1,0:T(8,128)(2,1)S(1)} %get-tuple-element.31), channel_id=1, source_target_pairs={{0,2},{1,3},{2,0},{3,1},{4,6},{5,7},{6,4},{7,5},{8,10},{9,11},{10,... | collective-permute-start | bytes 393224 | tf_op jit(solution)/shard_map/ppermute | solution.py:280
  19.6 15.2 %collective-permute-start.3 = (f32[4,128,128]{2,1,0:T(8,128)S(1)}, f32[4,128,128]{2,1,0:T(8,128)S(1)}, u32[]{:S(2)}, u32[]{:S(2)}) collective-permute-start(f32[4,128,128]{2,1,0:T(8,128)S(1)} %get-tuple-element.30), channel_id=1, source_target_pairs={{0,4},{1,5},{2,6},{3,7},{4,0},{5,1},{6,2},{7,3},{8,12},{9,13},{10,... | collective-permute-start | bytes 786440 | tf_op jit(solution)/shard_map/ppermute | solution.py:305
  22.5 12.4 %collective-permute-start.6 = (bf16[4,256,128]{2,1,0:T(8,128)(2,1)S(1)}, bf16[4,256,128]{2,1,0:T(8,128)(2,1)S(1)}, u32[]{:S(2)}, u32[]{:S(2)}) collective-permute-start(bf16[4,256,128]{2,1,0:T(8,128)(2,1)S(1)} %get-tuple-element.33), channel_id=1, source_target_pairs={{0,1},{1,0},{2,3},{3,2},{4,5},{5,4},{6,7},{7,6},{8,9},{9,8},{10,11... | collective-permute-start | bytes 786440 | tf_op jit(solution)/shard_map/ppermute | solution.py:280
  24.0 19.2 %collective-permute-start.7 = (bf16[4,256,128]{2,1,0:T(8,128)(2,1)S(1)}, bf16[4,256,128]{2,1,0:T(8,128)(2,1)S(1)}, u32[]{:S(2)}, u32[]{:S(2)}) collective-permute-start(bf16[4,256,128]{2,1,0:T(8,128)(2,1)S(1)} %get-tuple-element.34), channel_id=1, source_target_pairs={{0,2},{1,3},{2,0},{3,1},{4,6},{5,7},{6,4},{7,5},{8,10},{9,11},{10,... | collective-permute-start | bytes 786440 | tf_op jit(solution)/shard_map/ppermute | solution.py:280
  25.6 20.7 %collective-permute-start.8 = (bf16[4,256,128]{2,1,0:T(8,128)(2,1)S(1)}, bf16[4,256,128]{2,1,0:T(8,128)(2,1)S(1)}, u32[]{:S(2)}, u32[]{:S(2)}) collective-permute-start(bf16[4,256,128]{2,1,0:T(8,128)(2,1)S(1)} %get-tuple-element.35), channel_id=1, source_target_pairs={{0,3},{1,2},{2,1},{3,0},{4,7},{5,6},{6,5},{7,4},{8,11},{9,10},{10,... | collective-permute-start | bytes 786440 | tf_op jit(solution)/shard_map/ppermute | solution.py:280
  26.1 20.3 %collective-permute-start.5 = (f32[4,128,128]{2,1,0:T(8,128)S(1)}, f32[4,128,128]{2,1,0:T(8,128)S(1)}, u32[]{:S(2)}, u32[]{:S(2)}) collective-permute-start(f32[4,128,128]{2,1,0:T(8,128)S(1)} %far_sum.3), channel_id=1, source_target_pairs={{0,4},{1,5},{2,6},{3,7},{4,0},{5,1},{6,2},{7,3},{8,12},{9,13},{10,... | collective-permute-start | bytes 786440 | tf_op jit(solution)/shard_map/ppermute | solution.py:305
  46.8 4.3 %collective-permute-start.10 = (bf16[2,128,128]{2,1,0:T(8,128)(2,1)S(1)}, bf16[2,128,128]{2,1,0:T(8,128)(2,1)S(1)}, u32[]{:S(2)}, u32[]{:S(2)}) collective-permute-start(bf16[2,128,128]{2,1,0:T(8,128)(2,1)S(1)} %get-tuple-element.38), channel_id=1, source_target_pairs={{0,16},{8,24},{16,0},{24,8},{1,17},{9,25},{17,1},{25,9},{2,18},{10... | collective-permute-start | bytes 196616 | tf_op jit(solution)/shard_map/ppermute | solution.py:286
  48.4 4.2 %collective-permute-start.11 = (bf16[2,128,128]{2,1,0:T(8,128)(2,1)S(1)}, bf16[2,128,128]{2,1,0:T(8,128)(2,1)S(1)}, u32[]{:S(2)}, u32[]{:S(2)}) collective-permute-start(bf16[2,128,128]{2,1,0:T(8,128)(2,1)S(1)} %get-tuple-element.39), channel_id=1, source_target_pairs={{0,24},{8,16},{16,8},{24,0},{1,25},{9,17},{17,9},{25,1},{2,26},{10... | collective-permute-start | bytes 196616 | tf_op jit(solution)/shard_map/ppermute | solution.py:286
  48.4 4.2 %collective-permute-start.9 = (bf16[2,128,128]{2,1,0:T(8,128)(2,1)S(1)}, bf16[2,128,128]{2,1,0:T(8,128)(2,1)S(1)}, u32[]{:S(2)}, u32[]{:S(2)}) collective-permute-start(bf16[2,128,128]{2,1,0:T(8,128)(2,1)S(1)} %get-tuple-element.37), channel_id=1, source_target_pairs={{0,8},{8,0},{16,24},{24,16},{1,9},{9,1},{17,25},{25,17},{2,10},{10... | collective-permute-start | bytes 196616 | tf_op jit(solution)/shard_map/ppermute | solution.py:286

commit v8 on v7

--- a/solution.py
+++ b/solution.py
@@ -58,33 +58,33 @@
         self.units = groups // self.together
         self.columns = self.together * self.blocks
 
-    def shape(self):
-        return (self.units, QGROUP, self.columns)
-
-    def cuts(self, step, other):
-        return HALVES if other and self.half > 1 and step == self.half // 2 else 1
-
-
-def rotate_kernel(layout, other, values_ref, signs_ref, *refs):
+    def span(self, steps):
+        count = len(steps)
+        aligned = steps[0] % count == 0 and steps == list(range(steps[0], steps[0] + count))
+        return count if aligned and self.half & (self.half - 1) == 0 and count & (count - 1) == 0 else self.half
+
+
+def rotate_kernel(layout, other, steps, after, values_ref, signs_ref, *refs):
     values, flips, turned, matrix, value_sems, sign_sems = refs[-6:]
-    out_refs = list(refs[:-6])
-    step_refs = [[out_refs.pop(0) for _ in range(layout.cuts(step, other))] for step in range(layout.half)]
+    out_refs = refs[after:-6]
     half, portion, rows = layout.half, layout.portion, layout.rows
     node = lax.axis_index("node")
     member = lax.axis_index("local")
     inner = lax.rem(member, half)
     first = half - (member - inner) if other else member - inner
+    span = layout.span(steps)
+    lowest = partner(inner, steps[0], half) // span * span
 
     def fetches(unit, part):
-        place = partner(node, unit * layout.together + part, layout.groups) * layout.members + first
+        place = partner(node, unit * layout.together + part, layout.groups) * layout.members + first + lowest
         return (
             pltpu.make_async_copy(
-                values_ref.at[:, pl.ds(pl.multiple_of(place * portion, portion), half * portion)],
+                values_ref.at[:, pl.ds(pl.multiple_of(place * portion, portion), span * portion)],
                 values.at[unit, part],
                 value_sems.at[unit, part],
             ),
             pltpu.make_async_copy(
-                signs_ref.at[pl.ds(pl.multiple_of(place * rows, rows), half * rows), :],
+                signs_ref.at[pl.ds(pl.multiple_of(place * rows, rows), span * rows), :],
                 flips.at[unit, part],
                 sign_sems.at[unit, part],
             ),
@@ -108,59 +108,54 @@
         def _():
             fetch(unit + AHEAD)
 
-        for step in range(half):
-            owner = partner(inner, step, half)
+        for index, step in enumerate(steps):
+            owner = partner(inner, step, half) - lowest
             at = pl.ds(pl.multiple_of(owner * portion, portion), portion)
             at_rows = pl.ds(pl.multiple_of(owner * rows, rows), rows)
             for part in range(layout.together):
                 wide = values[unit, part, :, at].astype(jnp.float32).reshape(rows, LANES)
-                turned[step, part * rows : (part + 1) * rows] = jnp.where(
+                turned[index, part * rows : (part + 1) * rows] = jnp.where(
                     flips[unit, part, at_rows, :] == 0, wide, -wide
                 )
-            halves = [turned[step, pl.ds(part, layout.columns, stride=HALVES), :] for part in range(HALVES)]
+            halves = [turned[index, pl.ds(part, layout.columns, stride=HALVES), :] for part in range(HALVES)]
             signed = jnp.concatenate(halves, axis=1).astype(jnp.bfloat16)
             rotated = lax.dot_general(
                 matrix[...], signed, (((1,), (1,)), ((), ())), preferred_element_type=jnp.float32
             )
             for part in range(HALVES):
                 rows_of = slice(part * QGROUP, (part + 1) * QGROUP)
-                coded = recode(rotated[rows_of]).astype(jnp.bfloat16)
-                if len(step_refs[step]) > 1:
-                    step_refs[step][part][unit] = coded
-                else:
-                    step_refs[step][0][unit, rows_of] = coded
+                out_refs[index][unit, rows_of] = recode(rotated[rows_of]).astype(jnp.bfloat16)
         return carry
 
     lax.fori_loop(0, layout.units, body, 0)
     if not other:
-        out_refs[0][...] = flips[0, 0, pl.ds(pl.multiple_of(inner * rows, rows), rows), :]
-
-
-def rotate(values, signs, layout, other):
-    half, units, columns = layout.half, layout.units, layout.columns
-    entries = half * layout.groups * layout.portion
-    outs = []
-    for step in range(half):
-        cuts = layout.cuts(step, other)
-        outs += [jax.ShapeDtypeStruct((units, ROT // cuts, columns), jnp.bfloat16)] * cuts
+        out_refs[-1][...] = flips[0, 0, pl.ds(pl.multiple_of((inner - lowest) * rows, rows), rows), :]
+
+
+def rotate(values, signs, layout, other, steps, after=()):
+    units = layout.units
+    entries = len(steps) * layout.groups * layout.portion
+    outs = [jax.ShapeDtypeStruct((units, ROT, layout.columns), jnp.bfloat16)] * len(steps)
     if not other:
         outs.append(jax.ShapeDtypeStruct((layout.rows, LANES), jnp.int32))
-    return pl.pallas_call(
-        functools.partial(rotate_kernel, layout, other),
-        in_specs=[pl.BlockSpec(memory_space=pltpu.HBM)] * 2,
-        out_shape=outs,
-        scratch_shapes=[
-            pltpu.VMEM((units, layout.together, 1, half * layout.portion), jnp.bfloat16),
-            pltpu.VMEM((units, layout.together, half * layout.rows, LANES), jnp.int32),
-            pltpu.VMEM((half, layout.together * layout.rows, LANES), jnp.float32),
-            pltpu.VMEM((ROT, ROT), jnp.bfloat16),
-            pltpu.SemaphoreType.DMA((units, layout.together)),
-            pltpu.SemaphoreType.DMA((units, layout.together)),
-        ],
-        compiler_params=pltpu.CompilerParams(vmem_limit_bytes=VMEM_LIMIT),
-        cost_estimate=pl.CostEstimate(flops=2 * entries * ROT, bytes_accessed=10 * entries, transcendentals=0),
-        name="rotate_code",
-    )(values, signs)
+    return list(
+        pl.pallas_call(
+            functools.partial(rotate_kernel, layout, other, steps, len(after)),
+            in_specs=[pl.BlockSpec(memory_space=pltpu.HBM)] * 2 + [pl.BlockSpec(memory_space=pl.ANY)] * len(after),
+            out_shape=outs,
+            scratch_shapes=[
+                pltpu.VMEM((units, layout.together, 1, layout.span(steps) * layout.portion), jnp.bfloat16),
+                pltpu.VMEM((units, layout.together, layout.span(steps) * layout.rows, LANES), jnp.int32),
+                pltpu.VMEM((len(steps), layout.together * layout.rows, LANES), jnp.float32),
+                pltpu.VMEM((ROT, ROT), jnp.bfloat16),
+                pltpu.SemaphoreType.DMA((units, layout.together)),
+                pltpu.SemaphoreType.DMA((units, layout.together)),
+            ],
+            compiler_params=pltpu.CompilerParams(vmem_limit_bytes=VMEM_LIMIT),
+            cost_estimate=pl.CostEstimate(flops=2 * entries * ROT, bytes_accessed=10 * entries, transcendentals=0),
+            name="rotate_code",
+        )(values, signs, *after)
+    )
 
 
 def add_all(arrays):
@@ -170,23 +165,19 @@
     return total
 
 
-def far_sum_kernel(part, count, *refs):
-    arrays = []
-    for ref in refs[:count]:
-        cut = ref.shape[1] == QGROUP
-        arrays.append(ref[...] if cut else ref[:, part * QGROUP : (part + 1) * QGROUP])
-    refs[-1][...] = add_all(arrays)
-
-
-def far_sum(parts, layout, part, later):
-    size = QGROUP * layout.units * layout.columns
+def far_sum_kernel(count, *refs):
+    refs[-1][...] = add_all([ref[...] for ref in refs[:count]])
+
+
+def far_sum(parts, later):
+    size = parts[0].size
     *later, total = pl.pallas_call(
-        functools.partial(far_sum_kernel, part, len(parts)),
+        functools.partial(far_sum_kernel, len(parts)),
         in_specs=[pl.BlockSpec(memory_space=pltpu.VMEM)] * len(parts)
         + [pl.BlockSpec(memory_space=pl.ANY)] * len(later),
         out_specs=[pl.BlockSpec(memory_space=pl.ANY)] * len(later) + [pl.BlockSpec(memory_space=pltpu.VMEM)],
         out_shape=[jax.ShapeDtypeStruct(array.shape, array.dtype) for array in later]
-        + [jax.ShapeDtypeStruct(layout.shape(), jnp.float32)],
+        + [jax.ShapeDtypeStruct(parts[0].shape, jnp.float32)],
         input_output_aliases={len(parts) + index: index for index in range(len(later))},
         compiler_params=pltpu.CompilerParams(vmem_limit_bytes=SUM_VMEM_LIMIT),
         cost_estimate=pl.CostEstimate(
@@ -197,18 +188,18 @@
     return total, later
 
 
-def group_sum_kernel(layout, *refs):
-    across_refs, near_refs, out_refs = refs[:HALVES], refs[HALVES : HALVES + layout.half], refs[HALVES + layout.half :]
-    for half, across_ref in enumerate(across_refs):
-        near = [ref[:, half * QGROUP : (half + 1) * QGROUP] for ref in near_refs]
-        first = recode(add_all(near + [across_ref[...]])).astype(jnp.bfloat16)
+def group_sum_kernel(layout, across_ref, *refs):
+    near_refs, out_refs = refs[: layout.half], refs[layout.half :]
+    for half in range(HALVES):
+        at_rows = slice(half * QGROUP, (half + 1) * QGROUP)
+        first = recode(add_all([ref[:, at_rows] for ref in (*near_refs, across_ref)])).astype(jnp.bfloat16)
         for section, out_ref in enumerate(out_refs):
             at = section % layout.together * layout.blocks
             out_ref[half] = first[section // layout.together, :, at : at + layout.blocks]
 
 
 def group_sum(near, across, layout):
-    size = ROT * layout.units * layout.columns
+    size = across.size
     return pl.pallas_call(
         functools.partial(group_sum_kernel, layout),
         out_shape=[jax.ShapeDtypeStruct((HALVES, QGROUP, layout.blocks), jnp.bfloat16)] * layout.groups,
@@ -217,7 +208,7 @@
             flops=30 * size, bytes_accessed=2 * (layout.half + 3) * size, transcendentals=0
         ),
         name="group_sum_code",
-    )(*across, *near)
+    )(across, *near)
 
 
 def bfloat16_terms(values):
@@ -288,25 +279,16 @@
 
     values, sign_rows = partials.reshape(1, length), signs.reshape(length // LANES, LANES)
     counterparts = [(member, (member + half) % members) for member in range(members)]
-    steps = list(range(half - 1, 0, -1))
-    outs = list(rotate(values, sign_rows, layout, True))
-    far = [[outs.pop(0) for _ in range(layout.cuts(step, True))] for step in range(half)]
-    last = []
-    for step in steps:
-        far[step][0] = swap(far[step][0], step)
-        last += [step] if len(far[step]) > 1 else []
-    for step in last:
-        far[step][1] = swap(far[step][1], step)
-    *near, own_signs = rotate(values, sign_rows, layout, False)
-    across = []
-    for part in range(HALVES):
-        later = near[1:] if part == 0 else []
-        total, later = far_sum([arrays[min(part, len(arrays) - 1)] for arrays in far], layout, part, later)
-        across.append(lax.ppermute(total, "local", counterparts))
-        if part == 0:
-            near = near[:1] + later
-    for step in steps:
-        near[step] = swap(near[step], step)
+    slow = list(range(half // 2, half))
+    fast = list(range(half // 2))
+    far_slow = rotate(values, sign_rows, layout, True, slow)
+    far_fast = rotate(values, sign_rows, layout, True, fast, far_slow[:1])
+    far = [swap(part, step) for step, part in zip(slow, far_slow)]
+    far += [swap(part, step) if step else part for step, part in zip(fast, far_fast)]
+    *near, own_signs = rotate(values, sign_rows, layout, False, fast + slow, far_fast[:1])
+    total, near[1:-1] = far_sum(far, near[1:-1])
+    across = lax.ppermute(total, "local", counterparts)
+    near = [swap(part, step) if step else part for step, part in zip(fast + slow, near)]
     reduced, rotated_max = finish(share(group_sum(near, across, layout)), own_signs)
     return (reduced.reshape(-1), rotated_max.reshape(-1))
 

time: 53.7 us -> 54.3 us (1.011)
  starting transfers between devices: 15.3 us -> 12.9 us
  Pallas kernels: 9.48 us -> 11.7 us
  waiting for transfers between devices: 28 us -> 28.7 us
    ppermute x7 -> x6, waiting for transfers between devices: 15.9 us -> 24.9 us  [swap(): return lax.ppermute(part, 'local', pairs)]
    ppermute x2 -> x1, waiting for transfers between devices: 8.62 us -> 0.01 us  [shards(): across = lax.ppermute(total, 'local', counterparts)]
    pallas_call x4, Pallas kernels: 8.03 us -> 10.3 us  [the longest x3 10.2 us: rotate(): pl.pallas_call(functools.partial(rotate_kernel, layout, other, steps, len...]
    ppermute x7 -> x6, starting transfers between devices: 10.1 us -> 8.24 us  [swap(): return lax.ppermute(part, 'local', pairs)]
    ppermute x2 -> x1, starting transfers between devices: 3.06 us -> 2.72 us  [shards(): across = lax.ppermute(total, 'local', counterparts)]
  transfers between devices with their start and end apart: 12 -> 10, of which waited for: 7 -> 5; matrix products, arithmetic and copies ran while one was open for 0% -> 0% of each run, Pallas kernels for 8% -> 13%
where the time goes in v8:
time: 54.3 us; the launch traced here: 54 us
  waiting for transfers between devices  28.7 us (53%)
  starting transfers between devices  12.9 us (24%)
  Pallas kernels  11.7 us (22%)
  between operations  0.68 us (1%)
    ppermute x6, waiting for transfers between devices, swap(): return lax.ppermute(part, 'local', pairs)  24.9 us
    pallas_call x3, Pallas kernels, rotate(): pl.pallas_call(functools.partial(rotate_kernel, layout, other, steps, len...  10.2 us
    ppermute x6, starting transfers between devices, swap(): return lax.ppermute(part, 'local', pairs)  8.24 us
    ppermute x3, waiting for transfers between devices, share(): moved.append(lax.ppermute(parts[step], 'node', pairs))  3.78 us
    ppermute x1, starting transfers between devices, shards(): across = lax.ppermute(total, 'local', counterparts)  2.72 us
    ppermute x3, starting transfers between devices, share(): moved.append(lax.ppermute(parts[step], 'node', pairs))  1.93 us
  transfers between devices with their start and end apart: 10, of which 5 were waited for; matrix products, arithmetic and copies ran while one was open for 0% of the time, Pallas kernels for 13%

profile of v8, /device:TPU:0, one launch (start us, length us, event | category | flops | bytes accessed | tf_op | source)
XLA Modules:
  0.0 54.0 jit_solution(11368404248163935902)
XLA Ops:
  0.6 3.1 %rotate_code.3 = (bf16[4,256,128]{2,1,0:T(8,128)(2,1)S(1)}, bf16[4,256,128]{2,1,0:T(8,128)(2,1)S(1)}) custom-call(bf16[1,1048576]{1,0:T(2,128)(2,1)} %bitcast.4, s32[8192,128]{1,0:T(8,128)} %bitcast.7), custom_call_target="tpu_custom_call" | custom-call | flops 134217728 | bytes 2621440 | tf_op jit(solution)/shard_map/rotate_code/pallas_call | solution.py:142
  3.7 4.0 %collective-permute-start.1 = (bf16[4,256,128]{2,1,0:T(8,128)(2,1)S(1)}, bf16[4,256,128]{2,1,0:T(8,128)(2,1)S(1)}, u32[]{:S(2)}, u32[]{:S(2)}) collective-permute-start(bf16[4,256,128]{2,1,0:T(8,128)(2,1)S(1)} %get-tuple-element.23), channel_id=1, source_target_pairs={{0,3},{1,2},{2,1},{3,0},{4,7},{5,6},{6,5},{7,4},{8,11},{9,10},{10,... | collective-permute-start | bytes 786440 | tf_op jit(solution)/shard_map/ppermute | solution.py:271
  7.8 0.5 collective-permute-start
  8.2 3.1 %rotate_code.4 = (bf16[4,256,128]{2,1,0:T(8,128)(2,1)S(1)}, bf16[4,256,128]{2,1,0:T(8,128)(2,1)S(1)}) custom-call(bf16[1,1048576]{1,0:T(2,128)(2,1)} %bitcast.5, s32[8192,128]{1,0:T(8,128)} %bitcast.8, bf16[4,256,128]{2,1,0:T(8,128)(2,1)S(1)} %get-tuple-element.20.refs_0_), custom_call_target="tpu_custom_call" | custom-call | flops 134217728 | bytes 2621440 | tf_op jit(solution)/shard_map/rotate_code/pallas_call | solution.py:142
  11.4 0.3 collective-permute-start.2
  11.6 4.0 %rotate_code.5 = (bf16[4,256,128]{2,1,0:T(8,128)(2,1)S(1)}, bf16[4,256,128]{2,1,0:T(8,128)(2,1)S(1)}, bf16[4,256,128]{2,1,0:T(8,128)(2,1)S(1)}, bf16[4,256,128]{2,1,0:T(8,128)(2,1)S(1)}, s32[256,128]{1,0:T(8,128)S(1)}) custom-call(bf16[1,1048576]{1,0:T(2,128)(2,1)} %bitcast.6, s32[8192,128]{1,0:T(8,128)} %bitcast.9, ...), custom_call_target="tpu_custom_call" | custom-call | flops 268435456 | bytes 5242880 | tf_op jit(solution)/shard_map/rotate_code/pallas_call | solution.py:142
  15.6 0.0 collective-permute-done.1.refs_1_
  15.6 4.3 %collective-permute-done.refs_0_ = bf16[4,256,128]{2,1,0:T(8,128)(2,1)S(1)} collective-permute-done((bf16[4,256,128]{2,1,0:T(8,128)(2,1)S(1)}, bf16[4,256,128]{2,1,0:T(8,128)(2,1)S(1)}, u32[]{:S(2)}, u32[]{:S(2)}) %collective-permute-start) | collective-permute-done | bytes 262176 | tf_op jit(solution)/shard_map/ppermute | solution.py:271
  19.9 0.0 collective-permute-done.2.refs_3_
  19.9 0.1 far_sum.1
  20.0 2.7 %collective-permute-start.3 = (f32[4,256,128]{2,1,0:T(8,128)S(1)}, f32[4,256,128]{2,1,0:T(8,128)S(1)}, u32[]{:S(2)}, u32[]{:S(2)}) collective-permute-start(f32[4,256,128]{2,1,0:T(8,128)S(1)} %get-tuple-element.27), channel_id=1, source_target_pairs={{0,4},{1,5},{2,6},{3,7},{4,0},{5,1},{6,2},{7,3},{8,12},{9,13},{10,... | collective-permute-start | bytes 1572872 | tf_op jit(solution)/shard_map/ppermute | solution.py:290
  22.7 2.4 %collective-permute-start.6 = (bf16[4,256,128]{2,1,0:T(8,128)(2,1)S(1)}, bf16[4,256,128]{2,1,0:T(8,128)(2,1)S(1)}, u32[]{:S(2)}, u32[]{:S(2)}) collective-permute-start(bf16[4,256,128]{2,1,0:T(8,128)(2,1)S(1)} %get-tuple-element.31), channel_id=1, source_target_pairs={{0,3},{1,2},{2,1},{3,0},{4,7},{5,6},{6,5},{7,4},{8,11},{9,10},{10,... | collective-permute-start | bytes 786440 | tf_op jit(solution)/shard_map/ppermute | solution.py:271
  25.1 0.6 %collective-permute-start.4 = (bf16[4,256,128]{2,1,0:T(8,128)(2,1)S(1)}, bf16[4,256,128]{2,1,0:T(8,128)(2,1)S(1)}, u32[]{:S(2)}, u32[]{:S(2)}) collective-permute-start(bf16[4,256,128]{2,1,0:T(8,128)(2,1)S(1)} %get-tuple-element.29), channel_id=1, source_target_pairs={{0,1},{1,0},{2,3},{3,2},{4,5},{5,4},{6,7},{7,6},{8,9},{9,8},{10,11... | collective-permute-start | bytes 786440 | tf_op jit(solution)/shard_map/ppermute | solution.py:271
  25.8 0.5 collective-permute-start.5
  26.2 14.5 %collective-permute-done.6.refs_3_ = bf16[4,256,128]{2,1,0:T(8,128)(2,1)S(1)} collective-permute-done((bf16[4,256,128]{2,1,0:T(8,128)(2,1)S(1)}, bf16[4,256,128]{2,1,0:T(8,128)(2,1)S(1)}, u32[]{:S(2)}, u32[]{:S(2)}) %collective-permute-start.6) | collective-permute-done | bytes 262176 | tf_op jit(solution)/shard_map/ppermute | solution.py:271
  40.7 0.0 collective-permute-done.4.refs_1_
  40.7 6.1 %collective-permute-done.5.refs_2_ = bf16[4,256,128]{2,1,0:T(8,128)(2,1)S(1)} collective-permute-done((bf16[4,256,128]{2,1,0:T(8,128)(2,1)S(1)}, bf16[4,256,128]{2,1,0:T(8,128)(2,1)S(1)}, u32[]{:S(2)}, u32[]{:S(2)}) %collective-permute-start.5) | collective-permute-done | bytes 262176 | tf_op jit(solution)/shard_map/ppermute | solution.py:271
  46.8 0.0 collective-permute-done.3.across_ref
  46.8 0.5 group_sum_code.1
  47.3 0.1 collective-permute-start.7
  47.4 1.6 %collective-permute-start.8 = (bf16[2,128,128]{2,1,0:T(8,128)(2,1)S(1)}, bf16[2,128,128]{2,1,0:T(8,128)(2,1)S(1)}, u32[]{:S(2)}, u32[]{:S(2)}) collective-permute-start(bf16[2,128,128]{2,1,0:T(8,128)(2,1)S(1)} %get-tuple-element.34), channel_id=1, source_target_pairs={{0,16},{8,24},{16,0},{24,8},{1,17},{9,25},{17,1},{25,9},{2,18},{10... | collective-permute-start | bytes 196616 | tf_op jit(solution)/shard_map/ppermute | solution.py:277
  49.0 0.3 collective-permute-start.9
  49.3 0.0 collective-permute-done.7.refs_1_
  49.3 2.6 %collective-permute-done.8.refs_2_ = bf16[2,128,128]{2,1,0:T(8,128)(2,1)S(1)} collective-permute-done((bf16[2,128,128]{2,1,0:T(8,128)(2,1)S(1)}, bf16[2,128,128]{2,1,0:T(8,128)(2,1)S(1)}, u32[]{:S(2)}, u32[]{:S(2)}) %collective-permute-start.8) | collective-permute-done | bytes 65568 | tf_op jit(solution)/shard_map/ppermute | solution.py:277
  51.9 1.1 %collective-permute-done.9.refs_3_ = bf16[2,128,128]{2,1,0:T(8,128)(2,1)S(1)} collective-permute-done((bf16[2,128,128]{2,1,0:T(8,128)(2,1)S(1)}, bf16[2,128,128]{2,1,0:T(8,128)(2,1)S(1)}, u32[]{:S(2)}, u32[]{:S(2)}) %collective-permute-start.9) | collective-permute-done | bytes 65568 | tf_op jit(solution)/shard_map/ppermute | solution.py:277
  53.0 0.9 %sum_unrotate.1 = (f32[256,128]{1,0:T(8,128)}, f32[1,256]{1,0:T(1,128)}) custom-call(s32[256,128]{1,0:T(8,128)S(1)} %get-tuple-element.22.sign_ref, bf16[2,128,128]{2,1,0:T(8,128)(2,1)S(1)} %get-tuple-element.32.refs_0_, bf16[2,128,128]{2,1,0:T(8,128)(2,1)S(1)} %collective-permute-done.7.refs_1_, bf16[2,128,128]{2,1,0:T(8,128)(2,1)S(1)} %collective-permute-done.8.refs_2_, ...), custom_call_target="tpu_custom_call" | custom-call | tf_op jit(solution)/shard_map/sum_unrotate/pallas_call | solution.py:248
Async XLA Ops:
  3.7 11.8 %collective-permute-start.1 = (bf16[4,256,128]{2,1,0:T(8,128)(2,1)S(1)}, bf16[4,256,128]{2,1,0:T(8,128)(2,1)S(1)}, u32[]{:S(2)}, u32[]{:S(2)}) collective-permute-start(bf16[4,256,128]{2,1,0:T(8,128)(2,1)S(1)} %get-tuple-element.23), channel_id=1, source_target_pairs={{0,3},{1,2},{2,1},{3,0},{4,7},{5,6},{6,5},{7,4},{8,11},{9,10},{10,... | collective-permute-start | bytes 786440 | tf_op jit(solution)/shard_map/ppermute | solution.py:271
  7.8 12.1 %collective-permute-start = (bf16[4,256,128]{2,1,0:T(8,128)(2,1)S(1)}, bf16[4,256,128]{2,1,0:T(8,128)(2,1)S(1)}, u32[]{:S(2)}, u32[]{:S(2)}) collective-permute-start(bf16[4,256,128]{2,1,0:T(8,128)(2,1)S(1)} %get-tuple-element.20.refs_0_), channel_id=1, source_target_pairs={{0,2},{1,3},{2,0},{3,1},{4,6},{5,7},{6,4},{7,5},{8,10},{9,11},{10,... | collective-permute-start | bytes 786440 | tf_op jit(solution)/shard_map/ppermute | solution.py:271
  11.4 8.5 %collective-permute-start.2 = (bf16[4,256,128]{2,1,0:T(8,128)(2,1)S(1)}, bf16[4,256,128]{2,1,0:T(8,128)(2,1)S(1)}, u32[]{:S(2)}, u32[]{:S(2)}) collective-permute-start(bf16[4,256,128]{2,1,0:T(8,128)(2,1)S(1)} %get-tuple-element.24), channel_id=1, source_target_pairs={{0,1},{1,0},{2,3},{3,2},{4,5},{5,4},{6,7},{7,6},{8,9},{9,8},{10,11... | collective-permute-start | bytes 786440 | tf_op jit(solution)/shard_map/ppermute | solution.py:271
  20.0 26.8 %collective-permute-start.3 = (f32[4,256,128]{2,1,0:T(8,128)S(1)}, f32[4,256,128]{2,1,0:T(8,128)S(1)}, u32[]{:S(2)}, u32[]{:S(2)}) collective-permute-start(f32[4,256,128]{2,1,0:T(8,128)S(1)} %get-tuple-element.27), channel_id=1, source_target_pairs={{0,4},{1,5},{2,6},{3,7},{4,0},{5,1},{6,2},{7,3},{8,12},{9,13},{10,... | collective-permute-start | bytes 1572872 | tf_op jit(solution)/shard_map/ppermute | solution.py:290
  22.7 18.0 %collective-permute-start.6 = (bf16[4,256,128]{2,1,0:T(8,128)(2,1)S(1)}, bf16[4,256,128]{2,1,0:T(8,128)(2,1)S(1)}, u32[]{:S(2)}, u32[]{:S(2)}) collective-permute-start(bf16[4,256,128]{2,1,0:T(8,128)(2,1)S(1)} %get-tuple-element.31), channel_id=1, source_target_pairs={{0,3},{1,2},{2,1},{3,0},{4,7},{5,6},{6,5},{7,4},{8,11},{9,10},{10,... | collective-permute-start | bytes 786440 | tf_op jit(solution)/shard_map/ppermute | solution.py:271
  25.1 15.6 %collective-permute-start.4 = (bf16[4,256,128]{2,1,0:T(8,128)(2,1)S(1)}, bf16[4,256,128]{2,1,0:T(8,128)(2,1)S(1)}, u32[]{:S(2)}, u32[]{:S(2)}) collective-permute-start(bf16[4,256,128]{2,1,0:T(8,128)(2,1)S(1)} %get-tuple-element.29), channel_id=1, source_target_pairs={{0,1},{1,0},{2,3},{3,2},{4,5},{5,4},{6,7},{7,6},{8,9},{9,8},{10,11... | collective-permute-start | bytes 786440 | tf_op jit(solution)/shard_map/ppermute | solution.py:271
  25.8 21.1 %collective-permute-start.5 = (bf16[4,256,128]{2,1,0:T(8,128)(2,1)S(1)}, bf16[4,256,128]{2,1,0:T(8,128)(2,1)S(1)}, u32[]{:S(2)}, u32[]{:S(2)}) collective-permute-start(bf16[4,256,128]{2,1,0:T(8,128)(2,1)S(1)} %get-tuple-element.30), channel_id=1, source_target_pairs={{0,2},{1,3},{2,0},{3,1},{4,6},{5,7},{6,4},{7,5},{8,10},{9,11},{10,... | collective-permute-start | bytes 786440 | tf_op jit(solution)/shard_map/ppermute | solution.py:271
  47.3 1.9 %collective-permute-start.7 = (bf16[2,128,128]{2,1,0:T(8,128)(2,1)S(1)}, bf16[2,128,128]{2,1,0:T(8,128)(2,1)S(1)}, u32[]{:S(2)}, u32[]{:S(2)}) collective-permute-start(bf16[2,128,128]{2,1,0:T(8,128)(2,1)S(1)} %get-tuple-element.33), channel_id=1, source_target_pairs={{0,8},{8,0},{16,24},{24,16},{1,9},{9,1},{17,25},{25,17},{2,10},{10... | collective-permute-start | bytes 196616 | tf_op jit(solution)/shard_map/ppermute | solution.py:277
  47.4 4.5 %collective-permute-start.8 = (bf16[2,128,128]{2,1,0:T(8,128)(2,1)S(1)}, bf16[2,128,128]{2,1,0:T(8,128)(2,1)S(1)}, u32[]{:S(2)}, u32[]{:S(2)}) collective-permute-start(bf16[2,128,128]{2,1,0:T(8,128)(2,1)S(1)} %get-tuple-element.34), channel_id=1, source_target_pairs={{0,16},{8,24},{16,0},{24,8},{1,17},{9,25},{17,1},{25,9},{2,18},{10... | collective-permute-start | bytes 196616 | tf_op jit(solution)/shard_map/ppermute | solution.py:277
  49.0 4.0 %collective-permute-start.9 = (bf16[2,128,128]{2,1,0:T(8,128)(2,1)S(1)}, bf16[2,128,128]{2,1,0:T(8,128)(2,1)S(1)}, u32[]{:S(2)}, u32[]{:S(2)}) collective-permute-start(bf16[2,128,128]{2,1,0:T(8,128)(2,1)S(1)} %get-tuple-element.35), channel_id=1, source_target_pairs={{0,24},{8,16},{16,8},{24,0},{1,25},{9,17},{17,9},{25,1},{2,26},{10... | collective-permute-start | bytes 196616 | tf_op jit(solution)/shard_map/ppermute | solution.py:277

commit v9 on v8

--- a/solution.py
+++ b/solution.py
@@ -58,33 +58,29 @@
         self.units = groups // self.together
         self.columns = self.together * self.blocks
 
-    def span(self, steps):
-        count = len(steps)
-        aligned = steps[0] % count == 0 and steps == list(range(steps[0], steps[0] + count))
-        return count if aligned and self.half & (self.half - 1) == 0 and count & (count - 1) == 0 else self.half
-
-
-def rotate_kernel(layout, other, steps, after, values_ref, signs_ref, *refs):
+    def shape(self):
+        return (self.units, QGROUP, self.columns)
+
+
+def rotate_kernel(layout, other, later, values_ref, signs_ref, *refs):
     values, flips, turned, matrix, value_sems, sign_sems = refs[-6:]
-    out_refs = refs[after:-6]
+    out_refs = refs[2 * later : -6]
     half, portion, rows = layout.half, layout.portion, layout.rows
     node = lax.axis_index("node")
     member = lax.axis_index("local")
     inner = lax.rem(member, half)
     first = half - (member - inner) if other else member - inner
-    span = layout.span(steps)
-    lowest = partner(inner, steps[0], half) // span * span
 
     def fetches(unit, part):
-        place = partner(node, unit * layout.together + part, layout.groups) * layout.members + first + lowest
+        place = partner(node, unit * layout.together + part, layout.groups) * layout.members + first
         return (
             pltpu.make_async_copy(
-                values_ref.at[:, pl.ds(pl.multiple_of(place * portion, portion), span * portion)],
+                values_ref.at[:, pl.ds(pl.multiple_of(place * portion, portion), half * portion)],
                 values.at[unit, part],
                 value_sems.at[unit, part],
             ),
             pltpu.make_async_copy(
-                signs_ref.at[pl.ds(pl.multiple_of(place * rows, rows), span * rows), :],
+                signs_ref.at[pl.ds(pl.multiple_of(place * rows, rows), half * rows), :],
                 flips.at[unit, part],
                 sign_sems.at[unit, part],
             ),
@@ -108,45 +104,56 @@
         def _():
             fetch(unit + AHEAD)
 
-        for index, step in enumerate(steps):
-            owner = partner(inner, step, half) - lowest
+        for step in range(half):
+            owner = partner(inner, step, half)
             at = pl.ds(pl.multiple_of(owner * portion, portion), portion)
             at_rows = pl.ds(pl.multiple_of(owner * rows, rows), rows)
             for part in range(layout.together):
                 wide = values[unit, part, :, at].astype(jnp.float32).reshape(rows, LANES)
-                turned[index, part * rows : (part + 1) * rows] = jnp.where(
+                turned[step, part * rows : (part + 1) * rows] = jnp.where(
                     flips[unit, part, at_rows, :] == 0, wide, -wide
                 )
-            halves = [turned[index, pl.ds(part, layout.columns, stride=HALVES), :] for part in range(HALVES)]
+            halves = [turned[step, pl.ds(part, layout.columns, stride=HALVES), :] for part in range(HALVES)]
             signed = jnp.concatenate(halves, axis=1).astype(jnp.bfloat16)
             rotated = lax.dot_general(
                 matrix[...], signed, (((1,), (1,)), ((), ())), preferred_element_type=jnp.float32
             )
             for part in range(HALVES):
                 rows_of = slice(part * QGROUP, (part + 1) * QGROUP)
-                out_refs[index][unit, rows_of] = recode(rotated[rows_of]).astype(jnp.bfloat16)
+                coded = recode(rotated[rows_of]).astype(jnp.bfloat16)
+                if other:
+                    out_refs[step * HALVES + part][unit] = coded
+                else:
+                    out_refs[step][unit, rows_of] = coded
         return carry
 
     lax.fori_loop(0, layout.units, body, 0)
     if not other:
-        out_refs[-1][...] = flips[0, 0, pl.ds(pl.multiple_of((inner - lowest) * rows, rows), rows), :]
-
-
-def rotate(values, signs, layout, other, steps, after=()):
-    units = layout.units
-    entries = len(steps) * layout.groups * layout.portion
-    outs = [jax.ShapeDtypeStruct((units, ROT, layout.columns), jnp.bfloat16)] * len(steps)
-    if not other:
+        out_refs[-1][...] = flips[0, 0, pl.ds(pl.multiple_of(inner * rows, rows), rows), :]
+
+
+def rotate(values, signs, layout, other, later=()):
+    half, units, columns = layout.half, layout.units, layout.columns
+    entries = half * layout.groups * layout.portion
+    outs = [jax.ShapeDtypeStruct(array.shape, array.dtype) for array in later]
+    if other:
+        outs += [jax.ShapeDtypeStruct(layout.shape(), jnp.bfloat16)] * (HALVES * half)
+    else:
+        outs += [jax.ShapeDtypeStruct((units, ROT, columns), jnp.bfloat16)] * half
         outs.append(jax.ShapeDtypeStruct((layout.rows, LANES), jnp.int32))
+    own = len(outs) - len(later)
     return list(
         pl.pallas_call(
-            functools.partial(rotate_kernel, layout, other, steps, len(after)),
-            in_specs=[pl.BlockSpec(memory_space=pltpu.HBM)] * 2 + [pl.BlockSpec(memory_space=pl.ANY)] * len(after),
+            functools.partial(rotate_kernel, layout, other, len(later)),
+            in_specs=[pl.BlockSpec(memory_space=pltpu.HBM)] * 2 + [pl.BlockSpec(memory_space=pl.ANY)] * len(later),
+            out_specs=[pl.BlockSpec(memory_space=pl.ANY)] * len(later)
+            + [pl.BlockSpec(memory_space=pltpu.VMEM)] * own,
             out_shape=outs,
+            input_output_aliases={2 + index: index for index in range(len(later))},
             scratch_shapes=[
-                pltpu.VMEM((units, layout.together, 1, layout.span(steps) * layout.portion), jnp.bfloat16),
-                pltpu.VMEM((units, layout.together, layout.span(steps) * layout.rows, LANES), jnp.int32),
-                pltpu.VMEM((len(steps), layout.together * layout.rows, LANES), jnp.float32),
+                pltpu.VMEM((units, layout.together, 1, half * layout.portion), jnp.bfloat16),
+                pltpu.VMEM((units, layout.together, half * layout.rows, LANES), jnp.int32),
+                pltpu.VMEM((half, layout.together * layout.rows, LANES), jnp.float32),
                 pltpu.VMEM((ROT, ROT), jnp.bfloat16),
                 pltpu.SemaphoreType.DMA((units, layout.together)),
                 pltpu.SemaphoreType.DMA((units, layout.together)),
@@ -154,7 +161,7 @@
             compiler_params=pltpu.CompilerParams(vmem_limit_bytes=VMEM_LIMIT),
             cost_estimate=pl.CostEstimate(flops=2 * entries * ROT, bytes_accessed=10 * entries, transcendentals=0),
             name="rotate_code",
-        )(values, signs, *after)
+        )(values, signs, *later)
     )
 
 
@@ -188,18 +195,18 @@
     return total, later
 
 
-def group_sum_kernel(layout, across_ref, *refs):
-    near_refs, out_refs = refs[: layout.half], refs[layout.half :]
-    for half in range(HALVES):
-        at_rows = slice(half * QGROUP, (half + 1) * QGROUP)
-        first = recode(add_all([ref[:, at_rows] for ref in (*near_refs, across_ref)])).astype(jnp.bfloat16)
+def group_sum_kernel(layout, *refs):
+    across_refs, near_refs, out_refs = refs[:HALVES], refs[HALVES : HALVES + layout.half], refs[HALVES + layout.half :]
+    for half, across_ref in enumerate(across_refs):
+        near = [ref[:, half * QGROUP : (half + 1) * QGROUP] for ref in near_refs]
+        first = recode(add_all(near + [across_ref[...]])).astype(jnp.bfloat16)
         for section, out_ref in enumerate(out_refs):
             at = section % layout.together * layout.blocks
             out_ref[half] = first[section // layout.together, :, at : at + layout.blocks]
 
 
 def group_sum(near, across, layout):
-    size = across.size
+    size = near[0].size
     return pl.pallas_call(
         functools.partial(group_sum_kernel, layout),
         out_shape=[jax.ShapeDtypeStruct((HALVES, QGROUP, layout.blocks), jnp.bfloat16)] * layout.groups,
@@ -208,7 +215,7 @@
             flops=30 * size, bytes_accessed=2 * (layout.half + 3) * size, transcendentals=0
         ),
         name="group_sum_code",
-    )(across, *near)
+    )(*across, *near)
 
 
 def bfloat16_terms(values):
@@ -279,16 +286,30 @@
 
     values, sign_rows = partials.reshape(1, length), signs.reshape(length // LANES, LANES)
     counterparts = [(member, (member + half) % members) for member in range(members)]
-    slow = list(range(half // 2, half))
-    fast = list(range(half // 2))
-    far_slow = rotate(values, sign_rows, layout, True, slow)
-    far_fast = rotate(values, sign_rows, layout, True, fast, far_slow[:1])
-    far = [swap(part, step) for step, part in zip(slow, far_slow)]
-    far += [swap(part, step) if step else part for step, part in zip(fast, far_fast)]
-    *near, own_signs = rotate(values, sign_rows, layout, False, fast + slow, far_fast[:1])
-    total, near[1:-1] = far_sum(far, near[1:-1])
-    across = lax.ppermute(total, "local", counterparts)
-    near = [swap(part, step) if step else part for step, part in zip(fast + slow, near)]
+    fast, slow = list(range(1, half // 2)), list(range(half // 2, half))
+    outs = rotate(values, sign_rows, layout, True)
+    far = [[outs[HALVES * step + part] for step in range(half)] for part in range(HALVES)]
+    for step in slow + fast:
+        far[0][step] = swap(far[0][step], step)
+    for step in slow[:1]:
+        far[1][step] = swap(far[1][step], step)
+    outs = rotate(values, sign_rows, layout, False, [far[1][step] for step in slow[1:] + fast])
+    for step in slow[1:] + fast:
+        far[1][step] = outs.pop(0)
+    *near, own_signs = outs
+    for step in slow[1:]:
+        far[1][step] = swap(far[1][step], step)
+    first, later = far_sum(far[0], [far[1][step] for step in fast] + near[1:])
+    across = [lax.ppermute(first, "local", counterparts)]
+    for step in fast:
+        far[1][step] = swap(later.pop(0), step)
+    near[1:] = later
+    for step in slow[1:]:
+        near[step] = swap(near[step], step)
+    second, later = far_sum(far[1], [near[step] for step in fast + slow[:1]])
+    across.append(lax.ppermute(second, "local", counterparts))
+    for step, part in zip(fast + slow[:1], later):
+        near[step] = swap(part, step)
     reduced, rotated_max = finish(share(group_sum(near, across, layout)), own_signs)
     return (reduced.reshape(-1), rotated_max.reshape(-1))
 

time: 54.3 us -> 50.8 us (0.936)
  waiting for transfers between devices: 28.7 us -> 17.8 us
  starting transfers between devices: 12.9 us -> 22.7 us
  Pallas kernels: 11.7 us -> 9.48 us
    ppermute x6 -> x9, waiting for transfers between devices: 24.9 us -> 8.56 us  [swap(): return lax.ppermute(part, 'local', pairs)]
    ppermute x6 -> x9, starting transfers between devices: 8.24 us -> 17.2 us  [swap(): return lax.ppermute(part, 'local', pairs)]
    ppermute x1 -> x2, waiting for transfers between devices: 0.01 us -> 5.53 us  [the longest x1 5.13 us: shards(): across.append(lax.ppermute(second, 'local', counterparts))]
    pallas_call x3 -> x2, Pallas kernels: 10.2 us -> 7.9 us  [rotate(): pl.pallas_call(functools.partial(rotate_kernel, layout, other, len(later)...]
    ppermute x1 -> x2, starting transfers between devices: 2.72 us -> 3.54 us  [the longest x1 2.58 us: shards(): across = [lax.ppermute(first, 'local', counterparts)]]
  transfers between devices with their start and end apart: 10 -> 14, of which waited for: 5 -> 7; matrix products, arithmetic and copies ran while one was open for 0% -> 0% of each run, Pallas kernels for 13% -> 8%
where the time goes in v9:
time: 50.8 us; the launch traced here: 50.6 us
  starting transfers between devices  22.7 us (45%)
  waiting for transfers between devices  17.8 us (35%)
  Pallas kernels  9.48 us (19%)
  between operations  0.68 us (1%)
    ppermute x9, starting transfers between devices, swap(): return lax.ppermute(part, 'local', pairs)  17.2 us
    ppermute x9, waiting for transfers between devices, swap(): return lax.ppermute(part, 'local', pairs)  8.56 us
    pallas_call x2, Pallas kernels, rotate(): pl.pallas_call(functools.partial(rotate_kernel, layout, other, len(later)...  7.9 us
    ppermute x1, waiting for transfers between devices, shards(): across.append(lax.ppermute(second, 'local', counterparts))  5.13 us
    ppermute x3, waiting for transfers between devices, share(): moved.append(lax.ppermute(parts[step], 'node', pairs))  3.71 us
    ppermute x1, starting transfers between devices, shards(): across = [lax.ppermute(first, 'local', counterparts)]  2.58 us
    ppermute x3, starting transfers between devices, share(): moved.append(lax.ppermute(parts[step], 'node', pairs))  1.93 us
  transfers between devices with their start and end apart: 14, of which 7 were waited for; matrix products, arithmetic and copies ran while one was open for 0% of the time, Pallas kernels for 8%

profile of v9, /device:TPU:0, one launch (start us, length us, event | category | flops | bytes accessed | tf_op | source)
XLA Modules:
  0.0 50.6 jit_solution(12011761501076549400)
XLA Ops:
  0.6 4.0 %rotate_code.2 = (bf16[4,128,128]{2,1,0:T(8,128)(2,1)S(1)}, bf16[4,128,128]{2,1,0:T(8,128)(2,1)S(1)}, bf16[4,128,128]{2,1,0:T(8,128)(2,1)S(1)}, bf16[4,128,128]{...) custom-call(bf16[1,1048576]{1,0:T(2,128)(2,1)} %bitcast.4, ...), custom_call_target="tpu_custom_call" | custom-call | flops 268435456 | bytes 5242880 | tf_op jit(solution)/shard_map/rotate_code/pallas_call | solution.py:146
  4.6 3.0 %collective-permute-start = (bf16[4,128,128]{2,1,0:T(8,128)(2,1)S(1)}, bf16[4,128,128]{2,1,0:T(8,128)(2,1)S(1)}, u32[]{:S(2)}, u32[]{:S(2)}) collective-permute-start(bf16[4,128,128]{2,1,0:T(8,128)(2,1)S(1)} %get-tuple-element.35), channel_id=1, source_target_pairs={{0,1},{1,0},{2,3},{3,2},{4,5},{5,4},{6,7},{7,6},{8,9},{9,8},{10,11... | collective-permute-start | bytes 393224 | tf_op jit(solution)/shard_map/ppermute | solution.py:278
  7.6 1.6 %collective-permute-start.1 = (bf16[4,128,128]{2,1,0:T(8,128)(2,1)S(1)}, bf16[4,128,128]{2,1,0:T(8,128)(2,1)S(1)}, u32[]{:S(2)}, u32[]{:S(2)}) collective-permute-start(bf16[4,128,128]{2,1,0:T(8,128)(2,1)S(1)} %get-tuple-element.36), channel_id=1, source_target_pairs={{0,2},{1,3},{2,0},{3,1},{4,6},{5,7},{6,4},{7,5},{8,10},{9,11},{10,... | collective-permute-start | bytes 393224 | tf_op jit(solution)/shard_map/ppermute | solution.py:278
  9.2 0.0 collective-permute-start.2
  9.2 2.0 %collective-permute-start.5 = (bf16[4,128,128]{2,1,0:T(8,128)(2,1)S(1)}, bf16[4,128,128]{2,1,0:T(8,128)(2,1)S(1)}, u32[]{:S(2)}, u32[]{:S(2)}) collective-permute-start(bf16[4,128,128]{2,1,0:T(8,128)(2,1)S(1)} %get-tuple-element.45), channel_id=1, source_target_pairs={{0,2},{1,3},{2,0},{3,1},{4,6},{5,7},{6,4},{7,5},{8,10},{9,11},{10,... | collective-permute-start | bytes 393224 | tf_op jit(solution)/shard_map/ppermute | solution.py:278
  11.2 3.9 %rotate_code.3 = (bf16[4,128,128]{2,1,0:T(8,128)(2,1)S(1)}, bf16[4,128,128]{2,1,0:T(8,128)(2,1)S(1)}, bf16[4,256,128]{2,1,0:T(8,128)(2,1)S(1)}, bf16[4,256,128]{...) custom-call(bf16[1,1048576]{1,0:T(2,128)(2,1)} %bitcast.5, ...), custom_call_target="tpu_custom_call", output_to_operand_aliasing={{0}: (2, {}), {1}: (3, {})} | custom-call | flops 268435456 | bytes 5242880 | tf_op jit(solution)/shard_map/rotate_code/pallas_call | solution.py:146
  15.1 1.5 %collective-permute-start.6 = (bf16[4,128,128]{2,1,0:T(8,128)(2,1)S(1)}, bf16[4,128,128]{2,1,0:T(8,128)(2,1)S(1)}, u32[]{:S(2)}, u32[]{:S(2)}) collective-permute-start(bf16[4,128,128]{2,1,0:T(8,128)(2,1)S(1)} %get-tuple-element.46), channel_id=1, source_target_pairs={{0,3},{1,2},{2,1},{3,0},{4,7},{5,6},{6,5},{7,4},{8,11},{9,10},{10,... | collective-permute-start | bytes 393224 | tf_op jit(solution)/shard_map/ppermute | solution.py:278
  16.6 0.0 collective-permute-done.refs_1_
  16.6 0.0 collective-permute-done.1.refs_2_
  16.6 0.0 collective-permute-done.2.refs_3_
  16.6 0.1 far_sum.2
  16.7 1.7 %collective-permute-start.4 = (bf16[4,128,128]{2,1,0:T(8,128)(2,1)S(1)}, bf16[4,128,128]{2,1,0:T(8,128)(2,1)S(1)}, u32[]{:S(2)}, u32[]{:S(2)}) collective-permute-start(bf16[4,128,128]{2,1,0:T(8,128)(2,1)S(1)} %get-tuple-element.44), channel_id=1, source_target_pairs={{0,1},{1,0},{2,3},{3,2},{4,5},{5,4},{6,7},{7,6},{8,9},{9,8},{10,11... | collective-permute-start | bytes 393224 | tf_op jit(solution)/shard_map/ppermute | solution.py:278
  18.4 2.6 %collective-permute-start.3 = (f32[4,128,128]{2,1,0:T(8,128)S(1)}, f32[4,128,128]{2,1,0:T(8,128)S(1)}, u32[]{:S(2)}, u32[]{:S(2)}) collective-permute-start(f32[4,128,128]{2,1,0:T(8,128)S(1)} %get-tuple-element.42), channel_id=1, source_target_pairs={{0,4},{1,5},{2,6},{3,7},{4,0},{5,1},{6,2},{7,3},{8,12},{9,13},{10,... | collective-permute-start | bytes 786440 | tf_op jit(solution)/shard_map/ppermute | solution.py:303
  21.0 1.6 %collective-permute-start.10 = (bf16[4,256,128]{2,1,0:T(8,128)(2,1)S(1)}, bf16[4,256,128]{2,1,0:T(8,128)(2,1)S(1)}, u32[]{:S(2)}, u32[]{:S(2)}) collective-permute-start(bf16[4,256,128]{2,1,0:T(8,128)(2,1)S(1)} %get-tuple-element.53), channel_id=1, source_target_pairs={{0,3},{1,2},{2,1},{3,0},{4,7},{5,6},{6,5},{7,4},{8,11},{9,10},{10,... | collective-permute-start | bytes 786440 | tf_op jit(solution)/shard_map/ppermute | solution.py:278
  22.5 0.0 collective-permute-done.5.refs_2_
  22.6 2.7 %collective-permute-done.6.refs_3_ = bf16[4,128,128]{2,1,0:T(8,128)(2,1)S(1)} collective-permute-done((bf16[4,128,128]{2,1,0:T(8,128)(2,1)S(1)}, bf16[4,128,128]{2,1,0:T(8,128)(2,1)S(1)}, u32[]{:S(2)}, u32[]{:S(2)}) %collective-permute-start.6) | collective-permute-done | bytes 131104 | tf_op jit(solution)/shard_map/ppermute | solution.py:278
  25.2 0.0 collective-permute-done.4.refs_1_
  25.2 0.1 far_sum.3
  25.3 1.0 %collective-permute-start.7 = (f32[4,128,128]{2,1,0:T(8,128)S(1)}, f32[4,128,128]{2,1,0:T(8,128)S(1)}, u32[]{:S(2)}, u32[]{:S(2)}) collective-permute-start(f32[4,128,128]{2,1,0:T(8,128)S(1)} %get-tuple-element.49), channel_id=1, source_target_pairs={{0,4},{1,5},{2,6},{3,7},{4,0},{5,1},{6,2},{7,3},{8,12},{9,13},{10,... | collective-permute-start | bytes 786440 | tf_op jit(solution)/shard_map/ppermute | solution.py:310
  26.3 1.0 %collective-permute-start.8 = (bf16[4,256,128]{2,1,0:T(8,128)(2,1)S(1)}, bf16[4,256,128]{2,1,0:T(8,128)(2,1)S(1)}, u32[]{:S(2)}, u32[]{:S(2)}) collective-permute-start(bf16[4,256,128]{2,1,0:T(8,128)(2,1)S(1)} %get-tuple-element.51), channel_id=1, source_target_pairs={{0,1},{1,0},{2,3},{3,2},{4,5},{5,4},{6,7},{7,6},{8,9},{9,8},{10,11... | collective-permute-start | bytes 786440 | tf_op jit(solution)/shard_map/ppermute | solution.py:278
  27.2 4.9 %collective-permute-start.9 = (bf16[4,256,128]{2,1,0:T(8,128)(2,1)S(1)}, bf16[4,256,128]{2,1,0:T(8,128)(2,1)S(1)}, u32[]{:S(2)}, u32[]{:S(2)}) collective-permute-start(bf16[4,256,128]{2,1,0:T(8,128)(2,1)S(1)} %get-tuple-element.52), channel_id=1, source_target_pairs={{0,2},{1,3},{2,0},{3,1},{4,6},{5,7},{6,4},{7,5},{8,10},{9,11},{10,... | collective-permute-start | bytes 786440 | tf_op jit(solution)/shard_map/ppermute | solution.py:278
  32.1 0.4 collective-permute-done.3.refs_0_
  32.5 4.3 %collective-permute-done.10.refs_5_ = bf16[4,256,128]{2,1,0:T(8,128)(2,1)S(1)} collective-permute-done((bf16[4,256,128]{2,1,0:T(8,128)(2,1)S(1)}, bf16[4,256,128]{2,1,0:T(8,128)(2,1)S(1)}, u32[]{:S(2)}, u32[]{:S(2)}) %collective-permute-start.10) | collective-permute-done | bytes 262176 | tf_op jit(solution)/shard_map/ppermute | solution.py:278
  36.8 5.1 %collective-permute-done.7.refs_1_ = f32[4,128,128]{2,1,0:T(8,128)S(1)} collective-permute-done((f32[4,128,128]{2,1,0:T(8,128)S(1)}, f32[4,128,128]{2,1,0:T(8,128)S(1)}, u32[]{:S(2)}, u32[]{:S(2)}) %collective-permute-start.7) | collective-permute-done | bytes 262176 | tf_op jit(solution)/shard_map/ppermute | solution.py:310
  42.0 0.0 collective-permute-done.8.refs_3_
  42.0 1.6 %collective-permute-done.9.refs_4_ = bf16[4,256,128]{2,1,0:T(8,128)(2,1)S(1)} collective-permute-done((bf16[4,256,128]{2,1,0:T(8,128)(2,1)S(1)}, bf16[4,256,128]{2,1,0:T(8,128)(2,1)S(1)}, u32[]{:S(2)}, u32[]{:S(2)}) %collective-permute-start.9) | collective-permute-done | bytes 262176 | tf_op jit(solution)/shard_map/ppermute | solution.py:278
  43.5 0.5 %group_sum_code.1 = (bf16[2,128,128]{2,1,0:T(8,128)(2,1)S(1)}, bf16[2,128,128]{2,1,0:T(8,128)(2,1)S(1)}, bf16[2,128,128]{2,1,0:T(8,128)(2,1)S(1)}, bf16[2,128,128]{2,1,0:T(8,128)(2,1)S(1)}) custom-call(f32[4,128,128]{2,1,0:T(8,128)S(1)} %collective-permute-done.3.refs_0_, f32[4,128,128]{2,1,0:T(8,128)S(1)} %collective-permute-done.7.refs_1_, ...), custom_call_target="tpu_custom_call" | custom-call | flops 3932160 | bytes 1835008 | tf_op jit(solution)/shard_map/group_sum_code/pallas_call | solution.py:210
  44.0 0.1 collective-permute-start.11
  44.1 1.5 %collective-permute-start.12 = (bf16[2,128,128]{2,1,0:T(8,128)(2,1)S(1)}, bf16[2,128,128]{2,1,0:T(8,128)(2,1)S(1)}, u32[]{:S(2)}, u32[]{:S(2)}) collective-permute-start(bf16[2,128,128]{2,1,0:T(8,128)(2,1)S(1)} %get-tuple-element.56), channel_id=1, source_target_pairs={{0,16},{8,24},{16,0},{24,8},{1,17},{9,25},{17,1},{25,9},{2,18},{10... | collective-permute-start | bytes 196616 | tf_op jit(solution)/shard_map/ppermute | solution.py:284
  45.6 0.3 collective-permute-start.13
  46.0 0.0 collective-permute-done.11.refs_1_
  46.0 2.6 %collective-permute-done.12.refs_2_ = bf16[2,128,128]{2,1,0:T(8,128)(2,1)S(1)} collective-permute-done((bf16[2,128,128]{2,1,0:T(8,128)(2,1)S(1)}, bf16[2,128,128]{2,1,0:T(8,128)(2,1)S(1)}, u32[]{:S(2)}, u32[]{:S(2)}) %collective-permute-start.12) | collective-permute-done | bytes 65568 | tf_op jit(solution)/shard_map/ppermute | solution.py:284
  48.6 1.1 %collective-permute-done.13.refs_3_ = bf16[2,128,128]{2,1,0:T(8,128)(2,1)S(1)} collective-permute-done((bf16[2,128,128]{2,1,0:T(8,128)(2,1)S(1)}, bf16[2,128,128]{2,1,0:T(8,128)(2,1)S(1)}, u32[]{:S(2)}, u32[]{:S(2)}) %collective-permute-start.13) | collective-permute-done | bytes 65568 | tf_op jit(solution)/shard_map/ppermute | solution.py:284
  49.7 0.9 %sum_unrotate.1 = (f32[256,128]{1,0:T(8,128)}, f32[1,256]{1,0:T(1,128)}) custom-call(s32[256,128]{1,0:T(8,128)S(1)} %get-tuple-element.33.sign_ref, bf16[2,128,128]{2,1,0:T(8,128)(2,1)S(1)} %get-tuple-element.54.refs_0_, bf16[2,128,128]{2,1,0:T(8,128)(2,1)S(1)} %collective-permute-done.11.refs_1_, bf16[2,128,128]{2,1,0:T(8,128)(2,1)S(1)} %collective-permute-done.12.refs_2_, ...), custom_call_target="tpu_custom_call" | custom-call | tf_op jit(solution)/shard_map/sum_unrotate/pallas_call | solution.py:255
Async XLA Ops:
  4.6 12.0 %collective-permute-start = (bf16[4,128,128]{2,1,0:T(8,128)(2,1)S(1)}, bf16[4,128,128]{2,1,0:T(8,128)(2,1)S(1)}, u32[]{:S(2)}, u32[]{:S(2)}) collective-permute-start(bf16[4,128,128]{2,1,0:T(8,128)(2,1)S(1)} %get-tuple-element.35), channel_id=1, source_target_pairs={{0,1},{1,0},{2,3},{3,2},{4,5},{5,4},{6,7},{7,6},{8,9},{9,8},{10,11... | collective-permute-start | bytes 393224 | tf_op jit(solution)/shard_map/ppermute | solution.py:278
  7.6 9.0 %collective-permute-start.1 = (bf16[4,128,128]{2,1,0:T(8,128)(2,1)S(1)}, bf16[4,128,128]{2,1,0:T(8,128)(2,1)S(1)}, u32[]{:S(2)}, u32[]{:S(2)}) collective-permute-start(bf16[4,128,128]{2,1,0:T(8,128)(2,1)S(1)} %get-tuple-element.36), channel_id=1, source_target_pairs={{0,2},{1,3},{2,0},{3,1},{4,6},{5,7},{6,4},{7,5},{8,10},{9,11},{10,... | collective-permute-start | bytes 393224 | tf_op jit(solution)/shard_map/ppermute | solution.py:278
  9.2 7.4 %collective-permute-start.2 = (bf16[4,128,128]{2,1,0:T(8,128)(2,1)S(1)}, bf16[4,128,128]{2,1,0:T(8,128)(2,1)S(1)}, u32[]{:S(2)}, u32[]{:S(2)}) collective-permute-start(bf16[4,128,128]{2,1,0:T(8,128)(2,1)S(1)} %get-tuple-element.37), channel_id=1, source_target_pairs={{0,3},{1,2},{2,1},{3,0},{4,7},{5,6},{6,5},{7,4},{8,11},{9,10},{10,... | collective-permute-start | bytes 393224 | tf_op jit(solution)/shard_map/ppermute | solution.py:278
  9.2 13.4 %collective-permute-start.5 = (bf16[4,128,128]{2,1,0:T(8,128)(2,1)S(1)}, bf16[4,128,128]{2,1,0:T(8,128)(2,1)S(1)}, u32[]{:S(2)}, u32[]{:S(2)}) collective-permute-start(bf16[4,128,128]{2,1,0:T(8,128)(2,1)S(1)} %get-tuple-element.45), channel_id=1, source_target_pairs={{0,2},{1,3},{2,0},{3,1},{4,6},{5,7},{6,4},{7,5},{8,10},{9,11},{10,... | collective-permute-start | bytes 393224 | tf_op jit(solution)/shard_map/ppermute | solution.py:278
  15.1 10.1 %collective-permute-start.6 = (bf16[4,128,128]{2,1,0:T(8,128)(2,1)S(1)}, bf16[4,128,128]{2,1,0:T(8,128)(2,1)S(1)}, u32[]{:S(2)}, u32[]{:S(2)}) collective-permute-start(bf16[4,128,128]{2,1,0:T(8,128)(2,1)S(1)} %get-tuple-element.46), channel_id=1, source_target_pairs={{0,3},{1,2},{2,1},{3,0},{4,7},{5,6},{6,5},{7,4},{8,11},{9,10},{10,... | collective-permute-start | bytes 393224 | tf_op jit(solution)/shard_map/ppermute | solution.py:278
  16.7 8.6 %collective-permute-start.4 = (bf16[4,128,128]{2,1,0:T(8,128)(2,1)S(1)}, bf16[4,128,128]{2,1,0:T(8,128)(2,1)S(1)}, u32[]{:S(2)}, u32[]{:S(2)}) collective-permute-start(bf16[4,128,128]{2,1,0:T(8,128)(2,1)S(1)} %get-tuple-element.44), channel_id=1, source_target_pairs={{0,1},{1,0},{2,3},{3,2},{4,5},{5,4},{6,7},{7,6},{8,9},{9,8},{10,11... | collective-permute-start | bytes 393224 | tf_op jit(solution)/shard_map/ppermute | solution.py:278
  18.4 14.1 %collective-permute-start.3 = (f32[4,128,128]{2,1,0:T(8,128)S(1)}, f32[4,128,128]{2,1,0:T(8,128)S(1)}, u32[]{:S(2)}, u32[]{:S(2)}) collective-permute-start(f32[4,128,128]{2,1,0:T(8,128)S(1)} %get-tuple-element.42), channel_id=1, source_target_pairs={{0,4},{1,5},{2,6},{3,7},{4,0},{5,1},{6,2},{7,3},{8,12},{9,13},{10,... | collective-permute-start | bytes 786440 | tf_op jit(solution)/shard_map/ppermute | solution.py:303
  21.0 15.9 %collective-permute-start.10 = (bf16[4,256,128]{2,1,0:T(8,128)(2,1)S(1)}, bf16[4,256,128]{2,1,0:T(8,128)(2,1)S(1)}, u32[]{:S(2)}, u32[]{:S(2)}) collective-permute-start(bf16[4,256,128]{2,1,0:T(8,128)(2,1)S(1)} %get-tuple-element.53), channel_id=1, source_target_pairs={{0,3},{1,2},{2,1},{3,0},{4,7},{5,6},{6,5},{7,4},{8,11},{9,10},{10,... | collective-permute-start | bytes 786440 | tf_op jit(solution)/shard_map/ppermute | solution.py:278
  25.3 16.7 %collective-permute-start.7 = (f32[4,128,128]{2,1,0:T(8,128)S(1)}, f32[4,128,128]{2,1,0:T(8,128)S(1)}, u32[]{:S(2)}, u32[]{:S(2)}) collective-permute-start(f32[4,128,128]{2,1,0:T(8,128)S(1)} %get-tuple-element.49), channel_id=1, source_target_pairs={{0,4},{1,5},{2,6},{3,7},{4,0},{5,1},{6,2},{7,3},{8,12},{9,13},{10,... | collective-permute-start | bytes 786440 | tf_op jit(solution)/shard_map/ppermute | solution.py:310
  26.3 15.7 %collective-permute-start.8 = (bf16[4,256,128]{2,1,0:T(8,128)(2,1)S(1)}, bf16[4,256,128]{2,1,0:T(8,128)(2,1)S(1)}, u32[]{:S(2)}, u32[]{:S(2)}) collective-permute-start(bf16[4,256,128]{2,1,0:T(8,128)(2,1)S(1)} %get-tuple-element.51), channel_id=1, source_target_pairs={{0,1},{1,0},{2,3},{3,2},{4,5},{5,4},{6,7},{7,6},{8,9},{9,8},{10,11... | collective-permute-start | bytes 786440 | tf_op jit(solution)/shard_map/ppermute | solution.py:278
  27.2 16.3 %collective-permute-start.9 = (bf16[4,256,128]{2,1,0:T(8,128)(2,1)S(1)}, bf16[4,256,128]{2,1,0:T(8,128)(2,1)S(1)}, u32[]{:S(2)}, u32[]{:S(2)}) collective-permute-start(bf16[4,256,128]{2,1,0:T(8,128)(2,1)S(1)} %get-tuple-element.52), channel_id=1, source_target_pairs={{0,2},{1,3},{2,0},{3,1},{4,6},{5,7},{6,4},{7,5},{8,10},{9,11},{10,... | collective-permute-start | bytes 786440 | tf_op jit(solution)/shard_map/ppermute | solution.py:278
  44.0 1.9 %collective-permute-start.11 = (bf16[2,128,128]{2,1,0:T(8,128)(2,1)S(1)}, bf16[2,128,128]{2,1,0:T(8,128)(2,1)S(1)}, u32[]{:S(2)}, u32[]{:S(2)}) collective-permute-start(bf16[2,128,128]{2,1,0:T(8,128)(2,1)S(1)} %get-tuple-element.55), channel_id=1, source_target_pairs={{0,8},{8,0},{16,24},{24,16},{1,9},{9,1},{17,25},{25,17},{2,10},{10... | collective-permute-start | bytes 196616 | tf_op jit(solution)/shard_map/ppermute | solution.py:284
  44.1 4.5 %collective-permute-start.12 = (bf16[2,128,128]{2,1,0:T(8,128)(2,1)S(1)}, bf16[2,128,128]{2,1,0:T(8,128)(2,1)S(1)}, u32[]{:S(2)}, u32[]{:S(2)}) collective-permute-start(bf16[2,128,128]{2,1,0:T(8,128)(2,1)S(1)} %get-tuple-element.56), channel_id=1, source_target_pairs={{0,16},{8,24},{16,0},{24,8},{1,17},{9,25},{17,1},{25,9},{2,18},{10... | collective-permute-start | bytes 196616 | tf_op jit(solution)/shard_map/ppermute | solution.py:284
  45.6 4.0 %collective-permute-start.13 = (bf16[2,128,128]{2,1,0:T(8,128)(2,1)S(1)}, bf16[2,128,128]{2,1,0:T(8,128)(2,1)S(1)}, u32[]{:S(2)}, u32[]{:S(2)}) collective-permute-start(bf16[2,128,128]{2,1,0:T(8,128)(2,1)S(1)} %get-tuple-element.57), channel_id=1, source_target_pairs={{0,24},{8,16},{16,8},{24,0},{1,25},{9,17},{17,9},{25,1},{2,26},{10... | collective-permute-start | bytes 196616 | tf_op jit(solution)/shard_map/ppermute | solution.py:284

commit v10 on v9

--- a/solution.py
+++ b/solution.py
@@ -278,15 +278,16 @@
         return lax.ppermute(part, "local", pairs)
 
     def share(parts):
-        moved = [parts[0]]
-        for step in range(1, groups):
+        moved = []
+        for step in range(groups - 1, 0, -1):
             pairs = [(source, partner(source, step, groups)) for source in range(groups)]
             moved.append(lax.ppermute(parts[step], "node", pairs))
-        return moved
+        return moved + [parts[0]]
 
     values, sign_rows = partials.reshape(1, length), signs.reshape(length // LANES, LANES)
     counterparts = [(member, (member + half) % members) for member in range(members)]
-    fast, slow = list(range(1, half // 2)), list(range(half // 2, half))
+    slow, fast = list(range(max(half // 2, 1), half)), list(range(1, half // 2))
+    order = slow + fast + [0]
     outs = rotate(values, sign_rows, layout, True)
     far = [[outs[HALVES * step + part] for step in range(half)] for part in range(HALVES)]
     for step in slow + fast:
@@ -299,18 +300,19 @@
     *near, own_signs = outs
     for step in slow[1:]:
         far[1][step] = swap(far[1][step], step)
-    first, later = far_sum(far[0], [far[1][step] for step in fast] + near[1:])
+    first, later = far_sum([far[0][step] for step in order], [far[1][step] for step in fast] + near[1:])
     across = [lax.ppermute(first, "local", counterparts)]
     for step in fast:
         far[1][step] = swap(later.pop(0), step)
     near[1:] = later
-    for step in slow[1:]:
+    for step in slow[:1]:
         near[step] = swap(near[step], step)
-    second, later = far_sum(far[1], [near[step] for step in fast + slow[:1]])
+    rest = slow[1:] + fast
+    second, later = far_sum([far[1][step] for step in order], [near[step] for step in rest])
     across.append(lax.ppermute(second, "local", counterparts))
-    for step, part in zip(fast + slow[:1], later):
+    for step, part in zip(rest, later):
         near[step] = swap(part, step)
-    reduced, rotated_max = finish(share(group_sum(near, across, layout)), own_signs)
+    reduced, rotated_max = finish(share(group_sum([near[step] for step in order], across, layout)), own_signs)
     return (reduced.reshape(-1), rotated_max.reshape(-1))
 
 

time: 50.8 us -> 51.1 us (level)
  waiting for transfers between devices: 17.8 us -> 22.4 us
  starting transfers between devices: 22.7 us -> 18.3 us
    ppermute x9, starting transfers between devices: 17.2 us -> 12.7 us  [swap(): return lax.ppermute(part, 'local', pairs)]
    ppermute x1, waiting for transfers between devices: 0.4 us -> 4.59 us  [shards(): across = [lax.ppermute(first, 'local', counterparts)]]
where the time goes in v10:
time: 51.1 us; the launch traced here: 50.9 us
  waiting for transfers between devices  22.4 us (44%)
  starting transfers between devices  18.3 us (36%)
  Pallas kernels  9.48 us (19%)
  between operations  0.68 us (1%)
    ppermute x9, starting transfers between devices, swap(): return lax.ppermute(part, 'local', pairs)  12.7 us
    ppermute x9, waiting for transfers between devices, swap(): return lax.ppermute(part, 'local', pairs)  9.02 us
    pallas_call x2, Pallas kernels, rotate(): pl.pallas_call(functools.partial(rotate_kernel, layout, other, len(later)...  7.9 us
    ppermute x1, waiting for transfers between devices, shards(): across.append(lax.ppermute(second, 'local', counterparts))  4.86 us
    ppermute x1, waiting for transfers between devices, shards(): across = [lax.ppermute(first, 'local', counterparts)]  4.59 us
    ppermute x3, waiting for transfers between devices, share(): moved.append(lax.ppermute(parts[step], 'node', pairs))  3.94 us
    ppermute x1, starting transfers between devices, shards(): across = [lax.ppermute(first, 'local', counterparts)]  2.73 us
    ppermute x3, starting transfers between devices, share(): moved.append(lax.ppermute(parts[step], 'node', pairs))  1.92 us
  transfers between devices with their start and end apart: 14, of which 7 were waited for; matrix products, arithmetic and copies ran while one was open for 0% of the time, Pallas kernels for 8%

profile of v10, /device:TPU:0, one launch (start us, length us, event | category | flops | bytes accessed | tf_op | source)
XLA Modules:
  0.0 50.9 jit_solution(10572835200222822547)
XLA Ops:
  0.6 4.0 %rotate_code.2 = (bf16[4,128,128]{2,1,0:T(8,128)(2,1)S(1)}, bf16[4,128,128]{2,1,0:T(8,128)(2,1)S(1)}, bf16[4,128,128]{2,1,0:T(8,128)(2,1)S(1)}, bf16[4,128,128]{...) custom-call(bf16[1,1048576]{1,0:T(2,128)(2,1)} %bitcast.4, ...), custom_call_target="tpu_custom_call" | custom-call | flops 268435456 | bytes 5242880 | tf_op jit(solution)/shard_map/rotate_code/pallas_call | solution.py:146
  4.6 3.1 %collective-permute-start = (bf16[4,128,128]{2,1,0:T(8,128)(2,1)S(1)}, bf16[4,128,128]{2,1,0:T(8,128)(2,1)S(1)}, u32[]{:S(2)}, u32[]{:S(2)}) collective-permute-start(bf16[4,128,128]{2,1,0:T(8,128)(2,1)S(1)} %get-tuple-element.34), channel_id=1, source_target_pairs={{0,2},{1,3},{2,0},{3,1},{4,6},{5,7},{6,4},{7,5},{8,10},{9,11},{10,... | collective-permute-start | bytes 393224 | tf_op jit(solution)/shard_map/ppermute | solution.py:278
  7.7 1.4 %collective-permute-start.1 = (bf16[4,128,128]{2,1,0:T(8,128)(2,1)S(1)}, bf16[4,128,128]{2,1,0:T(8,128)(2,1)S(1)}, u32[]{:S(2)}, u32[]{:S(2)}) collective-permute-start(bf16[4,128,128]{2,1,0:T(8,128)(2,1)S(1)} %get-tuple-element.35), channel_id=1, source_target_pairs={{0,3},{1,2},{2,1},{3,0},{4,7},{5,6},{6,5},{7,4},{8,11},{9,10},{10,... | collective-permute-start | bytes 393224 | tf_op jit(solution)/shard_map/ppermute | solution.py:278
  9.1 0.1 collective-permute-start.2
  9.2 1.9 %collective-permute-start.4 = (bf16[4,128,128]{2,1,0:T(8,128)(2,1)S(1)}, bf16[4,128,128]{2,1,0:T(8,128)(2,1)S(1)}, u32[]{:S(2)}, u32[]{:S(2)}) collective-permute-start(bf16[4,128,128]{2,1,0:T(8,128)(2,1)S(1)} %get-tuple-element.43), channel_id=1, source_target_pairs={{0,2},{1,3},{2,0},{3,1},{4,6},{5,7},{6,4},{7,5},{8,10},{9,11},{10,... | collective-permute-start | bytes 393224 | tf_op jit(solution)/shard_map/ppermute | solution.py:278
  11.2 3.9 %rotate_code.3 = (bf16[4,128,128]{2,1,0:T(8,128)(2,1)S(1)}, bf16[4,128,128]{2,1,0:T(8,128)(2,1)S(1)}, bf16[4,256,128]{2,1,0:T(8,128)(2,1)S(1)}, bf16[4,256,128]{...) custom-call(bf16[1,1048576]{1,0:T(2,128)(2,1)} %bitcast.5, ...), custom_call_target="tpu_custom_call", output_to_operand_aliasing={{0}: (2, {}), {1}: (3, {})} | custom-call | flops 268435456 | bytes 5242880 | tf_op jit(solution)/shard_map/rotate_code/pallas_call | solution.py:146
  15.1 1.5 %collective-permute-start.5 = (bf16[4,128,128]{2,1,0:T(8,128)(2,1)S(1)}, bf16[4,128,128]{2,1,0:T(8,128)(2,1)S(1)}, u32[]{:S(2)}, u32[]{:S(2)}) collective-permute-start(bf16[4,128,128]{2,1,0:T(8,128)(2,1)S(1)} %get-tuple-element.44), channel_id=1, source_target_pairs={{0,3},{1,2},{2,1},{3,0},{4,7},{5,6},{6,5},{7,4},{8,11},{9,10},{10,... | collective-permute-start | bytes 393224 | tf_op jit(solution)/shard_map/ppermute | solution.py:278
  16.6 0.0 collective-permute-done.refs_0_
  16.6 0.0 collective-permute-done.1.refs_1_
  16.6 0.0 collective-permute-done.2.refs_2_
  16.6 0.1 far_sum.2
  16.7 0.4 collective-permute-start.6
  17.1 2.7 %collective-permute-start.3 = (f32[4,128,128]{2,1,0:T(8,128)S(1)}, f32[4,128,128]{2,1,0:T(8,128)S(1)}, u32[]{:S(2)}, u32[]{:S(2)}) collective-permute-start(f32[4,128,128]{2,1,0:T(8,128)S(1)} %get-tuple-element.42), channel_id=1, source_target_pairs={{0,4},{1,5},{2,6},{3,7},{4,0},{5,1},{6,2},{7,3},{8,12},{9,13},{10,... | collective-permute-start | bytes 786440 | tf_op jit(solution)/shard_map/ppermute | solution.py:304
  19.8 1.6 %collective-permute-start.8 = (bf16[4,256,128]{2,1,0:T(8,128)(2,1)S(1)}, bf16[4,256,128]{2,1,0:T(8,128)(2,1)S(1)}, u32[]{:S(2)}, u32[]{:S(2)}) collective-permute-start(bf16[4,256,128]{2,1,0:T(8,128)(2,1)S(1)} %get-tuple-element.50), channel_id=1, source_target_pairs={{0,2},{1,3},{2,0},{3,1},{4,6},{5,7},{6,4},{7,5},{8,10},{9,11},{10,... | collective-permute-start | bytes 786440 | tf_op jit(solution)/shard_map/ppermute | solution.py:278
  21.4 0.0 collective-permute-done.4.refs_0_
  21.4 3.6 %collective-permute-done.5.refs_1_ = bf16[4,128,128]{2,1,0:T(8,128)(2,1)S(1)} collective-permute-done((bf16[4,128,128]{2,1,0:T(8,128)(2,1)S(1)}, bf16[4,128,128]{2,1,0:T(8,128)(2,1)S(1)}, u32[]{:S(2)}, u32[]{:S(2)}) %collective-permute-start.5) | collective-permute-done | bytes 131104 | tf_op jit(solution)/shard_map/ppermute | solution.py:278
  25.0 0.0 collective-permute-done.6.refs_2_
  25.0 0.1 far_sum.3
  25.1 0.9 %collective-permute-start.7 = (f32[4,128,128]{2,1,0:T(8,128)S(1)}, f32[4,128,128]{2,1,0:T(8,128)S(1)}, u32[]{:S(2)}, u32[]{:S(2)}) collective-permute-start(f32[4,128,128]{2,1,0:T(8,128)S(1)} %get-tuple-element.49), channel_id=1, source_target_pairs={{0,4},{1,5},{2,6},{3,7},{4,0},{5,1},{6,2},{7,3},{8,12},{9,13},{10,... | collective-permute-start | bytes 786440 | tf_op jit(solution)/shard_map/ppermute | solution.py:312
  26.0 1.8 %collective-permute-start.9 = (bf16[4,256,128]{2,1,0:T(8,128)(2,1)S(1)}, bf16[4,256,128]{2,1,0:T(8,128)(2,1)S(1)}, u32[]{:S(2)}, u32[]{:S(2)}) collective-permute-start(bf16[4,256,128]{2,1,0:T(8,128)(2,1)S(1)} %get-tuple-element.51), channel_id=1, source_target_pairs={{0,3},{1,2},{2,1},{3,0},{4,7},{5,6},{6,5},{7,4},{8,11},{9,10},{10,... | collective-permute-start | bytes 786440 | tf_op jit(solution)/shard_map/ppermute | solution.py:278
  27.7 0.9 %collective-permute-start.10 = (bf16[4,256,128]{2,1,0:T(8,128)(2,1)S(1)}, bf16[4,256,128]{2,1,0:T(8,128)(2,1)S(1)}, u32[]{:S(2)}, u32[]{:S(2)}) collective-permute-start(bf16[4,256,128]{2,1,0:T(8,128)(2,1)S(1)} %get-tuple-element.52), channel_id=1, source_target_pairs={{0,1},{1,0},{2,3},{3,2},{4,5},{5,4},{6,7},{7,6},{8,9},{9,8},{10,11... | collective-permute-start | bytes 786440 | tf_op jit(solution)/shard_map/ppermute | solution.py:278
  28.6 4.6 %collective-permute-done.3.refs_0_ = f32[4,128,128]{2,1,0:T(8,128)S(1)} collective-permute-done((f32[4,128,128]{2,1,0:T(8,128)S(1)}, f32[4,128,128]{2,1,0:T(8,128)S(1)}, u32[]{:S(2)}, u32[]{:S(2)}) %collective-permute-start.3) | collective-permute-done | bytes 262176 | tf_op jit(solution)/shard_map/ppermute | solution.py:304
  33.2 3.2 %collective-permute-done.8.refs_2_ = bf16[4,256,128]{2,1,0:T(8,128)(2,1)S(1)} collective-permute-done((bf16[4,256,128]{2,1,0:T(8,128)(2,1)S(1)}, bf16[4,256,128]{2,1,0:T(8,128)(2,1)S(1)}, u32[]{:S(2)}, u32[]{:S(2)}) %collective-permute-start.8) | collective-permute-done | bytes 262176 | tf_op jit(solution)/shard_map/ppermute | solution.py:278
  36.4 4.9 %collective-permute-done.7.refs_1_ = f32[4,128,128]{2,1,0:T(8,128)S(1)} collective-permute-done((f32[4,128,128]{2,1,0:T(8,128)S(1)}, f32[4,128,128]{2,1,0:T(8,128)S(1)}, u32[]{:S(2)}, u32[]{:S(2)}) %collective-permute-start.7) | collective-permute-done | bytes 262176 | tf_op jit(solution)/shard_map/ppermute | solution.py:312
  41.3 2.2 %collective-permute-done.9.refs_3_ = bf16[4,256,128]{2,1,0:T(8,128)(2,1)S(1)} collective-permute-done((bf16[4,256,128]{2,1,0:T(8,128)(2,1)S(1)}, bf16[4,256,128]{2,1,0:T(8,128)(2,1)S(1)}, u32[]{:S(2)}, u32[]{:S(2)}) %collective-permute-start.9) | collective-permute-done | bytes 262176 | tf_op jit(solution)/shard_map/ppermute | solution.py:278
  43.5 0.0 collective-permute-done.10.refs_4_
  43.5 0.5 %group_sum_code.1 = (bf16[2,128,128]{2,1,0:T(8,128)(2,1)S(1)}, bf16[2,128,128]{2,1,0:T(8,128)(2,1)S(1)}, bf16[2,128,128]{2,1,0:T(8,128)(2,1)S(1)}, bf16[2,128,128]{2,1,0:T(8,128)(2,1)S(1)}) custom-call(f32[4,128,128]{2,1,0:T(8,128)S(1)} %collective-permute-done.3.refs_0_, f32[4,128,128]{2,1,0:T(8,128)S(1)} %collective-permute-done.7.refs_1_, ...), custom_call_target="tpu_custom_call" | custom-call | flops 3932160 | bytes 1835008 | tf_op jit(solution)/shard_map/group_sum_code/pallas_call | solution.py:210
  44.0 0.1 collective-permute-start.11
  44.1 1.6 %collective-permute-start.12 = (bf16[2,128,128]{2,1,0:T(8,128)(2,1)S(1)}, bf16[2,128,128]{2,1,0:T(8,128)(2,1)S(1)}, u32[]{:S(2)}, u32[]{:S(2)}) collective-permute-start(bf16[2,128,128]{2,1,0:T(8,128)(2,1)S(1)} %get-tuple-element.55), channel_id=1, source_target_pairs={{0,16},{8,24},{16,0},{24,8},{1,17},{9,25},{17,1},{25,9},{2,18},{10... | collective-permute-start | bytes 196616 | tf_op jit(solution)/shard_map/ppermute | solution.py:284
  45.7 0.3 collective-permute-start.13
  46.0 2.5 %collective-permute-done.11.refs_0_ = bf16[2,128,128]{2,1,0:T(8,128)(2,1)S(1)} collective-permute-done((bf16[2,128,128]{2,1,0:T(8,128)(2,1)S(1)}, bf16[2,128,128]{2,1,0:T(8,128)(2,1)S(1)}, u32[]{:S(2)}, u32[]{:S(2)}) %collective-permute-start.11) | collective-permute-done | bytes 65568 | tf_op jit(solution)/shard_map/ppermute | solution.py:284
  48.5 1.5 %collective-permute-done.12.refs_1_ = bf16[2,128,128]{2,1,0:T(8,128)(2,1)S(1)} collective-permute-done((bf16[2,128,128]{2,1,0:T(8,128)(2,1)S(1)}, bf16[2,128,128]{2,1,0:T(8,128)(2,1)S(1)}, u32[]{:S(2)}, u32[]{:S(2)}) %collective-permute-start.12) | collective-permute-done | bytes 65568 | tf_op jit(solution)/shard_map/ppermute | solution.py:284
  49.9 0.0 collective-permute-done.13.refs_2_
  49.9 0.9 %sum_unrotate.1 = (f32[256,128]{1,0:T(8,128)}, f32[1,256]{1,0:T(1,128)}) custom-call(s32[256,128]{1,0:T(8,128)S(1)} %get-tuple-element.33.sign_ref, bf16[2,128,128]{2,1,0:T(8,128)(2,1)S(1)} %collective-permute-done.11.refs_0_, bf16[2,128,128]{2,1,0:T(8,128)(2,1)S(1)} %collective-permute-done.12.refs_1_, ...), custom_call_target="tpu_custom_call" | custom-call | tf_op jit(solution)/shard_map/sum_unrotate/pallas_call | solution.py:255
Async XLA Ops:
  4.6 12.0 %collective-permute-start = (bf16[4,128,128]{2,1,0:T(8,128)(2,1)S(1)}, bf16[4,128,128]{2,1,0:T(8,128)(2,1)S(1)}, u32[]{:S(2)}, u32[]{:S(2)}) collective-permute-start(bf16[4,128,128]{2,1,0:T(8,128)(2,1)S(1)} %get-tuple-element.34), channel_id=1, source_target_pairs={{0,2},{1,3},{2,0},{3,1},{4,6},{5,7},{6,4},{7,5},{8,10},{9,11},{10,... | collective-permute-start | bytes 393224 | tf_op jit(solution)/shard_map/ppermute | solution.py:278
  7.7 8.9 %collective-permute-start.1 = (bf16[4,128,128]{2,1,0:T(8,128)(2,1)S(1)}, bf16[4,128,128]{2,1,0:T(8,128)(2,1)S(1)}, u32[]{:S(2)}, u32[]{:S(2)}) collective-permute-start(bf16[4,128,128]{2,1,0:T(8,128)(2,1)S(1)} %get-tuple-element.35), channel_id=1, source_target_pairs={{0,3},{1,2},{2,1},{3,0},{4,7},{5,6},{6,5},{7,4},{8,11},{9,10},{10,... | collective-permute-start | bytes 393224 | tf_op jit(solution)/shard_map/ppermute | solution.py:278
  9.1 7.5 %collective-permute-start.2 = (bf16[4,128,128]{2,1,0:T(8,128)(2,1)S(1)}, bf16[4,128,128]{2,1,0:T(8,128)(2,1)S(1)}, u32[]{:S(2)}, u32[]{:S(2)}) collective-permute-start(bf16[4,128,128]{2,1,0:T(8,128)(2,1)S(1)} %get-tuple-element.36), channel_id=1, source_target_pairs={{0,1},{1,0},{2,3},{3,2},{4,5},{5,4},{6,7},{7,6},{8,9},{9,8},{10,11... | collective-permute-start | bytes 393224 | tf_op jit(solution)/shard_map/ppermute | solution.py:278
  9.2 12.2 %collective-permute-start.4 = (bf16[4,128,128]{2,1,0:T(8,128)(2,1)S(1)}, bf16[4,128,128]{2,1,0:T(8,128)(2,1)S(1)}, u32[]{:S(2)}, u32[]{:S(2)}) collective-permute-start(bf16[4,128,128]{2,1,0:T(8,128)(2,1)S(1)} %get-tuple-element.43), channel_id=1, source_target_pairs={{0,2},{1,3},{2,0},{3,1},{4,6},{5,7},{6,4},{7,5},{8,10},{9,11},{10,... | collective-permute-start | bytes 393224 | tf_op jit(solution)/shard_map/ppermute | solution.py:278
  15.1 9.9 %collective-permute-start.5 = (bf16[4,128,128]{2,1,0:T(8,128)(2,1)S(1)}, bf16[4,128,128]{2,1,0:T(8,128)(2,1)S(1)}, u32[]{:S(2)}, u32[]{:S(2)}) collective-permute-start(bf16[4,128,128]{2,1,0:T(8,128)(2,1)S(1)} %get-tuple-element.44), channel_id=1, source_target_pairs={{0,3},{1,2},{2,1},{3,0},{4,7},{5,6},{6,5},{7,4},{8,11},{9,10},{10,... | collective-permute-start | bytes 393224 | tf_op jit(solution)/shard_map/ppermute | solution.py:278
  16.7 8.3 %collective-permute-start.6 = (bf16[4,128,128]{2,1,0:T(8,128)(2,1)S(1)}, bf16[4,128,128]{2,1,0:T(8,128)(2,1)S(1)}, u32[]{:S(2)}, u32[]{:S(2)}) collective-permute-start(bf16[4,128,128]{2,1,0:T(8,128)(2,1)S(1)} %get-tuple-element.45), channel_id=1, source_target_pairs={{0,1},{1,0},{2,3},{3,2},{4,5},{5,4},{6,7},{7,6},{8,9},{9,8},{10,11... | collective-permute-start | bytes 393224 | tf_op jit(solution)/shard_map/ppermute | solution.py:278
  17.1 16.1 %collective-permute-start.3 = (f32[4,128,128]{2,1,0:T(8,128)S(1)}, f32[4,128,128]{2,1,0:T(8,128)S(1)}, u32[]{:S(2)}, u32[]{:S(2)}) collective-permute-start(f32[4,128,128]{2,1,0:T(8,128)S(1)} %get-tuple-element.42), channel_id=1, source_target_pairs={{0,4},{1,5},{2,6},{3,7},{4,0},{5,1},{6,2},{7,3},{8,12},{9,13},{10,... | collective-permute-start | bytes 786440 | tf_op jit(solution)/shard_map/ppermute | solution.py:304
  19.8 16.6 %collective-permute-start.8 = (bf16[4,256,128]{2,1,0:T(8,128)(2,1)S(1)}, bf16[4,256,128]{2,1,0:T(8,128)(2,1)S(1)}, u32[]{:S(2)}, u32[]{:S(2)}) collective-permute-start(bf16[4,256,128]{2,1,0:T(8,128)(2,1)S(1)} %get-tuple-element.50), channel_id=1, source_target_pairs={{0,2},{1,3},{2,0},{3,1},{4,6},{5,7},{6,4},{7,5},{8,10},{9,11},{10,... | collective-permute-start | bytes 786440 | tf_op jit(solution)/shard_map/ppermute | solution.py:278
  25.1 16.2 %collective-permute-start.7 = (f32[4,128,128]{2,1,0:T(8,128)S(1)}, f32[4,128,128]{2,1,0:T(8,128)S(1)}, u32[]{:S(2)}, u32[]{:S(2)}) collective-permute-start(f32[4,128,128]{2,1,0:T(8,128)S(1)} %get-tuple-element.49), channel_id=1, source_target_pairs={{0,4},{1,5},{2,6},{3,7},{4,0},{5,1},{6,2},{7,3},{8,12},{9,13},{10,... | collective-permute-start | bytes 786440 | tf_op jit(solution)/shard_map/ppermute | solution.py:312
  26.0 17.6 %collective-permute-start.9 = (bf16[4,256,128]{2,1,0:T(8,128)(2,1)S(1)}, bf16[4,256,128]{2,1,0:T(8,128)(2,1)S(1)}, u32[]{:S(2)}, u32[]{:S(2)}) collective-permute-start(bf16[4,256,128]{2,1,0:T(8,128)(2,1)S(1)} %get-tuple-element.51), channel_id=1, source_target_pairs={{0,3},{1,2},{2,1},{3,0},{4,7},{5,6},{6,5},{7,4},{8,11},{9,10},{10,... | collective-permute-start | bytes 786440 | tf_op jit(solution)/shard_map/ppermute | solution.py:278
  27.7 15.8 %collective-permute-start.10 = (bf16[4,256,128]{2,1,0:T(8,128)(2,1)S(1)}, bf16[4,256,128]{2,1,0:T(8,128)(2,1)S(1)}, u32[]{:S(2)}, u32[]{:S(2)}) collective-permute-start(bf16[4,256,128]{2,1,0:T(8,128)(2,1)S(1)} %get-tuple-element.52), channel_id=1, source_target_pairs={{0,1},{1,0},{2,3},{3,2},{4,5},{5,4},{6,7},{7,6},{8,9},{9,8},{10,11... | collective-permute-start | bytes 786440 | tf_op jit(solution)/shard_map/ppermute | solution.py:278
  44.0 4.4 %collective-permute-start.11 = (bf16[2,128,128]{2,1,0:T(8,128)(2,1)S(1)}, bf16[2,128,128]{2,1,0:T(8,128)(2,1)S(1)}, u32[]{:S(2)}, u32[]{:S(2)}) collective-permute-start(bf16[2,128,128]{2,1,0:T(8,128)(2,1)S(1)} %get-tuple-element.54), channel_id=1, source_target_pairs={{0,24},{8,16},{16,8},{24,0},{1,25},{9,17},{17,9},{25,1},{2,26},{10... | collective-permute-start | bytes 196616 | tf_op jit(solution)/shard_map/ppermute | solution.py:284
  44.1 5.8 %collective-permute-start.12 = (bf16[2,128,128]{2,1,0:T(8,128)(2,1)S(1)}, bf16[2,128,128]{2,1,0:T(8,128)(2,1)S(1)}, u32[]{:S(2)}, u32[]{:S(2)}) collective-permute-start(bf16[2,128,128]{2,1,0:T(8,128)(2,1)S(1)} %get-tuple-element.55), channel_id=1, source_target_pairs={{0,16},{8,24},{16,0},{24,8},{1,17},{9,25},{17,1},{25,9},{2,18},{10... | collective-permute-start | bytes 196616 | tf_op jit(solution)/shard_map/ppermute | solution.py:284
  45.7 4.2 %collective-permute-start.13 = (bf16[2,128,128]{2,1,0:T(8,128)(2,1)S(1)}, bf16[2,128,128]{2,1,0:T(8,128)(2,1)S(1)}, u32[]{:S(2)}, u32[]{:S(2)}) collective-permute-start(bf16[2,128,128]{2,1,0:T(8,128)(2,1)S(1)} %get-tuple-element.56), channel_id=1, source_target_pairs={{0,8},{8,0},{16,24},{24,16},{1,9},{9,1},{17,25},{25,17},{2,10},{10... | collective-permute-start | bytes 196616 | tf_op jit(solution)/shard_map/ppermute | solution.py:284

commit v11 on v10

--- a/solution.py
+++ b/solution.py
@@ -13,6 +13,7 @@
 VMEM_LIMIT = 50 * 1024 * 1024
 SUM_VMEM_LIMIT = 24 * 1024 * 1024
 AHEAD = 2
+PIECES = 4
 
 
 def sylvester():
@@ -61,26 +62,36 @@
     def shape(self):
         return (self.units, QGROUP, self.columns)
 
-
-def rotate_kernel(layout, other, later, values_ref, signs_ref, *refs):
+    def span(self, steps):
+        return 1 if len(steps) == 1 else self.half
+
+    def batch(self, steps):
+        batch = max(1, PIECES // len(steps))
+        return batch if self.units % batch == 0 else 1
+
+
+def rotate_kernel(layout, other, steps, cut, signed_out, extra, values_ref, signs_ref, *refs):
     values, flips, turned, matrix, value_sems, sign_sems = refs[-6:]
-    out_refs = refs[2 * later : -6]
+    out_refs = list(refs[extra:-6])
+    step_refs = [[out_refs.pop(0) for _ in range(HALVES if step in cut else 1)] for step in steps]
     half, portion, rows = layout.half, layout.portion, layout.rows
     node = lax.axis_index("node")
     member = lax.axis_index("local")
     inner = lax.rem(member, half)
     first = half - (member - inner) if other else member - inner
+    span, batch = layout.span(steps), layout.batch(steps)
+    lowest = partner(inner, steps[0], half) if span == 1 else 0
 
     def fetches(unit, part):
-        place = partner(node, unit * layout.together + part, layout.groups) * layout.members + first
+        place = partner(node, unit * layout.together + part, layout.groups) * layout.members + first + lowest
         return (
             pltpu.make_async_copy(
-                values_ref.at[:, pl.ds(pl.multiple_of(place * portion, portion), half * portion)],
+                values_ref.at[:, pl.ds(pl.multiple_of(place * portion, portion), span * portion)],
                 values.at[unit, part],
                 value_sems.at[unit, part],
             ),
             pltpu.make_async_copy(
-                signs_ref.at[pl.ds(pl.multiple_of(place * rows, rows), half * rows), :],
+                signs_ref.at[pl.ds(pl.multiple_of(place * rows, rows), span * rows), :],
                 flips.at[unit, part],
                 sign_sems.at[unit, part],
             ),
@@ -91,29 +102,34 @@
             for copy in fetches(unit, part):
                 copy.start()
 
-    for unit in range(min(AHEAD, layout.units)):
+    ahead = min(max(AHEAD, batch), layout.units)
+    for unit in range(ahead):
         fetch(unit)
     matrix[...] = sylvester()
 
-    def body(unit, carry):
-        for part in range(layout.together):
-            for copy in fetches(unit, part):
-                copy.wait()
-
-        @pl.when(unit + AHEAD < layout.units)
-        def _():
-            fetch(unit + AHEAD)
-
-        for step in range(half):
-            owner = partner(inner, step, half)
+    def body(turn, carry):
+        for index in range(batch):
+            for part in range(layout.together):
+                for copy in fetches(turn * batch + index, part):
+                    copy.wait()
+
+        if ahead < layout.units:
+            for index in range(batch):
+
+                @pl.when(turn * batch + index + ahead < layout.units)
+                def _():
+                    fetch(turn * batch + index + ahead)
+
+        for index, (position, step) in [(i, p) for i in range(batch) for p in enumerate(steps)]:
+            unit = turn * batch + index
+            slot = turned.at[index * len(steps) + position]
+            owner = 0 if span == 1 else partner(inner, step, half)
             at = pl.ds(pl.multiple_of(owner * portion, portion), portion)
             at_rows = pl.ds(pl.multiple_of(owner * rows, rows), rows)
             for part in range(layout.together):
                 wide = values[unit, part, :, at].astype(jnp.float32).reshape(rows, LANES)
-                turned[step, part * rows : (part + 1) * rows] = jnp.where(
-                    flips[unit, part, at_rows, :] == 0, wide, -wide
-                )
-            halves = [turned[step, pl.ds(part, layout.columns, stride=HALVES), :] for part in range(HALVES)]
+                slot[part * rows : (part + 1) * rows] = jnp.where(flips[unit, part, at_rows, :] == 0, wide, -wide)
+            halves = [slot[pl.ds(part, layout.columns, stride=HALVES), :] for part in range(HALVES)]
             signed = jnp.concatenate(halves, axis=1).astype(jnp.bfloat16)
             rotated = lax.dot_general(
                 matrix[...], signed, (((1,), (1,)), ((), ())), preferred_element_type=jnp.float32
@@ -121,39 +137,42 @@
             for part in range(HALVES):
                 rows_of = slice(part * QGROUP, (part + 1) * QGROUP)
                 coded = recode(rotated[rows_of]).astype(jnp.bfloat16)
-                if other:
-                    out_refs[step * HALVES + part][unit] = coded
+                if step in cut:
+                    step_refs[position][part][unit] = coded
                 else:
-                    out_refs[step][unit, rows_of] = coded
+                    step_refs[position][0][unit, rows_of] = coded
         return carry
 
-    lax.fori_loop(0, layout.units, body, 0)
-    if not other:
-        out_refs[-1][...] = flips[0, 0, pl.ds(pl.multiple_of(inner * rows, rows), rows), :]
-
-
-def rotate(values, signs, layout, other, later=()):
+    lax.fori_loop(0, layout.units // batch, body, 0)
+    if signed_out:
+        out_refs[0][...] = flips[0, 0, pl.ds(pl.multiple_of(inner * rows, rows), rows), :]
+
+
+def rotate(values, signs, layout, other, steps, cut=(), signed_out=False, after=(), later=()):
     half, units, columns = layout.half, layout.units, layout.columns
-    entries = half * layout.groups * layout.portion
-    outs = [jax.ShapeDtypeStruct(array.shape, array.dtype) for array in later]
-    if other:
-        outs += [jax.ShapeDtypeStruct(layout.shape(), jnp.bfloat16)] * (HALVES * half)
-    else:
-        outs += [jax.ShapeDtypeStruct((units, ROT, columns), jnp.bfloat16)] * half
+    span, batch = layout.span(steps), layout.batch(steps)
+    entries = len(steps) * layout.groups * layout.portion
+    passed = [jax.ShapeDtypeStruct(array.shape, array.dtype) for array in later]
+    outs = []
+    for step in steps:
+        cuts = HALVES if step in cut else 1
+        outs += [jax.ShapeDtypeStruct((units, ROT // cuts, columns), jnp.bfloat16)] * cuts
+    if signed_out:
         outs.append(jax.ShapeDtypeStruct((layout.rows, LANES), jnp.int32))
-    own = len(outs) - len(later)
+    extra = len(after) + 2 * len(later)
     return list(
         pl.pallas_call(
-            functools.partial(rotate_kernel, layout, other, len(later)),
-            in_specs=[pl.BlockSpec(memory_space=pltpu.HBM)] * 2 + [pl.BlockSpec(memory_space=pl.ANY)] * len(later),
+            functools.partial(rotate_kernel, layout, other, steps, cut, signed_out, extra),
+            in_specs=[pl.BlockSpec(memory_space=pltpu.HBM)] * 2
+            + [pl.BlockSpec(memory_space=pl.ANY)] * (len(after) + len(later)),
             out_specs=[pl.BlockSpec(memory_space=pl.ANY)] * len(later)
-            + [pl.BlockSpec(memory_space=pltpu.VMEM)] * own,
-            out_shape=outs,
-            input_output_aliases={2 + index: index for index in range(len(later))},
+            + [pl.BlockSpec(memory_space=pltpu.VMEM)] * len(outs),
+            out_shape=passed + outs,
+            input_output_aliases={2 + len(after) + index: index for index in range(len(later))},
             scratch_shapes=[
-                pltpu.VMEM((units, layout.together, 1, half * layout.portion), jnp.bfloat16),
-                pltpu.VMEM((units, layout.together, half * layout.rows, LANES), jnp.int32),
-                pltpu.VMEM((half, layout.together * layout.rows, LANES), jnp.float32),
+                pltpu.VMEM((units, layout.together, 1, span * layout.portion), jnp.bfloat16),
+                pltpu.VMEM((units, layout.together, span * layout.rows, LANES), jnp.int32),
+                pltpu.VMEM((batch * len(steps), layout.together * layout.rows, LANES), jnp.float32),
                 pltpu.VMEM((ROT, ROT), jnp.bfloat16),
                 pltpu.SemaphoreType.DMA((units, layout.together)),
                 pltpu.SemaphoreType.DMA((units, layout.together)),
@@ -161,7 +180,7 @@
             compiler_params=pltpu.CompilerParams(vmem_limit_bytes=VMEM_LIMIT),
             cost_estimate=pl.CostEstimate(flops=2 * entries * ROT, bytes_accessed=10 * entries, transcendentals=0),
             name="rotate_code",
-        )(values, signs, *later)
+        )(values, signs, *after, *later)
     )
 
 
@@ -172,19 +191,23 @@
     return total
 
 
-def far_sum_kernel(count, *refs):
-    refs[-1][...] = add_all([ref[...] for ref in refs[:count]])
-
-
-def far_sum(parts, later):
-    size = parts[0].size
+def far_sum_kernel(part, count, *refs):
+    arrays = []
+    for ref in refs[:count]:
+        cut = ref.shape[1] == QGROUP
+        arrays.append(ref[...] if cut else ref[:, part * QGROUP : (part + 1) * QGROUP])
+    refs[-1][...] = add_all(arrays)
+
+
+def far_sum(parts, layout, part, later):
+    size = QGROUP * layout.units * layout.columns
     *later, total = pl.pallas_call(
-        functools.partial(far_sum_kernel, len(parts)),
+        functools.partial(far_sum_kernel, part, len(parts)),
         in_specs=[pl.BlockSpec(memory_space=pltpu.VMEM)] * len(parts)
         + [pl.BlockSpec(memory_space=pl.ANY)] * len(later),
         out_specs=[pl.BlockSpec(memory_space=pl.ANY)] * len(later) + [pl.BlockSpec(memory_space=pltpu.VMEM)],
         out_shape=[jax.ShapeDtypeStruct(array.shape, array.dtype) for array in later]
-        + [jax.ShapeDtypeStruct(parts[0].shape, jnp.float32)],
+        + [jax.ShapeDtypeStruct(layout.shape(), jnp.float32)],
         input_output_aliases={len(parts) + index: index for index in range(len(later))},
         compiler_params=pltpu.CompilerParams(vmem_limit_bytes=SUM_VMEM_LIMIT),
         cost_estimate=pl.CostEstimate(
@@ -286,32 +309,30 @@
 
     values, sign_rows = partials.reshape(1, length), signs.reshape(length // LANES, LANES)
     counterparts = [(member, (member + half) % members) for member in range(members)]
-    slow, fast = list(range(max(half // 2, 1), half)), list(range(1, half // 2))
-    order = slow + fast + [0]
-    outs = rotate(values, sign_rows, layout, True)
-    far = [[outs[HALVES * step + part] for step in range(half)] for part in range(HALVES)]
-    for step in slow + fast:
-        far[0][step] = swap(far[0][step], step)
-    for step in slow[:1]:
-        far[1][step] = swap(far[1][step], step)
-    outs = rotate(values, sign_rows, layout, False, [far[1][step] for step in slow[1:] + fast])
-    for step in slow[1:] + fast:
-        far[1][step] = outs.pop(0)
-    *near, own_signs = outs
-    for step in slow[1:]:
-        far[1][step] = swap(far[1][step], step)
-    first, later = far_sum([far[0][step] for step in order], [far[1][step] for step in fast] + near[1:])
+    slow = half // 2
+    others = [step for step in range(half - 1, 0, -1) if step != slow]
+    order = [slow] + others + [0]
+    (part,) = rotate(values, sign_rows, layout, True, [slow])
+    far = {slow: [swap(part, slow)]}
+    outs = rotate(values, sign_rows, layout, True, others + [0], others, after=[part])
+    for step in others:
+        far[step] = [outs.pop(0), outs.pop(0)]
+    far[0] = outs
+    for step in others:
+        far[step][0] = swap(far[step][0], step)
+    for step in others[:-1]:
+        far[step][1] = swap(far[step][1], step)
+    last = others[-1]
+    far[last][1], part = rotate(values, sign_rows, layout, False, [slow], later=[far[last][1]])
+    first, (part, far[last][1]) = far_sum([far[step][0] for step in order], layout, 0, [part, far[last][1]])
     across = [lax.ppermute(first, "local", counterparts)]
-    for step in fast:
-        far[1][step] = swap(later.pop(0), step)
-    near[1:] = later
-    for step in slow[:1]:
-        near[step] = swap(near[step], step)
-    rest = slow[1:] + fast
-    second, later = far_sum([far[1][step] for step in order], [near[step] for step in rest])
+    near = {slow: swap(part, slow)}
+    far[last][1] = swap(far[last][1], last)
+    *outs, own_signs = rotate(values, sign_rows, layout, False, others + [0], signed_out=True, after=[first])
+    second, outs[:-1] = far_sum([far[step][-1] for step in order], layout, 1, outs[:-1])
     across.append(lax.ppermute(second, "local", counterparts))
-    for step, part in zip(rest, later):
-        near[step] = swap(part, step)
+    for step, part in zip(others + [0], outs):
+        near[step] = swap(part, step) if step else part
     reduced, rotated_max = finish(share(group_sum([near[step] for step in order], across, layout)), own_signs)
     return (reduced.reshape(-1), rotated_max.reshape(-1))
 

time: 51.1 us -> 55.7 us (1.090)
  Pallas kernels: 9.48 us -> 13 us
  waiting for transfers between devices: 22.4 us -> 25.2 us
  starting transfers between devices: 18.3 us -> 16.6 us
    pallas_call x4 -> x6, Pallas kernels: 8.03 us -> 11.5 us  [the longest x4 11.4 us: rotate(): pl.pallas_call(functools.partial(rotate_kernel, layout, other, steps, cut...]
    ppermute x1, waiting for transfers between devices: 4.59 us -> 5.84 us  [shards(): across = [lax.ppermute(first, 'local', counterparts)]]
    ppermute x9 -> x8, starting transfers between devices: 12.7 us -> 11.7 us  [swap(): return lax.ppermute(part, 'local', pairs)]
    ppermute x1, waiting for transfers between devices: 4.86 us -> 5.77 us  [shards(): across.append(lax.ppermute(second, 'local', counterparts))]
    ppermute x9 -> x8, waiting for transfers between devices: 9.02 us -> 9.6 us  [swap(): return lax.ppermute(part, 'local', pairs)]
  transfers between devices with their start and end apart: 14 -> 13, of which waited for: 7 -> 7; matrix products, arithmetic and copies ran while one was open for 0% -> 0% of each run, Pallas kernels for 8% -> 17%
where the time goes in v11:
time: 55.7 us; the launch traced here: 55.5 us
  waiting for transfers between devices  25.2 us (45%)
  starting transfers between devices  16.6 us (30%)
  Pallas kernels  13 us (23%)
  between operations  0.7 us (1%)
    ppermute x8, starting transfers between devices, swap(): return lax.ppermute(part, 'local', pairs)  11.7 us
    pallas_call x4, Pallas kernels, rotate(): pl.pallas_call(functools.partial(rotate_kernel, layout, other, steps, cut...  11.4 us
    ppermute x8, waiting for transfers between devices, swap(): return lax.ppermute(part, 'local', pairs)  9.6 us
    ppermute x1, waiting for transfers between devices, shards(): across = [lax.ppermute(first, 'local', counterparts)]  5.84 us
    ppermute x1, waiting for transfers between devices, shards(): across.append(lax.ppermute(second, 'local', counterparts))  5.77 us
    ppermute x3, waiting for transfers between devices, share(): moved.append(lax.ppermute(parts[step], 'node', pairs))  3.94 us
    ppermute x1, starting transfers between devices, shards(): across = [lax.ppermute(first, 'local', counterparts)]  2.59 us
    ppermute x3, starting transfers between devices, share(): moved.append(lax.ppermute(parts[step], 'node', pairs))  1.93 us
  transfers between devices with their start and end apart: 13, of which 7 were waited for; matrix products, arithmetic and copies ran while one was open for 0% of the time, Pallas kernels for 17%

profile of v11, /device:TPU:0, one launch (start us, length us, event | category | flops | bytes accessed | tf_op | source)
XLA Modules:
  0.0 55.5 jit_solution(4474037998313915515)
XLA Ops:
  0.6 2.0 %rotate_code.4.refs_0_ = bf16[4,256,128]{2,1,0:T(8,128)(2,1)S(1)} custom-call(bf16[1,1048576]{1,0:T(2,128)(2,1)} %bitcast.4, s32[8192,128]{1,0:T(8,128)} %bitcast.8), custom_call_target="tpu_custom_call" | custom-call | flops 67108864 | bytes 1310720 | tf_op jit(solution)/shard_map/rotate_code/pallas_call | solution.py:164
  2.7 3.1 %collective-permute-start = (bf16[4,256,128]{2,1,0:T(8,128)(2,1)S(1)}, bf16[4,256,128]{2,1,0:T(8,128)(2,1)S(1)}, u32[]{:S(2)}, u32[]{:S(2)}) collective-permute-start(bf16[4,256,128]{2,1,0:T(8,128)(2,1)S(1)} %rotate_code.4.refs_0_), channel_id=1, source_target_pairs={{0,2},{1,3},{2,0},{3,1},{4,6},{5,7},{6,4},{7,5},{8,10},{9,11},{10,... | collective-permute-start | bytes 786440 | tf_op jit(solution)/shard_map/ppermute | solution.py:301
  5.8 3.7 %rotate_code.5 = (bf16[4,128,128]{2,1,0:T(8,128)(2,1)S(1)}, bf16[4,128,128]{2,1,0:T(8,128)(2,1)S(1)}, bf16[4,128,128]{2,1,0:T(8,128)(2,1)S(1)}, bf16[4,128,128]{2,1,0:T(8,128)(2,1)S(1)}, bf16[4,256,128]{2,1,0:T(8,128)(2,1)S(1)}) custom-call(bf16[1,1048576]{1,0:T(2,128)(2,1)} %bitcast.5, s32[8192,128]{1,0:T(8,128)} %bitcast.9, ...), custom_call_target="tpu_custom_call" | custom-call | flops 201326592 | bytes 3932160 | tf_op jit(solution)/shard_map/rotate_code/pallas_call | solution.py:164
  9.4 1.5 %collective-permute-start.1 = (bf16[4,128,128]{2,1,0:T(8,128)(2,1)S(1)}, bf16[4,128,128]{2,1,0:T(8,128)(2,1)S(1)}, u32[]{:S(2)}, u32[]{:S(2)}) collective-permute-start(bf16[4,128,128]{2,1,0:T(8,128)(2,1)S(1)} %get-tuple-element.25), channel_id=1, source_target_pairs={{0,3},{1,2},{2,1},{3,0},{4,7},{5,6},{6,5},{7,4},{8,11},{9,10},{10,... | collective-permute-start | bytes 393224 | tf_op jit(solution)/shard_map/ppermute | solution.py:301
  10.9 0.2 collective-permute-start.2
  11.1 2.8 %collective-permute-start.4 = (bf16[4,128,128]{2,1,0:T(8,128)(2,1)S(1)}, bf16[4,128,128]{2,1,0:T(8,128)(2,1)S(1)}, u32[]{:S(2)}, u32[]{:S(2)}) collective-permute-start(bf16[4,128,128]{2,1,0:T(8,128)(2,1)S(1)} %get-tuple-element.33), channel_id=1, source_target_pairs={{0,3},{1,2},{2,1},{3,0},{4,7},{5,6},{6,5},{7,4},{8,11},{9,10},{10,... | collective-permute-start | bytes 393224 | tf_op jit(solution)/shard_map/ppermute | solution.py:301
  13.9 2.0 %rotate_code.6 = (bf16[4,128,128]{2,1,0:T(8,128)(2,1)S(1)}, bf16[4,256,128]{2,1,0:T(8,128)(2,1)S(1)}) custom-call(bf16[1,1048576]{1,0:T(2,128)(2,1)} %bitcast.6, s32[8192,128]{1,0:T(8,128)} %bitcast.10, bf16[4,128,128]{2,1,0:T(8,128)(2,1)S(1)} %get-tuple-element.28.refs_0_), custom_call_target="tpu_custom_call", output_to_operand_aliasing={{0}: (2, {})} | custom-call | flops 67108864 | bytes 1310720 | tf_op jit(solution)/shard_map/rotate_code/pallas_call | solution.py:164
  16.0 0.9 %collective-permute-done.1.refs_1_ = bf16[4,128,128]{2,1,0:T(8,128)(2,1)S(1)} collective-permute-done((bf16[4,128,128]{2,1,0:T(8,128)(2,1)S(1)}, bf16[4,128,128]{2,1,0:T(8,128)(2,1)S(1)}, u32[]{:S(2)}, u32[]{:S(2)}) %collective-permute-start.1) | collective-permute-done | bytes 131104 | tf_op jit(solution)/shard_map/ppermute | solution.py:301
  16.9 4.2 %collective-permute-done.2.refs_2_ = bf16[4,128,128]{2,1,0:T(8,128)(2,1)S(1)} collective-permute-done((bf16[4,128,128]{2,1,0:T(8,128)(2,1)S(1)}, bf16[4,128,128]{2,1,0:T(8,128)(2,1)S(1)}, u32[]{:S(2)}, u32[]{:S(2)}) %collective-permute-start.2) | collective-permute-done | bytes 131104 | tf_op jit(solution)/shard_map/ppermute | solution.py:301
  21.1 0.0 collective-permute-done.refs_0_
  21.1 0.1 far_sum.2
  21.2 0.6 %collective-permute-start.5 = (bf16[4,128,128]{2,1,0:T(8,128)(2,1)S(1)}, bf16[4,128,128]{2,1,0:T(8,128)(2,1)S(1)}, u32[]{:S(2)}, u32[]{:S(2)}) collective-permute-start(bf16[4,128,128]{2,1,0:T(8,128)(2,1)S(1)} %get-tuple-element.34), channel_id=1, source_target_pairs={{0,1},{1,0},{2,3},{3,2},{4,5},{5,4},{6,7},{7,6},{8,9},{9,8},{10,11... | collective-permute-start | bytes 393224 | tf_op jit(solution)/shard_map/ppermute | solution.py:301
  21.8 1.5 %collective-permute-start.7 = (bf16[4,256,128]{2,1,0:T(8,128)(2,1)S(1)}, bf16[4,256,128]{2,1,0:T(8,128)(2,1)S(1)}, u32[]{:S(2)}, u32[]{:S(2)}) collective-permute-start(bf16[4,256,128]{2,1,0:T(8,128)(2,1)S(1)} %get-tuple-element.38), channel_id=1, source_target_pairs={{0,2},{1,3},{2,0},{3,1},{4,6},{5,7},{6,4},{7,5},{8,10},{9,11},{10,... | collective-permute-start | bytes 786440 | tf_op jit(solution)/shard_map/ppermute | solution.py:301
  23.3 2.6 %collective-permute-start.3 = (f32[4,128,128]{2,1,0:T(8,128)S(1)}, f32[4,128,128]{2,1,0:T(8,128)S(1)}, u32[]{:S(2)}, u32[]{:S(2)}) collective-permute-start(f32[4,128,128]{2,1,0:T(8,128)S(1)} %get-tuple-element.31.refs_0_), channel_id=1, source_target_pairs={{0,4},{1,5},{2,6},{3,7},{4,0},{5,1},{6,2},{7,3},{8,12},{9,13},{10,... | collective-permute-start | bytes 786440 | tf_op jit(solution)/shard_map/ppermute | solution.py:328
  25.9 3.7 %rotate_code.7 = (bf16[4,256,128]{2,1,0:T(8,128)(2,1)S(1)}, bf16[4,256,128]{2,1,0:T(8,128)(2,1)S(1)}, bf16[4,256,128]{2,1,0:T(8,128)(2,1)S(1)}, s32[256,128]{1,0:T(8,128)S(1)}) custom-call(bf16[1,1048576]{1,0:T(2,128)(2,1)} %bitcast.7, s32[8192,128]{1,0:T(8,128)} %bitcast.11, f32[4,128,128]{2,1,0:T(8,128)S(1)} %get-tuple-element.31.refs_0_), custom_call_target="tpu_custom_call" | custom-call | flops 201326592 | bytes 3932160 | tf_op jit(solution)/shard_map/rotate_code/pallas_call | solution.py:164
  29.5 0.0 collective-permute-done.4.refs_1_
  29.6 0.0 collective-permute-done.5.refs_2_
  29.6 0.1 far_sum.3
  29.6 0.4 collective-permute-start.6
  30.0 1.5 %collective-permute-start.8 = (bf16[4,256,128]{2,1,0:T(8,128)(2,1)S(1)}, bf16[4,256,128]{2,1,0:T(8,128)(2,1)S(1)}, u32[]{:S(2)}, u32[]{:S(2)}) collective-permute-start(bf16[4,256,128]{2,1,0:T(8,128)(2,1)S(1)} %get-tuple-element.39), channel_id=1, source_target_pairs={{0,3},{1,2},{2,1},{3,0},{4,7},{5,6},{6,5},{7,4},{8,11},{9,10},{10,... | collective-permute-start | bytes 786440 | tf_op jit(solution)/shard_map/ppermute | solution.py:301
  31.5 0.6 collective-permute-start.9
  32.1 4.5 %collective-permute-done.7.refs_2_ = bf16[4,256,128]{2,1,0:T(8,128)(2,1)S(1)} collective-permute-done((bf16[4,256,128]{2,1,0:T(8,128)(2,1)S(1)}, bf16[4,256,128]{2,1,0:T(8,128)(2,1)S(1)}, u32[]{:S(2)}, u32[]{:S(2)}) %collective-permute-start.7) | collective-permute-done | bytes 262176 | tf_op jit(solution)/shard_map/ppermute | solution.py:301
  36.5 5.8 %collective-permute-done.3.refs_0_ = f32[4,128,128]{2,1,0:T(8,128)S(1)} collective-permute-done((f32[4,128,128]{2,1,0:T(8,128)S(1)}, f32[4,128,128]{2,1,0:T(8,128)S(1)}, u32[]{:S(2)}, u32[]{:S(2)}) %collective-permute-start.3) | collective-permute-done | bytes 262176 | tf_op jit(solution)/shard_map/ppermute | solution.py:328
  42.4 5.8 %collective-permute-done.6.refs_1_ = f32[4,128,128]{2,1,0:T(8,128)S(1)} collective-permute-done((f32[4,128,128]{2,1,0:T(8,128)S(1)}, f32[4,128,128]{2,1,0:T(8,128)S(1)}, u32[]{:S(2)}, u32[]{:S(2)}) %collective-permute-start.6) | collective-permute-done | bytes 262176 | tf_op jit(solution)/shard_map/ppermute | solution.py:333
  48.1 0.0 collective-permute-done.8.refs_3_
  48.1 0.0 collective-permute-done.9.refs_4_
  48.1 0.5 group_sum_code.1
  48.7 0.4 collective-permute-start.10
  49.1 1.2 %collective-permute-start.11 = (bf16[2,128,128]{2,1,0:T(8,128)(2,1)S(1)}, bf16[2,128,128]{2,1,0:T(8,128)(2,1)S(1)}, u32[]{:S(2)}, u32[]{:S(2)}) collective-permute-start(bf16[2,128,128]{2,1,0:T(8,128)(2,1)S(1)} %get-tuple-element.43), channel_id=1, source_target_pairs={{0,16},{8,24},{16,0},{24,8},{1,17},{9,25},{17,1},{25,9},{2,18},{10... | collective-permute-start | bytes 196616 | tf_op jit(solution)/shard_map/ppermute | solution.py:307
  50.3 0.3 collective-permute-start.12
  50.6 2.5 %collective-permute-done.10.refs_0_ = bf16[2,128,128]{2,1,0:T(8,128)(2,1)S(1)} collective-permute-done((bf16[2,128,128]{2,1,0:T(8,128)(2,1)S(1)}, bf16[2,128,128]{2,1,0:T(8,128)(2,1)S(1)}, u32[]{:S(2)}, u32[]{:S(2)}) %collective-permute-start.10) | collective-permute-done | bytes 65568 | tf_op jit(solution)/shard_map/ppermute | solution.py:307
  53.1 1.4 %collective-permute-done.11.refs_1_ = bf16[2,128,128]{2,1,0:T(8,128)(2,1)S(1)} collective-permute-done((bf16[2,128,128]{2,1,0:T(8,128)(2,1)S(1)}, bf16[2,128,128]{2,1,0:T(8,128)(2,1)S(1)}, u32[]{:S(2)}, u32[]{:S(2)}) %collective-permute-start.11) | collective-permute-done | bytes 65568 | tf_op jit(solution)/shard_map/ppermute | solution.py:307
  54.5 0.0 collective-permute-done.12.refs_2_
  54.5 0.9 %sum_unrotate.1 = (f32[256,128]{1,0:T(8,128)}, f32[1,256]{1,0:T(1,128)}) custom-call(s32[256,128]{1,0:T(8,128)S(1)} %get-tuple-element.32.sign_ref, bf16[2,128,128]{2,1,0:T(8,128)(2,1)S(1)} %collective-permute-done.10.refs_0_, bf16[2,128,128]{2,1,0:T(8,128)(2,1)S(1)} %collective-permute-done.11.refs_1_, ...), custom_call_target="tpu_custom_call" | custom-call | tf_op jit(solution)/shard_map/sum_unrotate/pallas_call | solution.py:278
Async XLA Ops:
  2.7 18.4 %collective-permute-start = (bf16[4,256,128]{2,1,0:T(8,128)(2,1)S(1)}, bf16[4,256,128]{2,1,0:T(8,128)(2,1)S(1)}, u32[]{:S(2)}, u32[]{:S(2)}) collective-permute-start(bf16[4,256,128]{2,1,0:T(8,128)(2,1)S(1)} %rotate_code.4.refs_0_), channel_id=1, source_target_pairs={{0,2},{1,3},{2,0},{3,1},{4,6},{5,7},{6,4},{7,5},{8,10},{9,11},{10,... | collective-permute-start | bytes 786440 | tf_op jit(solution)/shard_map/ppermute | solution.py:301
  9.4 7.5 %collective-permute-start.1 = (bf16[4,128,128]{2,1,0:T(8,128)(2,1)S(1)}, bf16[4,128,128]{2,1,0:T(8,128)(2,1)S(1)}, u32[]{:S(2)}, u32[]{:S(2)}) collective-permute-start(bf16[4,128,128]{2,1,0:T(8,128)(2,1)S(1)} %get-tuple-element.25), channel_id=1, source_target_pairs={{0,3},{1,2},{2,1},{3,0},{4,7},{5,6},{6,5},{7,4},{8,11},{9,10},{10,... | collective-permute-start | bytes 393224 | tf_op jit(solution)/shard_map/ppermute | solution.py:301
  10.9 10.2 %collective-permute-start.2 = (bf16[4,128,128]{2,1,0:T(8,128)(2,1)S(1)}, bf16[4,128,128]{2,1,0:T(8,128)(2,1)S(1)}, u32[]{:S(2)}, u32[]{:S(2)}) collective-permute-start(bf16[4,128,128]{2,1,0:T(8,128)(2,1)S(1)} %get-tuple-element.26), channel_id=1, source_target_pairs={{0,1},{1,0},{2,3},{3,2},{4,5},{5,4},{6,7},{7,6},{8,9},{9,8},{10,11... | collective-permute-start | bytes 393224 | tf_op jit(solution)/shard_map/ppermute | solution.py:301
  11.1 18.4 %collective-permute-start.4 = (bf16[4,128,128]{2,1,0:T(8,128)(2,1)S(1)}, bf16[4,128,128]{2,1,0:T(8,128)(2,1)S(1)}, u32[]{:S(2)}, u32[]{:S(2)}) collective-permute-start(bf16[4,128,128]{2,1,0:T(8,128)(2,1)S(1)} %get-tuple-element.33), channel_id=1, source_target_pairs={{0,3},{1,2},{2,1},{3,0},{4,7},{5,6},{6,5},{7,4},{8,11},{9,10},{10,... | collective-permute-start | bytes 393224 | tf_op jit(solution)/shard_map/ppermute | solution.py:301
  21.2 8.4 %collective-permute-start.5 = (bf16[4,128,128]{2,1,0:T(8,128)(2,1)S(1)}, bf16[4,128,128]{2,1,0:T(8,128)(2,1)S(1)}, u32[]{:S(2)}, u32[]{:S(2)}) collective-permute-start(bf16[4,128,128]{2,1,0:T(8,128)(2,1)S(1)} %get-tuple-element.34), channel_id=1, source_target_pairs={{0,1},{1,0},{2,3},{3,2},{4,5},{5,4},{6,7},{7,6},{8,9},{9,8},{10,11... | collective-permute-start | bytes 393224 | tf_op jit(solution)/shard_map/ppermute | solution.py:301
  21.8 14.7 %collective-permute-start.7 = (bf16[4,256,128]{2,1,0:T(8,128)(2,1)S(1)}, bf16[4,256,128]{2,1,0:T(8,128)(2,1)S(1)}, u32[]{:S(2)}, u32[]{:S(2)}) collective-permute-start(bf16[4,256,128]{2,1,0:T(8,128)(2,1)S(1)} %get-tuple-element.38), channel_id=1, source_target_pairs={{0,2},{1,3},{2,0},{3,1},{4,6},{5,7},{6,4},{7,5},{8,10},{9,11},{10,... | collective-permute-start | bytes 786440 | tf_op jit(solution)/shard_map/ppermute | solution.py:301
  23.3 19.1 %collective-permute-start.3 = (f32[4,128,128]{2,1,0:T(8,128)S(1)}, f32[4,128,128]{2,1,0:T(8,128)S(1)}, u32[]{:S(2)}, u32[]{:S(2)}) collective-permute-start(f32[4,128,128]{2,1,0:T(8,128)S(1)} %get-tuple-element.31.refs_0_), channel_id=1, source_target_pairs={{0,4},{1,5},{2,6},{3,7},{4,0},{5,1},{6,2},{7,3},{8,12},{9,13},{10,... | collective-permute-start | bytes 786440 | tf_op jit(solution)/shard_map/ppermute | solution.py:328
  29.6 18.5 %collective-permute-start.6 = (f32[4,128,128]{2,1,0:T(8,128)S(1)}, f32[4,128,128]{2,1,0:T(8,128)S(1)}, u32[]{:S(2)}, u32[]{:S(2)}) collective-permute-start(f32[4,128,128]{2,1,0:T(8,128)S(1)} %get-tuple-element.37), channel_id=1, source_target_pairs={{0,4},{1,5},{2,6},{3,7},{4,0},{5,1},{6,2},{7,3},{8,12},{9,13},{10,... | collective-permute-start | bytes 786440 | tf_op jit(solution)/shard_map/ppermute | solution.py:333
  30.0 18.1 %collective-permute-start.8 = (bf16[4,256,128]{2,1,0:T(8,128)(2,1)S(1)}, bf16[4,256,128]{2,1,0:T(8,128)(2,1)S(1)}, u32[]{:S(2)}, u32[]{:S(2)}) collective-permute-start(bf16[4,256,128]{2,1,0:T(8,128)(2,1)S(1)} %get-tuple-element.39), channel_id=1, source_target_pairs={{0,3},{1,2},{2,1},{3,0},{4,7},{5,6},{6,5},{7,4},{8,11},{9,10},{10,... | collective-permute-start | bytes 786440 | tf_op jit(solution)/shard_map/ppermute | solution.py:301
  31.5 16.6 %collective-permute-start.9 = (bf16[4,256,128]{2,1,0:T(8,128)(2,1)S(1)}, bf16[4,256,128]{2,1,0:T(8,128)(2,1)S(1)}, u32[]{:S(2)}, u32[]{:S(2)}) collective-permute-start(bf16[4,256,128]{2,1,0:T(8,128)(2,1)S(1)} %get-tuple-element.40), channel_id=1, source_target_pairs={{0,1},{1,0},{2,3},{3,2},{4,5},{5,4},{6,7},{7,6},{8,9},{9,8},{10,11... | collective-permute-start | bytes 786440 | tf_op jit(solution)/shard_map/ppermute | solution.py:301
  48.7 4.4 %collective-permute-start.10 = (bf16[2,128,128]{2,1,0:T(8,128)(2,1)S(1)}, bf16[2,128,128]{2,1,0:T(8,128)(2,1)S(1)}, u32[]{:S(2)}, u32[]{:S(2)}) collective-permute-start(bf16[2,128,128]{2,1,0:T(8,128)(2,1)S(1)} %get-tuple-element.42), channel_id=1, source_target_pairs={{0,24},{8,16},{16,8},{24,0},{1,25},{9,17},{17,9},{25,1},{2,26},{10... | collective-permute-start | bytes 196616 | tf_op jit(solution)/shard_map/ppermute | solution.py:307
  49.1 5.5 %collective-permute-start.11 = (bf16[2,128,128]{2,1,0:T(8,128)(2,1)S(1)}, bf16[2,128,128]{2,1,0:T(8,128)(2,1)S(1)}, u32[]{:S(2)}, u32[]{:S(2)}) collective-permute-start(bf16[2,128,128]{2,1,0:T(8,128)(2,1)S(1)} %get-tuple-element.43), channel_id=1, source_target_pairs={{0,16},{8,24},{16,0},{24,8},{1,17},{9,25},{17,1},{25,9},{2,18},{10... | collective-permute-start | bytes 196616 | tf_op jit(solution)/shard_map/ppermute | solution.py:307
  50.3 4.2 %collective-permute-start.12 = (bf16[2,128,128]{2,1,0:T(8,128)(2,1)S(1)}, bf16[2,128,128]{2,1,0:T(8,128)(2,1)S(1)}, u32[]{:S(2)}, u32[]{:S(2)}) collective-permute-start(bf16[2,128,128]{2,1,0:T(8,128)(2,1)S(1)} %get-tuple-element.44), channel_id=1, source_target_pairs={{0,8},{8,0},{16,24},{24,16},{1,9},{9,1},{17,25},{25,17},{2,10},{10... | collective-permute-start | bytes 196616 | tf_op jit(solution)/shard_map/ppermute | solution.py:307

commit v12 on v11

--- a/solution.py
+++ b/solution.py
@@ -13,7 +13,7 @@
 VMEM_LIMIT = 50 * 1024 * 1024
 SUM_VMEM_LIMIT = 24 * 1024 * 1024
 AHEAD = 2
-PIECES = 4
+PIECES = 8
 
 
 def sylvester():
@@ -218,27 +218,28 @@
     return total, later
 
 
-def group_sum_kernel(layout, *refs):
-    across_refs, near_refs, out_refs = refs[:HALVES], refs[HALVES : HALVES + layout.half], refs[HALVES + layout.half :]
-    for half, across_ref in enumerate(across_refs):
-        near = [ref[:, half * QGROUP : (half + 1) * QGROUP] for ref in near_refs]
-        first = recode(add_all(near + [across_ref[...]])).astype(jnp.bfloat16)
-        for section, out_ref in enumerate(out_refs):
-            at = section % layout.together * layout.blocks
-            out_ref[half] = first[section // layout.together, :, at : at + layout.blocks]
-
-
-def group_sum(near, across, layout):
-    size = near[0].size
+def group_sum_kernel(layout, part, count, *refs):
+    arrays = []
+    for ref in refs[:count]:
+        cut = ref.shape[1] == QGROUP
+        arrays.append(ref[...] if cut else ref[:, part * QGROUP : (part + 1) * QGROUP])
+    first = recode(add_all(arrays)).astype(jnp.bfloat16)
+    for section, out_ref in enumerate(refs[count:]):
+        at = section % layout.together * layout.blocks
+        out_ref[...] = first[section // layout.together, :, at : at + layout.blocks]
+
+
+def group_sum(parts, layout, part):
+    size = QGROUP * layout.units * layout.columns
     return pl.pallas_call(
-        functools.partial(group_sum_kernel, layout),
-        out_shape=[jax.ShapeDtypeStruct((HALVES, QGROUP, layout.blocks), jnp.bfloat16)] * layout.groups,
+        functools.partial(group_sum_kernel, layout, part, len(parts)),
+        out_shape=[jax.ShapeDtypeStruct((QGROUP, layout.blocks), jnp.bfloat16)] * layout.groups,
         compiler_params=pltpu.CompilerParams(vmem_limit_bytes=SUM_VMEM_LIMIT),
         cost_estimate=pl.CostEstimate(
-            flops=30 * size, bytes_accessed=2 * (layout.half + 3) * size, transcendentals=0
+            flops=30 * size, bytes_accessed=2 * (len(parts) + 2) * size, transcendentals=0
         ),
         name="group_sum_code",
-    )(*across, *near)
+    )(*parts)
 
 
 def bfloat16_terms(values):
@@ -251,7 +252,8 @@
 
 def finish_kernel(sign_ref, *refs):
     out_ref, max_ref = refs[-2:]
-    second = [add_all([ref[half] for ref in refs[:-2]]) for half in range(HALVES)]
+    count = (len(refs) - 2) // HALVES
+    second = [add_all([ref[...] for ref in refs[half * count : (half + 1) * count]]) for half in range(HALVES)]
     blocks = second[0].shape[1]
     natural = jnp.concatenate([part.T for part in second], axis=1)
     block = lax.broadcasted_iota(jnp.int32, (blocks, HALVES * blocks), 0)
@@ -310,30 +312,36 @@
     values, sign_rows = partials.reshape(1, length), signs.reshape(length // LANES, LANES)
     counterparts = [(member, (member + half) % members) for member in range(members)]
     slow = half // 2
-    others = [step for step in range(half - 1, 0, -1) if step != slow]
-    order = [slow] + others + [0]
-    (part,) = rotate(values, sign_rows, layout, True, [slow])
-    far = {slow: [swap(part, slow)]}
-    outs = rotate(values, sign_rows, layout, True, others + [0], others, after=[part])
-    for step in others:
-        far[step] = [outs.pop(0), outs.pop(0)]
+    others = [slow] + [step for step in range(half - 1, 0, -1) if step != slow]
+    last = others[-1]
+    outs = rotate(values, sign_rows, layout, True, others + [0], others)
+    far = {step: [outs.pop(0), outs.pop(0)] for step in others}
     far[0] = outs
     for step in others:
         far[step][0] = swap(far[step][0], step)
     for step in others[:-1]:
         far[step][1] = swap(far[step][1], step)
-    last = others[-1]
-    far[last][1], part = rotate(values, sign_rows, layout, False, [slow], later=[far[last][1]])
-    first, (part, far[last][1]) = far_sum([far[step][0] for step in order], layout, 0, [part, far[last][1]])
+    part, *outs, own, own_signs = rotate(
+        values, sign_rows, layout, False, others + [0], others, signed_out=True, later=[far[last][1]]
+    )
+    first, outs = far_sum([far[step][0] for step in others + [0]], layout, 0, [part] + outs)
     across = [lax.ppermute(first, "local", counterparts)]
-    near = {slow: swap(part, slow)}
-    far[last][1] = swap(far[last][1], last)
-    *outs, own_signs = rotate(values, sign_rows, layout, False, others + [0], signed_out=True, after=[first])
-    second, outs[:-1] = far_sum([far[step][-1] for step in order], layout, 1, outs[:-1])
+    far[last][1] = swap(outs.pop(0), last)
+    near = {step: [outs.pop(0), outs.pop(0)] for step in others}
+    near[0] = [own]
+    near[slow][0] = swap(near[slow][0], slow)
+    later = [near[step][part] for part in range(HALVES) for step in others if part or step != slow]
+    second, outs = far_sum([far[step][-1] for step in others + [0]], layout, 1, later)
     across.append(lax.ppermute(second, "local", counterparts))
-    for step, part in zip(others + [0], outs):
-        near[step] = swap(part, step) if step else part
-    reduced, rotated_max = finish(share(group_sum([near[step] for step in order], across, layout)), own_signs)
+    for part in range(HALVES):
+        for step in others:
+            if part or step != slow:
+                near[step][part] = swap(outs.pop(0), step)
+    coded = []
+    for part in range(HALVES):
+        arrays = [near[step][min(part, len(near[step]) - 1)] for step in others + [0]]
+        coded += share(group_sum(arrays + [across[part]], layout, part))
+    reduced, rotated_max = finish(coded, own_signs)
     return (reduced.reshape(-1), rotated_max.reshape(-1))
 
 

time: 55.7 us -> 50.8 us (0.912)
  waiting for transfers between devices: 25.2 us -> 12.9 us
  starting transfers between devices: 16.6 us -> 26.7 us
  Pallas kernels: 13 us -> 10.3 us
    ppermute x1, waiting for transfers between devices: 5.84 us -> 0.01 us  [shards(): across = [lax.ppermute(first, 'local', counterparts)]]
    ppermute x1, waiting for transfers between devices: 5.77 us -> 0.01 us  [shards(): across.append(lax.ppermute(second, 'local', counterparts))]
    ppermute x8 -> x12, starting transfers between devices: 11.7 us -> 17.3 us  [swap(): return lax.ppermute(part, 'local', pairs)]
    pallas_call x4 -> x2, Pallas kernels: 11.4 us -> 8.65 us  [rotate(): pl.pallas_call(functools.partial(rotate_kernel, layout, other, steps, cut...]
    ppermute x1, starting transfers between devices: 0.4 us -> 2.6 us  [shards(): across.append(lax.ppermute(second, 'local', counterparts))]
    ppermute x3 -> x6, starting transfers between devices: 1.93 us -> 3.76 us  [share(): moved.append(lax.ppermute(parts[step], 'node', pairs))]
    ppermute x3 -> x6, waiting for transfers between devices: 3.94 us -> 3.36 us  [share(): moved.append(lax.ppermute(parts[step], 'node', pairs))]
    ppermute x8 -> x12, waiting for transfers between devices: 9.6 us -> 9.59 us  [swap(): return lax.ppermute(part, 'local', pairs)]
  transfers between devices with their start and end apart: 13 -> 20, of which waited for: 7 -> 7; matrix products, arithmetic and copies ran while one was open for 0% -> 0% of each run, Pallas kernels for 17% -> 10%
where the time goes in v12:
time: 50.8 us; the launch traced here: 50.6 us
  starting transfers between devices  26.7 us (53%)
  waiting for transfers between devices  12.9 us (25%)
  Pallas kernels  10.3 us (20%)
  between operations  0.72 us (1%)
    ppermute x12, starting transfers between devices, swap(): return lax.ppermute(part, 'local', pairs)  17.3 us
    ppermute x12, waiting for transfers between devices, swap(): return lax.ppermute(part, 'local', pairs)  9.59 us
    pallas_call x2, Pallas kernels, rotate(): pl.pallas_call(functools.partial(rotate_kernel, layout, other, steps, cut...  8.65 us
    ppermute x6, starting transfers between devices, share(): moved.append(lax.ppermute(parts[step], 'node', pairs))  3.76 us
    ppermute x6, waiting for transfers between devices, share(): moved.append(lax.ppermute(parts[step], 'node', pairs))  3.36 us
    ppermute x1, starting transfers between devices, shards(): across = [lax.ppermute(first, 'local', counterparts)]  2.96 us
    ppermute x1, starting transfers between devices, shards(): across.append(lax.ppermute(second, 'local', counterparts))  2.6 us
  transfers between devices with their start and end apart: 20, of which 7 were waited for; matrix products, arithmetic and copies ran while one was open for 0% of the time, Pallas kernels for 10%

profile of v12, /device:TPU:0, one launch (start us, length us, event | category | flops | bytes accessed | tf_op | source)
XLA Modules:
  0.0 50.6 jit_solution(15148194440582781379)
XLA Ops:
  0.6 4.3 %rotate_code.2 = (bf16[4,128,128]{2,1,0:T(8,128)(2,1)S(1)}, bf16[4,128,128]{2,1,0:T(8,128)(2,1)S(1)}, bf16[4,128,128]{2,1,0:T(8,128)(2,1)S(1)}, bf16[4,128,128]{...) custom-call(bf16[1,1048576]{1,0:T(2,128)(2,1)} %bitcast.4, ...), custom_call_target="tpu_custom_call" | custom-call | flops 268435456 | bytes 5242880 | tf_op jit(solution)/shard_map/rotate_code/pallas_call | solution.py:164
  5.0 3.1 %collective-permute-start = (bf16[4,128,128]{2,1,0:T(8,128)(2,1)S(1)}, bf16[4,128,128]{2,1,0:T(8,128)(2,1)S(1)}, u32[]{:S(2)}, u32[]{:S(2)}) collective-permute-start(bf16[4,128,128]{2,1,0:T(8,128)(2,1)S(1)} %get-tuple-element.44), channel_id=1, source_target_pairs={{0,2},{1,3},{2,0},{3,1},{4,6},{5,7},{6,4},{7,5},{8,10},{9,11},{10,... | collective-permute-start | bytes 393224 | tf_op jit(solution)/shard_map/ppermute | solution.py:303
  8.0 1.4 %collective-permute-start.1 = (bf16[4,128,128]{2,1,0:T(8,128)(2,1)S(1)}, bf16[4,128,128]{2,1,0:T(8,128)(2,1)S(1)}, u32[]{:S(2)}, u32[]{:S(2)}) collective-permute-start(bf16[4,128,128]{2,1,0:T(8,128)(2,1)S(1)} %get-tuple-element.45), channel_id=1, source_target_pairs={{0,3},{1,2},{2,1},{3,0},{4,7},{5,6},{6,5},{7,4},{8,11},{9,10},{10,... | collective-permute-start | bytes 393224 | tf_op jit(solution)/shard_map/ppermute | solution.py:303
  9.5 0.1 collective-permute-start.2
  9.6 1.9 %collective-permute-start.4 = (bf16[4,128,128]{2,1,0:T(8,128)(2,1)S(1)}, bf16[4,128,128]{2,1,0:T(8,128)(2,1)S(1)}, u32[]{:S(2)}, u32[]{:S(2)}) collective-permute-start(bf16[4,128,128]{2,1,0:T(8,128)(2,1)S(1)} %get-tuple-element.56), channel_id=1, source_target_pairs={{0,2},{1,3},{2,0},{3,1},{4,6},{5,7},{6,4},{7,5},{8,10},{9,11},{10,... | collective-permute-start | bytes 393224 | tf_op jit(solution)/shard_map/ppermute | solution.py:303
  11.5 1.4 %collective-permute-start.5 = (bf16[4,128,128]{2,1,0:T(8,128)(2,1)S(1)}, bf16[4,128,128]{2,1,0:T(8,128)(2,1)S(1)}, u32[]{:S(2)}, u32[]{:S(2)}) collective-permute-start(bf16[4,128,128]{2,1,0:T(8,128)(2,1)S(1)} %get-tuple-element.57), channel_id=1, source_target_pairs={{0,3},{1,2},{2,1},{3,0},{4,7},{5,6},{6,5},{7,4},{8,11},{9,10},{10,... | collective-permute-start | bytes 393224 | tf_op jit(solution)/shard_map/ppermute | solution.py:303
  12.9 4.3 %rotate_code.3 = (bf16[4,128,128]{2,1,0:T(8,128)(2,1)S(1)}, bf16[4,128,128]{2,1,0:T(8,128)(2,1)S(1)}, bf16[4,128,128]{2,1,0:T(8,128)(2,1)S(1)}, bf16[4,128,128]{...) custom-call(bf16[1,1048576]{1,0:T(2,128)(2,1)} %bitcast.5, ...), custom_call_target="tpu_custom_call", output_to_operand_aliasing={{0}: (2, {})} | custom-call | flops 268435456 | bytes 5242880 | tf_op jit(solution)/shard_map/rotate_code/pallas_call | solution.py:164
  17.3 0.0 collective-permute-done.refs_0_
  17.3 0.0 collective-permute-done.1.refs_1_
  17.3 0.0 collective-permute-done.2.refs_2_
  17.3 0.1 far_sum.2
  17.4 0.2 collective-permute-start.6
  17.6 3.0 %collective-permute-start.9 = (f32[4,128,128]{2,1,0:T(8,128)S(1)}, f32[4,128,128]{2,1,0:T(8,128)S(1)}, u32[]{:S(2)}, u32[]{:S(2)}) collective-permute-start(f32[4,128,128]{2,1,0:T(8,128)S(1)} %get-tuple-element.67), channel_id=1, source_target_pairs={{0,4},{1,5},{2,6},{3,7},{4,0},{5,1},{6,2},{7,3},{8,12},{9,13},{10,... | collective-permute-start | bytes 786440 | tf_op jit(solution)/shard_map/ppermute | solution.py:328
  20.6 1.6 %collective-permute-start.3 = (bf16[4,128,128]{2,1,0:T(8,128)(2,1)S(1)}, bf16[4,128,128]{2,1,0:T(8,128)(2,1)S(1)}, u32[]{:S(2)}, u32[]{:S(2)}) collective-permute-start(bf16[4,128,128]{2,1,0:T(8,128)(2,1)S(1)} %get-tuple-element.55), channel_id=1, source_target_pairs={{0,2},{1,3},{2,0},{3,1},{4,6},{5,7},{6,4},{7,5},{8,10},{9,11},{10,... | collective-permute-start | bytes 393224 | tf_op jit(solution)/shard_map/ppermute | solution.py:303
  22.1 0.0 collective-permute-done.4.refs_0_
  22.1 1.7 %collective-permute-done.5.refs_1_ = bf16[4,128,128]{2,1,0:T(8,128)(2,1)S(1)} collective-permute-done((bf16[4,128,128]{2,1,0:T(8,128)(2,1)S(1)}, bf16[4,128,128]{2,1,0:T(8,128)(2,1)S(1)}, u32[]{:S(2)}, u32[]{:S(2)}) %collective-permute-start.5) | collective-permute-done | bytes 131104 | tf_op jit(solution)/shard_map/ppermute | solution.py:303
  23.8 0.0 collective-permute-done.6.refs_2_
  23.8 0.1 far_sum.3
  23.9 1.2 %collective-permute-start.7 = (bf16[4,128,128]{2,1,0:T(8,128)(2,1)S(1)}, bf16[4,128,128]{2,1,0:T(8,128)(2,1)S(1)}, u32[]{:S(2)}, u32[]{:S(2)}) collective-permute-start(bf16[4,128,128]{2,1,0:T(8,128)(2,1)S(1)} %get-tuple-element.64), channel_id=1, source_target_pairs={{0,3},{1,2},{2,1},{3,0},{4,7},{5,6},{6,5},{7,4},{8,11},{9,10},{10,... | collective-permute-start | bytes 393224 | tf_op jit(solution)/shard_map/ppermute | solution.py:303
  25.1 1.5 %collective-permute-start.8 = (bf16[4,128,128]{2,1,0:T(8,128)(2,1)S(1)}, bf16[4,128,128]{2,1,0:T(8,128)(2,1)S(1)}, u32[]{:S(2)}, u32[]{:S(2)}) collective-permute-start(bf16[4,128,128]{2,1,0:T(8,128)(2,1)S(1)} %get-tuple-element.65), channel_id=1, source_target_pairs={{0,1},{1,0},{2,3},{3,2},{4,5},{5,4},{6,7},{7,6},{8,9},{9,8},{10,11... | collective-permute-start | bytes 393224 | tf_op jit(solution)/shard_map/ppermute | solution.py:303
  26.6 2.6 %collective-permute-start.16 = (f32[4,128,128]{2,1,0:T(8,128)S(1)}, f32[4,128,128]{2,1,0:T(8,128)S(1)}, u32[]{:S(2)}, u32[]{:S(2)}) collective-permute-start(f32[4,128,128]{2,1,0:T(8,128)S(1)} %get-tuple-element.75), channel_id=1, source_target_pairs={{0,4},{1,5},{2,6},{3,7},{4,0},{5,1},{6,2},{7,3},{8,12},{9,13},{10,... | collective-permute-start | bytes 786440 | tf_op jit(solution)/shard_map/ppermute | solution.py:335
  29.2 0.9 %collective-permute-done.3.refs_0_ = bf16[4,128,128]{2,1,0:T(8,128)(2,1)S(1)} collective-permute-done((bf16[4,128,128]{2,1,0:T(8,128)(2,1)S(1)}, bf16[4,128,128]{2,1,0:T(8,128)(2,1)S(1)}, u32[]{:S(2)}, u32[]{:S(2)}) %collective-permute-start.3) | collective-permute-done | bytes 131104 | tf_op jit(solution)/shard_map/ppermute | solution.py:303
  30.1 2.5 %collective-permute-start.13 = (bf16[4,128,128]{2,1,0:T(8,128)(2,1)S(1)}, bf16[4,128,128]{2,1,0:T(8,128)(2,1)S(1)}, u32[]{:S(2)}, u32[]{:S(2)}) collective-permute-start(bf16[4,128,128]{2,1,0:T(8,128)(2,1)S(1)} %get-tuple-element.72), channel_id=1, source_target_pairs={{0,2},{1,3},{2,0},{3,1},{4,6},{5,7},{6,4},{7,5},{8,10},{9,11},{10,... | collective-permute-start | bytes 393224 | tf_op jit(solution)/shard_map/ppermute | solution.py:303
  32.6 2.8 %collective-permute-done.7.refs_1_ = bf16[4,128,128]{2,1,0:T(8,128)(2,1)S(1)} collective-permute-done((bf16[4,128,128]{2,1,0:T(8,128)(2,1)S(1)}, bf16[4,128,128]{2,1,0:T(8,128)(2,1)S(1)}, u32[]{:S(2)}, u32[]{:S(2)}) %collective-permute-start.7) | collective-permute-done | bytes 131104 | tf_op jit(solution)/shard_map/ppermute | solution.py:303
  35.5 0.9 %collective-permute-start.14 = (bf16[4,128,128]{2,1,0:T(8,128)(2,1)S(1)}, bf16[4,128,128]{2,1,0:T(8,128)(2,1)S(1)}, u32[]{:S(2)}, u32[]{:S(2)}) collective-permute-start(bf16[4,128,128]{2,1,0:T(8,128)(2,1)S(1)} %get-tuple-element.73), channel_id=1, source_target_pairs={{0,3},{1,2},{2,1},{3,0},{4,7},{5,6},{6,5},{7,4},{8,11},{9,10},{10,... | collective-permute-start | bytes 393224 | tf_op jit(solution)/shard_map/ppermute | solution.py:303
  36.3 0.0 collective-permute-done.8.refs_2_
  36.3 1.5 %collective-permute-start.15 = (bf16[4,128,128]{2,1,0:T(8,128)(2,1)S(1)}, bf16[4,128,128]{2,1,0:T(8,128)(2,1)S(1)}, u32[]{:S(2)}, u32[]{:S(2)}) collective-permute-start(bf16[4,128,128]{2,1,0:T(8,128)(2,1)S(1)} %get-tuple-element.74), channel_id=1, source_target_pairs={{0,1},{1,0},{2,3},{3,2},{4,5},{5,4},{6,7},{7,6},{8,9},{9,8},{10,11... | collective-permute-start | bytes 393224 | tf_op jit(solution)/shard_map/ppermute | solution.py:303
  37.8 0.0 collective-permute-done.9.refs_4_
  37.8 0.3 group_sum_code.2
  38.1 0.1 collective-permute-start.10
  38.2 2.2 %collective-permute-done.13.refs_0_ = bf16[4,128,128]{2,1,0:T(8,128)(2,1)S(1)} collective-permute-done((bf16[4,128,128]{2,1,0:T(8,128)(2,1)S(1)}, bf16[4,128,128]{2,1,0:T(8,128)(2,1)S(1)}, u32[]{:S(2)}, u32[]{:S(2)}) %collective-permute-start.13) | collective-permute-done | bytes 131104 | tf_op jit(solution)/shard_map/ppermute | solution.py:303
  40.4 1.5 %collective-permute-start.11 = (bf16[128,128]{1,0:T(8,128)(2,1)S(1)}, bf16[128,128]{1,0:T(8,128)(2,1)S(1)}, u32[]{:S(2)}, u32[]{:S(2)}) collective-permute-start(bf16[128,128]{1,0:T(8,128)(2,1)S(1)} %get-tuple-element.69), channel_id=1, source_target_pairs={{0,16},{8,24},{16,0},{24,8},{1,17},{9,25},{17,1},{25,9},{2,18},{10... | collective-permute-start | bytes 98312 | tf_op jit(solution)/shard_map/ppermute | solution.py:309
  41.9 1.9 %collective-permute-done.14.refs_1_ = bf16[4,128,128]{2,1,0:T(8,128)(2,1)S(1)} collective-permute-done((bf16[4,128,128]{2,1,0:T(8,128)(2,1)S(1)}, bf16[4,128,128]{2,1,0:T(8,128)(2,1)S(1)}, u32[]{:S(2)}, u32[]{:S(2)}) %collective-permute-start.14) | collective-permute-done | bytes 131104 | tf_op jit(solution)/shard_map/ppermute | solution.py:303
  43.8 0.0 collective-permute-start.12
  43.8 0.0 collective-permute-done.15.refs_2_
  43.8 0.0 collective-permute-done.16.refs_4_
  43.8 0.3 group_sum_code.3
  44.1 1.7 %collective-permute-start.17 = (bf16[128,128]{1,0:T(8,128)(2,1)S(1)}, bf16[128,128]{1,0:T(8,128)(2,1)S(1)}, u32[]{:S(2)}, u32[]{:S(2)}) collective-permute-start(bf16[128,128]{1,0:T(8,128)(2,1)S(1)} %get-tuple-element.76), channel_id=1, source_target_pairs={{0,24},{8,16},{16,8},{24,0},{1,25},{9,17},{17,9},{25,1},{2,26},{10... | collective-permute-start | bytes 98312 | tf_op jit(solution)/shard_map/ppermute | solution.py:309
  45.7 0.5 %collective-permute-start.18 = (bf16[128,128]{1,0:T(8,128)(2,1)S(1)}, bf16[128,128]{1,0:T(8,128)(2,1)S(1)}, u32[]{:S(2)}, u32[]{:S(2)}) collective-permute-start(bf16[128,128]{1,0:T(8,128)(2,1)S(1)} %get-tuple-element.77), channel_id=1, source_target_pairs={{0,16},{8,24},{16,0},{24,8},{1,17},{9,25},{17,1},{25,9},{2,18},{10... | collective-permute-start | bytes 98312 | tf_op jit(solution)/shard_map/ppermute | solution.py:309
  46.3 0.0 collective-permute-done.10.refs_0_
  46.3 0.0 collective-permute-start.19
  46.3 0.0 collective-permute-done.11.refs_1_
  46.3 0.0 collective-permute-done.12.refs_2_
  46.3 1.2 %collective-permute-done.17.refs_4_ = bf16[128,128]{1,0:T(8,128)(2,1)S(1)} collective-permute-done((bf16[128,128]{1,0:T(8,128)(2,1)S(1)}, bf16[128,128]{1,0:T(8,128)(2,1)S(1)}, u32[]{:S(2)}, u32[]{:S(2)}) %collective-permute-start.17) | collective-permute-done | bytes 32800 | tf_op jit(solution)/shard_map/ppermute | solution.py:309
  47.5 2.2 %collective-permute-done.18.refs_5_ = bf16[128,128]{1,0:T(8,128)(2,1)S(1)} collective-permute-done((bf16[128,128]{1,0:T(8,128)(2,1)S(1)}, bf16[128,128]{1,0:T(8,128)(2,1)S(1)}, u32[]{:S(2)}, u32[]{:S(2)}) %collective-permute-start.18) | collective-permute-done | bytes 32800 | tf_op jit(solution)/shard_map/ppermute | solution.py:309
  49.6 0.0 collective-permute-done.19.refs_6_
  49.6 0.9 %sum_unrotate.1 = (f32[256,128]{1,0:T(8,128)}, f32[1,256]{1,0:T(1,128)}) custom-call(s32[256,128]{1,0:T(8,128)S(1)} %get-tuple-element.43.sign_ref, bf16[128,128]{1,0:T(8,128)(2,1)S(1)} %collective-permute-done.10.refs_0_, bf16[128,128]{1,0:T(8,128)(2,1)S(1)} %collective-permute-done.11.refs_1_, bf16[128,128]{1,0:T(8,128)(2,1)S(1)} %collective-permute-done.12.refs_2_, ...), custom_call_target="tpu_custom_call" | custom-call | tf_op jit(solution)/shard_map/sum_unrotate/pallas_call | solution.py:280
Async XLA Ops:
  5.0 12.3 %collective-permute-start = (bf16[4,128,128]{2,1,0:T(8,128)(2,1)S(1)}, bf16[4,128,128]{2,1,0:T(8,128)(2,1)S(1)}, u32[]{:S(2)}, u32[]{:S(2)}) collective-permute-start(bf16[4,128,128]{2,1,0:T(8,128)(2,1)S(1)} %get-tuple-element.44), channel_id=1, source_target_pairs={{0,2},{1,3},{2,0},{3,1},{4,6},{5,7},{6,4},{7,5},{8,10},{9,11},{10,... | collective-permute-start | bytes 393224 | tf_op jit(solution)/shard_map/ppermute | solution.py:303
  8.0 9.2 %collective-permute-start.1 = (bf16[4,128,128]{2,1,0:T(8,128)(2,1)S(1)}, bf16[4,128,128]{2,1,0:T(8,128)(2,1)S(1)}, u32[]{:S(2)}, u32[]{:S(2)}) collective-permute-start(bf16[4,128,128]{2,1,0:T(8,128)(2,1)S(1)} %get-tuple-element.45), channel_id=1, source_target_pairs={{0,3},{1,2},{2,1},{3,0},{4,7},{5,6},{6,5},{7,4},{8,11},{9,10},{10,... | collective-permute-start | bytes 393224 | tf_op jit(solution)/shard_map/ppermute | solution.py:303
  9.5 7.9 %collective-permute-start.2 = (bf16[4,128,128]{2,1,0:T(8,128)(2,1)S(1)}, bf16[4,128,128]{2,1,0:T(8,128)(2,1)S(1)}, u32[]{:S(2)}, u32[]{:S(2)}) collective-permute-start(bf16[4,128,128]{2,1,0:T(8,128)(2,1)S(1)} %get-tuple-element.46), channel_id=1, source_target_pairs={{0,1},{1,0},{2,3},{3,2},{4,5},{5,4},{6,7},{7,6},{8,9},{9,8},{10,11... | collective-permute-start | bytes 393224 | tf_op jit(solution)/shard_map/ppermute | solution.py:303
  9.6 12.5 %collective-permute-start.4 = (bf16[4,128,128]{2,1,0:T(8,128)(2,1)S(1)}, bf16[4,128,128]{2,1,0:T(8,128)(2,1)S(1)}, u32[]{:S(2)}, u32[]{:S(2)}) collective-permute-start(bf16[4,128,128]{2,1,0:T(8,128)(2,1)S(1)} %get-tuple-element.56), channel_id=1, source_target_pairs={{0,2},{1,3},{2,0},{3,1},{4,6},{5,7},{6,4},{7,5},{8,10},{9,11},{10,... | collective-permute-start | bytes 393224 | tf_op jit(solution)/shard_map/ppermute | solution.py:303
  11.5 12.3 %collective-permute-start.5 = (bf16[4,128,128]{2,1,0:T(8,128)(2,1)S(1)}, bf16[4,128,128]{2,1,0:T(8,128)(2,1)S(1)}, u32[]{:S(2)}, u32[]{:S(2)}) collective-permute-start(bf16[4,128,128]{2,1,0:T(8,128)(2,1)S(1)} %get-tuple-element.57), channel_id=1, source_target_pairs={{0,3},{1,2},{2,1},{3,0},{4,7},{5,6},{6,5},{7,4},{8,11},{9,10},{10,... | collective-permute-start | bytes 393224 | tf_op jit(solution)/shard_map/ppermute | solution.py:303
  17.4 6.4 %collective-permute-start.6 = (bf16[4,128,128]{2,1,0:T(8,128)(2,1)S(1)}, bf16[4,128,128]{2,1,0:T(8,128)(2,1)S(1)}, u32[]{:S(2)}, u32[]{:S(2)}) collective-permute-start(bf16[4,128,128]{2,1,0:T(8,128)(2,1)S(1)} %get-tuple-element.58), channel_id=1, source_target_pairs={{0,1},{1,0},{2,3},{3,2},{4,5},{5,4},{6,7},{7,6},{8,9},{9,8},{10,11... | collective-permute-start | bytes 393224 | tf_op jit(solution)/shard_map/ppermute | solution.py:303
  17.6 20.3 %collective-permute-start.9 = (f32[4,128,128]{2,1,0:T(8,128)S(1)}, f32[4,128,128]{2,1,0:T(8,128)S(1)}, u32[]{:S(2)}, u32[]{:S(2)}) collective-permute-start(f32[4,128,128]{2,1,0:T(8,128)S(1)} %get-tuple-element.67), channel_id=1, source_target_pairs={{0,4},{1,5},{2,6},{3,7},{4,0},{5,1},{6,2},{7,3},{8,12},{9,13},{10,... | collective-permute-start | bytes 786440 | tf_op jit(solution)/shard_map/ppermute | solution.py:328
  20.6 9.6 %collective-permute-start.3 = (bf16[4,128,128]{2,1,0:T(8,128)(2,1)S(1)}, bf16[4,128,128]{2,1,0:T(8,128)(2,1)S(1)}, u32[]{:S(2)}, u32[]{:S(2)}) collective-permute-start(bf16[4,128,128]{2,1,0:T(8,128)(2,1)S(1)} %get-tuple-element.55), channel_id=1, source_target_pairs={{0,2},{1,3},{2,0},{3,1},{4,6},{5,7},{6,4},{7,5},{8,10},{9,11},{10,... | collective-permute-start | bytes 393224 | tf_op jit(solution)/shard_map/ppermute | solution.py:303
  23.9 11.6 %collective-permute-start.7 = (bf16[4,128,128]{2,1,0:T(8,128)(2,1)S(1)}, bf16[4,128,128]{2,1,0:T(8,128)(2,1)S(1)}, u32[]{:S(2)}, u32[]{:S(2)}) collective-permute-start(bf16[4,128,128]{2,1,0:T(8,128)(2,1)S(1)} %get-tuple-element.64), channel_id=1, source_target_pairs={{0,3},{1,2},{2,1},{3,0},{4,7},{5,6},{6,5},{7,4},{8,11},{9,10},{10,... | collective-permute-start | bytes 393224 | tf_op jit(solution)/shard_map/ppermute | solution.py:303
  25.1 11.2 %collective-permute-start.8 = (bf16[4,128,128]{2,1,0:T(8,128)(2,1)S(1)}, bf16[4,128,128]{2,1,0:T(8,128)(2,1)S(1)}, u32[]{:S(2)}, u32[]{:S(2)}) collective-permute-start(bf16[4,128,128]{2,1,0:T(8,128)(2,1)S(1)} %get-tuple-element.65), channel_id=1, source_target_pairs={{0,1},{1,0},{2,3},{3,2},{4,5},{5,4},{6,7},{7,6},{8,9},{9,8},{10,11... | collective-permute-start | bytes 393224 | tf_op jit(solution)/shard_map/ppermute | solution.py:303
  26.6 17.2 %collective-permute-start.16 = (f32[4,128,128]{2,1,0:T(8,128)S(1)}, f32[4,128,128]{2,1,0:T(8,128)S(1)}, u32[]{:S(2)}, u32[]{:S(2)}) collective-permute-start(f32[4,128,128]{2,1,0:T(8,128)S(1)} %get-tuple-element.75), channel_id=1, source_target_pairs={{0,4},{1,5},{2,6},{3,7},{4,0},{5,1},{6,2},{7,3},{8,12},{9,13},{10,... | collective-permute-start | bytes 786440 | tf_op jit(solution)/shard_map/ppermute | solution.py:335
  30.1 10.3 %collective-permute-start.13 = (bf16[4,128,128]{2,1,0:T(8,128)(2,1)S(1)}, bf16[4,128,128]{2,1,0:T(8,128)(2,1)S(1)}, u32[]{:S(2)}, u32[]{:S(2)}) collective-permute-start(bf16[4,128,128]{2,1,0:T(8,128)(2,1)S(1)} %get-tuple-element.72), channel_id=1, source_target_pairs={{0,2},{1,3},{2,0},{3,1},{4,6},{5,7},{6,4},{7,5},{8,10},{9,11},{10,... | collective-permute-start | bytes 393224 | tf_op jit(solution)/shard_map/ppermute | solution.py:303
  35.5 8.3 %collective-permute-start.14 = (bf16[4,128,128]{2,1,0:T(8,128)(2,1)S(1)}, bf16[4,128,128]{2,1,0:T(8,128)(2,1)S(1)}, u32[]{:S(2)}, u32[]{:S(2)}) collective-permute-start(bf16[4,128,128]{2,1,0:T(8,128)(2,1)S(1)} %get-tuple-element.73), channel_id=1, source_target_pairs={{0,3},{1,2},{2,1},{3,0},{4,7},{5,6},{6,5},{7,4},{8,11},{9,10},{10,... | collective-permute-start | bytes 393224 | tf_op jit(solution)/shard_map/ppermute | solution.py:303
  36.3 7.5 %collective-permute-start.15 = (bf16[4,128,128]{2,1,0:T(8,128)(2,1)S(1)}, bf16[4,128,128]{2,1,0:T(8,128)(2,1)S(1)}, u32[]{:S(2)}, u32[]{:S(2)}) collective-permute-start(bf16[4,128,128]{2,1,0:T(8,128)(2,1)S(1)} %get-tuple-element.74), channel_id=1, source_target_pairs={{0,1},{1,0},{2,3},{3,2},{4,5},{5,4},{6,7},{7,6},{8,9},{9,8},{10,11... | collective-permute-start | bytes 393224 | tf_op jit(solution)/shard_map/ppermute | solution.py:303
  38.1 8.2 %collective-permute-start.10 = (bf16[128,128]{1,0:T(8,128)(2,1)S(1)}, bf16[128,128]{1,0:T(8,128)(2,1)S(1)}, u32[]{:S(2)}, u32[]{:S(2)}) collective-permute-start(bf16[128,128]{1,0:T(8,128)(2,1)S(1)} %get-tuple-element.68), channel_id=1, source_target_pairs={{0,24},{8,16},{16,8},{24,0},{1,25},{9,17},{17,9},{25,1},{2,26},{10... | collective-permute-start | bytes 98312 | tf_op jit(solution)/shard_map/ppermute | solution.py:309
  40.4 5.9 %collective-permute-start.11 = (bf16[128,128]{1,0:T(8,128)(2,1)S(1)}, bf16[128,128]{1,0:T(8,128)(2,1)S(1)}, u32[]{:S(2)}, u32[]{:S(2)}) collective-permute-start(bf16[128,128]{1,0:T(8,128)(2,1)S(1)} %get-tuple-element.69), channel_id=1, source_target_pairs={{0,16},{8,24},{16,0},{24,8},{1,17},{9,25},{17,1},{25,9},{2,18},{10... | collective-permute-start | bytes 98312 | tf_op jit(solution)/shard_map/ppermute | solution.py:309
  43.8 2.5 %collective-permute-start.12 = (bf16[128,128]{1,0:T(8,128)(2,1)S(1)}, bf16[128,128]{1,0:T(8,128)(2,1)S(1)}, u32[]{:S(2)}, u32[]{:S(2)}) collective-permute-start(bf16[128,128]{1,0:T(8,128)(2,1)S(1)} %get-tuple-element.70), channel_id=1, source_target_pairs={{0,8},{8,0},{16,24},{24,16},{1,9},{9,1},{17,25},{25,17},{2,10},{10... | collective-permute-start | bytes 98312 | tf_op jit(solution)/shard_map/ppermute | solution.py:309
  44.1 3.4 %collective-permute-start.17 = (bf16[128,128]{1,0:T(8,128)(2,1)S(1)}, bf16[128,128]{1,0:T(8,128)(2,1)S(1)}, u32[]{:S(2)}, u32[]{:S(2)}) collective-permute-start(bf16[128,128]{1,0:T(8,128)(2,1)S(1)} %get-tuple-element.76), channel_id=1, source_target_pairs={{0,24},{8,16},{16,8},{24,0},{1,25},{9,17},{17,9},{25,1},{2,26},{10... | collective-permute-start | bytes 98312 | tf_op jit(solution)/shard_map/ppermute | solution.py:309
  45.7 3.9 %collective-permute-start.18 = (bf16[128,128]{1,0:T(8,128)(2,1)S(1)}, bf16[128,128]{1,0:T(8,128)(2,1)S(1)}, u32[]{:S(2)}, u32[]{:S(2)}) collective-permute-start(bf16[128,128]{1,0:T(8,128)(2,1)S(1)} %get-tuple-element.77), channel_id=1, source_target_pairs={{0,16},{8,24},{16,0},{24,8},{1,17},{9,25},{17,1},{25,9},{2,18},{10... | collective-permute-start | bytes 98312 | tf_op jit(solution)/shard_map/ppermute | solution.py:309
  46.3 3.4 %collective-permute-start.19 = (bf16[128,128]{1,0:T(8,128)(2,1)S(1)}, bf16[128,128]{1,0:T(8,128)(2,1)S(1)}, u32[]{:S(2)}, u32[]{:S(2)}) collective-permute-start(bf16[128,128]{1,0:T(8,128)(2,1)S(1)} %get-tuple-element.78), channel_id=1, source_target_pairs={{0,8},{8,0},{16,24},{24,16},{1,9},{9,1},{17,25},{25,17},{2,10},{10... | collective-permute-start | bytes 98312 | tf_op jit(solution)/shard_map/ppermute | solution.py:309

commit v13 on v7

--- a/solution.py
+++ b/solution.py
@@ -61,106 +61,107 @@
     def shape(self):
         return (self.units, QGROUP, self.columns)
 
-    def cuts(self, step, other):
-        return HALVES if other and self.half > 1 and step == self.half // 2 else 1
-
-
-def rotate_kernel(layout, other, values_ref, signs_ref, *refs):
+
+def rotate_kernel(layout, cut, values_ref, signs_ref, *refs):
     values, flips, turned, matrix, value_sems, sign_sems = refs[-6:]
+    half, portion, rows = layout.half, layout.portion, layout.rows
     out_refs = list(refs[:-6])
-    step_refs = [[out_refs.pop(0) for _ in range(layout.cuts(step, other))] for step in range(layout.half)]
-    half, portion, rows = layout.half, layout.portion, layout.rows
+    far_refs = [[out_refs.pop(0) for _ in range(HALVES if step in cut else 1)] for step in range(half)]
+    near_refs = [[out_refs.pop(0)] for _ in range(half)]
     node = lax.axis_index("node")
     member = lax.axis_index("local")
     inner = lax.rem(member, half)
-    first = half - (member - inner) if other else member - inner
-
-    def fetches(unit, part):
-        place = partner(node, unit * layout.together + part, layout.groups) * layout.members + first
+    firsts = (half - (member - inner), member - inner)
+
+    def fetches(unit, side, part):
+        place = partner(node, unit * layout.together + part, layout.groups) * layout.members + firsts[side]
         return (
             pltpu.make_async_copy(
                 values_ref.at[:, pl.ds(pl.multiple_of(place * portion, portion), half * portion)],
-                values.at[unit, part],
-                value_sems.at[unit, part],
+                values.at[unit, side, part],
+                value_sems.at[unit, side, part],
             ),
             pltpu.make_async_copy(
                 signs_ref.at[pl.ds(pl.multiple_of(place * rows, rows), half * rows), :],
-                flips.at[unit, part],
-                sign_sems.at[unit, part],
+                flips.at[unit, side, part],
+                sign_sems.at[unit, side, part],
             ),
         )
 
     def fetch(unit):
-        for part in range(layout.together):
-            for copy in fetches(unit, part):
-                copy.start()
+        for side in range(2):
+            for part in range(layout.together):
+                for copy in fetches(unit, side, part):
+                    copy.start()
 
     for unit in range(min(AHEAD, layout.units)):
         fetch(unit)
     matrix[...] = sylvester()
 
     def body(unit, carry):
-        for part in range(layout.together):
-            for copy in fetches(unit, part):
-                copy.wait()
-
         @pl.when(unit + AHEAD < layout.units)
         def _():
             fetch(unit + AHEAD)
 
-        for step in range(half):
-            owner = partner(inner, step, half)
-            at = pl.ds(pl.multiple_of(owner * portion, portion), portion)
-            at_rows = pl.ds(pl.multiple_of(owner * rows, rows), rows)
+        for side, side_refs in enumerate((far_refs, near_refs)):
             for part in range(layout.together):
-                wide = values[unit, part, :, at].astype(jnp.float32).reshape(rows, LANES)
-                turned[step, part * rows : (part + 1) * rows] = jnp.where(
-                    flips[unit, part, at_rows, :] == 0, wide, -wide
+                for copy in fetches(unit, side, part):
+                    copy.wait()
+            for step in range(half):
+                slot = turned.at[side * half + step]
+                owner = partner(inner, step, half)
+                at = pl.ds(pl.multiple_of(owner * portion, portion), portion)
+                at_rows = pl.ds(pl.multiple_of(owner * rows, rows), rows)
+                for part in range(layout.together):
+                    wide = values[unit, side, part, :, at].astype(jnp.float32).reshape(rows, LANES)
+                    signed = jnp.where(flips[unit, side, part, at_rows, :] == 0, wide, -wide)
+                    slot[part * rows : (part + 1) * rows] = signed
+                halves = [slot[pl.ds(part, layout.columns, stride=HALVES), :] for part in range(HALVES)]
+                signed = jnp.concatenate(halves, axis=1).astype(jnp.bfloat16)
+                rotated = lax.dot_general(
+                    matrix[...], signed, (((1,), (1,)), ((), ())), preferred_element_type=jnp.float32
                 )
-            halves = [turned[step, pl.ds(part, layout.columns, stride=HALVES), :] for part in range(HALVES)]
-            signed = jnp.concatenate(halves, axis=1).astype(jnp.bfloat16)
-            rotated = lax.dot_general(
-                matrix[...], signed, (((1,), (1,)), ((), ())), preferred_element_type=jnp.float32
-            )
-            for part in range(HALVES):
-                rows_of = slice(part * QGROUP, (part + 1) * QGROUP)
-                coded = recode(rotated[rows_of]).astype(jnp.bfloat16)
-                if len(step_refs[step]) > 1:
-                    step_refs[step][part][unit] = coded
-                else:
-                    step_refs[step][0][unit, rows_of] = coded
+                for part in range(HALVES):
+                    rows_of = slice(part * QGROUP, (part + 1) * QGROUP)
+                    coded = recode(rotated[rows_of]).astype(jnp.bfloat16)
+                    if len(side_refs[step]) > 1:
+                        side_refs[step][part][unit] = coded
+                    else:
+                        side_refs[step][0][unit, rows_of] = coded
         return carry
 
     lax.fori_loop(0, layout.units, body, 0)
-    if not other:
-        out_refs[0][...] = flips[0, 0, pl.ds(pl.multiple_of(inner * rows, rows), rows), :]
-
-
-def rotate(values, signs, layout, other):
+    out_refs[0][...] = flips[0, 1, 0, pl.ds(pl.multiple_of(inner * rows, rows), rows), :]
+
+
+def rotate(values, signs, layout, cut):
     half, units, columns = layout.half, layout.units, layout.columns
-    entries = half * layout.groups * layout.portion
     outs = []
-    for step in range(half):
-        cuts = layout.cuts(step, other)
+    for step in list(range(half)) + [None] * half:
+        cuts = HALVES if step in cut else 1
         outs += [jax.ShapeDtypeStruct((units, ROT // cuts, columns), jnp.bfloat16)] * cuts
-    if not other:
-        outs.append(jax.ShapeDtypeStruct((layout.rows, LANES), jnp.int32))
-    return pl.pallas_call(
-        functools.partial(rotate_kernel, layout, other),
+    outs.append(jax.ShapeDtypeStruct((layout.rows, LANES), jnp.int32))
+    outs = pl.pallas_call(
+        functools.partial(rotate_kernel, layout, cut),
         in_specs=[pl.BlockSpec(memory_space=pltpu.HBM)] * 2,
         out_shape=outs,
         scratch_shapes=[
-            pltpu.VMEM((units, layout.together, 1, half * layout.portion), jnp.bfloat16),
-            pltpu.VMEM((units, layout.together, half * layout.rows, LANES), jnp.int32),
-            pltpu.VMEM((half, layout.together * layout.rows, LANES), jnp.float32),
+            pltpu.VMEM((units, 2, layout.together, 1, half * layout.portion), jnp.bfloat16),
+            pltpu.VMEM((units, 2, layout.together, half * layout.rows, LANES), jnp.int32),
+            pltpu.VMEM((2 * half, layout.together * layout.rows, LANES), jnp.float32),
             pltpu.VMEM((ROT, ROT), jnp.bfloat16),
-            pltpu.SemaphoreType.DMA((units, layout.together)),
-            pltpu.SemaphoreType.DMA((units, layout.together)),
+            pltpu.SemaphoreType.DMA((units, 2, layout.together)),
+            pltpu.SemaphoreType.DMA((units, 2, layout.together)),
         ],
         compiler_params=pltpu.CompilerParams(vmem_limit_bytes=VMEM_LIMIT),
-        cost_estimate=pl.CostEstimate(flops=2 * entries * ROT, bytes_accessed=10 * entries, transcendentals=0),
+        cost_estimate=pl.CostEstimate(
+            flops=2 * values.size * ROT, bytes_accessed=10 * values.size, transcendentals=0
+        ),
         name="rotate_code",
     )(values, signs)
+    outs = list(outs)
+    far = [[outs.pop(0) for _ in range(HALVES if step in cut else 1)] for step in range(half)]
+    return far, outs[:-1], outs[-1]
 
 
 def add_all(arrays):
@@ -208,7 +209,7 @@
 
 
 def group_sum(near, across, layout):
-    size = ROT * layout.units * layout.columns
+    size = near[0].size
     return pl.pallas_call(
         functools.partial(group_sum_kernel, layout),
         out_shape=[jax.ShapeDtypeStruct((HALVES, QGROUP, layout.blocks), jnp.bfloat16)] * layout.groups,
@@ -280,34 +281,34 @@
         return lax.ppermute(part, "local", pairs)
 
     def share(parts):
-        moved = [parts[0]]
-        for step in range(1, groups):
+        moved = []
+        for step in range(groups - 1, 0, -1):
             pairs = [(source, partner(source, step, groups)) for source in range(groups)]
             moved.append(lax.ppermute(parts[step], "node", pairs))
-        return moved
-
-    values, sign_rows = partials.reshape(1, length), signs.reshape(length // LANES, LANES)
+        return moved + [parts[0]]
+
     counterparts = [(member, (member + half) % members) for member in range(members)]
-    steps = list(range(half - 1, 0, -1))
-    outs = list(rotate(values, sign_rows, layout, True))
-    far = [[outs.pop(0) for _ in range(layout.cuts(step, True))] for step in range(half)]
-    last = []
-    for step in steps:
+    slow = half // 2
+    others = [slow] + [step for step in range(half - 1, 0, -1) if step != slow]
+    order = others + [0]
+    last = others[-1]
+    far, near, own_signs = rotate(
+        partials.reshape(1, length), signs.reshape(length // LANES, LANES), layout, others
+    )
+    for step in others:
         far[step][0] = swap(far[step][0], step)
-        last += [step] if len(far[step]) > 1 else []
-    for step in last:
+    for step in others[:-1]:
         far[step][1] = swap(far[step][1], step)
-    *near, own_signs = rotate(values, sign_rows, layout, False)
-    across = []
-    for part in range(HALVES):
-        later = near[1:] if part == 0 else []
-        total, later = far_sum([arrays[min(part, len(arrays) - 1)] for arrays in far], layout, part, later)
-        across.append(lax.ppermute(total, "local", counterparts))
-        if part == 0:
-            near = near[:1] + later
-    for step in steps:
-        near[step] = swap(near[step], step)
-    reduced, rotated_max = finish(share(group_sum(near, across, layout)), own_signs)
+    later = [far[last][1]] + [near[step] for step in others]
+    first, later = far_sum([far[step][0] for step in order], layout, 0, later)
+    across = [lax.ppermute(first, "local", counterparts)]
+    far[last][1] = swap(later.pop(0), last)
+    near[slow] = swap(later.pop(0), slow)
+    second, later = far_sum([far[step][-1] for step in order], layout, 1, later)
+    across.append(lax.ppermute(second, "local", counterparts))
+    for step, part in zip(others[1:], later):
+        near[step] = swap(part, step)
+    reduced, rotated_max = finish(share(group_sum([near[step] for step in order], across, layout)), own_signs)
     return (reduced.reshape(-1), rotated_max.reshape(-1))
 
 

time: 53.7 us -> 53.4 us (level)
  starting transfers between devices: 15.3 us -> 18.7 us
  waiting for transfers between devices: 28 us -> 25.6 us
  Pallas kernels: 9.48 us -> 8.29 us
    ppermute x7 -> x9, waiting for transfers between devices: 15.9 us -> 11.6 us  [swap(): return lax.ppermute(part, 'local', pairs)]
    ppermute x7 -> x9, starting transfers between devices: 10.1 us -> 13.1 us  [swap(): return lax.ppermute(part, 'local', pairs)]
    ppermute x2, waiting for transfers between devices: 8.62 us -> 10.1 us  [the longest x1 6.4 us: shards(): across.append(lax.ppermute(second, 'local', counterparts))]
    pallas_call x2 -> x1, Pallas kernels: 7.9 us -> 6.71 us  [rotate(): pl.pallas_call(functools.partial(rotate_kernel, layout, cut), in_specs=[p...]
    ppermute x2, starting transfers between devices: 3.06 us -> 3.68 us  [the longest x1 2.68 us: shards(): across = [lax.ppermute(first, 'local', counterparts)]]
  transfers between devices with their start and end apart: 12 -> 14, of which waited for: 7 -> 9; matrix products, arithmetic and copies ran while one was open for 0% -> 0% of each run, Pallas kernels for 8% -> 0%
where the time goes in v13:
time: 53.4 us; the launch traced here: 53.3 us
  waiting for transfers between devices  25.6 us (48%)
  starting transfers between devices  18.7 us (35%)
  Pallas kernels  8.29 us (16%)
  between operations  0.67 us (1%)
    ppermute x9, starting transfers between devices, swap(): return lax.ppermute(part, 'local', pairs)  13.1 us
    ppermute x9, waiting for transfers between devices, swap(): return lax.ppermute(part, 'local', pairs)  11.6 us
    pallas_call x1, Pallas kernels, rotate(): pl.pallas_call(functools.partial(rotate_kernel, layout, cut), in_specs=[p...  6.71 us
    ppermute x1, waiting for transfers between devices, shards(): across.append(lax.ppermute(second, 'local', counterparts))  6.4 us
    ppermute x3, waiting for transfers between devices, share(): moved.append(lax.ppermute(parts[step], 'node', pairs))  3.94 us
    ppermute x1, waiting for transfers between devices, shards(): across = [lax.ppermute(first, 'local', counterparts)]  3.75 us
    ppermute x1, starting transfers between devices, shards(): across = [lax.ppermute(first, 'local', counterparts)]  2.68 us
    ppermute x3, starting transfers between devices, share(): moved.append(lax.ppermute(parts[step], 'node', pairs))  1.92 us
  transfers between devices with their start and end apart: 14, of which 9 were waited for; matrix products, arithmetic and copies ran while one was open for 0% of the time, Pallas kernels for 0%

profile of v13, /device:TPU:0, one launch (start us, length us, event | category | flops | bytes accessed | tf_op | source)
XLA Modules:
  0.0 53.3 jit_solution(14467350141596454589)
XLA Ops:
  0.6 6.7 %rotate_code.1 = (bf16[4,256,128]{2,1,0:T(8,128)(2,1)S(1)}, bf16[4,128,128]{2,1,0:T(8,128)(2,1)S(1)}, bf16[4,128,128]{2,1,0:T(8,128)(2,1)S(1)}, bf16[4,128,128]{...) custom-call(bf16[1,1048576]{1,0:T(2,128)(2,1)} %bitcast.4, ...), custom_call_target="tpu_custom_call" | custom-call | flops 536870912 | bytes 10485760 | tf_op jit(solution)/shard_map/rotate_code/pallas_call | solution.py:144
  7.3 3.1 %collective-permute-start = (bf16[4,128,128]{2,1,0:T(8,128)(2,1)S(1)}, bf16[4,128,128]{2,1,0:T(8,128)(2,1)S(1)}, u32[]{:S(2)}, u32[]{:S(2)}) collective-permute-start(bf16[4,128,128]{2,1,0:T(8,128)(2,1)S(1)} %get-tuple-element.29), channel_id=1, source_target_pairs={{0,2},{1,3},{2,0},{3,1},{4,6},{5,7},{6,4},{7,5},{8,10},{9,11},{10,... | collective-permute-start | bytes 393224 | tf_op jit(solution)/shard_map/ppermute | solution.py:281
  10.4 1.4 %collective-permute-start.1 = (bf16[4,128,128]{2,1,0:T(8,128)(2,1)S(1)}, bf16[4,128,128]{2,1,0:T(8,128)(2,1)S(1)}, u32[]{:S(2)}, u32[]{:S(2)}) collective-permute-start(bf16[4,128,128]{2,1,0:T(8,128)(2,1)S(1)} %get-tuple-element.30), channel_id=1, source_target_pairs={{0,3},{1,2},{2,1},{3,0},{4,7},{5,6},{6,5},{7,4},{8,11},{9,10},{10,... | collective-permute-start | bytes 393224 | tf_op jit(solution)/shard_map/ppermute | solution.py:281
  11.8 0.1 collective-permute-start.2
  12.0 1.9 %collective-permute-start.4 = (bf16[4,128,128]{2,1,0:T(8,128)(2,1)S(1)}, bf16[4,128,128]{2,1,0:T(8,128)(2,1)S(1)}, u32[]{:S(2)}, u32[]{:S(2)}) collective-permute-start(bf16[4,128,128]{2,1,0:T(8,128)(2,1)S(1)} %get-tuple-element.38), channel_id=1, source_target_pairs={{0,2},{1,3},{2,0},{3,1},{4,6},{5,7},{6,4},{7,5},{8,10},{9,11},{10,... | collective-permute-start | bytes 393224 | tf_op jit(solution)/shard_map/ppermute | solution.py:281
  13.9 1.4 %collective-permute-start.5 = (bf16[4,128,128]{2,1,0:T(8,128)(2,1)S(1)}, bf16[4,128,128]{2,1,0:T(8,128)(2,1)S(1)}, u32[]{:S(2)}, u32[]{:S(2)}) collective-permute-start(bf16[4,128,128]{2,1,0:T(8,128)(2,1)S(1)} %get-tuple-element.39), channel_id=1, source_target_pairs={{0,3},{1,2},{2,1},{3,0},{4,7},{5,6},{6,5},{7,4},{8,11},{9,10},{10,... | collective-permute-start | bytes 393224 | tf_op jit(solution)/shard_map/ppermute | solution.py:281
  15.3 0.0 collective-permute-done.refs_0_
  15.3 3.7 %collective-permute-done.1.refs_1_ = bf16[4,128,128]{2,1,0:T(8,128)(2,1)S(1)} collective-permute-done((bf16[4,128,128]{2,1,0:T(8,128)(2,1)S(1)}, bf16[4,128,128]{2,1,0:T(8,128)(2,1)S(1)}, u32[]{:S(2)}, u32[]{:S(2)}) %collective-permute-start.1) | collective-permute-done | bytes 131104 | tf_op jit(solution)/shard_map/ppermute | solution.py:281
  19.0 0.3 collective-permute-done.2.refs_2_
  19.3 0.1 far_sum.2
  19.4 0.5 collective-permute-start.6
  19.9 2.7 %collective-permute-start.3 = (f32[4,128,128]{2,1,0:T(8,128)S(1)}, f32[4,128,128]{2,1,0:T(8,128)S(1)}, u32[]{:S(2)}, u32[]{:S(2)}) collective-permute-start(f32[4,128,128]{2,1,0:T(8,128)S(1)} %get-tuple-element.37), channel_id=1, source_target_pairs={{0,4},{1,5},{2,6},{3,7},{4,0},{5,1},{6,2},{7,3},{8,12},{9,13},{10,... | collective-permute-start | bytes 786440 | tf_op jit(solution)/shard_map/ppermute | solution.py:304
  22.6 1.6 %collective-permute-start.8 = (bf16[4,256,128]{2,1,0:T(8,128)(2,1)S(1)}, bf16[4,256,128]{2,1,0:T(8,128)(2,1)S(1)}, u32[]{:S(2)}, u32[]{:S(2)}) collective-permute-start(bf16[4,256,128]{2,1,0:T(8,128)(2,1)S(1)} %get-tuple-element.44), channel_id=1, source_target_pairs={{0,2},{1,3},{2,0},{3,1},{4,6},{5,7},{6,4},{7,5},{8,10},{9,11},{10,... | collective-permute-start | bytes 786440 | tf_op jit(solution)/shard_map/ppermute | solution.py:281
  24.1 0.0 collective-permute-done.4.refs_0_
  24.1 3.1 %collective-permute-done.5.refs_1_ = bf16[4,128,128]{2,1,0:T(8,128)(2,1)S(1)} collective-permute-done((bf16[4,128,128]{2,1,0:T(8,128)(2,1)S(1)}, bf16[4,128,128]{2,1,0:T(8,128)(2,1)S(1)}, u32[]{:S(2)}, u32[]{:S(2)}) %collective-permute-start.5) | collective-permute-done | bytes 131104 | tf_op jit(solution)/shard_map/ppermute | solution.py:281
  27.3 0.0 collective-permute-done.6.refs_2_
  27.3 0.1 far_sum.3
  27.3 1.0 %collective-permute-start.7 = (f32[4,128,128]{2,1,0:T(8,128)S(1)}, f32[4,128,128]{2,1,0:T(8,128)S(1)}, u32[]{:S(2)}, u32[]{:S(2)}) collective-permute-start(f32[4,128,128]{2,1,0:T(8,128)S(1)} %get-tuple-element.43), channel_id=1, source_target_pairs={{0,4},{1,5},{2,6},{3,7},{4,0},{5,1},{6,2},{7,3},{8,12},{9,13},{10,... | collective-permute-start | bytes 786440 | tf_op jit(solution)/shard_map/ppermute | solution.py:308
  28.3 1.5 %collective-permute-start.9 = (bf16[4,256,128]{2,1,0:T(8,128)(2,1)S(1)}, bf16[4,256,128]{2,1,0:T(8,128)(2,1)S(1)}, u32[]{:S(2)}, u32[]{:S(2)}) collective-permute-start(bf16[4,256,128]{2,1,0:T(8,128)(2,1)S(1)} %get-tuple-element.45), channel_id=1, source_target_pairs={{0,3},{1,2},{2,1},{3,0},{4,7},{5,6},{6,5},{7,4},{8,11},{9,10},{10,... | collective-permute-start | bytes 786440 | tf_op jit(solution)/shard_map/ppermute | solution.py:281
  29.9 1.5 %collective-permute-start.10 = (bf16[4,256,128]{2,1,0:T(8,128)(2,1)S(1)}, bf16[4,256,128]{2,1,0:T(8,128)(2,1)S(1)}, u32[]{:S(2)}, u32[]{:S(2)}) collective-permute-start(bf16[4,256,128]{2,1,0:T(8,128)(2,1)S(1)} %get-tuple-element.46), channel_id=1, source_target_pairs={{0,1},{1,0},{2,3},{3,2},{4,5},{5,4},{6,7},{7,6},{8,9},{9,8},{10,11... | collective-permute-start | bytes 786440 | tf_op jit(solution)/shard_map/ppermute | solution.py:281
  31.4 3.7 %collective-permute-done.3.refs_0_ = f32[4,128,128]{2,1,0:T(8,128)S(1)} collective-permute-done((f32[4,128,128]{2,1,0:T(8,128)S(1)}, f32[4,128,128]{2,1,0:T(8,128)S(1)}, u32[]{:S(2)}, u32[]{:S(2)}) %collective-permute-start.3) | collective-permute-done | bytes 262176 | tf_op jit(solution)/shard_map/ppermute | solution.py:304
  35.1 2.6 %collective-permute-done.8.refs_2_ = bf16[4,256,128]{2,1,0:T(8,128)(2,1)S(1)} collective-permute-done((bf16[4,256,128]{2,1,0:T(8,128)(2,1)S(1)}, bf16[4,256,128]{2,1,0:T(8,128)(2,1)S(1)}, u32[]{:S(2)}, u32[]{:S(2)}) %collective-permute-start.8) | collective-permute-done | bytes 262176 | tf_op jit(solution)/shard_map/ppermute | solution.py:281
  37.7 6.4 %collective-permute-done.7.refs_1_ = f32[4,128,128]{2,1,0:T(8,128)S(1)} collective-permute-done((f32[4,128,128]{2,1,0:T(8,128)S(1)}, f32[4,128,128]{2,1,0:T(8,128)S(1)}, u32[]{:S(2)}, u32[]{:S(2)}) %collective-permute-start.7) | collective-permute-done | bytes 262176 | tf_op jit(solution)/shard_map/ppermute | solution.py:308
  44.1 1.8 %collective-permute-done.9.refs_3_ = bf16[4,256,128]{2,1,0:T(8,128)(2,1)S(1)} collective-permute-done((bf16[4,256,128]{2,1,0:T(8,128)(2,1)S(1)}, bf16[4,256,128]{2,1,0:T(8,128)(2,1)S(1)}, u32[]{:S(2)}, u32[]{:S(2)}) %collective-permute-start.9) | collective-permute-done | bytes 262176 | tf_op jit(solution)/shard_map/ppermute | solution.py:281
  46.0 0.0 collective-permute-done.10.refs_4_
  46.0 0.5 group_sum_code.1
  46.5 0.1 collective-permute-start.11
  46.5 1.6 %collective-permute-start.12 = (bf16[2,128,128]{2,1,0:T(8,128)(2,1)S(1)}, bf16[2,128,128]{2,1,0:T(8,128)(2,1)S(1)}, u32[]{:S(2)}, u32[]{:S(2)}) collective-permute-start(bf16[2,128,128]{2,1,0:T(8,128)(2,1)S(1)} %get-tuple-element.49), channel_id=1, source_target_pairs={{0,16},{8,24},{16,0},{24,8},{1,17},{9,25},{17,1},{25,9},{2,18},{10... | collective-permute-start | bytes 196616 | tf_op jit(solution)/shard_map/ppermute | solution.py:287
  48.1 0.3 collective-permute-start.13
  48.4 2.5 %collective-permute-done.11.refs_0_ = bf16[2,128,128]{2,1,0:T(8,128)(2,1)S(1)} collective-permute-done((bf16[2,128,128]{2,1,0:T(8,128)(2,1)S(1)}, bf16[2,128,128]{2,1,0:T(8,128)(2,1)S(1)}, u32[]{:S(2)}, u32[]{:S(2)}) %collective-permute-start.11) | collective-permute-done | bytes 65568 | tf_op jit(solution)/shard_map/ppermute | solution.py:287
  50.9 1.5 %collective-permute-done.12.refs_1_ = bf16[2,128,128]{2,1,0:T(8,128)(2,1)S(1)} collective-permute-done((bf16[2,128,128]{2,1,0:T(8,128)(2,1)S(1)}, bf16[2,128,128]{2,1,0:T(8,128)(2,1)S(1)}, u32[]{:S(2)}, u32[]{:S(2)}) %collective-permute-start.12) | collective-permute-done | bytes 65568 | tf_op jit(solution)/shard_map/ppermute | solution.py:287
  52.3 0.0 collective-permute-done.13.refs_2_
  52.3 0.9 %sum_unrotate.1 = (f32[256,128]{1,0:T(8,128)}, f32[1,256]{1,0:T(1,128)}) custom-call(s32[256,128]{1,0:T(8,128)S(1)} %get-tuple-element.28.sign_ref, bf16[2,128,128]{2,1,0:T(8,128)(2,1)S(1)} %collective-permute-done.11.refs_0_, bf16[2,128,128]{2,1,0:T(8,128)(2,1)S(1)} %collective-permute-done.12.refs_1_, ...), custom_call_target="tpu_custom_call" | custom-call | tf_op jit(solution)/shard_map/sum_unrotate/pallas_call | solution.py:258
Async XLA Ops:
  7.3 8.0 %collective-permute-start = (bf16[4,128,128]{2,1,0:T(8,128)(2,1)S(1)}, bf16[4,128,128]{2,1,0:T(8,128)(2,1)S(1)}, u32[]{:S(2)}, u32[]{:S(2)}) collective-permute-start(bf16[4,128,128]{2,1,0:T(8,128)(2,1)S(1)} %get-tuple-element.29), channel_id=1, source_target_pairs={{0,2},{1,3},{2,0},{3,1},{4,6},{5,7},{6,4},{7,5},{8,10},{9,11},{10,... | collective-permute-start | bytes 393224 | tf_op jit(solution)/shard_map/ppermute | solution.py:281
  10.4 8.6 %collective-permute-start.1 = (bf16[4,128,128]{2,1,0:T(8,128)(2,1)S(1)}, bf16[4,128,128]{2,1,0:T(8,128)(2,1)S(1)}, u32[]{:S(2)}, u32[]{:S(2)}) collective-permute-start(bf16[4,128,128]{2,1,0:T(8,128)(2,1)S(1)} %get-tuple-element.30), channel_id=1, source_target_pairs={{0,3},{1,2},{2,1},{3,0},{4,7},{5,6},{6,5},{7,4},{8,11},{9,10},{10,... | collective-permute-start | bytes 393224 | tf_op jit(solution)/shard_map/ppermute | solution.py:281
  11.8 7.5 %collective-permute-start.2 = (bf16[4,128,128]{2,1,0:T(8,128)(2,1)S(1)}, bf16[4,128,128]{2,1,0:T(8,128)(2,1)S(1)}, u32[]{:S(2)}, u32[]{:S(2)}) collective-permute-start(bf16[4,128,128]{2,1,0:T(8,128)(2,1)S(1)} %get-tuple-element.31), channel_id=1, source_target_pairs={{0,1},{1,0},{2,3},{3,2},{4,5},{5,4},{6,7},{7,6},{8,9},{9,8},{10,11... | collective-permute-start | bytes 393224 | tf_op jit(solution)/shard_map/ppermute | solution.py:281
  12.0 12.2 %collective-permute-start.4 = (bf16[4,128,128]{2,1,0:T(8,128)(2,1)S(1)}, bf16[4,128,128]{2,1,0:T(8,128)(2,1)S(1)}, u32[]{:S(2)}, u32[]{:S(2)}) collective-permute-start(bf16[4,128,128]{2,1,0:T(8,128)(2,1)S(1)} %get-tuple-element.38), channel_id=1, source_target_pairs={{0,2},{1,3},{2,0},{3,1},{4,6},{5,7},{6,4},{7,5},{8,10},{9,11},{10,... | collective-permute-start | bytes 393224 | tf_op jit(solution)/shard_map/ppermute | solution.py:281
  13.9 13.3 %collective-permute-start.5 = (bf16[4,128,128]{2,1,0:T(8,128)(2,1)S(1)}, bf16[4,128,128]{2,1,0:T(8,128)(2,1)S(1)}, u32[]{:S(2)}, u32[]{:S(2)}) collective-permute-start(bf16[4,128,128]{2,1,0:T(8,128)(2,1)S(1)} %get-tuple-element.39), channel_id=1, source_target_pairs={{0,3},{1,2},{2,1},{3,0},{4,7},{5,6},{6,5},{7,4},{8,11},{9,10},{10,... | collective-permute-start | bytes 393224 | tf_op jit(solution)/shard_map/ppermute | solution.py:281
  19.4 7.9 %collective-permute-start.6 = (bf16[4,128,128]{2,1,0:T(8,128)(2,1)S(1)}, bf16[4,128,128]{2,1,0:T(8,128)(2,1)S(1)}, u32[]{:S(2)}, u32[]{:S(2)}) collective-permute-start(bf16[4,128,128]{2,1,0:T(8,128)(2,1)S(1)} %get-tuple-element.40), channel_id=1, source_target_pairs={{0,1},{1,0},{2,3},{3,2},{4,5},{5,4},{6,7},{7,6},{8,9},{9,8},{10,11... | collective-permute-start | bytes 393224 | tf_op jit(solution)/shard_map/ppermute | solution.py:281
  19.9 15.2 %collective-permute-start.3 = (f32[4,128,128]{2,1,0:T(8,128)S(1)}, f32[4,128,128]{2,1,0:T(8,128)S(1)}, u32[]{:S(2)}, u32[]{:S(2)}) collective-permute-start(f32[4,128,128]{2,1,0:T(8,128)S(1)} %get-tuple-element.37), channel_id=1, source_target_pairs={{0,4},{1,5},{2,6},{3,7},{4,0},{5,1},{6,2},{7,3},{8,12},{9,13},{10,... | collective-permute-start | bytes 786440 | tf_op jit(solution)/shard_map/ppermute | solution.py:304
  22.6 15.1 %collective-permute-start.8 = (bf16[4,256,128]{2,1,0:T(8,128)(2,1)S(1)}, bf16[4,256,128]{2,1,0:T(8,128)(2,1)S(1)}, u32[]{:S(2)}, u32[]{:S(2)}) collective-permute-start(bf16[4,256,128]{2,1,0:T(8,128)(2,1)S(1)} %get-tuple-element.44), channel_id=1, source_target_pairs={{0,2},{1,3},{2,0},{3,1},{4,6},{5,7},{6,4},{7,5},{8,10},{9,11},{10,... | collective-permute-start | bytes 786440 | tf_op jit(solution)/shard_map/ppermute | solution.py:281
  27.3 16.8 %collective-permute-start.7 = (f32[4,128,128]{2,1,0:T(8,128)S(1)}, f32[4,128,128]{2,1,0:T(8,128)S(1)}, u32[]{:S(2)}, u32[]{:S(2)}) collective-permute-start(f32[4,128,128]{2,1,0:T(8,128)S(1)} %get-tuple-element.43), channel_id=1, source_target_pairs={{0,4},{1,5},{2,6},{3,7},{4,0},{5,1},{6,2},{7,3},{8,12},{9,13},{10,... | collective-permute-start | bytes 786440 | tf_op jit(solution)/shard_map/ppermute | solution.py:308
  28.3 17.6 %collective-permute-start.9 = (bf16[4,256,128]{2,1,0:T(8,128)(2,1)S(1)}, bf16[4,256,128]{2,1,0:T(8,128)(2,1)S(1)}, u32[]{:S(2)}, u32[]{:S(2)}) collective-permute-start(bf16[4,256,128]{2,1,0:T(8,128)(2,1)S(1)} %get-tuple-element.45), channel_id=1, source_target_pairs={{0,3},{1,2},{2,1},{3,0},{4,7},{5,6},{6,5},{7,4},{8,11},{9,10},{10,... | collective-permute-start | bytes 786440 | tf_op jit(solution)/shard_map/ppermute | solution.py:281
  29.9 16.1 %collective-permute-start.10 = (bf16[4,256,128]{2,1,0:T(8,128)(2,1)S(1)}, bf16[4,256,128]{2,1,0:T(8,128)(2,1)S(1)}, u32[]{:S(2)}, u32[]{:S(2)}) collective-permute-start(bf16[4,256,128]{2,1,0:T(8,128)(2,1)S(1)} %get-tuple-element.46), channel_id=1, source_target_pairs={{0,1},{1,0},{2,3},{3,2},{4,5},{5,4},{6,7},{7,6},{8,9},{9,8},{10,11... | collective-permute-start | bytes 786440 | tf_op jit(solution)/shard_map/ppermute | solution.py:281
  46.5 4.4 %collective-permute-start.11 = (bf16[2,128,128]{2,1,0:T(8,128)(2,1)S(1)}, bf16[2,128,128]{2,1,0:T(8,128)(2,1)S(1)}, u32[]{:S(2)}, u32[]{:S(2)}) collective-permute-start(bf16[2,128,128]{2,1,0:T(8,128)(2,1)S(1)} %get-tuple-element.48), channel_id=1, source_target_pairs={{0,24},{8,16},{16,8},{24,0},{1,25},{9,17},{17,9},{25,1},{2,26},{10... | collective-permute-start | bytes 196616 | tf_op jit(solution)/shard_map/ppermute | solution.py:287
  46.5 5.8 %collective-permute-start.12 = (bf16[2,128,128]{2,1,0:T(8,128)(2,1)S(1)}, bf16[2,128,128]{2,1,0:T(8,128)(2,1)S(1)}, u32[]{:S(2)}, u32[]{:S(2)}) collective-permute-start(bf16[2,128,128]{2,1,0:T(8,128)(2,1)S(1)} %get-tuple-element.49), channel_id=1, source_target_pairs={{0,16},{8,24},{16,0},{24,8},{1,17},{9,25},{17,1},{25,9},{2,18},{10... | collective-permute-start | bytes 196616 | tf_op jit(solution)/shard_map/ppermute | solution.py:287
  48.1 4.2 %collective-permute-start.13 = (bf16[2,128,128]{2,1,0:T(8,128)(2,1)S(1)}, bf16[2,128,128]{2,1,0:T(8,128)(2,1)S(1)}, u32[]{:S(2)}, u32[]{:S(2)}) collective-permute-start(bf16[2,128,128]{2,1,0:T(8,128)(2,1)S(1)} %get-tuple-element.50), channel_id=1, source_target_pairs={{0,8},{8,0},{16,24},{24,16},{1,9},{9,1},{17,25},{25,17},{2,10},{10... | collective-permute-start | bytes 196616 | tf_op jit(solution)/shard_map/ppermute | solution.py:287

commit v14 on v11

--- a/solution.py
+++ b/solution.py
@@ -12,8 +12,8 @@
 LANES = 128
 VMEM_LIMIT = 50 * 1024 * 1024
 SUM_VMEM_LIMIT = 24 * 1024 * 1024
-AHEAD = 2
-PIECES = 4
+AHEAD = 4
+PIECES = 8
 
 
 def sylvester():
@@ -29,16 +29,16 @@
     return (index + step) % count
 
 
-def leading_power(x):
-    q = x * jnp.float32(2.0**23 + 1.0)
+def leading_power(x, factor):
+    q = x * jnp.float32((2.0**23 + 1.0) * factor)
     return q - q * jnp.float32(1.0 - 2.0**-24)
 
 
 def recode(values):
     magnitude = jnp.abs(values)
     largest = jnp.max(magnitude, axis=-2, keepdims=True)
-    least = leading_power(jnp.clip(largest, 2.0**-30, 2.0**30)) * jnp.float32(2.0**-13)
-    shift = leading_power(jnp.maximum(magnitude, least)) * jnp.float32(2.0**20)
+    least = jnp.clip(largest, 2.0**-30, 2.0**30) * jnp.float32(2.0**-13)
+    shift = leading_power(jnp.maximum(magnitude, least), 2.0**20)
     nearest = (magnitude + shift) - shift
     rest = magnitude - nearest
     coded = jnp.where(rest == shift * jnp.float32(2.0**-24), magnitude + rest, nearest)
@@ -312,17 +312,14 @@
     slow = half // 2
     others = [step for step in range(half - 1, 0, -1) if step != slow]
     order = [slow] + others + [0]
-    (part,) = rotate(values, sign_rows, layout, True, [slow])
-    far = {slow: [swap(part, slow)]}
-    outs = rotate(values, sign_rows, layout, True, others + [0], others, after=[part])
-    for step in others:
-        far[step] = [outs.pop(0), outs.pop(0)]
+    last = order[-2]
+    outs = rotate(values, sign_rows, layout, True, order, order[:-1])
+    far = {step: [outs.pop(0), outs.pop(0)] for step in order[:-1]}
     far[0] = outs
-    for step in others:
+    for step in order[:-1]:
         far[step][0] = swap(far[step][0], step)
-    for step in others[:-1]:
+    for step in order[:-2]:
         far[step][1] = swap(far[step][1], step)
-    last = others[-1]
     far[last][1], part = rotate(values, sign_rows, layout, False, [slow], later=[far[last][1]])
     first, (part, far[last][1]) = far_sum([far[step][0] for step in order], layout, 0, [part, far[last][1]])
     across = [lax.ppermute(first, "local", counterparts)]

time: 55.7 us -> 50.3 us (0.903)
  waiting for transfers between devices: 25.2 us -> 18.5 us
  starting transfers between devices: 16.6 us -> 20 us
  Pallas kernels: 13 us -> 11 us
    ppermute x1, waiting for transfers between devices: 5.84 us -> 0.01 us  [shards(): across = [lax.ppermute(first, 'local', counterparts)]]
    ppermute x8 -> x9, waiting for transfers between devices: 9.6 us -> 5.2 us  [swap(): return lax.ppermute(part, 'local', pairs)]
    ppermute x1, waiting for transfers between devices: 5.77 us -> 9.32 us  [shards(): across.append(lax.ppermute(second, 'local', counterparts))]
    ppermute x8 -> x9, starting transfers between devices: 11.7 us -> 15.2 us  [swap(): return lax.ppermute(part, 'local', pairs)]
    pallas_call x4 -> x3, Pallas kernels: 11.4 us -> 9.45 us  [rotate(): pl.pallas_call(functools.partial(rotate_kernel, layout, other, steps, cut...]
  transfers between devices with their start and end apart: 13 -> 14, of which waited for: 7 -> 6; matrix products, arithmetic and copies ran while one was open for 0% -> 0% of each run, Pallas kernels for 17% -> 11%
where the time goes in v14:
time: 50.3 us; the launch traced here: 50.2 us
  starting transfers between devices  20 us (40%)
  waiting for transfers between devices  18.5 us (37%)
  Pallas kernels  11 us (22%)
  between operations  0.7 us (1%)
    ppermute x9, starting transfers between devices, swap(): return lax.ppermute(part, 'local', pairs)  15.2 us
    pallas_call x3, Pallas kernels, rotate(): pl.pallas_call(functools.partial(rotate_kernel, layout, other, steps, cut...  9.45 us
    ppermute x1, waiting for transfers between devices, shards(): across.append(lax.ppermute(second, 'local', counterparts))  9.32 us
    ppermute x9, waiting for transfers between devices, swap(): return lax.ppermute(part, 'local', pairs)  5.2 us
    ppermute x3, waiting for transfers between devices, share(): moved.append(lax.ppermute(parts[step], 'node', pairs))  3.94 us
    ppermute x1, starting transfers between devices, shards(): across = [lax.ppermute(first, 'local', counterparts)]  2.58 us
    ppermute x3, starting transfers between devices, share(): moved.append(lax.ppermute(parts[step], 'node', pairs))  1.92 us
  transfers between devices with their start and end apart: 14, of which 6 were waited for; matrix products, arithmetic and copies ran while one was open for 0% of the time, Pallas kernels for 11%

profile of v14, /device:TPU:0, one launch (start us, length us, event | category | flops | bytes accessed | tf_op | source)
XLA Modules:
  0.0 50.2 jit_solution(16395411390924211536)
XLA Ops:
  0.6 3.9 %rotate_code.3 = (bf16[4,128,128]{2,1,0:T(8,128)(2,1)S(1)}, bf16[4,128,128]{2,1,0:T(8,128)(2,1)S(1)}, bf16[4,128,128]{2,1,0:T(8,128)(2,1)S(1)}, bf16[4,128,128]{...) custom-call(bf16[1,1048576]{1,0:T(2,128)(2,1)} %bitcast.4, ...), custom_call_target="tpu_custom_call" | custom-call | flops 268435456 | bytes 5242880 | tf_op jit(solution)/shard_map/rotate_code/pallas_call | solution.py:164
  4.5 3.1 %collective-permute-start = (bf16[4,128,128]{2,1,0:T(8,128)(2,1)S(1)}, bf16[4,128,128]{2,1,0:T(8,128)(2,1)S(1)}, u32[]{:S(2)}, u32[]{:S(2)}) collective-permute-start(bf16[4,128,128]{2,1,0:T(8,128)(2,1)S(1)} %get-tuple-element.27), channel_id=1, source_target_pairs={{0,2},{1,3},{2,0},{3,1},{4,6},{5,7},{6,4},{7,5},{8,10},{9,11},{10,... | collective-permute-start | bytes 393224 | tf_op jit(solution)/shard_map/ppermute | solution.py:301
  7.6 1.4 %collective-permute-start.1 = (bf16[4,128,128]{2,1,0:T(8,128)(2,1)S(1)}, bf16[4,128,128]{2,1,0:T(8,128)(2,1)S(1)}, u32[]{:S(2)}, u32[]{:S(2)}) collective-permute-start(bf16[4,128,128]{2,1,0:T(8,128)(2,1)S(1)} %get-tuple-element.28), channel_id=1, source_target_pairs={{0,3},{1,2},{2,1},{3,0},{4,7},{5,6},{6,5},{7,4},{8,11},{9,10},{10,... | collective-permute-start | bytes 393224 | tf_op jit(solution)/shard_map/ppermute | solution.py:301
  9.0 0.1 collective-permute-start.2
  9.2 1.9 %collective-permute-start.4 = (bf16[4,128,128]{2,1,0:T(8,128)(2,1)S(1)}, bf16[4,128,128]{2,1,0:T(8,128)(2,1)S(1)}, u32[]{:S(2)}, u32[]{:S(2)}) collective-permute-start(bf16[4,128,128]{2,1,0:T(8,128)(2,1)S(1)} %get-tuple-element.36), channel_id=1, source_target_pairs={{0,2},{1,3},{2,0},{3,1},{4,6},{5,7},{6,4},{7,5},{8,10},{9,11},{10,... | collective-permute-start | bytes 393224 | tf_op jit(solution)/shard_map/ppermute | solution.py:301
  11.1 1.4 %collective-permute-start.5 = (bf16[4,128,128]{2,1,0:T(8,128)(2,1)S(1)}, bf16[4,128,128]{2,1,0:T(8,128)(2,1)S(1)}, u32[]{:S(2)}, u32[]{:S(2)}) collective-permute-start(bf16[4,128,128]{2,1,0:T(8,128)(2,1)S(1)} %get-tuple-element.37), channel_id=1, source_target_pairs={{0,3},{1,2},{2,1},{3,0},{4,7},{5,6},{6,5},{7,4},{8,11},{9,10},{10,... | collective-permute-start | bytes 393224 | tf_op jit(solution)/shard_map/ppermute | solution.py:301
  12.5 2.3 %rotate_code.4 = (bf16[4,128,128]{2,1,0:T(8,128)(2,1)S(1)}, bf16[4,256,128]{2,1,0:T(8,128)(2,1)S(1)}) custom-call(bf16[1,1048576]{1,0:T(2,128)(2,1)} %bitcast.5, s32[8192,128]{1,0:T(8,128)} %bitcast.8, bf16[4,128,128]{2,1,0:T(8,128)(2,1)S(1)} %get-tuple-element.31.refs_0_), custom_call_target="tpu_custom_call", output_to_operand_aliasing={{0}: (2, {})} | custom-call | flops 67108864 | bytes 1310720 | tf_op jit(solution)/shard_map/rotate_code/pallas_call | solution.py:164
  14.8 0.0 collective-permute-done.refs_0_
  14.8 1.4 %collective-permute-done.1.refs_1_ = bf16[4,128,128]{2,1,0:T(8,128)(2,1)S(1)} collective-permute-done((bf16[4,128,128]{2,1,0:T(8,128)(2,1)S(1)}, bf16[4,128,128]{2,1,0:T(8,128)(2,1)S(1)}, u32[]{:S(2)}, u32[]{:S(2)}) %collective-permute-start.1) | collective-permute-done | bytes 131104 | tf_op jit(solution)/shard_map/ppermute | solution.py:301
  16.2 0.3 collective-permute-done.2.refs_2_
  16.5 0.1 far_sum.2
  16.6 0.5 collective-permute-start.6
  17.1 1.7 %collective-permute-start.8 = (bf16[4,256,128]{2,1,0:T(8,128)(2,1)S(1)}, bf16[4,256,128]{2,1,0:T(8,128)(2,1)S(1)}, u32[]{:S(2)}, u32[]{:S(2)}) collective-permute-start(bf16[4,256,128]{2,1,0:T(8,128)(2,1)S(1)} %get-tuple-element.42), channel_id=1, source_target_pairs={{0,2},{1,3},{2,0},{3,1},{4,6},{5,7},{6,4},{7,5},{8,10},{9,11},{10,... | collective-permute-start | bytes 786440 | tf_op jit(solution)/shard_map/ppermute | solution.py:301
  18.7 2.6 %collective-permute-start.3 = (f32[4,128,128]{2,1,0:T(8,128)S(1)}, f32[4,128,128]{2,1,0:T(8,128)S(1)}, u32[]{:S(2)}, u32[]{:S(2)}) collective-permute-start(f32[4,128,128]{2,1,0:T(8,128)S(1)} %get-tuple-element.34.refs_0_), channel_id=1, source_target_pairs={{0,4},{1,5},{2,6},{3,7},{4,0},{5,1},{6,2},{7,3},{8,12},{9,13},{10,... | collective-permute-start | bytes 786440 | tf_op jit(solution)/shard_map/ppermute | solution.py:325
  21.3 3.3 %rotate_code.5 = (bf16[4,256,128]{2,1,0:T(8,128)(2,1)S(1)}, bf16[4,256,128]{2,1,0:T(8,128)(2,1)S(1)}, bf16[4,256,128]{2,1,0:T(8,128)(2,1)S(1)}, s32[256,128]{1,0:T(8,128)S(1)}) custom-call(bf16[1,1048576]{1,0:T(2,128)(2,1)} %bitcast.6, s32[8192,128]{1,0:T(8,128)} %bitcast.9, f32[4,128,128]{2,1,0:T(8,128)S(1)} %get-tuple-element.34.refs_0_), custom_call_target="tpu_custom_call" | custom-call | flops 201326592 | bytes 3932160 | tf_op jit(solution)/shard_map/rotate_code/pallas_call | solution.py:164
  24.6 0.0 collective-permute-done.4.refs_0_
  24.6 3.5 %collective-permute-done.5.refs_1_ = bf16[4,128,128]{2,1,0:T(8,128)(2,1)S(1)} collective-permute-done((bf16[4,128,128]{2,1,0:T(8,128)(2,1)S(1)}, bf16[4,128,128]{2,1,0:T(8,128)(2,1)S(1)}, u32[]{:S(2)}, u32[]{:S(2)}) %collective-permute-start.5) | collective-permute-done | bytes 131104 | tf_op jit(solution)/shard_map/ppermute | solution.py:301
  28.1 0.0 collective-permute-done.6.refs_2_
  28.1 0.1 far_sum.3
  28.2 0.3 collective-permute-start.7
  28.5 3.5 %collective-permute-start.9 = (bf16[4,256,128]{2,1,0:T(8,128)(2,1)S(1)}, bf16[4,256,128]{2,1,0:T(8,128)(2,1)S(1)}, u32[]{:S(2)}, u32[]{:S(2)}) collective-permute-start(bf16[4,256,128]{2,1,0:T(8,128)(2,1)S(1)} %get-tuple-element.43), channel_id=1, source_target_pairs={{0,3},{1,2},{2,1},{3,0},{4,7},{5,6},{6,5},{7,4},{8,11},{9,10},{10,... | collective-permute-start | bytes 786440 | tf_op jit(solution)/shard_map/ppermute | solution.py:301
  32.0 1.5 %collective-permute-start.10 = (bf16[4,256,128]{2,1,0:T(8,128)(2,1)S(1)}, bf16[4,256,128]{2,1,0:T(8,128)(2,1)S(1)}, u32[]{:S(2)}, u32[]{:S(2)}) collective-permute-start(bf16[4,256,128]{2,1,0:T(8,128)(2,1)S(1)} %get-tuple-element.44), channel_id=1, source_target_pairs={{0,1},{1,0},{2,3},{3,2},{4,5},{5,4},{6,7},{7,6},{8,9},{9,8},{10,11... | collective-permute-start | bytes 786440 | tf_op jit(solution)/shard_map/ppermute | solution.py:301
  33.5 0.0 collective-permute-done.8.refs_2_
  33.5 0.0 collective-permute-done.3.refs_0_
  33.5 9.3 %collective-permute-done.7.refs_1_ = f32[4,128,128]{2,1,0:T(8,128)S(1)} collective-permute-done((f32[4,128,128]{2,1,0:T(8,128)S(1)}, f32[4,128,128]{2,1,0:T(8,128)S(1)}, u32[]{:S(2)}, u32[]{:S(2)}) %collective-permute-start.7) | collective-permute-done | bytes 262176 | tf_op jit(solution)/shard_map/ppermute | solution.py:330
  42.8 0.0 collective-permute-done.9.refs_3_
  42.9 0.0 collective-permute-done.10.refs_4_
  42.9 0.5 group_sum_code.1
  43.4 0.1 collective-permute-start.11
  43.4 1.6 %collective-permute-start.12 = (bf16[2,128,128]{2,1,0:T(8,128)(2,1)S(1)}, bf16[2,128,128]{2,1,0:T(8,128)(2,1)S(1)}, u32[]{:S(2)}, u32[]{:S(2)}) collective-permute-start(bf16[2,128,128]{2,1,0:T(8,128)(2,1)S(1)} %get-tuple-element.47), channel_id=1, source_target_pairs={{0,16},{8,24},{16,0},{24,8},{1,17},{9,25},{17,1},{25,9},{2,18},{10... | collective-permute-start | bytes 196616 | tf_op jit(solution)/shard_map/ppermute | solution.py:307
  45.0 0.3 collective-permute-start.13
  45.3 2.5 %collective-permute-done.11.refs_0_ = bf16[2,128,128]{2,1,0:T(8,128)(2,1)S(1)} collective-permute-done((bf16[2,128,128]{2,1,0:T(8,128)(2,1)S(1)}, bf16[2,128,128]{2,1,0:T(8,128)(2,1)S(1)}, u32[]{:S(2)}, u32[]{:S(2)}) %collective-permute-start.11) | collective-permute-done | bytes 65568 | tf_op jit(solution)/shard_map/ppermute | solution.py:307
  47.8 1.5 %collective-permute-done.12.refs_1_ = bf16[2,128,128]{2,1,0:T(8,128)(2,1)S(1)} collective-permute-done((bf16[2,128,128]{2,1,0:T(8,128)(2,1)S(1)}, bf16[2,128,128]{2,1,0:T(8,128)(2,1)S(1)}, u32[]{:S(2)}, u32[]{:S(2)}) %collective-permute-start.12) | collective-permute-done | bytes 65568 | tf_op jit(solution)/shard_map/ppermute | solution.py:307
  49.2 0.0 collective-permute-done.13.refs_2_
  49.2 0.9 %sum_unrotate.1 = (f32[256,128]{1,0:T(8,128)}, f32[1,256]{1,0:T(1,128)}) custom-call(s32[256,128]{1,0:T(8,128)S(1)} %get-tuple-element.35.sign_ref, bf16[2,128,128]{2,1,0:T(8,128)(2,1)S(1)} %collective-permute-done.11.refs_0_, bf16[2,128,128]{2,1,0:T(8,128)(2,1)S(1)} %collective-permute-done.12.refs_1_, ...), custom_call_target="tpu_custom_call" | custom-call | tf_op jit(solution)/shard_map/sum_unrotate/pallas_call | solution.py:278
Async XLA Ops:
  4.5 10.3 %collective-permute-start = (bf16[4,128,128]{2,1,0:T(8,128)(2,1)S(1)}, bf16[4,128,128]{2,1,0:T(8,128)(2,1)S(1)}, u32[]{:S(2)}, u32[]{:S(2)}) collective-permute-start(bf16[4,128,128]{2,1,0:T(8,128)(2,1)S(1)} %get-tuple-element.27), channel_id=1, source_target_pairs={{0,2},{1,3},{2,0},{3,1},{4,6},{5,7},{6,4},{7,5},{8,10},{9,11},{10,... | collective-permute-start | bytes 393224 | tf_op jit(solution)/shard_map/ppermute | solution.py:301
  7.6 8.6 %collective-permute-start.1 = (bf16[4,128,128]{2,1,0:T(8,128)(2,1)S(1)}, bf16[4,128,128]{2,1,0:T(8,128)(2,1)S(1)}, u32[]{:S(2)}, u32[]{:S(2)}) collective-permute-start(bf16[4,128,128]{2,1,0:T(8,128)(2,1)S(1)} %get-tuple-element.28), channel_id=1, source_target_pairs={{0,3},{1,2},{2,1},{3,0},{4,7},{5,6},{6,5},{7,4},{8,11},{9,10},{10,... | collective-permute-start | bytes 393224 | tf_op jit(solution)/shard_map/ppermute | solution.py:301
  9.0 7.5 %collective-permute-start.2 = (bf16[4,128,128]{2,1,0:T(8,128)(2,1)S(1)}, bf16[4,128,128]{2,1,0:T(8,128)(2,1)S(1)}, u32[]{:S(2)}, u32[]{:S(2)}) collective-permute-start(bf16[4,128,128]{2,1,0:T(8,128)(2,1)S(1)} %get-tuple-element.29), channel_id=1, source_target_pairs={{0,1},{1,0},{2,3},{3,2},{4,5},{5,4},{6,7},{7,6},{8,9},{9,8},{10,11... | collective-permute-start | bytes 393224 | tf_op jit(solution)/shard_map/ppermute | solution.py:301
  9.2 15.5 %collective-permute-start.4 = (bf16[4,128,128]{2,1,0:T(8,128)(2,1)S(1)}, bf16[4,128,128]{2,1,0:T(8,128)(2,1)S(1)}, u32[]{:S(2)}, u32[]{:S(2)}) collective-permute-start(bf16[4,128,128]{2,1,0:T(8,128)(2,1)S(1)} %get-tuple-element.36), channel_id=1, source_target_pairs={{0,2},{1,3},{2,0},{3,1},{4,6},{5,7},{6,4},{7,5},{8,10},{9,11},{10,... | collective-permute-start | bytes 393224 | tf_op jit(solution)/shard_map/ppermute | solution.py:301
  11.1 17.0 %collective-permute-start.5 = (bf16[4,128,128]{2,1,0:T(8,128)(2,1)S(1)}, bf16[4,128,128]{2,1,0:T(8,128)(2,1)S(1)}, u32[]{:S(2)}, u32[]{:S(2)}) collective-permute-start(bf16[4,128,128]{2,1,0:T(8,128)(2,1)S(1)} %get-tuple-element.37), channel_id=1, source_target_pairs={{0,3},{1,2},{2,1},{3,0},{4,7},{5,6},{6,5},{7,4},{8,11},{9,10},{10,... | collective-permute-start | bytes 393224 | tf_op jit(solution)/shard_map/ppermute | solution.py:301
  16.6 11.5 %collective-permute-start.6 = (bf16[4,128,128]{2,1,0:T(8,128)(2,1)S(1)}, bf16[4,128,128]{2,1,0:T(8,128)(2,1)S(1)}, u32[]{:S(2)}, u32[]{:S(2)}) collective-permute-start(bf16[4,128,128]{2,1,0:T(8,128)(2,1)S(1)} %get-tuple-element.38), channel_id=1, source_target_pairs={{0,1},{1,0},{2,3},{3,2},{4,5},{5,4},{6,7},{7,6},{8,9},{9,8},{10,11... | collective-permute-start | bytes 393224 | tf_op jit(solution)/shard_map/ppermute | solution.py:301
  17.1 16.5 %collective-permute-start.8 = (bf16[4,256,128]{2,1,0:T(8,128)(2,1)S(1)}, bf16[4,256,128]{2,1,0:T(8,128)(2,1)S(1)}, u32[]{:S(2)}, u32[]{:S(2)}) collective-permute-start(bf16[4,256,128]{2,1,0:T(8,128)(2,1)S(1)} %get-tuple-element.42), channel_id=1, source_target_pairs={{0,2},{1,3},{2,0},{3,1},{4,6},{5,7},{6,4},{7,5},{8,10},{9,11},{10,... | collective-permute-start | bytes 786440 | tf_op jit(solution)/shard_map/ppermute | solution.py:301
  18.7 14.8 %collective-permute-start.3 = (f32[4,128,128]{2,1,0:T(8,128)S(1)}, f32[4,128,128]{2,1,0:T(8,128)S(1)}, u32[]{:S(2)}, u32[]{:S(2)}) collective-permute-start(f32[4,128,128]{2,1,0:T(8,128)S(1)} %get-tuple-element.34.refs_0_), channel_id=1, source_target_pairs={{0,4},{1,5},{2,6},{3,7},{4,0},{5,1},{6,2},{7,3},{8,12},{9,13},{10,... | collective-permute-start | bytes 786440 | tf_op jit(solution)/shard_map/ppermute | solution.py:325
  28.2 14.7 %collective-permute-start.7 = (f32[4,128,128]{2,1,0:T(8,128)S(1)}, f32[4,128,128]{2,1,0:T(8,128)S(1)}, u32[]{:S(2)}, u32[]{:S(2)}) collective-permute-start(f32[4,128,128]{2,1,0:T(8,128)S(1)} %get-tuple-element.41), channel_id=1, source_target_pairs={{0,4},{1,5},{2,6},{3,7},{4,0},{5,1},{6,2},{7,3},{8,12},{9,13},{10,... | collective-permute-start | bytes 786440 | tf_op jit(solution)/shard_map/ppermute | solution.py:330
  28.5 14.4 %collective-permute-start.9 = (bf16[4,256,128]{2,1,0:T(8,128)(2,1)S(1)}, bf16[4,256,128]{2,1,0:T(8,128)(2,1)S(1)}, u32[]{:S(2)}, u32[]{:S(2)}) collective-permute-start(bf16[4,256,128]{2,1,0:T(8,128)(2,1)S(1)} %get-tuple-element.43), channel_id=1, source_target_pairs={{0,3},{1,2},{2,1},{3,0},{4,7},{5,6},{6,5},{7,4},{8,11},{9,10},{10,... | collective-permute-start | bytes 786440 | tf_op jit(solution)/shard_map/ppermute | solution.py:301
  32.0 10.9 %collective-permute-start.10 = (bf16[4,256,128]{2,1,0:T(8,128)(2,1)S(1)}, bf16[4,256,128]{2,1,0:T(8,128)(2,1)S(1)}, u32[]{:S(2)}, u32[]{:S(2)}) collective-permute-start(bf16[4,256,128]{2,1,0:T(8,128)(2,1)S(1)} %get-tuple-element.44), channel_id=1, source_target_pairs={{0,1},{1,0},{2,3},{3,2},{4,5},{5,4},{6,7},{7,6},{8,9},{9,8},{10,11... | collective-permute-start | bytes 786440 | tf_op jit(solution)/shard_map/ppermute | solution.py:301
  43.4 4.4 %collective-permute-start.11 = (bf16[2,128,128]{2,1,0:T(8,128)(2,1)S(1)}, bf16[2,128,128]{2,1,0:T(8,128)(2,1)S(1)}, u32[]{:S(2)}, u32[]{:S(2)}) collective-permute-start(bf16[2,128,128]{2,1,0:T(8,128)(2,1)S(1)} %get-tuple-element.46), channel_id=1, source_target_pairs={{0,24},{8,16},{16,8},{24,0},{1,25},{9,17},{17,9},{25,1},{2,26},{10... | collective-permute-start | bytes 196616 | tf_op jit(solution)/shard_map/ppermute | solution.py:307
  43.4 5.8 %collective-permute-start.12 = (bf16[2,128,128]{2,1,0:T(8,128)(2,1)S(1)}, bf16[2,128,128]{2,1,0:T(8,128)(2,1)S(1)}, u32[]{:S(2)}, u32[]{:S(2)}) collective-permute-start(bf16[2,128,128]{2,1,0:T(8,128)(2,1)S(1)} %get-tuple-element.47), channel_id=1, source_target_pairs={{0,16},{8,24},{16,0},{24,8},{1,17},{9,25},{17,1},{25,9},{2,18},{10... | collective-permute-start | bytes 196616 | tf_op jit(solution)/shard_map/ppermute | solution.py:307
  45.0 4.2 %collective-permute-start.13 = (bf16[2,128,128]{2,1,0:T(8,128)(2,1)S(1)}, bf16[2,128,128]{2,1,0:T(8,128)(2,1)S(1)}, u32[]{:S(2)}, u32[]{:S(2)}) collective-permute-start(bf16[2,128,128]{2,1,0:T(8,128)(2,1)S(1)} %get-tuple-element.48), channel_id=1, source_target_pairs={{0,8},{8,0},{16,24},{24,16},{1,9},{9,1},{17,25},{25,17},{2,10},{10... | collective-permute-start | bytes 196616 | tf_op jit(solution)/shard_map/ppermute | solution.py:307

commit v15 on v14

--- a/solution.py
+++ b/solution.py
@@ -66,7 +66,7 @@
         return 1 if len(steps) == 1 else self.half
 
     def batch(self, steps):
-        batch = max(1, PIECES // len(steps))
+        batch = min(self.units, max(1, PIECES // len(steps)))
         return batch if self.units % batch == 0 else 1
 
 
@@ -311,7 +311,7 @@
     counterparts = [(member, (member + half) % members) for member in range(members)]
     slow = half // 2
     others = [step for step in range(half - 1, 0, -1) if step != slow]
-    order = [slow] + others + [0]
+    order = others[:1] + [slow] + others[1:] + [0]
     last = order[-2]
     outs = rotate(values, sign_rows, layout, True, order, order[:-1])
     far = {step: [outs.pop(0), outs.pop(0)] for step in order[:-1]}
@@ -325,7 +325,7 @@
     across = [lax.ppermute(first, "local", counterparts)]
     near = {slow: swap(part, slow)}
     far[last][1] = swap(far[last][1], last)
-    *outs, own_signs = rotate(values, sign_rows, layout, False, others + [0], signed_out=True, after=[first])
+    *outs, own_signs = rotate(values, sign_rows, layout, False, others + [0], signed_out=True, after=[part])
     second, outs[:-1] = far_sum([far[step][-1] for step in order], layout, 1, outs[:-1])
     across.append(lax.ppermute(second, "local", counterparts))
     for step, part in zip(others + [0], outs):

time: 50.3 us -> 50.5 us (level)
  waiting for transfers between devices: 18.5 us -> 21 us
  starting transfers between devices: 20 us -> 17.9 us
    ppermute x1, waiting for transfers between devices: 0.01 us -> 5.92 us  [shards(): across = [lax.ppermute(first, 'local', counterparts)]]
    ppermute x9, starting transfers between devices: 15.2 us -> 13 us  [swap(): return lax.ppermute(part, 'local', pairs)]
    ppermute x9, waiting for transfers between devices: 5.2 us -> 3.31 us  [swap(): return lax.ppermute(part, 'local', pairs)]
    ppermute x1, waiting for transfers between devices: 9.32 us -> 8.25 us  [shards(): across.append(lax.ppermute(second, 'local', counterparts))]
where the time goes in v15:
time: 50.5 us; the launch traced here: 50.3 us
  waiting for transfers between devices  21 us (42%)
  starting transfers between devices  17.9 us (35%)
  Pallas kernels  10.8 us (21%)
  between operations  0.72 us (1%)
    ppermute x9, starting transfers between devices, swap(): return lax.ppermute(part, 'local', pairs)  13 us
    pallas_call x3, Pallas kernels, rotate(): pl.pallas_call(functools.partial(rotate_kernel, layout, other, steps, cut...  9.2 us
    ppermute x1, waiting for transfers between devices, shards(): across.append(lax.ppermute(second, 'local', counterparts))  8.25 us
    ppermute x1, waiting for transfers between devices, shards(): across = [lax.ppermute(first, 'local', counterparts)]  5.92 us
    ppermute x3, waiting for transfers between devices, share(): moved.append(lax.ppermute(parts[step], 'node', pairs))  3.47 us
    ppermute x9, waiting for transfers between devices, swap(): return lax.ppermute(part, 'local', pairs)  3.31 us
    ppermute x1, starting transfers between devices, shards(): across = [lax.ppermute(first, 'local', counterparts)]  2.59 us
    ppermute x3, starting transfers between devices, share(): moved.append(lax.ppermute(parts[step], 'node', pairs))  1.92 us
  transfers between devices with their start and end apart: 14, of which 6 were waited for; matrix products, arithmetic and copies ran while one was open for 0% of the time, Pallas kernels for 11%

profile of v15, /device:TPU:0, one launch (start us, length us, event | category | flops | bytes accessed | tf_op | source)
XLA Modules:
  0.0 50.3 jit_solution(10684903954346084131)
XLA Ops:
  0.6 3.9 %rotate_code.3 = (bf16[4,128,128]{2,1,0:T(8,128)(2,1)S(1)}, bf16[4,128,128]{2,1,0:T(8,128)(2,1)S(1)}, bf16[4,128,128]{2,1,0:T(8,128)(2,1)S(1)}, bf16[4,128,128]{...) custom-call(bf16[1,1048576]{1,0:T(2,128)(2,1)} %bitcast.4, ...), custom_call_target="tpu_custom_call" | custom-call | flops 268435456 | bytes 5242880 | tf_op jit(solution)/shard_map/rotate_code/pallas_call | solution.py:164
  4.5 4.0 %collective-permute-start = (bf16[4,128,128]{2,1,0:T(8,128)(2,1)S(1)}, bf16[4,128,128]{2,1,0:T(8,128)(2,1)S(1)}, u32[]{:S(2)}, u32[]{:S(2)}) collective-permute-start(bf16[4,128,128]{2,1,0:T(8,128)(2,1)S(1)} %get-tuple-element.27), channel_id=1, source_target_pairs={{0,3},{1,2},{2,1},{3,0},{4,7},{5,6},{6,5},{7,4},{8,11},{9,10},{10,... | collective-permute-start | bytes 393224 | tf_op jit(solution)/shard_map/ppermute | solution.py:301
  8.6 0.4 collective-permute-start.1
  9.0 0.2 collective-permute-start.2
  9.2 2.8 %collective-permute-start.4 = (bf16[4,128,128]{2,1,0:T(8,128)(2,1)S(1)}, bf16[4,128,128]{2,1,0:T(8,128)(2,1)S(1)}, u32[]{:S(2)}, u32[]{:S(2)}) collective-permute-start(bf16[4,128,128]{2,1,0:T(8,128)(2,1)S(1)} %get-tuple-element.37), channel_id=1, source_target_pairs={{0,3},{1,2},{2,1},{3,0},{4,7},{5,6},{6,5},{7,4},{8,11},{9,10},{10,... | collective-permute-start | bytes 393224 | tf_op jit(solution)/shard_map/ppermute | solution.py:301
  12.1 0.4 collective-permute-start.5
  12.5 2.0 %rotate_code.4 = (bf16[4,128,128]{2,1,0:T(8,128)(2,1)S(1)}, bf16[4,256,128]{2,1,0:T(8,128)(2,1)S(1)}) custom-call(bf16[1,1048576]{1,0:T(2,128)(2,1)} %bitcast.5, s32[8192,128]{1,0:T(8,128)} %bitcast.8, bf16[4,128,128]{2,1,0:T(8,128)(2,1)S(1)} %get-tuple-element.31.refs_0_), custom_call_target="tpu_custom_call", output_to_operand_aliasing={{0}: (2, {})} | custom-call | flops 67108864 | bytes 1310720 | tf_op jit(solution)/shard_map/rotate_code/pallas_call | solution.py:164
  14.5 0.0 collective-permute-done.refs_0_
  14.5 1.7 %collective-permute-done.1.refs_1_ = bf16[4,128,128]{2,1,0:T(8,128)(2,1)S(1)} collective-permute-done((bf16[4,128,128]{2,1,0:T(8,128)(2,1)S(1)}, bf16[4,128,128]{2,1,0:T(8,128)(2,1)S(1)}, u32[]{:S(2)}, u32[]{:S(2)}) %collective-permute-start.1) | collective-permute-done | bytes 131104 | tf_op jit(solution)/shard_map/ppermute | solution.py:301
  16.2 0.0 collective-permute-done.2.refs_2_
  16.2 0.1 far_sum.2
  16.3 1.5 %collective-permute-start.6 = (bf16[4,128,128]{2,1,0:T(8,128)(2,1)S(1)}, bf16[4,128,128]{2,1,0:T(8,128)(2,1)S(1)}, u32[]{:S(2)}, u32[]{:S(2)}) collective-permute-start(bf16[4,128,128]{2,1,0:T(8,128)(2,1)S(1)} %get-tuple-element.39), channel_id=1, source_target_pairs={{0,1},{1,0},{2,3},{3,2},{4,5},{5,4},{6,7},{7,6},{8,9},{9,8},{10,11... | collective-permute-start | bytes 393224 | tf_op jit(solution)/shard_map/ppermute | solution.py:301
  17.8 2.6 %collective-permute-start.3 = (f32[4,128,128]{2,1,0:T(8,128)S(1)}, f32[4,128,128]{2,1,0:T(8,128)S(1)}, u32[]{:S(2)}, u32[]{:S(2)}) collective-permute-start(f32[4,128,128]{2,1,0:T(8,128)S(1)} %get-tuple-element.36), channel_id=1, source_target_pairs={{0,4},{1,5},{2,6},{3,7},{4,0},{5,1},{6,2},{7,3},{8,12},{9,13},{10,... | collective-permute-start | bytes 786440 | tf_op jit(solution)/shard_map/ppermute | solution.py:325
  20.4 1.6 %collective-permute-start.9 = (bf16[4,256,128]{2,1,0:T(8,128)(2,1)S(1)}, bf16[4,256,128]{2,1,0:T(8,128)(2,1)S(1)}, u32[]{:S(2)}, u32[]{:S(2)}) collective-permute-start(bf16[4,256,128]{2,1,0:T(8,128)(2,1)S(1)} %get-tuple-element.34.refs_0_), channel_id=1, source_target_pairs={{0,2},{1,3},{2,0},{3,1},{4,6},{5,7},{6,4},{7,5},{8,10},{9,11},{10,... | collective-permute-start | bytes 786440 | tf_op jit(solution)/shard_map/ppermute | solution.py:301
  22.0 3.3 %rotate_code.5 = (bf16[4,256,128]{2,1,0:T(8,128)(2,1)S(1)}, bf16[4,256,128]{2,1,0:T(8,128)(2,1)S(1)}, bf16[4,256,128]{2,1,0:T(8,128)(2,1)S(1)}, s32[256,128]{1,0:T(8,128)S(1)}) custom-call(bf16[1,1048576]{1,0:T(2,128)(2,1)} %bitcast.6, s32[8192,128]{1,0:T(8,128)} %bitcast.9, bf16[4,256,128]{2,1,0:T(8,128)(2,1)S(1)} %get-tuple-element.34.refs_0_), custom_call_target="tpu_custom_call" | custom-call | flops 201326592 | bytes 3932160 | tf_op jit(solution)/shard_map/rotate_code/pallas_call | solution.py:164
  25.3 0.0 collective-permute-done.4.refs_0_
  25.3 0.0 collective-permute-done.5.refs_1_
  25.3 0.0 collective-permute-done.6.refs_2_
  25.3 0.1 far_sum.3
  25.4 0.4 collective-permute-start.7
  25.8 1.0 %collective-permute-start.8 = (bf16[4,256,128]{2,1,0:T(8,128)(2,1)S(1)}, bf16[4,256,128]{2,1,0:T(8,128)(2,1)S(1)}, u32[]{:S(2)}, u32[]{:S(2)}) collective-permute-start(bf16[4,256,128]{2,1,0:T(8,128)(2,1)S(1)} %get-tuple-element.43), channel_id=1, source_target_pairs={{0,3},{1,2},{2,1},{3,0},{4,7},{5,6},{6,5},{7,4},{8,11},{9,10},{10,... | collective-permute-start | bytes 786440 | tf_op jit(solution)/shard_map/ppermute | solution.py:301
  26.7 0.9 %collective-permute-start.10 = (bf16[4,256,128]{2,1,0:T(8,128)(2,1)S(1)}, bf16[4,256,128]{2,1,0:T(8,128)(2,1)S(1)}, u32[]{:S(2)}, u32[]{:S(2)}) collective-permute-start(bf16[4,256,128]{2,1,0:T(8,128)(2,1)S(1)} %get-tuple-element.44), channel_id=1, source_target_pairs={{0,1},{1,0},{2,3},{3,2},{4,5},{5,4},{6,7},{7,6},{8,9},{9,8},{10,11... | collective-permute-start | bytes 786440 | tf_op jit(solution)/shard_map/ppermute | solution.py:301
  27.7 5.9 %collective-permute-done.3.refs_0_ = f32[4,128,128]{2,1,0:T(8,128)S(1)} collective-permute-done((f32[4,128,128]{2,1,0:T(8,128)S(1)}, f32[4,128,128]{2,1,0:T(8,128)S(1)}, u32[]{:S(2)}, u32[]{:S(2)}) %collective-permute-start.3) | collective-permute-done | bytes 262176 | tf_op jit(solution)/shard_map/ppermute | solution.py:325
  33.6 1.6 %collective-permute-done.9.refs_3_ = bf16[4,256,128]{2,1,0:T(8,128)(2,1)S(1)} collective-permute-done((bf16[4,256,128]{2,1,0:T(8,128)(2,1)S(1)}, bf16[4,256,128]{2,1,0:T(8,128)(2,1)S(1)}, u32[]{:S(2)}, u32[]{:S(2)}) %collective-permute-start.9) | collective-permute-done | bytes 262176 | tf_op jit(solution)/shard_map/ppermute | solution.py:301
  35.2 8.3 %collective-permute-done.7.refs_1_ = f32[4,128,128]{2,1,0:T(8,128)S(1)} collective-permute-done((f32[4,128,128]{2,1,0:T(8,128)S(1)}, f32[4,128,128]{2,1,0:T(8,128)S(1)}, u32[]{:S(2)}, u32[]{:S(2)}) %collective-permute-start.7) | collective-permute-done | bytes 262176 | tf_op jit(solution)/shard_map/ppermute | solution.py:330
  43.5 0.0 collective-permute-done.8.refs_2_
  43.5 0.0 collective-permute-done.10.refs_4_
  43.5 0.5 group_sum_code.1
  44.0 0.1 collective-permute-start.11
  44.1 1.3 %collective-permute-start.12 = (bf16[2,128,128]{2,1,0:T(8,128)(2,1)S(1)}, bf16[2,128,128]{2,1,0:T(8,128)(2,1)S(1)}, u32[]{:S(2)}, u32[]{:S(2)}) collective-permute-start(bf16[2,128,128]{2,1,0:T(8,128)(2,1)S(1)} %get-tuple-element.47), channel_id=1, source_target_pairs={{0,16},{8,24},{16,0},{24,8},{1,17},{9,25},{17,1},{25,9},{2,18},{10... | collective-permute-start | bytes 196616 | tf_op jit(solution)/shard_map/ppermute | solution.py:307
  45.4 0.6 %collective-permute-start.13 = (bf16[2,128,128]{2,1,0:T(8,128)(2,1)S(1)}, bf16[2,128,128]{2,1,0:T(8,128)(2,1)S(1)}, u32[]{:S(2)}, u32[]{:S(2)}) collective-permute-start(bf16[2,128,128]{2,1,0:T(8,128)(2,1)S(1)} %get-tuple-element.48), channel_id=1, source_target_pairs={{0,8},{8,0},{16,24},{24,16},{1,9},{9,1},{17,25},{25,17},{2,10},{10... | collective-permute-start | bytes 196616 | tf_op jit(solution)/shard_map/ppermute | solution.py:307
  45.9 2.5 %collective-permute-done.11.refs_0_ = bf16[2,128,128]{2,1,0:T(8,128)(2,1)S(1)} collective-permute-done((bf16[2,128,128]{2,1,0:T(8,128)(2,1)S(1)}, bf16[2,128,128]{2,1,0:T(8,128)(2,1)S(1)}, u32[]{:S(2)}, u32[]{:S(2)}) %collective-permute-start.11) | collective-permute-done | bytes 65568 | tf_op jit(solution)/shard_map/ppermute | solution.py:307
  48.5 0.9 %collective-permute-done.12.refs_1_ = bf16[2,128,128]{2,1,0:T(8,128)(2,1)S(1)} collective-permute-done((bf16[2,128,128]{2,1,0:T(8,128)(2,1)S(1)}, bf16[2,128,128]{2,1,0:T(8,128)(2,1)S(1)}, u32[]{:S(2)}, u32[]{:S(2)}) %collective-permute-start.12) | collective-permute-done | bytes 65568 | tf_op jit(solution)/shard_map/ppermute | solution.py:307
  49.4 0.0 collective-permute-done.13.refs_2_
  49.4 0.9 %sum_unrotate.1 = (f32[256,128]{1,0:T(8,128)}, f32[1,256]{1,0:T(1,128)}) custom-call(s32[256,128]{1,0:T(8,128)S(1)} %get-tuple-element.35.sign_ref, bf16[2,128,128]{2,1,0:T(8,128)(2,1)S(1)} %collective-permute-done.11.refs_0_, bf16[2,128,128]{2,1,0:T(8,128)(2,1)S(1)} %collective-permute-done.12.refs_1_, ...), custom_call_target="tpu_custom_call" | custom-call | tf_op jit(solution)/shard_map/sum_unrotate/pallas_call | solution.py:278
Async XLA Ops:
  4.5 10.0 %collective-permute-start = (bf16[4,128,128]{2,1,0:T(8,128)(2,1)S(1)}, bf16[4,128,128]{2,1,0:T(8,128)(2,1)S(1)}, u32[]{:S(2)}, u32[]{:S(2)}) collective-permute-start(bf16[4,128,128]{2,1,0:T(8,128)(2,1)S(1)} %get-tuple-element.27), channel_id=1, source_target_pairs={{0,3},{1,2},{2,1},{3,0},{4,7},{5,6},{6,5},{7,4},{8,11},{9,10},{10,... | collective-permute-start | bytes 393224 | tf_op jit(solution)/shard_map/ppermute | solution.py:301
  8.6 7.6 %collective-permute-start.1 = (bf16[4,128,128]{2,1,0:T(8,128)(2,1)S(1)}, bf16[4,128,128]{2,1,0:T(8,128)(2,1)S(1)}, u32[]{:S(2)}, u32[]{:S(2)}) collective-permute-start(bf16[4,128,128]{2,1,0:T(8,128)(2,1)S(1)} %get-tuple-element.28), channel_id=1, source_target_pairs={{0,2},{1,3},{2,0},{3,1},{4,6},{5,7},{6,4},{7,5},{8,10},{9,11},{10,... | collective-permute-start | bytes 393224 | tf_op jit(solution)/shard_map/ppermute | solution.py:301
  9.0 7.2 %collective-permute-start.2 = (bf16[4,128,128]{2,1,0:T(8,128)(2,1)S(1)}, bf16[4,128,128]{2,1,0:T(8,128)(2,1)S(1)}, u32[]{:S(2)}, u32[]{:S(2)}) collective-permute-start(bf16[4,128,128]{2,1,0:T(8,128)(2,1)S(1)} %get-tuple-element.29), channel_id=1, source_target_pairs={{0,1},{1,0},{2,3},{3,2},{4,5},{5,4},{6,7},{7,6},{8,9},{9,8},{10,11... | collective-permute-start | bytes 393224 | tf_op jit(solution)/shard_map/ppermute | solution.py:301
  9.2 16.1 %collective-permute-start.4 = (bf16[4,128,128]{2,1,0:T(8,128)(2,1)S(1)}, bf16[4,128,128]{2,1,0:T(8,128)(2,1)S(1)}, u32[]{:S(2)}, u32[]{:S(2)}) collective-permute-start(bf16[4,128,128]{2,1,0:T(8,128)(2,1)S(1)} %get-tuple-element.37), channel_id=1, source_target_pairs={{0,3},{1,2},{2,1},{3,0},{4,7},{5,6},{6,5},{7,4},{8,11},{9,10},{10,... | collective-permute-start | bytes 393224 | tf_op jit(solution)/shard_map/ppermute | solution.py:301
  12.1 13.2 %collective-permute-start.5 = (bf16[4,128,128]{2,1,0:T(8,128)(2,1)S(1)}, bf16[4,128,128]{2,1,0:T(8,128)(2,1)S(1)}, u32[]{:S(2)}, u32[]{:S(2)}) collective-permute-start(bf16[4,128,128]{2,1,0:T(8,128)(2,1)S(1)} %get-tuple-element.38), channel_id=1, source_target_pairs={{0,2},{1,3},{2,0},{3,1},{4,6},{5,7},{6,4},{7,5},{8,10},{9,11},{10,... | collective-permute-start | bytes 393224 | tf_op jit(solution)/shard_map/ppermute | solution.py:301
  16.3 9.0 %collective-permute-start.6 = (bf16[4,128,128]{2,1,0:T(8,128)(2,1)S(1)}, bf16[4,128,128]{2,1,0:T(8,128)(2,1)S(1)}, u32[]{:S(2)}, u32[]{:S(2)}) collective-permute-start(bf16[4,128,128]{2,1,0:T(8,128)(2,1)S(1)} %get-tuple-element.39), channel_id=1, source_target_pairs={{0,1},{1,0},{2,3},{3,2},{4,5},{5,4},{6,7},{7,6},{8,9},{9,8},{10,11... | collective-permute-start | bytes 393224 | tf_op jit(solution)/shard_map/ppermute | solution.py:301
  17.8 15.8 %collective-permute-start.3 = (f32[4,128,128]{2,1,0:T(8,128)S(1)}, f32[4,128,128]{2,1,0:T(8,128)S(1)}, u32[]{:S(2)}, u32[]{:S(2)}) collective-permute-start(f32[4,128,128]{2,1,0:T(8,128)S(1)} %get-tuple-element.36), channel_id=1, source_target_pairs={{0,4},{1,5},{2,6},{3,7},{4,0},{5,1},{6,2},{7,3},{8,12},{9,13},{10,... | collective-permute-start | bytes 786440 | tf_op jit(solution)/shard_map/ppermute | solution.py:325
  20.4 14.9 %collective-permute-start.9 = (bf16[4,256,128]{2,1,0:T(8,128)(2,1)S(1)}, bf16[4,256,128]{2,1,0:T(8,128)(2,1)S(1)}, u32[]{:S(2)}, u32[]{:S(2)}) collective-permute-start(bf16[4,256,128]{2,1,0:T(8,128)(2,1)S(1)} %get-tuple-element.34.refs_0_), channel_id=1, source_target_pairs={{0,2},{1,3},{2,0},{3,1},{4,6},{5,7},{6,4},{7,5},{8,10},{9,11},{10,... | collective-permute-start | bytes 786440 | tf_op jit(solution)/shard_map/ppermute | solution.py:301
  25.4 18.1 %collective-permute-start.7 = (f32[4,128,128]{2,1,0:T(8,128)S(1)}, f32[4,128,128]{2,1,0:T(8,128)S(1)}, u32[]{:S(2)}, u32[]{:S(2)}) collective-permute-start(f32[4,128,128]{2,1,0:T(8,128)S(1)} %get-tuple-element.42), channel_id=1, source_target_pairs={{0,4},{1,5},{2,6},{3,7},{4,0},{5,1},{6,2},{7,3},{8,12},{9,13},{10,... | collective-permute-start | bytes 786440 | tf_op jit(solution)/shard_map/ppermute | solution.py:330
  25.8 17.7 %collective-permute-start.8 = (bf16[4,256,128]{2,1,0:T(8,128)(2,1)S(1)}, bf16[4,256,128]{2,1,0:T(8,128)(2,1)S(1)}, u32[]{:S(2)}, u32[]{:S(2)}) collective-permute-start(bf16[4,256,128]{2,1,0:T(8,128)(2,1)S(1)} %get-tuple-element.43), channel_id=1, source_target_pairs={{0,3},{1,2},{2,1},{3,0},{4,7},{5,6},{6,5},{7,4},{8,11},{9,10},{10,... | collective-permute-start | bytes 786440 | tf_op jit(solution)/shard_map/ppermute | solution.py:301
  26.7 16.8 %collective-permute-start.10 = (bf16[4,256,128]{2,1,0:T(8,128)(2,1)S(1)}, bf16[4,256,128]{2,1,0:T(8,128)(2,1)S(1)}, u32[]{:S(2)}, u32[]{:S(2)}) collective-permute-start(bf16[4,256,128]{2,1,0:T(8,128)(2,1)S(1)} %get-tuple-element.44), channel_id=1, source_target_pairs={{0,1},{1,0},{2,3},{3,2},{4,5},{5,4},{6,7},{7,6},{8,9},{9,8},{10,11... | collective-permute-start | bytes 786440 | tf_op jit(solution)/shard_map/ppermute | solution.py:301
  44.0 4.5 %collective-permute-start.11 = (bf16[2,128,128]{2,1,0:T(8,128)(2,1)S(1)}, bf16[2,128,128]{2,1,0:T(8,128)(2,1)S(1)}, u32[]{:S(2)}, u32[]{:S(2)}) collective-permute-start(bf16[2,128,128]{2,1,0:T(8,128)(2,1)S(1)} %get-tuple-element.46), channel_id=1, source_target_pairs={{0,24},{8,16},{16,8},{24,0},{1,25},{9,17},{17,9},{25,1},{2,26},{10... | collective-permute-start | bytes 196616 | tf_op jit(solution)/shard_map/ppermute | solution.py:307
  44.1 5.3 %collective-permute-start.12 = (bf16[2,128,128]{2,1,0:T(8,128)(2,1)S(1)}, bf16[2,128,128]{2,1,0:T(8,128)(2,1)S(1)}, u32[]{:S(2)}, u32[]{:S(2)}) collective-permute-start(bf16[2,128,128]{2,1,0:T(8,128)(2,1)S(1)} %get-tuple-element.47), channel_id=1, source_target_pairs={{0,16},{8,24},{16,0},{24,8},{1,17},{9,25},{17,1},{25,9},{2,18},{10... | collective-permute-start | bytes 196616 | tf_op jit(solution)/shard_map/ppermute | solution.py:307
  45.4 4.0 %collective-permute-start.13 = (bf16[2,128,128]{2,1,0:T(8,128)(2,1)S(1)}, bf16[2,128,128]{2,1,0:T(8,128)(2,1)S(1)}, u32[]{:S(2)}, u32[]{:S(2)}) collective-permute-start(bf16[2,128,128]{2,1,0:T(8,128)(2,1)S(1)} %get-tuple-element.48), channel_id=1, source_target_pairs={{0,8},{8,0},{16,24},{24,16},{1,9},{9,1},{17,25},{25,17},{2,10},{10... | collective-permute-start | bytes 196616 | tf_op jit(solution)/shard_map/ppermute | solution.py:307

commit v16 on v15

--- a/solution.py
+++ b/solution.py
@@ -311,25 +311,29 @@
     counterparts = [(member, (member + half) % members) for member in range(members)]
     slow = half // 2
     others = [step for step in range(half - 1, 0, -1) if step != slow]
-    order = others[:1] + [slow] + others[1:] + [0]
-    last = order[-2]
-    outs = rotate(values, sign_rows, layout, True, order, order[:-1])
-    far = {step: [outs.pop(0), outs.pop(0)] for step in order[:-1]}
+    order = others + [slow, 0]
+    (part,) = rotate(values, sign_rows, layout, True, [slow])
+    far = {slow: [swap(part, slow)]}
+    outs = rotate(values, sign_rows, layout, True, others + [0], others, after=[part])
+    for step in others:
+        far[step] = [swap(outs.pop(0), step), outs.pop(0)]
     far[0] = outs
-    for step in order[:-1]:
-        far[step][0] = swap(far[step][0], step)
-    for step in order[:-2]:
-        far[step][1] = swap(far[step][1], step)
-    far[last][1], part = rotate(values, sign_rows, layout, False, [slow], later=[far[last][1]])
-    first, (part, far[last][1]) = far_sum([far[step][0] for step in order], layout, 0, [part, far[last][1]])
+    *later, part = rotate(values, sign_rows, layout, False, [slow], later=[far[step][1] for step in others])
+    near = {slow: swap(part, slow)}
+    first, later = far_sum([far[step][0] for step in order], layout, 0, later)
     across = [lax.ppermute(first, "local", counterparts)]
-    near = {slow: swap(part, slow)}
-    far[last][1] = swap(far[last][1], last)
-    *outs, own_signs = rotate(values, sign_rows, layout, False, others + [0], signed_out=True, after=[part])
-    second, outs[:-1] = far_sum([far[step][-1] for step in order], layout, 1, outs[:-1])
+    for step, part in zip(others, later):
+        far[step][1] = swap(part, step)
+    *outs, own_signs = rotate(values, sign_rows, layout, False, others + [0], signed_out=True, after=[first])
+    for step in others[:1]:
+        near[step] = swap(outs[0], step)
+    second, (near[slow], *later) = far_sum(
+        [far[step][-1] for step in order], layout, 1, [near[slow]] + outs[1:-1]
+    )
     across.append(lax.ppermute(second, "local", counterparts))
-    for step, part in zip(others + [0], outs):
-        near[step] = swap(part, step) if step else part
+    for step, part in zip(others[1:], later):
+        near[step] = swap(part, step)
+    near[0] = outs[-1]
     reduced, rotated_max = finish(share(group_sum([near[step] for step in order], across, layout)), own_signs)
     return (reduced.reshape(-1), rotated_max.reshape(-1))
 

time: 50.5 us -> 53.2 us (1.053)
  waiting for transfers between devices: 21 us -> 22.9 us
  Pallas kernels: 10.8 us -> 12.2 us
  starting transfers between devices: 17.9 us -> 17.2 us
    ppermute x9 -> x8, waiting for transfers between devices: 3.31 us -> 6.88 us  [swap(): return lax.ppermute(part, 'local', pairs)]
    ppermute x1, waiting for transfers between devices: 8.25 us -> 5.58 us  [shards(): across.append(lax.ppermute(second, 'local', counterparts))]
    ppermute x9 -> x8, starting transfers between devices: 13 us -> 11.4 us  [swap(): return lax.ppermute(part, 'local', pairs)]
    pallas_call x3 -> x4, Pallas kernels: 9.2 us -> 10.6 us  [rotate(): pl.pallas_call(functools.partial(rotate_kernel, layout, other, steps, cut...]
    ppermute x1, starting transfers between devices: 0.4 us -> 1.3 us  [shards(): across.append(lax.ppermute(second, 'local', counterparts))]
    ppermute x1, waiting for transfers between devices: 5.92 us -> 6.54 us  [shards(): across = [lax.ppermute(first, 'local', counterparts)]]
  transfers between devices with their start and end apart: 14 -> 13, of which waited for: 6 -> 8; matrix products, arithmetic and copies ran while one was open for 0% -> 0% of each run, Pallas kernels for 11% -> 17%
where the time goes in v16:
time: 53.2 us; the launch traced here: 53 us
  waiting for transfers between devices  22.9 us (43%)
  starting transfers between devices  17.2 us (32%)
  Pallas kernels  12.2 us (23%)
  between operations  0.69 us (1%)
    ppermute x8, starting transfers between devices, swap(): return lax.ppermute(part, 'local', pairs)  11.4 us
    pallas_call x4, Pallas kernels, rotate(): pl.pallas_call(functools.partial(rotate_kernel, layout, other, steps, cut...  10.6 us
    ppermute x8, waiting for transfers between devices, swap(): return lax.ppermute(part, 'local', pairs)  6.88 us
    ppermute x1, waiting for transfers between devices, shards(): across = [lax.ppermute(first, 'local', counterparts)]  6.54 us
    ppermute x1, waiting for transfers between devices, shards(): across.append(lax.ppermute(second, 'local', counterparts))  5.58 us
    ppermute x3, waiting for transfers between devices, share(): moved.append(lax.ppermute(parts[step], 'node', pairs))  3.94 us
    ppermute x1, starting transfers between devices, shards(): across = [lax.ppermute(first, 'local', counterparts)]  2.59 us
    ppermute x3, starting transfers between devices, share(): moved.append(lax.ppermute(parts[step], 'node', pairs))  1.92 us
  transfers between devices with their start and end apart: 13, of which 8 were waited for; matrix products, arithmetic and copies ran while one was open for 0% of the time, Pallas kernels for 17%

profile of v16, /device:TPU:0, one launch (start us, length us, event | category | flops | bytes accessed | tf_op | source)
XLA Modules:
  0.0 53.0 jit_solution(1629097944642348581)
XLA Ops:
  0.6 2.0 %rotate_code.4.refs_0_ = bf16[4,256,128]{2,1,0:T(8,128)(2,1)S(1)} custom-call(bf16[1,1048576]{1,0:T(2,128)(2,1)} %bitcast.4, s32[8192,128]{1,0:T(8,128)} %bitcast.8), custom_call_target="tpu_custom_call" | custom-call | flops 67108864 | bytes 1310720 | tf_op jit(solution)/shard_map/rotate_code/pallas_call | solution.py:164
  2.6 3.1 %collective-permute-start.2 = (bf16[4,256,128]{2,1,0:T(8,128)(2,1)S(1)}, bf16[4,256,128]{2,1,0:T(8,128)(2,1)S(1)}, u32[]{:S(2)}, u32[]{:S(2)}) collective-permute-start(bf16[4,256,128]{2,1,0:T(8,128)(2,1)S(1)} %rotate_code.4.refs_0_), channel_id=1, source_target_pairs={{0,2},{1,3},{2,0},{3,1},{4,6},{5,7},{6,4},{7,5},{8,10},{9,11},{10,... | collective-permute-start | bytes 786440 | tf_op jit(solution)/shard_map/ppermute | solution.py:301
  5.7 3.3 %rotate_code.5 = (bf16[4,128,128]{2,1,0:T(8,128)(2,1)S(1)}, bf16[4,128,128]{2,1,0:T(8,128)(2,1)S(1)}, bf16[4,128,128]{2,1,0:T(8,128)(2,1)S(1)}, bf16[4,128,128]{2,1,0:T(8,128)(2,1)S(1)}, bf16[4,256,128]{2,1,0:T(8,128)(2,1)S(1)}) custom-call(bf16[1,1048576]{1,0:T(2,128)(2,1)} %bitcast.5, s32[8192,128]{1,0:T(8,128)} %bitcast.9, ...), custom_call_target="tpu_custom_call" | custom-call | flops 201326592 | bytes 3932160 | tf_op jit(solution)/shard_map/rotate_code/pallas_call | solution.py:164
  9.1 1.5 %collective-permute-start = (bf16[4,128,128]{2,1,0:T(8,128)(2,1)S(1)}, bf16[4,128,128]{2,1,0:T(8,128)(2,1)S(1)}, u32[]{:S(2)}, u32[]{:S(2)}) collective-permute-start(bf16[4,128,128]{2,1,0:T(8,128)(2,1)S(1)} %get-tuple-element.26), channel_id=1, source_target_pairs={{0,3},{1,2},{2,1},{3,0},{4,7},{5,6},{6,5},{7,4},{8,11},{9,10},{10,... | collective-permute-start | bytes 393224 | tf_op jit(solution)/shard_map/ppermute | solution.py:301
  10.5 0.2 collective-permute-start.1
  10.7 2.0 %rotate_code.6 = (bf16[4,128,128]{2,1,0:T(8,128)(2,1)S(1)}, bf16[4,128,128]{2,1,0:T(8,128)(2,1)S(1)}, bf16[4,256,128]{2,1,0:T(8,128)(2,1)S(1)}) custom-call(bf16[1,1048576]{1,0:T(2,128)(2,1)} %bitcast.6, s32[8192,128]{1,0:T(8,128)} %bitcast.10, bf16[4,128,128]{2,1,0:T(8,128)(2,1)S(1)} %get-tuple-element.29.refs_0_, ...), custom_call_target="tpu_custom_call", output_to_operand_aliasing={{0}: (2, {}), {1}: (3, {})} | custom-call | flops 67108864 | bytes 1310720 | tf_op jit(solution)/shard_map/rotate_code/pallas_call | solution.py:164
  12.7 2.0 %collective-permute-start.6 = (bf16[4,256,128]{2,1,0:T(8,128)(2,1)S(1)}, bf16[4,256,128]{2,1,0:T(8,128)(2,1)S(1)}, u32[]{:S(2)}, u32[]{:S(2)}) collective-permute-start(bf16[4,256,128]{2,1,0:T(8,128)(2,1)S(1)} %get-tuple-element.37), channel_id=1, source_target_pairs={{0,2},{1,3},{2,0},{3,1},{4,6},{5,7},{6,4},{7,5},{8,10},{9,11},{10,... | collective-permute-start | bytes 786440 | tf_op jit(solution)/shard_map/ppermute | solution.py:301
  14.7 1.6 %collective-permute-done.refs_0_ = bf16[4,128,128]{2,1,0:T(8,128)(2,1)S(1)} collective-permute-done((bf16[4,128,128]{2,1,0:T(8,128)(2,1)S(1)}, bf16[4,128,128]{2,1,0:T(8,128)(2,1)S(1)}, u32[]{:S(2)}, u32[]{:S(2)}) %collective-permute-start) | collective-permute-done | bytes 131104 | tf_op jit(solution)/shard_map/ppermute | solution.py:301
  16.3 1.6 %collective-permute-done.1.refs_1_ = bf16[4,128,128]{2,1,0:T(8,128)(2,1)S(1)} collective-permute-done((bf16[4,128,128]{2,1,0:T(8,128)(2,1)S(1)}, bf16[4,128,128]{2,1,0:T(8,128)(2,1)S(1)}, u32[]{:S(2)}, u32[]{:S(2)}) %collective-permute-start.1) | collective-permute-done | bytes 131104 | tf_op jit(solution)/shard_map/ppermute | solution.py:301
  17.9 0.0 collective-permute-done.2.refs_2_
  17.9 0.1 far_sum.2
  18.0 1.5 %collective-permute-start.4 = (bf16[4,128,128]{2,1,0:T(8,128)(2,1)S(1)}, bf16[4,128,128]{2,1,0:T(8,128)(2,1)S(1)}, u32[]{:S(2)}, u32[]{:S(2)}) collective-permute-start(bf16[4,128,128]{2,1,0:T(8,128)(2,1)S(1)} %get-tuple-element.35), channel_id=1, source_target_pairs={{0,3},{1,2},{2,1},{3,0},{4,7},{5,6},{6,5},{7,4},{8,11},{9,10},{10,... | collective-permute-start | bytes 393224 | tf_op jit(solution)/shard_map/ppermute | solution.py:301
  19.5 1.5 %collective-permute-start.5 = (bf16[4,128,128]{2,1,0:T(8,128)(2,1)S(1)}, bf16[4,128,128]{2,1,0:T(8,128)(2,1)S(1)}, u32[]{:S(2)}, u32[]{:S(2)}) collective-permute-start(bf16[4,128,128]{2,1,0:T(8,128)(2,1)S(1)} %get-tuple-element.36), channel_id=1, source_target_pairs={{0,1},{1,0},{2,3},{3,2},{4,5},{5,4},{6,7},{7,6},{8,9},{9,8},{10,11... | collective-permute-start | bytes 393224 | tf_op jit(solution)/shard_map/ppermute | solution.py:301
  21.0 2.6 %collective-permute-start.3 = (f32[4,128,128]{2,1,0:T(8,128)S(1)}, f32[4,128,128]{2,1,0:T(8,128)S(1)}, u32[]{:S(2)}, u32[]{:S(2)}) collective-permute-start(f32[4,128,128]{2,1,0:T(8,128)S(1)} %get-tuple-element.33.refs_0_), channel_id=1, source_target_pairs={{0,4},{1,5},{2,6},{3,7},{4,0},{5,1},{6,2},{7,3},{8,12},{9,13},{10,... | collective-permute-start | bytes 786440 | tf_op jit(solution)/shard_map/ppermute | solution.py:324
  23.6 3.3 %rotate_code.7 = (bf16[4,256,128]{2,1,0:T(8,128)(2,1)S(1)}, bf16[4,256,128]{2,1,0:T(8,128)(2,1)S(1)}, bf16[4,256,128]{2,1,0:T(8,128)(2,1)S(1)}, s32[256,128]{1,0:T(8,128)S(1)}) custom-call(bf16[1,1048576]{1,0:T(2,128)(2,1)} %bitcast.7, s32[8192,128]{1,0:T(8,128)} %bitcast.11, f32[4,128,128]{2,1,0:T(8,128)S(1)} %get-tuple-element.33.refs_0_), custom_call_target="tpu_custom_call" | custom-call | flops 201326592 | bytes 3932160 | tf_op jit(solution)/shard_map/rotate_code/pallas_call | solution.py:164
  26.9 0.6 %collective-permute-start.8 = (bf16[4,256,128]{2,1,0:T(8,128)(2,1)S(1)}, bf16[4,256,128]{2,1,0:T(8,128)(2,1)S(1)}, u32[]{:S(2)}, u32[]{:S(2)}) collective-permute-start(bf16[4,256,128]{2,1,0:T(8,128)(2,1)S(1)} %get-tuple-element.40), channel_id=1, source_target_pairs={{0,3},{1,2},{2,1},{3,0},{4,7},{5,6},{6,5},{7,4},{8,11},{9,10},{10,... | collective-permute-start | bytes 786440 | tf_op jit(solution)/shard_map/ppermute | solution.py:301
  27.5 0.0 collective-permute-done.6.refs_4_
  27.5 0.3 collective-permute-done.4.refs_0_
  27.9 0.0 collective-permute-done.5.refs_1_
  27.9 0.1 far_sum.3
  28.0 1.3 %collective-permute-start.7 = (f32[4,128,128]{2,1,0:T(8,128)S(1)}, f32[4,128,128]{2,1,0:T(8,128)S(1)}, u32[]{:S(2)}, u32[]{:S(2)}) collective-permute-start(f32[4,128,128]{2,1,0:T(8,128)S(1)} %get-tuple-element.39), channel_id=1, source_target_pairs={{0,4},{1,5},{2,6},{3,7},{4,0},{5,1},{6,2},{7,3},{8,12},{9,13},{10,... | collective-permute-start | bytes 786440 | tf_op jit(solution)/shard_map/ppermute | solution.py:333
  29.3 1.0 %collective-permute-start.9 = (bf16[4,256,128]{2,1,0:T(8,128)(2,1)S(1)}, bf16[4,256,128]{2,1,0:T(8,128)(2,1)S(1)}, u32[]{:S(2)}, u32[]{:S(2)}) collective-permute-start(bf16[4,256,128]{2,1,0:T(8,128)(2,1)S(1)} %get-tuple-element.41), channel_id=1, source_target_pairs={{0,1},{1,0},{2,3},{3,2},{4,5},{5,4},{6,7},{7,6},{8,9},{9,8},{10,11... | collective-permute-start | bytes 786440 | tf_op jit(solution)/shard_map/ppermute | solution.py:301
  30.3 6.5 %collective-permute-done.3.refs_0_ = f32[4,128,128]{2,1,0:T(8,128)S(1)} collective-permute-done((f32[4,128,128]{2,1,0:T(8,128)S(1)}, f32[4,128,128]{2,1,0:T(8,128)S(1)}, u32[]{:S(2)}, u32[]{:S(2)}) %collective-permute-start.3) | collective-permute-done | bytes 262176 | tf_op jit(solution)/shard_map/ppermute | solution.py:324
  36.8 3.3 %collective-permute-done.8.refs_2_ = bf16[4,256,128]{2,1,0:T(8,128)(2,1)S(1)} collective-permute-done((bf16[4,256,128]{2,1,0:T(8,128)(2,1)S(1)}, bf16[4,256,128]{2,1,0:T(8,128)(2,1)S(1)}, u32[]{:S(2)}, u32[]{:S(2)}) %collective-permute-start.8) | collective-permute-done | bytes 262176 | tf_op jit(solution)/shard_map/ppermute | solution.py:301
  40.1 5.6 %collective-permute-done.7.refs_1_ = f32[4,128,128]{2,1,0:T(8,128)S(1)} collective-permute-done((f32[4,128,128]{2,1,0:T(8,128)S(1)}, f32[4,128,128]{2,1,0:T(8,128)S(1)}, u32[]{:S(2)}, u32[]{:S(2)}) %collective-permute-start.7) | collective-permute-done | bytes 262176 | tf_op jit(solution)/shard_map/ppermute | solution.py:333
  45.7 0.0 collective-permute-done.9.refs_3_
  45.7 0.5 group_sum_code.1
  46.2 0.1 collective-permute-start.10
  46.3 1.6 %collective-permute-start.11 = (bf16[2,128,128]{2,1,0:T(8,128)(2,1)S(1)}, bf16[2,128,128]{2,1,0:T(8,128)(2,1)S(1)}, u32[]{:S(2)}, u32[]{:S(2)}) collective-permute-start(bf16[2,128,128]{2,1,0:T(8,128)(2,1)S(1)} %get-tuple-element.45), channel_id=1, source_target_pairs={{0,16},{8,24},{16,0},{24,8},{1,17},{9,25},{17,1},{25,9},{2,18},{10... | collective-permute-start | bytes 196616 | tf_op jit(solution)/shard_map/ppermute | solution.py:307
  47.8 0.3 collective-permute-start.12
  48.1 2.5 %collective-permute-done.10.refs_0_ = bf16[2,128,128]{2,1,0:T(8,128)(2,1)S(1)} collective-permute-done((bf16[2,128,128]{2,1,0:T(8,128)(2,1)S(1)}, bf16[2,128,128]{2,1,0:T(8,128)(2,1)S(1)}, u32[]{:S(2)}, u32[]{:S(2)}) %collective-permute-start.10) | collective-permute-done | bytes 65568 | tf_op jit(solution)/shard_map/ppermute | solution.py:307
  50.6 1.5 %collective-permute-done.11.refs_1_ = bf16[2,128,128]{2,1,0:T(8,128)(2,1)S(1)} collective-permute-done((bf16[2,128,128]{2,1,0:T(8,128)(2,1)S(1)}, bf16[2,128,128]{2,1,0:T(8,128)(2,1)S(1)}, u32[]{:S(2)}, u32[]{:S(2)}) %collective-permute-start.11) | collective-permute-done | bytes 65568 | tf_op jit(solution)/shard_map/ppermute | solution.py:307
  52.1 0.0 collective-permute-done.12.refs_2_
  52.1 0.9 %sum_unrotate.1 = (f32[256,128]{1,0:T(8,128)}, f32[1,256]{1,0:T(1,128)}) custom-call(s32[256,128]{1,0:T(8,128)S(1)} %get-tuple-element.34.sign_ref, bf16[2,128,128]{2,1,0:T(8,128)(2,1)S(1)} %collective-permute-done.10.refs_0_, bf16[2,128,128]{2,1,0:T(8,128)(2,1)S(1)} %collective-permute-done.11.refs_1_, ...), custom_call_target="tpu_custom_call" | custom-call | tf_op jit(solution)/shard_map/sum_unrotate/pallas_call | solution.py:278
Async XLA Ops:
  2.6 15.3 %collective-permute-start.2 = (bf16[4,256,128]{2,1,0:T(8,128)(2,1)S(1)}, bf16[4,256,128]{2,1,0:T(8,128)(2,1)S(1)}, u32[]{:S(2)}, u32[]{:S(2)}) collective-permute-start(bf16[4,256,128]{2,1,0:T(8,128)(2,1)S(1)} %rotate_code.4.refs_0_), channel_id=1, source_target_pairs={{0,2},{1,3},{2,0},{3,1},{4,6},{5,7},{6,4},{7,5},{8,10},{9,11},{10,... | collective-permute-start | bytes 786440 | tf_op jit(solution)/shard_map/ppermute | solution.py:301
  9.1 7.3 %collective-permute-start = (bf16[4,128,128]{2,1,0:T(8,128)(2,1)S(1)}, bf16[4,128,128]{2,1,0:T(8,128)(2,1)S(1)}, u32[]{:S(2)}, u32[]{:S(2)}) collective-permute-start(bf16[4,128,128]{2,1,0:T(8,128)(2,1)S(1)} %get-tuple-element.26), channel_id=1, source_target_pairs={{0,3},{1,2},{2,1},{3,0},{4,7},{5,6},{6,5},{7,4},{8,11},{9,10},{10,... | collective-permute-start | bytes 393224 | tf_op jit(solution)/shard_map/ppermute | solution.py:301
  10.5 7.4 %collective-permute-start.1 = (bf16[4,128,128]{2,1,0:T(8,128)(2,1)S(1)}, bf16[4,128,128]{2,1,0:T(8,128)(2,1)S(1)}, u32[]{:S(2)}, u32[]{:S(2)}) collective-permute-start(bf16[4,128,128]{2,1,0:T(8,128)(2,1)S(1)} %get-tuple-element.27), channel_id=1, source_target_pairs={{0,1},{1,0},{2,3},{3,2},{4,5},{5,4},{6,7},{7,6},{8,9},{9,8},{10,11... | collective-permute-start | bytes 393224 | tf_op jit(solution)/shard_map/ppermute | solution.py:301
  12.7 14.8 %collective-permute-start.6 = (bf16[4,256,128]{2,1,0:T(8,128)(2,1)S(1)}, bf16[4,256,128]{2,1,0:T(8,128)(2,1)S(1)}, u32[]{:S(2)}, u32[]{:S(2)}) collective-permute-start(bf16[4,256,128]{2,1,0:T(8,128)(2,1)S(1)} %get-tuple-element.37), channel_id=1, source_target_pairs={{0,2},{1,3},{2,0},{3,1},{4,6},{5,7},{6,4},{7,5},{8,10},{9,11},{10,... | collective-permute-start | bytes 786440 | tf_op jit(solution)/shard_map/ppermute | solution.py:301
  18.0 9.9 %collective-permute-start.4 = (bf16[4,128,128]{2,1,0:T(8,128)(2,1)S(1)}, bf16[4,128,128]{2,1,0:T(8,128)(2,1)S(1)}, u32[]{:S(2)}, u32[]{:S(2)}) collective-permute-start(bf16[4,128,128]{2,1,0:T(8,128)(2,1)S(1)} %get-tuple-element.35), channel_id=1, source_target_pairs={{0,3},{1,2},{2,1},{3,0},{4,7},{5,6},{6,5},{7,4},{8,11},{9,10},{10,... | collective-permute-start | bytes 393224 | tf_op jit(solution)/shard_map/ppermute | solution.py:301
  19.5 8.4 %collective-permute-start.5 = (bf16[4,128,128]{2,1,0:T(8,128)(2,1)S(1)}, bf16[4,128,128]{2,1,0:T(8,128)(2,1)S(1)}, u32[]{:S(2)}, u32[]{:S(2)}) collective-permute-start(bf16[4,128,128]{2,1,0:T(8,128)(2,1)S(1)} %get-tuple-element.36), channel_id=1, source_target_pairs={{0,1},{1,0},{2,3},{3,2},{4,5},{5,4},{6,7},{7,6},{8,9},{9,8},{10,11... | collective-permute-start | bytes 393224 | tf_op jit(solution)/shard_map/ppermute | solution.py:301
  21.0 15.8 %collective-permute-start.3 = (f32[4,128,128]{2,1,0:T(8,128)S(1)}, f32[4,128,128]{2,1,0:T(8,128)S(1)}, u32[]{:S(2)}, u32[]{:S(2)}) collective-permute-start(f32[4,128,128]{2,1,0:T(8,128)S(1)} %get-tuple-element.33.refs_0_), channel_id=1, source_target_pairs={{0,4},{1,5},{2,6},{3,7},{4,0},{5,1},{6,2},{7,3},{8,12},{9,13},{10,... | collective-permute-start | bytes 786440 | tf_op jit(solution)/shard_map/ppermute | solution.py:324
  26.9 13.2 %collective-permute-start.8 = (bf16[4,256,128]{2,1,0:T(8,128)(2,1)S(1)}, bf16[4,256,128]{2,1,0:T(8,128)(2,1)S(1)}, u32[]{:S(2)}, u32[]{:S(2)}) collective-permute-start(bf16[4,256,128]{2,1,0:T(8,128)(2,1)S(1)} %get-tuple-element.40), channel_id=1, source_target_pairs={{0,3},{1,2},{2,1},{3,0},{4,7},{5,6},{6,5},{7,4},{8,11},{9,10},{10,... | collective-permute-start | bytes 786440 | tf_op jit(solution)/shard_map/ppermute | solution.py:301
  28.0 17.7 %collective-permute-start.7 = (f32[4,128,128]{2,1,0:T(8,128)S(1)}, f32[4,128,128]{2,1,0:T(8,128)S(1)}, u32[]{:S(2)}, u32[]{:S(2)}) collective-permute-start(f32[4,128,128]{2,1,0:T(8,128)S(1)} %get-tuple-element.39), channel_id=1, source_target_pairs={{0,4},{1,5},{2,6},{3,7},{4,0},{5,1},{6,2},{7,3},{8,12},{9,13},{10,... | collective-permute-start | bytes 786440 | tf_op jit(solution)/shard_map/ppermute | solution.py:333
  29.3 16.4 %collective-permute-start.9 = (bf16[4,256,128]{2,1,0:T(8,128)(2,1)S(1)}, bf16[4,256,128]{2,1,0:T(8,128)(2,1)S(1)}, u32[]{:S(2)}, u32[]{:S(2)}) collective-permute-start(bf16[4,256,128]{2,1,0:T(8,128)(2,1)S(1)} %get-tuple-element.41), channel_id=1, source_target_pairs={{0,1},{1,0},{2,3},{3,2},{4,5},{5,4},{6,7},{7,6},{8,9},{9,8},{10,11... | collective-permute-start | bytes 786440 | tf_op jit(solution)/shard_map/ppermute | solution.py:301
  46.2 4.4 %collective-permute-start.10 = (bf16[2,128,128]{2,1,0:T(8,128)(2,1)S(1)}, bf16[2,128,128]{2,1,0:T(8,128)(2,1)S(1)}, u32[]{:S(2)}, u32[]{:S(2)}) collective-permute-start(bf16[2,128,128]{2,1,0:T(8,128)(2,1)S(1)} %get-tuple-element.44), channel_id=1, source_target_pairs={{0,24},{8,16},{16,8},{24,0},{1,25},{9,17},{17,9},{25,1},{2,26},{10... | collective-permute-start | bytes 196616 | tf_op jit(solution)/shard_map/ppermute | solution.py:307
  46.3 5.8 %collective-permute-start.11 = (bf16[2,128,128]{2,1,0:T(8,128)(2,1)S(1)}, bf16[2,128,128]{2,1,0:T(8,128)(2,1)S(1)}, u32[]{:S(2)}, u32[]{:S(2)}) collective-permute-start(bf16[2,128,128]{2,1,0:T(8,128)(2,1)S(1)} %get-tuple-element.45), channel_id=1, source_target_pairs={{0,16},{8,24},{16,0},{24,8},{1,17},{9,25},{17,1},{25,9},{2,18},{10... | collective-permute-start | bytes 196616 | tf_op jit(solution)/shard_map/ppermute | solution.py:307
  47.8 4.2 %collective-permute-start.12 = (bf16[2,128,128]{2,1,0:T(8,128)(2,1)S(1)}, bf16[2,128,128]{2,1,0:T(8,128)(2,1)S(1)}, u32[]{:S(2)}, u32[]{:S(2)}) collective-permute-start(bf16[2,128,128]{2,1,0:T(8,128)(2,1)S(1)} %get-tuple-element.46), channel_id=1, source_target_pairs={{0,8},{8,0},{16,24},{24,16},{1,9},{9,1},{17,25},{25,17},{2,10},{10... | collective-permute-start | bytes 196616 | tf_op jit(solution)/shard_map/ppermute | solution.py:307

commit v17 on v15

--- a/solution.py
+++ b/solution.py
@@ -199,12 +199,12 @@
     refs[-1][...] = add_all(arrays)
 
 
-def far_sum(parts, layout, part, later):
+def far_sum(parts, layout, part, later, after=()):
     size = QGROUP * layout.units * layout.columns
     *later, total = pl.pallas_call(
         functools.partial(far_sum_kernel, part, len(parts)),
         in_specs=[pl.BlockSpec(memory_space=pltpu.VMEM)] * len(parts)
-        + [pl.BlockSpec(memory_space=pl.ANY)] * len(later),
+        + [pl.BlockSpec(memory_space=pl.ANY)] * (len(later) + len(after)),
         out_specs=[pl.BlockSpec(memory_space=pl.ANY)] * len(later) + [pl.BlockSpec(memory_space=pltpu.VMEM)],
         out_shape=[jax.ShapeDtypeStruct(array.shape, array.dtype) for array in later]
         + [jax.ShapeDtypeStruct(layout.shape(), jnp.float32)],
@@ -214,7 +214,7 @@
             flops=2 * len(parts) * size, bytes_accessed=(2 * len(parts) + 4) * size, transcendentals=0
         ),
         name="far_sum",
-    )(*parts, *later)
+    )(*parts, *later, *after)
     return total, later
 
 
@@ -316,18 +316,16 @@
     outs = rotate(values, sign_rows, layout, True, order, order[:-1])
     far = {step: [outs.pop(0), outs.pop(0)] for step in order[:-1]}
     far[0] = outs
-    for step in order[:-1]:
-        far[step][0] = swap(far[step][0], step)
-    for step in order[:-2]:
-        far[step][1] = swap(far[step][1], step)
-    far[last][1], part = rotate(values, sign_rows, layout, False, [slow], later=[far[last][1]])
-    first, (part, far[last][1]) = far_sum([far[step][0] for step in order], layout, 0, [part, far[last][1]])
+    for part in range(HALVES):
+        for step in order[:-1]:
+            far[step][part] = swap(far[step][part], step)
+    (part,) = rotate(values, sign_rows, layout, False, [slow], after=far[0])
+    first, (part,) = far_sum([far[step][0] for step in order], layout, 0, [part])
     across = [lax.ppermute(first, "local", counterparts)]
     near = {slow: swap(part, slow)}
-    far[last][1] = swap(far[last][1], last)
-    *outs, own_signs = rotate(values, sign_rows, layout, False, others + [0], signed_out=True, after=[part])
-    second, outs[:-1] = far_sum([far[step][-1] for step in order], layout, 1, outs[:-1])
+    second, _ = far_sum([far[step][-1] for step in order], layout, 1, [], [first, part])
     across.append(lax.ppermute(second, "local", counterparts))
+    *outs, own_signs = rotate(values, sign_rows, layout, False, others + [0], signed_out=True, after=[second])
     for step, part in zip(others + [0], outs):
         near[step] = swap(part, step) if step else part
     reduced, rotated_max = finish(share(group_sum([near[step] for step in order], across, layout)), own_signs)

time: 50.5 us -> 49.7 us (0.984)
  waiting for transfers between devices: 21 us -> 16.8 us
  starting transfers between devices: 17.9 us -> 21.4 us
    ppermute x1, waiting for transfers between devices: 5.92 us -> 0.01 us  [shards(): across = [lax.ppermute(first, 'local', counterparts)]]
    ppermute x9, starting transfers between devices: 13 us -> 15.9 us  [swap(): return lax.ppermute(part, 'local', pairs)]
    ppermute x9, waiting for transfers between devices: 3.31 us -> 4.95 us  [swap(): return lax.ppermute(part, 'local', pairs)]
  transfers between devices with their start and end apart: 14 -> 14, of which waited for: 6 -> 8; matrix products, arithmetic and copies ran while one was open for 0% -> 0% of each run, Pallas kernels for 11% -> 11%
where the time goes in v17:
time: 49.7 us; the launch traced here: 49.6 us
  starting transfers between devices  21.4 us (43%)
  waiting for transfers between devices  16.8 us (34%)
  Pallas kernels  10.8 us (22%)
  between operations  0.69 us (1%)
    ppermute x9, starting transfers between devices, swap(): return lax.ppermute(part, 'local', pairs)  15.9 us
    pallas_call x3, Pallas kernels, rotate(): pl.pallas_call(functools.partial(rotate_kernel, layout, other, steps, cut...  9.2 us
    ppermute x1, waiting for transfers between devices, shards(): across.append(lax.ppermute(second, 'local', counterparts))  8.43 us
    ppermute x9, waiting for transfers between devices, swap(): return lax.ppermute(part, 'local', pairs)  4.95 us
    ppermute x3, waiting for transfers between devices, share(): moved.append(lax.ppermute(parts[step], 'node', pairs))  3.38 us
    ppermute x1, starting transfers between devices, shards(): across = [lax.ppermute(first, 'local', counterparts)]  2.7 us
    ppermute x3, starting transfers between devices, share(): moved.append(lax.ppermute(parts[step], 'node', pairs))  2.15 us
  transfers between devices with their start and end apart: 14, of which 8 were waited for; matrix products, arithmetic and copies ran while one was open for 0% of the time, Pallas kernels for 11%

profile of v17, /device:TPU:0, one launch (start us, length us, event | category | flops | bytes accessed | tf_op | source)
XLA Modules:
  0.0 49.6 jit_solution(4475034365339154091)
XLA Ops:
  0.6 3.9 %rotate_code.3 = (bf16[4,128,128]{2,1,0:T(8,128)(2,1)S(1)}, bf16[4,128,128]{2,1,0:T(8,128)(2,1)S(1)}, bf16[4,128,128]{2,1,0:T(8,128)(2,1)S(1)}, bf16[4,128,128]{...) custom-call(bf16[1,1048576]{1,0:T(2,128)(2,1)} %bitcast.4, ...), custom_call_target="tpu_custom_call" | custom-call | flops 268435456 | bytes 5242880 | tf_op jit(solution)/shard_map/rotate_code/pallas_call | solution.py:164
  4.5 4.0 %collective-permute-start.3 = (bf16[4,128,128]{2,1,0:T(8,128)(2,1)S(1)}, bf16[4,128,128]{2,1,0:T(8,128)(2,1)S(1)}, u32[]{:S(2)}, u32[]{:S(2)}) collective-permute-start(bf16[4,128,128]{2,1,0:T(8,128)(2,1)S(1)} %get-tuple-element.25), channel_id=1, source_target_pairs={{0,3},{1,2},{2,1},{3,0},{4,7},{5,6},{6,5},{7,4},{8,11},{9,10},{10,... | collective-permute-start | bytes 393224 | tf_op jit(solution)/shard_map/ppermute | solution.py:301
  8.6 0.4 collective-permute-start.4
  9.0 0.2 collective-permute-start.5
  9.2 2.8 %collective-permute-start = (bf16[4,128,128]{2,1,0:T(8,128)(2,1)S(1)}, bf16[4,128,128]{2,1,0:T(8,128)(2,1)S(1)}, u32[]{:S(2)}, u32[]{:S(2)}) collective-permute-start(bf16[4,128,128]{2,1,0:T(8,128)(2,1)S(1)} %get-tuple-element.21), channel_id=1, source_target_pairs={{0,3},{1,2},{2,1},{3,0},{4,7},{5,6},{6,5},{7,4},{8,11},{9,10},{10,... | collective-permute-start | bytes 393224 | tf_op jit(solution)/shard_map/ppermute | solution.py:301
  12.1 0.4 collective-permute-start.1
  12.5 0.4 collective-permute-done.3.refs_0_
  12.9 1.9 %collective-permute-start.2 = (bf16[4,128,128]{2,1,0:T(8,128)(2,1)S(1)}, bf16[4,128,128]{2,1,0:T(8,128)(2,1)S(1)}, u32[]{:S(2)}, u32[]{:S(2)}) collective-permute-start(bf16[4,128,128]{2,1,0:T(8,128)(2,1)S(1)} %get-tuple-element.23), channel_id=1, source_target_pairs={{0,1},{1,0},{2,3},{3,2},{4,5},{5,4},{6,7},{7,6},{8,9},{9,8},{10,11... | collective-permute-start | bytes 393224 | tf_op jit(solution)/shard_map/ppermute | solution.py:301
  14.8 2.0 %rotate_code.4.refs_4_ = bf16[4,256,128]{2,1,0:T(8,128)(2,1)S(1)} custom-call(bf16[1,1048576]{1,0:T(2,128)(2,1)} %bitcast.5, s32[8192,128]{1,0:T(8,128)} %bitcast.8, bf16[4,256,128]{2,1,0:T(8,128)(2,1)S(1)} %get-tuple-element.24.refs_0_.refs_3_), custom_call_target="tpu_custom_call" | custom-call | flops 67108864 | bytes 1310720 | tf_op jit(solution)/shard_map/rotate_code/pallas_call | solution.py:164
  16.9 0.0 collective-permute-done.4.refs_1_
  16.9 1.4 %collective-permute-done.5.refs_2_ = bf16[4,128,128]{2,1,0:T(8,128)(2,1)S(1)} collective-permute-done((bf16[4,128,128]{2,1,0:T(8,128)(2,1)S(1)}, bf16[4,128,128]{2,1,0:T(8,128)(2,1)S(1)}, u32[]{:S(2)}, u32[]{:S(2)}) %collective-permute-start.5) | collective-permute-done | bytes 131104 | tf_op jit(solution)/shard_map/ppermute | solution.py:301
  18.3 0.1 far_sum.2
  18.3 2.7 %collective-permute-start.6 = (f32[4,128,128]{2,1,0:T(8,128)S(1)}, f32[4,128,128]{2,1,0:T(8,128)S(1)}, u32[]{:S(2)}, u32[]{:S(2)}) collective-permute-start(f32[4,128,128]{2,1,0:T(8,128)S(1)} %get-tuple-element.28.refs_4_), channel_id=1, source_target_pairs={{0,4},{1,5},{2,6},{3,7},{4,0},{5,1},{6,2},{7,3},{8,12},{9,13},{10,... | collective-permute-start | bytes 786440 | tf_op jit(solution)/shard_map/ppermute | solution.py:324
  21.0 1.6 %collective-permute-start.9 = (bf16[4,256,128]{2,1,0:T(8,128)(2,1)S(1)}, bf16[4,256,128]{2,1,0:T(8,128)(2,1)S(1)}, u32[]{:S(2)}, u32[]{:S(2)}) collective-permute-start(bf16[4,256,128]{2,1,0:T(8,128)(2,1)S(1)} %get-tuple-element.29.refs_5_), channel_id=1, source_target_pairs={{0,2},{1,3},{2,0},{3,1},{4,6},{5,7},{6,4},{7,5},{8,10},{9,11},{10,... | collective-permute-start | bytes 786440 | tf_op jit(solution)/shard_map/ppermute | solution.py:301
  22.6 0.0 collective-permute-done.refs_0_
  22.6 2.6 %collective-permute-done.1.refs_1_ = bf16[4,128,128]{2,1,0:T(8,128)(2,1)S(1)} collective-permute-done((bf16[4,128,128]{2,1,0:T(8,128)(2,1)S(1)}, bf16[4,128,128]{2,1,0:T(8,128)(2,1)S(1)}, u32[]{:S(2)}, u32[]{:S(2)}) %collective-permute-start.1) | collective-permute-done | bytes 131104 | tf_op jit(solution)/shard_map/ppermute | solution.py:301
  25.2 0.0 collective-permute-done.2.refs_2_
  25.2 0.1 far_sum.3.refs_0_
  25.3 0.6 %collective-permute-start.7 = (f32[4,128,128]{2,1,0:T(8,128)S(1)}, f32[4,128,128]{2,1,0:T(8,128)S(1)}, u32[]{:S(2)}, u32[]{:S(2)}) collective-permute-start(f32[4,128,128]{2,1,0:T(8,128)S(1)} %far_sum.3.refs_0_), channel_id=1, source_target_pairs={{0,4},{1,5},{2,6},{3,7},{4,0},{5,1},{6,2},{7,3},{8,12},{9,13},{10,... | collective-permute-start | bytes 786440 | tf_op jit(solution)/shard_map/ppermute | solution.py:327
  25.8 3.3 %rotate_code.5 = (bf16[4,256,128]{2,1,0:T(8,128)(2,1)S(1)}, bf16[4,256,128]{2,1,0:T(8,128)(2,1)S(1)}, bf16[4,256,128]{2,1,0:T(8,128)(2,1)S(1)}, s32[256,128]{1,0:T(8,128)S(1)}) custom-call(bf16[1,1048576]{1,0:T(2,128)(2,1)} %bitcast.6, s32[8192,128]{1,0:T(8,128)} %bitcast.9, f32[4,128,128]{2,1,0:T(8,128)S(1)} %far_sum.3.refs_0_), custom_call_target="tpu_custom_call" | custom-call | flops 201326592 | bytes 3932160 | tf_op jit(solution)/shard_map/rotate_code/pallas_call | solution.py:164
  29.2 0.5 %collective-permute-start.8 = (bf16[4,256,128]{2,1,0:T(8,128)(2,1)S(1)}, bf16[4,256,128]{2,1,0:T(8,128)(2,1)S(1)}, u32[]{:S(2)}, u32[]{:S(2)}) collective-permute-start(bf16[4,256,128]{2,1,0:T(8,128)(2,1)S(1)} %get-tuple-element.31), channel_id=1, source_target_pairs={{0,3},{1,2},{2,1},{3,0},{4,7},{5,6},{6,5},{7,4},{8,11},{9,10},{10,... | collective-permute-start | bytes 786440 | tf_op jit(solution)/shard_map/ppermute | solution.py:301
  29.7 3.9 %collective-permute-start.10 = (bf16[4,256,128]{2,1,0:T(8,128)(2,1)S(1)}, bf16[4,256,128]{2,1,0:T(8,128)(2,1)S(1)}, u32[]{:S(2)}, u32[]{:S(2)}) collective-permute-start(bf16[4,256,128]{2,1,0:T(8,128)(2,1)S(1)} %get-tuple-element.32), channel_id=1, source_target_pairs={{0,1},{1,0},{2,3},{3,2},{4,5},{5,4},{6,7},{7,6},{8,9},{9,8},{10,11... | collective-permute-start | bytes 786440 | tf_op jit(solution)/shard_map/ppermute | solution.py:301
  33.6 8.4 %collective-permute-done.7.refs_1_ = f32[4,128,128]{2,1,0:T(8,128)S(1)} collective-permute-done((f32[4,128,128]{2,1,0:T(8,128)S(1)}, f32[4,128,128]{2,1,0:T(8,128)S(1)}, u32[]{:S(2)}, u32[]{:S(2)}) %collective-permute-start.7) | collective-permute-done | bytes 262176 | tf_op jit(solution)/shard_map/ppermute | solution.py:327
  42.0 0.0 collective-permute-done.6.refs_0_
  42.0 0.0 collective-permute-done.9.refs_3_
  42.0 0.2 collective-permute-done.8.refs_2_
  42.3 0.3 collective-permute-done.10.refs_4_
  42.6 0.5 %group_sum_code.1 = (bf16[2,128,128]{2,1,0:T(8,128)(2,1)S(1)}, bf16[2,128,128]{2,1,0:T(8,128)(2,1)S(1)}, bf16[2,128,128]{2,1,0:T(8,128)(2,1)S(1)}, bf16[2,128,128]{2,1,0:T(8,128)(2,1)S(1)}) custom-call(f32[4,128,128]{2,1,0:T(8,128)S(1)} %collective-permute-done.6.refs_0_, f32[4,128,128]{2,1,0:T(8,128)S(1)} %collective-permute-done.7.refs_1_, ...), custom_call_target="tpu_custom_call" | custom-call | flops 3932160 | bytes 1835008 | tf_op jit(solution)/shard_map/group_sum_code/pallas_call | solution.py:233
  43.1 0.1 collective-permute-start.11
  43.2 2.0 %collective-permute-start.12 = (bf16[2,128,128]{2,1,0:T(8,128)(2,1)S(1)}, bf16[2,128,128]{2,1,0:T(8,128)(2,1)S(1)}, u32[]{:S(2)}, u32[]{:S(2)}) collective-permute-start(bf16[2,128,128]{2,1,0:T(8,128)(2,1)S(1)} %get-tuple-element.35), channel_id=1, source_target_pairs={{0,16},{8,24},{16,0},{24,8},{1,17},{9,25},{17,1},{25,9},{2,18},{10... | collective-permute-start | bytes 196616 | tf_op jit(solution)/shard_map/ppermute | solution.py:307
  45.2 0.0 collective-permute-start.13
  45.3 1.8 %collective-permute-done.11.refs_0_ = bf16[2,128,128]{2,1,0:T(8,128)(2,1)S(1)} collective-permute-done((bf16[2,128,128]{2,1,0:T(8,128)(2,1)S(1)}, bf16[2,128,128]{2,1,0:T(8,128)(2,1)S(1)}, u32[]{:S(2)}, u32[]{:S(2)}) %collective-permute-start.11) | collective-permute-done | bytes 65568 | tf_op jit(solution)/shard_map/ppermute | solution.py:307
  47.1 1.6 %collective-permute-done.12.refs_1_ = bf16[2,128,128]{2,1,0:T(8,128)(2,1)S(1)} collective-permute-done((bf16[2,128,128]{2,1,0:T(8,128)(2,1)S(1)}, bf16[2,128,128]{2,1,0:T(8,128)(2,1)S(1)}, u32[]{:S(2)}, u32[]{:S(2)}) %collective-permute-start.12) | collective-permute-done | bytes 65568 | tf_op jit(solution)/shard_map/ppermute | solution.py:307
  48.6 0.0 collective-permute-done.13.refs_2_
  48.6 0.9 %sum_unrotate.1 = (f32[256,128]{1,0:T(8,128)}, f32[1,256]{1,0:T(1,128)}) custom-call(s32[256,128]{1,0:T(8,128)S(1)} %get-tuple-element.30.sign_ref, bf16[2,128,128]{2,1,0:T(8,128)(2,1)S(1)} %collective-permute-done.11.refs_0_, bf16[2,128,128]{2,1,0:T(8,128)(2,1)S(1)} %collective-permute-done.12.refs_1_, ...), custom_call_target="tpu_custom_call" | custom-call | tf_op jit(solution)/shard_map/sum_unrotate/pallas_call | solution.py:278
Async XLA Ops:
  4.5 8.4 %collective-permute-start.3 = (bf16[4,128,128]{2,1,0:T(8,128)(2,1)S(1)}, bf16[4,128,128]{2,1,0:T(8,128)(2,1)S(1)}, u32[]{:S(2)}, u32[]{:S(2)}) collective-permute-start(bf16[4,128,128]{2,1,0:T(8,128)(2,1)S(1)} %get-tuple-element.25), channel_id=1, source_target_pairs={{0,3},{1,2},{2,1},{3,0},{4,7},{5,6},{6,5},{7,4},{8,11},{9,10},{10,... | collective-permute-start | bytes 393224 | tf_op jit(solution)/shard_map/ppermute | solution.py:301
  8.6 8.3 %collective-permute-start.4 = (bf16[4,128,128]{2,1,0:T(8,128)(2,1)S(1)}, bf16[4,128,128]{2,1,0:T(8,128)(2,1)S(1)}, u32[]{:S(2)}, u32[]{:S(2)}) collective-permute-start(bf16[4,128,128]{2,1,0:T(8,128)(2,1)S(1)} %get-tuple-element.26), channel_id=1, source_target_pairs={{0,2},{1,3},{2,0},{3,1},{4,6},{5,7},{6,4},{7,5},{8,10},{9,11},{10,... | collective-permute-start | bytes 393224 | tf_op jit(solution)/shard_map/ppermute | solution.py:301
  9.0 9.3 %collective-permute-start.5 = (bf16[4,128,128]{2,1,0:T(8,128)(2,1)S(1)}, bf16[4,128,128]{2,1,0:T(8,128)(2,1)S(1)}, u32[]{:S(2)}, u32[]{:S(2)}) collective-permute-start(bf16[4,128,128]{2,1,0:T(8,128)(2,1)S(1)} %get-tuple-element.27), channel_id=1, source_target_pairs={{0,1},{1,0},{2,3},{3,2},{4,5},{5,4},{6,7},{7,6},{8,9},{9,8},{10,11... | collective-permute-start | bytes 393224 | tf_op jit(solution)/shard_map/ppermute | solution.py:301
  9.2 13.4 %collective-permute-start = (bf16[4,128,128]{2,1,0:T(8,128)(2,1)S(1)}, bf16[4,128,128]{2,1,0:T(8,128)(2,1)S(1)}, u32[]{:S(2)}, u32[]{:S(2)}) collective-permute-start(bf16[4,128,128]{2,1,0:T(8,128)(2,1)S(1)} %get-tuple-element.21), channel_id=1, source_target_pairs={{0,3},{1,2},{2,1},{3,0},{4,7},{5,6},{6,5},{7,4},{8,11},{9,10},{10,... | collective-permute-start | bytes 393224 | tf_op jit(solution)/shard_map/ppermute | solution.py:301
  12.1 13.1 %collective-permute-start.1 = (bf16[4,128,128]{2,1,0:T(8,128)(2,1)S(1)}, bf16[4,128,128]{2,1,0:T(8,128)(2,1)S(1)}, u32[]{:S(2)}, u32[]{:S(2)}) collective-permute-start(bf16[4,128,128]{2,1,0:T(8,128)(2,1)S(1)} %get-tuple-element.22), channel_id=1, source_target_pairs={{0,2},{1,3},{2,0},{3,1},{4,6},{5,7},{6,4},{7,5},{8,10},{9,11},{10,... | collective-permute-start | bytes 393224 | tf_op jit(solution)/shard_map/ppermute | solution.py:301
  12.9 12.3 %collective-permute-start.2 = (bf16[4,128,128]{2,1,0:T(8,128)(2,1)S(1)}, bf16[4,128,128]{2,1,0:T(8,128)(2,1)S(1)}, u32[]{:S(2)}, u32[]{:S(2)}) collective-permute-start(bf16[4,128,128]{2,1,0:T(8,128)(2,1)S(1)} %get-tuple-element.23), channel_id=1, source_target_pairs={{0,1},{1,0},{2,3},{3,2},{4,5},{5,4},{6,7},{7,6},{8,9},{9,8},{10,11... | collective-permute-start | bytes 393224 | tf_op jit(solution)/shard_map/ppermute | solution.py:301
  18.3 23.7 %collective-permute-start.6 = (f32[4,128,128]{2,1,0:T(8,128)S(1)}, f32[4,128,128]{2,1,0:T(8,128)S(1)}, u32[]{:S(2)}, u32[]{:S(2)}) collective-permute-start(f32[4,128,128]{2,1,0:T(8,128)S(1)} %get-tuple-element.28.refs_4_), channel_id=1, source_target_pairs={{0,4},{1,5},{2,6},{3,7},{4,0},{5,1},{6,2},{7,3},{8,12},{9,13},{10,... | collective-permute-start | bytes 786440 | tf_op jit(solution)/shard_map/ppermute | solution.py:324
  21.0 21.0 %collective-permute-start.9 = (bf16[4,256,128]{2,1,0:T(8,128)(2,1)S(1)}, bf16[4,256,128]{2,1,0:T(8,128)(2,1)S(1)}, u32[]{:S(2)}, u32[]{:S(2)}) collective-permute-start(bf16[4,256,128]{2,1,0:T(8,128)(2,1)S(1)} %get-tuple-element.29.refs_5_), channel_id=1, source_target_pairs={{0,2},{1,3},{2,0},{3,1},{4,6},{5,7},{6,4},{7,5},{8,10},{9,11},{10,... | collective-permute-start | bytes 786440 | tf_op jit(solution)/shard_map/ppermute | solution.py:301
  25.3 16.7 %collective-permute-start.7 = (f32[4,128,128]{2,1,0:T(8,128)S(1)}, f32[4,128,128]{2,1,0:T(8,128)S(1)}, u32[]{:S(2)}, u32[]{:S(2)}) collective-permute-start(f32[4,128,128]{2,1,0:T(8,128)S(1)} %far_sum.3.refs_0_), channel_id=1, source_target_pairs={{0,4},{1,5},{2,6},{3,7},{4,0},{5,1},{6,2},{7,3},{8,12},{9,13},{10,... | collective-permute-start | bytes 786440 | tf_op jit(solution)/shard_map/ppermute | solution.py:327
  29.2 13.1 %collective-permute-start.8 = (bf16[4,256,128]{2,1,0:T(8,128)(2,1)S(1)}, bf16[4,256,128]{2,1,0:T(8,128)(2,1)S(1)}, u32[]{:S(2)}, u32[]{:S(2)}) collective-permute-start(bf16[4,256,128]{2,1,0:T(8,128)(2,1)S(1)} %get-tuple-element.31), channel_id=1, source_target_pairs={{0,3},{1,2},{2,1},{3,0},{4,7},{5,6},{6,5},{7,4},{8,11},{9,10},{10,... | collective-permute-start | bytes 786440 | tf_op jit(solution)/shard_map/ppermute | solution.py:301
  29.7 12.9 %collective-permute-start.10 = (bf16[4,256,128]{2,1,0:T(8,128)(2,1)S(1)}, bf16[4,256,128]{2,1,0:T(8,128)(2,1)S(1)}, u32[]{:S(2)}, u32[]{:S(2)}) collective-permute-start(bf16[4,256,128]{2,1,0:T(8,128)(2,1)S(1)} %get-tuple-element.32), channel_id=1, source_target_pairs={{0,1},{1,0},{2,3},{3,2},{4,5},{5,4},{6,7},{7,6},{8,9},{9,8},{10,11... | collective-permute-start | bytes 786440 | tf_op jit(solution)/shard_map/ppermute | solution.py:301
  43.1 4.0 %collective-permute-start.11 = (bf16[2,128,128]{2,1,0:T(8,128)(2,1)S(1)}, bf16[2,128,128]{2,1,0:T(8,128)(2,1)S(1)}, u32[]{:S(2)}, u32[]{:S(2)}) collective-permute-start(bf16[2,128,128]{2,1,0:T(8,128)(2,1)S(1)} %get-tuple-element.34), channel_id=1, source_target_pairs={{0,24},{8,16},{16,8},{24,0},{1,25},{9,17},{17,9},{25,1},{2,26},{10... | collective-permute-start | bytes 196616 | tf_op jit(solution)/shard_map/ppermute | solution.py:307
  43.2 5.5 %collective-permute-start.12 = (bf16[2,128,128]{2,1,0:T(8,128)(2,1)S(1)}, bf16[2,128,128]{2,1,0:T(8,128)(2,1)S(1)}, u32[]{:S(2)}, u32[]{:S(2)}) collective-permute-start(bf16[2,128,128]{2,1,0:T(8,128)(2,1)S(1)} %get-tuple-element.35), channel_id=1, source_target_pairs={{0,16},{8,24},{16,0},{24,8},{1,17},{9,25},{17,1},{25,9},{2,18},{10... | collective-permute-start | bytes 196616 | tf_op jit(solution)/shard_map/ppermute | solution.py:307
  45.2 3.4 %collective-permute-start.13 = (bf16[2,128,128]{2,1,0:T(8,128)(2,1)S(1)}, bf16[2,128,128]{2,1,0:T(8,128)(2,1)S(1)}, u32[]{:S(2)}, u32[]{:S(2)}) collective-permute-start(bf16[2,128,128]{2,1,0:T(8,128)(2,1)S(1)} %get-tuple-element.36), channel_id=1, source_target_pairs={{0,8},{8,0},{16,24},{24,16},{1,9},{9,1},{17,25},{25,17},{2,10},{10... | collective-permute-start | bytes 196616 | tf_op jit(solution)/shard_map/ppermute | solution.py:307

commit v18 on v17

--- a/solution.py
+++ b/solution.py
@@ -12,7 +12,6 @@
 LANES = 128
 VMEM_LIMIT = 50 * 1024 * 1024
 SUM_VMEM_LIMIT = 24 * 1024 * 1024
-AHEAD = 4
 PIECES = 8
 
 
@@ -62,68 +61,74 @@
     def shape(self):
         return (self.units, QGROUP, self.columns)
 
-    def span(self, steps):
-        return 1 if len(steps) == 1 else self.half
+    def runs(self, steps, inner):
+        half = self.half
+        if half & (half - 1) or len(steps) == half:
+            return [(0, half)]
+        low = 1
+        while low < half and all(step in steps for step in range(2 * low)):
+            low *= 2
+        runs = [(inner // low * low, low)] if 0 in steps else []
+        count = low if 0 in steps else 1
+        while count < half:
+            present = [step for step in range(count, 2 * count) if step in steps]
+            if len(present) == count:
+                runs.append(((inner ^ count) // count * count, count))
+            else:
+                runs += [(inner ^ step, 1) for step in present]
+            count *= 2
+        return runs
 
     def batch(self, steps):
         batch = min(self.units, max(1, PIECES // len(steps)))
         return batch if self.units % batch == 0 else 1
 
 
-def rotate_kernel(layout, other, steps, cut, signed_out, extra, values_ref, signs_ref, *refs):
+def rotate_kernel(layout, other, steps, parts, signed_out, extra, values_ref, signs_ref, *refs):
     values, flips, turned, matrix, value_sems, sign_sems = refs[-6:]
-    out_refs = list(refs[extra:-6])
-    step_refs = [[out_refs.pop(0) for _ in range(HALVES if step in cut else 1)] for step in steps]
+    out_refs = refs[extra:-6]
     half, portion, rows = layout.half, layout.portion, layout.rows
     node = lax.axis_index("node")
     member = lax.axis_index("local")
     inner = lax.rem(member, half)
     first = half - (member - inner) if other else member - inner
-    span, batch = layout.span(steps), layout.batch(steps)
-    lowest = partner(inner, steps[0], half) if span == 1 else 0
-
-    def fetches(unit, part):
-        place = partner(node, unit * layout.together + part, layout.groups) * layout.members + first + lowest
-        return (
-            pltpu.make_async_copy(
-                values_ref.at[:, pl.ds(pl.multiple_of(place * portion, portion), span * portion)],
-                values.at[unit, part],
-                value_sems.at[unit, part],
-            ),
-            pltpu.make_async_copy(
-                signs_ref.at[pl.ds(pl.multiple_of(place * rows, rows), span * rows), :],
-                flips.at[unit, part],
-                sign_sems.at[unit, part],
-            ),
-        )
-
-    def fetch(unit):
+    runs, batch = layout.runs(steps, inner), layout.batch(steps)
+
+    def fetches(unit):
+        copies = []
         for part in range(layout.together):
-            for copy in fetches(unit, part):
-                copy.start()
-
-    ahead = min(max(AHEAD, batch), layout.units)
-    for unit in range(ahead):
-        fetch(unit)
+            section = partner(node, unit * layout.together + part, layout.groups) * layout.members + first
+            for index, (owner, count) in enumerate(runs):
+                place = section + owner
+                copies.append(
+                    pltpu.make_async_copy(
+                        values_ref.at[:, pl.ds(pl.multiple_of(place * portion, portion), count * portion)],
+                        values.at[unit, part, :, pl.ds(pl.multiple_of(owner * portion, portion), count * portion)],
+                        value_sems.at[unit, part, index],
+                    )
+                )
+                copies.append(
+                    pltpu.make_async_copy(
+                        signs_ref.at[pl.ds(pl.multiple_of(place * rows, rows), count * rows), :],
+                        flips.at[unit, part, pl.ds(pl.multiple_of(owner * rows, rows), count * rows), :],
+                        sign_sems.at[unit, part, index],
+                    )
+                )
+        return copies
+
+    for unit in range(layout.units):
+        for copy in fetches(unit):
+            copy.start()
     matrix[...] = sylvester()
 
     def body(turn, carry):
         for index in range(batch):
-            for part in range(layout.together):
-                for copy in fetches(turn * batch + index, part):
-                    copy.wait()
-
-        if ahead < layout.units:
-            for index in range(batch):
-
-                @pl.when(turn * batch + index + ahead < layout.units)
-                def _():
-                    fetch(turn * batch + index + ahead)
-
+            for copy in fetches(turn * batch + index):
+                copy.wait()
         for index, (position, step) in [(i, p) for i in range(batch) for p in enumerate(steps)]:
             unit = turn * batch + index
             slot = turned.at[index * len(steps) + position]
-            owner = 0 if span == 1 else partner(inner, step, half)
+            owner = partner(inner, step, half)
             at = pl.ds(pl.multiple_of(owner * portion, portion), portion)
             at_rows = pl.ds(pl.multiple_of(owner * rows, rows), rows)
             for part in range(layout.together):
@@ -131,56 +136,50 @@
                 slot[part * rows : (part + 1) * rows] = jnp.where(flips[unit, part, at_rows, :] == 0, wide, -wide)
             halves = [slot[pl.ds(part, layout.columns, stride=HALVES), :] for part in range(HALVES)]
             signed = jnp.concatenate(halves, axis=1).astype(jnp.bfloat16)
+            wanted = parts[position]
+            lowest = wanted[0] * QGROUP
             rotated = lax.dot_general(
-                matrix[...], signed, (((1,), (1,)), ((), ())), preferred_element_type=jnp.float32
+                matrix[lowest : lowest + len(wanted) * QGROUP],
+                signed,
+                (((1,), (1,)), ((), ())),
+                preferred_element_type=jnp.float32,
             )
-            for part in range(HALVES):
+            for part in range(len(wanted)):
                 rows_of = slice(part * QGROUP, (part + 1) * QGROUP)
-                coded = recode(rotated[rows_of]).astype(jnp.bfloat16)
-                if step in cut:
-                    step_refs[position][part][unit] = coded
-                else:
-                    step_refs[position][0][unit, rows_of] = coded
+                out_refs[position][unit, rows_of] = recode(rotated[rows_of]).astype(jnp.bfloat16)
         return carry
 
     lax.fori_loop(0, layout.units // batch, body, 0)
     if signed_out:
-        out_refs[0][...] = flips[0, 0, pl.ds(pl.multiple_of(inner * rows, rows), rows), :]
-
-
-def rotate(values, signs, layout, other, steps, cut=(), signed_out=False, after=(), later=()):
+        out_refs[-1][...] = flips[0, 0, pl.ds(pl.multiple_of(inner * rows, rows), rows), :]
+
+
+def rotate(values, signs, layout, other, steps, parts, signed_out=False, after=()):
     half, units, columns = layout.half, layout.units, layout.columns
-    span, batch = layout.span(steps), layout.batch(steps)
+    batch = layout.batch(steps)
+    runs = len(layout.runs(steps, 0))
     entries = len(steps) * layout.groups * layout.portion
-    passed = [jax.ShapeDtypeStruct(array.shape, array.dtype) for array in later]
-    outs = []
-    for step in steps:
-        cuts = HALVES if step in cut else 1
-        outs += [jax.ShapeDtypeStruct((units, ROT // cuts, columns), jnp.bfloat16)] * cuts
+    outs = [jax.ShapeDtypeStruct((units, len(wanted) * QGROUP, columns), jnp.bfloat16) for wanted in parts]
     if signed_out:
         outs.append(jax.ShapeDtypeStruct((layout.rows, LANES), jnp.int32))
-    extra = len(after) + 2 * len(later)
     return list(
         pl.pallas_call(
-            functools.partial(rotate_kernel, layout, other, steps, cut, signed_out, extra),
-            in_specs=[pl.BlockSpec(memory_space=pltpu.HBM)] * 2
-            + [pl.BlockSpec(memory_space=pl.ANY)] * (len(after) + len(later)),
-            out_specs=[pl.BlockSpec(memory_space=pl.ANY)] * len(later)
-            + [pl.BlockSpec(memory_space=pltpu.VMEM)] * len(outs),
-            out_shape=passed + outs,
-            input_output_aliases={2 + len(after) + index: index for index in range(len(later))},
+            functools.partial(rotate_kernel, layout, other, steps, parts, signed_out, len(after)),
+            in_specs=[pl.BlockSpec(memory_space=pltpu.HBM)] * 2 + [pl.BlockSpec(memory_space=pl.ANY)] * len(after),
+            out_specs=[pl.BlockSpec(memory_space=pltpu.VMEM)] * len(outs),
+            out_shape=outs,
             scratch_shapes=[
-                pltpu.VMEM((units, layout.together, 1, span * layout.portion), jnp.bfloat16),
-                pltpu.VMEM((units, layout.together, span * layout.rows, LANES), jnp.int32),
+                pltpu.VMEM((units, layout.together, 1, half * layout.portion), jnp.bfloat16),
+                pltpu.VMEM((units, layout.together, half * layout.rows, LANES), jnp.int32),
                 pltpu.VMEM((batch * len(steps), layout.together * layout.rows, LANES), jnp.float32),
                 pltpu.VMEM((ROT, ROT), jnp.bfloat16),
-                pltpu.SemaphoreType.DMA((units, layout.together)),
-                pltpu.SemaphoreType.DMA((units, layout.together)),
+                pltpu.SemaphoreType.DMA((units, layout.together, runs)),
+                pltpu.SemaphoreType.DMA((units, layout.together, runs)),
             ],
             compiler_params=pltpu.CompilerParams(vmem_limit_bytes=VMEM_LIMIT),
             cost_estimate=pl.CostEstimate(flops=2 * entries * ROT, bytes_accessed=10 * entries, transcendentals=0),
             name="rotate_code",
-        )(values, signs, *after, *later)
+        )(values, signs, *after)
     )
 
 
@@ -199,23 +198,20 @@
     refs[-1][...] = add_all(arrays)
 
 
-def far_sum(parts, layout, part, later, after=()):
+def far_sum(parts, layout, part, after=()):
     size = QGROUP * layout.units * layout.columns
-    *later, total = pl.pallas_call(
+    return pl.pallas_call(
         functools.partial(far_sum_kernel, part, len(parts)),
         in_specs=[pl.BlockSpec(memory_space=pltpu.VMEM)] * len(parts)
-        + [pl.BlockSpec(memory_space=pl.ANY)] * (len(later) + len(after)),
-        out_specs=[pl.BlockSpec(memory_space=pl.ANY)] * len(later) + [pl.BlockSpec(memory_space=pltpu.VMEM)],
-        out_shape=[jax.ShapeDtypeStruct(array.shape, array.dtype) for array in later]
-        + [jax.ShapeDtypeStruct(layout.shape(), jnp.float32)],
-        input_output_aliases={len(parts) + index: index for index in range(len(later))},
+        + [pl.BlockSpec(memory_space=pl.ANY)] * len(after),
+        out_specs=pl.BlockSpec(memory_space=pltpu.VMEM),
+        out_shape=jax.ShapeDtypeStruct(layout.shape(), jnp.float32),
         compiler_params=pltpu.CompilerParams(vmem_limit_bytes=SUM_VMEM_LIMIT),
         cost_estimate=pl.CostEstimate(
             flops=2 * len(parts) * size, bytes_accessed=(2 * len(parts) + 4) * size, transcendentals=0
         ),
         name="far_sum",
-    )(*parts, *later, *after)
-    return total, later
+    )(*parts, *after)
 
 
 def group_sum_kernel(layout, *refs):
@@ -311,24 +307,26 @@
     counterparts = [(member, (member + half) % members) for member in range(members)]
     slow = half // 2
     others = [step for step in range(half - 1, 0, -1) if step != slow]
-    order = others[:1] + [slow] + others[1:] + [0]
-    last = order[-2]
-    outs = rotate(values, sign_rows, layout, True, order, order[:-1])
-    far = {step: [outs.pop(0), outs.pop(0)] for step in order[:-1]}
-    far[0] = outs
-    for part in range(HALVES):
-        for step in order[:-1]:
-            far[step][part] = swap(far[step][part], step)
-    (part,) = rotate(values, sign_rows, layout, False, [slow], after=far[0])
-    first, (part,) = far_sum([far[step][0] for step in order], layout, 0, [part])
+    order = others[:1] + [slow] + others[1:]
+    whole = tuple(range(HALVES))
+    far0 = rotate(values, sign_rows, layout, True, order, [(0,)] * len(order))
+    *far1, own = rotate(
+        values, sign_rows, layout, True, order + [0], [(1,)] * len(order) + [whole], after=far0
+    )
+    far0 = [swap(part, step) for step, part in zip(order, far0)] + [own]
+    early = far1
+    (near_slow,) = rotate(values, sign_rows, layout, False, [slow], [whole], after=early)
+    first = far_sum(far0, layout, 0, [near_slow])
     across = [lax.ppermute(first, "local", counterparts)]
-    near = {slow: swap(part, slow)}
-    second, _ = far_sum([far[step][-1] for step in order], layout, 1, [], [first, part])
+    far1 = [swap(part, step) for step, part in zip(order, far1)] + [own]
+    second = far_sum(far1, layout, 1, [first, near_slow])
     across.append(lax.ppermute(second, "local", counterparts))
-    *outs, own_signs = rotate(values, sign_rows, layout, False, others + [0], signed_out=True, after=[second])
-    for step, part in zip(others + [0], outs):
-        near[step] = swap(part, step) if step else part
-    reduced, rotated_max = finish(share(group_sum([near[step] for step in order], across, layout)), own_signs)
+    *outs, own_signs = rotate(
+        values, sign_rows, layout, False, others + [0], [whole] * (len(others) + 1), signed_out=True, after=[second]
+    )
+    near = {step: swap(part, step) if step else part for step, part in zip(others + [0], outs)}
+    near[slow] = swap(near_slow, slow)
+    reduced, rotated_max = finish(share(group_sum([near[step] for step in order + [0]], across, layout)), own_signs)
     return (reduced.reshape(-1), rotated_max.reshape(-1))
 
 

time: 49.7 us -> 52.4 us (1.054)
  Pallas kernels: 10.8 us -> 12.9 us
  waiting for transfers between devices: 16.8 us -> 18.7 us
  starting transfers between devices: 21.4 us -> 19.9 us
    ppermute x9, waiting for transfers between devices: 4.95 us -> 8.45 us  [swap(): return lax.ppermute(part, 'local', pairs)]
    ppermute x1, waiting for transfers between devices: 8.43 us -> 6.3 us  [shards(): across.append(lax.ppermute(second, 'local', counterparts))]
    pallas_call x3 -> x4, Pallas kernels: 9.2 us -> 11.3 us  [rotate(): pl.pallas_call(functools.partial(rotate_kernel, layout, other, steps, par...]
    ppermute x9, starting transfers between devices: 15.9 us -> 14.3 us  [swap(): return lax.ppermute(part, 'local', pairs)]
    ppermute x3, waiting for transfers between devices: 3.38 us -> 3.94 us  [share(): moved.append(lax.ppermute(parts[step], 'node', pairs))]
  transfers between devices with their start and end apart: 14 -> 14, of which waited for: 8 -> 5; matrix products, arithmetic and copies ran while one was open for 0% -> 0% of each run, Pallas kernels for 11% -> 17%
where the time goes in v18:
time: 52.4 us; the launch traced here: 52.2 us
  starting transfers between devices  19.9 us (38%)
  waiting for transfers between devices  18.7 us (36%)
  Pallas kernels  12.9 us (25%)
  between operations  0.71 us (1%)
    ppermute x9, starting transfers between devices, swap(): return lax.ppermute(part, 'local', pairs)  14.3 us
    pallas_call x4, Pallas kernels, rotate(): pl.pallas_call(functools.partial(rotate_kernel, layout, other, steps, par...  11.3 us
    ppermute x9, waiting for transfers between devices, swap(): return lax.ppermute(part, 'local', pairs)  8.45 us
    ppermute x1, waiting for transfers between devices, shards(): across.append(lax.ppermute(second, 'local', counterparts))  6.3 us
    ppermute x3, waiting for transfers between devices, share(): moved.append(lax.ppermute(parts[step], 'node', pairs))  3.94 us
    ppermute x1, starting transfers between devices, shards(): across = [lax.ppermute(first, 'local', counterparts)]  2.65 us
    ppermute x3, starting transfers between devices, share(): moved.append(lax.ppermute(parts[step], 'node', pairs))  1.92 us
  transfers between devices with their start and end apart: 14, of which 5 were waited for; matrix products, arithmetic and copies ran while one was open for 0% of the time, Pallas kernels for 17%

profile of v18, /device:TPU:0, one launch (start us, length us, event | category | flops | bytes accessed | tf_op | source)
XLA Modules:
  0.0 52.2 jit_solution(7813370464315201524)
XLA Ops:
  0.6 2.8 %rotate_code.4 = (bf16[4,128,128]{2,1,0:T(8,128)(2,1)S(1)}, bf16[4,128,128]{2,1,0:T(8,128)(2,1)S(1)}, bf16[4,128,128]{2,1,0:T(8,128)(2,1)S(1)}) custom-call(bf16[1,1048576]{1,0:T(2,128)(2,1)} %bitcast.4, s32[8192,128]{1,0:T(8,128)} %bitcast.8), custom_call_target="tpu_custom_call" | custom-call | flops 201326592 | bytes 3932160 | tf_op jit(solution)/shard_map/rotate_code/pallas_call | solution.py:166
  3.4 4.0 %collective-permute-start.3 = (bf16[4,128,128]{2,1,0:T(8,128)(2,1)S(1)}, bf16[4,128,128]{2,1,0:T(8,128)(2,1)S(1)}, u32[]{:S(2)}, u32[]{:S(2)}) collective-permute-start(bf16[4,128,128]{2,1,0:T(8,128)(2,1)S(1)} %get-tuple-element.19.refs_0_), channel_id=1, source_target_pairs={{0,3},{1,2},{2,1},{3,0},{4,7},{5,6},{6,5},{7,4},{8,11},{9,10},{10,... | collective-permute-start | bytes 393224 | tf_op jit(solution)/shard_map/ppermute | solution.py:297
  7.5 0.4 collective-permute-start.4
  7.9 0.2 collective-permute-start.5
  8.1 3.3 %rotate_code.5 = (bf16[4,128,128]{2,1,0:T(8,128)(2,1)S(1)}, bf16[4,128,128]{2,1,0:T(8,128)(2,1)S(1)}, bf16[4,128,128]{2,1,0:T(8,128)(2,1)S(1)}, bf16[4,256,128]{2,1,0:T(8,128)(2,1)S(1)}) custom-call(bf16[1,1048576]{1,0:T(2,128)(2,1)} %bitcast.5, s32[8192,128]{1,0:T(8,128)} %bitcast.9, bf16[4,128,128]{2,1,0:T(8,128)(2,1)S(1)} %get-tuple-element.19.refs_0_, ...), custom_call_target="tpu_custom_call" | custom-call | flops 268435456 | bytes 5242880 | tf_op jit(solution)/shard_map/rotate_code/pallas_call | solution.py:166
  11.4 2.9 %collective-permute-start = (bf16[4,128,128]{2,1,0:T(8,128)(2,1)S(1)}, bf16[4,128,128]{2,1,0:T(8,128)(2,1)S(1)}, u32[]{:S(2)}, u32[]{:S(2)}) collective-permute-start(bf16[4,128,128]{2,1,0:T(8,128)(2,1)S(1)} %get-tuple-element.22.refs_0_), channel_id=1, source_target_pairs={{0,3},{1,2},{2,1},{3,0},{4,7},{5,6},{6,5},{7,4},{8,11},{9,10},{10,... | collective-permute-start | bytes 393224 | tf_op jit(solution)/shard_map/ppermute | solution.py:297
  14.4 0.4 collective-permute-start.1
  14.8 0.0 collective-permute-done.3.refs_0_
  14.8 0.2 collective-permute-start.2
  15.0 2.0 %rotate_code.6.refs_4_.refs_5_ = bf16[4,256,128]{2,1,0:T(8,128)(2,1)S(1)} custom-call(bf16[1,1048576]{1,0:T(2,128)(2,1)} %bitcast.6, s32[8192,128]{1,0:T(8,128)} %bitcast.10, bf16[4,128,128]{2,1,0:T(8,128)(2,1)S(1)} %get-tuple-element.22.refs_0_, bf16[4,128,128]{2,1,0:T(8,128)(2,1)S(1)} %get-tuple-element.23.refs_1_, ...), custom_call_target="tpu_custom_call" | custom-call | flops 67108864 | bytes 1310720 | tf_op jit(solution)/shard_map/rotate_code/pallas_call | solution.py:166
  17.0 0.0 collective-permute-done.4.refs_1_
  17.0 2.0 %collective-permute-start.9 = (bf16[4,256,128]{2,1,0:T(8,128)(2,1)S(1)}, bf16[4,256,128]{2,1,0:T(8,128)(2,1)S(1)}, u32[]{:S(2)}, u32[]{:S(2)}) collective-permute-start(bf16[4,256,128]{2,1,0:T(8,128)(2,1)S(1)} %rotate_code.6.refs_4_.refs_5_), channel_id=1, source_target_pairs={{0,2},{1,3},{2,0},{3,1},{4,6},{5,7},{6,4},{7,5},{8,10},{9,11},{10,... | collective-permute-start | bytes 786440 | tf_op jit(solution)/shard_map/ppermute | solution.py:297
  19.0 0.0 collective-permute-done.5.refs_2_
  19.0 0.1 far_sum.2.refs_4_
  19.1 2.7 %collective-permute-start.6 = (f32[4,128,128]{2,1,0:T(8,128)S(1)}, f32[4,128,128]{2,1,0:T(8,128)S(1)}, u32[]{:S(2)}, u32[]{:S(2)}) collective-permute-start(f32[4,128,128]{2,1,0:T(8,128)S(1)} %far_sum.2.refs_4_), channel_id=1, source_target_pairs={{0,4},{1,5},{2,6},{3,7},{4,0},{5,1},{6,2},{7,3},{8,12},{9,13},{10,... | collective-permute-start | bytes 786440 | tf_op jit(solution)/shard_map/ppermute | solution.py:320
  21.7 0.0 collective-permute-done.refs_0_
  21.7 6.6 %collective-permute-done.1.refs_1_ = bf16[4,128,128]{2,1,0:T(8,128)(2,1)S(1)} collective-permute-done((bf16[4,128,128]{2,1,0:T(8,128)(2,1)S(1)}, bf16[4,128,128]{2,1,0:T(8,128)(2,1)S(1)}, u32[]{:S(2)}, u32[]{:S(2)}) %collective-permute-start.1) | collective-permute-done | bytes 131104 | tf_op jit(solution)/shard_map/ppermute | solution.py:297
  28.4 0.0 collective-permute-done.2.refs_2_
  28.4 0.1 far_sum.3.refs_0_
  28.4 1.0 %collective-permute-start.7 = (f32[4,128,128]{2,1,0:T(8,128)S(1)}, f32[4,128,128]{2,1,0:T(8,128)S(1)}, u32[]{:S(2)}, u32[]{:S(2)}) collective-permute-start(f32[4,128,128]{2,1,0:T(8,128)S(1)} %far_sum.3.refs_0_), channel_id=1, source_target_pairs={{0,4},{1,5},{2,6},{3,7},{4,0},{5,1},{6,2},{7,3},{8,12},{9,13},{10,... | collective-permute-start | bytes 786440 | tf_op jit(solution)/shard_map/ppermute | solution.py:323
  29.4 3.2 %rotate_code.7 = (bf16[4,256,128]{2,1,0:T(8,128)(2,1)S(1)}, bf16[4,256,128]{2,1,0:T(8,128)(2,1)S(1)}, bf16[4,256,128]{2,1,0:T(8,128)(2,1)S(1)}, s32[256,128]{1,0:T(8,128)S(1)}) custom-call(bf16[1,1048576]{1,0:T(2,128)(2,1)} %bitcast.7, s32[8192,128]{1,0:T(8,128)} %bitcast.11, f32[4,128,128]{2,1,0:T(8,128)S(1)} %far_sum.3.refs_0_), custom_call_target="tpu_custom_call" | custom-call | flops 201326592 | bytes 3932160 | tf_op jit(solution)/shard_map/rotate_code/pallas_call | solution.py:166
  32.7 0.1 collective-permute-start.8
  32.7 4.1 %collective-permute-start.10 = (bf16[4,256,128]{2,1,0:T(8,128)(2,1)S(1)}, bf16[4,256,128]{2,1,0:T(8,128)(2,1)S(1)}, u32[]{:S(2)}, u32[]{:S(2)}) collective-permute-start(bf16[4,256,128]{2,1,0:T(8,128)(2,1)S(1)} %get-tuple-element.28), channel_id=1, source_target_pairs={{0,1},{1,0},{2,3},{3,2},{4,5},{5,4},{6,7},{7,6},{8,9},{9,8},{10,11... | collective-permute-start | bytes 786440 | tf_op jit(solution)/shard_map/ppermute | solution.py:297
  36.8 0.0 collective-permute-done.9.refs_3_
  36.8 6.3 %collective-permute-done.7.refs_1_ = f32[4,128,128]{2,1,0:T(8,128)S(1)} collective-permute-done((f32[4,128,128]{2,1,0:T(8,128)S(1)}, f32[4,128,128]{2,1,0:T(8,128)S(1)}, u32[]{:S(2)}, u32[]{:S(2)}) %collective-permute-start.7) | collective-permute-done | bytes 262176 | tf_op jit(solution)/shard_map/ppermute | solution.py:323
  43.1 0.0 collective-permute-done.6.refs_0_
  43.1 1.8 %collective-permute-done.8.refs_2_ = bf16[4,256,128]{2,1,0:T(8,128)(2,1)S(1)} collective-permute-done((bf16[4,256,128]{2,1,0:T(8,128)(2,1)S(1)}, bf16[4,256,128]{2,1,0:T(8,128)(2,1)S(1)}, u32[]{:S(2)}, u32[]{:S(2)}) %collective-permute-start.8) | collective-permute-done | bytes 262176 | tf_op jit(solution)/shard_map/ppermute | solution.py:297
  44.9 0.0 collective-permute-done.10.refs_4_
  44.9 0.5 group_sum_code.1
  45.4 0.1 collective-permute-start.11
  45.5 1.6 %collective-permute-start.12 = (bf16[2,128,128]{2,1,0:T(8,128)(2,1)S(1)}, bf16[2,128,128]{2,1,0:T(8,128)(2,1)S(1)}, u32[]{:S(2)}, u32[]{:S(2)}) collective-permute-start(bf16[2,128,128]{2,1,0:T(8,128)(2,1)S(1)} %get-tuple-element.31), channel_id=1, source_target_pairs={{0,16},{8,24},{16,0},{24,8},{1,17},{9,25},{17,1},{25,9},{2,18},{10... | collective-permute-start | bytes 196616 | tf_op jit(solution)/shard_map/ppermute | solution.py:303
  47.0 0.3 collective-permute-start.13
  47.3 2.5 %collective-permute-done.11.refs_0_ = bf16[2,128,128]{2,1,0:T(8,128)(2,1)S(1)} collective-permute-done((bf16[2,128,128]{2,1,0:T(8,128)(2,1)S(1)}, bf16[2,128,128]{2,1,0:T(8,128)(2,1)S(1)}, u32[]{:S(2)}, u32[]{:S(2)}) %collective-permute-start.11) | collective-permute-done | bytes 65568 | tf_op jit(solution)/shard_map/ppermute | solution.py:303
  49.8 1.5 %collective-permute-done.12.refs_1_ = bf16[2,128,128]{2,1,0:T(8,128)(2,1)S(1)} collective-permute-done((bf16[2,128,128]{2,1,0:T(8,128)(2,1)S(1)}, bf16[2,128,128]{2,1,0:T(8,128)(2,1)S(1)}, u32[]{:S(2)}, u32[]{:S(2)}) %collective-permute-start.12) | collective-permute-done | bytes 65568 | tf_op jit(solution)/shard_map/ppermute | solution.py:303
  51.3 0.0 collective-permute-done.13.refs_2_
  51.3 0.9 %sum_unrotate.1 = (f32[256,128]{1,0:T(8,128)}, f32[1,256]{1,0:T(1,128)}) custom-call(s32[256,128]{1,0:T(8,128)S(1)} %get-tuple-element.26.sign_ref, bf16[2,128,128]{2,1,0:T(8,128)(2,1)S(1)} %collective-permute-done.11.refs_0_, bf16[2,128,128]{2,1,0:T(8,128)(2,1)S(1)} %collective-permute-done.12.refs_1_, ...), custom_call_target="tpu_custom_call" | custom-call | tf_op jit(solution)/shard_map/sum_unrotate/pallas_call | solution.py:274
Async XLA Ops:
  3.4 11.4 %collective-permute-start.3 = (bf16[4,128,128]{2,1,0:T(8,128)(2,1)S(1)}, bf16[4,128,128]{2,1,0:T(8,128)(2,1)S(1)}, u32[]{:S(2)}, u32[]{:S(2)}) collective-permute-start(bf16[4,128,128]{2,1,0:T(8,128)(2,1)S(1)} %get-tuple-element.19.refs_0_), channel_id=1, source_target_pairs={{0,3},{1,2},{2,1},{3,0},{4,7},{5,6},{6,5},{7,4},{8,11},{9,10},{10,... | collective-permute-start | bytes 393224 | tf_op jit(solution)/shard_map/ppermute | solution.py:297
  7.5 9.6 %collective-permute-start.4 = (bf16[4,128,128]{2,1,0:T(8,128)(2,1)S(1)}, bf16[4,128,128]{2,1,0:T(8,128)(2,1)S(1)}, u32[]{:S(2)}, u32[]{:S(2)}) collective-permute-start(bf16[4,128,128]{2,1,0:T(8,128)(2,1)S(1)} %get-tuple-element.20.refs_1_), channel_id=1, source_target_pairs={{0,2},{1,3},{2,0},{3,1},{4,6},{5,7},{6,4},{7,5},{8,10},{9,11},{10,... | collective-permute-start | bytes 393224 | tf_op jit(solution)/shard_map/ppermute | solution.py:297
  7.9 11.1 %collective-permute-start.5 = (bf16[4,128,128]{2,1,0:T(8,128)(2,1)S(1)}, bf16[4,128,128]{2,1,0:T(8,128)(2,1)S(1)}, u32[]{:S(2)}, u32[]{:S(2)}) collective-permute-start(bf16[4,128,128]{2,1,0:T(8,128)(2,1)S(1)} %get-tuple-element.21.refs_2_), channel_id=1, source_target_pairs={{0,1},{1,0},{2,3},{3,2},{4,5},{5,4},{6,7},{7,6},{8,9},{9,8},{10,11... | collective-permute-start | bytes 393224 | tf_op jit(solution)/shard_map/ppermute | solution.py:297
  11.4 10.3 %collective-permute-start = (bf16[4,128,128]{2,1,0:T(8,128)(2,1)S(1)}, bf16[4,128,128]{2,1,0:T(8,128)(2,1)S(1)}, u32[]{:S(2)}, u32[]{:S(2)}) collective-permute-start(bf16[4,128,128]{2,1,0:T(8,128)(2,1)S(1)} %get-tuple-element.22.refs_0_), channel_id=1, source_target_pairs={{0,3},{1,2},{2,1},{3,0},{4,7},{5,6},{6,5},{7,4},{8,11},{9,10},{10,... | collective-permute-start | bytes 393224 | tf_op jit(solution)/shard_map/ppermute | solution.py:297
  14.4 14.0 %collective-permute-start.1 = (bf16[4,128,128]{2,1,0:T(8,128)(2,1)S(1)}, bf16[4,128,128]{2,1,0:T(8,128)(2,1)S(1)}, u32[]{:S(2)}, u32[]{:S(2)}) collective-permute-start(bf16[4,128,128]{2,1,0:T(8,128)(2,1)S(1)} %get-tuple-element.23.refs_1_), channel_id=1, source_target_pairs={{0,2},{1,3},{2,0},{3,1},{4,6},{5,7},{6,4},{7,5},{8,10},{9,11},{10,... | collective-permute-start | bytes 393224 | tf_op jit(solution)/shard_map/ppermute | solution.py:297
  14.8 13.6 %collective-permute-start.2 = (bf16[4,128,128]{2,1,0:T(8,128)(2,1)S(1)}, bf16[4,128,128]{2,1,0:T(8,128)(2,1)S(1)}, u32[]{:S(2)}, u32[]{:S(2)}) collective-permute-start(bf16[4,128,128]{2,1,0:T(8,128)(2,1)S(1)} %get-tuple-element.24.refs_2_), channel_id=1, source_target_pairs={{0,1},{1,0},{2,3},{3,2},{4,5},{5,4},{6,7},{7,6},{8,9},{9,8},{10,11... | collective-permute-start | bytes 393224 | tf_op jit(solution)/shard_map/ppermute | solution.py:297
  17.0 19.8 %collective-permute-start.9 = (bf16[4,256,128]{2,1,0:T(8,128)(2,1)S(1)}, bf16[4,256,128]{2,1,0:T(8,128)(2,1)S(1)}, u32[]{:S(2)}, u32[]{:S(2)}) collective-permute-start(bf16[4,256,128]{2,1,0:T(8,128)(2,1)S(1)} %rotate_code.6.refs_4_.refs_5_), channel_id=1, source_target_pairs={{0,2},{1,3},{2,0},{3,1},{4,6},{5,7},{6,4},{7,5},{8,10},{9,11},{10,... | collective-permute-start | bytes 786440 | tf_op jit(solution)/shard_map/ppermute | solution.py:297
  19.1 24.1 %collective-permute-start.6 = (f32[4,128,128]{2,1,0:T(8,128)S(1)}, f32[4,128,128]{2,1,0:T(8,128)S(1)}, u32[]{:S(2)}, u32[]{:S(2)}) collective-permute-start(f32[4,128,128]{2,1,0:T(8,128)S(1)} %far_sum.2.refs_4_), channel_id=1, source_target_pairs={{0,4},{1,5},{2,6},{3,7},{4,0},{5,1},{6,2},{7,3},{8,12},{9,13},{10,... | collective-permute-start | bytes 786440 | tf_op jit(solution)/shard_map/ppermute | solution.py:320
  28.4 14.7 %collective-permute-start.7 = (f32[4,128,128]{2,1,0:T(8,128)S(1)}, f32[4,128,128]{2,1,0:T(8,128)S(1)}, u32[]{:S(2)}, u32[]{:S(2)}) collective-permute-start(f32[4,128,128]{2,1,0:T(8,128)S(1)} %far_sum.3.refs_0_), channel_id=1, source_target_pairs={{0,4},{1,5},{2,6},{3,7},{4,0},{5,1},{6,2},{7,3},{8,12},{9,13},{10,... | collective-permute-start | bytes 786440 | tf_op jit(solution)/shard_map/ppermute | solution.py:323
  32.7 12.2 %collective-permute-start.8 = (bf16[4,256,128]{2,1,0:T(8,128)(2,1)S(1)}, bf16[4,256,128]{2,1,0:T(8,128)(2,1)S(1)}, u32[]{:S(2)}, u32[]{:S(2)}) collective-permute-start(bf16[4,256,128]{2,1,0:T(8,128)(2,1)S(1)} %get-tuple-element.27), channel_id=1, source_target_pairs={{0,3},{1,2},{2,1},{3,0},{4,7},{5,6},{6,5},{7,4},{8,11},{9,10},{10,... | collective-permute-start | bytes 786440 | tf_op jit(solution)/shard_map/ppermute | solution.py:297
  32.7 12.2 %collective-permute-start.10 = (bf16[4,256,128]{2,1,0:T(8,128)(2,1)S(1)}, bf16[4,256,128]{2,1,0:T(8,128)(2,1)S(1)}, u32[]{:S(2)}, u32[]{:S(2)}) collective-permute-start(bf16[4,256,128]{2,1,0:T(8,128)(2,1)S(1)} %get-tuple-element.28), channel_id=1, source_target_pairs={{0,1},{1,0},{2,3},{3,2},{4,5},{5,4},{6,7},{7,6},{8,9},{9,8},{10,11... | collective-permute-start | bytes 786440 | tf_op jit(solution)/shard_map/ppermute | solution.py:297
  45.4 4.4 %collective-permute-start.11 = (bf16[2,128,128]{2,1,0:T(8,128)(2,1)S(1)}, bf16[2,128,128]{2,1,0:T(8,128)(2,1)S(1)}, u32[]{:S(2)}, u32[]{:S(2)}) collective-permute-start(bf16[2,128,128]{2,1,0:T(8,128)(2,1)S(1)} %get-tuple-element.30), channel_id=1, source_target_pairs={{0,24},{8,16},{16,8},{24,0},{1,25},{9,17},{17,9},{25,1},{2,26},{10... | collective-permute-start | bytes 196616 | tf_op jit(solution)/shard_map/ppermute | solution.py:303
  45.5 5.8 %collective-permute-start.12 = (bf16[2,128,128]{2,1,0:T(8,128)(2,1)S(1)}, bf16[2,128,128]{2,1,0:T(8,128)(2,1)S(1)}, u32[]{:S(2)}, u32[]{:S(2)}) collective-permute-start(bf16[2,128,128]{2,1,0:T(8,128)(2,1)S(1)} %get-tuple-element.31), channel_id=1, source_target_pairs={{0,16},{8,24},{16,0},{24,8},{1,17},{9,25},{17,1},{25,9},{2,18},{10... | collective-permute-start | bytes 196616 | tf_op jit(solution)/shard_map/ppermute | solution.py:303
  47.0 4.2 %collective-permute-start.13 = (bf16[2,128,128]{2,1,0:T(8,128)(2,1)S(1)}, bf16[2,128,128]{2,1,0:T(8,128)(2,1)S(1)}, u32[]{:S(2)}, u32[]{:S(2)}) collective-permute-start(bf16[2,128,128]{2,1,0:T(8,128)(2,1)S(1)} %get-tuple-element.32), channel_id=1, source_target_pairs={{0,8},{8,0},{16,24},{24,16},{1,9},{9,1},{17,25},{25,17},{2,10},{10... | collective-permute-start | bytes 196616 | tf_op jit(solution)/shard_map/ppermute | solution.py:303

commit v19 on v18

--- a/solution.py
+++ b/solution.py
@@ -315,11 +315,11 @@
     )
     far0 = [swap(part, step) for step, part in zip(order, far0)] + [own]
     early = far1
-    (near_slow,) = rotate(values, sign_rows, layout, False, [slow], [whole], after=early)
-    first = far_sum(far0, layout, 0, [near_slow])
+    first = far_sum(far0, layout, 0, [*early])
     across = [lax.ppermute(first, "local", counterparts)]
+    (near_slow,) = rotate(values, sign_rows, layout, False, [slow], [whole], after=[first])
     far1 = [swap(part, step) for step, part in zip(order, far1)] + [own]
-    second = far_sum(far1, layout, 1, [first, near_slow])
+    second = far_sum(far1, layout, 1, [near_slow])
     across.append(lax.ppermute(second, "local", counterparts))
     *outs, own_signs = rotate(
         values, sign_rows, layout, False, others + [0], [whole] * (len(others) + 1), signed_out=True, after=[second]

time: 52.4 us -> 50.5 us (0.964)
  starting transfers between devices: 19.9 us -> 18.3 us
    ppermute x1, waiting for transfers between devices: 6.3 us -> 4.9 us  [shards(): across.append(lax.ppermute(second, 'local', counterparts))]
    ppermute x9, waiting for transfers between devices: 8.45 us -> 9.7 us  [swap(): return lax.ppermute(part, 'local', pairs)]
    ppermute x9, starting transfers between devices: 14.3 us -> 13.3 us  [swap(): return lax.ppermute(part, 'local', pairs)]
    ppermute x1, starting transfers between devices: 1 us -> 0.07 us  [shards(): across.append(lax.ppermute(second, 'local', counterparts))]
  transfers between devices with their start and end apart: 14 -> 14, of which waited for: 5 -> 6; matrix products, arithmetic and copies ran while one was open for 0% -> 0% of each run, Pallas kernels for 17% -> 17%
where the time goes in v19:
time: 50.5 us; the launch traced here: 50.4 us
  waiting for transfers between devices  18.5 us (37%)
  starting transfers between devices  18.3 us (36%)
  Pallas kernels  12.9 us (26%)
  between operations  0.71 us (1%)
    ppermute x9, starting transfers between devices, swap(): return lax.ppermute(part, 'local', pairs)  13.3 us
    pallas_call x4, Pallas kernels, rotate(): pl.pallas_call(functools.partial(rotate_kernel, layout, other, steps, par...  11.3 us
    ppermute x9, waiting for transfers between devices, swap(): return lax.ppermute(part, 'local', pairs)  9.7 us
    ppermute x1, waiting for transfers between devices, shards(): across.append(lax.ppermute(second, 'local', counterparts))  4.9 us
    ppermute x3, waiting for transfers between devices, share(): moved.append(lax.ppermute(parts[step], 'node', pairs))  3.89 us
    ppermute x1, starting transfers between devices, shards(): across = [lax.ppermute(first, 'local', counterparts)]  2.96 us
    ppermute x3, starting transfers between devices, share(): moved.append(lax.ppermute(parts[step], 'node', pairs))  1.92 us
  transfers between devices with their start and end apart: 14, of which 6 were waited for; matrix products, arithmetic and copies ran while one was open for 0% of the time, Pallas kernels for 17%

profile of v19, /device:TPU:0, one launch (start us, length us, event | category | flops | bytes accessed | tf_op | source)
XLA Modules:
  0.0 50.4 jit_solution(15758763546212332894)
XLA Ops:
  0.6 2.8 %rotate_code.4 = (bf16[4,128,128]{2,1,0:T(8,128)(2,1)S(1)}, bf16[4,128,128]{2,1,0:T(8,128)(2,1)S(1)}, bf16[4,128,128]{2,1,0:T(8,128)(2,1)S(1)}) custom-call(bf16[1,1048576]{1,0:T(2,128)(2,1)} %bitcast.4, s32[8192,128]{1,0:T(8,128)} %bitcast.8), custom_call_target="tpu_custom_call" | custom-call | flops 201326592 | bytes 3932160 | tf_op jit(solution)/shard_map/rotate_code/pallas_call | solution.py:166
  3.4 4.0 %collective-permute-start.3 = (bf16[4,128,128]{2,1,0:T(8,128)(2,1)S(1)}, bf16[4,128,128]{2,1,0:T(8,128)(2,1)S(1)}, u32[]{:S(2)}, u32[]{:S(2)}) collective-permute-start(bf16[4,128,128]{2,1,0:T(8,128)(2,1)S(1)} %get-tuple-element.19.refs_0_), channel_id=1, source_target_pairs={{0,3},{1,2},{2,1},{3,0},{4,7},{5,6},{6,5},{7,4},{8,11},{9,10},{10,... | collective-permute-start | bytes 393224 | tf_op jit(solution)/shard_map/ppermute | solution.py:297
  7.5 0.4 collective-permute-start.4
  7.9 0.2 collective-permute-start.5
  8.1 3.3 %rotate_code.5 = (bf16[4,128,128]{2,1,0:T(8,128)(2,1)S(1)}, bf16[4,128,128]{2,1,0:T(8,128)(2,1)S(1)}, bf16[4,128,128]{2,1,0:T(8,128)(2,1)S(1)}, bf16[4,256,128]{2,1,0:T(8,128)(2,1)S(1)}) custom-call(bf16[1,1048576]{1,0:T(2,128)(2,1)} %bitcast.5, s32[8192,128]{1,0:T(8,128)} %bitcast.9, bf16[4,128,128]{2,1,0:T(8,128)(2,1)S(1)} %get-tuple-element.19.refs_0_, ...), custom_call_target="tpu_custom_call" | custom-call | flops 268435456 | bytes 5242880 | tf_op jit(solution)/shard_map/rotate_code/pallas_call | solution.py:166
  11.4 2.9 %collective-permute-start = (bf16[4,128,128]{2,1,0:T(8,128)(2,1)S(1)}, bf16[4,128,128]{2,1,0:T(8,128)(2,1)S(1)}, u32[]{:S(2)}, u32[]{:S(2)}) collective-permute-start(bf16[4,128,128]{2,1,0:T(8,128)(2,1)S(1)} %get-tuple-element.22.refs_4_), channel_id=1, source_target_pairs={{0,3},{1,2},{2,1},{3,0},{4,7},{5,6},{6,5},{7,4},{8,11},{9,10},{10,... | collective-permute-start | bytes 393224 | tf_op jit(solution)/shard_map/ppermute | solution.py:297
  14.4 0.4 collective-permute-start.1
  14.8 0.0 collective-permute-done.3.refs_0_
  14.8 0.2 collective-permute-start.2
  15.0 0.0 collective-permute-done.4.refs_1_
  15.0 0.0 collective-permute-done.5.refs_2_
  15.0 0.1 far_sum.2.refs_0_
  15.1 3.0 %collective-permute-start.6 = (f32[4,128,128]{2,1,0:T(8,128)S(1)}, f32[4,128,128]{2,1,0:T(8,128)S(1)}, u32[]{:S(2)}, u32[]{:S(2)}) collective-permute-start(f32[4,128,128]{2,1,0:T(8,128)S(1)} %far_sum.2.refs_0_), channel_id=1, source_target_pairs={{0,4},{1,5},{2,6},{3,7},{4,0},{5,1},{6,2},{7,3},{8,12},{9,13},{10,... | collective-permute-start | bytes 786440 | tf_op jit(solution)/shard_map/ppermute | solution.py:319
  18.0 2.0 %rotate_code.6.refs_4_ = bf16[4,256,128]{2,1,0:T(8,128)(2,1)S(1)} custom-call(bf16[1,1048576]{1,0:T(2,128)(2,1)} %bitcast.6, s32[8192,128]{1,0:T(8,128)} %bitcast.10, f32[4,128,128]{2,1,0:T(8,128)S(1)} %far_sum.2.refs_0_), custom_call_target="tpu_custom_call" | custom-call | flops 67108864 | bytes 1310720 | tf_op jit(solution)/shard_map/rotate_code/pallas_call | solution.py:166
  20.1 1.6 %collective-permute-start.9 = (bf16[4,256,128]{2,1,0:T(8,128)(2,1)S(1)}, bf16[4,256,128]{2,1,0:T(8,128)(2,1)S(1)}, u32[]{:S(2)}, u32[]{:S(2)}) collective-permute-start(bf16[4,256,128]{2,1,0:T(8,128)(2,1)S(1)} %rotate_code.6.refs_4_), channel_id=1, source_target_pairs={{0,2},{1,3},{2,0},{3,1},{4,6},{5,7},{6,4},{7,5},{8,10},{9,11},{10,... | collective-permute-start | bytes 786440 | tf_op jit(solution)/shard_map/ppermute | solution.py:297
  21.7 0.0 collective-permute-done.refs_0_
  21.7 6.6 %collective-permute-done.1.refs_1_ = bf16[4,128,128]{2,1,0:T(8,128)(2,1)S(1)} collective-permute-done((bf16[4,128,128]{2,1,0:T(8,128)(2,1)S(1)}, bf16[4,128,128]{2,1,0:T(8,128)(2,1)S(1)}, u32[]{:S(2)}, u32[]{:S(2)}) %collective-permute-start.1) | collective-permute-done | bytes 131104 | tf_op jit(solution)/shard_map/ppermute | solution.py:297
  28.3 0.0 collective-permute-done.2.refs_2_
  28.3 0.1 far_sum.3.refs_0_
  28.4 0.1 collective-permute-start.7
  28.5 3.2 %rotate_code.7 = (bf16[4,256,128]{2,1,0:T(8,128)(2,1)S(1)}, bf16[4,256,128]{2,1,0:T(8,128)(2,1)S(1)}, bf16[4,256,128]{2,1,0:T(8,128)(2,1)S(1)}, s32[256,128]{1,0:T(8,128)S(1)}) custom-call(bf16[1,1048576]{1,0:T(2,128)(2,1)} %bitcast.7, s32[8192,128]{1,0:T(8,128)} %bitcast.11, f32[4,128,128]{2,1,0:T(8,128)S(1)} %far_sum.3.refs_0_), custom_call_target="tpu_custom_call" | custom-call | flops 201326592 | bytes 3932160 | tf_op jit(solution)/shard_map/rotate_code/pallas_call | solution.py:166
  31.7 0.1 collective-permute-start.8
  31.8 3.4 %collective-permute-start.10 = (bf16[4,256,128]{2,1,0:T(8,128)(2,1)S(1)}, bf16[4,256,128]{2,1,0:T(8,128)(2,1)S(1)}, u32[]{:S(2)}, u32[]{:S(2)}) collective-permute-start(bf16[4,256,128]{2,1,0:T(8,128)(2,1)S(1)} %get-tuple-element.28), channel_id=1, source_target_pairs={{0,1},{1,0},{2,3},{3,2},{4,5},{5,4},{6,7},{7,6},{8,9},{9,8},{10,11... | collective-permute-start | bytes 786440 | tf_op jit(solution)/shard_map/ppermute | solution.py:297
  35.1 4.9 %collective-permute-done.7.refs_1_ = f32[4,128,128]{2,1,0:T(8,128)S(1)} collective-permute-done((f32[4,128,128]{2,1,0:T(8,128)S(1)}, f32[4,128,128]{2,1,0:T(8,128)S(1)}, u32[]{:S(2)}, u32[]{:S(2)}) %collective-permute-start.7) | collective-permute-done | bytes 262176 | tf_op jit(solution)/shard_map/ppermute | solution.py:323
  40.0 0.0 collective-permute-done.9.refs_3_
  40.0 0.0 collective-permute-done.6.refs_0_
  40.0 2.4 %collective-permute-done.8.refs_2_ = bf16[4,256,128]{2,1,0:T(8,128)(2,1)S(1)} collective-permute-done((bf16[4,256,128]{2,1,0:T(8,128)(2,1)S(1)}, bf16[4,256,128]{2,1,0:T(8,128)(2,1)S(1)}, u32[]{:S(2)}, u32[]{:S(2)}) %collective-permute-start.8) | collective-permute-done | bytes 262176 | tf_op jit(solution)/shard_map/ppermute | solution.py:297
  42.4 0.7 %collective-permute-done.10.refs_4_ = bf16[4,256,128]{2,1,0:T(8,128)(2,1)S(1)} collective-permute-done((bf16[4,256,128]{2,1,0:T(8,128)(2,1)S(1)}, bf16[4,256,128]{2,1,0:T(8,128)(2,1)S(1)}, u32[]{:S(2)}, u32[]{:S(2)}) %collective-permute-start.10) | collective-permute-done | bytes 262176 | tf_op jit(solution)/shard_map/ppermute | solution.py:297
  43.1 0.5 group_sum_code.1
  43.6 0.1 collective-permute-start.11
  43.7 1.8 %collective-permute-start.12 = (bf16[2,128,128]{2,1,0:T(8,128)(2,1)S(1)}, bf16[2,128,128]{2,1,0:T(8,128)(2,1)S(1)}, u32[]{:S(2)}, u32[]{:S(2)}) collective-permute-start(bf16[2,128,128]{2,1,0:T(8,128)(2,1)S(1)} %get-tuple-element.31), channel_id=1, source_target_pairs={{0,16},{8,24},{16,0},{24,8},{1,17},{9,25},{17,1},{25,9},{2,18},{10... | collective-permute-start | bytes 196616 | tf_op jit(solution)/shard_map/ppermute | solution.py:303
  45.5 0.1 collective-permute-start.13
  45.5 2.3 %collective-permute-done.11.refs_0_ = bf16[2,128,128]{2,1,0:T(8,128)(2,1)S(1)} collective-permute-done((bf16[2,128,128]{2,1,0:T(8,128)(2,1)S(1)}, bf16[2,128,128]{2,1,0:T(8,128)(2,1)S(1)}, u32[]{:S(2)}, u32[]{:S(2)}) %collective-permute-start.11) | collective-permute-done | bytes 65568 | tf_op jit(solution)/shard_map/ppermute | solution.py:303
  47.8 1.6 %collective-permute-done.12.refs_1_ = bf16[2,128,128]{2,1,0:T(8,128)(2,1)S(1)} collective-permute-done((bf16[2,128,128]{2,1,0:T(8,128)(2,1)S(1)}, bf16[2,128,128]{2,1,0:T(8,128)(2,1)S(1)}, u32[]{:S(2)}, u32[]{:S(2)}) %collective-permute-start.12) | collective-permute-done | bytes 65568 | tf_op jit(solution)/shard_map/ppermute | solution.py:303
  49.4 0.0 collective-permute-done.13.refs_2_
  49.4 0.9 %sum_unrotate.1 = (f32[256,128]{1,0:T(8,128)}, f32[1,256]{1,0:T(1,128)}) custom-call(s32[256,128]{1,0:T(8,128)S(1)} %get-tuple-element.26.sign_ref, bf16[2,128,128]{2,1,0:T(8,128)(2,1)S(1)} %collective-permute-done.11.refs_0_, bf16[2,128,128]{2,1,0:T(8,128)(2,1)S(1)} %collective-permute-done.12.refs_1_, ...), custom_call_target="tpu_custom_call" | custom-call | tf_op jit(solution)/shard_map/sum_unrotate/pallas_call | solution.py:274
Async XLA Ops:
  3.4 11.4 %collective-permute-start.3 = (bf16[4,128,128]{2,1,0:T(8,128)(2,1)S(1)}, bf16[4,128,128]{2,1,0:T(8,128)(2,1)S(1)}, u32[]{:S(2)}, u32[]{:S(2)}) collective-permute-start(bf16[4,128,128]{2,1,0:T(8,128)(2,1)S(1)} %get-tuple-element.19.refs_0_), channel_id=1, source_target_pairs={{0,3},{1,2},{2,1},{3,0},{4,7},{5,6},{6,5},{7,4},{8,11},{9,10},{10,... | collective-permute-start | bytes 393224 | tf_op jit(solution)/shard_map/ppermute | solution.py:297
  7.5 7.5 %collective-permute-start.4 = (bf16[4,128,128]{2,1,0:T(8,128)(2,1)S(1)}, bf16[4,128,128]{2,1,0:T(8,128)(2,1)S(1)}, u32[]{:S(2)}, u32[]{:S(2)}) collective-permute-start(bf16[4,128,128]{2,1,0:T(8,128)(2,1)S(1)} %get-tuple-element.20.refs_1_), channel_id=1, source_target_pairs={{0,2},{1,3},{2,0},{3,1},{4,6},{5,7},{6,4},{7,5},{8,10},{9,11},{10,... | collective-permute-start | bytes 393224 | tf_op jit(solution)/shard_map/ppermute | solution.py:297
  7.9 7.1 %collective-permute-start.5 = (bf16[4,128,128]{2,1,0:T(8,128)(2,1)S(1)}, bf16[4,128,128]{2,1,0:T(8,128)(2,1)S(1)}, u32[]{:S(2)}, u32[]{:S(2)}) collective-permute-start(bf16[4,128,128]{2,1,0:T(8,128)(2,1)S(1)} %get-tuple-element.21.refs_2_), channel_id=1, source_target_pairs={{0,1},{1,0},{2,3},{3,2},{4,5},{5,4},{6,7},{7,6},{8,9},{9,8},{10,11... | collective-permute-start | bytes 393224 | tf_op jit(solution)/shard_map/ppermute | solution.py:297
  11.4 10.3 %collective-permute-start = (bf16[4,128,128]{2,1,0:T(8,128)(2,1)S(1)}, bf16[4,128,128]{2,1,0:T(8,128)(2,1)S(1)}, u32[]{:S(2)}, u32[]{:S(2)}) collective-permute-start(bf16[4,128,128]{2,1,0:T(8,128)(2,1)S(1)} %get-tuple-element.22.refs_4_), channel_id=1, source_target_pairs={{0,3},{1,2},{2,1},{3,0},{4,7},{5,6},{6,5},{7,4},{8,11},{9,10},{10,... | collective-permute-start | bytes 393224 | tf_op jit(solution)/shard_map/ppermute | solution.py:297
  14.4 13.9 %collective-permute-start.1 = (bf16[4,128,128]{2,1,0:T(8,128)(2,1)S(1)}, bf16[4,128,128]{2,1,0:T(8,128)(2,1)S(1)}, u32[]{:S(2)}, u32[]{:S(2)}) collective-permute-start(bf16[4,128,128]{2,1,0:T(8,128)(2,1)S(1)} %get-tuple-element.23.refs_5_), channel_id=1, source_target_pairs={{0,2},{1,3},{2,0},{3,1},{4,6},{5,7},{6,4},{7,5},{8,10},{9,11},{10,... | collective-permute-start | bytes 393224 | tf_op jit(solution)/shard_map/ppermute | solution.py:297
  14.8 13.5 %collective-permute-start.2 = (bf16[4,128,128]{2,1,0:T(8,128)(2,1)S(1)}, bf16[4,128,128]{2,1,0:T(8,128)(2,1)S(1)}, u32[]{:S(2)}, u32[]{:S(2)}) collective-permute-start(bf16[4,128,128]{2,1,0:T(8,128)(2,1)S(1)} %get-tuple-element.24.refs_6_), channel_id=1, source_target_pairs={{0,1},{1,0},{2,3},{3,2},{4,5},{5,4},{6,7},{7,6},{8,9},{9,8},{10,11... | collective-permute-start | bytes 393224 | tf_op jit(solution)/shard_map/ppermute | solution.py:297
  15.1 24.9 %collective-permute-start.6 = (f32[4,128,128]{2,1,0:T(8,128)S(1)}, f32[4,128,128]{2,1,0:T(8,128)S(1)}, u32[]{:S(2)}, u32[]{:S(2)}) collective-permute-start(f32[4,128,128]{2,1,0:T(8,128)S(1)} %far_sum.2.refs_0_), channel_id=1, source_target_pairs={{0,4},{1,5},{2,6},{3,7},{4,0},{5,1},{6,2},{7,3},{8,12},{9,13},{10,... | collective-permute-start | bytes 786440 | tf_op jit(solution)/shard_map/ppermute | solution.py:319
  20.1 19.9 %collective-permute-start.9 = (bf16[4,256,128]{2,1,0:T(8,128)(2,1)S(1)}, bf16[4,256,128]{2,1,0:T(8,128)(2,1)S(1)}, u32[]{:S(2)}, u32[]{:S(2)}) collective-permute-start(bf16[4,256,128]{2,1,0:T(8,128)(2,1)S(1)} %rotate_code.6.refs_4_), channel_id=1, source_target_pairs={{0,2},{1,3},{2,0},{3,1},{4,6},{5,7},{6,4},{7,5},{8,10},{9,11},{10,... | collective-permute-start | bytes 786440 | tf_op jit(solution)/shard_map/ppermute | solution.py:297
  28.4 11.6 %collective-permute-start.7 = (f32[4,128,128]{2,1,0:T(8,128)S(1)}, f32[4,128,128]{2,1,0:T(8,128)S(1)}, u32[]{:S(2)}, u32[]{:S(2)}) collective-permute-start(f32[4,128,128]{2,1,0:T(8,128)S(1)} %far_sum.3.refs_0_), channel_id=1, source_target_pairs={{0,4},{1,5},{2,6},{3,7},{4,0},{5,1},{6,2},{7,3},{8,12},{9,13},{10,... | collective-permute-start | bytes 786440 | tf_op jit(solution)/shard_map/ppermute | solution.py:323
  31.7 10.8 %collective-permute-start.8 = (bf16[4,256,128]{2,1,0:T(8,128)(2,1)S(1)}, bf16[4,256,128]{2,1,0:T(8,128)(2,1)S(1)}, u32[]{:S(2)}, u32[]{:S(2)}) collective-permute-start(bf16[4,256,128]{2,1,0:T(8,128)(2,1)S(1)} %get-tuple-element.27), channel_id=1, source_target_pairs={{0,3},{1,2},{2,1},{3,0},{4,7},{5,6},{6,5},{7,4},{8,11},{9,10},{10,... | collective-permute-start | bytes 786440 | tf_op jit(solution)/shard_map/ppermute | solution.py:297
  31.8 11.4 %collective-permute-start.10 = (bf16[4,256,128]{2,1,0:T(8,128)(2,1)S(1)}, bf16[4,256,128]{2,1,0:T(8,128)(2,1)S(1)}, u32[]{:S(2)}, u32[]{:S(2)}) collective-permute-start(bf16[4,256,128]{2,1,0:T(8,128)(2,1)S(1)} %get-tuple-element.28), channel_id=1, source_target_pairs={{0,1},{1,0},{2,3},{3,2},{4,5},{5,4},{6,7},{7,6},{8,9},{9,8},{10,11... | collective-permute-start | bytes 786440 | tf_op jit(solution)/shard_map/ppermute | solution.py:297
  43.6 4.2 %collective-permute-start.11 = (bf16[2,128,128]{2,1,0:T(8,128)(2,1)S(1)}, bf16[2,128,128]{2,1,0:T(8,128)(2,1)S(1)}, u32[]{:S(2)}, u32[]{:S(2)}) collective-permute-start(bf16[2,128,128]{2,1,0:T(8,128)(2,1)S(1)} %get-tuple-element.30), channel_id=1, source_target_pairs={{0,24},{8,16},{16,8},{24,0},{1,25},{9,17},{17,9},{25,1},{2,26},{10... | collective-permute-start | bytes 196616 | tf_op jit(solution)/shard_map/ppermute | solution.py:303
  43.7 5.7 %collective-permute-start.12 = (bf16[2,128,128]{2,1,0:T(8,128)(2,1)S(1)}, bf16[2,128,128]{2,1,0:T(8,128)(2,1)S(1)}, u32[]{:S(2)}, u32[]{:S(2)}) collective-permute-start(bf16[2,128,128]{2,1,0:T(8,128)(2,1)S(1)} %get-tuple-element.31), channel_id=1, source_target_pairs={{0,16},{8,24},{16,0},{24,8},{1,17},{9,25},{17,1},{25,9},{2,18},{10... | collective-permute-start | bytes 196616 | tf_op jit(solution)/shard_map/ppermute | solution.py:303
  45.5 4.0 %collective-permute-start.13 = (bf16[2,128,128]{2,1,0:T(8,128)(2,1)S(1)}, bf16[2,128,128]{2,1,0:T(8,128)(2,1)S(1)}, u32[]{:S(2)}, u32[]{:S(2)}) collective-permute-start(bf16[2,128,128]{2,1,0:T(8,128)(2,1)S(1)} %get-tuple-element.32), channel_id=1, source_target_pairs={{0,8},{8,0},{16,24},{24,16},{1,9},{9,1},{17,25},{25,17},{2,10},{10... | collective-permute-start | bytes 196616 | tf_op jit(solution)/shard_map/ppermute | solution.py:303

commit v20 on v19

--- a/solution.py
+++ b/solution.py
@@ -63,7 +63,7 @@
 
     def runs(self, steps, inner):
         half = self.half
-        if half & (half - 1) or len(steps) == half:
+        if half & (half - 1) or len(set(steps)) == half:
             return [(0, half)]
         low = 1
         while low < half and all(step in steps for step in range(2 * low)):
@@ -309,23 +309,25 @@
     others = [step for step in range(half - 1, 0, -1) if step != slow]
     order = others[:1] + [slow] + others[1:]
     whole = tuple(range(HALVES))
-    far0 = rotate(values, sign_rows, layout, True, order, [(0,)] * len(order))
+    fast = order[-1]
+    *far0, half1 = rotate(values, sign_rows, layout, True, order + [slow], [(0,)] * len(order) + [(1,)])
     *far1, own = rotate(
-        values, sign_rows, layout, True, order + [0], [(1,)] * len(order) + [whole], after=far0
+        values, sign_rows, layout, True, others + [0], [(1,)] * len(others) + [whole], after=[*far0, half1]
     )
     far0 = [swap(part, step) for step, part in zip(order, far0)] + [own]
     early = far1
     first = far_sum(far0, layout, 0, [*early])
     across = [lax.ppermute(first, "local", counterparts)]
-    (near_slow,) = rotate(values, sign_rows, layout, False, [slow], [whole], after=[first])
-    far1 = [swap(part, step) for step, part in zip(order, far1)] + [own]
-    second = far_sum(far1, layout, 1, [near_slow])
+    middle = [slow] + [fast] * (fast != slow)
+    near = rotate(values, sign_rows, layout, False, middle, [whole] * len(middle), after=[first])
+    far1 = [swap(part, step) for step, part in zip(others + [slow], far1 + [half1])] + [own]
+    second = far_sum(far1, layout, 1, [*near])
     across.append(lax.ppermute(second, "local", counterparts))
+    ends = [step for step in others if step not in middle] + [0]
     *outs, own_signs = rotate(
-        values, sign_rows, layout, False, others + [0], [whole] * (len(others) + 1), signed_out=True, after=[second]
+        values, sign_rows, layout, False, ends, [whole] * len(ends), signed_out=True, after=[second]
     )
-    near = {step: swap(part, step) if step else part for step, part in zip(others + [0], outs)}
-    near[slow] = swap(near_slow, slow)
+    near = {step: swap(part, step) if step else part for step, part in zip(middle + ends, near + outs)}
     reduced, rotated_max = finish(share(group_sum([near[step] for step in order + [0]], across, layout)), own_signs)
     return (reduced.reshape(-1), rotated_max.reshape(-1))
 

time: 50.5 us -> 49.8 us (0.986)
  waiting for transfers between devices: 18.5 us -> 15 us
  starting transfers between devices: 18.3 us -> 20.5 us
    ppermute x9, waiting for transfers between devices: 9.7 us -> 3.68 us  [swap(): return lax.ppermute(part, 'local', pairs)]
    ppermute x1, waiting for transfers between devices: 4.9 us -> 7.6 us  [shards(): across.append(lax.ppermute(second, 'local', counterparts))]
    ppermute x1, starting transfers between devices: 0.07 us -> 1.43 us  [shards(): across.append(lax.ppermute(second, 'local', counterparts))]
    ppermute x9, starting transfers between devices: 13.3 us -> 14.5 us  [swap(): return lax.ppermute(part, 'local', pairs)]
  transfers between devices with their start and end apart: 14 -> 14, of which waited for: 6 -> 6; matrix products, arithmetic and copies ran while one was open for 0% -> 0% of each run, Pallas kernels for 17% -> 18%
where the time goes in v20:
time: 49.8 us; the launch traced here: 49.6 us
  starting transfers between devices  20.5 us (41%)
  waiting for transfers between devices  15 us (30%)
  Pallas kernels  13.4 us (27%)
  between operations  0.69 us (1%)
    ppermute x9, starting transfers between devices, swap(): return lax.ppermute(part, 'local', pairs)  14.5 us
    pallas_call x4, Pallas kernels, rotate(): pl.pallas_call(functools.partial(rotate_kernel, layout, other, steps, par...  11.8 us
    ppermute x1, waiting for transfers between devices, shards(): across.append(lax.ppermute(second, 'local', counterparts))  7.6 us
    ppermute x3, waiting for transfers between devices, share(): moved.append(lax.ppermute(parts[step], 'node', pairs))  3.71 us
    ppermute x9, waiting for transfers between devices, swap(): return lax.ppermute(part, 'local', pairs)  3.68 us
    ppermute x1, starting transfers between devices, shards(): across = [lax.ppermute(first, 'local', counterparts)]  2.66 us
    ppermute x3, starting transfers between devices, share(): moved.append(lax.ppermute(parts[step], 'node', pairs))  1.93 us
    ppermute x1, starting transfers between devices, shards(): across.append(lax.ppermute(second, 'local', counterparts))  1.43 us
  transfers between devices with their start and end apart: 14, of which 6 were waited for; matrix products, arithmetic and copies ran while one was open for 0% of the time, Pallas kernels for 18%

profile of v20, /device:TPU:0, one launch (start us, length us, event | category | flops | bytes accessed | tf_op | source)
XLA Modules:
  0.0 49.6 jit_solution(16685728579193551958)
XLA Ops:
  0.6 3.2 %rotate_code.4 = (bf16[4,128,128]{2,1,0:T(8,128)(2,1)S(1)}, bf16[4,128,128]{2,1,0:T(8,128)(2,1)S(1)}, bf16[4,128,128]{2,1,0:T(8,128)(2,1)S(1)}, bf16[4,128,128]{2,1,0:T(8,128)(2,1)S(1)}) custom-call(bf16[1,1048576]{1,0:T(2,128)(2,1)} %bitcast.4, s32[8192,128]{1,0:T(8,128)} %bitcast.8), custom_call_target="tpu_custom_call" | custom-call | flops 268435456 | bytes 5242880 | tf_op jit(solution)/shard_map/rotate_code/pallas_call | solution.py:166
  3.8 4.1 %collective-permute-start.3 = (bf16[4,128,128]{2,1,0:T(8,128)(2,1)S(1)}, bf16[4,128,128]{2,1,0:T(8,128)(2,1)S(1)}, u32[]{:S(2)}, u32[]{:S(2)}) collective-permute-start(bf16[4,128,128]{2,1,0:T(8,128)(2,1)S(1)} %get-tuple-element.20.refs_0_), channel_id=1, source_target_pairs={{0,3},{1,2},{2,1},{3,0},{4,7},{5,6},{6,5},{7,4},{8,11},{9,10},{10,... | collective-permute-start | bytes 393224 | tf_op jit(solution)/shard_map/ppermute | solution.py:297
  7.8 0.4 collective-permute-start.4
  8.3 0.2 collective-permute-start.5
  8.5 1.9 %collective-permute-start.2 = (bf16[4,128,128]{2,1,0:T(8,128)(2,1)S(1)}, bf16[4,128,128]{2,1,0:T(8,128)(2,1)S(1)}, u32[]{:S(2)}, u32[]{:S(2)}) collective-permute-start(bf16[4,128,128]{2,1,0:T(8,128)(2,1)S(1)} %get-tuple-element.23.refs_3_), channel_id=1, source_target_pairs={{0,2},{1,3},{2,0},{3,1},{4,6},{5,7},{6,4},{7,5},{8,10},{9,11},{10,... | collective-permute-start | bytes 393224 | tf_op jit(solution)/shard_map/ppermute | solution.py:297
  10.4 2.9 %rotate_code.5 = (bf16[4,128,128]{2,1,0:T(8,128)(2,1)S(1)}, bf16[4,128,128]{2,1,0:T(8,128)(2,1)S(1)}, bf16[4,256,128]{2,1,0:T(8,128)(2,1)S(1)}) custom-call(bf16[1,1048576]{1,0:T(2,128)(2,1)} %bitcast.5, s32[8192,128]{1,0:T(8,128)} %bitcast.9, bf16[4,128,128]{2,1,0:T(8,128)(2,1)S(1)} %get-tuple-element.20.refs_0_, ...), custom_call_target="tpu_custom_call" | custom-call | flops 201326592 | bytes 3932160 | tf_op jit(solution)/shard_map/rotate_code/pallas_call | solution.py:166
  13.2 1.5 %collective-permute-start = (bf16[4,128,128]{2,1,0:T(8,128)(2,1)S(1)}, bf16[4,128,128]{2,1,0:T(8,128)(2,1)S(1)}, u32[]{:S(2)}, u32[]{:S(2)}) collective-permute-start(bf16[4,128,128]{2,1,0:T(8,128)(2,1)S(1)} %get-tuple-element.24.refs_4_), channel_id=1, source_target_pairs={{0,3},{1,2},{2,1},{3,0},{4,7},{5,6},{6,5},{7,4},{8,11},{9,10},{10,... | collective-permute-start | bytes 393224 | tf_op jit(solution)/shard_map/ppermute | solution.py:297
  14.7 0.0 collective-permute-done.3.refs_0_
  14.7 0.2 collective-permute-start.1
  14.9 0.5 %collective-permute-done.4.refs_1_ = bf16[4,128,128]{2,1,0:T(8,128)(2,1)S(1)} collective-permute-done((bf16[4,128,128]{2,1,0:T(8,128)(2,1)S(1)}, bf16[4,128,128]{2,1,0:T(8,128)(2,1)S(1)}, u32[]{:S(2)}, u32[]{:S(2)}) %collective-permute-start.4) | collective-permute-done | bytes 131104 | tf_op jit(solution)/shard_map/ppermute | solution.py:297
  15.5 0.0 collective-permute-done.5.refs_2_
  15.5 0.1 far_sum.2.refs_0_
  15.5 2.7 %collective-permute-start.6 = (f32[4,128,128]{2,1,0:T(8,128)S(1)}, f32[4,128,128]{2,1,0:T(8,128)S(1)}, u32[]{:S(2)}, u32[]{:S(2)}) collective-permute-start(f32[4,128,128]{2,1,0:T(8,128)S(1)} %far_sum.2.refs_0_), channel_id=1, source_target_pairs={{0,4},{1,5},{2,6},{3,7},{4,0},{5,1},{6,2},{7,3},{8,12},{9,13},{10,... | collective-permute-start | bytes 786440 | tf_op jit(solution)/shard_map/ppermute | solution.py:320
  18.2 2.9 %rotate_code.6 = (bf16[4,256,128]{2,1,0:T(8,128)(2,1)S(1)}, bf16[4,256,128]{2,1,0:T(8,128)(2,1)S(1)}) custom-call(bf16[1,1048576]{1,0:T(2,128)(2,1)} %bitcast.6, s32[8192,128]{1,0:T(8,128)} %bitcast.10, f32[4,128,128]{2,1,0:T(8,128)S(1)} %far_sum.2.refs_0_), custom_call_target="tpu_custom_call" | custom-call | flops 134217728 | bytes 2621440 | tf_op jit(solution)/shard_map/rotate_code/pallas_call | solution.py:166
  21.1 1.6 %collective-permute-start.9 = (bf16[4,256,128]{2,1,0:T(8,128)(2,1)S(1)}, bf16[4,256,128]{2,1,0:T(8,128)(2,1)S(1)}, u32[]{:S(2)}, u32[]{:S(2)}) collective-permute-start(bf16[4,256,128]{2,1,0:T(8,128)(2,1)S(1)} %get-tuple-element.27.refs_4_), channel_id=1, source_target_pairs={{0,2},{1,3},{2,0},{3,1},{4,6},{5,7},{6,4},{7,5},{8,10},{9,11},{10,... | collective-permute-start | bytes 786440 | tf_op jit(solution)/shard_map/ppermute | solution.py:297
  22.7 0.1 collective-permute-done.2.refs_2_
  22.8 1.2 %collective-permute-start.10 = (bf16[4,256,128]{2,1,0:T(8,128)(2,1)S(1)}, bf16[4,256,128]{2,1,0:T(8,128)(2,1)S(1)}, u32[]{:S(2)}, u32[]{:S(2)}) collective-permute-start(bf16[4,256,128]{2,1,0:T(8,128)(2,1)S(1)} %get-tuple-element.28.refs_5_), channel_id=1, source_target_pairs={{0,1},{1,0},{2,3},{3,2},{4,5},{5,4},{6,7},{7,6},{8,9},{9,8},{10,11... | collective-permute-start | bytes 786440 | tf_op jit(solution)/shard_map/ppermute | solution.py:297
  24.0 0.0 collective-permute-done.refs_0_
  24.0 0.0 collective-permute-done.1.refs_1_
  24.0 0.1 far_sum.3.refs_0_
  24.1 1.4 %collective-permute-start.7 = (f32[4,128,128]{2,1,0:T(8,128)S(1)}, f32[4,128,128]{2,1,0:T(8,128)S(1)}, u32[]{:S(2)}, u32[]{:S(2)}) collective-permute-start(f32[4,128,128]{2,1,0:T(8,128)S(1)} %far_sum.3.refs_0_), channel_id=1, source_target_pairs={{0,4},{1,5},{2,6},{3,7},{4,0},{5,1},{6,2},{7,3},{8,12},{9,13},{10,... | collective-permute-start | bytes 786440 | tf_op jit(solution)/shard_map/ppermute | solution.py:325
  25.5 2.9 %rotate_code.7 = (bf16[4,256,128]{2,1,0:T(8,128)(2,1)S(1)}, bf16[4,256,128]{2,1,0:T(8,128)(2,1)S(1)}, s32[256,128]{1,0:T(8,128)S(1)}) custom-call(bf16[1,1048576]{1,0:T(2,128)(2,1)} %bitcast.7, s32[8192,128]{1,0:T(8,128)} %bitcast.11, f32[4,128,128]{2,1,0:T(8,128)S(1)} %far_sum.3.refs_0_), custom_call_target="tpu_custom_call" | custom-call | flops 134217728 | bytes 2621440 | tf_op jit(solution)/shard_map/rotate_code/pallas_call | solution.py:166
  28.4 3.4 %collective-permute-start.8 = (bf16[4,256,128]{2,1,0:T(8,128)(2,1)S(1)}, bf16[4,256,128]{2,1,0:T(8,128)(2,1)S(1)}, u32[]{:S(2)}, u32[]{:S(2)}) collective-permute-start(bf16[4,256,128]{2,1,0:T(8,128)(2,1)S(1)} %get-tuple-element.30), channel_id=1, source_target_pairs={{0,3},{1,2},{2,1},{3,0},{4,7},{5,6},{6,5},{7,4},{8,11},{9,10},{10,... | collective-permute-start | bytes 786440 | tf_op jit(solution)/shard_map/ppermute | solution.py:297
  31.9 0.0 collective-permute-done.6.refs_0_
  31.9 7.6 %collective-permute-done.7.refs_1_ = f32[4,128,128]{2,1,0:T(8,128)S(1)} collective-permute-done((f32[4,128,128]{2,1,0:T(8,128)S(1)}, f32[4,128,128]{2,1,0:T(8,128)S(1)}, u32[]{:S(2)}, u32[]{:S(2)}) %collective-permute-start.7) | collective-permute-done | bytes 262176 | tf_op jit(solution)/shard_map/ppermute | solution.py:325
  39.5 0.0 collective-permute-done.9.refs_3_
  39.5 0.0 collective-permute-done.10.refs_4_
  39.5 3.0 %collective-permute-done.8.refs_2_ = bf16[4,256,128]{2,1,0:T(8,128)(2,1)S(1)} collective-permute-done((bf16[4,256,128]{2,1,0:T(8,128)(2,1)S(1)}, bf16[4,256,128]{2,1,0:T(8,128)(2,1)S(1)}, u32[]{:S(2)}, u32[]{:S(2)}) %collective-permute-start.8) | collective-permute-done | bytes 262176 | tf_op jit(solution)/shard_map/ppermute | solution.py:297
  42.5 0.5 %group_sum_code.1 = (bf16[2,128,128]{2,1,0:T(8,128)(2,1)S(1)}, bf16[2,128,128]{2,1,0:T(8,128)(2,1)S(1)}, bf16[2,128,128]{2,1,0:T(8,128)(2,1)S(1)}, bf16[2,128,128]{2,1,0:T(8,128)(2,1)S(1)}) custom-call(f32[4,128,128]{2,1,0:T(8,128)S(1)} %collective-permute-done.6.refs_0_, f32[4,128,128]{2,1,0:T(8,128)S(1)} %collective-permute-done.7.refs_1_, ...), custom_call_target="tpu_custom_call" | custom-call | flops 3932160 | bytes 1835008 | tf_op jit(solution)/shard_map/group_sum_code/pallas_call | solution.py:229
  43.0 0.1 collective-permute-start.11
  43.1 1.4 %collective-permute-start.12 = (bf16[2,128,128]{2,1,0:T(8,128)(2,1)S(1)}, bf16[2,128,128]{2,1,0:T(8,128)(2,1)S(1)}, u32[]{:S(2)}, u32[]{:S(2)}) collective-permute-start(bf16[2,128,128]{2,1,0:T(8,128)(2,1)S(1)} %get-tuple-element.33), channel_id=1, source_target_pairs={{0,16},{8,24},{16,0},{24,8},{1,17},{9,25},{17,1},{25,9},{2,18},{10... | collective-permute-start | bytes 196616 | tf_op jit(solution)/shard_map/ppermute | solution.py:303
  44.5 0.4 collective-permute-start.13
  44.9 2.5 %collective-permute-done.11.refs_0_ = bf16[2,128,128]{2,1,0:T(8,128)(2,1)S(1)} collective-permute-done((bf16[2,128,128]{2,1,0:T(8,128)(2,1)S(1)}, bf16[2,128,128]{2,1,0:T(8,128)(2,1)S(1)}, u32[]{:S(2)}, u32[]{:S(2)}) %collective-permute-start.11) | collective-permute-done | bytes 65568 | tf_op jit(solution)/shard_map/ppermute | solution.py:303
  47.5 1.2 %collective-permute-done.12.refs_1_ = bf16[2,128,128]{2,1,0:T(8,128)(2,1)S(1)} collective-permute-done((bf16[2,128,128]{2,1,0:T(8,128)(2,1)S(1)}, bf16[2,128,128]{2,1,0:T(8,128)(2,1)S(1)}, u32[]{:S(2)}, u32[]{:S(2)}) %collective-permute-start.12) | collective-permute-done | bytes 65568 | tf_op jit(solution)/shard_map/ppermute | solution.py:303
  48.6 0.0 collective-permute-done.13.refs_2_
  48.6 0.9 %sum_unrotate.1 = (f32[256,128]{1,0:T(8,128)}, f32[1,256]{1,0:T(1,128)}) custom-call(s32[256,128]{1,0:T(8,128)S(1)} %get-tuple-element.29.sign_ref, bf16[2,128,128]{2,1,0:T(8,128)(2,1)S(1)} %collective-permute-done.11.refs_0_, bf16[2,128,128]{2,1,0:T(8,128)(2,1)S(1)} %collective-permute-done.12.refs_1_, ...), custom_call_target="tpu_custom_call" | custom-call | tf_op jit(solution)/shard_map/sum_unrotate/pallas_call | solution.py:274
Async XLA Ops:
  3.8 10.9 %collective-permute-start.3 = (bf16[4,128,128]{2,1,0:T(8,128)(2,1)S(1)}, bf16[4,128,128]{2,1,0:T(8,128)(2,1)S(1)}, u32[]{:S(2)}, u32[]{:S(2)}) collective-permute-start(bf16[4,128,128]{2,1,0:T(8,128)(2,1)S(1)} %get-tuple-element.20.refs_0_), channel_id=1, source_target_pairs={{0,3},{1,2},{2,1},{3,0},{4,7},{5,6},{6,5},{7,4},{8,11},{9,10},{10,... | collective-permute-start | bytes 393224 | tf_op jit(solution)/shard_map/ppermute | solution.py:297
  7.8 7.6 %collective-permute-start.4 = (bf16[4,128,128]{2,1,0:T(8,128)(2,1)S(1)}, bf16[4,128,128]{2,1,0:T(8,128)(2,1)S(1)}, u32[]{:S(2)}, u32[]{:S(2)}) collective-permute-start(bf16[4,128,128]{2,1,0:T(8,128)(2,1)S(1)} %get-tuple-element.21.refs_1_), channel_id=1, source_target_pairs={{0,2},{1,3},{2,0},{3,1},{4,6},{5,7},{6,4},{7,5},{8,10},{9,11},{10,... | collective-permute-start | bytes 393224 | tf_op jit(solution)/shard_map/ppermute | solution.py:297
  8.3 7.2 %collective-permute-start.5 = (bf16[4,128,128]{2,1,0:T(8,128)(2,1)S(1)}, bf16[4,128,128]{2,1,0:T(8,128)(2,1)S(1)}, u32[]{:S(2)}, u32[]{:S(2)}) collective-permute-start(bf16[4,128,128]{2,1,0:T(8,128)(2,1)S(1)} %get-tuple-element.22.refs_2_), channel_id=1, source_target_pairs={{0,1},{1,0},{2,3},{3,2},{4,5},{5,4},{6,7},{7,6},{8,9},{9,8},{10,11... | collective-permute-start | bytes 393224 | tf_op jit(solution)/shard_map/ppermute | solution.py:297
  8.5 14.3 %collective-permute-start.2 = (bf16[4,128,128]{2,1,0:T(8,128)(2,1)S(1)}, bf16[4,128,128]{2,1,0:T(8,128)(2,1)S(1)}, u32[]{:S(2)}, u32[]{:S(2)}) collective-permute-start(bf16[4,128,128]{2,1,0:T(8,128)(2,1)S(1)} %get-tuple-element.23.refs_3_), channel_id=1, source_target_pairs={{0,2},{1,3},{2,0},{3,1},{4,6},{5,7},{6,4},{7,5},{8,10},{9,11},{10,... | collective-permute-start | bytes 393224 | tf_op jit(solution)/shard_map/ppermute | solution.py:297
  13.2 10.8 %collective-permute-start = (bf16[4,128,128]{2,1,0:T(8,128)(2,1)S(1)}, bf16[4,128,128]{2,1,0:T(8,128)(2,1)S(1)}, u32[]{:S(2)}, u32[]{:S(2)}) collective-permute-start(bf16[4,128,128]{2,1,0:T(8,128)(2,1)S(1)} %get-tuple-element.24.refs_4_), channel_id=1, source_target_pairs={{0,3},{1,2},{2,1},{3,0},{4,7},{5,6},{6,5},{7,4},{8,11},{9,10},{10,... | collective-permute-start | bytes 393224 | tf_op jit(solution)/shard_map/ppermute | solution.py:297
  14.7 9.3 %collective-permute-start.1 = (bf16[4,128,128]{2,1,0:T(8,128)(2,1)S(1)}, bf16[4,128,128]{2,1,0:T(8,128)(2,1)S(1)}, u32[]{:S(2)}, u32[]{:S(2)}) collective-permute-start(bf16[4,128,128]{2,1,0:T(8,128)(2,1)S(1)} %get-tuple-element.25.refs_5_), channel_id=1, source_target_pairs={{0,1},{1,0},{2,3},{3,2},{4,5},{5,4},{6,7},{7,6},{8,9},{9,8},{10,11... | collective-permute-start | bytes 393224 | tf_op jit(solution)/shard_map/ppermute | solution.py:297
  15.5 16.3 %collective-permute-start.6 = (f32[4,128,128]{2,1,0:T(8,128)S(1)}, f32[4,128,128]{2,1,0:T(8,128)S(1)}, u32[]{:S(2)}, u32[]{:S(2)}) collective-permute-start(f32[4,128,128]{2,1,0:T(8,128)S(1)} %far_sum.2.refs_0_), channel_id=1, source_target_pairs={{0,4},{1,5},{2,6},{3,7},{4,0},{5,1},{6,2},{7,3},{8,12},{9,13},{10,... | collective-permute-start | bytes 786440 | tf_op jit(solution)/shard_map/ppermute | solution.py:320
  21.1 18.4 %collective-permute-start.9 = (bf16[4,256,128]{2,1,0:T(8,128)(2,1)S(1)}, bf16[4,256,128]{2,1,0:T(8,128)(2,1)S(1)}, u32[]{:S(2)}, u32[]{:S(2)}) collective-permute-start(bf16[4,256,128]{2,1,0:T(8,128)(2,1)S(1)} %get-tuple-element.27.refs_4_), channel_id=1, source_target_pairs={{0,2},{1,3},{2,0},{3,1},{4,6},{5,7},{6,4},{7,5},{8,10},{9,11},{10,... | collective-permute-start | bytes 786440 | tf_op jit(solution)/shard_map/ppermute | solution.py:297
  22.8 16.7 %collective-permute-start.10 = (bf16[4,256,128]{2,1,0:T(8,128)(2,1)S(1)}, bf16[4,256,128]{2,1,0:T(8,128)(2,1)S(1)}, u32[]{:S(2)}, u32[]{:S(2)}) collective-permute-start(bf16[4,256,128]{2,1,0:T(8,128)(2,1)S(1)} %get-tuple-element.28.refs_5_), channel_id=1, source_target_pairs={{0,1},{1,0},{2,3},{3,2},{4,5},{5,4},{6,7},{7,6},{8,9},{9,8},{10,11... | collective-permute-start | bytes 786440 | tf_op jit(solution)/shard_map/ppermute | solution.py:297
  24.1 15.4 %collective-permute-start.7 = (f32[4,128,128]{2,1,0:T(8,128)S(1)}, f32[4,128,128]{2,1,0:T(8,128)S(1)}, u32[]{:S(2)}, u32[]{:S(2)}) collective-permute-start(f32[4,128,128]{2,1,0:T(8,128)S(1)} %far_sum.3.refs_0_), channel_id=1, source_target_pairs={{0,4},{1,5},{2,6},{3,7},{4,0},{5,1},{6,2},{7,3},{8,12},{9,13},{10,... | collective-permute-start | bytes 786440 | tf_op jit(solution)/shard_map/ppermute | solution.py:325
  28.4 14.1 %collective-permute-start.8 = (bf16[4,256,128]{2,1,0:T(8,128)(2,1)S(1)}, bf16[4,256,128]{2,1,0:T(8,128)(2,1)S(1)}, u32[]{:S(2)}, u32[]{:S(2)}) collective-permute-start(bf16[4,256,128]{2,1,0:T(8,128)(2,1)S(1)} %get-tuple-element.30), channel_id=1, source_target_pairs={{0,3},{1,2},{2,1},{3,0},{4,7},{5,6},{6,5},{7,4},{8,11},{9,10},{10,... | collective-permute-start | bytes 786440 | tf_op jit(solution)/shard_map/ppermute | solution.py:297
  43.0 4.5 %collective-permute-start.11 = (bf16[2,128,128]{2,1,0:T(8,128)(2,1)S(1)}, bf16[2,128,128]{2,1,0:T(8,128)(2,1)S(1)}, u32[]{:S(2)}, u32[]{:S(2)}) collective-permute-start(bf16[2,128,128]{2,1,0:T(8,128)(2,1)S(1)} %get-tuple-element.32), channel_id=1, source_target_pairs={{0,24},{8,16},{16,8},{24,0},{1,25},{9,17},{17,9},{25,1},{2,26},{10... | collective-permute-start | bytes 196616 | tf_op jit(solution)/shard_map/ppermute | solution.py:303
  43.1 5.5 %collective-permute-start.12 = (bf16[2,128,128]{2,1,0:T(8,128)(2,1)S(1)}, bf16[2,128,128]{2,1,0:T(8,128)(2,1)S(1)}, u32[]{:S(2)}, u32[]{:S(2)}) collective-permute-start(bf16[2,128,128]{2,1,0:T(8,128)(2,1)S(1)} %get-tuple-element.33), channel_id=1, source_target_pairs={{0,16},{8,24},{16,0},{24,8},{1,17},{9,25},{17,1},{25,9},{2,18},{10... | collective-permute-start | bytes 196616 | tf_op jit(solution)/shard_map/ppermute | solution.py:303
  44.5 4.2 %collective-permute-start.13 = (bf16[2,128,128]{2,1,0:T(8,128)(2,1)S(1)}, bf16[2,128,128]{2,1,0:T(8,128)(2,1)S(1)}, u32[]{:S(2)}, u32[]{:S(2)}) collective-permute-start(bf16[2,128,128]{2,1,0:T(8,128)(2,1)S(1)} %get-tuple-element.34), channel_id=1, source_target_pairs={{0,8},{8,0},{16,24},{24,16},{1,9},{9,1},{17,25},{25,17},{2,10},{10... | collective-permute-start | bytes 196616 | tf_op jit(solution)/shard_map/ppermute | solution.py:303

commit v21 on v20

--- a/solution.py
+++ b/solution.py
@@ -309,7 +309,6 @@
     others = [step for step in range(half - 1, 0, -1) if step != slow]
     order = others[:1] + [slow] + others[1:]
     whole = tuple(range(HALVES))
-    fast = order[-1]
     *far0, half1 = rotate(values, sign_rows, layout, True, order + [slow], [(0,)] * len(order) + [(1,)])
     *far1, own = rotate(
         values, sign_rows, layout, True, others + [0], [(1,)] * len(others) + [whole], after=[*far0, half1]
@@ -318,7 +317,7 @@
     early = far1
     first = far_sum(far0, layout, 0, [*early])
     across = [lax.ppermute(first, "local", counterparts)]
-    middle = [slow] + [fast] * (fast != slow)
+    middle = others[:1] + [slow]
     near = rotate(values, sign_rows, layout, False, middle, [whole] * len(middle), after=[first])
     far1 = [swap(part, step) for step, part in zip(others + [slow], far1 + [half1])] + [own]
     second = far_sum(far1, layout, 1, [*near])

time: 49.8 us -> 50 us (level)
  waiting for transfers between devices: 15 us -> 16.6 us
  starting transfers between devices: 20.5 us -> 19.4 us
    ppermute x1, waiting for transfers between devices: 7.6 us -> 11.2 us  [shards(): across.append(lax.ppermute(second, 'local', counterparts))]
    ppermute x9, waiting for transfers between devices: 3.68 us -> 1.45 us  [swap(): return lax.ppermute(part, 'local', pairs)]
    ppermute x9, starting transfers between devices: 14.5 us -> 13.1 us  [swap(): return lax.ppermute(part, 'local', pairs)]
  transfers between devices with their start and end apart: 14 -> 14, of which waited for: 6 -> 5; matrix products, arithmetic and copies ran while one was open for 0% -> 0% of each run, Pallas kernels for 18% -> 17%
where the time goes in v21:
time: 50 us; the launch traced here: 49.8 us
  starting transfers between devices  19.4 us (39%)
  waiting for transfers between devices  16.6 us (33%)
  Pallas kernels  13.1 us (26%)
  between operations  0.69 us (1%)
    ppermute x9, starting transfers between devices, swap(): return lax.ppermute(part, 'local', pairs)  13.1 us
    pallas_call x4, Pallas kernels, rotate(): pl.pallas_call(functools.partial(rotate_kernel, layout, other, steps, par...  11.5 us
    ppermute x1, waiting for transfers between devices, shards(): across.append(lax.ppermute(second, 'local', counterparts))  11.2 us
    ppermute x3, waiting for transfers between devices, share(): moved.append(lax.ppermute(parts[step], 'node', pairs))  3.94 us
    ppermute x1, starting transfers between devices, shards(): across = [lax.ppermute(first, 'local', counterparts)]  2.66 us
    ppermute x3, starting transfers between devices, share(): moved.append(lax.ppermute(parts[step], 'node', pairs))  1.93 us
    ppermute x1, starting transfers between devices, shards(): across.append(lax.ppermute(second, 'local', counterparts))  1.7 us
    ppermute x9, waiting for transfers between devices, swap(): return lax.ppermute(part, 'local', pairs)  1.45 us
  transfers between devices with their start and end apart: 14, of which 5 were waited for; matrix products, arithmetic and copies ran while one was open for 0% of the time, Pallas kernels for 17%

profile of v21, /device:TPU:0, one launch (start us, length us, event | category | flops | bytes accessed | tf_op | source)
XLA Modules:
  0.0 49.8 jit_solution(1828696135558925363)
XLA Ops:
  0.6 3.2 %rotate_code.4 = (bf16[4,128,128]{2,1,0:T(8,128)(2,1)S(1)}, bf16[4,128,128]{2,1,0:T(8,128)(2,1)S(1)}, bf16[4,128,128]{2,1,0:T(8,128)(2,1)S(1)}, bf16[4,128,128]{2,1,0:T(8,128)(2,1)S(1)}) custom-call(bf16[1,1048576]{1,0:T(2,128)(2,1)} %bitcast.4, s32[8192,128]{1,0:T(8,128)} %bitcast.8), custom_call_target="tpu_custom_call" | custom-call | flops 268435456 | bytes 5242880 | tf_op jit(solution)/shard_map/rotate_code/pallas_call | solution.py:166
  3.8 4.1 %collective-permute-start.3 = (bf16[4,128,128]{2,1,0:T(8,128)(2,1)S(1)}, bf16[4,128,128]{2,1,0:T(8,128)(2,1)S(1)}, u32[]{:S(2)}, u32[]{:S(2)}) collective-permute-start(bf16[4,128,128]{2,1,0:T(8,128)(2,1)S(1)} %get-tuple-element.20.refs_0_), channel_id=1, source_target_pairs={{0,3},{1,2},{2,1},{3,0},{4,7},{5,6},{6,5},{7,4},{8,11},{9,10},{10,... | collective-permute-start | bytes 393224 | tf_op jit(solution)/shard_map/ppermute | solution.py:297
  7.8 0.4 collective-permute-start.4
  8.3 0.2 collective-permute-start.5
  8.5 1.9 %collective-permute-start.2 = (bf16[4,128,128]{2,1,0:T(8,128)(2,1)S(1)}, bf16[4,128,128]{2,1,0:T(8,128)(2,1)S(1)}, u32[]{:S(2)}, u32[]{:S(2)}) collective-permute-start(bf16[4,128,128]{2,1,0:T(8,128)(2,1)S(1)} %get-tuple-element.23.refs_3_), channel_id=1, source_target_pairs={{0,2},{1,3},{2,0},{3,1},{4,6},{5,7},{6,4},{7,5},{8,10},{9,11},{10,... | collective-permute-start | bytes 393224 | tf_op jit(solution)/shard_map/ppermute | solution.py:297
  10.4 2.9 %rotate_code.5 = (bf16[4,128,128]{2,1,0:T(8,128)(2,1)S(1)}, bf16[4,128,128]{2,1,0:T(8,128)(2,1)S(1)}, bf16[4,256,128]{2,1,0:T(8,128)(2,1)S(1)}) custom-call(bf16[1,1048576]{1,0:T(2,128)(2,1)} %bitcast.5, s32[8192,128]{1,0:T(8,128)} %bitcast.9, bf16[4,128,128]{2,1,0:T(8,128)(2,1)S(1)} %get-tuple-element.20.refs_0_, ...), custom_call_target="tpu_custom_call" | custom-call | flops 201326592 | bytes 3932160 | tf_op jit(solution)/shard_map/rotate_code/pallas_call | solution.py:166
  13.2 1.5 %collective-permute-start = (bf16[4,128,128]{2,1,0:T(8,128)(2,1)S(1)}, bf16[4,128,128]{2,1,0:T(8,128)(2,1)S(1)}, u32[]{:S(2)}, u32[]{:S(2)}) collective-permute-start(bf16[4,128,128]{2,1,0:T(8,128)(2,1)S(1)} %get-tuple-element.24.refs_4_), channel_id=1, source_target_pairs={{0,3},{1,2},{2,1},{3,0},{4,7},{5,6},{6,5},{7,4},{8,11},{9,10},{10,... | collective-permute-start | bytes 393224 | tf_op jit(solution)/shard_map/ppermute | solution.py:297
  14.7 0.0 collective-permute-done.3.refs_0_
  14.7 0.2 collective-permute-start.1
  14.9 0.5 %collective-permute-done.4.refs_1_ = bf16[4,128,128]{2,1,0:T(8,128)(2,1)S(1)} collective-permute-done((bf16[4,128,128]{2,1,0:T(8,128)(2,1)S(1)}, bf16[4,128,128]{2,1,0:T(8,128)(2,1)S(1)}, u32[]{:S(2)}, u32[]{:S(2)}) %collective-permute-start.4) | collective-permute-done | bytes 131104 | tf_op jit(solution)/shard_map/ppermute | solution.py:297
  15.5 0.0 collective-permute-done.5.refs_2_
  15.5 0.1 far_sum.2.refs_0_
  15.5 2.7 %collective-permute-start.6 = (f32[4,128,128]{2,1,0:T(8,128)S(1)}, f32[4,128,128]{2,1,0:T(8,128)S(1)}, u32[]{:S(2)}, u32[]{:S(2)}) collective-permute-start(f32[4,128,128]{2,1,0:T(8,128)S(1)} %far_sum.2.refs_0_), channel_id=1, source_target_pairs={{0,4},{1,5},{2,6},{3,7},{4,0},{5,1},{6,2},{7,3},{8,12},{9,13},{10,... | collective-permute-start | bytes 786440 | tf_op jit(solution)/shard_map/ppermute | solution.py:319
  18.2 2.7 %rotate_code.6 = (bf16[4,256,128]{2,1,0:T(8,128)(2,1)S(1)}, bf16[4,256,128]{2,1,0:T(8,128)(2,1)S(1)}) custom-call(bf16[1,1048576]{1,0:T(2,128)(2,1)} %bitcast.6, s32[8192,128]{1,0:T(8,128)} %bitcast.10, f32[4,128,128]{2,1,0:T(8,128)S(1)} %far_sum.2.refs_0_), custom_call_target="tpu_custom_call" | custom-call | flops 134217728 | bytes 2621440 | tf_op jit(solution)/shard_map/rotate_code/pallas_call | solution.py:166
  20.9 2.4 %collective-permute-start.8 = (bf16[4,256,128]{2,1,0:T(8,128)(2,1)S(1)}, bf16[4,256,128]{2,1,0:T(8,128)(2,1)S(1)}, u32[]{:S(2)}, u32[]{:S(2)}) collective-permute-start(bf16[4,256,128]{2,1,0:T(8,128)(2,1)S(1)} %get-tuple-element.27.refs_4_), channel_id=1, source_target_pairs={{0,3},{1,2},{2,1},{3,0},{4,7},{5,6},{6,5},{7,4},{8,11},{9,10},{10,... | collective-permute-start | bytes 786440 | tf_op jit(solution)/shard_map/ppermute | solution.py:297
  23.3 0.0 collective-permute-done.2.refs_2_
  23.3 0.5 collective-permute-start.9
  23.7 0.0 collective-permute-done.refs_0_
  23.8 0.0 collective-permute-done.1.refs_1_
  23.8 0.1 far_sum.3.refs_0_
  23.8 1.7 %collective-permute-start.7 = (f32[4,128,128]{2,1,0:T(8,128)S(1)}, f32[4,128,128]{2,1,0:T(8,128)S(1)}, u32[]{:S(2)}, u32[]{:S(2)}) collective-permute-start(f32[4,128,128]{2,1,0:T(8,128)S(1)} %far_sum.3.refs_0_), channel_id=1, source_target_pairs={{0,4},{1,5},{2,6},{3,7},{4,0},{5,1},{6,2},{7,3},{8,12},{9,13},{10,... | collective-permute-start | bytes 786440 | tf_op jit(solution)/shard_map/ppermute | solution.py:324
  25.5 2.7 %rotate_code.7 = (bf16[4,256,128]{2,1,0:T(8,128)(2,1)S(1)}, bf16[4,256,128]{2,1,0:T(8,128)(2,1)S(1)}, s32[256,128]{1,0:T(8,128)S(1)}) custom-call(bf16[1,1048576]{1,0:T(2,128)(2,1)} %bitcast.7, s32[8192,128]{1,0:T(8,128)} %bitcast.11, f32[4,128,128]{2,1,0:T(8,128)S(1)} %far_sum.3.refs_0_), custom_call_target="tpu_custom_call" | custom-call | flops 134217728 | bytes 2621440 | tf_op jit(solution)/shard_map/rotate_code/pallas_call | solution.py:166
  28.3 2.0 %collective-permute-start.10 = (bf16[4,256,128]{2,1,0:T(8,128)(2,1)S(1)}, bf16[4,256,128]{2,1,0:T(8,128)(2,1)S(1)}, u32[]{:S(2)}, u32[]{:S(2)}) collective-permute-start(bf16[4,256,128]{2,1,0:T(8,128)(2,1)S(1)} %get-tuple-element.30), channel_id=1, source_target_pairs={{0,1},{1,0},{2,3},{3,2},{4,5},{5,4},{6,7},{7,6},{8,9},{9,8},{10,11... | collective-permute-start | bytes 786440 | tf_op jit(solution)/shard_map/ppermute | solution.py:297
  30.3 0.0 collective-permute-done.6.refs_0_
  30.3 11.2 %collective-permute-done.7.refs_1_ = f32[4,128,128]{2,1,0:T(8,128)S(1)} collective-permute-done((f32[4,128,128]{2,1,0:T(8,128)S(1)}, f32[4,128,128]{2,1,0:T(8,128)S(1)}, u32[]{:S(2)}, u32[]{:S(2)}) %collective-permute-start.7) | collective-permute-done | bytes 262176 | tf_op jit(solution)/shard_map/ppermute | solution.py:324
  41.5 0.0 collective-permute-done.8.refs_2_
  41.6 0.9 %collective-permute-done.9.refs_3_ = bf16[4,256,128]{2,1,0:T(8,128)(2,1)S(1)} collective-permute-done((bf16[4,256,128]{2,1,0:T(8,128)(2,1)S(1)}, bf16[4,256,128]{2,1,0:T(8,128)(2,1)S(1)}, u32[]{:S(2)}, u32[]{:S(2)}) %collective-permute-start.9) | collective-permute-done | bytes 262176 | tf_op jit(solution)/shard_map/ppermute | solution.py:297
  42.4 0.0 collective-permute-done.10.refs_4_
  42.5 0.5 %group_sum_code.1 = (bf16[2,128,128]{2,1,0:T(8,128)(2,1)S(1)}, bf16[2,128,128]{2,1,0:T(8,128)(2,1)S(1)}, bf16[2,128,128]{2,1,0:T(8,128)(2,1)S(1)}, bf16[2,128,128]{2,1,0:T(8,128)(2,1)S(1)}) custom-call(f32[4,128,128]{2,1,0:T(8,128)S(1)} %collective-permute-done.6.refs_0_, f32[4,128,128]{2,1,0:T(8,128)S(1)} %collective-permute-done.7.refs_1_, ...), custom_call_target="tpu_custom_call" | custom-call | flops 3932160 | bytes 1835008 | tf_op jit(solution)/shard_map/group_sum_code/pallas_call | solution.py:229
  43.0 0.1 collective-permute-start.11
  43.1 1.5 %collective-permute-start.12 = (bf16[2,128,128]{2,1,0:T(8,128)(2,1)S(1)}, bf16[2,128,128]{2,1,0:T(8,128)(2,1)S(1)}, u32[]{:S(2)}, u32[]{:S(2)}) collective-permute-start(bf16[2,128,128]{2,1,0:T(8,128)(2,1)S(1)} %get-tuple-element.33), channel_id=1, source_target_pairs={{0,16},{8,24},{16,0},{24,8},{1,17},{9,25},{17,1},{25,9},{2,18},{10... | collective-permute-start | bytes 196616 | tf_op jit(solution)/shard_map/ppermute | solution.py:303
  44.6 0.3 collective-permute-start.13
  44.9 2.5 %collective-permute-done.11.refs_0_ = bf16[2,128,128]{2,1,0:T(8,128)(2,1)S(1)} collective-permute-done((bf16[2,128,128]{2,1,0:T(8,128)(2,1)S(1)}, bf16[2,128,128]{2,1,0:T(8,128)(2,1)S(1)}, u32[]{:S(2)}, u32[]{:S(2)}) %collective-permute-start.11) | collective-permute-done | bytes 65568 | tf_op jit(solution)/shard_map/ppermute | solution.py:303
  47.4 1.4 %collective-permute-done.12.refs_1_ = bf16[2,128,128]{2,1,0:T(8,128)(2,1)S(1)} collective-permute-done((bf16[2,128,128]{2,1,0:T(8,128)(2,1)S(1)}, bf16[2,128,128]{2,1,0:T(8,128)(2,1)S(1)}, u32[]{:S(2)}, u32[]{:S(2)}) %collective-permute-start.12) | collective-permute-done | bytes 65568 | tf_op jit(solution)/shard_map/ppermute | solution.py:303
  48.8 0.0 collective-permute-done.13.refs_2_
  48.8 0.9 %sum_unrotate.1 = (f32[256,128]{1,0:T(8,128)}, f32[1,256]{1,0:T(1,128)}) custom-call(s32[256,128]{1,0:T(8,128)S(1)} %get-tuple-element.29.sign_ref, bf16[2,128,128]{2,1,0:T(8,128)(2,1)S(1)} %collective-permute-done.11.refs_0_, bf16[2,128,128]{2,1,0:T(8,128)(2,1)S(1)} %collective-permute-done.12.refs_1_, ...), custom_call_target="tpu_custom_call" | custom-call | tf_op jit(solution)/shard_map/sum_unrotate/pallas_call | solution.py:274
Async XLA Ops:
  3.8 10.9 %collective-permute-start.3 = (bf16[4,128,128]{2,1,0:T(8,128)(2,1)S(1)}, bf16[4,128,128]{2,1,0:T(8,128)(2,1)S(1)}, u32[]{:S(2)}, u32[]{:S(2)}) collective-permute-start(bf16[4,128,128]{2,1,0:T(8,128)(2,1)S(1)} %get-tuple-element.20.refs_0_), channel_id=1, source_target_pairs={{0,3},{1,2},{2,1},{3,0},{4,7},{5,6},{6,5},{7,4},{8,11},{9,10},{10,... | collective-permute-start | bytes 393224 | tf_op jit(solution)/shard_map/ppermute | solution.py:297
  7.8 7.6 %collective-permute-start.4 = (bf16[4,128,128]{2,1,0:T(8,128)(2,1)S(1)}, bf16[4,128,128]{2,1,0:T(8,128)(2,1)S(1)}, u32[]{:S(2)}, u32[]{:S(2)}) collective-permute-start(bf16[4,128,128]{2,1,0:T(8,128)(2,1)S(1)} %get-tuple-element.21.refs_1_), channel_id=1, source_target_pairs={{0,2},{1,3},{2,0},{3,1},{4,6},{5,7},{6,4},{7,5},{8,10},{9,11},{10,... | collective-permute-start | bytes 393224 | tf_op jit(solution)/shard_map/ppermute | solution.py:297
  8.3 7.2 %collective-permute-start.5 = (bf16[4,128,128]{2,1,0:T(8,128)(2,1)S(1)}, bf16[4,128,128]{2,1,0:T(8,128)(2,1)S(1)}, u32[]{:S(2)}, u32[]{:S(2)}) collective-permute-start(bf16[4,128,128]{2,1,0:T(8,128)(2,1)S(1)} %get-tuple-element.22.refs_2_), channel_id=1, source_target_pairs={{0,1},{1,0},{2,3},{3,2},{4,5},{5,4},{6,7},{7,6},{8,9},{9,8},{10,11... | collective-permute-start | bytes 393224 | tf_op jit(solution)/shard_map/ppermute | solution.py:297
  8.5 14.8 %collective-permute-start.2 = (bf16[4,128,128]{2,1,0:T(8,128)(2,1)S(1)}, bf16[4,128,128]{2,1,0:T(8,128)(2,1)S(1)}, u32[]{:S(2)}, u32[]{:S(2)}) collective-permute-start(bf16[4,128,128]{2,1,0:T(8,128)(2,1)S(1)} %get-tuple-element.23.refs_3_), channel_id=1, source_target_pairs={{0,2},{1,3},{2,0},{3,1},{4,6},{5,7},{6,4},{7,5},{8,10},{9,11},{10,... | collective-permute-start | bytes 393224 | tf_op jit(solution)/shard_map/ppermute | solution.py:297
  13.2 10.5 %collective-permute-start = (bf16[4,128,128]{2,1,0:T(8,128)(2,1)S(1)}, bf16[4,128,128]{2,1,0:T(8,128)(2,1)S(1)}, u32[]{:S(2)}, u32[]{:S(2)}) collective-permute-start(bf16[4,128,128]{2,1,0:T(8,128)(2,1)S(1)} %get-tuple-element.24.refs_4_), channel_id=1, source_target_pairs={{0,3},{1,2},{2,1},{3,0},{4,7},{5,6},{6,5},{7,4},{8,11},{9,10},{10,... | collective-permute-start | bytes 393224 | tf_op jit(solution)/shard_map/ppermute | solution.py:297
  14.7 9.0 %collective-permute-start.1 = (bf16[4,128,128]{2,1,0:T(8,128)(2,1)S(1)}, bf16[4,128,128]{2,1,0:T(8,128)(2,1)S(1)}, u32[]{:S(2)}, u32[]{:S(2)}) collective-permute-start(bf16[4,128,128]{2,1,0:T(8,128)(2,1)S(1)} %get-tuple-element.25.refs_5_), channel_id=1, source_target_pairs={{0,1},{1,0},{2,3},{3,2},{4,5},{5,4},{6,7},{7,6},{8,9},{9,8},{10,11... | collective-permute-start | bytes 393224 | tf_op jit(solution)/shard_map/ppermute | solution.py:297
  15.5 14.8 %collective-permute-start.6 = (f32[4,128,128]{2,1,0:T(8,128)S(1)}, f32[4,128,128]{2,1,0:T(8,128)S(1)}, u32[]{:S(2)}, u32[]{:S(2)}) collective-permute-start(f32[4,128,128]{2,1,0:T(8,128)S(1)} %far_sum.2.refs_0_), channel_id=1, source_target_pairs={{0,4},{1,5},{2,6},{3,7},{4,0},{5,1},{6,2},{7,3},{8,12},{9,13},{10,... | collective-permute-start | bytes 786440 | tf_op jit(solution)/shard_map/ppermute | solution.py:319
  20.9 20.6 %collective-permute-start.8 = (bf16[4,256,128]{2,1,0:T(8,128)(2,1)S(1)}, bf16[4,256,128]{2,1,0:T(8,128)(2,1)S(1)}, u32[]{:S(2)}, u32[]{:S(2)}) collective-permute-start(bf16[4,256,128]{2,1,0:T(8,128)(2,1)S(1)} %get-tuple-element.27.refs_4_), channel_id=1, source_target_pairs={{0,3},{1,2},{2,1},{3,0},{4,7},{5,6},{6,5},{7,4},{8,11},{9,10},{10,... | collective-permute-start | bytes 786440 | tf_op jit(solution)/shard_map/ppermute | solution.py:297
  23.3 19.2 %collective-permute-start.9 = (bf16[4,256,128]{2,1,0:T(8,128)(2,1)S(1)}, bf16[4,256,128]{2,1,0:T(8,128)(2,1)S(1)}, u32[]{:S(2)}, u32[]{:S(2)}) collective-permute-start(bf16[4,256,128]{2,1,0:T(8,128)(2,1)S(1)} %get-tuple-element.28.refs_5_), channel_id=1, source_target_pairs={{0,2},{1,3},{2,0},{3,1},{4,6},{5,7},{6,4},{7,5},{8,10},{9,11},{10,... | collective-permute-start | bytes 786440 | tf_op jit(solution)/shard_map/ppermute | solution.py:297
  23.8 17.7 %collective-permute-start.7 = (f32[4,128,128]{2,1,0:T(8,128)S(1)}, f32[4,128,128]{2,1,0:T(8,128)S(1)}, u32[]{:S(2)}, u32[]{:S(2)}) collective-permute-start(f32[4,128,128]{2,1,0:T(8,128)S(1)} %far_sum.3.refs_0_), channel_id=1, source_target_pairs={{0,4},{1,5},{2,6},{3,7},{4,0},{5,1},{6,2},{7,3},{8,12},{9,13},{10,... | collective-permute-start | bytes 786440 | tf_op jit(solution)/shard_map/ppermute | solution.py:324
  28.3 14.2 %collective-permute-start.10 = (bf16[4,256,128]{2,1,0:T(8,128)(2,1)S(1)}, bf16[4,256,128]{2,1,0:T(8,128)(2,1)S(1)}, u32[]{:S(2)}, u32[]{:S(2)}) collective-permute-start(bf16[4,256,128]{2,1,0:T(8,128)(2,1)S(1)} %get-tuple-element.30), channel_id=1, source_target_pairs={{0,1},{1,0},{2,3},{3,2},{4,5},{5,4},{6,7},{7,6},{8,9},{9,8},{10,11... | collective-permute-start | bytes 786440 | tf_op jit(solution)/shard_map/ppermute | solution.py:297
  43.0 4.4 %collective-permute-start.11 = (bf16[2,128,128]{2,1,0:T(8,128)(2,1)S(1)}, bf16[2,128,128]{2,1,0:T(8,128)(2,1)S(1)}, u32[]{:S(2)}, u32[]{:S(2)}) collective-permute-start(bf16[2,128,128]{2,1,0:T(8,128)(2,1)S(1)} %get-tuple-element.32), channel_id=1, source_target_pairs={{0,24},{8,16},{16,8},{24,0},{1,25},{9,17},{17,9},{25,1},{2,26},{10... | collective-permute-start | bytes 196616 | tf_op jit(solution)/shard_map/ppermute | solution.py:303
  43.1 5.7 %collective-permute-start.12 = (bf16[2,128,128]{2,1,0:T(8,128)(2,1)S(1)}, bf16[2,128,128]{2,1,0:T(8,128)(2,1)S(1)}, u32[]{:S(2)}, u32[]{:S(2)}) collective-permute-start(bf16[2,128,128]{2,1,0:T(8,128)(2,1)S(1)} %get-tuple-element.33), channel_id=1, source_target_pairs={{0,16},{8,24},{16,0},{24,8},{1,17},{9,25},{17,1},{25,9},{2,18},{10... | collective-permute-start | bytes 196616 | tf_op jit(solution)/shard_map/ppermute | solution.py:303
  44.6 4.2 %collective-permute-start.13 = (bf16[2,128,128]{2,1,0:T(8,128)(2,1)S(1)}, bf16[2,128,128]{2,1,0:T(8,128)(2,1)S(1)}, u32[]{:S(2)}, u32[]{:S(2)}) collective-permute-start(bf16[2,128,128]{2,1,0:T(8,128)(2,1)S(1)} %get-tuple-element.34), channel_id=1, source_target_pairs={{0,8},{8,0},{16,24},{24,16},{1,9},{9,1},{17,25},{25,17},{2,10},{10... | collective-permute-start | bytes 196616 | tf_op jit(solution)/shard_map/ppermute | solution.py:303

commit v22 on v21

--- a/solution.py
+++ b/solution.py
@@ -151,7 +151,8 @@
 
     lax.fori_loop(0, layout.units // batch, body, 0)
     if signed_out:
-        out_refs[-1][...] = flips[0, 0, pl.ds(pl.multiple_of(inner * rows, rows), rows), :]
+        out_refs[-2][...] = flips[0, 0, pl.ds(pl.multiple_of(inner * rows, rows), rows), :]
+        out_refs[-1][...] = matrix[...]
 
 
 def rotate(values, signs, layout, other, steps, parts, signed_out=False, after=()):
@@ -162,6 +163,7 @@
     outs = [jax.ShapeDtypeStruct((units, len(wanted) * QGROUP, columns), jnp.bfloat16) for wanted in parts]
     if signed_out:
         outs.append(jax.ShapeDtypeStruct((layout.rows, LANES), jnp.int32))
+        outs.append(jax.ShapeDtypeStruct((ROT, ROT), jnp.bfloat16))
     return list(
         pl.pallas_call(
             functools.partial(rotate_kernel, layout, other, steps, parts, signed_out, len(after)),
@@ -245,7 +247,7 @@
     return terms
 
 
-def finish_kernel(sign_ref, *refs):
+def finish_kernel(matrix_ref, sign_ref, *refs):
     out_ref, max_ref = refs[-2:]
     second = [add_all([ref[half] for ref in refs[:-2]]) for half in range(HALVES)]
     blocks = second[0].shape[1]
@@ -258,7 +260,7 @@
         chosen = jnp.where(lane == HALVES * block + half, peak, 0.0)
         largest = jnp.maximum(largest, jnp.max(chosen, axis=0, keepdims=True))
     max_ref[...] = largest * jnp.float32(ROT**-0.5)
-    matrix = sylvester()
+    matrix = matrix_ref[...]
     high, middle, low = [
         jnp.dot(term, matrix, preferred_element_type=jnp.float32) for term in bfloat16_terms(natural)
     ]
@@ -269,7 +271,7 @@
         out_ref[at, :] = jnp.where(sign_ref[at, :] == 0, part, -part)
 
 
-def finish(parts, signs):
+def finish(parts, signs, matrix):
     rows = signs.shape[0]
     return pl.pallas_call(
         finish_kernel,
@@ -279,7 +281,7 @@
         ],
         compiler_params=pltpu.CompilerParams(vmem_limit_bytes=SUM_VMEM_LIMIT),
         name="sum_unrotate",
-    )(signs, *parts)
+    )(matrix, signs, *parts)
 
 
 def shards(partials, signs):
@@ -317,17 +319,17 @@
     early = far1
     first = far_sum(far0, layout, 0, [*early])
     across = [lax.ppermute(first, "local", counterparts)]
-    middle = others[:1] + [slow]
+    middle = order
     near = rotate(values, sign_rows, layout, False, middle, [whole] * len(middle), after=[first])
     far1 = [swap(part, step) for step, part in zip(others + [slow], far1 + [half1])] + [own]
-    second = far_sum(far1, layout, 1, [*near])
+    second = far_sum(far1, layout, 1, near[2:])
     across.append(lax.ppermute(second, "local", counterparts))
     ends = [step for step in others if step not in middle] + [0]
-    *outs, own_signs = rotate(
+    *outs, own_signs, matrix = rotate(
         values, sign_rows, layout, False, ends, [whole] * len(ends), signed_out=True, after=[second]
     )
     near = {step: swap(part, step) if step else part for step, part in zip(middle + ends, near + outs)}
-    reduced, rotated_max = finish(share(group_sum([near[step] for step in order + [0]], across, layout)), own_signs)
+    reduced, rotated_max = finish(share(group_sum([near[step] for step in order + [0]], across, layout)), own_signs, matrix)
     return (reduced.reshape(-1), rotated_max.reshape(-1))
 
 

time: 50 us -> 49.9 us (level)
  waiting for transfers between devices: 16.6 us -> 17.3 us
  starting transfers between devices: 19.4 us -> 18.9 us
    ppermute x9, waiting for transfers between devices: 1.45 us -> 13.4 us  [swap(): return lax.ppermute(part, 'local', pairs)]
    ppermute x1, waiting for transfers between devices: 11.2 us -> 0.01 us  [shards(): across.append(lax.ppermute(second, 'local', counterparts))]
    ppermute x1, starting transfers between devices: 1.7 us -> 1.16 us  [shards(): across.append(lax.ppermute(second, 'local', counterparts))]
where the time goes in v22:
time: 49.9 us; the launch traced here: 49.7 us
  starting transfers between devices  18.9 us (38%)
  waiting for transfers between devices  17.3 us (35%)
  Pallas kernels  12.9 us (26%)
  between operations  0.69 us (1%)
    ppermute x9, waiting for transfers between devices, swap(): return lax.ppermute(part, 'local', pairs)  13.4 us
    ppermute x9, starting transfers between devices, swap(): return lax.ppermute(part, 'local', pairs)  13.1 us
    pallas_call x4, Pallas kernels, rotate(): pl.pallas_call(functools.partial(rotate_kernel, layout, other, steps, par...  11.3 us
    ppermute x3, waiting for transfers between devices, share(): moved.append(lax.ppermute(parts[step], 'node', pairs))  3.94 us
    ppermute x1, starting transfers between devices, shards(): across = [lax.ppermute(first, 'local', counterparts)]  2.66 us
    ppermute x3, starting transfers between devices, share(): moved.append(lax.ppermute(parts[step], 'node', pairs))  1.93 us
    ppermute x1, starting transfers between devices, shards(): across.append(lax.ppermute(second, 'local', counterparts))  1.16 us
  transfers between devices with their start and end apart: 14, of which 5 were waited for; matrix products, arithmetic and copies ran while one was open for 0% of the time, Pallas kernels for 17%

profile of v22, /device:TPU:0, one launch (start us, length us, event | category | flops | bytes accessed | tf_op | source)
XLA Modules:
  0.0 49.7 jit_solution(6252849686281891590)
XLA Ops:
  0.6 3.2 %rotate_code.4 = (bf16[4,128,128]{2,1,0:T(8,128)(2,1)S(1)}, bf16[4,128,128]{2,1,0:T(8,128)(2,1)S(1)}, bf16[4,128,128]{2,1,0:T(8,128)(2,1)S(1)}, bf16[4,128,128]{2,1,0:T(8,128)(2,1)S(1)}) custom-call(bf16[1,1048576]{1,0:T(2,128)(2,1)} %bitcast.4, s32[8192,128]{1,0:T(8,128)} %bitcast.8), custom_call_target="tpu_custom_call" | custom-call | flops 268435456 | bytes 5242880 | tf_op jit(solution)/shard_map/rotate_code/pallas_call | solution.py:168
  3.8 4.1 %collective-permute-start.3 = (bf16[4,128,128]{2,1,0:T(8,128)(2,1)S(1)}, bf16[4,128,128]{2,1,0:T(8,128)(2,1)S(1)}, u32[]{:S(2)}, u32[]{:S(2)}) collective-permute-start(bf16[4,128,128]{2,1,0:T(8,128)(2,1)S(1)} %get-tuple-element.21.refs_0_), channel_id=1, source_target_pairs={{0,3},{1,2},{2,1},{3,0},{4,7},{5,6},{6,5},{7,4},{8,11},{9,10},{10,... | collective-permute-start | bytes 393224 | tf_op jit(solution)/shard_map/ppermute | solution.py:299
  7.8 0.4 collective-permute-start.4
  8.3 0.2 collective-permute-start.5
  8.5 1.9 %collective-permute-start.2 = (bf16[4,128,128]{2,1,0:T(8,128)(2,1)S(1)}, bf16[4,128,128]{2,1,0:T(8,128)(2,1)S(1)}, u32[]{:S(2)}, u32[]{:S(2)}) collective-permute-start(bf16[4,128,128]{2,1,0:T(8,128)(2,1)S(1)} %get-tuple-element.24.refs_3_), channel_id=1, source_target_pairs={{0,2},{1,3},{2,0},{3,1},{4,6},{5,7},{6,4},{7,5},{8,10},{9,11},{10,... | collective-permute-start | bytes 393224 | tf_op jit(solution)/shard_map/ppermute | solution.py:299
  10.4 2.9 %rotate_code.5 = (bf16[4,128,128]{2,1,0:T(8,128)(2,1)S(1)}, bf16[4,128,128]{2,1,0:T(8,128)(2,1)S(1)}, bf16[4,256,128]{2,1,0:T(8,128)(2,1)S(1)}) custom-call(bf16[1,1048576]{1,0:T(2,128)(2,1)} %bitcast.5, s32[8192,128]{1,0:T(8,128)} %bitcast.9, bf16[4,128,128]{2,1,0:T(8,128)(2,1)S(1)} %get-tuple-element.21.refs_0_, ...), custom_call_target="tpu_custom_call" | custom-call | flops 201326592 | bytes 3932160 | tf_op jit(solution)/shard_map/rotate_code/pallas_call | solution.py:168
  13.2 1.5 %collective-permute-start = (bf16[4,128,128]{2,1,0:T(8,128)(2,1)S(1)}, bf16[4,128,128]{2,1,0:T(8,128)(2,1)S(1)}, u32[]{:S(2)}, u32[]{:S(2)}) collective-permute-start(bf16[4,128,128]{2,1,0:T(8,128)(2,1)S(1)} %get-tuple-element.25.refs_4_), channel_id=1, source_target_pairs={{0,3},{1,2},{2,1},{3,0},{4,7},{5,6},{6,5},{7,4},{8,11},{9,10},{10,... | collective-permute-start | bytes 393224 | tf_op jit(solution)/shard_map/ppermute | solution.py:299
  14.7 0.0 collective-permute-done.3.refs_0_
  14.7 0.2 collective-permute-start.1
  14.9 0.5 %collective-permute-done.4.refs_1_ = bf16[4,128,128]{2,1,0:T(8,128)(2,1)S(1)} collective-permute-done((bf16[4,128,128]{2,1,0:T(8,128)(2,1)S(1)}, bf16[4,128,128]{2,1,0:T(8,128)(2,1)S(1)}, u32[]{:S(2)}, u32[]{:S(2)}) %collective-permute-start.4) | collective-permute-done | bytes 131104 | tf_op jit(solution)/shard_map/ppermute | solution.py:299
  15.5 0.0 collective-permute-done.5.refs_2_
  15.5 0.1 far_sum.2.refs_0_
  15.5 2.7 %collective-permute-start.6 = (f32[4,128,128]{2,1,0:T(8,128)S(1)}, f32[4,128,128]{2,1,0:T(8,128)S(1)}, u32[]{:S(2)}, u32[]{:S(2)}) collective-permute-start(f32[4,128,128]{2,1,0:T(8,128)S(1)} %far_sum.2.refs_0_), channel_id=1, source_target_pairs={{0,4},{1,5},{2,6},{3,7},{4,0},{5,1},{6,2},{7,3},{8,12},{9,13},{10,... | collective-permute-start | bytes 786440 | tf_op jit(solution)/shard_map/ppermute | solution.py:321
  18.2 3.3 %rotate_code.6 = (bf16[4,256,128]{2,1,0:T(8,128)(2,1)S(1)}, bf16[4,256,128]{2,1,0:T(8,128)(2,1)S(1)}, bf16[4,256,128]{2,1,0:T(8,128)(2,1)S(1)}) custom-call(bf16[1,1048576]{1,0:T(2,128)(2,1)} %bitcast.6, s32[8192,128]{1,0:T(8,128)} %bitcast.10, f32[4,128,128]{2,1,0:T(8,128)S(1)} %far_sum.2.refs_0_), custom_call_target="tpu_custom_call" | custom-call | flops 201326592 | bytes 3932160 | tf_op jit(solution)/shard_map/rotate_code/pallas_call | solution.py:168
  21.5 2.4 %collective-permute-start.8 = (bf16[4,256,128]{2,1,0:T(8,128)(2,1)S(1)}, bf16[4,256,128]{2,1,0:T(8,128)(2,1)S(1)}, u32[]{:S(2)}, u32[]{:S(2)}) collective-permute-start(bf16[4,256,128]{2,1,0:T(8,128)(2,1)S(1)} %get-tuple-element.31), channel_id=1, source_target_pairs={{0,3},{1,2},{2,1},{3,0},{4,7},{5,6},{6,5},{7,4},{8,11},{9,10},{10,... | collective-permute-start | bytes 786440 | tf_op jit(solution)/shard_map/ppermute | solution.py:299
  23.8 0.0 collective-permute-done.2.refs_2_
  23.8 0.5 collective-permute-start.9
  24.3 0.0 collective-permute-done.refs_0_
  24.3 0.0 collective-permute-done.1.refs_1_
  24.3 0.1 far_sum.3.refs_0_
  24.4 1.2 %collective-permute-start.7 = (f32[4,128,128]{2,1,0:T(8,128)S(1)}, f32[4,128,128]{2,1,0:T(8,128)S(1)}, u32[]{:S(2)}, u32[]{:S(2)}) collective-permute-start(f32[4,128,128]{2,1,0:T(8,128)S(1)} %far_sum.3.refs_0_), channel_id=1, source_target_pairs={{0,4},{1,5},{2,6},{3,7},{4,0},{5,1},{6,2},{7,3},{8,12},{9,13},{10,... | collective-permute-start | bytes 786440 | tf_op jit(solution)/shard_map/ppermute | solution.py:326
  25.5 2.0 %collective-permute-start.10 = (bf16[4,256,128]{2,1,0:T(8,128)(2,1)S(1)}, bf16[4,256,128]{2,1,0:T(8,128)(2,1)S(1)}, u32[]{:S(2)}, u32[]{:S(2)}) collective-permute-start(bf16[4,256,128]{2,1,0:T(8,128)(2,1)S(1)} %get-tuple-element.28.refs_4_), channel_id=1, source_target_pairs={{0,1},{1,0},{2,3},{3,2},{4,5},{5,4},{6,7},{7,6},{8,9},{9,8},{10,11... | collective-permute-start | bytes 786440 | tf_op jit(solution)/shard_map/ppermute | solution.py:299
  27.6 2.0 %rotate_code.7 = (bf16[4,256,128]{2,1,0:T(8,128)(2,1)S(1)}, s32[256,128]{1,0:T(8,128)S(1)}, bf16[256,256]{1,0:T(8,128)(2,1)S(1)}) custom-call(bf16[1,1048576]{1,0:T(2,128)(2,1)} %bitcast.7, s32[8192,128]{1,0:T(8,128)} %bitcast.11, f32[4,128,128]{2,1,0:T(8,128)S(1)} %far_sum.3.refs_0_), custom_call_target="tpu_custom_call" | custom-call | flops 67108864 | bytes 1310720 | tf_op jit(solution)/shard_map/rotate_code/pallas_call | solution.py:168
  29.6 0.0 collective-permute-done.6.refs_0_
  29.6 10.2 %collective-permute-done.8.refs_2_ = bf16[4,256,128]{2,1,0:T(8,128)(2,1)S(1)} collective-permute-done((bf16[4,256,128]{2,1,0:T(8,128)(2,1)S(1)}, bf16[4,256,128]{2,1,0:T(8,128)(2,1)S(1)}, u32[]{:S(2)}, u32[]{:S(2)}) %collective-permute-start.8) | collective-permute-done | bytes 262176 | tf_op jit(solution)/shard_map/ppermute | solution.py:299
  39.8 2.6 %collective-permute-done.9.refs_3_ = bf16[4,256,128]{2,1,0:T(8,128)(2,1)S(1)} collective-permute-done((bf16[4,256,128]{2,1,0:T(8,128)(2,1)S(1)}, bf16[4,256,128]{2,1,0:T(8,128)(2,1)S(1)}, u32[]{:S(2)}, u32[]{:S(2)}) %collective-permute-start.9) | collective-permute-done | bytes 262176 | tf_op jit(solution)/shard_map/ppermute | solution.py:299
  42.4 0.0 collective-permute-done.7.refs_1_
  42.4 0.0 collective-permute-done.10.refs_4_
  42.4 0.5 %group_sum_code.1 = (bf16[2,128,128]{2,1,0:T(8,128)(2,1)S(1)}, bf16[2,128,128]{2,1,0:T(8,128)(2,1)S(1)}, bf16[2,128,128]{2,1,0:T(8,128)(2,1)S(1)}, bf16[2,128,128]{2,1,0:T(8,128)(2,1)S(1)}) custom-call(f32[4,128,128]{2,1,0:T(8,128)S(1)} %collective-permute-done.6.refs_0_, f32[4,128,128]{2,1,0:T(8,128)S(1)} %collective-permute-done.7.refs_1_, ...), custom_call_target="tpu_custom_call" | custom-call | flops 3932160 | bytes 1835008 | tf_op jit(solution)/shard_map/group_sum_code/pallas_call | solution.py:231
  42.9 0.1 collective-permute-start.11
  43.0 1.5 %collective-permute-start.12 = (bf16[2,128,128]{2,1,0:T(8,128)(2,1)S(1)}, bf16[2,128,128]{2,1,0:T(8,128)(2,1)S(1)}, u32[]{:S(2)}, u32[]{:S(2)}) collective-permute-start(bf16[2,128,128]{2,1,0:T(8,128)(2,1)S(1)} %get-tuple-element.35), channel_id=1, source_target_pairs={{0,16},{8,24},{16,0},{24,8},{1,17},{9,25},{17,1},{25,9},{2,18},{10... | collective-permute-start | bytes 196616 | tf_op jit(solution)/shard_map/ppermute | solution.py:305
  44.5 0.3 collective-permute-start.13
  44.8 2.5 %collective-permute-done.11.refs_0_ = bf16[2,128,128]{2,1,0:T(8,128)(2,1)S(1)} collective-permute-done((bf16[2,128,128]{2,1,0:T(8,128)(2,1)S(1)}, bf16[2,128,128]{2,1,0:T(8,128)(2,1)S(1)}, u32[]{:S(2)}, u32[]{:S(2)}) %collective-permute-start.11) | collective-permute-done | bytes 65568 | tf_op jit(solution)/shard_map/ppermute | solution.py:305
  47.3 1.4 %collective-permute-done.12.refs_1_ = bf16[2,128,128]{2,1,0:T(8,128)(2,1)S(1)} collective-permute-done((bf16[2,128,128]{2,1,0:T(8,128)(2,1)S(1)}, bf16[2,128,128]{2,1,0:T(8,128)(2,1)S(1)}, u32[]{:S(2)}, u32[]{:S(2)}) %collective-permute-start.12) | collective-permute-done | bytes 65568 | tf_op jit(solution)/shard_map/ppermute | solution.py:305
  48.8 0.0 collective-permute-done.13.refs_2_
  48.8 0.9 %sum_unrotate.1 = (f32[256,128]{1,0:T(8,128)}, f32[1,256]{1,0:T(1,128)}) custom-call(bf16[256,256]{1,0:T(8,128)(2,1)S(1)} %get-tuple-element.29.matrix_ref, s32[256,128]{1,0:T(8,128)S(1)} %get-tuple-element.30.sign_ref, bf16[2,128,128]{2,1,0:T(8,128)(2,1)S(1)} %collective-permute-done.11.refs_0_, bf16[2,128,128]{2,1,0:T(8,128)(2,1)S(1)} %collective-permute-done.12.refs_1_, ...), custom_call_target="tpu_custom_call" | custom-call | tf_op jit(solution)/shard_map/sum_unrotate/pallas_call | solution.py:276
Async XLA Ops:
  3.8 10.9 %collective-permute-start.3 = (bf16[4,128,128]{2,1,0:T(8,128)(2,1)S(1)}, bf16[4,128,128]{2,1,0:T(8,128)(2,1)S(1)}, u32[]{:S(2)}, u32[]{:S(2)}) collective-permute-start(bf16[4,128,128]{2,1,0:T(8,128)(2,1)S(1)} %get-tuple-element.21.refs_0_), channel_id=1, source_target_pairs={{0,3},{1,2},{2,1},{3,0},{4,7},{5,6},{6,5},{7,4},{8,11},{9,10},{10,... | collective-permute-start | bytes 393224 | tf_op jit(solution)/shard_map/ppermute | solution.py:299
  7.8 7.6 %collective-permute-start.4 = (bf16[4,128,128]{2,1,0:T(8,128)(2,1)S(1)}, bf16[4,128,128]{2,1,0:T(8,128)(2,1)S(1)}, u32[]{:S(2)}, u32[]{:S(2)}) collective-permute-start(bf16[4,128,128]{2,1,0:T(8,128)(2,1)S(1)} %get-tuple-element.22.refs_1_), channel_id=1, source_target_pairs={{0,2},{1,3},{2,0},{3,1},{4,6},{5,7},{6,4},{7,5},{8,10},{9,11},{10,... | collective-permute-start | bytes 393224 | tf_op jit(solution)/shard_map/ppermute | solution.py:299
  8.3 7.2 %collective-permute-start.5 = (bf16[4,128,128]{2,1,0:T(8,128)(2,1)S(1)}, bf16[4,128,128]{2,1,0:T(8,128)(2,1)S(1)}, u32[]{:S(2)}, u32[]{:S(2)}) collective-permute-start(bf16[4,128,128]{2,1,0:T(8,128)(2,1)S(1)} %get-tuple-element.23.refs_2_), channel_id=1, source_target_pairs={{0,1},{1,0},{2,3},{3,2},{4,5},{5,4},{6,7},{7,6},{8,9},{9,8},{10,11... | collective-permute-start | bytes 393224 | tf_op jit(solution)/shard_map/ppermute | solution.py:299
  8.5 15.3 %collective-permute-start.2 = (bf16[4,128,128]{2,1,0:T(8,128)(2,1)S(1)}, bf16[4,128,128]{2,1,0:T(8,128)(2,1)S(1)}, u32[]{:S(2)}, u32[]{:S(2)}) collective-permute-start(bf16[4,128,128]{2,1,0:T(8,128)(2,1)S(1)} %get-tuple-element.24.refs_3_), channel_id=1, source_target_pairs={{0,2},{1,3},{2,0},{3,1},{4,6},{5,7},{6,4},{7,5},{8,10},{9,11},{10,... | collective-permute-start | bytes 393224 | tf_op jit(solution)/shard_map/ppermute | solution.py:299
  13.2 11.0 %collective-permute-start = (bf16[4,128,128]{2,1,0:T(8,128)(2,1)S(1)}, bf16[4,128,128]{2,1,0:T(8,128)(2,1)S(1)}, u32[]{:S(2)}, u32[]{:S(2)}) collective-permute-start(bf16[4,128,128]{2,1,0:T(8,128)(2,1)S(1)} %get-tuple-element.25.refs_4_), channel_id=1, source_target_pairs={{0,3},{1,2},{2,1},{3,0},{4,7},{5,6},{6,5},{7,4},{8,11},{9,10},{10,... | collective-permute-start | bytes 393224 | tf_op jit(solution)/shard_map/ppermute | solution.py:299
  14.7 9.6 %collective-permute-start.1 = (bf16[4,128,128]{2,1,0:T(8,128)(2,1)S(1)}, bf16[4,128,128]{2,1,0:T(8,128)(2,1)S(1)}, u32[]{:S(2)}, u32[]{:S(2)}) collective-permute-start(bf16[4,128,128]{2,1,0:T(8,128)(2,1)S(1)} %get-tuple-element.26.refs_5_), channel_id=1, source_target_pairs={{0,1},{1,0},{2,3},{3,2},{4,5},{5,4},{6,7},{7,6},{8,9},{9,8},{10,11... | collective-permute-start | bytes 393224 | tf_op jit(solution)/shard_map/ppermute | solution.py:299
  15.5 14.1 %collective-permute-start.6 = (f32[4,128,128]{2,1,0:T(8,128)S(1)}, f32[4,128,128]{2,1,0:T(8,128)S(1)}, u32[]{:S(2)}, u32[]{:S(2)}) collective-permute-start(f32[4,128,128]{2,1,0:T(8,128)S(1)} %far_sum.2.refs_0_), channel_id=1, source_target_pairs={{0,4},{1,5},{2,6},{3,7},{4,0},{5,1},{6,2},{7,3},{8,12},{9,13},{10,... | collective-permute-start | bytes 786440 | tf_op jit(solution)/shard_map/ppermute | solution.py:321
  21.5 18.3 %collective-permute-start.8 = (bf16[4,256,128]{2,1,0:T(8,128)(2,1)S(1)}, bf16[4,256,128]{2,1,0:T(8,128)(2,1)S(1)}, u32[]{:S(2)}, u32[]{:S(2)}) collective-permute-start(bf16[4,256,128]{2,1,0:T(8,128)(2,1)S(1)} %get-tuple-element.31), channel_id=1, source_target_pairs={{0,3},{1,2},{2,1},{3,0},{4,7},{5,6},{6,5},{7,4},{8,11},{9,10},{10,... | collective-permute-start | bytes 786440 | tf_op jit(solution)/shard_map/ppermute | solution.py:299
  23.8 18.6 %collective-permute-start.9 = (bf16[4,256,128]{2,1,0:T(8,128)(2,1)S(1)}, bf16[4,256,128]{2,1,0:T(8,128)(2,1)S(1)}, u32[]{:S(2)}, u32[]{:S(2)}) collective-permute-start(bf16[4,256,128]{2,1,0:T(8,128)(2,1)S(1)} %get-tuple-element.32), channel_id=1, source_target_pairs={{0,2},{1,3},{2,0},{3,1},{4,6},{5,7},{6,4},{7,5},{8,10},{9,11},{10,... | collective-permute-start | bytes 786440 | tf_op jit(solution)/shard_map/ppermute | solution.py:299
  24.4 18.1 %collective-permute-start.7 = (f32[4,128,128]{2,1,0:T(8,128)S(1)}, f32[4,128,128]{2,1,0:T(8,128)S(1)}, u32[]{:S(2)}, u32[]{:S(2)}) collective-permute-start(f32[4,128,128]{2,1,0:T(8,128)S(1)} %far_sum.3.refs_0_), channel_id=1, source_target_pairs={{0,4},{1,5},{2,6},{3,7},{4,0},{5,1},{6,2},{7,3},{8,12},{9,13},{10,... | collective-permute-start | bytes 786440 | tf_op jit(solution)/shard_map/ppermute | solution.py:326
  25.5 16.9 %collective-permute-start.10 = (bf16[4,256,128]{2,1,0:T(8,128)(2,1)S(1)}, bf16[4,256,128]{2,1,0:T(8,128)(2,1)S(1)}, u32[]{:S(2)}, u32[]{:S(2)}) collective-permute-start(bf16[4,256,128]{2,1,0:T(8,128)(2,1)S(1)} %get-tuple-element.28.refs_4_), channel_id=1, source_target_pairs={{0,1},{1,0},{2,3},{3,2},{4,5},{5,4},{6,7},{7,6},{8,9},{9,8},{10,11... | collective-permute-start | bytes 786440 | tf_op jit(solution)/shard_map/ppermute | solution.py:299
  42.9 4.4 %collective-permute-start.11 = (bf16[2,128,128]{2,1,0:T(8,128)(2,1)S(1)}, bf16[2,128,128]{2,1,0:T(8,128)(2,1)S(1)}, u32[]{:S(2)}, u32[]{:S(2)}) collective-permute-start(bf16[2,128,128]{2,1,0:T(8,128)(2,1)S(1)} %get-tuple-element.34), channel_id=1, source_target_pairs={{0,24},{8,16},{16,8},{24,0},{1,25},{9,17},{17,9},{25,1},{2,26},{10... | collective-permute-start | bytes 196616 | tf_op jit(solution)/shard_map/ppermute | solution.py:305
  43.0 5.7 %collective-permute-start.12 = (bf16[2,128,128]{2,1,0:T(8,128)(2,1)S(1)}, bf16[2,128,128]{2,1,0:T(8,128)(2,1)S(1)}, u32[]{:S(2)}, u32[]{:S(2)}) collective-permute-start(bf16[2,128,128]{2,1,0:T(8,128)(2,1)S(1)} %get-tuple-element.35), channel_id=1, source_target_pairs={{0,16},{8,24},{16,0},{24,8},{1,17},{9,25},{17,1},{25,9},{2,18},{10... | collective-permute-start | bytes 196616 | tf_op jit(solution)/shard_map/ppermute | solution.py:305
  44.5 4.2 %collective-permute-start.13 = (bf16[2,128,128]{2,1,0:T(8,128)(2,1)S(1)}, bf16[2,128,128]{2,1,0:T(8,128)(2,1)S(1)}, u32[]{:S(2)}, u32[]{:S(2)}) collective-permute-start(bf16[2,128,128]{2,1,0:T(8,128)(2,1)S(1)} %get-tuple-element.36), channel_id=1, source_target_pairs={{0,8},{8,0},{16,24},{24,16},{1,9},{9,1},{17,25},{25,17},{2,10},{10... | collective-permute-start | bytes 196616 | tf_op jit(solution)/shard_map/ppermute | solution.py:305

commit v23 on v20

--- a/solution.py
+++ b/solution.py
@@ -214,27 +214,28 @@
     )(*parts, *after)
 
 
-def group_sum_kernel(layout, *refs):
-    across_refs, near_refs, out_refs = refs[:HALVES], refs[HALVES : HALVES + layout.half], refs[HALVES + layout.half :]
-    for half, across_ref in enumerate(across_refs):
-        near = [ref[:, half * QGROUP : (half + 1) * QGROUP] for ref in near_refs]
-        first = recode(add_all(near + [across_ref[...]])).astype(jnp.bfloat16)
-        for section, out_ref in enumerate(out_refs):
-            at = section % layout.together * layout.blocks
-            out_ref[half] = first[section // layout.together, :, at : at + layout.blocks]
-
-
-def group_sum(near, across, layout):
-    size = near[0].size
+def group_sum_kernel(layout, part, count, *refs):
+    arrays = []
+    for ref in refs[:count]:
+        cut = ref.shape[1] == QGROUP
+        arrays.append(ref[...] if cut else ref[:, part * QGROUP : (part + 1) * QGROUP])
+    first = recode(add_all(arrays)).astype(jnp.bfloat16)
+    for section, out_ref in enumerate(refs[count:]):
+        at = section % layout.together * layout.blocks
+        out_ref[...] = first[section // layout.together, :, at : at + layout.blocks]
+
+
+def group_sum(parts, layout, part):
+    size = QGROUP * layout.units * layout.columns
     return pl.pallas_call(
-        functools.partial(group_sum_kernel, layout),
-        out_shape=[jax.ShapeDtypeStruct((HALVES, QGROUP, layout.blocks), jnp.bfloat16)] * layout.groups,
+        functools.partial(group_sum_kernel, layout, part, len(parts)),
+        out_shape=[jax.ShapeDtypeStruct((QGROUP, layout.blocks), jnp.bfloat16)] * layout.groups,
         compiler_params=pltpu.CompilerParams(vmem_limit_bytes=SUM_VMEM_LIMIT),
         cost_estimate=pl.CostEstimate(
-            flops=30 * size, bytes_accessed=2 * (layout.half + 3) * size, transcendentals=0
+            flops=30 * size, bytes_accessed=2 * (len(parts) + 2) * size, transcendentals=0
         ),
         name="group_sum_code",
-    )(*across, *near)
+    )(*parts)
 
 
 def bfloat16_terms(values):
@@ -247,7 +248,8 @@
 
 def finish_kernel(sign_ref, *refs):
     out_ref, max_ref = refs[-2:]
-    second = [add_all([ref[half] for ref in refs[:-2]]) for half in range(HALVES)]
+    count = (len(refs) - 2) // HALVES
+    second = [add_all([ref[...] for ref in refs[half * count : (half + 1) * count]]) for half in range(HALVES)]
     blocks = second[0].shape[1]
     natural = jnp.concatenate([part.T for part in second], axis=1)
     block = lax.broadcasted_iota(jnp.int32, (blocks, HALVES * blocks), 0)
@@ -323,12 +325,24 @@
     far1 = [swap(part, step) for step, part in zip(others + [slow], far1 + [half1])] + [own]
     second = far_sum(far1, layout, 1, [*near])
     across.append(lax.ppermute(second, "local", counterparts))
-    ends = [step for step in others if step not in middle] + [0]
-    *outs, own_signs = rotate(
-        values, sign_rows, layout, False, ends, [whole] * len(ends), signed_out=True, after=[second]
+    ends = [step for step in others if step not in middle]
+    *outs, own, own_signs = rotate(
+        values,
+        sign_rows,
+        layout,
+        False,
+        ends + ends + [0],
+        [(0,)] * len(ends) + [(1,)] * len(ends) + [whole],
+        signed_out=True,
+        after=[first],
     )
-    near = {step: swap(part, step) if step else part for step, part in zip(middle + ends, near + outs)}
-    reduced, rotated_max = finish(share(group_sum([near[step] for step in order + [0]], across, layout)), own_signs)
+    near = [swap(part, step) for step, part in zip(middle, near)] + [own]
+    outs = [swap(part, step) for step, part in zip(ends + ends, outs)]
+    coded = []
+    for part in range(HALVES):
+        cut = outs[part * len(ends) : (part + 1) * len(ends)]
+        coded += share(group_sum(near + cut + [across[part]], layout, part))
+    reduced, rotated_max = finish(coded, own_signs)
     return (reduced.reshape(-1), rotated_max.reshape(-1))
 
 

time: 49.8 us -> 51 us (1.024)
  waiting for transfers between devices: 15 us -> 16.8 us
    ppermute x9 -> x10, waiting for transfers between devices: 3.68 us -> 14.6 us  [swap(): return lax.ppermute(part, 'local', pairs)]
    ppermute x1, waiting for transfers between devices: 7.6 us -> 0.01 us  [shards(): across.append(lax.ppermute(second, 'local', counterparts))]
    ppermute x9 -> x10, starting transfers between devices: 14.5 us -> 11.8 us  [swap(): return lax.ppermute(part, 'local', pairs)]
    ppermute x3 -> x6, starting transfers between devices: 1.93 us -> 3.84 us  [share(): moved.append(lax.ppermute(parts[step], 'node', pairs))]
    ppermute x3 -> x6, waiting for transfers between devices: 3.71 us -> 2.13 us  [share(): moved.append(lax.ppermute(parts[step], 'node', pairs))]
  transfers between devices with their start and end apart: 14 -> 18, of which waited for: 6 -> 6; matrix products, arithmetic and copies ran while one was open for 0% -> 0% of each run, Pallas kernels for 18% -> 18%
where the time goes in v23:
time: 51 us; the launch traced here: 50.8 us
  starting transfers between devices  20 us (39%)
  waiting for transfers between devices  16.8 us (33%)
  Pallas kernels  13.3 us (26%)
  between operations  0.73 us (1%)
    ppermute x10, waiting for transfers between devices, swap(): return lax.ppermute(part, 'local', pairs)  14.6 us
    ppermute x10, starting transfers between devices, swap(): return lax.ppermute(part, 'local', pairs)  11.8 us
    pallas_call x4, Pallas kernels, rotate(): pl.pallas_call(functools.partial(rotate_kernel, layout, other, steps, par...  11.7 us
    ppermute x6, starting transfers between devices, share(): moved.append(lax.ppermute(parts[step], 'node', pairs))  3.84 us
    ppermute x1, starting transfers between devices, shards(): across = [lax.ppermute(first, 'local', counterparts)]  2.66 us
    ppermute x6, waiting for transfers between devices, share(): moved.append(lax.ppermute(parts[step], 'node', pairs))  2.13 us
    ppermute x1, starting transfers between devices, shards(): across.append(lax.ppermute(second, 'local', counterparts))  1.77 us
  transfers between devices with their start and end apart: 18, of which 6 were waited for; matrix products, arithmetic and copies ran while one was open for 0% of the time, Pallas kernels for 18%

profile of v23, /device:TPU:0, one launch (start us, length us, event | category | flops | bytes accessed | tf_op | source)
XLA Modules:
  0.0 50.8 jit_solution(17112869467238270713)
XLA Ops:
  0.6 3.2 %rotate_code.4 = (bf16[4,128,128]{2,1,0:T(8,128)(2,1)S(1)}, bf16[4,128,128]{2,1,0:T(8,128)(2,1)S(1)}, bf16[4,128,128]{2,1,0:T(8,128)(2,1)S(1)}, bf16[4,128,128]{2,1,0:T(8,128)(2,1)S(1)}) custom-call(bf16[1,1048576]{1,0:T(2,128)(2,1)} %bitcast.4, s32[8192,128]{1,0:T(8,128)} %bitcast.8), custom_call_target="tpu_custom_call" | custom-call | flops 268435456 | bytes 5242880 | tf_op jit(solution)/shard_map/rotate_code/pallas_call | solution.py:166
  3.8 4.1 %collective-permute-start = (bf16[4,128,128]{2,1,0:T(8,128)(2,1)S(1)}, bf16[4,128,128]{2,1,0:T(8,128)(2,1)S(1)}, u32[]{:S(2)}, u32[]{:S(2)}) collective-permute-start(bf16[4,128,128]{2,1,0:T(8,128)(2,1)S(1)} %get-tuple-element.25.refs_0_), channel_id=1, source_target_pairs={{0,3},{1,2},{2,1},{3,0},{4,7},{5,6},{6,5},{7,4},{8,11},{9,10},{10,... | collective-permute-start | bytes 393224 | tf_op jit(solution)/shard_map/ppermute | solution.py:299
  7.8 0.4 collective-permute-start.1
  8.3 0.2 collective-permute-start.2
  8.5 1.9 %collective-permute-start.13 = (bf16[4,128,128]{2,1,0:T(8,128)(2,1)S(1)}, bf16[4,128,128]{2,1,0:T(8,128)(2,1)S(1)}, u32[]{:S(2)}, u32[]{:S(2)}) collective-permute-start(bf16[4,128,128]{2,1,0:T(8,128)(2,1)S(1)} %get-tuple-element.28.refs_3_), channel_id=1, source_target_pairs={{0,2},{1,3},{2,0},{3,1},{4,6},{5,7},{6,4},{7,5},{8,10},{9,11},{10,... | collective-permute-start | bytes 393224 | tf_op jit(solution)/shard_map/ppermute | solution.py:299
  10.4 2.9 %rotate_code.5 = (bf16[4,128,128]{2,1,0:T(8,128)(2,1)S(1)}, bf16[4,128,128]{2,1,0:T(8,128)(2,1)S(1)}, bf16[4,256,128]{2,1,0:T(8,128)(2,1)S(1)}) custom-call(bf16[1,1048576]{1,0:T(2,128)(2,1)} %bitcast.5, s32[8192,128]{1,0:T(8,128)} %bitcast.9, bf16[4,128,128]{2,1,0:T(8,128)(2,1)S(1)} %get-tuple-element.25.refs_0_, ...), custom_call_target="tpu_custom_call" | custom-call | flops 201326592 | bytes 3932160 | tf_op jit(solution)/shard_map/rotate_code/pallas_call | solution.py:166
  13.2 1.5 %collective-permute-start.11 = (bf16[4,128,128]{2,1,0:T(8,128)(2,1)S(1)}, bf16[4,128,128]{2,1,0:T(8,128)(2,1)S(1)}, u32[]{:S(2)}, u32[]{:S(2)}) collective-permute-start(bf16[4,128,128]{2,1,0:T(8,128)(2,1)S(1)} %get-tuple-element.30.refs_4_), channel_id=1, source_target_pairs={{0,3},{1,2},{2,1},{3,0},{4,7},{5,6},{6,5},{7,4},{8,11},{9,10},{10,... | collective-permute-start | bytes 393224 | tf_op jit(solution)/shard_map/ppermute | solution.py:299
  14.7 0.0 collective-permute-done.refs_0_
  14.7 0.2 collective-permute-start.12
  14.9 0.5 %collective-permute-done.1.refs_1_ = bf16[4,128,128]{2,1,0:T(8,128)(2,1)S(1)} collective-permute-done((bf16[4,128,128]{2,1,0:T(8,128)(2,1)S(1)}, bf16[4,128,128]{2,1,0:T(8,128)(2,1)S(1)}, u32[]{:S(2)}, u32[]{:S(2)}) %collective-permute-start.1) | collective-permute-done | bytes 131104 | tf_op jit(solution)/shard_map/ppermute | solution.py:299
  15.5 0.0 collective-permute-done.2.refs_2_
  15.5 0.1 far_sum.2.refs_0_
  15.5 2.7 %collective-permute-start.6 = (f32[4,128,128]{2,1,0:T(8,128)S(1)}, f32[4,128,128]{2,1,0:T(8,128)S(1)}, u32[]{:S(2)}, u32[]{:S(2)}) collective-permute-start(f32[4,128,128]{2,1,0:T(8,128)S(1)} %far_sum.2.refs_0_), channel_id=1, source_target_pairs={{0,4},{1,5},{2,6},{3,7},{4,0},{5,1},{6,2},{7,3},{8,12},{9,13},{10,... | collective-permute-start | bytes 786440 | tf_op jit(solution)/shard_map/ppermute | solution.py:322
  18.2 2.9 %rotate_code.7 = (bf16[4,256,128]{2,1,0:T(8,128)(2,1)S(1)}, bf16[4,256,128]{2,1,0:T(8,128)(2,1)S(1)}) custom-call(bf16[1,1048576]{1,0:T(2,128)(2,1)} %bitcast.6, s32[8192,128]{1,0:T(8,128)} %bitcast.10, f32[4,128,128]{2,1,0:T(8,128)S(1)} %far_sum.2.refs_0_), custom_call_target="tpu_custom_call" | custom-call | flops 134217728 | bytes 2621440 | tf_op jit(solution)/shard_map/rotate_code/pallas_call | solution.py:166
  21.1 1.6 %collective-permute-start.3 = (bf16[4,256,128]{2,1,0:T(8,128)(2,1)S(1)}, bf16[4,256,128]{2,1,0:T(8,128)(2,1)S(1)}, u32[]{:S(2)}, u32[]{:S(2)}) collective-permute-start(bf16[4,256,128]{2,1,0:T(8,128)(2,1)S(1)} %get-tuple-element.33.refs_4_), channel_id=1, source_target_pairs={{0,2},{1,3},{2,0},{3,1},{4,6},{5,7},{6,4},{7,5},{8,10},{9,11},{10,... | collective-permute-start | bytes 786440 | tf_op jit(solution)/shard_map/ppermute | solution.py:299
  22.7 0.1 collective-permute-done.13.refs_2_
  22.8 1.2 %collective-permute-start.4 = (bf16[4,256,128]{2,1,0:T(8,128)(2,1)S(1)}, bf16[4,256,128]{2,1,0:T(8,128)(2,1)S(1)}, u32[]{:S(2)}, u32[]{:S(2)}) collective-permute-start(bf16[4,256,128]{2,1,0:T(8,128)(2,1)S(1)} %get-tuple-element.34.refs_5_), channel_id=1, source_target_pairs={{0,1},{1,0},{2,3},{3,2},{4,5},{5,4},{6,7},{7,6},{8,9},{9,8},{10,11... | collective-permute-start | bytes 786440 | tf_op jit(solution)/shard_map/ppermute | solution.py:299
  24.0 2.8 %rotate_code.6 = (bf16[4,128,128]{2,1,0:T(8,128)(2,1)S(1)}, bf16[4,128,128]{2,1,0:T(8,128)(2,1)S(1)}, bf16[4,256,128]{2,1,0:T(8,128)(2,1)S(1)}, s32[256,128]{1,0:T(8,128)S(1)}) custom-call(bf16[1,1048576]{1,0:T(2,128)(2,1)} %bitcast.7, s32[8192,128]{1,0:T(8,128)} %bitcast.11, f32[4,128,128]{2,1,0:T(8,128)S(1)} %far_sum.2.refs_0_), custom_call_target="tpu_custom_call" | custom-call | flops 201326592 | bytes 3932160 | tf_op jit(solution)/shard_map/rotate_code/pallas_call | solution.py:166
  26.8 0.0 collective-permute-done.11.refs_0_
  26.8 0.7 %collective-permute-start.5 = (bf16[4,128,128]{2,1,0:T(8,128)(2,1)S(1)}, bf16[4,128,128]{2,1,0:T(8,128)(2,1)S(1)}, u32[]{:S(2)}, u32[]{:S(2)}) collective-permute-start(bf16[4,128,128]{2,1,0:T(8,128)(2,1)S(1)} %get-tuple-element.36), channel_id=1, source_target_pairs={{0,3},{1,2},{2,1},{3,0},{4,7},{5,6},{6,5},{7,4},{8,11},{9,10},{10,... | collective-permute-start | bytes 393224 | tf_op jit(solution)/shard_map/ppermute | solution.py:299
  27.5 0.0 collective-permute-done.12.refs_1_
  27.5 0.1 far_sum.3
  27.6 1.8 %collective-permute-start.14 = (f32[4,128,128]{2,1,0:T(8,128)S(1)}, f32[4,128,128]{2,1,0:T(8,128)S(1)}, u32[]{:S(2)}, u32[]{:S(2)}) collective-permute-start(f32[4,128,128]{2,1,0:T(8,128)S(1)} %far_sum.3), channel_id=1, source_target_pairs={{0,4},{1,5},{2,6},{3,7},{4,0},{5,1},{6,2},{7,3},{8,12},{9,13},{10,... | collective-permute-start | bytes 786440 | tf_op jit(solution)/shard_map/ppermute | solution.py:327
  29.4 10.3 %collective-permute-done.5.refs_3_ = bf16[4,128,128]{2,1,0:T(8,128)(2,1)S(1)} collective-permute-done((bf16[4,128,128]{2,1,0:T(8,128)(2,1)S(1)}, bf16[4,128,128]{2,1,0:T(8,128)(2,1)S(1)}, u32[]{:S(2)}, u32[]{:S(2)}) %collective-permute-start.5) | collective-permute-done | bytes 131104 | tf_op jit(solution)/shard_map/ppermute | solution.py:299
  39.7 0.0 collective-permute-start.10
  39.7 0.0 collective-permute-done.6.refs_4_
  39.7 0.0 collective-permute-done.3.refs_0_
  39.7 0.0 collective-permute-done.4.refs_1_
  39.7 0.3 group_sum_code.2
  40.0 0.1 collective-permute-start.7
  40.1 1.4 %collective-permute-start.8 = (bf16[128,128]{1,0:T(8,128)(2,1)S(1)}, bf16[128,128]{1,0:T(8,128)(2,1)S(1)}, u32[]{:S(2)}, u32[]{:S(2)}) collective-permute-start(bf16[128,128]{1,0:T(8,128)(2,1)S(1)} %get-tuple-element.38), channel_id=1, source_target_pairs={{0,16},{8,24},{16,0},{24,8},{1,17},{9,25},{17,1},{25,9},{2,18},{10... | collective-permute-start | bytes 98312 | tf_op jit(solution)/shard_map/ppermute | solution.py:305
  41.5 0.4 collective-permute-start.9
  41.9 3.7 %collective-permute-done.10.refs_3_ = bf16[4,128,128]{2,1,0:T(8,128)(2,1)S(1)} collective-permute-done((bf16[4,128,128]{2,1,0:T(8,128)(2,1)S(1)}, bf16[4,128,128]{2,1,0:T(8,128)(2,1)S(1)}, u32[]{:S(2)}, u32[]{:S(2)}) %collective-permute-start.10) | collective-permute-done | bytes 131104 | tf_op jit(solution)/shard_map/ppermute | solution.py:299
  45.6 0.0 collective-permute-done.14.refs_4_
  45.6 0.3 group_sum_code.3
  45.8 0.1 collective-permute-start.15
  45.9 1.4 %collective-permute-start.16 = (bf16[128,128]{1,0:T(8,128)(2,1)S(1)}, bf16[128,128]{1,0:T(8,128)(2,1)S(1)}, u32[]{:S(2)}, u32[]{:S(2)}) collective-permute-start(bf16[128,128]{1,0:T(8,128)(2,1)S(1)} %get-tuple-element.43), channel_id=1, source_target_pairs={{0,16},{8,24},{16,0},{24,8},{1,17},{9,25},{17,1},{25,9},{2,18},{10... | collective-permute-start | bytes 98312 | tf_op jit(solution)/shard_map/ppermute | solution.py:305
  47.3 0.0 collective-permute-done.7.refs_0_
  47.3 0.4 collective-permute-start.17
  47.8 0.0 collective-permute-done.8.refs_1_
  47.8 0.0 collective-permute-done.9.refs_2_
  47.8 1.7 %collective-permute-done.15.refs_4_ = bf16[128,128]{1,0:T(8,128)(2,1)S(1)} collective-permute-done((bf16[128,128]{1,0:T(8,128)(2,1)S(1)}, bf16[128,128]{1,0:T(8,128)(2,1)S(1)}, u32[]{:S(2)}, u32[]{:S(2)}) %collective-permute-start.15) | collective-permute-done | bytes 32800 | tf_op jit(solution)/shard_map/ppermute | solution.py:305
  49.5 0.4 collective-permute-done.16.refs_5_
  49.9 0.0 collective-permute-done.17.refs_6_
  49.9 0.9 %sum_unrotate.1 = (f32[256,128]{1,0:T(8,128)}, f32[1,256]{1,0:T(1,128)}) custom-call(s32[256,128]{1,0:T(8,128)S(1)} %get-tuple-element.32.sign_ref, bf16[128,128]{1,0:T(8,128)(2,1)S(1)} %collective-permute-done.7.refs_0_, bf16[128,128]{1,0:T(8,128)(2,1)S(1)} %collective-permute-done.8.refs_1_, bf16[128,128]{1,0:T(8,128)(2,1)S(1)} %collective-permute-done.9.refs_2_, ...), custom_call_target="tpu_custom_call" | custom-call | tf_op jit(solution)/shard_map/sum_unrotate/pallas_call | solution.py:276
Async XLA Ops:
  3.8 10.9 %collective-permute-start = (bf16[4,128,128]{2,1,0:T(8,128)(2,1)S(1)}, bf16[4,128,128]{2,1,0:T(8,128)(2,1)S(1)}, u32[]{:S(2)}, u32[]{:S(2)}) collective-permute-start(bf16[4,128,128]{2,1,0:T(8,128)(2,1)S(1)} %get-tuple-element.25.refs_0_), channel_id=1, source_target_pairs={{0,3},{1,2},{2,1},{3,0},{4,7},{5,6},{6,5},{7,4},{8,11},{9,10},{10,... | collective-permute-start | bytes 393224 | tf_op jit(solution)/shard_map/ppermute | solution.py:299
  7.8 7.6 %collective-permute-start.1 = (bf16[4,128,128]{2,1,0:T(8,128)(2,1)S(1)}, bf16[4,128,128]{2,1,0:T(8,128)(2,1)S(1)}, u32[]{:S(2)}, u32[]{:S(2)}) collective-permute-start(bf16[4,128,128]{2,1,0:T(8,128)(2,1)S(1)} %get-tuple-element.26.refs_1_), channel_id=1, source_target_pairs={{0,2},{1,3},{2,0},{3,1},{4,6},{5,7},{6,4},{7,5},{8,10},{9,11},{10,... | collective-permute-start | bytes 393224 | tf_op jit(solution)/shard_map/ppermute | solution.py:299
  8.3 7.2 %collective-permute-start.2 = (bf16[4,128,128]{2,1,0:T(8,128)(2,1)S(1)}, bf16[4,128,128]{2,1,0:T(8,128)(2,1)S(1)}, u32[]{:S(2)}, u32[]{:S(2)}) collective-permute-start(bf16[4,128,128]{2,1,0:T(8,128)(2,1)S(1)} %get-tuple-element.27.refs_2_), channel_id=1, source_target_pairs={{0,1},{1,0},{2,3},{3,2},{4,5},{5,4},{6,7},{7,6},{8,9},{9,8},{10,11... | collective-permute-start | bytes 393224 | tf_op jit(solution)/shard_map/ppermute | solution.py:299
  8.5 14.3 %collective-permute-start.13 = (bf16[4,128,128]{2,1,0:T(8,128)(2,1)S(1)}, bf16[4,128,128]{2,1,0:T(8,128)(2,1)S(1)}, u32[]{:S(2)}, u32[]{:S(2)}) collective-permute-start(bf16[4,128,128]{2,1,0:T(8,128)(2,1)S(1)} %get-tuple-element.28.refs_3_), channel_id=1, source_target_pairs={{0,2},{1,3},{2,0},{3,1},{4,6},{5,7},{6,4},{7,5},{8,10},{9,11},{10,... | collective-permute-start | bytes 393224 | tf_op jit(solution)/shard_map/ppermute | solution.py:299
  13.2 13.6 %collective-permute-start.11 = (bf16[4,128,128]{2,1,0:T(8,128)(2,1)S(1)}, bf16[4,128,128]{2,1,0:T(8,128)(2,1)S(1)}, u32[]{:S(2)}, u32[]{:S(2)}) collective-permute-start(bf16[4,128,128]{2,1,0:T(8,128)(2,1)S(1)} %get-tuple-element.30.refs_4_), channel_id=1, source_target_pairs={{0,3},{1,2},{2,1},{3,0},{4,7},{5,6},{6,5},{7,4},{8,11},{9,10},{10,... | collective-permute-start | bytes 393224 | tf_op jit(solution)/shard_map/ppermute | solution.py:299
  14.7 12.8 %collective-permute-start.12 = (bf16[4,128,128]{2,1,0:T(8,128)(2,1)S(1)}, bf16[4,128,128]{2,1,0:T(8,128)(2,1)S(1)}, u32[]{:S(2)}, u32[]{:S(2)}) collective-permute-start(bf16[4,128,128]{2,1,0:T(8,128)(2,1)S(1)} %get-tuple-element.31.refs_5_), channel_id=1, source_target_pairs={{0,1},{1,0},{2,3},{3,2},{4,5},{5,4},{6,7},{7,6},{8,9},{9,8},{10,11... | collective-permute-start | bytes 393224 | tf_op jit(solution)/shard_map/ppermute | solution.py:299
  15.5 24.2 %collective-permute-start.6 = (f32[4,128,128]{2,1,0:T(8,128)S(1)}, f32[4,128,128]{2,1,0:T(8,128)S(1)}, u32[]{:S(2)}, u32[]{:S(2)}) collective-permute-start(f32[4,128,128]{2,1,0:T(8,128)S(1)} %far_sum.2.refs_0_), channel_id=1, source_target_pairs={{0,4},{1,5},{2,6},{3,7},{4,0},{5,1},{6,2},{7,3},{8,12},{9,13},{10,... | collective-permute-start | bytes 786440 | tf_op jit(solution)/shard_map/ppermute | solution.py:322
  21.1 18.6 %collective-permute-start.3 = (bf16[4,256,128]{2,1,0:T(8,128)(2,1)S(1)}, bf16[4,256,128]{2,1,0:T(8,128)(2,1)S(1)}, u32[]{:S(2)}, u32[]{:S(2)}) collective-permute-start(bf16[4,256,128]{2,1,0:T(8,128)(2,1)S(1)} %get-tuple-element.33.refs_4_), channel_id=1, source_target_pairs={{0,2},{1,3},{2,0},{3,1},{4,6},{5,7},{6,4},{7,5},{8,10},{9,11},{10,... | collective-permute-start | bytes 786440 | tf_op jit(solution)/shard_map/ppermute | solution.py:299
  22.8 16.9 %collective-permute-start.4 = (bf16[4,256,128]{2,1,0:T(8,128)(2,1)S(1)}, bf16[4,256,128]{2,1,0:T(8,128)(2,1)S(1)}, u32[]{:S(2)}, u32[]{:S(2)}) collective-permute-start(bf16[4,256,128]{2,1,0:T(8,128)(2,1)S(1)} %get-tuple-element.34.refs_5_), channel_id=1, source_target_pairs={{0,1},{1,0},{2,3},{3,2},{4,5},{5,4},{6,7},{7,6},{8,9},{9,8},{10,11... | collective-permute-start | bytes 786440 | tf_op jit(solution)/shard_map/ppermute | solution.py:299
  26.8 12.9 %collective-permute-start.5 = (bf16[4,128,128]{2,1,0:T(8,128)(2,1)S(1)}, bf16[4,128,128]{2,1,0:T(8,128)(2,1)S(1)}, u32[]{:S(2)}, u32[]{:S(2)}) collective-permute-start(bf16[4,128,128]{2,1,0:T(8,128)(2,1)S(1)} %get-tuple-element.36), channel_id=1, source_target_pairs={{0,3},{1,2},{2,1},{3,0},{4,7},{5,6},{6,5},{7,4},{8,11},{9,10},{10,... | collective-permute-start | bytes 393224 | tf_op jit(solution)/shard_map/ppermute | solution.py:299
  27.6 18.0 %collective-permute-start.14 = (f32[4,128,128]{2,1,0:T(8,128)S(1)}, f32[4,128,128]{2,1,0:T(8,128)S(1)}, u32[]{:S(2)}, u32[]{:S(2)}) collective-permute-start(f32[4,128,128]{2,1,0:T(8,128)S(1)} %far_sum.3), channel_id=1, source_target_pairs={{0,4},{1,5},{2,6},{3,7},{4,0},{5,1},{6,2},{7,3},{8,12},{9,13},{10,... | collective-permute-start | bytes 786440 | tf_op jit(solution)/shard_map/ppermute | solution.py:327
  39.7 5.9 %collective-permute-start.10 = (bf16[4,128,128]{2,1,0:T(8,128)(2,1)S(1)}, bf16[4,128,128]{2,1,0:T(8,128)(2,1)S(1)}, u32[]{:S(2)}, u32[]{:S(2)}) collective-permute-start(bf16[4,128,128]{2,1,0:T(8,128)(2,1)S(1)} %get-tuple-element.41), channel_id=1, source_target_pairs={{0,3},{1,2},{2,1},{3,0},{4,7},{5,6},{6,5},{7,4},{8,11},{9,10},{10,... | collective-permute-start | bytes 393224 | tf_op jit(solution)/shard_map/ppermute | solution.py:299
  40.0 7.3 %collective-permute-start.7 = (bf16[128,128]{1,0:T(8,128)(2,1)S(1)}, bf16[128,128]{1,0:T(8,128)(2,1)S(1)}, u32[]{:S(2)}, u32[]{:S(2)}) collective-permute-start(bf16[128,128]{1,0:T(8,128)(2,1)S(1)} %get-tuple-element.37), channel_id=1, source_target_pairs={{0,24},{8,16},{16,8},{24,0},{1,25},{9,17},{17,9},{25,1},{2,26},{10... | collective-permute-start | bytes 98312 | tf_op jit(solution)/shard_map/ppermute | solution.py:305
  40.1 7.7 %collective-permute-start.8 = (bf16[128,128]{1,0:T(8,128)(2,1)S(1)}, bf16[128,128]{1,0:T(8,128)(2,1)S(1)}, u32[]{:S(2)}, u32[]{:S(2)}) collective-permute-start(bf16[128,128]{1,0:T(8,128)(2,1)S(1)} %get-tuple-element.38), channel_id=1, source_target_pairs={{0,16},{8,24},{16,0},{24,8},{1,17},{9,25},{17,1},{25,9},{2,18},{10... | collective-permute-start | bytes 98312 | tf_op jit(solution)/shard_map/ppermute | solution.py:305
  41.5 6.3 %collective-permute-start.9 = (bf16[128,128]{1,0:T(8,128)(2,1)S(1)}, bf16[128,128]{1,0:T(8,128)(2,1)S(1)}, u32[]{:S(2)}, u32[]{:S(2)}) collective-permute-start(bf16[128,128]{1,0:T(8,128)(2,1)S(1)} %get-tuple-element.39), channel_id=1, source_target_pairs={{0,8},{8,0},{16,24},{24,16},{1,9},{9,1},{17,25},{25,17},{2,10},{10... | collective-permute-start | bytes 98312 | tf_op jit(solution)/shard_map/ppermute | solution.py:305
  45.8 3.6 %collective-permute-start.15 = (bf16[128,128]{1,0:T(8,128)(2,1)S(1)}, bf16[128,128]{1,0:T(8,128)(2,1)S(1)}, u32[]{:S(2)}, u32[]{:S(2)}) collective-permute-start(bf16[128,128]{1,0:T(8,128)(2,1)S(1)} %get-tuple-element.42), channel_id=1, source_target_pairs={{0,24},{8,16},{16,8},{24,0},{1,25},{9,17},{17,9},{25,1},{2,26},{10... | collective-permute-start | bytes 98312 | tf_op jit(solution)/shard_map/ppermute | solution.py:305
  45.9 4.0 %collective-permute-start.16 = (bf16[128,128]{1,0:T(8,128)(2,1)S(1)}, bf16[128,128]{1,0:T(8,128)(2,1)S(1)}, u32[]{:S(2)}, u32[]{:S(2)}) collective-permute-start(bf16[128,128]{1,0:T(8,128)(2,1)S(1)} %get-tuple-element.43), channel_id=1, source_target_pairs={{0,16},{8,24},{16,0},{24,8},{1,17},{9,25},{17,1},{25,9},{2,18},{10... | collective-permute-start | bytes 98312 | tf_op jit(solution)/shard_map/ppermute | solution.py:305
  47.3 2.6 %collective-permute-start.17 = (bf16[128,128]{1,0:T(8,128)(2,1)S(1)}, bf16[128,128]{1,0:T(8,128)(2,1)S(1)}, u32[]{:S(2)}, u32[]{:S(2)}) collective-permute-start(bf16[128,128]{1,0:T(8,128)(2,1)S(1)} %get-tuple-element.44), channel_id=1, source_target_pairs={{0,8},{8,0},{16,24},{24,16},{1,9},{9,1},{17,25},{25,17},{2,10},{10... | collective-permute-start | bytes 98312 | tf_op jit(solution)/shard_map/ppermute | solution.py:305

commit v24 on v23

--- a/solution.py
+++ b/solution.py
@@ -188,6 +188,23 @@
     for array in arrays[1:]:
         total = total + array.astype(jnp.float32)
     return total
+
+
+def hand_on_kernel(*refs):
+    del refs
+
+
+def hand_on(arrays, after):
+    return list(
+        pl.pallas_call(
+            hand_on_kernel,
+            in_specs=[pl.BlockSpec(memory_space=pl.ANY)] * (len(arrays) + 1),
+            out_specs=[pl.BlockSpec(memory_space=pl.ANY)] * len(arrays),
+            out_shape=[jax.ShapeDtypeStruct(array.shape, array.dtype) for array in arrays],
+            input_output_aliases={index: index for index in range(len(arrays))},
+            name="hand_on",
+        )(*arrays, after)
+    )
 
 
 def far_sum_kernel(part, count, *refs):
@@ -337,6 +354,8 @@
         after=[first],
     )
     near = [swap(part, step) for step, part in zip(middle, near)] + [own]
+    if ends:
+        outs[len(ends) :] = hand_on(outs[len(ends) :], across[0])
     outs = [swap(part, step) for step, part in zip(ends + ends, outs)]
     coded = []
     for part in range(HALVES):

time: 51 us -> 49.6 us (0.973)
  waiting for transfers between devices: 16.8 us -> 10.4 us
  starting transfers between devices: 20 us -> 22.6 us
  local copies, waits for them, and re-layouts: 0 us -> 2.3 us
    ppermute x10, waiting for transfers between devices: 14.6 us -> 7.27 us  [swap(): return lax.ppermute(part, 'local', pairs)]
    ppermute x10, starting transfers between devices: 11.8 us -> 14.7 us  [swap(): return lax.ppermute(part, 'local', pairs)]
    unnamed x0 -> x6, local copies, waits for them, and re-layouts: none -> 2.3 us
    ppermute x6, waiting for transfers between devices: 2.13 us -> 3.15 us  [share(): moved.append(lax.ppermute(parts[step], 'node', pairs))]
  transfers between devices with their start and end apart: 18 -> 18, of which waited for: 6 -> 5; matrix products, arithmetic and copies ran while one was open for 0% -> 0% of each run, Pallas kernels for 18% -> 19%
where the time goes in v24:
time: 49.6 us; the launch traced here: 49.4 us
  starting transfers between devices  22.6 us (46%)
  Pallas kernels  13.3 us (27%)
  waiting for transfers between devices  10.4 us (21%)
  local copies, waits for them, and re-layouts  2.3 us (5%)
  between operations  0.71 us (1%)
    ppermute x10, starting transfers between devices, swap(): return lax.ppermute(part, 'local', pairs)  14.7 us
    pallas_call x4, Pallas kernels, rotate(): pl.pallas_call(functools.partial(rotate_kernel, layout, other, steps, par...  11.7 us
    ppermute x10, waiting for transfers between devices, swap(): return lax.ppermute(part, 'local', pairs)  7.27 us
    ppermute x6, starting transfers between devices, share(): moved.append(lax.ppermute(parts[step], 'node', pairs))  3.85 us
    ppermute x6, waiting for transfers between devices, share(): moved.append(lax.ppermute(parts[step], 'node', pairs))  3.15 us
    ppermute x1, starting transfers between devices, shards(): across = [lax.ppermute(first, 'local', counterparts)]  2.66 us
    unnamed x6, local copies, waits for them, and re-layouts  2.3 us
    ppermute x1, starting transfers between devices, shards(): across.append(lax.ppermute(second, 'local', counterparts))  1.43 us
  transfers between devices with their start and end apart: 18, of which 5 were waited for; matrix products, arithmetic and copies ran while one was open for 0% of the time, Pallas kernels for 19%

profile of v24, /device:TPU:0, one launch (start us, length us, event | category | flops | bytes accessed | tf_op | source)
XLA Modules:
  0.0 49.4 jit_solution(17540373196040728411)
XLA Ops:
  0.6 3.2 %rotate_code.4 = (bf16[4,128,128]{2,1,0:T(8,128)(2,1)S(1)}, bf16[4,128,128]{2,1,0:T(8,128)(2,1)S(1)}, bf16[4,128,128]{2,1,0:T(8,128)(2,1)S(1)}, bf16[4,128,128]{2,1,0:T(8,128)(2,1)S(1)}) custom-call(bf16[1,1048576]{1,0:T(2,128)(2,1)} %bitcast.4, s32[8192,128]{1,0:T(8,128)} %bitcast.8), custom_call_target="tpu_custom_call" | custom-call | flops 268435456 | bytes 5242880 | tf_op jit(solution)/shard_map/rotate_code/pallas_call | solution.py:166
  3.8 4.1 %collective-permute-start = (bf16[4,128,128]{2,1,0:T(8,128)(2,1)S(1)}, bf16[4,128,128]{2,1,0:T(8,128)(2,1)S(1)}, u32[]{:S(2)}, u32[]{:S(2)}) collective-permute-start(bf16[4,128,128]{2,1,0:T(8,128)(2,1)S(1)} %get-tuple-element.25.refs_0_), channel_id=1, source_target_pairs={{0,3},{1,2},{2,1},{3,0},{4,7},{5,6},{6,5},{7,4},{8,11},{9,10},{10,... | collective-permute-start | bytes 393224 | tf_op jit(solution)/shard_map/ppermute | solution.py:316
  7.8 0.4 collective-permute-start.1
  8.3 0.2 collective-permute-start.2
  8.5 1.9 %collective-permute-start.13 = (bf16[4,128,128]{2,1,0:T(8,128)(2,1)S(1)}, bf16[4,128,128]{2,1,0:T(8,128)(2,1)S(1)}, u32[]{:S(2)}, u32[]{:S(2)}) collective-permute-start(bf16[4,128,128]{2,1,0:T(8,128)(2,1)S(1)} %get-tuple-element.28.refs_3_), channel_id=1, source_target_pairs={{0,2},{1,3},{2,0},{3,1},{4,6},{5,7},{6,4},{7,5},{8,10},{9,11},{10,... | collective-permute-start | bytes 393224 | tf_op jit(solution)/shard_map/ppermute | solution.py:316
  10.4 2.9 %rotate_code.5 = (bf16[4,128,128]{2,1,0:T(8,128)(2,1)S(1)}, bf16[4,128,128]{2,1,0:T(8,128)(2,1)S(1)}, bf16[4,256,128]{2,1,0:T(8,128)(2,1)S(1)}) custom-call(bf16[1,1048576]{1,0:T(2,128)(2,1)} %bitcast.5, s32[8192,128]{1,0:T(8,128)} %bitcast.9, bf16[4,128,128]{2,1,0:T(8,128)(2,1)S(1)} %get-tuple-element.25.refs_0_, ...), custom_call_target="tpu_custom_call" | custom-call | flops 201326592 | bytes 3932160 | tf_op jit(solution)/shard_map/rotate_code/pallas_call | solution.py:166
  13.2 1.5 %collective-permute-start.11 = (bf16[4,128,128]{2,1,0:T(8,128)(2,1)S(1)}, bf16[4,128,128]{2,1,0:T(8,128)(2,1)S(1)}, u32[]{:S(2)}, u32[]{:S(2)}) collective-permute-start(bf16[4,128,128]{2,1,0:T(8,128)(2,1)S(1)} %get-tuple-element.30.refs_4_), channel_id=1, source_target_pairs={{0,3},{1,2},{2,1},{3,0},{4,7},{5,6},{6,5},{7,4},{8,11},{9,10},{10,... | collective-permute-start | bytes 393224 | tf_op jit(solution)/shard_map/ppermute | solution.py:316
  14.7 0.0 collective-permute-done.refs_0_
  14.7 0.2 collective-permute-start.12
  14.9 0.5 %collective-permute-done.1.refs_1_ = bf16[4,128,128]{2,1,0:T(8,128)(2,1)S(1)} collective-permute-done((bf16[4,128,128]{2,1,0:T(8,128)(2,1)S(1)}, bf16[4,128,128]{2,1,0:T(8,128)(2,1)S(1)}, u32[]{:S(2)}, u32[]{:S(2)}) %collective-permute-start.1) | collective-permute-done | bytes 131104 | tf_op jit(solution)/shard_map/ppermute | solution.py:316
  15.5 0.0 collective-permute-done.2.refs_2_
  15.5 0.1 far_sum.2.refs_0_
  15.5 2.7 %collective-permute-start.6 = (f32[4,128,128]{2,1,0:T(8,128)S(1)}, f32[4,128,128]{2,1,0:T(8,128)S(1)}, u32[]{:S(2)}, u32[]{:S(2)}) collective-permute-start(f32[4,128,128]{2,1,0:T(8,128)S(1)} %far_sum.2.refs_0_), channel_id=1, source_target_pairs={{0,4},{1,5},{2,6},{3,7},{4,0},{5,1},{6,2},{7,3},{8,12},{9,13},{10,... | collective-permute-start | bytes 786440 | tf_op jit(solution)/shard_map/ppermute | solution.py:339
  18.2 2.9 %rotate_code.7 = (bf16[4,256,128]{2,1,0:T(8,128)(2,1)S(1)}, bf16[4,256,128]{2,1,0:T(8,128)(2,1)S(1)}) custom-call(bf16[1,1048576]{1,0:T(2,128)(2,1)} %bitcast.6, s32[8192,128]{1,0:T(8,128)} %bitcast.10, f32[4,128,128]{2,1,0:T(8,128)S(1)} %far_sum.2.refs_0_), custom_call_target="tpu_custom_call" | custom-call | flops 134217728 | bytes 2621440 | tf_op jit(solution)/shard_map/rotate_code/pallas_call | solution.py:166
  21.1 1.6 %collective-permute-start.3 = (bf16[4,256,128]{2,1,0:T(8,128)(2,1)S(1)}, bf16[4,256,128]{2,1,0:T(8,128)(2,1)S(1)}, u32[]{:S(2)}, u32[]{:S(2)}) collective-permute-start(bf16[4,256,128]{2,1,0:T(8,128)(2,1)S(1)} %get-tuple-element.33.refs_4_), channel_id=1, source_target_pairs={{0,2},{1,3},{2,0},{3,1},{4,6},{5,7},{6,4},{7,5},{8,10},{9,11},{10,... | collective-permute-start | bytes 786440 | tf_op jit(solution)/shard_map/ppermute | solution.py:316
  22.7 0.1 collective-permute-done.13.refs_2_
  22.8 1.2 %collective-permute-start.4 = (bf16[4,256,128]{2,1,0:T(8,128)(2,1)S(1)}, bf16[4,256,128]{2,1,0:T(8,128)(2,1)S(1)}, u32[]{:S(2)}, u32[]{:S(2)}) collective-permute-start(bf16[4,256,128]{2,1,0:T(8,128)(2,1)S(1)} %get-tuple-element.34.refs_5_), channel_id=1, source_target_pairs={{0,1},{1,0},{2,3},{3,2},{4,5},{5,4},{6,7},{7,6},{8,9},{9,8},{10,11... | collective-permute-start | bytes 786440 | tf_op jit(solution)/shard_map/ppermute | solution.py:316
  24.0 0.0 collective-permute-done.11.refs_0_
  24.0 0.0 collective-permute-done.12.refs_1_
  24.0 0.1 far_sum.3
  24.1 1.4 %collective-permute-start.14 = (f32[4,128,128]{2,1,0:T(8,128)S(1)}, f32[4,128,128]{2,1,0:T(8,128)S(1)}, u32[]{:S(2)}, u32[]{:S(2)}) collective-permute-start(f32[4,128,128]{2,1,0:T(8,128)S(1)} %far_sum.3), channel_id=1, source_target_pairs={{0,4},{1,5},{2,6},{3,7},{4,0},{5,1},{6,2},{7,3},{8,12},{9,13},{10,... | collective-permute-start | bytes 786440 | tf_op jit(solution)/shard_map/ppermute | solution.py:344
  25.5 2.8 %rotate_code.6 = (bf16[4,128,128]{2,1,0:T(8,128)(2,1)S(1)}, bf16[4,128,128]{2,1,0:T(8,128)(2,1)S(1)}, bf16[4,256,128]{2,1,0:T(8,128)(2,1)S(1)}, s32[256,128]{1,0:T(8,128)S(1)}) custom-call(bf16[1,1048576]{1,0:T(2,128)(2,1)} %bitcast.7, s32[8192,128]{1,0:T(8,128)} %bitcast.11, f32[4,128,128]{2,1,0:T(8,128)S(1)} %far_sum.2.refs_0_), custom_call_target="tpu_custom_call" | custom-call | flops 201326592 | bytes 3932160 | tf_op jit(solution)/shard_map/rotate_code/pallas_call | solution.py:166
  28.3 0.0 copy-start.2
  28.3 0.6 %copy-done.2 = bf16[4,128,128]{2,1,0:T(8,128)(2,1)} copy-done((bf16[4,128,128]{2,1,0:T(8,128)(2,1)}, bf16[4,128,128]{2,1,0:T(8,128)(2,1)S(1)}, u32[]{:S(2)}) %copy-start.2) | copy-done | bytes 131096
  29.0 3.4 %collective-permute-start.5 = (bf16[4,128,128]{2,1,0:T(8,128)(2,1)S(1)}, bf16[4,128,128]{2,1,0:T(8,128)(2,1)S(1)}, u32[]{:S(2)}, u32[]{:S(2)}) collective-permute-start(bf16[4,128,128]{2,1,0:T(8,128)(2,1)S(1)} %get-tuple-element.36), channel_id=1, source_target_pairs={{0,3},{1,2},{2,1},{3,0},{4,7},{5,6},{6,5},{7,4},{8,11},{9,10},{10,... | collective-permute-start | bytes 393224 | tf_op jit(solution)/shard_map/ppermute | solution.py:316
  32.4 0.0 collective-permute-done.6.refs_4_.refs_1_
  32.4 0.0 copy-start
  32.4 0.7 %copy-done = f32[4,128,128]{2,1,0:T(8,128)} copy-done((f32[4,128,128]{2,1,0:T(8,128)}, f32[4,128,128]{2,1,0:T(8,128)S(1)}, u32[]{:S(2)}) %copy-start) | copy-done | bytes 262168
  33.1 0.3 collective-permute-start.10
  33.3 6.6 %collective-permute-done.5.refs_3_ = bf16[4,128,128]{2,1,0:T(8,128)(2,1)S(1)} collective-permute-done((bf16[4,128,128]{2,1,0:T(8,128)(2,1)S(1)}, bf16[4,128,128]{2,1,0:T(8,128)(2,1)S(1)}, u32[]{:S(2)}, u32[]{:S(2)}) %collective-permute-start.5) | collective-permute-done | bytes 131104 | tf_op jit(solution)/shard_map/ppermute | solution.py:316
  39.9 0.0 collective-permute-done.3.refs_0_
  39.9 0.0 collective-permute-done.4.refs_1_
  39.9 0.0 copy-start.1
  39.9 0.9 %copy-done.1 = f32[4,128,128]{2,1,0:T(8,128)S(1)} copy-done((f32[4,128,128]{2,1,0:T(8,128)S(1)}, f32[4,128,128]{2,1,0:T(8,128)}, u32[]{:S(2)}) %copy-start.1) | copy-done | bytes 262168
  40.9 0.3 group_sum_code.2
  41.1 0.1 collective-permute-start.7
  41.2 1.6 %collective-permute-start.8 = (bf16[128,128]{1,0:T(8,128)(2,1)S(1)}, bf16[128,128]{1,0:T(8,128)(2,1)S(1)}, u32[]{:S(2)}, u32[]{:S(2)}) collective-permute-start(bf16[128,128]{1,0:T(8,128)(2,1)S(1)} %get-tuple-element.38), channel_id=1, source_target_pairs={{0,16},{8,24},{16,0},{24,8},{1,17},{9,25},{17,1},{25,9},{2,18},{10... | collective-permute-start | bytes 98312 | tf_op jit(solution)/shard_map/ppermute | solution.py:322
  42.8 0.3 collective-permute-start.9
  43.1 0.0 collective-permute-done.14.refs_4_
  43.1 0.0 collective-permute-done.10.refs_3_
  43.1 0.3 group_sum_code.3
  43.3 1.2 %collective-permute-start.15 = (bf16[128,128]{1,0:T(8,128)(2,1)S(1)}, bf16[128,128]{1,0:T(8,128)(2,1)S(1)}, u32[]{:S(2)}, u32[]{:S(2)}) collective-permute-start(bf16[128,128]{1,0:T(8,128)(2,1)S(1)} %get-tuple-element.42), channel_id=1, source_target_pairs={{0,24},{8,16},{16,8},{24,0},{1,25},{9,17},{17,9},{25,1},{2,26},{10... | collective-permute-start | bytes 98312 | tf_op jit(solution)/shard_map/ppermute | solution.py:322
  44.5 0.7 %collective-permute-start.16 = (bf16[128,128]{1,0:T(8,128)(2,1)S(1)}, bf16[128,128]{1,0:T(8,128)(2,1)S(1)}, u32[]{:S(2)}, u32[]{:S(2)}) collective-permute-start(bf16[128,128]{1,0:T(8,128)(2,1)S(1)} %get-tuple-element.43), channel_id=1, source_target_pairs={{0,16},{8,24},{16,0},{24,8},{1,17},{9,25},{17,1},{25,9},{2,18},{10... | collective-permute-start | bytes 98312 | tf_op jit(solution)/shard_map/ppermute | solution.py:322
  45.2 0.0 collective-permute-done.7.refs_0_
  45.3 0.0 collective-permute-start.17
  45.3 0.0 collective-permute-done.8.refs_1_
  45.3 0.0 collective-permute-done.9.refs_2_
  45.3 1.5 %collective-permute-done.15.refs_4_ = bf16[128,128]{1,0:T(8,128)(2,1)S(1)} collective-permute-done((bf16[128,128]{1,0:T(8,128)(2,1)S(1)}, bf16[128,128]{1,0:T(8,128)(2,1)S(1)}, u32[]{:S(2)}, u32[]{:S(2)}) %collective-permute-start.15) | collective-permute-done | bytes 32800 | tf_op jit(solution)/shard_map/ppermute | solution.py:322
  46.7 1.7 %collective-permute-done.16.refs_5_ = bf16[128,128]{1,0:T(8,128)(2,1)S(1)} collective-permute-done((bf16[128,128]{1,0:T(8,128)(2,1)S(1)}, bf16[128,128]{1,0:T(8,128)(2,1)S(1)}, u32[]{:S(2)}, u32[]{:S(2)}) %collective-permute-start.16) | collective-permute-done | bytes 32800 | tf_op jit(solution)/shard_map/ppermute | solution.py:322
  48.4 0.0 collective-permute-done.17.refs_6_
  48.4 0.9 %sum_unrotate.1 = (f32[256,128]{1,0:T(8,128)}, f32[1,256]{1,0:T(1,128)}) custom-call(s32[256,128]{1,0:T(8,128)S(1)} %get-tuple-element.32.sign_ref, bf16[128,128]{1,0:T(8,128)(2,1)S(1)} %collective-permute-done.7.refs_0_, bf16[128,128]{1,0:T(8,128)(2,1)S(1)} %collective-permute-done.8.refs_1_, bf16[128,128]{1,0:T(8,128)(2,1)S(1)} %collective-permute-done.9.refs_2_, ...), custom_call_target="tpu_custom_call" | custom-call | tf_op jit(solution)/shard_map/sum_unrotate/pallas_call | solution.py:293
  (1 shorter events, 0.0 us)
Async XLA Ops:
  3.8 10.9 %collective-permute-start = (bf16[4,128,128]{2,1,0:T(8,128)(2,1)S(1)}, bf16[4,128,128]{2,1,0:T(8,128)(2,1)S(1)}, u32[]{:S(2)}, u32[]{:S(2)}) collective-permute-start(bf16[4,128,128]{2,1,0:T(8,128)(2,1)S(1)} %get-tuple-element.25.refs_0_), channel_id=1, source_target_pairs={{0,3},{1,2},{2,1},{3,0},{4,7},{5,6},{6,5},{7,4},{8,11},{9,10},{10,... | collective-permute-start | bytes 393224 | tf_op jit(solution)/shard_map/ppermute | solution.py:316
  7.8 7.6 %collective-permute-start.1 = (bf16[4,128,128]{2,1,0:T(8,128)(2,1)S(1)}, bf16[4,128,128]{2,1,0:T(8,128)(2,1)S(1)}, u32[]{:S(2)}, u32[]{:S(2)}) collective-permute-start(bf16[4,128,128]{2,1,0:T(8,128)(2,1)S(1)} %get-tuple-element.26.refs_1_), channel_id=1, source_target_pairs={{0,2},{1,3},{2,0},{3,1},{4,6},{5,7},{6,4},{7,5},{8,10},{9,11},{10,... | collective-permute-start | bytes 393224 | tf_op jit(solution)/shard_map/ppermute | solution.py:316
  8.3 7.2 %collective-permute-start.2 = (bf16[4,128,128]{2,1,0:T(8,128)(2,1)S(1)}, bf16[4,128,128]{2,1,0:T(8,128)(2,1)S(1)}, u32[]{:S(2)}, u32[]{:S(2)}) collective-permute-start(bf16[4,128,128]{2,1,0:T(8,128)(2,1)S(1)} %get-tuple-element.27.refs_2_), channel_id=1, source_target_pairs={{0,1},{1,0},{2,3},{3,2},{4,5},{5,4},{6,7},{7,6},{8,9},{9,8},{10,11... | collective-permute-start | bytes 393224 | tf_op jit(solution)/shard_map/ppermute | solution.py:316
  8.5 14.3 %collective-permute-start.13 = (bf16[4,128,128]{2,1,0:T(8,128)(2,1)S(1)}, bf16[4,128,128]{2,1,0:T(8,128)(2,1)S(1)}, u32[]{:S(2)}, u32[]{:S(2)}) collective-permute-start(bf16[4,128,128]{2,1,0:T(8,128)(2,1)S(1)} %get-tuple-element.28.refs_3_), channel_id=1, source_target_pairs={{0,2},{1,3},{2,0},{3,1},{4,6},{5,7},{6,4},{7,5},{8,10},{9,11},{10,... | collective-permute-start | bytes 393224 | tf_op jit(solution)/shard_map/ppermute | solution.py:316
  13.2 10.8 %collective-permute-start.11 = (bf16[4,128,128]{2,1,0:T(8,128)(2,1)S(1)}, bf16[4,128,128]{2,1,0:T(8,128)(2,1)S(1)}, u32[]{:S(2)}, u32[]{:S(2)}) collective-permute-start(bf16[4,128,128]{2,1,0:T(8,128)(2,1)S(1)} %get-tuple-element.30.refs_4_), channel_id=1, source_target_pairs={{0,3},{1,2},{2,1},{3,0},{4,7},{5,6},{6,5},{7,4},{8,11},{9,10},{10,... | collective-permute-start | bytes 393224 | tf_op jit(solution)/shard_map/ppermute | solution.py:316
  14.7 9.3 %collective-permute-start.12 = (bf16[4,128,128]{2,1,0:T(8,128)(2,1)S(1)}, bf16[4,128,128]{2,1,0:T(8,128)(2,1)S(1)}, u32[]{:S(2)}, u32[]{:S(2)}) collective-permute-start(bf16[4,128,128]{2,1,0:T(8,128)(2,1)S(1)} %get-tuple-element.31.refs_5_), channel_id=1, source_target_pairs={{0,1},{1,0},{2,3},{3,2},{4,5},{5,4},{6,7},{7,6},{8,9},{9,8},{10,11... | collective-permute-start | bytes 393224 | tf_op jit(solution)/shard_map/ppermute | solution.py:316
  15.5 16.8 %collective-permute-start.6 = (f32[4,128,128]{2,1,0:T(8,128)S(1)}, f32[4,128,128]{2,1,0:T(8,128)S(1)}, u32[]{:S(2)}, u32[]{:S(2)}) collective-permute-start(f32[4,128,128]{2,1,0:T(8,128)S(1)} %far_sum.2.refs_0_), channel_id=1, source_target_pairs={{0,4},{1,5},{2,6},{3,7},{4,0},{5,1},{6,2},{7,3},{8,12},{9,13},{10,... | collective-permute-start | bytes 786440 | tf_op jit(solution)/shard_map/ppermute | solution.py:339
  21.1 18.9 %collective-permute-start.3 = (bf16[4,256,128]{2,1,0:T(8,128)(2,1)S(1)}, bf16[4,256,128]{2,1,0:T(8,128)(2,1)S(1)}, u32[]{:S(2)}, u32[]{:S(2)}) collective-permute-start(bf16[4,256,128]{2,1,0:T(8,128)(2,1)S(1)} %get-tuple-element.33.refs_4_), channel_id=1, source_target_pairs={{0,2},{1,3},{2,0},{3,1},{4,6},{5,7},{6,4},{7,5},{8,10},{9,11},{10,... | collective-permute-start | bytes 786440 | tf_op jit(solution)/shard_map/ppermute | solution.py:316
  22.8 17.1 %collective-permute-start.4 = (bf16[4,256,128]{2,1,0:T(8,128)(2,1)S(1)}, bf16[4,256,128]{2,1,0:T(8,128)(2,1)S(1)}, u32[]{:S(2)}, u32[]{:S(2)}) collective-permute-start(bf16[4,256,128]{2,1,0:T(8,128)(2,1)S(1)} %get-tuple-element.34.refs_5_), channel_id=1, source_target_pairs={{0,1},{1,0},{2,3},{3,2},{4,5},{5,4},{6,7},{7,6},{8,9},{9,8},{10,11... | collective-permute-start | bytes 786440 | tf_op jit(solution)/shard_map/ppermute | solution.py:316
  24.1 19.0 %collective-permute-start.14 = (f32[4,128,128]{2,1,0:T(8,128)S(1)}, f32[4,128,128]{2,1,0:T(8,128)S(1)}, u32[]{:S(2)}, u32[]{:S(2)}) collective-permute-start(f32[4,128,128]{2,1,0:T(8,128)S(1)} %far_sum.3), channel_id=1, source_target_pairs={{0,4},{1,5},{2,6},{3,7},{4,0},{5,1},{6,2},{7,3},{8,12},{9,13},{10,... | collective-permute-start | bytes 786440 | tf_op jit(solution)/shard_map/ppermute | solution.py:344
  28.3 0.7 %copy-start.2 = (bf16[4,128,128]{2,1,0:T(8,128)(2,1)}, bf16[4,128,128]{2,1,0:T(8,128)(2,1)S(1)}, u32[]{:S(2)}) copy-start(bf16[4,128,128]{2,1,0:T(8,128)(2,1)S(1)} %get-tuple-element.41.refs_0_) | copy-start | bytes 393220
  29.0 10.9 %collective-permute-start.5 = (bf16[4,128,128]{2,1,0:T(8,128)(2,1)S(1)}, bf16[4,128,128]{2,1,0:T(8,128)(2,1)S(1)}, u32[]{:S(2)}, u32[]{:S(2)}) collective-permute-start(bf16[4,128,128]{2,1,0:T(8,128)(2,1)S(1)} %get-tuple-element.36), channel_id=1, source_target_pairs={{0,3},{1,2},{2,1},{3,0},{4,7},{5,6},{6,5},{7,4},{8,11},{9,10},{10,... | collective-permute-start | bytes 393224 | tf_op jit(solution)/shard_map/ppermute | solution.py:316
  32.4 0.7 %copy-start = (f32[4,128,128]{2,1,0:T(8,128)}, f32[4,128,128]{2,1,0:T(8,128)S(1)}, u32[]{:S(2)}) copy-start(f32[4,128,128]{2,1,0:T(8,128)S(1)} %collective-permute-done.6.refs_4_.refs_1_) | copy-start | bytes 786436
  33.1 10.0 %collective-permute-start.10 = (bf16[4,128,128]{2,1,0:T(8,128)(2,1)}, bf16[4,128,128]{2,1,0:T(8,128)(2,1)S(1)}, u32[]{:S(2)}, u32[]{:S(2)}) collective-permute-start(bf16[4,128,128]{2,1,0:T(8,128)(2,1)} %hand_on.1), channel_id=1, source_target_pairs={{0,3},{1,2},{2,1},{3,0},{4,7},{5,6},{6,5},{7,4},{8,11},{9,10},{10,... | collective-permute-start | bytes 393224 | tf_op jit(solution)/shard_map/ppermute | solution.py:316
  39.9 1.0 %copy-start.1 = (f32[4,128,128]{2,1,0:T(8,128)S(1)}, f32[4,128,128]{2,1,0:T(8,128)}, u32[]{:S(2)}) copy-start(f32[4,128,128]{2,1,0:T(8,128)} %copy-done) | copy-start | bytes 786436
  41.1 4.1 %collective-permute-start.7 = (bf16[128,128]{1,0:T(8,128)(2,1)S(1)}, bf16[128,128]{1,0:T(8,128)(2,1)S(1)}, u32[]{:S(2)}, u32[]{:S(2)}) collective-permute-start(bf16[128,128]{1,0:T(8,128)(2,1)S(1)} %get-tuple-element.37), channel_id=1, source_target_pairs={{0,24},{8,16},{16,8},{24,0},{1,25},{9,17},{17,9},{25,1},{2,26},{10... | collective-permute-start | bytes 98312 | tf_op jit(solution)/shard_map/ppermute | solution.py:322
  41.2 4.0 %collective-permute-start.8 = (bf16[128,128]{1,0:T(8,128)(2,1)S(1)}, bf16[128,128]{1,0:T(8,128)(2,1)S(1)}, u32[]{:S(2)}, u32[]{:S(2)}) collective-permute-start(bf16[128,128]{1,0:T(8,128)(2,1)S(1)} %get-tuple-element.38), channel_id=1, source_target_pairs={{0,16},{8,24},{16,0},{24,8},{1,17},{9,25},{17,1},{25,9},{2,18},{10... | collective-permute-start | bytes 98312 | tf_op jit(solution)/shard_map/ppermute | solution.py:322
  42.8 2.5 %collective-permute-start.9 = (bf16[128,128]{1,0:T(8,128)(2,1)S(1)}, bf16[128,128]{1,0:T(8,128)(2,1)S(1)}, u32[]{:S(2)}, u32[]{:S(2)}) collective-permute-start(bf16[128,128]{1,0:T(8,128)(2,1)S(1)} %get-tuple-element.39), channel_id=1, source_target_pairs={{0,8},{8,0},{16,24},{24,16},{1,9},{9,1},{17,25},{25,17},{2,10},{10... | collective-permute-start | bytes 98312 | tf_op jit(solution)/shard_map/ppermute | solution.py:322
  43.3 3.4 %collective-permute-start.15 = (bf16[128,128]{1,0:T(8,128)(2,1)S(1)}, bf16[128,128]{1,0:T(8,128)(2,1)S(1)}, u32[]{:S(2)}, u32[]{:S(2)}) collective-permute-start(bf16[128,128]{1,0:T(8,128)(2,1)S(1)} %get-tuple-element.42), channel_id=1, source_target_pairs={{0,24},{8,16},{16,8},{24,0},{1,25},{9,17},{17,9},{25,1},{2,26},{10... | collective-permute-start | bytes 98312 | tf_op jit(solution)/shard_map/ppermute | solution.py:322
  44.5 3.9 %collective-permute-start.16 = (bf16[128,128]{1,0:T(8,128)(2,1)S(1)}, bf16[128,128]{1,0:T(8,128)(2,1)S(1)}, u32[]{:S(2)}, u32[]{:S(2)}) collective-permute-start(bf16[128,128]{1,0:T(8,128)(2,1)S(1)} %get-tuple-element.43), channel_id=1, source_target_pairs={{0,16},{8,24},{16,0},{24,8},{1,17},{9,25},{17,1},{25,9},{2,18},{10... | collective-permute-start | bytes 98312 | tf_op jit(solution)/shard_map/ppermute | solution.py:322
  45.3 3.2 %collective-permute-start.17 = (bf16[128,128]{1,0:T(8,128)(2,1)S(1)}, bf16[128,128]{1,0:T(8,128)(2,1)S(1)}, u32[]{:S(2)}, u32[]{:S(2)}) collective-permute-start(bf16[128,128]{1,0:T(8,128)(2,1)S(1)} %get-tuple-element.44), channel_id=1, source_target_pairs={{0,8},{8,0},{16,24},{24,16},{1,9},{9,1},{17,25},{25,17},{2,10},{10... | collective-permute-start | bytes 98312 | tf_op jit(solution)/shard_map/ppermute | solution.py:322

commit v25 on v24

--- a/solution.py
+++ b/solution.py
@@ -202,6 +202,7 @@
             out_specs=[pl.BlockSpec(memory_space=pl.ANY)] * len(arrays),
             out_shape=[jax.ShapeDtypeStruct(array.shape, array.dtype) for array in arrays],
             input_output_aliases={index: index for index in range(len(arrays))},
+            compiler_params=pltpu.CompilerParams(vmem_limit_bytes=SUM_VMEM_LIMIT),
             name="hand_on",
         )(*arrays, after)
     )

time: 49.6 us -> 48.7 us (0.982)
  local copies, waits for them, and re-layouts: 2.3 us -> 0 us
  waiting for transfers between devices: 10.4 us -> 11.2 us
  starting transfers between devices: 22.6 us -> 23.3 us
    unnamed x6 -> x0, local copies, waits for them, and re-layouts: 2.3 us -> none
    ppermute x10, waiting for transfers between devices: 7.27 us -> 8.34 us  [swap(): return lax.ppermute(part, 'local', pairs)]
    ppermute x10, starting transfers between devices: 14.7 us -> 15.4 us  [swap(): return lax.ppermute(part, 'local', pairs)]
  transfers between devices with their start and end apart: 18 -> 18, of which waited for: 5 -> 6; matrix products, arithmetic and copies ran while one was open for 0% -> 0% of each run, Pallas kernels for 19% -> 19%
where the time goes in v25:
time: 48.7 us; the launch traced here: 48.5 us
  starting transfers between devices  23.3 us (48%)
  Pallas kernels  13.3 us (27%)
  waiting for transfers between devices  11.2 us (23%)
  between operations  0.7 us (1%)
    ppermute x10, starting transfers between devices, swap(): return lax.ppermute(part, 'local', pairs)  15.4 us
    pallas_call x4, Pallas kernels, rotate(): pl.pallas_call(functools.partial(rotate_kernel, layout, other, steps, par...  11.7 us
    ppermute x10, waiting for transfers between devices, swap(): return lax.ppermute(part, 'local', pairs)  8.34 us
    ppermute x6, starting transfers between devices, share(): moved.append(lax.ppermute(parts[step], 'node', pairs))  3.85 us
    ppermute x6, waiting for transfers between devices, share(): moved.append(lax.ppermute(parts[step], 'node', pairs))  2.88 us
    ppermute x1, starting transfers between devices, shards(): across = [lax.ppermute(first, 'local', counterparts)]  2.66 us
    ppermute x1, starting transfers between devices, shards(): across.append(lax.ppermute(second, 'local', counterparts))  1.43 us
  transfers between devices with their start and end apart: 18, of which 6 were waited for; matrix products, arithmetic and copies ran while one was open for 0% of the time, Pallas kernels for 19%

profile of v25, /device:TPU:0, one launch (start us, length us, event | category | flops | bytes accessed | tf_op | source)
XLA Modules:
  0.0 48.5 jit_solution(3038581818787039423)
XLA Ops:
  0.6 3.2 %rotate_code.4 = (bf16[4,128,128]{2,1,0:T(8,128)(2,1)S(1)}, bf16[4,128,128]{2,1,0:T(8,128)(2,1)S(1)}, bf16[4,128,128]{2,1,0:T(8,128)(2,1)S(1)}, bf16[4,128,128]{2,1,0:T(8,128)(2,1)S(1)}) custom-call(bf16[1,1048576]{1,0:T(2,128)(2,1)} %bitcast.4, s32[8192,128]{1,0:T(8,128)} %bitcast.8), custom_call_target="tpu_custom_call" | custom-call | flops 268435456 | bytes 5242880 | tf_op jit(solution)/shard_map/rotate_code/pallas_call | solution.py:166
  3.8 4.1 %collective-permute-start = (bf16[4,128,128]{2,1,0:T(8,128)(2,1)S(1)}, bf16[4,128,128]{2,1,0:T(8,128)(2,1)S(1)}, u32[]{:S(2)}, u32[]{:S(2)}) collective-permute-start(bf16[4,128,128]{2,1,0:T(8,128)(2,1)S(1)} %get-tuple-element.25.refs_0_), channel_id=1, source_target_pairs={{0,3},{1,2},{2,1},{3,0},{4,7},{5,6},{6,5},{7,4},{8,11},{9,10},{10,... | collective-permute-start | bytes 393224 | tf_op jit(solution)/shard_map/ppermute | solution.py:317
  7.8 0.4 collective-permute-start.1
  8.3 0.2 collective-permute-start.2
  8.5 1.9 %collective-permute-start.13 = (bf16[4,128,128]{2,1,0:T(8,128)(2,1)S(1)}, bf16[4,128,128]{2,1,0:T(8,128)(2,1)S(1)}, u32[]{:S(2)}, u32[]{:S(2)}) collective-permute-start(bf16[4,128,128]{2,1,0:T(8,128)(2,1)S(1)} %get-tuple-element.28.refs_3_), channel_id=1, source_target_pairs={{0,2},{1,3},{2,0},{3,1},{4,6},{5,7},{6,4},{7,5},{8,10},{9,11},{10,... | collective-permute-start | bytes 393224 | tf_op jit(solution)/shard_map/ppermute | solution.py:317
  10.4 2.9 %rotate_code.5 = (bf16[4,128,128]{2,1,0:T(8,128)(2,1)S(1)}, bf16[4,128,128]{2,1,0:T(8,128)(2,1)S(1)}, bf16[4,256,128]{2,1,0:T(8,128)(2,1)S(1)}) custom-call(bf16[1,1048576]{1,0:T(2,128)(2,1)} %bitcast.5, s32[8192,128]{1,0:T(8,128)} %bitcast.9, bf16[4,128,128]{2,1,0:T(8,128)(2,1)S(1)} %get-tuple-element.25.refs_0_, ...), custom_call_target="tpu_custom_call" | custom-call | flops 201326592 | bytes 3932160 | tf_op jit(solution)/shard_map/rotate_code/pallas_call | solution.py:166
  13.2 1.5 %collective-permute-start.11 = (bf16[4,128,128]{2,1,0:T(8,128)(2,1)S(1)}, bf16[4,128,128]{2,1,0:T(8,128)(2,1)S(1)}, u32[]{:S(2)}, u32[]{:S(2)}) collective-permute-start(bf16[4,128,128]{2,1,0:T(8,128)(2,1)S(1)} %get-tuple-element.30.refs_4_), channel_id=1, source_target_pairs={{0,3},{1,2},{2,1},{3,0},{4,7},{5,6},{6,5},{7,4},{8,11},{9,10},{10,... | collective-permute-start | bytes 393224 | tf_op jit(solution)/shard_map/ppermute | solution.py:317
  14.7 0.0 collective-permute-done.refs_0_
  14.7 0.2 collective-permute-start.12
  14.9 0.5 %collective-permute-done.1.refs_1_ = bf16[4,128,128]{2,1,0:T(8,128)(2,1)S(1)} collective-permute-done((bf16[4,128,128]{2,1,0:T(8,128)(2,1)S(1)}, bf16[4,128,128]{2,1,0:T(8,128)(2,1)S(1)}, u32[]{:S(2)}, u32[]{:S(2)}) %collective-permute-start.1) | collective-permute-done | bytes 131104 | tf_op jit(solution)/shard_map/ppermute | solution.py:317
  15.5 0.0 collective-permute-done.2.refs_2_
  15.5 0.1 far_sum.2.refs_0_
  15.5 2.7 %collective-permute-start.6 = (f32[4,128,128]{2,1,0:T(8,128)S(1)}, f32[4,128,128]{2,1,0:T(8,128)S(1)}, u32[]{:S(2)}, u32[]{:S(2)}) collective-permute-start(f32[4,128,128]{2,1,0:T(8,128)S(1)} %far_sum.2.refs_0_), channel_id=1, source_target_pairs={{0,4},{1,5},{2,6},{3,7},{4,0},{5,1},{6,2},{7,3},{8,12},{9,13},{10,... | collective-permute-start | bytes 786440 | tf_op jit(solution)/shard_map/ppermute | solution.py:340
  18.2 2.9 %rotate_code.7 = (bf16[4,256,128]{2,1,0:T(8,128)(2,1)S(1)}, bf16[4,256,128]{2,1,0:T(8,128)(2,1)S(1)}) custom-call(bf16[1,1048576]{1,0:T(2,128)(2,1)} %bitcast.6, s32[8192,128]{1,0:T(8,128)} %bitcast.10, f32[4,128,128]{2,1,0:T(8,128)S(1)} %far_sum.2.refs_0_), custom_call_target="tpu_custom_call" | custom-call | flops 134217728 | bytes 2621440 | tf_op jit(solution)/shard_map/rotate_code/pallas_call | solution.py:166
  21.1 1.6 %collective-permute-start.3 = (bf16[4,256,128]{2,1,0:T(8,128)(2,1)S(1)}, bf16[4,256,128]{2,1,0:T(8,128)(2,1)S(1)}, u32[]{:S(2)}, u32[]{:S(2)}) collective-permute-start(bf16[4,256,128]{2,1,0:T(8,128)(2,1)S(1)} %get-tuple-element.33.refs_4_), channel_id=1, source_target_pairs={{0,2},{1,3},{2,0},{3,1},{4,6},{5,7},{6,4},{7,5},{8,10},{9,11},{10,... | collective-permute-start | bytes 786440 | tf_op jit(solution)/shard_map/ppermute | solution.py:317
  22.7 0.1 collective-permute-done.13.refs_2_
  22.8 1.2 %collective-permute-start.4 = (bf16[4,256,128]{2,1,0:T(8,128)(2,1)S(1)}, bf16[4,256,128]{2,1,0:T(8,128)(2,1)S(1)}, u32[]{:S(2)}, u32[]{:S(2)}) collective-permute-start(bf16[4,256,128]{2,1,0:T(8,128)(2,1)S(1)} %get-tuple-element.34.refs_5_), channel_id=1, source_target_pairs={{0,1},{1,0},{2,3},{3,2},{4,5},{5,4},{6,7},{7,6},{8,9},{9,8},{10,11... | collective-permute-start | bytes 786440 | tf_op jit(solution)/shard_map/ppermute | solution.py:317
  24.0 0.0 collective-permute-done.11.refs_0_
  24.0 0.0 collective-permute-done.12.refs_1_
  24.0 0.1 far_sum.3
  24.1 1.4 %collective-permute-start.14 = (f32[4,128,128]{2,1,0:T(8,128)S(1)}, f32[4,128,128]{2,1,0:T(8,128)S(1)}, u32[]{:S(2)}, u32[]{:S(2)}) collective-permute-start(f32[4,128,128]{2,1,0:T(8,128)S(1)} %far_sum.3), channel_id=1, source_target_pairs={{0,4},{1,5},{2,6},{3,7},{4,0},{5,1},{6,2},{7,3},{8,12},{9,13},{10,... | collective-permute-start | bytes 786440 | tf_op jit(solution)/shard_map/ppermute | solution.py:345
  25.5 2.8 %rotate_code.6 = (bf16[4,128,128]{2,1,0:T(8,128)(2,1)S(1)}, bf16[4,128,128]{2,1,0:T(8,128)(2,1)S(1)}, bf16[4,256,128]{2,1,0:T(8,128)(2,1)S(1)}, s32[256,128]{1,0:T(8,128)S(1)}) custom-call(bf16[1,1048576]{1,0:T(2,128)(2,1)} %bitcast.7, s32[8192,128]{1,0:T(8,128)} %bitcast.11, f32[4,128,128]{2,1,0:T(8,128)S(1)} %far_sum.2.refs_0_), custom_call_target="tpu_custom_call" | custom-call | flops 201326592 | bytes 3932160 | tf_op jit(solution)/shard_map/rotate_code/pallas_call | solution.py:166
  28.3 3.5 %collective-permute-start.5 = (bf16[4,128,128]{2,1,0:T(8,128)(2,1)S(1)}, bf16[4,128,128]{2,1,0:T(8,128)(2,1)S(1)}, u32[]{:S(2)}, u32[]{:S(2)}) collective-permute-start(bf16[4,128,128]{2,1,0:T(8,128)(2,1)S(1)} %get-tuple-element.36), channel_id=1, source_target_pairs={{0,3},{1,2},{2,1},{3,0},{4,7},{5,6},{6,5},{7,4},{8,11},{9,10},{10,... | collective-permute-start | bytes 393224 | tf_op jit(solution)/shard_map/ppermute | solution.py:317
  31.8 0.0 collective-permute-done.6.refs_4_.refs_1_
  31.8 0.8 %collective-permute-start.10 = (bf16[4,128,128]{2,1,0:T(8,128)(2,1)S(1)}, bf16[4,128,128]{2,1,0:T(8,128)(2,1)S(1)}, u32[]{:S(2)}, u32[]{:S(2)}) collective-permute-start(bf16[4,128,128]{2,1,0:T(8,128)(2,1)S(1)} %hand_on.1), channel_id=1, source_target_pairs={{0,3},{1,2},{2,1},{3,0},{4,7},{5,6},{6,5},{7,4},{8,11},{9,10},{10,... | collective-permute-start | bytes 393224 | tf_op jit(solution)/shard_map/ppermute | solution.py:317
  32.6 7.3 %collective-permute-done.5.refs_3_ = bf16[4,128,128]{2,1,0:T(8,128)(2,1)S(1)} collective-permute-done((bf16[4,128,128]{2,1,0:T(8,128)(2,1)S(1)}, bf16[4,128,128]{2,1,0:T(8,128)(2,1)S(1)}, u32[]{:S(2)}, u32[]{:S(2)}) %collective-permute-start.5) | collective-permute-done | bytes 131104 | tf_op jit(solution)/shard_map/ppermute | solution.py:317
  39.9 0.0 collective-permute-done.3.refs_0_
  39.9 0.0 collective-permute-done.4.refs_1_
  39.9 0.3 group_sum_code.2
  40.2 0.1 collective-permute-start.7
  40.3 1.6 %collective-permute-start.8 = (bf16[128,128]{1,0:T(8,128)(2,1)S(1)}, bf16[128,128]{1,0:T(8,128)(2,1)S(1)}, u32[]{:S(2)}, u32[]{:S(2)}) collective-permute-start(bf16[128,128]{1,0:T(8,128)(2,1)S(1)} %get-tuple-element.38), channel_id=1, source_target_pairs={{0,16},{8,24},{16,0},{24,8},{1,17},{9,25},{17,1},{25,9},{2,18},{10... | collective-permute-start | bytes 98312 | tf_op jit(solution)/shard_map/ppermute | solution.py:323
  41.8 0.3 collective-permute-start.9
  42.1 0.0 collective-permute-done.14.refs_4_
  42.1 0.4 collective-permute-done.10.refs_3_
  42.5 0.3 group_sum_code.3
  42.8 0.8 %collective-permute-start.15 = (bf16[128,128]{1,0:T(8,128)(2,1)S(1)}, bf16[128,128]{1,0:T(8,128)(2,1)S(1)}, u32[]{:S(2)}, u32[]{:S(2)}) collective-permute-start(bf16[128,128]{1,0:T(8,128)(2,1)S(1)} %get-tuple-element.42), channel_id=1, source_target_pairs={{0,24},{8,16},{16,8},{24,0},{1,25},{9,17},{17,9},{25,1},{2,26},{10... | collective-permute-start | bytes 98312 | tf_op jit(solution)/shard_map/ppermute | solution.py:323
  43.6 0.7 %collective-permute-start.16 = (bf16[128,128]{1,0:T(8,128)(2,1)S(1)}, bf16[128,128]{1,0:T(8,128)(2,1)S(1)}, u32[]{:S(2)}, u32[]{:S(2)}) collective-permute-start(bf16[128,128]{1,0:T(8,128)(2,1)S(1)} %get-tuple-element.43), channel_id=1, source_target_pairs={{0,16},{8,24},{16,0},{24,8},{1,17},{9,25},{17,1},{25,9},{2,18},{10... | collective-permute-start | bytes 98312 | tf_op jit(solution)/shard_map/ppermute | solution.py:323
  44.3 0.0 collective-permute-done.7.refs_0_
  44.3 0.4 collective-permute-start.17
  44.7 0.0 collective-permute-done.8.refs_1_
  44.7 0.0 collective-permute-done.9.refs_2_
  44.7 1.8 %collective-permute-done.15.refs_4_ = bf16[128,128]{1,0:T(8,128)(2,1)S(1)} collective-permute-done((bf16[128,128]{1,0:T(8,128)(2,1)S(1)}, bf16[128,128]{1,0:T(8,128)(2,1)S(1)}, u32[]{:S(2)}, u32[]{:S(2)}) %collective-permute-start.15) | collective-permute-done | bytes 32800 | tf_op jit(solution)/shard_map/ppermute | solution.py:323
  46.5 1.1 %collective-permute-done.16.refs_5_ = bf16[128,128]{1,0:T(8,128)(2,1)S(1)} collective-permute-done((bf16[128,128]{1,0:T(8,128)(2,1)S(1)}, bf16[128,128]{1,0:T(8,128)(2,1)S(1)}, u32[]{:S(2)}, u32[]{:S(2)}) %collective-permute-start.16) | collective-permute-done | bytes 32800 | tf_op jit(solution)/shard_map/ppermute | solution.py:323
  47.6 0.0 collective-permute-done.17.refs_6_
  47.6 0.9 %sum_unrotate.1 = (f32[256,128]{1,0:T(8,128)}, f32[1,256]{1,0:T(1,128)}) custom-call(s32[256,128]{1,0:T(8,128)S(1)} %get-tuple-element.32.sign_ref, bf16[128,128]{1,0:T(8,128)(2,1)S(1)} %collective-permute-done.7.refs_0_, bf16[128,128]{1,0:T(8,128)(2,1)S(1)} %collective-permute-done.8.refs_1_, bf16[128,128]{1,0:T(8,128)(2,1)S(1)} %collective-permute-done.9.refs_2_, ...), custom_call_target="tpu_custom_call" | custom-call | tf_op jit(solution)/shard_map/sum_unrotate/pallas_call | solution.py:294
  (1 shorter events, 0.0 us)
Async XLA Ops:
  3.8 10.9 %collective-permute-start = (bf16[4,128,128]{2,1,0:T(8,128)(2,1)S(1)}, bf16[4,128,128]{2,1,0:T(8,128)(2,1)S(1)}, u32[]{:S(2)}, u32[]{:S(2)}) collective-permute-start(bf16[4,128,128]{2,1,0:T(8,128)(2,1)S(1)} %get-tuple-element.25.refs_0_), channel_id=1, source_target_pairs={{0,3},{1,2},{2,1},{3,0},{4,7},{5,6},{6,5},{7,4},{8,11},{9,10},{10,... | collective-permute-start | bytes 393224 | tf_op jit(solution)/shard_map/ppermute | solution.py:317
  7.8 7.6 %collective-permute-start.1 = (bf16[4,128,128]{2,1,0:T(8,128)(2,1)S(1)}, bf16[4,128,128]{2,1,0:T(8,128)(2,1)S(1)}, u32[]{:S(2)}, u32[]{:S(2)}) collective-permute-start(bf16[4,128,128]{2,1,0:T(8,128)(2,1)S(1)} %get-tuple-element.26.refs_1_), channel_id=1, source_target_pairs={{0,2},{1,3},{2,0},{3,1},{4,6},{5,7},{6,4},{7,5},{8,10},{9,11},{10,... | collective-permute-start | bytes 393224 | tf_op jit(solution)/shard_map/ppermute | solution.py:317
  8.3 7.2 %collective-permute-start.2 = (bf16[4,128,128]{2,1,0:T(8,128)(2,1)S(1)}, bf16[4,128,128]{2,1,0:T(8,128)(2,1)S(1)}, u32[]{:S(2)}, u32[]{:S(2)}) collective-permute-start(bf16[4,128,128]{2,1,0:T(8,128)(2,1)S(1)} %get-tuple-element.27.refs_2_), channel_id=1, source_target_pairs={{0,1},{1,0},{2,3},{3,2},{4,5},{5,4},{6,7},{7,6},{8,9},{9,8},{10,11... | collective-permute-start | bytes 393224 | tf_op jit(solution)/shard_map/ppermute | solution.py:317
  8.5 14.3 %collective-permute-start.13 = (bf16[4,128,128]{2,1,0:T(8,128)(2,1)S(1)}, bf16[4,128,128]{2,1,0:T(8,128)(2,1)S(1)}, u32[]{:S(2)}, u32[]{:S(2)}) collective-permute-start(bf16[4,128,128]{2,1,0:T(8,128)(2,1)S(1)} %get-tuple-element.28.refs_3_), channel_id=1, source_target_pairs={{0,2},{1,3},{2,0},{3,1},{4,6},{5,7},{6,4},{7,5},{8,10},{9,11},{10,... | collective-permute-start | bytes 393224 | tf_op jit(solution)/shard_map/ppermute | solution.py:317
  13.2 10.8 %collective-permute-start.11 = (bf16[4,128,128]{2,1,0:T(8,128)(2,1)S(1)}, bf16[4,128,128]{2,1,0:T(8,128)(2,1)S(1)}, u32[]{:S(2)}, u32[]{:S(2)}) collective-permute-start(bf16[4,128,128]{2,1,0:T(8,128)(2,1)S(1)} %get-tuple-element.30.refs_4_), channel_id=1, source_target_pairs={{0,3},{1,2},{2,1},{3,0},{4,7},{5,6},{6,5},{7,4},{8,11},{9,10},{10,... | collective-permute-start | bytes 393224 | tf_op jit(solution)/shard_map/ppermute | solution.py:317
  14.7 9.3 %collective-permute-start.12 = (bf16[4,128,128]{2,1,0:T(8,128)(2,1)S(1)}, bf16[4,128,128]{2,1,0:T(8,128)(2,1)S(1)}, u32[]{:S(2)}, u32[]{:S(2)}) collective-permute-start(bf16[4,128,128]{2,1,0:T(8,128)(2,1)S(1)} %get-tuple-element.31.refs_5_), channel_id=1, source_target_pairs={{0,1},{1,0},{2,3},{3,2},{4,5},{5,4},{6,7},{7,6},{8,9},{9,8},{10,11... | collective-permute-start | bytes 393224 | tf_op jit(solution)/shard_map/ppermute | solution.py:317
  15.5 16.3 %collective-permute-start.6 = (f32[4,128,128]{2,1,0:T(8,128)S(1)}, f32[4,128,128]{2,1,0:T(8,128)S(1)}, u32[]{:S(2)}, u32[]{:S(2)}) collective-permute-start(f32[4,128,128]{2,1,0:T(8,128)S(1)} %far_sum.2.refs_0_), channel_id=1, source_target_pairs={{0,4},{1,5},{2,6},{3,7},{4,0},{5,1},{6,2},{7,3},{8,12},{9,13},{10,... | collective-permute-start | bytes 786440 | tf_op jit(solution)/shard_map/ppermute | solution.py:340
  21.1 18.9 %collective-permute-start.3 = (bf16[4,256,128]{2,1,0:T(8,128)(2,1)S(1)}, bf16[4,256,128]{2,1,0:T(8,128)(2,1)S(1)}, u32[]{:S(2)}, u32[]{:S(2)}) collective-permute-start(bf16[4,256,128]{2,1,0:T(8,128)(2,1)S(1)} %get-tuple-element.33.refs_4_), channel_id=1, source_target_pairs={{0,2},{1,3},{2,0},{3,1},{4,6},{5,7},{6,4},{7,5},{8,10},{9,11},{10,... | collective-permute-start | bytes 786440 | tf_op jit(solution)/shard_map/ppermute | solution.py:317
  22.8 17.1 %collective-permute-start.4 = (bf16[4,256,128]{2,1,0:T(8,128)(2,1)S(1)}, bf16[4,256,128]{2,1,0:T(8,128)(2,1)S(1)}, u32[]{:S(2)}, u32[]{:S(2)}) collective-permute-start(bf16[4,256,128]{2,1,0:T(8,128)(2,1)S(1)} %get-tuple-element.34.refs_5_), channel_id=1, source_target_pairs={{0,1},{1,0},{2,3},{3,2},{4,5},{5,4},{6,7},{7,6},{8,9},{9,8},{10,11... | collective-permute-start | bytes 786440 | tf_op jit(solution)/shard_map/ppermute | solution.py:317
  24.1 18.0 %collective-permute-start.14 = (f32[4,128,128]{2,1,0:T(8,128)S(1)}, f32[4,128,128]{2,1,0:T(8,128)S(1)}, u32[]{:S(2)}, u32[]{:S(2)}) collective-permute-start(f32[4,128,128]{2,1,0:T(8,128)S(1)} %far_sum.3), channel_id=1, source_target_pairs={{0,4},{1,5},{2,6},{3,7},{4,0},{5,1},{6,2},{7,3},{8,12},{9,13},{10,... | collective-permute-start | bytes 786440 | tf_op jit(solution)/shard_map/ppermute | solution.py:345
  28.3 11.6 %collective-permute-start.5 = (bf16[4,128,128]{2,1,0:T(8,128)(2,1)S(1)}, bf16[4,128,128]{2,1,0:T(8,128)(2,1)S(1)}, u32[]{:S(2)}, u32[]{:S(2)}) collective-permute-start(bf16[4,128,128]{2,1,0:T(8,128)(2,1)S(1)} %get-tuple-element.36), channel_id=1, source_target_pairs={{0,3},{1,2},{2,1},{3,0},{4,7},{5,6},{6,5},{7,4},{8,11},{9,10},{10,... | collective-permute-start | bytes 393224 | tf_op jit(solution)/shard_map/ppermute | solution.py:317
  31.8 10.7 %collective-permute-start.10 = (bf16[4,128,128]{2,1,0:T(8,128)(2,1)S(1)}, bf16[4,128,128]{2,1,0:T(8,128)(2,1)S(1)}, u32[]{:S(2)}, u32[]{:S(2)}) collective-permute-start(bf16[4,128,128]{2,1,0:T(8,128)(2,1)S(1)} %hand_on.1), channel_id=1, source_target_pairs={{0,3},{1,2},{2,1},{3,0},{4,7},{5,6},{6,5},{7,4},{8,11},{9,10},{10,... | collective-permute-start | bytes 393224 | tf_op jit(solution)/shard_map/ppermute | solution.py:317
  40.2 4.1 %collective-permute-start.7 = (bf16[128,128]{1,0:T(8,128)(2,1)S(1)}, bf16[128,128]{1,0:T(8,128)(2,1)S(1)}, u32[]{:S(2)}, u32[]{:S(2)}) collective-permute-start(bf16[128,128]{1,0:T(8,128)(2,1)S(1)} %get-tuple-element.37), channel_id=1, source_target_pairs={{0,24},{8,16},{16,8},{24,0},{1,25},{9,17},{17,9},{25,1},{2,26},{10... | collective-permute-start | bytes 98312 | tf_op jit(solution)/shard_map/ppermute | solution.py:323
  40.3 4.4 %collective-permute-start.8 = (bf16[128,128]{1,0:T(8,128)(2,1)S(1)}, bf16[128,128]{1,0:T(8,128)(2,1)S(1)}, u32[]{:S(2)}, u32[]{:S(2)}) collective-permute-start(bf16[128,128]{1,0:T(8,128)(2,1)S(1)} %get-tuple-element.38), channel_id=1, source_target_pairs={{0,16},{8,24},{16,0},{24,8},{1,17},{9,25},{17,1},{25,9},{2,18},{10... | collective-permute-start | bytes 98312 | tf_op jit(solution)/shard_map/ppermute | solution.py:323
  41.8 2.9 %collective-permute-start.9 = (bf16[128,128]{1,0:T(8,128)(2,1)S(1)}, bf16[128,128]{1,0:T(8,128)(2,1)S(1)}, u32[]{:S(2)}, u32[]{:S(2)}) collective-permute-start(bf16[128,128]{1,0:T(8,128)(2,1)S(1)} %get-tuple-element.39), channel_id=1, source_target_pairs={{0,8},{8,0},{16,24},{24,16},{1,9},{9,1},{17,25},{25,17},{2,10},{10... | collective-permute-start | bytes 98312 | tf_op jit(solution)/shard_map/ppermute | solution.py:323
  42.8 3.7 %collective-permute-start.15 = (bf16[128,128]{1,0:T(8,128)(2,1)S(1)}, bf16[128,128]{1,0:T(8,128)(2,1)S(1)}, u32[]{:S(2)}, u32[]{:S(2)}) collective-permute-start(bf16[128,128]{1,0:T(8,128)(2,1)S(1)} %get-tuple-element.42), channel_id=1, source_target_pairs={{0,24},{8,16},{16,8},{24,0},{1,25},{9,17},{17,9},{25,1},{2,26},{10... | collective-permute-start | bytes 98312 | tf_op jit(solution)/shard_map/ppermute | solution.py:323
  43.6 4.0 %collective-permute-start.16 = (bf16[128,128]{1,0:T(8,128)(2,1)S(1)}, bf16[128,128]{1,0:T(8,128)(2,1)S(1)}, u32[]{:S(2)}, u32[]{:S(2)}) collective-permute-start(bf16[128,128]{1,0:T(8,128)(2,1)S(1)} %get-tuple-element.43), channel_id=1, source_target_pairs={{0,16},{8,24},{16,0},{24,8},{1,17},{9,25},{17,1},{25,9},{2,18},{10... | collective-permute-start | bytes 98312 | tf_op jit(solution)/shard_map/ppermute | solution.py:323
  44.3 3.3 %collective-permute-start.17 = (bf16[128,128]{1,0:T(8,128)(2,1)S(1)}, bf16[128,128]{1,0:T(8,128)(2,1)S(1)}, u32[]{:S(2)}, u32[]{:S(2)}) collective-permute-start(bf16[128,128]{1,0:T(8,128)(2,1)S(1)} %get-tuple-element.44), channel_id=1, source_target_pairs={{0,8},{8,0},{16,24},{24,16},{1,9},{9,1},{17,25},{25,17},{2,10},{10... | collective-permute-start | bytes 98312 | tf_op jit(solution)/shard_map/ppermute | solution.py:323

commit v26 on v25

--- a/solution.py
+++ b/solution.py
@@ -339,24 +339,32 @@
     first = far_sum(far0, layout, 0, [*early])
     across = [lax.ppermute(first, "local", counterparts)]
     middle = [slow] + [fast] * (fast != slow)
-    near = rotate(values, sign_rows, layout, False, middle, [whole] * len(middle), after=[first])
-    far1 = [swap(part, step) for step, part in zip(others + [slow], far1 + [half1])] + [own]
-    second = far_sum(far1, layout, 1, [*near])
-    across.append(lax.ppermute(second, "local", counterparts))
     ends = [step for step in others if step not in middle]
-    *outs, own, own_signs = rotate(
+    near = rotate(
         values,
         sign_rows,
         layout,
         False,
-        ends + ends + [0],
-        [(0,)] * len(ends) + [(1,)] * len(ends) + [whole],
+        middle + ends,
+        [whole] * len(middle) + [(0,)] * len(ends),
+        after=[first],
+    )
+    outs, near = near[len(middle) :], near[: len(middle)]
+    far1 = [swap(part, step) for step, part in zip(others + [slow], far1 + [half1])] + [own]
+    second = far_sum(far1, layout, 1, [*near])
+    across.append(lax.ppermute(second, "local", counterparts))
+    *half1, own, own_signs = rotate(
+        values,
+        sign_rows,
+        layout,
+        False,
+        ends + [0],
+        [(1,)] * len(ends) + [whole],
         signed_out=True,
         after=[first],
     )
     near = [swap(part, step) for step, part in zip(middle, near)] + [own]
-    if ends:
-        outs[len(ends) :] = hand_on(outs[len(ends) :], across[0])
+    outs += hand_on(half1, across[0]) if ends else []
     outs = [swap(part, step) for step, part in zip(ends + ends, outs)]
     coded = []
     for part in range(HALVES):

time: 48.7 us -> 50.1 us (1.029)
  waiting for transfers between devices: 11.2 us -> 13.9 us
  starting transfers between devices: 23.3 us -> 22 us
    ppermute x10, waiting for transfers between devices: 8.34 us -> 10.9 us  [swap(): return lax.ppermute(part, 'local', pairs)]
    ppermute x1, starting transfers between devices: 1.43 us -> 0.07 us  [shards(): across.append(lax.ppermute(second, 'local', counterparts))]
  transfers between devices with their start and end apart: 18 -> 18, of which waited for: 6 -> 4; matrix products, arithmetic and copies ran while one was open for 0% -> 0% of each run, Pallas kernels for 19% -> 19%
where the time goes in v26:
time: 50.1 us; the launch traced here: 49.9 us
  starting transfers between devices  22 us (44%)
  waiting for transfers between devices  13.9 us (28%)
  Pallas kernels  13.4 us (27%)
  between operations  0.73 us (1%)
    ppermute x10, starting transfers between devices, swap(): return lax.ppermute(part, 'local', pairs)  15.1 us
    pallas_call x4, Pallas kernels, rotate(): pl.pallas_call(functools.partial(rotate_kernel, layout, other, steps, par...  11.8 us
    ppermute x10, waiting for transfers between devices, swap(): return lax.ppermute(part, 'local', pairs)  10.9 us
    ppermute x6, starting transfers between devices, share(): moved.append(lax.ppermute(parts[step], 'node', pairs))  3.85 us
    ppermute x6, waiting for transfers between devices, share(): moved.append(lax.ppermute(parts[step], 'node', pairs))  2.99 us
    ppermute x1, starting transfers between devices, shards(): across = [lax.ppermute(first, 'local', counterparts)]  2.96 us
  transfers between devices with their start and end apart: 18, of which 4 were waited for; matrix products, arithmetic and copies ran while one was open for 0% of the time, Pallas kernels for 19%

profile of v26, /device:TPU:0, one launch (start us, length us, event | category | flops | bytes accessed | tf_op | source)
XLA Modules:
  0.0 49.9 jit_solution(4110882429916003213)
XLA Ops:
  0.6 3.2 %rotate_code.4 = (bf16[4,128,128]{2,1,0:T(8,128)(2,1)S(1)}, bf16[4,128,128]{2,1,0:T(8,128)(2,1)S(1)}, bf16[4,128,128]{2,1,0:T(8,128)(2,1)S(1)}, bf16[4,128,128]{2,1,0:T(8,128)(2,1)S(1)}) custom-call(bf16[1,1048576]{1,0:T(2,128)(2,1)} %bitcast.4, s32[8192,128]{1,0:T(8,128)} %bitcast.8), custom_call_target="tpu_custom_call" | custom-call | flops 268435456 | bytes 5242880 | tf_op jit(solution)/shard_map/rotate_code/pallas_call | solution.py:166
  3.8 4.1 %collective-permute-start = (bf16[4,128,128]{2,1,0:T(8,128)(2,1)S(1)}, bf16[4,128,128]{2,1,0:T(8,128)(2,1)S(1)}, u32[]{:S(2)}, u32[]{:S(2)}) collective-permute-start(bf16[4,128,128]{2,1,0:T(8,128)(2,1)S(1)} %get-tuple-element.25.refs_0_), channel_id=1, source_target_pairs={{0,3},{1,2},{2,1},{3,0},{4,7},{5,6},{6,5},{7,4},{8,11},{9,10},{10,... | collective-permute-start | bytes 393224 | tf_op jit(solution)/shard_map/ppermute | solution.py:317
  7.8 0.4 collective-permute-start.1
  8.3 0.2 collective-permute-start.2
  8.5 2.9 %rotate_code.5 = (bf16[4,128,128]{2,1,0:T(8,128)(2,1)S(1)}, bf16[4,128,128]{2,1,0:T(8,128)(2,1)S(1)}, bf16[4,256,128]{2,1,0:T(8,128)(2,1)S(1)}) custom-call(bf16[1,1048576]{1,0:T(2,128)(2,1)} %bitcast.5, s32[8192,128]{1,0:T(8,128)} %bitcast.9, bf16[4,128,128]{2,1,0:T(8,128)(2,1)S(1)} %get-tuple-element.25.refs_0_, ...), custom_call_target="tpu_custom_call" | custom-call | flops 201326592 | bytes 3932160 | tf_op jit(solution)/shard_map/rotate_code/pallas_call | solution.py:166
  11.4 2.9 %collective-permute-start.11 = (bf16[4,128,128]{2,1,0:T(8,128)(2,1)S(1)}, bf16[4,128,128]{2,1,0:T(8,128)(2,1)S(1)}, u32[]{:S(2)}, u32[]{:S(2)}) collective-permute-start(bf16[4,128,128]{2,1,0:T(8,128)(2,1)S(1)} %get-tuple-element.30.refs_4_), channel_id=1, source_target_pairs={{0,3},{1,2},{2,1},{3,0},{4,7},{5,6},{6,5},{7,4},{8,11},{9,10},{10,... | collective-permute-start | bytes 393224 | tf_op jit(solution)/shard_map/ppermute | solution.py:317
  14.3 0.4 collective-permute-start.13
  14.7 0.0 collective-permute-done.refs_0_
  14.7 0.2 collective-permute-start.12
  14.9 0.0 collective-permute-done.1.refs_1_
  14.9 0.0 collective-permute-done.2.refs_2_
  14.9 0.1 far_sum.2.refs_0_
  15.0 3.0 %collective-permute-start.6 = (f32[4,128,128]{2,1,0:T(8,128)S(1)}, f32[4,128,128]{2,1,0:T(8,128)S(1)}, u32[]{:S(2)}, u32[]{:S(2)}) collective-permute-start(f32[4,128,128]{2,1,0:T(8,128)S(1)} %far_sum.2.refs_0_), channel_id=1, source_target_pairs={{0,4},{1,5},{2,6},{3,7},{4,0},{5,1},{6,2},{7,3},{8,12},{9,13},{10,... | collective-permute-start | bytes 786440 | tf_op jit(solution)/shard_map/ppermute | solution.py:340
  18.0 3.1 %rotate_code.7 = (bf16[4,256,128]{2,1,0:T(8,128)(2,1)S(1)}, bf16[4,256,128]{2,1,0:T(8,128)(2,1)S(1)}, bf16[4,128,128]{2,1,0:T(8,128)(2,1)S(1)}) custom-call(bf16[1,1048576]{1,0:T(2,128)(2,1)} %bitcast.6, s32[8192,128]{1,0:T(8,128)} %bitcast.10, f32[4,128,128]{2,1,0:T(8,128)S(1)} %far_sum.2.refs_0_), custom_call_target="tpu_custom_call" | custom-call | flops 201326592 | bytes 3932160 | tf_op jit(solution)/shard_map/rotate_code/pallas_call | solution.py:166
  21.0 1.6 %collective-permute-start.3 = (bf16[4,256,128]{2,1,0:T(8,128)(2,1)S(1)}, bf16[4,256,128]{2,1,0:T(8,128)(2,1)S(1)}, u32[]{:S(2)}, u32[]{:S(2)}) collective-permute-start(bf16[4,256,128]{2,1,0:T(8,128)(2,1)S(1)} %get-tuple-element.33.refs_4_), channel_id=1, source_target_pairs={{0,2},{1,3},{2,0},{3,1},{4,6},{5,7},{6,4},{7,5},{8,10},{9,11},{10,... | collective-permute-start | bytes 786440 | tf_op jit(solution)/shard_map/ppermute | solution.py:317
  22.7 0.0 collective-permute-done.11.refs_0_
  22.7 2.2 %collective-permute-start.4 = (bf16[4,256,128]{2,1,0:T(8,128)(2,1)S(1)}, bf16[4,256,128]{2,1,0:T(8,128)(2,1)S(1)}, u32[]{:S(2)}, u32[]{:S(2)}) collective-permute-start(bf16[4,256,128]{2,1,0:T(8,128)(2,1)S(1)} %get-tuple-element.34.refs_5_), channel_id=1, source_target_pairs={{0,1},{1,0},{2,3},{3,2},{4,5},{5,4},{6,7},{7,6},{8,9},{9,8},{10,11... | collective-permute-start | bytes 786440 | tf_op jit(solution)/shard_map/ppermute | solution.py:317
  24.8 0.0 collective-permute-done.12.refs_1_
  24.8 2.6 %collective-permute-done.13.refs_2_ = bf16[4,128,128]{2,1,0:T(8,128)(2,1)S(1)} collective-permute-done((bf16[4,128,128]{2,1,0:T(8,128)(2,1)S(1)}, bf16[4,128,128]{2,1,0:T(8,128)(2,1)S(1)}, u32[]{:S(2)}, u32[]{:S(2)}) %collective-permute-start.13) | collective-permute-done | bytes 131104 | tf_op jit(solution)/shard_map/ppermute | solution.py:317
  27.4 0.1 far_sum.3
  27.5 0.1 collective-permute-start.14
  27.6 0.1 collective-permute-start.5
  27.6 2.7 %rotate_code.6 = (bf16[4,128,128]{2,1,0:T(8,128)(2,1)S(1)}, bf16[4,256,128]{2,1,0:T(8,128)(2,1)S(1)}, s32[256,128]{1,0:T(8,128)S(1)}) custom-call(bf16[1,1048576]{1,0:T(2,128)(2,1)} %bitcast.7, s32[8192,128]{1,0:T(8,128)} %bitcast.11, f32[4,128,128]{2,1,0:T(8,128)S(1)} %far_sum.2.refs_0_), custom_call_target="tpu_custom_call" | custom-call | flops 134217728 | bytes 2621440 | tf_op jit(solution)/shard_map/rotate_code/pallas_call | solution.py:166
  30.4 0.0 collective-permute-done.6.refs_4_.refs_1_
  30.4 3.0 %collective-permute-start.10 = (bf16[4,128,128]{2,1,0:T(8,128)(2,1)S(1)}, bf16[4,128,128]{2,1,0:T(8,128)(2,1)S(1)}, u32[]{:S(2)}, u32[]{:S(2)}) collective-permute-start(bf16[4,128,128]{2,1,0:T(8,128)(2,1)S(1)} %hand_on.1), channel_id=1, source_target_pairs={{0,3},{1,2},{2,1},{3,0},{4,7},{5,6},{6,5},{7,4},{8,11},{9,10},{10,... | collective-permute-start | bytes 393224 | tf_op jit(solution)/shard_map/ppermute | solution.py:317
  33.4 8.2 %collective-permute-done.5.refs_3_ = bf16[4,128,128]{2,1,0:T(8,128)(2,1)S(1)} collective-permute-done((bf16[4,128,128]{2,1,0:T(8,128)(2,1)S(1)}, bf16[4,128,128]{2,1,0:T(8,128)(2,1)S(1)}, u32[]{:S(2)}, u32[]{:S(2)}) %collective-permute-start.5) | collective-permute-done | bytes 131104 | tf_op jit(solution)/shard_map/ppermute | solution.py:317
  41.6 0.0 collective-permute-done.3.refs_0_
  41.6 0.0 collective-permute-done.4.refs_1_
  41.6 0.3 group_sum_code.2
  41.9 0.1 collective-permute-start.7
  42.0 1.4 %collective-permute-start.8 = (bf16[128,128]{1,0:T(8,128)(2,1)S(1)}, bf16[128,128]{1,0:T(8,128)(2,1)S(1)}, u32[]{:S(2)}, u32[]{:S(2)}) collective-permute-start(bf16[128,128]{1,0:T(8,128)(2,1)S(1)} %get-tuple-element.38), channel_id=1, source_target_pairs={{0,16},{8,24},{16,0},{24,8},{1,17},{9,25},{17,1},{25,9},{2,18},{10... | collective-permute-start | bytes 98312 | tf_op jit(solution)/shard_map/ppermute | solution.py:323
  43.4 0.5 collective-permute-start.9
  43.8 0.0 collective-permute-done.14.refs_4_
  43.8 0.0 collective-permute-done.10.refs_3_
  43.8 0.3 group_sum_code.3
  44.1 1.0 %collective-permute-start.15 = (bf16[128,128]{1,0:T(8,128)(2,1)S(1)}, bf16[128,128]{1,0:T(8,128)(2,1)S(1)}, u32[]{:S(2)}, u32[]{:S(2)}) collective-permute-start(bf16[128,128]{1,0:T(8,128)(2,1)S(1)} %get-tuple-element.42), channel_id=1, source_target_pairs={{0,24},{8,16},{16,8},{24,0},{1,25},{9,17},{17,9},{25,1},{2,26},{10... | collective-permute-start | bytes 98312 | tf_op jit(solution)/shard_map/ppermute | solution.py:323
  45.1 0.7 %collective-permute-start.16 = (bf16[128,128]{1,0:T(8,128)(2,1)S(1)}, bf16[128,128]{1,0:T(8,128)(2,1)S(1)}, u32[]{:S(2)}, u32[]{:S(2)}) collective-permute-start(bf16[128,128]{1,0:T(8,128)(2,1)S(1)} %get-tuple-element.43), channel_id=1, source_target_pairs={{0,16},{8,24},{16,0},{24,8},{1,17},{9,25},{17,1},{25,9},{2,18},{10... | collective-permute-start | bytes 98312 | tf_op jit(solution)/shard_map/ppermute | solution.py:323
  45.8 0.0 collective-permute-done.7.refs_0_
  45.8 0.2 collective-permute-start.17
  46.0 0.0 collective-permute-done.8.refs_1_
  46.0 0.0 collective-permute-done.9.refs_2_
  46.0 1.6 %collective-permute-done.15.refs_4_ = bf16[128,128]{1,0:T(8,128)(2,1)S(1)} collective-permute-done((bf16[128,128]{1,0:T(8,128)(2,1)S(1)}, bf16[128,128]{1,0:T(8,128)(2,1)S(1)}, u32[]{:S(2)}, u32[]{:S(2)}) %collective-permute-start.15) | collective-permute-done | bytes 32800 | tf_op jit(solution)/shard_map/ppermute | solution.py:323
  47.6 1.4 %collective-permute-done.16.refs_5_ = bf16[128,128]{1,0:T(8,128)(2,1)S(1)} collective-permute-done((bf16[128,128]{1,0:T(8,128)(2,1)S(1)}, bf16[128,128]{1,0:T(8,128)(2,1)S(1)}, u32[]{:S(2)}, u32[]{:S(2)}) %collective-permute-start.16) | collective-permute-done | bytes 32800 | tf_op jit(solution)/shard_map/ppermute | solution.py:323
  49.0 0.0 collective-permute-done.17.refs_6_
  49.0 0.9 %sum_unrotate.1 = (f32[256,128]{1,0:T(8,128)}, f32[1,256]{1,0:T(1,128)}) custom-call(s32[256,128]{1,0:T(8,128)S(1)} %get-tuple-element.32.sign_ref, bf16[128,128]{1,0:T(8,128)(2,1)S(1)} %collective-permute-done.7.refs_0_, bf16[128,128]{1,0:T(8,128)(2,1)S(1)} %collective-permute-done.8.refs_1_, bf16[128,128]{1,0:T(8,128)(2,1)S(1)} %collective-permute-done.9.refs_2_, ...), custom_call_target="tpu_custom_call" | custom-call | tf_op jit(solution)/shard_map/sum_unrotate/pallas_call | solution.py:294
  (1 shorter events, 0.0 us)
Async XLA Ops:
  3.8 10.9 %collective-permute-start = (bf16[4,128,128]{2,1,0:T(8,128)(2,1)S(1)}, bf16[4,128,128]{2,1,0:T(8,128)(2,1)S(1)}, u32[]{:S(2)}, u32[]{:S(2)}) collective-permute-start(bf16[4,128,128]{2,1,0:T(8,128)(2,1)S(1)} %get-tuple-element.25.refs_0_), channel_id=1, source_target_pairs={{0,3},{1,2},{2,1},{3,0},{4,7},{5,6},{6,5},{7,4},{8,11},{9,10},{10,... | collective-permute-start | bytes 393224 | tf_op jit(solution)/shard_map/ppermute | solution.py:317
  7.8 7.1 %collective-permute-start.1 = (bf16[4,128,128]{2,1,0:T(8,128)(2,1)S(1)}, bf16[4,128,128]{2,1,0:T(8,128)(2,1)S(1)}, u32[]{:S(2)}, u32[]{:S(2)}) collective-permute-start(bf16[4,128,128]{2,1,0:T(8,128)(2,1)S(1)} %get-tuple-element.26.refs_1_), channel_id=1, source_target_pairs={{0,2},{1,3},{2,0},{3,1},{4,6},{5,7},{6,4},{7,5},{8,10},{9,11},{10,... | collective-permute-start | bytes 393224 | tf_op jit(solution)/shard_map/ppermute | solution.py:317
  8.3 6.6 %collective-permute-start.2 = (bf16[4,128,128]{2,1,0:T(8,128)(2,1)S(1)}, bf16[4,128,128]{2,1,0:T(8,128)(2,1)S(1)}, u32[]{:S(2)}, u32[]{:S(2)}) collective-permute-start(bf16[4,128,128]{2,1,0:T(8,128)(2,1)S(1)} %get-tuple-element.27.refs_2_), channel_id=1, source_target_pairs={{0,1},{1,0},{2,3},{3,2},{4,5},{5,4},{6,7},{7,6},{8,9},{9,8},{10,11... | collective-permute-start | bytes 393224 | tf_op jit(solution)/shard_map/ppermute | solution.py:317
  11.4 11.3 %collective-permute-start.11 = (bf16[4,128,128]{2,1,0:T(8,128)(2,1)S(1)}, bf16[4,128,128]{2,1,0:T(8,128)(2,1)S(1)}, u32[]{:S(2)}, u32[]{:S(2)}) collective-permute-start(bf16[4,128,128]{2,1,0:T(8,128)(2,1)S(1)} %get-tuple-element.30.refs_4_), channel_id=1, source_target_pairs={{0,3},{1,2},{2,1},{3,0},{4,7},{5,6},{6,5},{7,4},{8,11},{9,10},{10,... | collective-permute-start | bytes 393224 | tf_op jit(solution)/shard_map/ppermute | solution.py:317
  14.3 13.2 %collective-permute-start.13 = (bf16[4,128,128]{2,1,0:T(8,128)(2,1)S(1)}, bf16[4,128,128]{2,1,0:T(8,128)(2,1)S(1)}, u32[]{:S(2)}, u32[]{:S(2)}) collective-permute-start(bf16[4,128,128]{2,1,0:T(8,128)(2,1)S(1)} %get-tuple-element.28.refs_3_), channel_id=1, source_target_pairs={{0,2},{1,3},{2,0},{3,1},{4,6},{5,7},{6,4},{7,5},{8,10},{9,11},{10,... | collective-permute-start | bytes 393224 | tf_op jit(solution)/shard_map/ppermute | solution.py:317
  14.7 10.1 %collective-permute-start.12 = (bf16[4,128,128]{2,1,0:T(8,128)(2,1)S(1)}, bf16[4,128,128]{2,1,0:T(8,128)(2,1)S(1)}, u32[]{:S(2)}, u32[]{:S(2)}) collective-permute-start(bf16[4,128,128]{2,1,0:T(8,128)(2,1)S(1)} %get-tuple-element.31.refs_5_), channel_id=1, source_target_pairs={{0,1},{1,0},{2,3},{3,2},{4,5},{5,4},{6,7},{7,6},{8,9},{9,8},{10,11... | collective-permute-start | bytes 393224 | tf_op jit(solution)/shard_map/ppermute | solution.py:317
  15.0 15.4 %collective-permute-start.6 = (f32[4,128,128]{2,1,0:T(8,128)S(1)}, f32[4,128,128]{2,1,0:T(8,128)S(1)}, u32[]{:S(2)}, u32[]{:S(2)}) collective-permute-start(f32[4,128,128]{2,1,0:T(8,128)S(1)} %far_sum.2.refs_0_), channel_id=1, source_target_pairs={{0,4},{1,5},{2,6},{3,7},{4,0},{5,1},{6,2},{7,3},{8,12},{9,13},{10,... | collective-permute-start | bytes 786440 | tf_op jit(solution)/shard_map/ppermute | solution.py:340
  21.0 20.6 %collective-permute-start.3 = (bf16[4,256,128]{2,1,0:T(8,128)(2,1)S(1)}, bf16[4,256,128]{2,1,0:T(8,128)(2,1)S(1)}, u32[]{:S(2)}, u32[]{:S(2)}) collective-permute-start(bf16[4,256,128]{2,1,0:T(8,128)(2,1)S(1)} %get-tuple-element.33.refs_4_), channel_id=1, source_target_pairs={{0,2},{1,3},{2,0},{3,1},{4,6},{5,7},{6,4},{7,5},{8,10},{9,11},{10,... | collective-permute-start | bytes 786440 | tf_op jit(solution)/shard_map/ppermute | solution.py:317
  22.7 18.9 %collective-permute-start.4 = (bf16[4,256,128]{2,1,0:T(8,128)(2,1)S(1)}, bf16[4,256,128]{2,1,0:T(8,128)(2,1)S(1)}, u32[]{:S(2)}, u32[]{:S(2)}) collective-permute-start(bf16[4,256,128]{2,1,0:T(8,128)(2,1)S(1)} %get-tuple-element.34.refs_5_), channel_id=1, source_target_pairs={{0,1},{1,0},{2,3},{3,2},{4,5},{5,4},{6,7},{7,6},{8,9},{9,8},{10,11... | collective-permute-start | bytes 786440 | tf_op jit(solution)/shard_map/ppermute | solution.py:317
  27.5 16.3 %collective-permute-start.14 = (f32[4,128,128]{2,1,0:T(8,128)S(1)}, f32[4,128,128]{2,1,0:T(8,128)S(1)}, u32[]{:S(2)}, u32[]{:S(2)}) collective-permute-start(f32[4,128,128]{2,1,0:T(8,128)S(1)} %far_sum.3), channel_id=1, source_target_pairs={{0,4},{1,5},{2,6},{3,7},{4,0},{5,1},{6,2},{7,3},{8,12},{9,13},{10,... | collective-permute-start | bytes 786440 | tf_op jit(solution)/shard_map/ppermute | solution.py:355
  27.6 14.0 %collective-permute-start.5 = (bf16[4,128,128]{2,1,0:T(8,128)(2,1)S(1)}, bf16[4,128,128]{2,1,0:T(8,128)(2,1)S(1)}, u32[]{:S(2)}, u32[]{:S(2)}) collective-permute-start(bf16[4,128,128]{2,1,0:T(8,128)(2,1)S(1)} %get-tuple-element.36), channel_id=1, source_target_pairs={{0,3},{1,2},{2,1},{3,0},{4,7},{5,6},{6,5},{7,4},{8,11},{9,10},{10,... | collective-permute-start | bytes 393224 | tf_op jit(solution)/shard_map/ppermute | solution.py:317
  30.4 13.4 %collective-permute-start.10 = (bf16[4,128,128]{2,1,0:T(8,128)(2,1)S(1)}, bf16[4,128,128]{2,1,0:T(8,128)(2,1)S(1)}, u32[]{:S(2)}, u32[]{:S(2)}) collective-permute-start(bf16[4,128,128]{2,1,0:T(8,128)(2,1)S(1)} %hand_on.1), channel_id=1, source_target_pairs={{0,3},{1,2},{2,1},{3,0},{4,7},{5,6},{6,5},{7,4},{8,11},{9,10},{10,... | collective-permute-start | bytes 393224 | tf_op jit(solution)/shard_map/ppermute | solution.py:317
  41.9 4.0 %collective-permute-start.7 = (bf16[128,128]{1,0:T(8,128)(2,1)S(1)}, bf16[128,128]{1,0:T(8,128)(2,1)S(1)}, u32[]{:S(2)}, u32[]{:S(2)}) collective-permute-start(bf16[128,128]{1,0:T(8,128)(2,1)S(1)} %get-tuple-element.37), channel_id=1, source_target_pairs={{0,24},{8,16},{16,8},{24,0},{1,25},{9,17},{17,9},{25,1},{2,26},{10... | collective-permute-start | bytes 98312 | tf_op jit(solution)/shard_map/ppermute | solution.py:323
  42.0 4.0 %collective-permute-start.8 = (bf16[128,128]{1,0:T(8,128)(2,1)S(1)}, bf16[128,128]{1,0:T(8,128)(2,1)S(1)}, u32[]{:S(2)}, u32[]{:S(2)}) collective-permute-start(bf16[128,128]{1,0:T(8,128)(2,1)S(1)} %get-tuple-element.38), channel_id=1, source_target_pairs={{0,16},{8,24},{16,0},{24,8},{1,17},{9,25},{17,1},{25,9},{2,18},{10... | collective-permute-start | bytes 98312 | tf_op jit(solution)/shard_map/ppermute | solution.py:323
  43.4 2.7 %collective-permute-start.9 = (bf16[128,128]{1,0:T(8,128)(2,1)S(1)}, bf16[128,128]{1,0:T(8,128)(2,1)S(1)}, u32[]{:S(2)}, u32[]{:S(2)}) collective-permute-start(bf16[128,128]{1,0:T(8,128)(2,1)S(1)} %get-tuple-element.39), channel_id=1, source_target_pairs={{0,8},{8,0},{16,24},{24,16},{1,9},{9,1},{17,25},{25,17},{2,10},{10... | collective-permute-start | bytes 98312 | tf_op jit(solution)/shard_map/ppermute | solution.py:323
  44.1 3.5 %collective-permute-start.15 = (bf16[128,128]{1,0:T(8,128)(2,1)S(1)}, bf16[128,128]{1,0:T(8,128)(2,1)S(1)}, u32[]{:S(2)}, u32[]{:S(2)}) collective-permute-start(bf16[128,128]{1,0:T(8,128)(2,1)S(1)} %get-tuple-element.42), channel_id=1, source_target_pairs={{0,24},{8,16},{16,8},{24,0},{1,25},{9,17},{17,9},{25,1},{2,26},{10... | collective-permute-start | bytes 98312 | tf_op jit(solution)/shard_map/ppermute | solution.py:323
  45.1 3.9 %collective-permute-start.16 = (bf16[128,128]{1,0:T(8,128)(2,1)S(1)}, bf16[128,128]{1,0:T(8,128)(2,1)S(1)}, u32[]{:S(2)}, u32[]{:S(2)}) collective-permute-start(bf16[128,128]{1,0:T(8,128)(2,1)S(1)} %get-tuple-element.43), channel_id=1, source_target_pairs={{0,16},{8,24},{16,0},{24,8},{1,17},{9,25},{17,1},{25,9},{2,18},{10... | collective-permute-start | bytes 98312 | tf_op jit(solution)/shard_map/ppermute | solution.py:323
  45.8 3.2 %collective-permute-start.17 = (bf16[128,128]{1,0:T(8,128)(2,1)S(1)}, bf16[128,128]{1,0:T(8,128)(2,1)S(1)}, u32[]{:S(2)}, u32[]{:S(2)}) collective-permute-start(bf16[128,128]{1,0:T(8,128)(2,1)S(1)} %get-tuple-element.44), channel_id=1, source_target_pairs={{0,8},{8,0},{16,24},{24,16},{1,9},{9,1},{17,25},{25,17},{2,10},{10... | collective-permute-start | bytes 98312 | tf_op jit(solution)/shard_map/ppermute | solution.py:323
